TPU v7x, 128 devices: a whole 4x4x4 slice. The times are simulated.
128 devices in a mesh: frame: 4 (over z_hi, core), row: 8 (over z_lo, x), col: 4 (over y).
Axes of the slice: x: 4, y: 4, z: 4 (z_hi: 2, z_lo: 2; z = z_hi * 2 + z_lo), core: 2. Of those that a mesh axis runs over, the one named last changes fastest.
Arguments:
- tokens_in: bfloat16 [16, 128, 64, 3072], P('frame', 'row', 'col'), may hold values from -4 to 4
- queries: bfloat16 [16, 128, 64, 1536], P('frame', 'row', 'col'), may hold values from -100 to 100
- key_rows: bfloat16 [16, 128, 64, 1536], P('frame', 'row', 'col'), may hold values from -6 to 6
- value_rows: bfloat16 [16, 128, 64, 1536], P('frame', 'row', 'col'), may hold values from -6 to 6
- out_weight: bfloat16 [1536, 3072], P(None, ('frame', 'row', 'col')), may hold values from -2.5 to 2.5
- row_valid: int32 [128], replicated, may hold values from 0 to 1, as said below
Outputs:
- layer_out: bfloat16 [16, 128, 64, 3072], P('frame', 'row', 'col')
Inputs may be any that keep to these rules, and one draw needn't show every extreme that they name: row_valid is 1 on a leading run of rows and 0 on the rest; at least one row is 0 and at most 24 are.
All inputs are finite; a program needn't handle non-finite values.
Results may differ from a plain program's by a relative error of at most 0.014.
Values may be sent and summed in bfloat16 or wider, within the bound.
No kernel may reach another device: no remote copies, remote signals or barrier semaphores. Data moves between devices by JAX's collectives and lax.ppermute only.
A program may use at most 192 MiB of HBM per device.

v0:
```python
import jax
import jax.numpy as jnp
from jax import lax
from jax.sharding import PartitionSpec as P

D = 3072
HS = 128
WF = 4
WR = 16
WC = 16


def shifted(value, axis, steps):
    count = lax.axis_size(axis)
    pairs = [(source, (source + steps) % count) for source in range(count)]
    return lax.ppermute(value, axis, pairs)


def attend_window(query_win, key_win, value_win, frame_ids, row_ids, col_ids, alive_mask):
    tokens_win = query_win.shape[0]
    head_count = query_win.shape[1] // HS
    query_heads = query_win.reshape(tokens_win, head_count, HS)
    key_heads = key_win.reshape(tokens_win, head_count, HS)
    value_heads = value_win.reshape(tokens_win, head_count, HS)
    scores = jnp.einsum(
        "qhd,khd->hqk", query_heads, key_heads, preferred_element_type=jnp.float32
    ) * HS ** (-0.5)
    allowed = (frame_ids[:, None] == frame_ids[None, :]) & (row_ids[:, None] == row_ids[None, :])
    allowed = allowed & (col_ids[:, None] == col_ids[None, :])
    allowed = allowed & (alive_mask[:, None] > 0) & (alive_mask[None, :] > 0)
    scores = jnp.where(allowed[None], scores, -1e30)
    row_max = jnp.max(scores, axis=2, keepdims=True)
    exponent = jnp.exp(scores - row_max)
    row_total = jnp.sum(exponent, axis=2, keepdims=True)
    weights = (exponent / row_total).astype(jnp.bfloat16)
    mixed_heads = jnp.einsum(
        "hqk,khd->qhd", weights, value_heads, preferred_element_type=jnp.float32
    )
    mixed_heads = mixed_heads * alive_mask[:, None, None].astype(jnp.float32)
    return mixed_heads.reshape(tokens_win, head_count * HS).astype(jnp.bfloat16)


def to_windows(array):
    frames, rows_all, cols_all, channels = array.shape
    split = array.reshape(frames // WF, WF, rows_all // WR, WR, cols_all // WC, WC, channels)
    split = split.transpose(0, 2, 4, 1, 3, 5, 6)
    return split.reshape(-1, WF * WR * WC, channels)


def shift_frames(slab, offset):
    return shifted(slab, "frame", offset)


def shift_rows(slab, offset):
    return shifted(slab, "row", offset)


def shift_cols(slab, offset):
    return shifted(slab, "col", offset)


def roll_block(field_block, axis_dim, half_width, offset, sender):
    extent = field_block.shape[axis_dim]
    if offset > 0:
        arrived = sender(
            lax.slice_in_dim(field_block, extent - half_width, extent, axis=axis_dim), offset
        )
        kept = lax.slice_in_dim(field_block, 0, extent - half_width, axis=axis_dim)
        return jnp.concatenate([arrived, kept], axis=axis_dim)
    arrived = sender(lax.slice_in_dim(field_block, 0, half_width, axis=axis_dim), offset)
    kept = lax.slice_in_dim(field_block, half_width, extent, axis=axis_dim)
    return jnp.concatenate([kept, arrived], axis=axis_dim)


def roll_all(field_block, offset, sections):
    for axis_dim, half_width, sender in sections:
        field_block = roll_block(field_block, axis_dim, half_width, offset, sender)
    return field_block


def local(tokens_in, queries, key_rows, value_rows, out_weight, row_valid):
    frame_count, row_count, col_count, feature_width = queries.shape
    total_frames = frame_count * lax.axis_size("frame")
    total_rows = row_count * lax.axis_size("row")
    total_cols = col_count * lax.axis_size("col")
    frame_section = (1, WF // 2, shift_frames)
    packed = jnp.stack((queries, key_rows, value_rows))
    row_section = (2, WR // 2, shift_rows)
    col_section = (3, WC // 2, shift_cols)
    sections = (frame_section, row_section, col_section)
    rolled = roll_all(packed, 1, sections)
    frame_place = (
        lax.axis_index("frame") * frame_count + jnp.arange(frame_count, dtype=jnp.int32) - WF // 2
    ) % total_frames
    row_place = (
        lax.axis_index("row") * row_count + jnp.arange(row_count, dtype=jnp.int32) - WR // 2
    ) % total_rows
    col_place = (
        lax.axis_index("col") * col_count + jnp.arange(col_count, dtype=jnp.int32) - WC // 2
    ) % total_cols
    frame_ids = (frame_place + WF // 2) // WF
    row_ids = (row_place + WR // 2) // WR
    col_ids = (col_place + WC // 2) // WC
    matches = row_place[:, None] == jnp.arange(total_rows, dtype=jnp.int32)[None, :]
    alive_rows = jnp.sum(jnp.where(matches, row_valid[None, :], 0), axis=1)
    grid_shape = (frame_count, row_count, col_count)
    frame_grid = jnp.broadcast_to(frame_ids[:, None, None], grid_shape)[..., None]
    row_grid = jnp.broadcast_to(row_ids[None, :, None], grid_shape)[..., None]
    col_grid = jnp.broadcast_to(col_ids[None, None, :], grid_shape)[..., None]
    alive_grid = jnp.broadcast_to(alive_rows[None, :, None], grid_shape)[..., None]
    bundle = (
        to_windows(rolled[0]),
        to_windows(rolled[1]),
        to_windows(rolled[2]),
        to_windows(frame_grid)[..., 0],
        to_windows(row_grid)[..., 0],
        to_windows(col_grid)[..., 0],
        to_windows(alive_grid)[..., 0],
    )
    attended = lax.map(lambda items: attend_window(*items), bundle)
    attended = attended.reshape(
        frame_count // WF, row_count // WR, col_count // WC, WF, WR, WC, feature_width
    )
    attended = attended.transpose(0, 3, 1, 4, 2, 5, 6).reshape(
        1, frame_count, row_count, col_count, feature_width
    )
    restored = roll_all(attended, -1, sections)[0]
    flat_rows = restored.reshape(-1, feature_width)
    projected = jnp.dot(
        flat_rows,
        lax.all_gather(out_weight, ("frame", "row", "col"), axis=1, tiled=True),
        preferred_element_type=jnp.float32,
    )
    summed = projected + tokens_in.reshape(-1, D).astype(jnp.float32)
    return summed.astype(jnp.bfloat16).reshape(frame_count, row_count, col_count, D)


def solution(mesh):
    return jax.shard_map(
        local,
        mesh=mesh,
        in_specs=(
            P("frame", "row", "col", None),
            P("frame", "row", "col", None),
            P("frame", "row", "col", None),
            P("frame", "row", "col", None),
            P(None, ("frame", "row", "col")),
            P(),
        ),
        out_specs=P("frame", "row", "col", None),
        check_vma=False,
    )
```

profile of v0, /device:TPU:1, one launch (start us, length us, event | category | flops | bytes accessed | tf_op | source)
XLA Modules:
  0.0 541.9 jit_solution(1012328299784104710)
XLA Ops:
  6.5 8.4 %pad_maximum_fusion.1 = bf16[3,4,16,16,1536]{4,3,2,1,0:T(8,128)(2,1)} fusion(bf16[1,4,16,16,1536]{4,3,2,1,0:T(8,128)(2,1)} %bitcast.18, bf16[1,4,16,16,1536]{4,3,2,1,0:T(8,128)(2,1)} %bitcast.19, bf16[1,4,16,16,1536]{4,3,2,1,0:T(8,128)(2,1)} %bitcast.20), kind=kLoop, calls=%fused_computation.17 | loop fusion | flops 9437184 | bytes 18874368 | tf_op jit(solution)/shard_map/stack | solution.py:87
  14.9 4.6 fusion.38
  19.6 5.1 collective-permute-start
  24.6 51.1 %collective-permute-done = bf16[3,2,16,16,1536]{4,3,2,1,0:T(8,128)(2,1)S(1)} collective-permute-done((bf16[3,2,16,16,1536]{4,3,2,1,0:T(8,128)(2,1)S(1)}, bf16[3,2,16,16,1536]{4,3,2,1,0:T(8,128)(2,1)S(1)}, u32[]{:S(2)}, u32[]{:S(2)}) %collective-permute-start) | collective-permute-done | bytes 4718624 | tf_op jit(solution)/shard_map/ppermute | solution.py:16
  75.7 0.4 fusion.10
  76.1 1.3 collective-permute-start.1
  77.4 103.7 %collective-permute-done.1 = bf16[3,4,8,16,1536]{4,3,2,1,0:T(8,128)(2,1)S(1)} collective-permute-done((bf16[3,4,8,16,1536]{4,3,2,1,0:T(8,128)(2,1)S(1)}, bf16[3,4,8,16,1536]{4,3,2,1,0:T(8,128)(2,1)S(1)}, u32[]{:S(2)}, u32[]{:S(2)}) %collective-permute-start.1) | collective-permute-done | bytes 4718624 | tf_op jit(solution)/shard_map/ppermute | solution.py:16
  181.1 4.3 fusion.7
  185.4 8.5 %fusion.37 = (bf16[3,4,16,8,1536]{4,3,2,1,0:T(8,128)(2,1)}, bf16[3,4,16,8,1536]{4,3,2,1,0:T(8,128)(2,1)}) fusion(bf16[3,4,16,16,1536]{4,3,2,1,0:T(8,128)(2,1)} %fusion.7), kind=kLoop, calls=%fused_computation.74 | loop fusion | bytes 18874368 | tf_op jit(solution)/shard_map/slice | solution.py:66
  193.9 1.3 collective-permute-start.2
  196.2 2.6 and_and_fusion
  198.8 98.6 %collective-permute-done.2 = bf16[3,4,16,8,1536]{4,3,2,1,0:T(8,128)(2,1)} collective-permute-done((bf16[3,4,16,8,1536]{4,3,2,1,0:T(8,128)(2,1)}, bf16[3,4,16,8,1536]{4,3,2,1,0:T(8,128)(2,1)}, u32[]{:S(2)}, u32[]{:S(2)}) %collective-permute-start.2) | collective-permute-done | bytes 4718624 | tf_op jit(solution)/shard_map/ppermute | solution.py:16
  297.4 6.1 %fusion.13 = (bf16[1,4,16,16,1536]{4,3,2,1,0:T(8,128)(2,1)S(1)}, bf16[1,4,16,16,1536]{4,3,2,1,0:T(8,128)(2,1)}, bf16[1,4,16,16,1536]{4,3,2,1,0:T(8,128)(2,1)}) fusion(bf16[3,4,16,8,1536]{4,3,2,1,0:T(8,128)(2,1)} %collective-permute-done.2, bf16[3,4,16,8,1536]{4,3,2,1,0:T(8,128)(2,1)} %get-tuple-element.25), kind=kLoop, calls=%fused_computation.26 | loop fusion | flops 18874368 | bytes 18874368 | tf_op jit(solution)/shard_map/concatenate | solution.py:69
  303.5 6.9 %reshape.255 = bf16[1024,12,128]{2,1,0:T(8,128)(2,1)} reshape(bf16[1,4,16,16,1536]{4,3,2,1,0:T(8,128)(2,1)} %get-tuple-element.23) | data formatting | bytes 6291456 | tf_op jit(solution)/shard_map/while/body/eval_jaxpr/reshape | solution.py:22
  310.4 6.9 %reshape.256 = bf16[1024,12,128]{2,1,0:T(8,128)(2,1)} reshape(bf16[1,4,16,16,1536]{4,3,2,1,0:T(8,128)(2,1)} %get-tuple-element.22) | data formatting | bytes 6291456 | tf_op jit(solution)/shard_map/while/body/eval_jaxpr/reshape | solution.py:23
  317.3 3.6 reshape.254
  320.9 25.6 %fusion.40 = (f32[12,1024]{1,0:T(8,128)S(1)}, f32[12,1024,1024]{1,2,0:T(8,128)}) fusion(pred[1024,1024]{0,1:T(8,128)(4,1)} %and_and_fusion, bf16[1024,12,128]{2,1,0:T(8,128)(2,1)} %reshape.256, bf16[1024,12,128]{2,1,0:T(8,128)(2,1)} %reshape.255), kind=kOutput, calls=%fused_computation.77 | convolution fusion | flops 3271558144 | bytes 57720832 | tf_op jit(solution)/shard_map/while/body/eval_jaxpr/sub | solution.py:33
  346.5 19.5 %fusion.11 = bf16[1024,12,128]{0,2,1:T(8,128)(2,1)S(1)} fusion(f32[1024]{0:T(1024)S(1)} %convert_element_type.45, f32[12,1024,1024]{1,2,0:T(8,128)} %get-tuple-element.46, f32[12,1024]{1,0:T(8,128)S(1)} %get-tuple-element.45, bf16[1024,12,128]{2,1,0:T(8,128)(2,1)} %reshape.254), kind=kOutput, calls=%fused_computation.24 | convolution fusion | flops 3249537024 | bytes 56676352 | tf_op jit(solution)/shard_map/while/body/eval_jaxpr/hqk,khd->qhd/dot_general | solution.py:36
  366.0 7.7 %copy.18 = bf16[1024,12,128]{2,1,0:T(8,128)(2,1)} copy(bf16[1024,12,128]{0,2,1:T(8,128)(2,1)S(1)} %fusion.11) | data formatting | bytes 6291456 | tf_op jit(solution)/shard_map/while/body/eval_jaxpr/convert_element_type | solution.py:40
  373.6 5.5 %convert_element_type.48 = bf16[1,4,16,16,1536]{4,3,2,1,0:T(8,128)(2,1)S(1)} reshape(bf16[1024,12,128]{2,1,0:T(8,128)(2,1)} %copy.18) | data formatting | bytes 6291456 | tf_op jit(solution)/shard_map/while/body/eval_jaxpr/convert_element_type | solution.py:40
  379.2 0.2 fusion.39
  379.4 2.6 collective-permute-start.3
  381.9 21.4 %collective-permute-done.3 = bf16[1,2,16,16,1536]{4,3,2,1,0:T(8,128)(2,1)S(1)} collective-permute-done((bf16[1,2,16,16,1536]{4,3,2,1,0:T(8,128)(2,1)S(1)}, bf16[1,2,16,16,1536]{4,3,2,1,0:T(8,128)(2,1)S(1)}, u32[]{:S(2)}, u32[]{:S(2)}) %collective-permute-start.3) | collective-permute-done | bytes 1572896 | tf_op jit(solution)/shard_map/ppermute | solution.py:16
  403.4 0.3 fusion.29
  403.7 10.9 %collective-permute-start.4 = (bf16[1,4,8,16,1536]{4,3,2,1,0:T(8,128)(2,1)S(1)}, bf16[1,4,8,16,1536]{4,3,2,1,0:T(8,128)(2,1)S(1)}, u32[]{:S(2)}, u32[]{:S(2)}) collective-permute-start(bf16[1,4,8,16,1536]{4,3,2,1,0:T(8,128)(2,1)S(1)} %get-tuple-element.42), channel_id=1, source_target_pairs={{0,28},{4,0},{8,4},{12,8},{16,12},{20,16},{24,20},{28,24},{1,29},{... | collective-permute-start | bytes 4718600 | tf_op jit(solution)/shard_map/ppermute | solution.py:16
  414.6 33.5 %collective-permute-done.4 = bf16[1,4,8,16,1536]{4,3,2,1,0:T(8,128)(2,1)S(1)} collective-permute-done((bf16[1,4,8,16,1536]{4,3,2,1,0:T(8,128)(2,1)S(1)}, bf16[1,4,8,16,1536]{4,3,2,1,0:T(8,128)(2,1)S(1)}, u32[]{:S(2)}, u32[]{:S(2)}) %collective-permute-start.4) | collective-permute-done | bytes 1572896 | tf_op jit(solution)/shard_map/ppermute | solution.py:16
  448.1 0.3 fusion.28
  448.4 14.5 %collective-permute-start.5 = (bf16[1,4,16,8,1536]{4,3,2,1,0:T(8,128)(2,1)S(1)}, bf16[1,4,16,8,1536]{4,3,2,1,0:T(8,128)(2,1)S(1)}, u32[]{:S(2)}, u32[]{:S(2)}) collective-permute-start(bf16[1,4,16,8,1536]{4,3,2,1,0:T(8,128)(2,1)S(1)} %get-tuple-element.40), channel_id=1, source_target_pairs={{0,3},{1,0},{2,1},{3,2},{4,7},{5,4},{6,5},{7,6},{8,11},{9,8},{10,9... | collective-permute-start | bytes 4718600 | tf_op jit(solution)/shard_map/ppermute | solution.py:16
  462.9 33.7 %collective-permute-done.5 = bf16[1,4,16,8,1536]{4,3,2,1,0:T(8,128)(2,1)S(1)} collective-permute-done((bf16[1,4,16,8,1536]{4,3,2,1,0:T(8,128)(2,1)S(1)}, bf16[1,4,16,8,1536]{4,3,2,1,0:T(8,128)(2,1)S(1)}, u32[]{:S(2)}, u32[]{:S(2)}) %collective-permute-start.5) | collective-permute-done | bytes 1572896 | tf_op jit(solution)/shard_map/ppermute | solution.py:16
  496.6 0.4 pad_maximum_fusion.3
  497.0 22.1 %all-gather.2.cloned.1.call-done = bf16[1536,3072]{0,1:T(8,128)(2,1)} async-done(((bf16[1536,24]{0,1:T(8,128)(2,1)}), bf16[1536,3072]{0,1:T(8,128)(2,1)}) %all-gather.2.cloned.1.call-update) | async-done | bytes 9437200 | tf_op jit(solution)/shard_map/all_gather | solution.py:131
  519.2 15.9 %fusion.6 = bf16[1024,3072]{1,0:T(8,128)(2,1)} fusion(bf16[4,16,16,3072]{3,2,1,0:T(8,128)(2,1)} %param.6, bf16[1024,1536]{1,0:T(8,128)(2,1)S(1)} %bitcast.21, bf16[1536,3072]{0,1:T(8,128)(2,1)} %all-gather.2.cloned.1.call-done), kind=kOutput, calls=%fused_computation.10 | convolution fusion | flops 9673113600 | bytes 25165824 | tf_op jit(solution)/shard_map/dot_general | solution.py:129
  (20 shorter events, 1.0 us)
Async XLA Ops:
  6.5 512.6 %all-gather.2.cloned.1.call-start = ((), (), s32[]{:S(2)}) async-start(), calls=%async_computation | async-start | bytes 9510912 | tf_op jit(solution)/shard_map/all_gather | solution.py:131
  19.6 56.1 %collective-permute-start = (bf16[3,2,16,16,1536]{4,3,2,1,0:T(8,128)(2,1)S(1)}, bf16[3,2,16,16,1536]{4,3,2,1,0:T(8,128)(2,1)S(1)}, u32[]{:S(2)}, u32[]{:S(2)}) collective-permute-start(bf16[3,2,16,16,1536]{4,3,2,1,0:T(8,128)(2,1)S(1)} %get-tuple-element.26), channel_id=1, source_target_pairs={{0,32},{32,64},{64,96},{96,0},{1,33},{33,65},{65,97},{97,1},{2,34}... | collective-permute-start | bytes 14155784 | tf_op jit(solution)/shard_map/ppermute | solution.py:16
  76.1 105.0 %collective-permute-start.1 = (bf16[3,4,8,16,1536]{4,3,2,1,0:T(8,128)(2,1)S(1)}, bf16[3,4,8,16,1536]{4,3,2,1,0:T(8,128)(2,1)S(1)}, u32[]{:S(2)}, u32[]{:S(2)}) collective-permute-start(bf16[3,4,8,16,1536]{4,3,2,1,0:T(8,128)(2,1)S(1)} %fusion.10), channel_id=1, source_target_pairs={{0,4},{4,8},{8,12},{12,16},{16,20},{20,24},{24,28},{28,0},{1,5},{5... | collective-permute-start | bytes 14155784 | tf_op jit(solution)/shard_map/ppermute | solution.py:16
  185.4 9.8 %copy-start = (s32[128]{0:T(128)S(1)}, s32[128]{0:T(128)}, u32[]{:S(2)}) copy-start(s32[128]{0:T(128)} %param.11) | copy-start | bytes 1540
  193.9 103.5 %collective-permute-start.2 = (bf16[3,4,16,8,1536]{4,3,2,1,0:T(8,128)(2,1)}, bf16[3,4,16,8,1536]{4,3,2,1,0:T(8,128)(2,1)}, u32[]{:S(2)}, u32[]{:S(2)}) collective-permute-start(bf16[3,4,16,8,1536]{4,3,2,1,0:T(8,128)(2,1)} %get-tuple-element.24), channel_id=1, source_target_pairs={{0,1},{1,2},{2,3},{3,0},{4,5},{5,6},{6,7},{7,4},{8,9},{9,10},{10,1... | collective-permute-start | bytes 14155784 | tf_op jit(solution)/shard_map/ppermute | solution.py:16
  379.4 24.0 %collective-permute-start.3 = (bf16[1,2,16,16,1536]{4,3,2,1,0:T(8,128)(2,1)S(1)}, bf16[1,2,16,16,1536]{4,3,2,1,0:T(8,128)(2,1)S(1)}, u32[]{:S(2)}, u32[]{:S(2)}) collective-permute-start(bf16[1,2,16,16,1536]{4,3,2,1,0:T(8,128)(2,1)S(1)} %get-tuple-element.44), channel_id=1, source_target_pairs={{0,96},{32,0},{64,32},{96,64},{1,97},{33,1},{65,33},{97,65},{2,98}... | collective-permute-start | bytes 4718600 | tf_op jit(solution)/shard_map/ppermute | solution.py:16
  403.7 44.4 %collective-permute-start.4 = (bf16[1,4,8,16,1536]{4,3,2,1,0:T(8,128)(2,1)S(1)}, bf16[1,4,8,16,1536]{4,3,2,1,0:T(8,128)(2,1)S(1)}, u32[]{:S(2)}, u32[]{:S(2)}) collective-permute-start(bf16[1,4,8,16,1536]{4,3,2,1,0:T(8,128)(2,1)S(1)} %get-tuple-element.42), channel_id=1, source_target_pairs={{0,28},{4,0},{8,4},{12,8},{16,12},{20,16},{24,20},{28,24},{1,29},{... | collective-permute-start | bytes 4718600 | tf_op jit(solution)/shard_map/ppermute | solution.py:16
  448.4 48.2 %collective-permute-start.5 = (bf16[1,4,16,8,1536]{4,3,2,1,0:T(8,128)(2,1)S(1)}, bf16[1,4,16,8,1536]{4,3,2,1,0:T(8,128)(2,1)S(1)}, u32[]{:S(2)}, u32[]{:S(2)}) collective-permute-start(bf16[1,4,16,8,1536]{4,3,2,1,0:T(8,128)(2,1)S(1)} %get-tuple-element.40), channel_id=1, source_target_pairs={{0,3},{1,0},{2,1},{3,2},{4,7},{5,4},{6,5},{7,6},{8,11},{9,8},{10,9... | collective-permute-start | bytes 4718600 | tf_op jit(solution)/shard_map/ppermute | solution.py:16
Sparse Core Ops, SparseCore 0:
  195.4 323.7 all-gather.1
where the time goes:
time: 552 us; the launch traced here: 542 us
  waiting for transfers between devices  364 us (66%)
  matrix products  61 us (11%)
  local copies, waits for them, and re-layouts  44.6 us (8%)
  starting transfers between devices  35.6 us (6%)
  other arithmetic  23.1 us (4%)
  between operations  13.5 us (2%)
    ppermute x6, waiting for transfers between devices, shifted(): return lax.ppermute(value, axis, pairs)  342 us
    ppermute x6, starting transfers between devices, shifted(): return lax.ppermute(value, axis, pairs)  35.6 us
    sub x1, matrix products, attend_window(): exponent = jnp.exp(scores - row_max)  25.6 us
    all_gather x1, waiting for transfers between devices, local(): lax.all_gather(out_weight, ('frame', 'row', 'col'), axis=1, tiled=True)  22.1 us
    dot_general x1, matrix products, attend_window(): jnp.einsum('hqk,khd->qhd', weights, value_heads, preferred_element_type=j...  19.5 us
    dot_general x1, matrix products, local(): jnp.dot(flat_rows, lax.all_gather(out_weight, ('frame', 'row', 'col'), ax...  15.9 us
    convert_element_type x2, local copies, waits for them, and re-layouts, attend_window(): return mixed_heads.reshape(tokens_win, head_count * HS).astype(jnp.bfloat16)  13.2 us
    slice x2, local copies, waits for them, and re-layouts, roll_block(): lax.slice_in_dim(field_block, extent - half_width, extent, axis=axis_dim)  13.1 us
  transfers between devices with their start and end apart: 7, of which 7 were waited for; matrix products, arithmetic and copies ran while one was open for 16% of the time, Pallas kernels for 0%

commit v1 on v0

v1 whole, which is shorter than its diff:
```python
import functools
import math

import jax
import jax.numpy as jnp
from jax import lax
from jax.experimental import pallas as pl
from jax.experimental.pallas import tpu as pltpu
from jax.sharding import PartitionSpec as P

D = 3072
H = 12
HS = 128
HD = 1536
F, R, C = 4, 8, 4
AXES = ("frame", "row", "col")
GROUPS = ((0, 6), (6, 6))
BIG = 1e30
TILE = 384
VMEM = 56 * 1024 * 1024


def index(f, r, c):
    return ((f % F) * R + (r % R)) * C + (c % C)


def every():
    return [(f, r, c) for f in range(F) for r in range(R) for c in range(C)]


def window_pairs(half, dr, dc, back=False):
    pairs = []
    for f, r, c in every():
        step = 1 if (f + half) % 2 == 0 else -1
        here, there = index(f, r, c), index(f, r + step * dr, c + step * dc)
        pairs.append((there, here) if back else (here, there))
    return pairs


def frame_pairs(step):
    return [(index(f, r, c), index(f + step, r, c)) for f, r, c in every() if 0 <= f + step < F]


def core_pairs():
    return [(index(f, r, c), index(f ^ 1, r, c)) for f, r, c in every()]


def plane_pairs(dx, dy):
    pairs = []
    for f, r, c in every():
        zlo, x = divmod(r, 4)
        pairs.append((index(f, r, c), index(f, zlo * 4 + (x + dx) % 4, c + dy)))
    return pairs


def depth_pairs():
    pairs = []
    for f, r, c in every():
        zhi, core = divmod(f, 2)
        zlo, x = divmod(r, 4)
        z = (zhi * 2 + zlo + (1 if core == 0 else -1)) % 4
        pairs.append((index(f, r, c), index((z // 2) * 2 + core, (z % 2) * 4 + x, c)))
    return pairs


def send(value, pairs):
    return lax.ppermute(value, AXES, pairs)


MOVES = ((0, 0), (1, 0), (0, 1), (1, 1))


def pack_kernel(half, lane, width, sign_ref, q_ref, k_ref, v_ref, *rest):
    outs, sems = rest[:4], rest[4]
    s = sign_ref[0]
    copies = []
    for piece, (a, b) in enumerate(MOVES):
        i = s + a * (1 - 2 * s)
        j = s + b * (1 - 2 * s)
        for n, src in enumerate((q_ref, k_ref, v_ref)):
            for fr in range(2):
                copies.append(
                    pltpu.make_async_copy(
                        src.at[2 * half + fr, i, :, j, :, pl.ds(lane, width)],
                        outs[piece].at[n, fr],
                        sems.at[piece * 6 + n * 2 + fr],
                    )
                )
    for copy in copies:
        copy.start()
    for copy in copies:
        copy.wait()


def pack(half, first, heads, sign, q, k, v):
    width = heads * HS
    any_spec = pl.BlockSpec(memory_space=pl.ANY)
    shape = jax.ShapeDtypeStruct((3, 2, 8, 8, width), jnp.bfloat16)
    outs = pl.pallas_call(
        functools.partial(pack_kernel, half, first * HS, width),
        out_shape=[shape] * 4,
        in_specs=[pl.BlockSpec(memory_space=pltpu.SMEM)] + [any_spec] * 3,
        out_specs=[any_spec] * 4,
        scratch_shapes=[pltpu.SemaphoreType.DMA((24,))],
        cost_estimate=pl.CostEstimate(flops=0, bytes_accessed=24 * 128 * width * 2, transcendentals=0),
        name=f"pack_{half}_{first}",
    )(sign, q, k, v)
    return [o.reshape(3, 128, width) for o in outs]


def halo_kernel(*refs):
    srcs, out, sems = refs[:4], refs[4], refs[5]
    copies = []
    for piece, src in enumerate(srcs):
        for n in range(2):
            copies.append(pltpu.make_async_copy(src.at[1 + n], out.at[n, piece], sems.at[piece * 2 + n]))
    for copy in copies:
        copy.start()
    for copy in copies:
        copy.wait()


def halo_pack(pieces):
    width = pieces[0].shape[2]
    any_spec = pl.BlockSpec(memory_space=pl.ANY)
    return pl.pallas_call(
        halo_kernel,
        out_shape=jax.ShapeDtypeStruct((2, 4, 128, width), jnp.bfloat16),
        in_specs=[any_spec] * 4,
        out_specs=any_spec,
        scratch_shapes=[pltpu.SemaphoreType.DMA((8,))],
        cost_estimate=pl.CostEstimate(flops=0, bytes_accessed=16 * 128 * width * 2, transcendentals=0),
        name="halo_pack",
    )(*pieces)


def attend_kernel(p0, p1, p2, p3, halo, kf, qf, alive, o0, o1, o2, o3, kaug, vaug, qaug):
    pieces, outs = (p0, p1, p2, p3), (o0, o1, o2, o3)

    @pl.when(pl.program_id(0) == 0)
    def _():
        kaug[:, HS:] = kf[...]
        qaug[:, HS:] = qf[...]
        vaug[:, HS:] = jnp.ones((1024, HS), jnp.bfloat16)

    for n, piece in enumerate(pieces):
        rows = pl.ds(n * 128, 128)
        qaug[rows, :HS] = piece[0]
        kaug[rows, :HS] = piece[1]
        vaug[rows, :HS] = piece[2]
        rows = pl.ds(512 + n * 128, 128)
        kaug[rows, :HS] = halo[0, n]
        vaug[rows, :HS] = halo[1, n]
    scale = math.log2(math.e) / math.sqrt(HS)
    for part in range(2):
        rows = pl.ds(part * 256, 256)
        scores = lax.dot_general(
            qaug[rows, :], kaug[...], (((1,), (1,)), ((), ())), preferred_element_type=jnp.float32
        )
        top = jnp.max(scores, axis=1, keepdims=True)
        weights = jnp.exp2((scores - top) * scale).astype(jnp.bfloat16)
        mixed = jnp.dot(weights, vaug[...], preferred_element_type=jnp.float32)
        result = (mixed[:, :HS] / mixed[:, HS:] * alive[rows, :]).astype(jnp.bfloat16)
        outs[2 * part][...] = result[:128]
        outs[2 * part + 1][...] = result[128:]


def attend(pieces, halo, kf, qf, alive):
    width = pieces[0].shape[2]
    heads = width // HS
    out = jax.ShapeDtypeStruct((128, width), jnp.bfloat16)
    return pl.pallas_call(
        attend_kernel,
        grid=(heads,),
        out_shape=[out] * 4,
        in_specs=[pl.BlockSpec((3, 128, HS), lambda h: (0, 0, h))] * 4
        + [
            pl.BlockSpec((2, 4, 128, HS), lambda h: (0, 0, 0, h)),
            pl.BlockSpec((1024, HS), lambda h: (0, 0)),
            pl.BlockSpec((512, HS), lambda h: (0, 0)),
            pl.BlockSpec((512, HS), lambda h: (0, 0)),
        ],
        out_specs=[pl.BlockSpec((128, HS), lambda h: (0, h))] * 4,
        scratch_shapes=[
            pltpu.VMEM((1024, 2 * HS), jnp.bfloat16),
            pltpu.VMEM((1024, 2 * HS), jnp.bfloat16),
            pltpu.VMEM((512, 2 * HS), jnp.bfloat16),
        ],
        compiler_params=pltpu.CompilerParams(vmem_limit_bytes=VMEM),
        cost_estimate=pl.CostEstimate(
            flops=heads * 4 * 512 * 1024 * 256, bytes_accessed=heads * 20 * 128 * 256, transcendentals=heads * 512 * 1024
        ),
        name="attend",
    )(*pieces, halo, kf, qf, alive)


def project_kernel(groups, signs, places, *refs):
    count = 8 * len(groups)
    attended, w_ref, tokens, out, lhs = refs[:count], refs[count], refs[count + 1], refs[count + 2], refs[count + 3]

    @pl.when(pl.program_id(0) == 0)
    def _():
        for half in range(2):
            s = signs[half]
            for piece, (a, b) in enumerate(MOVES):
                i = s + a * (1 - 2 * s)
                j = s + b * (1 - 2 * s)
                for g, (first, heads) in enumerate(groups):
                    lanes = pl.ds(first * HS, heads * HS)
                    lhs[half * 4 + i * 2 + j, :, lanes] = attended[g * 8 + half * 4 + piece][...]

    total = lax.dot_general(
        lhs[...].reshape(1024, HD), w_ref[...], (((1,), (1,)), ((), ())), preferred_element_type=jnp.float32
    ).reshape(2, 2, 2, 2, 8, 8, TILE)
    for half in range(2):
        for i in range(2):
            block = jnp.concatenate([total[half, i, 0], total[half, i, 1]], axis=2)
            at = (slice(2 * half, 2 * half + 2), slice(8 * i, 8 * i + 8))
            out[at] = (block + tokens[at].astype(jnp.float32)).astype(jnp.bfloat16)


def project(groups, attended, signs, places, w, tokens):
    whole = [pl.BlockSpec((128, heads * HS), lambda t, s, p: (0, 0)) for _, heads in groups for _ in range(8)]
    grid_spec = pltpu.PrefetchScalarGridSpec(
        num_scalar_prefetch=2,
        grid=(D // TILE,),
        in_specs=whole
        + [
            pl.BlockSpec((TILE, HD), lambda t, s, p: (t, 0)),
            pl.BlockSpec((4, 16, 16, TILE), lambda t, s, p: (0, 0, 0, p[t])),
        ],
        out_specs=pl.BlockSpec((4, 16, 16, TILE), lambda t, s, p: (0, 0, 0, p[t])),
        scratch_shapes=[pltpu.VMEM((8, 128, HD), jnp.bfloat16)],
    )
    return pl.pallas_call(
        functools.partial(project_kernel, groups),
        grid_spec=grid_spec,
        out_shape=jax.ShapeDtypeStruct((4, 16, 16, D), jnp.bfloat16),
        compiler_params=pltpu.CompilerParams(vmem_limit_bytes=VMEM),
        cost_estimate=pl.CostEstimate(flops=2 * 1024 * HD * D, bytes_accessed=25 * 2**20, transcendentals=0),
        name="project",
    )(signs, places, *attended, w, tokens)


def ring_order(own, first, second, third, place):
    row = jnp.stack([third, second, first, own, third, second, first])
    return lax.dynamic_slice_in_dim(row, 3 - place, 4, axis=0).reshape((-1,) + own.shape[1:])


def gather_weight(out_weight):
    f, r, c = (lax.axis_index(a) for a in AXES)
    core, x, z = f % 2, r % 4, (f // 2) * 2 + r // 4
    mine = out_weight.T
    mine = ring_order(mine, *(send(mine, plane_pairs(0, d)) for d in (1, 2, 3)), c)
    mine = ring_order(mine, *(send(mine, plane_pairs(d, 0)) for d in (1, 2, 3)), x)
    chunks = [mine]
    for _ in range(3):
        chunks.append(send(chunks[-1], depth_pairs()))
    others = [send(chunk, core_pairs()) for chunk in chunks]
    places = []
    for k in (core, 1 - core):
        for n in range(4):
            at = (z + n * (2 * k - 1) + 4) % 4
            places.append(((at // 2) * 2 + k) * 2 + at % 2)
    return jnp.concatenate(chunks + others), jnp.stack(places).astype(jnp.int32)


def masks(half, sign, row_valid):
    f, r, c = (lax.axis_index(a) for a in AXES)
    valid = row_valid.reshape(16, 8)
    stay = 2 * r + sign
    moved = (stay + 2 * sign - 1 + 16) % 16
    pick = lambda at: lax.dynamic_index_in_dim(valid, at, 0, keepdims=False)
    live = jnp.stack([pick(stay), pick(moved)])
    xbit = jnp.array([0, 1, 0, 1], jnp.int32)
    ybit = jnp.array([0, 0, 1, 1], jnp.int32)
    live = jnp.concatenate([live, live])
    live = jnp.broadcast_to(live[:, None, :, None], (4, 2, 8, 8)).reshape(512, 1)
    row_split = jnp.where(sign == 0, r == 0, r == R - 1)
    col_split = jnp.where(sign == 0, c == 0, c == C - 1)
    apart = (row_split & (xbit[:, None] != xbit[None, :])) | (col_split & (ybit[:, None] != ybit[None, :]))
    missing = (f == 0) if half == 0 else (f == F - 1)
    lane = jnp.arange(HS, dtype=jnp.int32)[None, :]
    piece = (jnp.arange(512, dtype=jnp.int32) // 128)[:, None]
    dead = (lane == 4) & (live == 0)
    own = (lane == piece) | dead
    kf = jnp.concatenate([own, own | (lane == 5)]).astype(jnp.bfloat16)
    apart = jnp.pad(apart, ((0, 0), (0, HS - 4)))
    apart = jnp.broadcast_to(apart[:, None, :], (4, 128, HS)).reshape(512, HS)
    qf = jnp.where(apart | (lane == 4) | ((lane == 5) & missing), -BIG, 0.0).astype(jnp.bfloat16)
    alive = jnp.broadcast_to(live, (512, HS)).astype(jnp.float32)
    return kf, qf, alive


def local(tokens_in, queries, key_rows, value_rows, out_weight, row_valid):
    f = lax.axis_index("frame")
    signs = jnp.stack([f % 2, 1 - f % 2]).astype(jnp.int32)
    split = lambda a: a.reshape(4, 2, 8, 2, 8, HD)
    q, k, v = split(queries), split(key_rows), split(value_rows)
    weight, places = gather_weight(out_weight)
    features = [masks(half, signs[half], row_valid) for half in range(2)]
    attended = []
    for first, heads in GROUPS:
        windows = []
        for half in range(2):
            packed = pack(half, first, heads, signs[half : half + 1], q, k, v)
            windows.append(
                [packed[0]] + [send(packed[n], window_pairs(half, *MOVES[n])) for n in (1, 2, 3)]
            )
        kv = [halo_pack(pieces) for pieces in windows]
        halos = [send(kv[1], frame_pairs(1)), send(kv[0], frame_pairs(-1))]
        for half in range(2):
            mixed = attend(windows[half], halos[half], *features[half])
            attended += [mixed[0]] + [send(mixed[n], window_pairs(half, *MOVES[n], back=True)) for n in (1, 2, 3)]
    return project(GROUPS, attended, signs, places, weight, tokens_in)


def solution(mesh):
    return jax.shard_map(
        local,
        mesh=mesh,
        in_specs=(
            P("frame", "row", "col", None),
            P("frame", "row", "col", None),
            P("frame", "row", "col", None),
            P("frame", "row", "col", None),
            P(None, ("frame", "row", "col")),
            P(),
        ),
        out_specs=P("frame", "row", "col", None),
        check_vma=False,
    )
```

time: 552 us -> 679 us (1.23); the launches traced: 542 us -> 678 us
  Pallas kernels: 0 us -> 544 us
  waiting for transfers between devices: 364 us -> 36.6 us
  matrix products: 61 us -> 0 us
  starting transfers between devices: 35.6 us -> 63.3 us
  local copies, waits for them, and re-layouts: 44.6 us -> 22.3 us
  between operations: 13.5 us -> 0.94 us
  other arithmetic: 23.1 us -> 10.8 us
    pallas_call x0 -> x13, Pallas kernels: none -> 544 us  [the longest x4 291 us: pack(): pl.pallas_call(functools.partial(pack_kernel, half, first * HS, width), o...]
    ppermute x6 -> x41, waiting for transfers between devices: 342 us -> 36.6 us  [send(): return lax.ppermute(value, AXES, pairs)]
    dot_general x2 -> x0, matrix products: 35.4 us -> none  [the longest x1 19.5 us: attend_window(): jnp.einsum('hqk,khd->qhd', weights, value_heads, preferred_element_type=j...]
    ppermute x6 -> x41, starting transfers between devices: 35.6 us -> 63.3 us  [send(): return lax.ppermute(value, AXES, pairs)]
    sub x1 -> x0, matrix products: 25.6 us -> none  [attend_window(): exponent = jnp.exp(scores - row_max)]
    all_gather x1 -> x0, waiting for transfers between devices: 22.1 us -> none  [local(): lax.all_gather(out_weight, ('frame', 'row', 'col'), axis=1, tiled=True)]
    reshape x3 -> x1, local copies, waits for them, and re-layouts: 17.4 us -> 0.08 us  [masks(): valid = row_valid.reshape(16, 8)]
    slice x3 -> x0, local copies, waits for them, and re-layouts: 13.3 us -> none  [the longest x2 13.1 us: roll_block(): lax.slice_in_dim(field_block, extent - half_width, extent, axis=axis_dim)]
  transfers between devices with their start and end apart: 7 -> 41, of which waited for: 7 -> 8; matrix products, arithmetic and copies ran while one was open for 16% -> 5% of each run, Pallas kernels for 0% -> 77%
where the time goes in v1:
time: 679 us; the launch traced here: 678 us
  Pallas kernels  544 us (80%)
  starting transfers between devices  63.3 us (9%)
  waiting for transfers between devices  36.6 us (5%)
  local copies, waits for them, and re-layouts  22.3 us (3%)
  other arithmetic  10.8 us (2%)
    pallas_call x4, Pallas kernels, pack(): pl.pallas_call(functools.partial(pack_kernel, half, first * HS, width), o...  291 us
    pallas_call x4, Pallas kernels, halo_pack(): pl.pallas_call(halo_kernel, out_shape=jax.ShapeDtypeStruct((2, 4, 128, wi...  195 us
    ppermute x41, starting transfers between devices, send(): return lax.ppermute(value, AXES, pairs)  63.3 us
    pallas_call x4, Pallas kernels, attend(): pl.pallas_call(attend_kernel, grid=(heads,), out_shape=[out] * 4, in_spec...  38.2 us
    ppermute x41, waiting for transfers between devices, send(): return lax.ppermute(value, AXES, pairs)  36.6 us
    pallas_call x1, Pallas kernels, project(): pl.pallas_call(functools.partial(project_kernel, groups), grid_spec=grid_...  19.4 us
  transfers between devices with their start and end apart: 41, of which 8 were waited for; matrix products, arithmetic and copies ran while one was open for 5% of the time, Pallas kernels for 77%

profile of v1, /device:TPU:1, one launch (start us, length us, event | category | flops | bytes accessed | tf_op | source)
XLA Modules:
  0.0 677.9 jit_solution(9481346312150400801)
XLA Ops:
  0.0 3.6 collective-permute-start.28
  5.3 3.3 collective-permute-done.29
  10.7 2.5 collective-permute-start.31
  13.2 72.8 %pack_0_6.1 = (bf16[3,2,8,8,768]{4,3,2,1,0:T(8,128)(2,1)}, bf16[3,2,8,8,768]{4,3,2,1,0:T(8,128)(2,1)}, bf16[3,2,8,8,768]{4,3,2,1,0:T(8,128)(2,1)}, bf16[3,2,8,8,768]{4,3,2,1,0:T(8,128)(2,1)}) custom-call(s32[1]{0:T(128)} %bitcast.sign_ref, bf16[4,2,8,2,8,1536]{5,4,3,2,1,0:T(8,128)(2,1)} %bitcast.76, bf16[4,2,8,2,8,1536]{5,4,3,2,1,0:T(8,128)(2,1)} %bitcast.80, ...), custom_call_target="tpu_custom_call" | custom-call | bytes 4718592 | tf_op jit(solution)/shard_map/pack_0_6/pallas_call | solution.py:99
  86.0 2.0 collective-permute-start.14
  89.3 72.8 %pack_1_6.1 = (bf16[3,2,8,8,768]{4,3,2,1,0:T(8,128)(2,1)}, bf16[3,2,8,8,768]{4,3,2,1,0:T(8,128)(2,1)}, bf16[3,2,8,8,768]{4,3,2,1,0:T(8,128)(2,1)}, bf16[3,2,8,8,768]{4,3,2,1,0:T(8,128)(2,1)}) custom-call(s32[1]{0:T(128)} %bitcast.1.sign_ref, bf16[4,2,8,2,8,1536]{5,4,3,2,1,0:T(8,128)(2,1)} %bitcast.77, bf16[4,2,8,2,8,1536]{5,4,3,2,1,0:T(8,128)(2,1)} %bitcast.81, ...), custom_call_target="tpu_custom_call" | custom-call | bytes 4718592 | tf_op jit(solution)/shard_map/pack_1_6/pallas_call | solution.py:99
  163.4 13.8 %collective-permute-done.32 = bf16[96,1536]{1,0:T(8,128)(2,1)S(1)} collective-permute-done((bf16[96,1536]{1,0:T(8,128)(2,1)S(1)}, bf16[96,1536]{1,0:T(8,128)(2,1)S(1)}, u32[]{:S(2)}, u32[]{:S(2)}) %collective-permute-start.32) | collective-permute-done | bytes 294944 | tf_op jit(solution)/shard_map/ppermute | solution.py:67
  177.2 8.6 %collective-permute-done.33 = bf16[96,1536]{1,0:T(8,128)(2,1)S(1)} collective-permute-done((bf16[96,1536]{1,0:T(8,128)(2,1)S(1)}, bf16[96,1536]{1,0:T(8,128)(2,1)S(1)}, u32[]{:S(2)}, u32[]{:S(2)}) %collective-permute-start.33) | collective-permute-done | bytes 294944 | tf_op jit(solution)/shard_map/ppermute | solution.py:67
  186.4 3.7 collective-permute-start.34
  190.1 72.8 %pack_0_0.1 = (bf16[3,2,8,8,768]{4,3,2,1,0:T(8,128)(2,1)}, bf16[3,2,8,8,768]{4,3,2,1,0:T(8,128)(2,1)}, bf16[3,2,8,8,768]{4,3,2,1,0:T(8,128)(2,1)}, bf16[3,2,8,8,768]{4,3,2,1,0:T(8,128)(2,1)}) custom-call(s32[1]{0:T(128)} %bitcast.sign_ref, bf16[4,2,8,2,8,1536]{5,4,3,2,1,0:T(8,128)(2,1)} %bitcast.78, bf16[4,2,8,2,8,1536]{5,4,3,2,1,0:T(8,128)(2,1)} %bitcast.82, ...), custom_call_target="tpu_custom_call" | custom-call | bytes 4718592 | tf_op jit(solution)/shard_map/pack_0_0/pallas_call | solution.py:99
  264.1 2.7 collective-permute-start.1
  267.9 72.8 %pack_1_0.1 = (bf16[3,2,8,8,768]{4,3,2,1,0:T(8,128)(2,1)}, bf16[3,2,8,8,768]{4,3,2,1,0:T(8,128)(2,1)}, bf16[3,2,8,8,768]{4,3,2,1,0:T(8,128)(2,1)}, bf16[3,2,8,8,768]{4,3,2,1,0:T(8,128)(2,1)}) custom-call(s32[1]{0:T(128)} %bitcast.1.sign_ref, bf16[4,2,8,2,8,1536]{5,4,3,2,1,0:T(8,128)(2,1)} %bitcast.79, bf16[4,2,8,2,8,1536]{5,4,3,2,1,0:T(8,128)(2,1)} %bitcast.83, ...), custom_call_target="tpu_custom_call" | custom-call | bytes 4718592 | tf_op jit(solution)/shard_map/pack_1_0/pallas_call | solution.py:99
  345.8 48.8 %halo_pack.7 = bf16[2,4,128,768]{3,2,1,0:T(8,128)(2,1)} custom-call(bf16[3,128,768]{2,1,0:T(8,128)(2,1)} %bitcast.95, bf16[3,128,768]{2,1,0:T(8,128)(2,1)} %copy-done, bf16[3,128,768]{2,1,0:T(8,128)(2,1)} %copy-done.1, bf16[3,128,768]{2,1,0:T(8,128)(2,1)} %collective-permute-done.16.p3.refs_3_), custom_call_target="tpu_custom_call" | custom-call | bytes 3145728 | tf_op jit(solution)/shard_map/halo_pack/pallas_call | solution.py:126
  394.7 8.4 %collective-permute-start.24 = (bf16[2,4,128,768]{3,2,1,0:T(8,128)(2,1)}, bf16[2,4,128,768]{3,2,1,0:T(8,128)(2,1)}, u32[]{:S(2)}, u32[]{:S(2)}) collective-permute-start(bf16[2,4,128,768]{3,2,1,0:T(8,128)(2,1)} %halo_pack.7), channel_id=1, source_target_pairs={{32,0},{33,1},{34,2},{35,3},{36,4},{37,5},{38,6},{39,7},{40,8},{41... | collective-permute-start | bytes 4718600 | tf_op jit(solution)/shard_map/ppermute | solution.py:67
  404.8 48.8 %halo_pack.5 = bf16[2,4,128,768]{3,2,1,0:T(8,128)(2,1)} custom-call(bf16[3,128,768]{2,1,0:T(8,128)(2,1)} %bitcast.99, bf16[3,128,768]{2,1,0:T(8,128)(2,1)} %copy-done.2, bf16[3,128,768]{2,1,0:T(8,128)(2,1)} %copy-done.3, bf16[3,128,768]{2,1,0:T(8,128)(2,1)} %collective-permute-done.2.p3.refs_3_), custom_call_target="tpu_custom_call" | custom-call | bytes 3145728 | tf_op jit(solution)/shard_map/halo_pack/pallas_call | solution.py:126
  456.4 4.5 collective-permute-start.35
  463.2 48.8 %halo_pack.6 = bf16[2,4,128,768]{3,2,1,0:T(8,128)(2,1)} custom-call(bf16[3,128,768]{2,1,0:T(8,128)(2,1)} %bitcast.97, bf16[3,128,768]{2,1,0:T(8,128)(2,1)} %collective-permute-done.17.refs_1_.p1, bf16[3,128,768]{2,1,0:T(8,128)(2,1)} %collective-permute-done.18.refs_2_.p2, bf16[3,128,768]{2,1,0:T(8,128)(2,1)} %collective-permute-done.19.refs_3_.p3), custom_call_target="tpu_custom_call" | custom-call | bytes 3145728 | tf_op jit(solution)/shard_map/halo_pack/pallas_call | solution.py:126
  512.0 4.7 collective-permute-start.20
  518.1 48.8 %halo_pack.4 = bf16[2,4,128,768]{3,2,1,0:T(8,128)(2,1)} custom-call(bf16[3,128,768]{2,1,0:T(8,128)(2,1)} %bitcast.101, bf16[3,128,768]{2,1,0:T(8,128)(2,1)} %collective-permute-done.3.refs_1_.p1, bf16[3,128,768]{2,1,0:T(8,128)(2,1)} %collective-permute-done.4.refs_2_.p2, bf16[3,128,768]{2,1,0:T(8,128)(2,1)} %collective-permute-done.5.refs_3_.p3), custom_call_target="tpu_custom_call" | custom-call | bytes 3145728 | tf_op jit(solution)/shard_map/halo_pack/pallas_call | solution.py:126
  567.0 1.9 collective-permute-start.6
  583.6 9.5 %attend.7 = (bf16[128,768]{1,0:T(8,128)(2,1)}, bf16[128,768]{1,0:T(8,128)(2,1)}, bf16[128,768]{1,0:T(8,128)(2,1)}, bf16[128,768]{1,0:T(8,128)(2,1)}) custom-call(bf16[3,128,768]{2,1,0:T(8,128)(2,1)} %bitcast.98, bf16[3,128,768]{2,1,0:T(8,128)(2,1)} %collective-permute-done.17.refs_1_.p1, bf16[3,128,768]{2,1,0:T(8,128)(2,1)} %collective-permute-done.18.refs_2_.p2, ...), custom_call_target="tpu_custom_call" | custom-call | flops 3221225472 | bytes 3932160 | tf_op jit(solution)/shard_map/attend/pallas_call | solution.py:172
  593.5 9.5 %attend.5 = (bf16[128,768]{1,0:T(8,128)(2,1)}, bf16[128,768]{1,0:T(8,128)(2,1)}, bf16[128,768]{1,0:T(8,128)(2,1)}, bf16[128,768]{1,0:T(8,128)(2,1)}) custom-call(bf16[3,128,768]{2,1,0:T(8,128)(2,1)} %bitcast.102, bf16[3,128,768]{2,1,0:T(8,128)(2,1)} %collective-permute-done.3.refs_1_.p1, bf16[3,128,768]{2,1,0:T(8,128)(2,1)} %collective-permute-done.4.refs_2_.p2, ...), custom_call_target="tpu_custom_call" | custom-call | flops 3221225472 | bytes 3932160 | tf_op jit(solution)/shard_map/attend/pallas_call | solution.py:172
  604.0 9.5 %attend.6 = (bf16[128,768]{1,0:T(8,128)(2,1)}, bf16[128,768]{1,0:T(8,128)(2,1)}, bf16[128,768]{1,0:T(8,128)(2,1)}, bf16[128,768]{1,0:T(8,128)(2,1)}) custom-call(bf16[3,128,768]{2,1,0:T(8,128)(2,1)} %bitcast.96, bf16[3,128,768]{2,1,0:T(8,128)(2,1)} %copy-done, bf16[3,128,768]{2,1,0:T(8,128)(2,1)} %copy-done.1, ...), custom_call_target="tpu_custom_call" | custom-call | flops 3221225472 | bytes 3932160 | tf_op jit(solution)/shard_map/attend/pallas_call | solution.py:172
  614.0 9.5 %attend.4 = (bf16[128,768]{1,0:T(8,128)(2,1)}, bf16[128,768]{1,0:T(8,128)(2,1)}, bf16[128,768]{1,0:T(8,128)(2,1)}, bf16[128,768]{1,0:T(8,128)(2,1)}) custom-call(bf16[3,128,768]{2,1,0:T(8,128)(2,1)} %bitcast.100, bf16[3,128,768]{2,1,0:T(8,128)(2,1)} %copy-done.2, bf16[3,128,768]{2,1,0:T(8,128)(2,1)} %copy-done.3, ...), custom_call_target="tpu_custom_call" | custom-call | flops 3221225472 | bytes 3932160 | tf_op jit(solution)/shard_map/attend/pallas_call | solution.py:172
  627.3 3.2 collective-permute-start.27
  633.5 1.9 collective-permute-start.23
  635.4 4.3 collective-permute-start.11
  639.7 2.5 constant_dynamic-update-slice_fusion.1
  642.3 3.6 collective-permute-start.13
  649.6 5.5 collective-permute-done.7.refs_1_
  655.1 2.6 collective-permute-done.9.refs_3_
  658.5 19.4 %project.1 = bf16[4,16,16,3072]{3,2,1,0:T(8,128)(2,1)} custom-call(s32[2]{0:T(128)} %pad_add_fusion.2.signs, s32[8]{0:T(128)} %stack.86.places, bf16[128,768]{1,0:T(8,128)(2,1)} %get-tuple-element.45.refs_0_, bf16[128,768]{1,0:T(8,128)(2,1)} %copy-done.34, bf16[128,768]{1,0:T(8,128)(2,1)} %copy-done.35, bf16[128,768]{1,0:T(8,128)(2,1)} %copy-done.36, ...), custom_call_target="tpu_custom_call" | custom-call | flops 9663676416 | bytes 26214400 | tf_op jit(solution)/shard_map/project/pallas_call | solution.py:235
  (187 shorter events, 49.7 us)
Async XLA Ops:
  10.7 152.7 %collective-permute-start.31 = (bf16[96,1536]{1,0:T(8,128)(2,1)S(1)}, bf16[96,1536]{1,0:T(8,128)(2,1)S(1)}, u32[]{:S(2)}, u32[]{:S(2)}) collective-permute-start(bf16[96,1536]{1,0:T(8,128)(2,1)S(1)} %bitcast.91), channel_id=1, source_target_pairs={{0,12},{1,13},{2,14},{3,15},{4,0},{5,1},{6,2},{7,3},{8,4},{9,5},{1... | collective-permute-start | bytes 884744 | tf_op jit(solution)/shard_map/ppermute | solution.py:67
  86.0 100.0 %collective-permute-start.14 = (bf16[3,128,768]{2,1,0:T(8,128)(2,1)}, bf16[3,128,768]{2,1,0:T(8,128)(2,1)S(1)}, u32[]{:S(2)}, u32[]{:S(2)}) collective-permute-start(bf16[3,128,768]{2,1,0:T(8,128)(2,1)} %bitcast.116), channel_id=1, source_target_pairs={{0,4},{1,5},{2,6},{3,7},{4,8},{5,9},{6,10},{7,11},{8,12},{9,13},{1... | collective-permute-start | bytes 1769480 | tf_op jit(solution)/shard_map/ppermute | solution.py:67
  88.0 98.4 %collective-permute-start.15 = (bf16[3,128,768]{2,1,0:T(8,128)(2,1)}, bf16[3,128,768]{2,1,0:T(8,128)(2,1)S(1)}, u32[]{:S(2)}, u32[]{:S(2)}) collective-permute-start(bf16[3,128,768]{2,1,0:T(8,128)(2,1)} %bitcast.115), channel_id=1, source_target_pairs={{0,1},{1,2},{2,3},{3,0},{4,5},{5,6},{6,7},{7,4},{8,9},{9,10},{10,1... | collective-permute-start | bytes 1769480 | tf_op jit(solution)/shard_map/ppermute | solution.py:67
  88.2 174.6 %collective-permute-start.16 = (bf16[3,128,768]{2,1,0:T(8,128)(2,1)}, bf16[3,128,768]{2,1,0:T(8,128)(2,1)}, u32[]{:S(2)}, u32[]{:S(2)}) collective-permute-start(bf16[3,128,768]{2,1,0:T(8,128)(2,1)} %bitcast.112), channel_id=1, source_target_pairs={{0,5},{1,6},{2,7},{3,4},{4,9},{5,10},{6,11},{7,8},{8,13},{9,14},{1... | collective-permute-start | bytes 1769480 | tf_op jit(solution)/shard_map/ppermute | solution.py:67
  162.1 102.1 %collective-permute-start.17 = (bf16[3,128,768]{2,1,0:T(8,128)(2,1)}, bf16[3,128,768]{2,1,0:T(8,128)(2,1)}, u32[]{:S(2)}, u32[]{:S(2)}) collective-permute-start(bf16[3,128,768]{2,1,0:T(8,128)(2,1)} %bitcast.114), channel_id=1, source_target_pairs={{0,28},{1,29},{2,30},{3,31},{4,0},{5,1},{6,2},{7,3},{8,4},{9,5},{1... | collective-permute-start | bytes 1769480 | tf_op jit(solution)/shard_map/ppermute | solution.py:67
  163.4 13.8 %collective-permute-start.32 = (bf16[96,1536]{1,0:T(8,128)(2,1)S(1)}, bf16[96,1536]{1,0:T(8,128)(2,1)S(1)}, u32[]{:S(2)}, u32[]{:S(2)}) collective-permute-start(bf16[96,1536]{1,0:T(8,128)(2,1)S(1)} %bitcast.92), channel_id=1, source_target_pairs={{0,8},{1,9},{2,10},{3,11},{4,12},{5,13},{6,14},{7,15},{8,0},{9,1},... | collective-permute-start | bytes 884744 | tf_op jit(solution)/shard_map/ppermute | solution.py:67
  185.8 81.0 %collective-permute-start.18 = (bf16[3,128,768]{2,1,0:T(8,128)(2,1)}, bf16[3,128,768]{2,1,0:T(8,128)(2,1)}, u32[]{:S(2)}, u32[]{:S(2)}) collective-permute-start(bf16[3,128,768]{2,1,0:T(8,128)(2,1)} %bitcast.113), channel_id=1, source_target_pairs={{0,3},{1,0},{2,1},{3,2},{4,7},{5,4},{6,5},{7,6},{8,11},{9,8},{10,9... | collective-permute-start | bytes 1769480 | tf_op jit(solution)/shard_map/ppermute | solution.py:67
  186.1 154.7 %collective-permute-start.19 = (bf16[3,128,768]{2,1,0:T(8,128)(2,1)}, bf16[3,128,768]{2,1,0:T(8,128)(2,1)}, u32[]{:S(2)}, u32[]{:S(2)}) collective-permute-start(bf16[3,128,768]{2,1,0:T(8,128)(2,1)} %bitcast.30), channel_id=1, source_target_pairs={{0,31},{1,28},{2,29},{3,30},{4,3},{5,0},{6,1},{7,2},{8,7},{9,4},{1... | collective-permute-start | bytes 1769480 | tf_op jit(solution)/shard_map/ppermute | solution.py:67
  186.4 270.0 %collective-permute-start.34 = (bf16[384,1536]{1,0:T(8,128)(2,1)S(1)}, bf16[384,1536]{1,0:T(8,128)(2,1)S(1)}, u32[]{:S(2)}, u32[]{:S(2)}) collective-permute-start(bf16[384,1536]{1,0:T(8,128)(2,1)S(1)} %bitcast.88), channel_id=1, source_target_pairs={{0,16},{1,17},{2,18},{3,19},{4,20},{5,21},{6,22},{7,23},{8,24},{9,... | collective-permute-start | bytes 3538952 | tf_op jit(solution)/shard_map/ppermute | solution.py:67
  262.9 80.0 %collective-permute-start = (bf16[3,128,768]{2,1,0:T(8,128)(2,1)}, bf16[3,128,768]{2,1,0:T(8,128)(2,1)S(1)}, u32[]{:S(2)}, u32[]{:S(2)}) collective-permute-start(bf16[3,128,768]{2,1,0:T(8,128)(2,1)} %bitcast.111), channel_id=1, source_target_pairs={{0,4},{1,5},{2,6},{3,7},{4,8},{5,9},{6,10},{7,11},{8,12},{9,13},{1... | collective-permute-start | bytes 1769480 | tf_op jit(solution)/shard_map/ppermute | solution.py:67
  264.1 130.5 %collective-permute-start.1 = (bf16[3,128,768]{2,1,0:T(8,128)(2,1)}, bf16[3,128,768]{2,1,0:T(8,128)(2,1)S(1)}, u32[]{:S(2)}, u32[]{:S(2)}) collective-permute-start(bf16[3,128,768]{2,1,0:T(8,128)(2,1)} %bitcast.109), channel_id=1, source_target_pairs={{0,1},{1,2},{2,3},{3,0},{4,5},{5,6},{6,7},{7,4},{8,9},{9,10},{10,1... | collective-permute-start | bytes 1769480 | tf_op jit(solution)/shard_map/ppermute | solution.py:67
  266.8 127.9 %collective-permute-start.2 = (bf16[3,128,768]{2,1,0:T(8,128)(2,1)}, bf16[3,128,768]{2,1,0:T(8,128)(2,1)}, u32[]{:S(2)}, u32[]{:S(2)}) collective-permute-start(bf16[3,128,768]{2,1,0:T(8,128)(2,1)} %bitcast.108), channel_id=1, source_target_pairs={{0,5},{1,6},{2,7},{3,4},{4,9},{5,10},{6,11},{7,8},{8,13},{9,14},{1... | collective-permute-start | bytes 1769480 | tf_op jit(solution)/shard_map/ppermute | solution.py:67
  340.7 112.9 %collective-permute-start.3 = (bf16[3,128,768]{2,1,0:T(8,128)(2,1)}, bf16[3,128,768]{2,1,0:T(8,128)(2,1)}, u32[]{:S(2)}, u32[]{:S(2)}) collective-permute-start(bf16[3,128,768]{2,1,0:T(8,128)(2,1)} %bitcast.110), channel_id=1, source_target_pairs={{0,28},{1,29},{2,30},{3,31},{4,0},{5,1},{6,2},{7,3},{8,4},{9,5},{1... | collective-permute-start | bytes 1769480 | tf_op jit(solution)/shard_map/ppermute | solution.py:67
  342.9 169.1 %collective-permute-start.4 = (bf16[3,128,768]{2,1,0:T(8,128)(2,1)}, bf16[3,128,768]{2,1,0:T(8,128)(2,1)}, u32[]{:S(2)}, u32[]{:S(2)}) collective-permute-start(bf16[3,128,768]{2,1,0:T(8,128)(2,1)} %bitcast.107), channel_id=1, source_target_pairs={{0,3},{1,0},{2,1},{3,2},{4,7},{5,4},{6,5},{7,6},{8,11},{9,8},{10,9... | collective-permute-start | bytes 1769480 | tf_op jit(solution)/shard_map/ppermute | solution.py:67
  394.6 123.5 %collective-permute-start.5 = (bf16[3,128,768]{2,1,0:T(8,128)(2,1)}, bf16[3,128,768]{2,1,0:T(8,128)(2,1)}, u32[]{:S(2)}, u32[]{:S(2)}) collective-permute-start(bf16[3,128,768]{2,1,0:T(8,128)(2,1)} %bitcast.106), channel_id=1, source_target_pairs={{0,31},{1,28},{2,29},{3,30},{4,3},{5,0},{6,1},{7,2},{8,7},{9,4},{1... | collective-permute-start | bytes 1769480 | tf_op jit(solution)/shard_map/ppermute | solution.py:67
  394.7 186.4 %collective-permute-start.24 = (bf16[2,4,128,768]{3,2,1,0:T(8,128)(2,1)}, bf16[2,4,128,768]{3,2,1,0:T(8,128)(2,1)}, u32[]{:S(2)}, u32[]{:S(2)}) collective-permute-start(bf16[2,4,128,768]{3,2,1,0:T(8,128)(2,1)} %halo_pack.7), channel_id=1, source_target_pairs={{32,0},{33,1},{34,2},{35,3},{36,4},{37,5},{38,6},{39,7},{40,8},{41... | collective-permute-start | bytes 4718600 | tf_op jit(solution)/shard_map/ppermute | solution.py:67
  453.6 139.6 %collective-permute-start.10 = (bf16[2,4,128,768]{3,2,1,0:T(8,128)(2,1)}, bf16[2,4,128,768]{3,2,1,0:T(8,128)(2,1)}, u32[]{:S(2)}, u32[]{:S(2)}) collective-permute-start(bf16[2,4,128,768]{3,2,1,0:T(8,128)(2,1)} %halo_pack.5), channel_id=1, source_target_pairs={{32,0},{33,1},{34,2},{35,3},{36,4},{37,5},{38,6},{39,7},{40,8},{41... | collective-permute-start | bytes 4718600 | tf_op jit(solution)/shard_map/ppermute | solution.py:67
  456.4 126.4 %collective-permute-start.35 = (bf16[384,1536]{1,0:T(8,128)(2,1)S(1)}, bf16[384,1536]{1,0:T(8,128)(2,1)S(1)}, u32[]{:S(2)}, u32[]{:S(2)}) collective-permute-start(bf16[384,1536]{1,0:T(8,128)(2,1)S(1)} %collective-permute-done.34), channel_id=1, source_target_pairs={{0,16},{1,17},{2,18},{3,19},{4,20},{5,21},{6,22},{7,23},{8,24},{9,... | collective-permute-start | bytes 3538952 | tf_op jit(solution)/shard_map/ppermute | solution.py:67
  512.0 91.1 %collective-permute-start.20 = (bf16[2,4,128,768]{3,2,1,0:T(8,128)(2,1)}, bf16[2,4,128,768]{3,2,1,0:T(8,128)(2,1)}, u32[]{:S(2)}, u32[]{:S(2)}) collective-permute-start(bf16[2,4,128,768]{3,2,1,0:T(8,128)(2,1)} %halo_pack.6), channel_id=1, source_target_pairs={{0,32},{1,33},{2,34},{3,35},{4,36},{5,37},{6,38},{7,39},{8,40},{9,... | collective-permute-start | bytes 4718600 | tf_op jit(solution)/shard_map/ppermute | solution.py:67
  567.0 46.6 %collective-permute-start.6 = (bf16[2,4,128,768]{3,2,1,0:T(8,128)(2,1)}, bf16[2,4,128,768]{3,2,1,0:T(8,128)(2,1)}, u32[]{:S(2)}, u32[]{:S(2)}) collective-permute-start(bf16[2,4,128,768]{3,2,1,0:T(8,128)(2,1)} %halo_pack.4), channel_id=1, source_target_pairs={{0,32},{1,33},{2,34},{3,35},{4,36},{5,37},{6,38},{7,39},{8,40},{9,... | collective-permute-start | bytes 4718600 | tf_op jit(solution)/shard_map/ppermute | solution.py:67
  581.1 44.9 %collective-permute-start.37 = (bf16[384,1536]{1,0:T(8,128)(2,1)S(1)}, bf16[384,1536]{1,0:T(8,128)(2,1)S(1)}, u32[]{:S(2)}, u32[]{:S(2)}) collective-permute-start(bf16[384,1536]{1,0:T(8,128)(2,1)S(1)} %bitcast.90), channel_id=1, source_target_pairs={{0,32},{1,33},{2,34},{3,35},{4,36},{5,37},{6,38},{7,39},{8,40},{9,... | collective-permute-start | bytes 3538952 | tf_op jit(solution)/shard_map/ppermute | solution.py:67
  582.8 40.7 %collective-permute-start.36 = (bf16[384,1536]{1,0:T(8,128)(2,1)S(1)}, bf16[384,1536]{1,0:T(8,128)(2,1)S(1)}, u32[]{:S(2)}, u32[]{:S(2)}) collective-permute-start(bf16[384,1536]{1,0:T(8,128)(2,1)S(1)} %collective-permute-done.35), channel_id=1, source_target_pairs={{0,16},{1,17},{2,18},{3,19},{4,20},{5,21},{6,22},{7,23},{8,24},{9,... | collective-permute-start | bytes 3538952 | tf_op jit(solution)/shard_map/ppermute | solution.py:67
  593.2 34.1 %collective-permute-start.38 = (bf16[384,1536]{1,0:T(8,128)(2,1)S(1)}, bf16[384,1536]{1,0:T(8,128)(2,1)S(1)}, u32[]{:S(2)}, u32[]{:S(2)}) collective-permute-start(bf16[384,1536]{1,0:T(8,128)(2,1)S(1)} %collective-permute-done.34), channel_id=1, source_target_pairs={{0,32},{1,33},{2,34},{3,35},{4,36},{5,37},{6,38},{7,39},{8,40},{9,... | collective-permute-start | bytes 3538952 | tf_op jit(solution)/shard_map/ppermute | solution.py:67
  603.1 28.6 %collective-permute-start.25 = (bf16[128,768]{1,0:T(8,128)(2,1)S(1)}, bf16[128,768]{1,0:T(8,128)(2,1)S(1)}, u32[]{:S(2)}, u32[]{:S(2)}) collective-permute-start(bf16[128,768]{1,0:T(8,128)(2,1)S(1)} %copy-done.25), channel_id=1, source_target_pairs={{28,0},{29,1},{30,2},{31,3},{0,4},{1,5},{2,6},{3,7},{4,8},{5,9},{6... | collective-permute-start | bytes 589832 | tf_op jit(solution)/shard_map/ppermute | solution.py:67
  613.6 21.9 %collective-permute-start.39 = (bf16[384,1536]{1,0:T(8,128)(2,1)S(1)}, bf16[384,1536]{1,0:T(8,128)(2,1)}, u32[]{:S(2)}, u32[]{:S(2)}) collective-permute-start(bf16[384,1536]{1,0:T(8,128)(2,1)S(1)} %collective-permute-done.35), channel_id=1, source_target_pairs={{0,32},{1,33},{2,34},{3,35},{4,36},{5,37},{6,38},{7,39},{8,40},{9,... | collective-permute-start | bytes 3538952 | tf_op jit(solution)/shard_map/ppermute | solution.py:67
  623.5 23.9 %collective-permute-start.40 = (bf16[384,1536]{1,0:T(8,128)(2,1)S(1)}, bf16[384,1536]{1,0:T(8,128)(2,1)S(1)}, u32[]{:S(2)}, u32[]{:S(2)}) collective-permute-start(bf16[384,1536]{1,0:T(8,128)(2,1)S(1)} %collective-permute-done.36), channel_id=1, source_target_pairs={{0,32},{1,33},{2,34},{3,35},{4,36},{5,37},{6,38},{7,39},{8,40},{9,... | collective-permute-start | bytes 3538952 | tf_op jit(solution)/shard_map/ppermute | solution.py:67
  631.7 10.5 %collective-permute-start.21 = (bf16[128,768]{1,0:T(8,128)(2,1)S(1)}, bf16[128,768]{1,0:T(8,128)(2,1)S(1)}, u32[]{:S(2)}, u32[]{:S(2)}) collective-permute-start(bf16[128,768]{1,0:T(8,128)(2,1)S(1)} %copy-done.28), channel_id=1, source_target_pairs={{4,0},{5,1},{6,2},{7,3},{8,4},{9,5},{10,6},{11,7},{12,8},{13,9},{1... | collective-permute-start | bytes 589832 | tf_op jit(solution)/shard_map/ppermute | solution.py:67
  631.8 10.5 %collective-permute-start.22 = (bf16[128,768]{1,0:T(8,128)(2,1)S(1)}, bf16[128,768]{1,0:T(8,128)(2,1)S(1)}, u32[]{:S(2)}, u32[]{:S(2)}) collective-permute-start(bf16[128,768]{1,0:T(8,128)(2,1)S(1)} %copy-done.26), channel_id=1, source_target_pairs={{1,0},{2,1},{3,2},{0,3},{5,4},{6,5},{7,6},{4,7},{9,8},{10,9},{11,1... | collective-permute-start | bytes 589832 | tf_op jit(solution)/shard_map/ppermute | solution.py:67
  633.5 12.4 %collective-permute-start.23 = (bf16[128,768]{1,0:T(8,128)(2,1)S(1)}, bf16[128,768]{1,0:T(8,128)(2,1)S(1)}, u32[]{:S(2)}, u32[]{:S(2)}) collective-permute-start(bf16[128,768]{1,0:T(8,128)(2,1)S(1)} %copy-done.24), channel_id=1, source_target_pairs={{5,0},{6,1},{7,2},{4,3},{9,4},{10,5},{11,6},{8,7},{13,8},{14,9},{1... | collective-permute-start | bytes 589832 | tf_op jit(solution)/shard_map/ppermute | solution.py:67
  635.4 10.5 %collective-permute-start.11 = (bf16[128,768]{1,0:T(8,128)(2,1)S(1)}, bf16[128,768]{1,0:T(8,128)(2,1)S(1)}, u32[]{:S(2)}, u32[]{:S(2)}) collective-permute-start(bf16[128,768]{1,0:T(8,128)(2,1)S(1)} %copy-done.16), channel_id=1, source_target_pairs={{28,0},{29,1},{30,2},{31,3},{0,4},{1,5},{2,6},{3,7},{4,8},{5,9},{6... | collective-permute-start | bytes 589832 | tf_op jit(solution)/shard_map/ppermute | solution.py:67
  645.9 9.3 %collective-permute-start.7 = (bf16[128,768]{1,0:T(8,128)(2,1)S(1)}, bf16[128,768]{1,0:T(8,128)(2,1)S(1)}, u32[]{:S(2)}, u32[]{:S(2)}) collective-permute-start(bf16[128,768]{1,0:T(8,128)(2,1)S(1)} %copy-done.19), channel_id=1, source_target_pairs={{4,0},{5,1},{6,2},{7,3},{8,4},{9,5},{10,6},{11,7},{12,8},{13,9},{1... | collective-permute-start | bytes 589832 | tf_op jit(solution)/shard_map/ppermute | solution.py:67
  647.5 10.3 %collective-permute-start.9 = (bf16[128,768]{1,0:T(8,128)(2,1)S(1)}, bf16[128,768]{1,0:T(8,128)(2,1)S(1)}, u32[]{:S(2)}, u32[]{:S(2)}) collective-permute-start(bf16[128,768]{1,0:T(8,128)(2,1)S(1)} %copy-done.17), channel_id=1, source_target_pairs={{5,0},{6,1},{7,2},{4,3},{9,4},{10,5},{11,6},{8,7},{13,8},{14,9},{1... | collective-permute-start | bytes 589832 | tf_op jit(solution)/shard_map/ppermute | solution.py:67
  (46 other events, 896.9 us)

commit v2 on v1

--- a/solution.py
+++ b/solution.py
@@ -70,26 +70,30 @@
 MOVES = ((0, 0), (1, 0), (0, 1), (1, 1))
 
 
+def relay(moves, sems):
+    inward = [pltpu.make_async_copy(src, held, sems.at[0, n]) for n, (src, held, _) in enumerate(moves)]
+    outward = [pltpu.make_async_copy(held, dst, sems.at[1, n]) for n, (_, held, dst) in enumerate(moves)]
+    for copy in inward:
+        copy.start()
+    for arrives, leaves in zip(inward, outward):
+        arrives.wait()
+        leaves.start()
+    for copy in outward:
+        copy.wait()
+
+
 def pack_kernel(half, lane, width, sign_ref, q_ref, k_ref, v_ref, *rest):
-    outs, sems = rest[:4], rest[4]
+    outs, held, sems = rest[:4], rest[4], rest[5]
     s = sign_ref[0]
-    copies = []
-    for piece, (a, b) in enumerate(MOVES):
+    moves = []
+    for piece in (1, 2, 3, 0):
+        a, b = MOVES[piece]
         i = s + a * (1 - 2 * s)
         j = s + b * (1 - 2 * s)
         for n, src in enumerate((q_ref, k_ref, v_ref)):
-            for fr in range(2):
-                copies.append(
-                    pltpu.make_async_copy(
-                        src.at[2 * half + fr, i, :, j, :, pl.ds(lane, width)],
-                        outs[piece].at[n, fr],
-                        sems.at[piece * 6 + n * 2 + fr],
-                    )
-                )
-    for copy in copies:
-        copy.start()
-    for copy in copies:
-        copy.wait()
+            at = src.at[pl.ds(2 * half, 2), i, :, j, :, pl.ds(lane, width)]
+            moves.append((at, held.at[piece, n], outs[piece].at[n]))
+    relay(moves, sems)
 
 
 def pack(half, first, heads, sign, q, k, v):
@@ -101,7 +105,8 @@
         out_shape=[shape] * 4,
         in_specs=[pl.BlockSpec(memory_space=pltpu.SMEM)] + [any_spec] * 3,
         out_specs=[any_spec] * 4,
-        scratch_shapes=[pltpu.SemaphoreType.DMA((24,))],
+        scratch_shapes=[pltpu.VMEM((4, 3, 2, 8, 8, width), jnp.bfloat16), pltpu.SemaphoreType.DMA((2, 12))],
+        compiler_params=pltpu.CompilerParams(vmem_limit_bytes=VMEM),
         cost_estimate=pl.CostEstimate(flops=0, bytes_accessed=24 * 128 * width * 2, transcendentals=0),
         name=f"pack_{half}_{first}",
     )(sign, q, k, v)
@@ -109,15 +114,9 @@
 
 
 def halo_kernel(*refs):
-    srcs, out, sems = refs[:4], refs[4], refs[5]
-    copies = []
-    for piece, src in enumerate(srcs):
-        for n in range(2):
-            copies.append(pltpu.make_async_copy(src.at[1 + n], out.at[n, piece], sems.at[piece * 2 + n]))
-    for copy in copies:
-        copy.start()
-    for copy in copies:
-        copy.wait()
+    srcs, out, held, sems = refs[:4], refs[4], refs[5], refs[6]
+    moves = [(src.at[pl.ds(1, 2)], held.at[piece], out.at[piece]) for piece, src in enumerate(srcs)]
+    relay(moves, sems)
 
 
 def halo_pack(pieces):
@@ -125,10 +124,11 @@
     any_spec = pl.BlockSpec(memory_space=pl.ANY)
     return pl.pallas_call(
         halo_kernel,
-        out_shape=jax.ShapeDtypeStruct((2, 4, 128, width), jnp.bfloat16),
+        out_shape=jax.ShapeDtypeStruct((4, 2, 128, width), jnp.bfloat16),
         in_specs=[any_spec] * 4,
         out_specs=any_spec,
-        scratch_shapes=[pltpu.SemaphoreType.DMA((8,))],
+        scratch_shapes=[pltpu.VMEM((4, 2, 128, width), jnp.bfloat16), pltpu.SemaphoreType.DMA((2, 4))],
+        compiler_params=pltpu.CompilerParams(vmem_limit_bytes=VMEM),
         cost_estimate=pl.CostEstimate(flops=0, bytes_accessed=16 * 128 * width * 2, transcendentals=0),
         name="halo_pack",
     )(*pieces)
@@ -149,8 +149,8 @@
         kaug[rows, :HS] = piece[1]
         vaug[rows, :HS] = piece[2]
         rows = pl.ds(512 + n * 128, 128)
-        kaug[rows, :HS] = halo[0, n]
-        vaug[rows, :HS] = halo[1, n]
+        kaug[rows, :HS] = halo[n, 0]
+        vaug[rows, :HS] = halo[n, 1]
     scale = math.log2(math.e) / math.sqrt(HS)
     for part in range(2):
         rows = pl.ds(part * 256, 256)
@@ -175,7 +175,7 @@
         out_shape=[out] * 4,
         in_specs=[pl.BlockSpec((3, 128, HS), lambda h: (0, 0, h))] * 4
         + [
-            pl.BlockSpec((2, 4, 128, HS), lambda h: (0, 0, 0, h)),
+            pl.BlockSpec((4, 2, 128, HS), lambda h: (0, 0, 0, h)),
             pl.BlockSpec((1024, HS), lambda h: (0, 0)),
             pl.BlockSpec((512, HS), lambda h: (0, 0)),
             pl.BlockSpec((512, HS), lambda h: (0, 0)),

time: 679 us -> 258 us (0.38)
  Pallas kernels: 544 us -> 77.1 us
  starting transfers between devices: 63.3 us -> 95.6 us
  waiting for transfers between devices: 36.6 us -> 50.9 us
    pallas_call x4, Pallas kernels: 291 us -> 10.6 us  [pack(): pl.pallas_call(functools.partial(pack_kernel, half, first * HS, width), o...]
    pallas_call x4, Pallas kernels: 195 us -> 8.94 us  [halo_pack(): pl.pallas_call(halo_kernel, out_shape=jax.ShapeDtypeStruct((4, 2, 128, wi...]
    ppermute x41, starting transfers between devices: 63.3 us -> 95.6 us  [send(): return lax.ppermute(value, AXES, pairs)]
    ppermute x41, waiting for transfers between devices: 36.6 us -> 50.9 us  [send(): return lax.ppermute(value, AXES, pairs)]
  transfers between devices with their start and end apart: 41 -> 41, of which waited for: 8 -> 11; matrix products, arithmetic and copies ran while one was open for 5% -> 11% of each run, Pallas kernels for 77% -> 23%
where the time goes in v2:
time: 258 us; the launch traced here: 256 us
  starting transfers between devices  95.6 us (37%)
  Pallas kernels  77.1 us (30%)
  waiting for transfers between devices  50.9 us (20%)
  local copies, waits for them, and re-layouts  22.8 us (9%)
  other arithmetic  8.48 us (3%)
    ppermute x41, starting transfers between devices, send(): return lax.ppermute(value, AXES, pairs)  95.6 us
    ppermute x41, waiting for transfers between devices, send(): return lax.ppermute(value, AXES, pairs)  50.9 us
    pallas_call x4, Pallas kernels, attend(): pl.pallas_call(attend_kernel, grid=(heads,), out_shape=[out] * 4, in_spec...  38.2 us
    pallas_call x1, Pallas kernels, project(): pl.pallas_call(functools.partial(project_kernel, groups), grid_spec=grid_...  19.4 us
    unnamed x109, local copies, waits for them, and re-layouts  11.8 us
    pallas_call x4, Pallas kernels, pack(): pl.pallas_call(functools.partial(pack_kernel, half, first * HS, width), o...  10.6 us
    pallas_call x4, Pallas kernels, halo_pack(): pl.pallas_call(halo_kernel, out_shape=jax.ShapeDtypeStruct((4, 2, 128, wi...  8.94 us
  transfers between devices with their start and end apart: 41, of which 11 were waited for; matrix products, arithmetic and copies ran while one was open for 11% of the time, Pallas kernels for 23%

profile of v2, /device:TPU:1, one launch (start us, length us, event | category | flops | bytes accessed | tf_op | source)
XLA Modules:
  0.0 255.8 jit_solution(5398647052841811965)
XLA Ops:
  0.0 3.6 %collective-permute-start.28 = (bf16[24,1536]{1,0:T(8,128)(2,1)}, bf16[24,1536]{1,0:T(8,128)(2,1)S(1)}, u32[]{:S(2)}, u32[]{:S(2)}) collective-permute-start(bf16[24,1536]{1,0:T(8,128)(2,1)} %bitcast.103), channel_id=1, source_target_pairs={{0,3},{1,0},{2,1},{3,2},{4,7},{5,4},{6,5},{7,6},{8,11},{9,8},{10,9... | collective-permute-start | bytes 221192 | tf_op jit(solution)/shard_map/ppermute | solution.py:67
  5.3 3.3 %collective-permute-done.29 = bf16[24,1536]{1,0:T(8,128)(2,1)S(1)} collective-permute-done((bf16[24,1536]{1,0:T(8,128)(2,1)}, bf16[24,1536]{1,0:T(8,128)(2,1)S(1)}, u32[]{:S(2)}, u32[]{:S(2)}) %collective-permute-start.29) | collective-permute-done | bytes 73760 | tf_op jit(solution)/shard_map/ppermute | solution.py:67
  10.7 2.5 collective-permute-start.31
  13.2 2.6 %pack_0_6.1 = (bf16[3,2,8,8,768]{4,3,2,1,0:T(8,128)(2,1)}, bf16[3,2,8,8,768]{4,3,2,1,0:T(8,128)(2,1)}, bf16[3,2,8,8,768]{4,3,2,1,0:T(8,128)(2,1)}, bf16[3,2,8,8,768]{4,3,2,1,0:T(8,128)(2,1)}) custom-call(s32[1]{0:T(128)} %bitcast.sign_ref, bf16[4,2,8,2,8,1536]{5,4,3,2,1,0:T(8,128)(2,1)} %bitcast.76, bf16[4,2,8,2,8,1536]{5,4,3,2,1,0:T(8,128)(2,1)} %bitcast.80, ...), custom_call_target="tpu_custom_call" | custom-call | bytes 4718592 | tf_op jit(solution)/shard_map/pack_0_6/pallas_call | solution.py:103
  19.1 2.6 %pack_1_6.1 = (bf16[3,2,8,8,768]{4,3,2,1,0:T(8,128)(2,1)}, bf16[3,2,8,8,768]{4,3,2,1,0:T(8,128)(2,1)}, bf16[3,2,8,8,768]{4,3,2,1,0:T(8,128)(2,1)}, bf16[3,2,8,8,768]{4,3,2,1,0:T(8,128)(2,1)}) custom-call(s32[1]{0:T(128)} %bitcast.1.sign_ref, bf16[4,2,8,2,8,1536]{5,4,3,2,1,0:T(8,128)(2,1)} %bitcast.77, bf16[4,2,8,2,8,1536]{5,4,3,2,1,0:T(8,128)(2,1)} %bitcast.81, ...), custom_call_target="tpu_custom_call" | custom-call | bytes 4718592 | tf_op jit(solution)/shard_map/pack_1_6/pallas_call | solution.py:103
  23.1 20.4 %collective-permute-done.32 = bf16[96,1536]{1,0:T(8,128)(2,1)S(1)} collective-permute-done((bf16[96,1536]{1,0:T(8,128)(2,1)S(1)}, bf16[96,1536]{1,0:T(8,128)(2,1)S(1)}, u32[]{:S(2)}, u32[]{:S(2)}) %collective-permute-start.32) | collective-permute-done | bytes 294944 | tf_op jit(solution)/shard_map/ppermute | solution.py:67
  45.6 7.4 %collective-permute-done.33 = bf16[96,1536]{1,0:T(8,128)(2,1)S(1)} collective-permute-done((bf16[96,1536]{1,0:T(8,128)(2,1)S(1)}, bf16[96,1536]{1,0:T(8,128)(2,1)S(1)}, u32[]{:S(2)}, u32[]{:S(2)}) %collective-permute-start.33) | collective-permute-done | bytes 294944 | tf_op jit(solution)/shard_map/ppermute | solution.py:67
  53.4 3.7 %collective-permute-start.34 = (bf16[384,1536]{1,0:T(8,128)(2,1)S(1)}, bf16[384,1536]{1,0:T(8,128)(2,1)S(1)}, u32[]{:S(2)}, u32[]{:S(2)}) collective-permute-start(bf16[384,1536]{1,0:T(8,128)(2,1)S(1)} %bitcast.88), channel_id=1, source_target_pairs={{0,16},{1,17},{2,18},{3,19},{4,20},{5,21},{6,22},{7,23},{8,24},{9,... | collective-permute-start | bytes 3538952 | tf_op jit(solution)/shard_map/ppermute | solution.py:67
  57.1 2.6 %pack_0_0.1 = (bf16[3,2,8,8,768]{4,3,2,1,0:T(8,128)(2,1)}, bf16[3,2,8,8,768]{4,3,2,1,0:T(8,128)(2,1)}, bf16[3,2,8,8,768]{4,3,2,1,0:T(8,128)(2,1)}, bf16[3,2,8,8,768]{4,3,2,1,0:T(8,128)(2,1)}) custom-call(s32[1]{0:T(128)} %bitcast.sign_ref, bf16[4,2,8,2,8,1536]{5,4,3,2,1,0:T(8,128)(2,1)} %bitcast.78, bf16[4,2,8,2,8,1536]{5,4,3,2,1,0:T(8,128)(2,1)} %bitcast.82, ...), custom_call_target="tpu_custom_call" | custom-call | bytes 4718592 | tf_op jit(solution)/shard_map/pack_0_0/pallas_call | solution.py:103
  61.1 3.4 %collective-permute-start.1 = (bf16[3,128,768]{2,1,0:T(8,128)(2,1)}, bf16[3,128,768]{2,1,0:T(8,128)(2,1)S(1)}, u32[]{:S(2)}, u32[]{:S(2)}) collective-permute-start(bf16[3,128,768]{2,1,0:T(8,128)(2,1)} %bitcast.108), channel_id=1, source_target_pairs={{0,1},{1,2},{2,3},{3,0},{4,5},{5,6},{6,7},{7,4},{8,9},{9,10},{10,1... | collective-permute-start | bytes 1769480 | tf_op jit(solution)/shard_map/ppermute | solution.py:67
  64.5 6.6 %collective-permute-done.18.refs_2_.p2 = bf16[3,128,768]{2,1,0:T(8,128)(2,1)S(1)} collective-permute-done((bf16[3,128,768]{2,1,0:T(8,128)(2,1)}, bf16[3,128,768]{2,1,0:T(8,128)(2,1)S(1)}, u32[]{:S(2)}, u32[]{:S(2)}) %collective-permute-start.18) | collective-permute-done | bytes 589856 | tf_op jit(solution)/shard_map/ppermute | solution.py:67
  71.2 6.7 %collective-permute-start.2 = (bf16[3,128,768]{2,1,0:T(8,128)(2,1)}, bf16[3,128,768]{2,1,0:T(8,128)(2,1)}, u32[]{:S(2)}, u32[]{:S(2)}) collective-permute-start(bf16[3,128,768]{2,1,0:T(8,128)(2,1)} %bitcast.107), channel_id=1, source_target_pairs={{0,5},{1,6},{2,7},{3,4},{4,9},{5,10},{6,11},{7,8},{8,13},{9,14},{1... | collective-permute-start | bytes 1769480 | tf_op jit(solution)/shard_map/ppermute | solution.py:67
  77.9 2.6 %pack_1_0.1 = (bf16[3,2,8,8,768]{4,3,2,1,0:T(8,128)(2,1)}, bf16[3,2,8,8,768]{4,3,2,1,0:T(8,128)(2,1)}, bf16[3,2,8,8,768]{4,3,2,1,0:T(8,128)(2,1)}, bf16[3,2,8,8,768]{4,3,2,1,0:T(8,128)(2,1)}) custom-call(s32[1]{0:T(128)} %bitcast.1.sign_ref, bf16[4,2,8,2,8,1536]{5,4,3,2,1,0:T(8,128)(2,1)} %bitcast.79, bf16[4,2,8,2,8,1536]{5,4,3,2,1,0:T(8,128)(2,1)} %bitcast.83, ...), custom_call_target="tpu_custom_call" | custom-call | bytes 4718592 | tf_op jit(solution)/shard_map/pack_1_0/pallas_call | solution.py:103
  89.3 14.4 %collective-permute-start.24 = (bf16[4,2,128,768]{3,2,1,0:T(8,128)(2,1)}, bf16[4,2,128,768]{3,2,1,0:T(8,128)(2,1)}, u32[]{:S(2)}, u32[]{:S(2)}) collective-permute-start(bf16[4,2,128,768]{3,2,1,0:T(8,128)(2,1)} %halo_pack.7), channel_id=1, source_target_pairs={{32,0},{33,1},{34,2},{35,3},{36,4},{37,5},{38,6},{39,7},{40,8},{41... | collective-permute-start | bytes 4718600 | tf_op jit(solution)/shard_map/ppermute | solution.py:67
  104.7 2.2 halo_pack.5
  111.8 2.3 halo_pack.6
  114.1 4.6 %collective-permute-start.20 = (bf16[4,2,128,768]{3,2,1,0:T(8,128)(2,1)}, bf16[4,2,128,768]{3,2,1,0:T(8,128)(2,1)}, u32[]{:S(2)}, u32[]{:S(2)}) collective-permute-start(bf16[4,2,128,768]{3,2,1,0:T(8,128)(2,1)} %halo_pack.6), channel_id=1, source_target_pairs={{0,32},{1,33},{2,34},{3,35},{4,36},{5,37},{6,38},{7,39},{8,40},{9,... | collective-permute-start | bytes 4718600 | tf_op jit(solution)/shard_map/ppermute | solution.py:67
  121.6 3.1 %collective-permute-start.6 = (bf16[4,2,128,768]{3,2,1,0:T(8,128)(2,1)}, bf16[4,2,128,768]{3,2,1,0:T(8,128)(2,1)}, u32[]{:S(2)}, u32[]{:S(2)}) collective-permute-start(bf16[4,2,128,768]{3,2,1,0:T(8,128)(2,1)} %halo_pack.4), channel_id=1, source_target_pairs={{0,32},{1,33},{2,34},{3,35},{4,36},{5,37},{6,38},{7,39},{8,40},{9,... | collective-permute-start | bytes 4718600 | tf_op jit(solution)/shard_map/ppermute | solution.py:67
  140.0 9.5 %attend.7 = (bf16[128,768]{1,0:T(8,128)(2,1)}, bf16[128,768]{1,0:T(8,128)(2,1)}, bf16[128,768]{1,0:T(8,128)(2,1)}, bf16[128,768]{1,0:T(8,128)(2,1)}) custom-call(bf16[3,128,768]{2,1,0:T(8,128)(2,1)} %bitcast.98, bf16[3,128,768]{2,1,0:T(8,128)(2,1)} %collective-permute-done.17.refs_1_.p1, bf16[3,128,768]{2,1,0:T(8,128)(2,1)} %copy-done.4, ...), custom_call_target="tpu_custom_call" | custom-call | flops 3221225472 | bytes 3932160 | tf_op jit(solution)/shard_map/attend/pallas_call | solution.py:172
  149.6 21.0 %collective-permute-start.38 = (bf16[384,1536]{1,0:T(8,128)(2,1)S(1)}, bf16[384,1536]{1,0:T(8,128)(2,1)S(1)}, u32[]{:S(2)}, u32[]{:S(2)}) collective-permute-start(bf16[384,1536]{1,0:T(8,128)(2,1)S(1)} %collective-permute-done.34), channel_id=1, source_target_pairs={{0,32},{1,33},{2,34},{3,35},{4,36},{5,37},{6,38},{7,39},{8,40},{9,... | collective-permute-start | bytes 3538952 | tf_op jit(solution)/shard_map/ppermute | solution.py:67
  170.5 9.6 %attend.5 = (bf16[128,768]{1,0:T(8,128)(2,1)}, bf16[128,768]{1,0:T(8,128)(2,1)}, bf16[128,768]{1,0:T(8,128)(2,1)}, bf16[128,768]{1,0:T(8,128)(2,1)}) custom-call(bf16[3,128,768]{2,1,0:T(8,128)(2,1)} %bitcast.102, bf16[3,128,768]{2,1,0:T(8,128)(2,1)} %collective-permute-done.3.refs_1_.p1, bf16[3,128,768]{2,1,0:T(8,128)(2,1)} %collective-permute-done.4.refs_2_.p2, ...), custom_call_target="tpu_custom_call" | custom-call | flops 3221225472 | bytes 3932160 | tf_op jit(solution)/shard_map/attend/pallas_call | solution.py:172
  181.0 9.5 %attend.6 = (bf16[128,768]{1,0:T(8,128)(2,1)}, bf16[128,768]{1,0:T(8,128)(2,1)}, bf16[128,768]{1,0:T(8,128)(2,1)}, bf16[128,768]{1,0:T(8,128)(2,1)}) custom-call(bf16[3,128,768]{2,1,0:T(8,128)(2,1)} %bitcast.96, bf16[3,128,768]{2,1,0:T(8,128)(2,1)} %copy-done, bf16[3,128,768]{2,1,0:T(8,128)(2,1)} %copy-done.1, ...), custom_call_target="tpu_custom_call" | custom-call | flops 3221225472 | bytes 3932160 | tf_op jit(solution)/shard_map/attend/pallas_call | solution.py:172
  190.7 9.6 %attend.4 = (bf16[128,768]{1,0:T(8,128)(2,1)}, bf16[128,768]{1,0:T(8,128)(2,1)}, bf16[128,768]{1,0:T(8,128)(2,1)}, bf16[128,768]{1,0:T(8,128)(2,1)}) custom-call(bf16[3,128,768]{2,1,0:T(8,128)(2,1)} %bitcast.100, bf16[3,128,768]{2,1,0:T(8,128)(2,1)} %copy-done.2, bf16[3,128,768]{2,1,0:T(8,128)(2,1)} %copy-done.3, ...), custom_call_target="tpu_custom_call" | custom-call | flops 3221225472 | bytes 3932160 | tf_op jit(solution)/shard_map/attend/pallas_call | solution.py:172
  204.3 4.8 %collective-permute-start.27 = (bf16[128,768]{1,0:T(8,128)(2,1)S(1)}, bf16[128,768]{1,0:T(8,128)(2,1)S(1)}, u32[]{:S(2)}, u32[]{:S(2)}) collective-permute-start(bf16[128,768]{1,0:T(8,128)(2,1)S(1)} %copy-done.29), channel_id=1, source_target_pairs={{31,0},{28,1},{29,2},{30,3},{3,4},{0,5},{1,6},{2,7},{7,8},{4,9},{5... | collective-permute-start | bytes 589832 | tf_op jit(solution)/shard_map/ppermute | solution.py:67
  212.8 2.7 %collective-permute-start.11 = (bf16[128,768]{1,0:T(8,128)(2,1)S(1)}, bf16[128,768]{1,0:T(8,128)(2,1)S(1)}, u32[]{:S(2)}, u32[]{:S(2)}) collective-permute-start(bf16[128,768]{1,0:T(8,128)(2,1)S(1)} %copy-done.24), channel_id=1, source_target_pairs={{28,0},{29,1},{30,2},{31,3},{0,4},{1,5},{2,6},{3,7},{4,8},{5,9},{6... | collective-permute-start | bytes 589832 | tf_op jit(solution)/shard_map/ppermute | solution.py:67
  215.4 2.5 constant_dynamic-update-slice_fusion.1
  217.9 3.8 %collective-permute-start.12 = (bf16[128,768]{1,0:T(8,128)(2,1)S(1)}, bf16[128,768]{1,0:T(8,128)(2,1)S(1)}, u32[]{:S(2)}, u32[]{:S(2)}) collective-permute-start(bf16[128,768]{1,0:T(8,128)(2,1)S(1)} %copy-done.23), channel_id=1, source_target_pairs={{3,0},{0,1},{1,2},{2,3},{7,4},{4,5},{5,6},{6,7},{11,8},{8,9},{9,10... | collective-permute-start | bytes 589832 | tf_op jit(solution)/shard_map/ppermute | solution.py:67
  221.7 2.3 collective-permute-start.13
  226.4 2.7 %collective-permute-done.13.refs_7_ = bf16[128,768]{1,0:T(8,128)(2,1)S(1)} collective-permute-done((bf16[128,768]{1,0:T(8,128)(2,1)S(1)}, bf16[128,768]{1,0:T(8,128)(2,1)S(1)}, u32[]{:S(2)}, u32[]{:S(2)}) %collective-permute-start.13) | collective-permute-done | bytes 196640 | tf_op jit(solution)/shard_map/ppermute | solution.py:67
  229.1 3.9 %collective-permute-done.7.refs_1_ = bf16[128,768]{1,0:T(8,128)(2,1)S(1)} collective-permute-done((bf16[128,768]{1,0:T(8,128)(2,1)S(1)}, bf16[128,768]{1,0:T(8,128)(2,1)S(1)}, u32[]{:S(2)}, u32[]{:S(2)}) %collective-permute-start.7) | collective-permute-done | bytes 196640 | tf_op jit(solution)/shard_map/ppermute | solution.py:67
  233.0 2.8 %collective-permute-done.9.refs_3_ = bf16[128,768]{1,0:T(8,128)(2,1)S(1)} collective-permute-done((bf16[128,768]{1,0:T(8,128)(2,1)S(1)}, bf16[128,768]{1,0:T(8,128)(2,1)S(1)}, u32[]{:S(2)}, u32[]{:S(2)}) %collective-permute-start.9) | collective-permute-done | bytes 196640 | tf_op jit(solution)/shard_map/ppermute | solution.py:67
  236.5 19.4 %project.1 = bf16[4,16,16,3072]{3,2,1,0:T(8,128)(2,1)} custom-call(s32[2]{0:T(128)} %pad_add_fusion.2.signs, s32[8]{0:T(128)} %stack.86.places, bf16[128,768]{1,0:T(8,128)(2,1)} %get-tuple-element.45.refs_0_, bf16[128,768]{1,0:T(8,128)(2,1)} %copy-done.42, bf16[128,768]{1,0:T(8,128)(2,1)} %copy-done.43, bf16[128,768]{1,0:T(8,128)(2,1)} %copy-done.44, ...), custom_call_target="tpu_custom_call" | custom-call | flops 9663676416 | bytes 26214400 | tf_op jit(solution)/shard_map/project/pallas_call | solution.py:235
  (203 shorter events, 56.1 us)
Async XLA Ops:
  10.7 12.4 %collective-permute-start.31 = (bf16[96,1536]{1,0:T(8,128)(2,1)S(1)}, bf16[96,1536]{1,0:T(8,128)(2,1)S(1)}, u32[]{:S(2)}, u32[]{:S(2)}) collective-permute-start(bf16[96,1536]{1,0:T(8,128)(2,1)S(1)} %bitcast.91), channel_id=1, source_target_pairs={{0,12},{1,13},{2,14},{3,15},{4,0},{5,1},{6,2},{7,3},{8,4},{9,5},{1... | collective-permute-start | bytes 884744 | tf_op jit(solution)/shard_map/ppermute | solution.py:67
  15.8 37.3 %collective-permute-start.14 = (bf16[3,128,768]{2,1,0:T(8,128)(2,1)}, bf16[3,128,768]{2,1,0:T(8,128)(2,1)S(1)}, u32[]{:S(2)}, u32[]{:S(2)}) collective-permute-start(bf16[3,128,768]{2,1,0:T(8,128)(2,1)} %bitcast.116), channel_id=1, source_target_pairs={{0,4},{1,5},{2,6},{3,7},{4,8},{5,9},{6,10},{7,11},{8,12},{9,13},{1... | collective-permute-start | bytes 1769480 | tf_op jit(solution)/shard_map/ppermute | solution.py:67
  17.8 35.6 %collective-permute-start.15 = (bf16[3,128,768]{2,1,0:T(8,128)(2,1)}, bf16[3,128,768]{2,1,0:T(8,128)(2,1)S(1)}, u32[]{:S(2)}, u32[]{:S(2)}) collective-permute-start(bf16[3,128,768]{2,1,0:T(8,128)(2,1)} %bitcast.115), channel_id=1, source_target_pairs={{0,1},{1,2},{2,3},{3,0},{4,5},{5,6},{6,7},{7,4},{8,9},{9,10},{10,1... | collective-permute-start | bytes 1769480 | tf_op jit(solution)/shard_map/ppermute | solution.py:67
  18.1 41.7 %collective-permute-start.16 = (bf16[3,128,768]{2,1,0:T(8,128)(2,1)}, bf16[3,128,768]{2,1,0:T(8,128)(2,1)}, u32[]{:S(2)}, u32[]{:S(2)}) collective-permute-start(bf16[3,128,768]{2,1,0:T(8,128)(2,1)} %bitcast.112), channel_id=1, source_target_pairs={{0,5},{1,6},{2,7},{3,4},{4,9},{5,10},{6,11},{7,8},{8,13},{9,14},{1... | collective-permute-start | bytes 1769480 | tf_op jit(solution)/shard_map/ppermute | solution.py:67
  21.8 39.4 %collective-permute-start.17 = (bf16[3,128,768]{2,1,0:T(8,128)(2,1)}, bf16[3,128,768]{2,1,0:T(8,128)(2,1)}, u32[]{:S(2)}, u32[]{:S(2)}) collective-permute-start(bf16[3,128,768]{2,1,0:T(8,128)(2,1)} %bitcast.114), channel_id=1, source_target_pairs={{0,28},{1,29},{2,30},{3,31},{4,0},{5,1},{6,2},{7,3},{8,4},{9,5},{1... | collective-permute-start | bytes 1769480 | tf_op jit(solution)/shard_map/ppermute | solution.py:67
  23.0 20.5 %collective-permute-start.32 = (bf16[96,1536]{1,0:T(8,128)(2,1)S(1)}, bf16[96,1536]{1,0:T(8,128)(2,1)S(1)}, u32[]{:S(2)}, u32[]{:S(2)}) collective-permute-start(bf16[96,1536]{1,0:T(8,128)(2,1)S(1)} %bitcast.92), channel_id=1, source_target_pairs={{0,8},{1,9},{2,10},{3,11},{4,12},{5,13},{6,14},{7,15},{8,0},{9,1},... | collective-permute-start | bytes 884744 | tf_op jit(solution)/shard_map/ppermute | solution.py:67
  43.5 9.4 %collective-permute-start.33 = (bf16[96,1536]{1,0:T(8,128)(2,1)S(1)}, bf16[96,1536]{1,0:T(8,128)(2,1)S(1)}, u32[]{:S(2)}, u32[]{:S(2)}) collective-permute-start(bf16[96,1536]{1,0:T(8,128)(2,1)S(1)} %bitcast.93), channel_id=1, source_target_pairs={{0,4},{1,5},{2,6},{3,7},{4,8},{5,9},{6,10},{7,11},{8,12},{9,13},{1... | collective-permute-start | bytes 884744 | tf_op jit(solution)/shard_map/ppermute | solution.py:67
  52.9 18.2 %collective-permute-start.18 = (bf16[3,128,768]{2,1,0:T(8,128)(2,1)}, bf16[3,128,768]{2,1,0:T(8,128)(2,1)S(1)}, u32[]{:S(2)}, u32[]{:S(2)}) collective-permute-start(bf16[3,128,768]{2,1,0:T(8,128)(2,1)} %bitcast.113), channel_id=1, source_target_pairs={{0,3},{1,0},{2,1},{3,2},{4,7},{5,4},{6,5},{7,6},{8,11},{9,8},{10,9... | collective-permute-start | bytes 1769480 | tf_op jit(solution)/shard_map/ppermute | solution.py:67
  53.1 27.4 %collective-permute-start.19 = (bf16[3,128,768]{2,1,0:T(8,128)(2,1)S(1)}, bf16[3,128,768]{2,1,0:T(8,128)(2,1)S(1)}, u32[]{:S(2)}, u32[]{:S(2)}) collective-permute-start(bf16[3,128,768]{2,1,0:T(8,128)(2,1)S(1)} %bitcast.111), channel_id=1, source_target_pairs={{0,31},{1,28},{2,29},{3,30},{4,3},{5,0},{6,1},{7,2},{8,7},{9,4},{1... | collective-permute-start | bytes 1769480 | tf_op jit(solution)/shard_map/ppermute | solution.py:67
  53.4 55.5 %collective-permute-start.34 = (bf16[384,1536]{1,0:T(8,128)(2,1)S(1)}, bf16[384,1536]{1,0:T(8,128)(2,1)S(1)}, u32[]{:S(2)}, u32[]{:S(2)}) collective-permute-start(bf16[384,1536]{1,0:T(8,128)(2,1)S(1)} %bitcast.88), channel_id=1, source_target_pairs={{0,16},{1,17},{2,18},{3,19},{4,20},{5,21},{6,22},{7,23},{8,24},{9,... | collective-permute-start | bytes 3538952 | tf_op jit(solution)/shard_map/ppermute | solution.py:67
  59.8 22.3 %collective-permute-start = (bf16[3,128,768]{2,1,0:T(8,128)(2,1)}, bf16[3,128,768]{2,1,0:T(8,128)(2,1)S(1)}, u32[]{:S(2)}, u32[]{:S(2)}) collective-permute-start(bf16[3,128,768]{2,1,0:T(8,128)(2,1)} %bitcast.110), channel_id=1, source_target_pairs={{0,4},{1,5},{2,6},{3,7},{4,8},{5,9},{6,10},{7,11},{8,12},{9,13},{1... | collective-permute-start | bytes 1769480 | tf_op jit(solution)/shard_map/ppermute | solution.py:67
  61.1 28.0 %collective-permute-start.1 = (bf16[3,128,768]{2,1,0:T(8,128)(2,1)}, bf16[3,128,768]{2,1,0:T(8,128)(2,1)S(1)}, u32[]{:S(2)}, u32[]{:S(2)}) collective-permute-start(bf16[3,128,768]{2,1,0:T(8,128)(2,1)} %bitcast.108), channel_id=1, source_target_pairs={{0,1},{1,2},{2,3},{3,0},{4,5},{5,6},{6,7},{7,4},{8,9},{9,10},{10,1... | collective-permute-start | bytes 1769480 | tf_op jit(solution)/shard_map/ppermute | solution.py:67
  71.2 18.1 %collective-permute-start.2 = (bf16[3,128,768]{2,1,0:T(8,128)(2,1)}, bf16[3,128,768]{2,1,0:T(8,128)(2,1)}, u32[]{:S(2)}, u32[]{:S(2)}) collective-permute-start(bf16[3,128,768]{2,1,0:T(8,128)(2,1)} %bitcast.107), channel_id=1, source_target_pairs={{0,5},{1,6},{2,7},{3,4},{4,9},{5,10},{6,11},{7,8},{8,13},{9,14},{1... | collective-permute-start | bytes 1769480 | tf_op jit(solution)/shard_map/ppermute | solution.py:67
  81.4 25.6 %collective-permute-start.3 = (bf16[3,128,768]{2,1,0:T(8,128)(2,1)}, bf16[3,128,768]{2,1,0:T(8,128)(2,1)}, u32[]{:S(2)}, u32[]{:S(2)}) collective-permute-start(bf16[3,128,768]{2,1,0:T(8,128)(2,1)} %bitcast.109), channel_id=1, source_target_pairs={{0,28},{1,29},{2,30},{3,31},{4,0},{5,1},{6,2},{7,3},{8,4},{9,5},{1... | collective-permute-start | bytes 1769480 | tf_op jit(solution)/shard_map/ppermute | solution.py:67
  82.1 31.9 %collective-permute-start.4 = (bf16[3,128,768]{2,1,0:T(8,128)(2,1)}, bf16[3,128,768]{2,1,0:T(8,128)(2,1)}, u32[]{:S(2)}, u32[]{:S(2)}) collective-permute-start(bf16[3,128,768]{2,1,0:T(8,128)(2,1)} %bitcast.106), channel_id=1, source_target_pairs={{0,3},{1,0},{2,1},{3,2},{4,7},{5,4},{6,5},{7,6},{8,11},{9,8},{10,9... | collective-permute-start | bytes 1769480 | tf_op jit(solution)/shard_map/ppermute | solution.py:67
  89.2 30.2 %collective-permute-start.5 = (bf16[3,128,768]{2,1,0:T(8,128)(2,1)}, bf16[3,128,768]{2,1,0:T(8,128)(2,1)}, u32[]{:S(2)}, u32[]{:S(2)}) collective-permute-start(bf16[3,128,768]{2,1,0:T(8,128)(2,1)} %bitcast.20), channel_id=1, source_target_pairs={{0,31},{1,28},{2,29},{3,30},{4,3},{5,0},{6,1},{7,2},{8,7},{9,4},{1... | collective-permute-start | bytes 1769480 | tf_op jit(solution)/shard_map/ppermute | solution.py:67
  89.3 47.2 %collective-permute-start.24 = (bf16[4,2,128,768]{3,2,1,0:T(8,128)(2,1)}, bf16[4,2,128,768]{3,2,1,0:T(8,128)(2,1)}, u32[]{:S(2)}, u32[]{:S(2)}) collective-permute-start(bf16[4,2,128,768]{3,2,1,0:T(8,128)(2,1)} %halo_pack.7), channel_id=1, source_target_pairs={{32,0},{33,1},{34,2},{35,3},{36,4},{37,5},{38,6},{39,7},{40,8},{41... | collective-permute-start | bytes 4718600 | tf_op jit(solution)/shard_map/ppermute | solution.py:67
  107.0 42.6 %collective-permute-start.10 = (bf16[4,2,128,768]{3,2,1,0:T(8,128)(2,1)}, bf16[4,2,128,768]{3,2,1,0:T(8,128)(2,1)}, u32[]{:S(2)}, u32[]{:S(2)}) collective-permute-start(bf16[4,2,128,768]{3,2,1,0:T(8,128)(2,1)} %halo_pack.5), channel_id=1, source_target_pairs={{32,0},{33,1},{34,2},{35,3},{36,4},{37,5},{38,6},{39,7},{40,8},{41... | collective-permute-start | bytes 4718600 | tf_op jit(solution)/shard_map/ppermute | solution.py:67
  109.0 28.0 %collective-permute-start.35 = (bf16[384,1536]{1,0:T(8,128)(2,1)S(1)}, bf16[384,1536]{1,0:T(8,128)(2,1)S(1)}, u32[]{:S(2)}, u32[]{:S(2)}) collective-permute-start(bf16[384,1536]{1,0:T(8,128)(2,1)S(1)} %collective-permute-done.34), channel_id=1, source_target_pairs={{0,16},{1,17},{2,18},{3,19},{4,20},{5,21},{6,22},{7,23},{8,24},{9,... | collective-permute-start | bytes 3538952 | tf_op jit(solution)/shard_map/ppermute | solution.py:67
  114.1 66.0 %collective-permute-start.20 = (bf16[4,2,128,768]{3,2,1,0:T(8,128)(2,1)}, bf16[4,2,128,768]{3,2,1,0:T(8,128)(2,1)}, u32[]{:S(2)}, u32[]{:S(2)}) collective-permute-start(bf16[4,2,128,768]{3,2,1,0:T(8,128)(2,1)} %halo_pack.6), channel_id=1, source_target_pairs={{0,32},{1,33},{2,34},{3,35},{4,36},{5,37},{6,38},{7,39},{8,40},{9,... | collective-permute-start | bytes 4718600 | tf_op jit(solution)/shard_map/ppermute | solution.py:67
  121.6 69.0 %collective-permute-start.6 = (bf16[4,2,128,768]{3,2,1,0:T(8,128)(2,1)}, bf16[4,2,128,768]{3,2,1,0:T(8,128)(2,1)}, u32[]{:S(2)}, u32[]{:S(2)}) collective-permute-start(bf16[4,2,128,768]{3,2,1,0:T(8,128)(2,1)} %halo_pack.4), channel_id=1, source_target_pairs={{0,32},{1,33},{2,34},{3,35},{4,36},{5,37},{6,38},{7,39},{8,40},{9,... | collective-permute-start | bytes 4718600 | tf_op jit(solution)/shard_map/ppermute | solution.py:67
  136.5 66.5 %collective-permute-start.37 = (bf16[384,1536]{1,0:T(8,128)(2,1)S(1)}, bf16[384,1536]{1,0:T(8,128)(2,1)S(1)}, u32[]{:S(2)}, u32[]{:S(2)}) collective-permute-start(bf16[384,1536]{1,0:T(8,128)(2,1)S(1)} %bitcast.90), channel_id=1, source_target_pairs={{0,32},{1,33},{2,34},{3,35},{4,36},{5,37},{6,38},{7,39},{8,40},{9,... | collective-permute-start | bytes 3538952 | tf_op jit(solution)/shard_map/ppermute | solution.py:67
  137.0 63.3 %collective-permute-start.36 = (bf16[384,1536]{1,0:T(8,128)(2,1)S(1)}, bf16[384,1536]{1,0:T(8,128)(2,1)S(1)}, u32[]{:S(2)}, u32[]{:S(2)}) collective-permute-start(bf16[384,1536]{1,0:T(8,128)(2,1)S(1)} %collective-permute-done.35), channel_id=1, source_target_pairs={{0,16},{1,17},{2,18},{3,19},{4,20},{5,21},{6,22},{7,23},{8,24},{9,... | collective-permute-start | bytes 3538952 | tf_op jit(solution)/shard_map/ppermute | solution.py:67
  149.6 54.7 %collective-permute-start.38 = (bf16[384,1536]{1,0:T(8,128)(2,1)S(1)}, bf16[384,1536]{1,0:T(8,128)(2,1)S(1)}, u32[]{:S(2)}, u32[]{:S(2)}) collective-permute-start(bf16[384,1536]{1,0:T(8,128)(2,1)S(1)} %collective-permute-done.34), channel_id=1, source_target_pairs={{0,32},{1,33},{2,34},{3,35},{4,36},{5,37},{6,38},{7,39},{8,40},{9,... | collective-permute-start | bytes 3538952 | tf_op jit(solution)/shard_map/ppermute | solution.py:67
  180.1 30.2 %collective-permute-start.25 = (bf16[128,768]{1,0:T(8,128)(2,1)S(1)}, bf16[128,768]{1,0:T(8,128)(2,1)S(1)}, u32[]{:S(2)}, u32[]{:S(2)}) collective-permute-start(bf16[128,768]{1,0:T(8,128)(2,1)S(1)} %copy-done.33), channel_id=1, source_target_pairs={{28,0},{29,1},{30,2},{31,3},{0,4},{1,5},{2,6},{3,7},{4,8},{5,9},{6... | collective-permute-start | bytes 589832 | tf_op jit(solution)/shard_map/ppermute | solution.py:67
  190.6 22.2 %collective-permute-start.39 = (bf16[384,1536]{1,0:T(8,128)(2,1)S(1)}, bf16[384,1536]{1,0:T(8,128)(2,1)}, u32[]{:S(2)}, u32[]{:S(2)}) collective-permute-start(bf16[384,1536]{1,0:T(8,128)(2,1)S(1)} %collective-permute-done.35), channel_id=1, source_target_pairs={{0,32},{1,33},{2,34},{3,35},{4,36},{5,37},{6,38},{7,39},{8,40},{9,... | collective-permute-start | bytes 3538952 | tf_op jit(solution)/shard_map/ppermute | solution.py:67
  200.3 24.3 %collective-permute-start.40 = (bf16[384,1536]{1,0:T(8,128)(2,1)S(1)}, bf16[384,1536]{1,0:T(8,128)(2,1)S(1)}, u32[]{:S(2)}, u32[]{:S(2)}) collective-permute-start(bf16[384,1536]{1,0:T(8,128)(2,1)S(1)} %collective-permute-done.36), channel_id=1, source_target_pairs={{0,32},{1,33},{2,34},{3,35},{4,36},{5,37},{6,38},{7,39},{8,40},{9,... | collective-permute-start | bytes 3538952 | tf_op jit(solution)/shard_map/ppermute | solution.py:67
  210.4 11.2 %collective-permute-start.22 = (bf16[128,768]{1,0:T(8,128)(2,1)S(1)}, bf16[128,768]{1,0:T(8,128)(2,1)S(1)}, u32[]{:S(2)}, u32[]{:S(2)}) collective-permute-start(bf16[128,768]{1,0:T(8,128)(2,1)S(1)} %copy-done.34), channel_id=1, source_target_pairs={{1,0},{2,1},{3,2},{0,3},{5,4},{6,5},{7,6},{4,7},{9,8},{10,9},{11,1... | collective-permute-start | bytes 589832 | tf_op jit(solution)/shard_map/ppermute | solution.py:67
  211.8 12.3 %collective-permute-start.23 = (bf16[128,768]{1,0:T(8,128)(2,1)S(1)}, bf16[128,768]{1,0:T(8,128)(2,1)S(1)}, u32[]{:S(2)}, u32[]{:S(2)}) collective-permute-start(bf16[128,768]{1,0:T(8,128)(2,1)S(1)} %copy-done.32), channel_id=1, source_target_pairs={{5,0},{6,1},{7,2},{4,3},{9,4},{10,5},{11,6},{8,7},{13,8},{14,9},{1... | collective-permute-start | bytes 589832 | tf_op jit(solution)/shard_map/ppermute | solution.py:67
  212.8 11.4 %collective-permute-start.11 = (bf16[128,768]{1,0:T(8,128)(2,1)S(1)}, bf16[128,768]{1,0:T(8,128)(2,1)S(1)}, u32[]{:S(2)}, u32[]{:S(2)}) collective-permute-start(bf16[128,768]{1,0:T(8,128)(2,1)S(1)} %copy-done.24), channel_id=1, source_target_pairs={{28,0},{29,1},{30,2},{31,3},{0,4},{1,5},{2,6},{3,7},{4,8},{5,9},{6... | collective-permute-start | bytes 589832 | tf_op jit(solution)/shard_map/ppermute | solution.py:67
  224.1 8.9 %collective-permute-start.7 = (bf16[128,768]{1,0:T(8,128)(2,1)S(1)}, bf16[128,768]{1,0:T(8,128)(2,1)S(1)}, u32[]{:S(2)}, u32[]{:S(2)}) collective-permute-start(bf16[128,768]{1,0:T(8,128)(2,1)S(1)} %copy-done.27), channel_id=1, source_target_pairs={{4,0},{5,1},{6,2},{7,3},{8,4},{9,5},{10,6},{11,7},{12,8},{13,9},{1... | collective-permute-start | bytes 589832 | tf_op jit(solution)/shard_map/ppermute | solution.py:67
  224.6 11.2 %collective-permute-start.9 = (bf16[128,768]{1,0:T(8,128)(2,1)S(1)}, bf16[128,768]{1,0:T(8,128)(2,1)S(1)}, u32[]{:S(2)}, u32[]{:S(2)}) collective-permute-start(bf16[128,768]{1,0:T(8,128)(2,1)S(1)} %copy-done.25), channel_id=1, source_target_pairs={{5,0},{6,1},{7,2},{4,3},{9,4},{10,5},{11,6},{8,7},{13,8},{14,9},{1... | collective-permute-start | bytes 589832 | tf_op jit(solution)/shard_map/ppermute | solution.py:67
  (54 other events, 563.4 us)

commit v3 on v2

v3 whole, which is shorter than its diff:
```python
import functools
import math

import jax
import jax.numpy as jnp
from jax import lax
from jax.experimental import pallas as pl
from jax.experimental.pallas import tpu as pltpu
from jax.sharding import PartitionSpec as P

D = 3072
H = 12
HS = 128
HD = 1536
F, R, C = 4, 8, 4
AXES = ("frame", "row", "col")
STEP = 2
BIG = 1e30
TILE = 384
VMEM = 56 * 1024 * 1024


def index(f, r, c):
    return ((f % F) * R + (r % R)) * C + (c % C)


def every():
    return [(f, r, c) for f in range(F) for r in range(R) for c in range(C)]


def window_pairs(half, dr, dc, back=False):
    pairs = []
    for f, r, c in every():
        step = 1 if (f + half) % 2 == 0 else -1
        here, there = index(f, r, c), index(f, r + step * dr, c + step * dc)
        pairs.append((there, here) if back else (here, there))
    return pairs


def frame_pairs(step):
    return [(index(f, r, c), index(f + step, r, c)) for f, r, c in every() if 0 <= f + step < F]


def core_pairs():
    return [(index(f, r, c), index(f ^ 1, r, c)) for f, r, c in every()]


def depth_pairs():
    pairs = []
    for f, r, c in every():
        zhi, core = divmod(f, 2)
        zlo, x = divmod(r, 4)
        z = (zhi * 2 + zlo + (1 if core == 0 else -1)) % 4
        pairs.append((index(f, r, c), index((z // 2) * 2 + core, (z % 2) * 4 + x, c)))
    return pairs


def send(value, pairs):
    return lax.ppermute(value, AXES, pairs)


MOVES = ((0, 0), (1, 0), (0, 1), (1, 1))


def after(value, *first):
    return lax.optimization_barrier((value, *first))[0]


def sign_of(half, frame):
    return lax.rem(frame + half, 2)


def relay(moves, sems):
    inward = [pltpu.make_async_copy(src, held, sems.at[0, n]) for n, (src, held, _) in enumerate(moves)]
    outward = [pltpu.make_async_copy(held, dst, sems.at[1, n]) for n, (_, held, dst) in enumerate(moves)]
    for copy in inward:
        copy.start()
    for arrives, leaves in zip(inward, outward):
        arrives.wait()
        leaves.start()
    for copy in outward:
        copy.wait()


def pack_kernel(parts, meta, k_ref, v_ref, q_ref, *rest):
    outs, held, sems = rest[: len(parts)], rest[-2], rest[-1]
    moves = []
    for out, (half, piece, names) in zip(outs, parts):
        s = sign_of(half, meta[0])
        a, b = MOVES[piece]
        i = s + a * (1 - 2 * s)
        j = s + b * (1 - 2 * s)
        for n, name in enumerate(names):
            src = {"k": k_ref, "v": v_ref, "q": q_ref}[name]
            moves.append((src.at[pl.ds(2 * half, 2), i, :, j], held.at[len(moves)], out.at[n]))
    relay(moves, sems)


def pack(parts, meta, k, v, q):
    any_spec = pl.BlockSpec(memory_space=pl.ANY)
    count = sum(len(names) for _, _, names in parts)
    outs = pl.pallas_call(
        functools.partial(pack_kernel, parts),
        out_shape=[jax.ShapeDtypeStruct((len(names), 2, 8, 8, HD), jnp.bfloat16) for _, _, names in parts],
        in_specs=[pl.BlockSpec(memory_space=pltpu.SMEM)] + [any_spec] * 3,
        out_specs=[any_spec] * len(parts),
        scratch_shapes=[pltpu.VMEM((count, 2, 8, 8, HD), jnp.bfloat16), pltpu.SemaphoreType.DMA((2, count))],
        compiler_params=pltpu.CompilerParams(vmem_limit_bytes=VMEM),
        cost_estimate=pl.CostEstimate(flops=0, bytes_accessed=count * 2**20, transcendentals=0),
        name="pack",
    )(meta, k, v, q)
    return [o.reshape(-1, 128, HD) for o in outs]


def halo_kernel(*refs):
    srcs, out, held, sems = refs[:-3], refs[-3], refs[-2], refs[-1]
    relay([(src.at[pl.ds(0, 2)], held.at[n], out.at[n]) for n, src in enumerate(srcs)], sems)


def halo_pack(*pieces):
    any_spec = pl.BlockSpec(memory_space=pl.ANY)
    count = len(pieces)
    return pl.pallas_call(
        halo_kernel,
        out_shape=jax.ShapeDtypeStruct((count, 2, 128, HD), jnp.bfloat16),
        in_specs=[any_spec] * count,
        out_specs=any_spec,
        scratch_shapes=[pltpu.VMEM((count, 2, 128, HD), jnp.bfloat16), pltpu.SemaphoreType.DMA((2, count))],
        compiler_params=pltpu.CompilerParams(vmem_limit_bytes=VMEM),
        cost_estimate=pl.CostEstimate(flops=0, bytes_accessed=count * 3 * 2**19, transcendentals=0),
        name="halo_pack",
    )(*pieces)


def features(half, meta, kaug, qaug, alive):
    f, r, c, live_rows = (meta[n] for n in range(4))
    s = sign_of(half, f)
    stay = 2 * r + s
    moved = lax.rem(stay + 2 * s + 15, 16)
    row_split = r == s * (R - 1)
    col_split = c == s * (C - 1)
    missing = f == half * (F - 1)

    def places(count):
        token = lax.broadcasted_iota(jnp.int32, (count, HS), 0)
        lane = lax.broadcasted_iota(jnp.int32, (count, HS), 1)
        piece = (token // 128) % 4
        row = jnp.where(piece % 2 == 1, moved, stay) * 8 + (token // 8) % 8
        return token, lane, piece, row < live_rows

    token, lane, piece, live = places(1024)
    dead = (lane == 4) & jnp.logical_not(live)
    on = (lane == piece) | dead | ((lane == 5) & (token >= 512))
    kaug[:, HS:] = jnp.where(on, 1.0, 0.0).astype(jnp.bfloat16)
    token, lane, piece, live = places(512)
    rows_apart = (lane % 2 != piece % 2) & row_split
    cols_apart = (lane // 2 != piece // 2) & col_split
    off = ((lane < 4) & (rows_apart | cols_apart)) | (lane == 4) | ((lane == 5) & missing)
    qaug[:, HS:] = jnp.where(off, -BIG, 0.0).astype(jnp.bfloat16)
    alive[...] = jnp.where(live, 1.0, 0.0)


def attend_kernel(half, meta, skv, sq, x, y, dkv, dq, h0, hxy, hd, o0, o1, o2, o3, kaug, vaug, qaug, alive):
    outs = (o0, o1, o2, o3)

    @pl.when(pl.program_id(0) == 0)
    def _():
        features(half, meta, kaug.at[0], qaug.at[0], alive)
        for n in range(1, STEP):
            kaug[n, :, HS:] = kaug[0, :, HS:]
            qaug[n, :, HS:] = qaug[0, :, HS:]
        vaug[:, :, HS:] = jnp.ones((STEP, 1024, HS), jnp.bfloat16)

    keys = (skv, x, y, dkv, h0, hxy.at[0], hxy.at[1], hd)
    asks = (sq.at[0], x.at[2], y.at[2], dq.at[0])
    for h in range(STEP):
        lanes = pl.ds(h * HS, HS)
        for n, ref in enumerate(keys):
            kaug[h, pl.ds(n * 128, 128), :HS] = ref[0, :, lanes]
            vaug[h, pl.ds(n * 128, 128), :HS] = ref[1, :, lanes]
        for n, ref in enumerate(asks):
            qaug[h, pl.ds(n * 128, 128), :HS] = ref[:, lanes]
    scale = math.log2(math.e) / math.sqrt(HS)

    def score(at):
        h, part = divmod(at, 2)
        return lax.dot_general(
            qaug[h, pl.ds(part * 256, 256), :], kaug[h], (((1,), (1,)), ((), ())), preferred_element_type=jnp.float32
        )

    scores = score(0)
    for at in range(2 * STEP):
        later = score(at + 1) if at + 1 < 2 * STEP else None
        h, part = divmod(at, 2)
        lanes = pl.ds(h * HS, HS)
        top = jnp.max(scores, axis=1, keepdims=True)
        weights = jnp.exp2((scores - top) * scale).astype(jnp.bfloat16)
        mixed = jnp.dot(weights, vaug[h], preferred_element_type=jnp.float32)
        result = (mixed[:, :HS] / mixed[:, HS:] * alive[pl.ds(part * 256, 256), :]).astype(jnp.bfloat16)
        outs[2 * part][:, lanes] = result[:128]
        outs[2 * part + 1][:, lanes] = result[128:]
        scores = later


def attend(half, meta, *pieces):
    width = STEP * HS

    def spec(piece):
        lead = piece.shape[:-1]
        return pl.BlockSpec((*lead, width), lambda h: (0,) * len(lead) + (h,))

    return pl.pallas_call(
        functools.partial(attend_kernel, half),
        grid=(H // STEP,),
        out_shape=[jax.ShapeDtypeStruct((128, HD), jnp.bfloat16)] * 4,
        in_specs=[pl.BlockSpec(memory_space=pltpu.SMEM)] + [spec(piece) for piece in pieces],
        out_specs=[pl.BlockSpec((128, width), lambda h: (0, h))] * 4,
        scratch_shapes=[
            pltpu.VMEM((STEP, 1024, 2 * HS), jnp.bfloat16),
            pltpu.VMEM((STEP, 1024, 2 * HS), jnp.bfloat16),
            pltpu.VMEM((STEP, 512, 2 * HS), jnp.bfloat16),
            pltpu.VMEM((512, HS), jnp.float32),
        ],
        compiler_params=pltpu.CompilerParams(vmem_limit_bytes=VMEM),
        cost_estimate=pl.CostEstimate(flops=H * 4 * 512 * 1024 * 256, bytes_accessed=10 * 2**20, transcendentals=H * 2**19),
        name="attend",
    )(meta, *pieces)


def project_kernel(meta, places, *refs):
    attended, (c0, c1, c2, c3, near, far), (tokens, out, lhs, held, sems) = refs[:8], refs[8:14], refs[14:]
    chunks = (c0, c1, c2, c3, near.at[0], near.at[1], near.at[2], far)
    step = pl.program_id(0)

    def fetch(n):
        return pltpu.make_async_copy(chunks[n], held.at[n % 2], sems.at[n % 2])

    @pl.when(step == 0)
    def _():
        fetch(0).start()
        for half in range(2):
            s = sign_of(half, meta[0])
            for piece, (a, b) in enumerate(MOVES):
                i = s + a * (1 - 2 * s)
                j = s + b * (1 - 2 * s)
                lhs[half * 4 + i * 2 + j] = attended[half * 4 + piece][...]

    for n in range(8):

        @pl.when(step == n)
        def _():
            fetch(n).wait()
            if n < 7:
                fetch(n + 1).start()

    total = lax.dot_general(
        lhs[...].reshape(1024, HD), held[lax.rem(step, 2)], (((1,), (1,)), ((), ())), preferred_element_type=jnp.float32
    ).reshape(2, 2, 2, 2, 8, 8, TILE)
    for half in range(2):
        for i in range(2):
            block = jnp.concatenate([total[half, i, 0], total[half, i, 1]], axis=2)
            at = (slice(2 * half, 2 * half + 2), slice(8 * i, 8 * i + 8))
            out[at] = (block + tokens[at].astype(jnp.float32)).astype(jnp.bfloat16)


def project(attended, meta, places, chunks, tokens):
    grid_spec = pltpu.PrefetchScalarGridSpec(
        num_scalar_prefetch=2,
        grid=(D // TILE,),
        in_specs=[pl.BlockSpec((128, HD), lambda t, m, p: (0, 0))] * 8
        + [pl.BlockSpec(memory_space=pl.ANY)] * 6
        + [pl.BlockSpec((4, 16, 16, TILE), lambda t, m, p: (0, 0, 0, p[t]))],
        out_specs=pl.BlockSpec((4, 16, 16, TILE), lambda t, m, p: (0, 0, 0, p[t])),
        scratch_shapes=[
            pltpu.VMEM((8, 128, HD), jnp.bfloat16),
            pltpu.VMEM((2, TILE, HD), jnp.bfloat16),
            pltpu.SemaphoreType.DMA((2,)),
        ],
    )
    return pl.pallas_call(
        project_kernel,
        grid_spec=grid_spec,
        out_shape=jax.ShapeDtypeStruct((4, 16, 16, D), jnp.bfloat16),
        compiler_params=pltpu.CompilerParams(vmem_limit_bytes=VMEM),
        cost_estimate=pl.CostEstimate(flops=2 * 1024 * HD * D, bytes_accessed=25 * 2**20, transcendentals=0),
        name="project",
    )(meta, places, *attended, *chunks, tokens)


def plane_groups():
    return [[index(f, zlo * 4 + x, c) for x in range(4) for c in range(C)] for f in range(F) for zlo in range(2)]


def weight_places(f, r):
    core, z = f % 2, (f // 2) * 2 + r // 4
    places = []
    for k in (core, 1 - core):
        for n in range(4):
            at = (z + n * (2 * k - 1) + 4) % 4
            places.append(((at // 2) * 2 + k) * 2 + at % 2)
    return jnp.stack(places).astype(jnp.int32)


def local(tokens_in, queries, key_rows, value_rows, out_weight, row_valid):
    f, r, c = (lax.axis_index(a) for a in AXES)
    meta = jnp.stack([f, r, c, jnp.sum(row_valid)]).astype(jnp.int32)
    split = lambda a: a.reshape(4, 2, 8, 2, 8, HD)
    arrays = (meta, split(key_rows), split(value_rows), split(queries))
    chunk = lax.all_gather(out_weight.T, AXES, axis=0, tiled=True, axis_index_groups=plane_groups())

    row, col, both = MOVES[1:]
    go = lambda value, half, move: send(value, window_pairs(half, *move))
    skv0, skv1, x0, y0 = pack(((0, 0, "kv"), (1, 0, "kv"), (0, 1, "kvq"), (0, 2, "kvq")), *arrays)
    up0, down0 = send(skv1, frame_pairs(1)), send(skv0, frame_pairs(-1))
    x0, y0 = go(x0, 0, row), go(y0, 0, col)
    x1, y1, dkv0, dkv1, dq0, dq1, sq0, sq1 = pack(
        ((1, 1, "kvq"), (1, 2, "kvq"), (0, 3, "kv"), (1, 3, "kv"), (0, 3, "q"), (1, 3, "q"), (0, 0, "q"), (1, 0, "q")), *arrays
    )
    x1, y1 = go(after(x1, up0), 1, row), go(after(y1, down0), 1, col)
    down1 = send(halo_pack(x0, y0), frame_pairs(-1))
    dkv0, dkv1 = go(after(dkv0, x1), 0, both), go(after(dkv1, y1), 1, both)
    up1 = send(halo_pack(x1, y1), frame_pairs(1))
    dq0, dq1 = go(after(dq0, dkv0), 0, both), go(after(dq1, dkv1), 1, both)
    down2, up2 = send(dkv0, frame_pairs(-1)), send(dkv1, frame_pairs(1))

    ring = [after(chunk, up2)]
    for _ in range(3):
        ring.append(send(ring[-1], depth_pairs()))
    near = send(jnp.stack(ring[:3]), core_pairs())
    far = send(ring[3], core_pairs())

    mixed1 = attend(1, meta, skv1, sq1, x1, y1, dkv1, dq1, down0, down1, down2)
    mixed0 = attend(0, meta, skv0, sq0, x0, y0, dkv0, dq0, up0, up1, up2)
    attended = []
    for half, mixed in enumerate((mixed0, mixed1)):
        attended += [mixed[0]] + [send(mixed[n], window_pairs(half, *MOVES[n], back=True)) for n in (1, 2, 3)]
    return project(attended, meta, weight_places(f, r), (*ring, near, far), tokens_in)


def solution(mesh):
    return jax.shard_map(
        local,
        mesh=mesh,
        in_specs=(
            P("frame", "row", "col", None),
            P("frame", "row", "col", None),
            P("frame", "row", "col", None),
            P("frame", "row", "col", None),
            P(None, ("frame", "row", "col")),
            P(),
        ),
        out_specs=P("frame", "row", "col", None),
        check_vma=False,
    )
```

time: 258 us -> 270 us (1.047)
  waiting for transfers between devices: 50.9 us -> 134 us
  starting transfers between devices: 95.6 us -> 49.3 us
  local copies, waits for them, and re-layouts: 22.8 us -> 6.59 us
  Pallas kernels: 77.1 us -> 62 us
  between operations: 1.01 us -> 13.6 us
  other arithmetic: 8.48 us -> 2.97 us
    ppermute x41 -> x25, waiting for transfers between devices: 50.9 us -> 120 us  [send(): return lax.ppermute(value, AXES, pairs)]
    ppermute x41 -> x25, starting transfers between devices: 95.6 us -> 49.3 us  [send(): return lax.ppermute(value, AXES, pairs)]
    pallas_call x13 -> x7, Pallas kernels: 77.1 us -> 62 us  [the longest x2 27.3 us: attend(): pl.pallas_call(functools.partial(attend_kernel, half), grid=(H // STEP,),...]
    all_gather x0 -> x1, waiting for transfers between devices: none -> 13.8 us  [local(): lax.all_gather(out_weight.T, AXES, axis=0, tiled=True, axis_index_groups=...]
    unnamed x109 -> x32, local copies, waits for them, and re-layouts: 11.8 us -> 5.9 us
    convert_element_type x4 -> x0, other arithmetic: 4.65 us -> none  [the longest x2 3.27 us: masks(): kf = jnp.concatenate([own, own | (lane == 5)]).astype(jnp.bfloat16)]
    broadcast_in_dim x6 -> x0, local copies, waits for them, and re-layouts: 3.8 us -> none  [the longest x4 2.15 us: masks(): jnp.broadcast_to(live[:, None, :, None], (4, 2, 8, 8)).reshape(512, 1)]
  transfers between devices with their start and end apart: 41 -> 26, of which waited for: 11 -> 14; matrix products, arithmetic and copies ran while one was open for 11% -> 0% of each run, Pallas kernels for 23% -> 14%
where the time goes in v3:
time: 270 us; the launch traced here: 268 us
  waiting for transfers between devices  134 us (50%)
  Pallas kernels  62 us (23%)
  starting transfers between devices  49.3 us (18%)
  between operations  13.6 us (5%)
  local copies, waits for them, and re-layouts  6.59 us (2%)
  other arithmetic  2.97 us (1%)
    ppermute x25, waiting for transfers between devices, send(): return lax.ppermute(value, AXES, pairs)  120 us
    ppermute x25, starting transfers between devices, send(): return lax.ppermute(value, AXES, pairs)  49.3 us
    pallas_call x2, Pallas kernels, attend(): pl.pallas_call(functools.partial(attend_kernel, half), grid=(H // STEP,),...  27.3 us
    pallas_call x1, Pallas kernels, project(): pl.pallas_call(project_kernel, grid_spec=grid_spec, out_shape=jax.ShapeDt...  20.1 us
    all_gather x1, waiting for transfers between devices, local(): lax.all_gather(out_weight.T, AXES, axis=0, tiled=True, axis_index_groups=...  13.8 us
    pallas_call x2, Pallas kernels, pack(): pl.pallas_call(functools.partial(pack_kernel, parts), out_shape=[jax.Shap...  9.92 us
    unnamed x32, local copies, waits for them, and re-layouts  5.9 us
  transfers between devices with their start and end apart: 26, of which 14 were waited for; matrix products, arithmetic and copies ran while one was open for 0% of the time, Pallas kernels for 14%

profile of v3, /device:TPU:1, one launch (start us, length us, event | category | flops | bytes accessed | tf_op | source)
XLA Modules:
  0.0 268.5 jit_solution(655479359049052651)
XLA Ops:
  9.1 4.1 %pack.2 = (bf16[2,2,8,8,1536]{4,3,2,1,0:T(8,128)(2,1)}, bf16[2,2,8,8,1536]{4,3,2,1,0:T(8,128)(2,1)}, bf16[3,2,8,8,1536]{4,3,2,1,0:T(8,128)(2,1)}, bf16[3,2,8,8,1536]{4,3,2,1,0:T(8,128)(2,1)}) custom-call(s32[4]{0:T(128)} %pad_add_fusion.meta, bf16[4,2,8,2,8,1536]{5,4,3,2,1,0:T(8,128)(2,1)} %bitcast.31, bf16[4,2,8,2,8,1536]{5,4,3,2,1,0:T(8,128)(2,1)} %bitcast.33, ...), custom_call_target="tpu_custom_call" | custom-call | bytes 10485760 | tf_op jit(solution)/shard_map/pack/pallas_call | solution.py:102
  13.2 3.5 %collective-permute-start.6 = (bf16[2,128,1536]{2,1,0:T(8,128)(2,1)}, bf16[2,128,1536]{2,1,0:T(8,128)(2,1)S(1)}, u32[]{:S(2)}, u32[]{:S(2)}) collective-permute-start(bf16[2,128,1536]{2,1,0:T(8,128)(2,1)} %bitcast.44), channel_id=1, source_target_pairs={{32,0},{33,1},{34,2},{35,3},{36,4},{37,5},{38,6},{39,7},{40,8},{41... | collective-permute-start | bytes 2359304 | tf_op jit(solution)/shard_map/ppermute | solution.py:59
  16.7 5.8 %pack.3 = (bf16[3,2,8,8,1536]{4,3,2,1,0:T(8,128)(2,1)}, bf16[3,2,8,8,1536]{4,3,2,1,0:T(8,128)(2,1)}, bf16[2,2,8,8,1536]{4,3,2,1,0:T(8,128)(2,1)}, bf16[2,2,8,8,1...) custom-call(s32[4]{0:T(128)} %pad_add_fusion.meta, ...), custom_call_target="tpu_custom_call" | custom-call | bytes 14680064 | tf_op jit(solution)/shard_map/pack/pallas_call | solution.py:102
  22.5 7.6 %collective-permute-done.6.h0 = bf16[2,128,1536]{2,1,0:T(8,128)(2,1)S(1)} collective-permute-done((bf16[2,128,1536]{2,1,0:T(8,128)(2,1)}, bf16[2,128,1536]{2,1,0:T(8,128)(2,1)S(1)}, u32[]{:S(2)}, u32[]{:S(2)}) %collective-permute-start.6) | collective-permute-done | bytes 786464 | tf_op jit(solution)/shard_map/ppermute | solution.py:59
  32.3 15.9 %collective-permute-done.7.refs_1_.y = bf16[3,128,1536]{2,1,0:T(8,128)(2,1)S(1)} collective-permute-done((bf16[3,128,1536]{2,1,0:T(8,128)(2,1)}, bf16[3,128,1536]{2,1,0:T(8,128)(2,1)S(1)}, u32[]{:S(2)}, u32[]{:S(2)}) %collective-permute-start.7) | collective-permute-done | bytes 1179680 | tf_op jit(solution)/shard_map/ppermute | solution.py:59
  49.3 14.4 %collective-permute-done.9.dkv = bf16[2,128,1536]{2,1,0:T(8,128)(2,1)} collective-permute-done((bf16[2,128,1536]{2,1,0:T(8,128)(2,1)}, bf16[2,128,1536]{2,1,0:T(8,128)(2,1)}, u32[]{:S(2)}, u32[]{:S(2)}) %collective-permute-start.9) | collective-permute-done | bytes 786464 | tf_op jit(solution)/shard_map/ppermute | solution.py:59
  63.7 3.3 %collective-permute-start.10 = (bf16[2,128,1536]{2,1,0:T(8,128)(2,1)}, bf16[2,128,1536]{2,1,0:T(8,128)(2,1)S(1)}, u32[]{:S(2)}, u32[]{:S(2)}) collective-permute-start(bf16[2,128,1536]{2,1,0:T(8,128)(2,1)} %collective-permute-done.9.dkv), channel_id=1, source_target_pairs={{0,32},{1,33},{2,34},{3,35},{4,36},{5,37},{6,38},{7,39},{8,40},{9,... | collective-permute-start | bytes 2359304 | tf_op jit(solution)/shard_map/ppermute | solution.py:59
  67.0 13.8 %all-gather.2.cloned.1.call-done.refs_8_ = bf16[384,1536]{1,0:T(8,128)(2,1)} async-done(((bf16[24,1536]{1,0:T(8,128)(2,1)}), bf16[384,1536]{1,0:T(8,128)(2,1)}) %all-gather.2.cloned.1.call-update) | async-done | bytes 1179664 | tf_op jit(solution)/shard_map/all_gather | solution.py:309
  80.8 2.7 collective-permute-start.20
  83.4 4.8 %collective-permute-start.2 = (bf16[2,128,1536]{2,1,0:T(8,128)(2,1)}, bf16[2,128,1536]{2,1,0:T(8,128)(2,1)S(1)}, u32[]{:S(2)}, u32[]{:S(2)}) collective-permute-start(bf16[2,128,1536]{2,1,0:T(8,128)(2,1)} %bitcast.21.skv), channel_id=1, source_target_pairs={{0,32},{1,33},{2,34},{3,35},{4,36},{5,37},{6,38},{7,39},{8,40},{9,... | collective-permute-start | bytes 2359304 | tf_op jit(solution)/shard_map/ppermute | solution.py:59
  90.3 18.4 %collective-permute-done.20.refs_9_ = bf16[384,1536]{1,0:T(8,128)(2,1)S(1)} collective-permute-done((bf16[384,1536]{1,0:T(8,128)(2,1)}, bf16[384,1536]{1,0:T(8,128)(2,1)S(1)}, u32[]{:S(2)}, u32[]{:S(2)}) %collective-permute-start.20) | collective-permute-done | bytes 1179680 | tf_op jit(solution)/shard_map/ppermute | solution.py:59
  108.7 1.4 collective-permute-start.21
  110.0 8.6 %collective-permute-done.2.h0 = bf16[2,128,1536]{2,1,0:T(8,128)(2,1)S(1)} collective-permute-done((bf16[2,128,1536]{2,1,0:T(8,128)(2,1)}, bf16[2,128,1536]{2,1,0:T(8,128)(2,1)S(1)}, u32[]{:S(2)}, u32[]{:S(2)}) %collective-permute-start.2) | collective-permute-done | bytes 786464 | tf_op jit(solution)/shard_map/ppermute | solution.py:59
  121.6 2.3 halo_pack.3
  123.9 5.7 %collective-permute-start.15 = (bf16[2,2,128,1536]{3,2,1,0:T(8,128)(2,1)}, bf16[2,2,128,1536]{3,2,1,0:T(8,128)(2,1)}, u32[]{:S(2)}, u32[]{:S(2)}) collective-permute-start(bf16[2,2,128,1536]{3,2,1,0:T(8,128)(2,1)} %halo_pack.3), channel_id=1, source_target_pairs={{32,0},{33,1},{34,2},{35,3},{36,4},{37,5},{38,6},{39,7},{40,8},{41... | collective-permute-start | bytes 4718600 | tf_op jit(solution)/shard_map/ppermute | solution.py:59
  129.6 12.8 %collective-permute-done.21.refs_10_ = bf16[384,1536]{1,0:T(8,128)(2,1)S(1)} collective-permute-done((bf16[384,1536]{1,0:T(8,128)(2,1)S(1)}, bf16[384,1536]{1,0:T(8,128)(2,1)S(1)}, u32[]{:S(2)}, u32[]{:S(2)}) %collective-permute-start.21) | collective-permute-done | bytes 1179680 | tf_op jit(solution)/shard_map/ppermute | solution.py:59
  142.9 4.3 %collective-permute-start.23 = (bf16[3,384,1536]{2,1,0:T(8,128)(2,1)S(1)}, bf16[3,384,1536]{2,1,0:T(8,128)(2,1)}, u32[]{:S(2)}, u32[]{:S(2)}) collective-permute-start(bf16[3,384,1536]{2,1,0:T(8,128)(2,1)S(1)} %pad_maximum_fusion), channel_id=1, source_target_pairs={{0,32},{1,33},{2,34},{3,35},{4,36},{5,37},{6,38},{7,39},{8,40},{9,... | collective-permute-start | bytes 10616840 | tf_op jit(solution)/shard_map/ppermute | solution.py:59
  147.2 5.5 %collective-permute-start.4 = (bf16[2,128,1536]{2,1,0:T(8,128)(2,1)S(1)}, bf16[2,128,1536]{2,1,0:T(8,128)(2,1)S(1)}, u32[]{:S(2)}, u32[]{:S(2)}) collective-permute-start(bf16[2,128,1536]{2,1,0:T(8,128)(2,1)S(1)} %bitcast.46), channel_id=1, source_target_pairs={{0,5},{1,6},{2,7},{3,4},{4,9},{5,10},{6,11},{7,8},{8,13},{9,14},{1... | collective-permute-start | bytes 2359304 | tf_op jit(solution)/shard_map/ppermute | solution.py:59
  152.6 2.3 halo_pack.2
  154.9 1.9 collective-permute-start.8
  156.9 4.7 %collective-permute-done.4.dkv = bf16[2,128,1536]{2,1,0:T(8,128)(2,1)S(1)} collective-permute-done((bf16[2,128,1536]{2,1,0:T(8,128)(2,1)S(1)}, bf16[2,128,1536]{2,1,0:T(8,128)(2,1)S(1)}, u32[]{:S(2)}, u32[]{:S(2)}) %collective-permute-start.4) | collective-permute-done | bytes 786464 | tf_op jit(solution)/shard_map/ppermute | solution.py:59
  161.6 4.8 %collective-permute-start.16 = (bf16[2,128,1536]{2,1,0:T(8,128)(2,1)S(1)}, bf16[2,128,1536]{2,1,0:T(8,128)(2,1)S(1)}, u32[]{:S(2)}, u32[]{:S(2)}) collective-permute-start(bf16[2,128,1536]{2,1,0:T(8,128)(2,1)S(1)} %collective-permute-done.4.dkv), channel_id=1, source_target_pairs={{32,0},{33,1},{34,2},{35,3},{36,4},{37,5},{38,6},{39,7},{40,8},{41... | collective-permute-start | bytes 2359304 | tf_op jit(solution)/shard_map/ppermute | solution.py:59
  167.3 25.6 %collective-permute-done.14.dq = bf16[1,128,1536]{2,1,0:T(8,128)(2,1)S(1)} collective-permute-done((bf16[1,128,1536]{2,1,0:T(8,128)(2,1)}, bf16[1,128,1536]{2,1,0:T(8,128)(2,1)S(1)}, u32[]{:S(2)}, u32[]{:S(2)}) %collective-permute-start.14) | collective-permute-done | bytes 393248 | tf_op jit(solution)/shard_map/ppermute | solution.py:59
  193.0 2.3 collective-permute-start.5
  195.2 1.4 collective-permute-done.16.hd
  197.6 13.7 %attend.3 = (bf16[128,1536]{1,0:T(8,128)(2,1)}, bf16[128,1536]{1,0:T(8,128)(2,1)}, bf16[128,1536]{1,0:T(8,128)(2,1)}, bf16[128,1536]{1,0:T(8,128)(2,1)}) custom-call(s32[4]{0:T(128)} %pad_add_fusion.meta, bf16[2,128,1536]{2,1,0:T(8,128)(2,1)} %bitcast.21.skv, bf16[1,128,1536]{2,1,0:T(8,128)(2,1)} %bitcast.50, ...), custom_call_target="tpu_custom_call" | custom-call | flops 6442450944 | bytes 10485760 | tf_op jit(solution)/shard_map/attend/pallas_call | solution.py:212
  211.4 1.9 collective-permute-start.18
  214.5 13.6 %attend.2 = (bf16[128,1536]{1,0:T(8,128)(2,1)}, bf16[128,1536]{1,0:T(8,128)(2,1)}, bf16[128,1536]{1,0:T(8,128)(2,1)}, bf16[128,1536]{1,0:T(8,128)(2,1)}) custom-call(s32[4]{0:T(128)} %pad_add_fusion.meta, bf16[2,128,1536]{2,1,0:T(8,128)(2,1)} %bitcast.45, bf16[1,128,1536]{2,1,0:T(8,128)(2,1)} %bitcast.48, bf16[3,128,1536]{2,1,0:T(8,128)(2,1)} %copy-done.4, ...), custom_call_target="tpu_custom_call" | custom-call | flops 6442450944 | bytes 10485760 | tf_op jit(solution)/shard_map/attend/pallas_call | solution.py:212
  228.2 1.4 collective-permute-start.11
  231.6 5.9 %collective-permute-done.11.refs_1_ = bf16[128,1536]{1,0:T(8,128)(2,1)} collective-permute-done((bf16[128,1536]{1,0:T(8,128)(2,1)}, bf16[128,1536]{1,0:T(8,128)(2,1)}, u32[]{:S(2)}, u32[]{:S(2)}) %collective-permute-start.11) | collective-permute-done | bytes 393248 | tf_op jit(solution)/shard_map/ppermute | solution.py:59
  237.9 3.6 %collective-permute-done.13.refs_3_ = bf16[128,1536]{1,0:T(8,128)(2,1)} collective-permute-done((bf16[128,1536]{1,0:T(8,128)(2,1)}, bf16[128,1536]{1,0:T(8,128)(2,1)}, u32[]{:S(2)}, u32[]{:S(2)}) %collective-permute-start.13) | collective-permute-done | bytes 393248 | tf_op jit(solution)/shard_map/ppermute | solution.py:59
  241.5 20.1 %project.1 = bf16[4,16,16,3072]{3,2,1,0:T(8,128)(2,1)} custom-call(s32[4]{0:T(128)} %pad_add_fusion.meta, s32[8]{0:T(128)} %stack.67.places, bf16[128,1536]{1,0:T(8,128)(2,1)} %get-tuple-element.47.refs_0_, bf16[128,1536]{1,0:T(8,128)(2,1)} %collective-permute-done.11.refs_1_, bf16[128,1536]{1,0:T(8,128)(2,1)} %collective-permute-done.12.refs_2_, ...), custom_call_target="tpu_custom_call" | custom-call | flops 9663676416 | bytes 26214400 | tf_op jit(solution)/shard_map/project/pallas_call | solution.py:280
  (64 shorter events, 16.9 us)
Async XLA Ops:
  6.5 74.2 %all-gather.2.cloned.1.call-start = ((), (), s32[]{:S(2)}) async-start(), calls=%async_computation | async-start | bytes 1253376 | tf_op jit(solution)/shard_map/all_gather | solution.py:309
  13.2 76.3 %copy-start.7 = (bf16[3,2,8,8,1536]{4,3,2,1,0:T(8,128)(2,1)S(1)}, bf16[3,2,8,8,1536]{4,3,2,1,0:T(8,128)(2,1)}, u32[]{:S(2)}) copy-start(bf16[3,2,8,8,1536]{4,3,2,1,0:T(8,128)(2,1)} %get-tuple-element.35) | copy-start | bytes 3538948
  13.2 16.9 %collective-permute-start.6 = (bf16[2,128,1536]{2,1,0:T(8,128)(2,1)}, bf16[2,128,1536]{2,1,0:T(8,128)(2,1)S(1)}, u32[]{:S(2)}, u32[]{:S(2)}) collective-permute-start(bf16[2,128,1536]{2,1,0:T(8,128)(2,1)} %bitcast.44), channel_id=1, source_target_pairs={{32,0},{33,1},{34,2},{35,3},{36,4},{37,5},{38,6},{39,7},{40,8},{41... | collective-permute-start | bytes 2359304 | tf_op jit(solution)/shard_map/ppermute | solution.py:59
  31.0 17.2 %collective-permute-start.7 = (bf16[3,128,1536]{2,1,0:T(8,128)(2,1)}, bf16[3,128,1536]{2,1,0:T(8,128)(2,1)S(1)}, u32[]{:S(2)}, u32[]{:S(2)}) collective-permute-start(bf16[3,128,1536]{2,1,0:T(8,128)(2,1)} %bitcast.43), channel_id=1, source_target_pairs={{0,3},{1,0},{2,1},{3,2},{4,7},{5,4},{6,5},{7,6},{8,11},{9,8},{10,9... | collective-permute-start | bytes 3538952 | tf_op jit(solution)/shard_map/ppermute | solution.py:59
  48.2 75.7 %copy-start.3 = (bf16[3,128,1536]{2,1,0:T(8,128)(2,1)}, bf16[3,128,1536]{2,1,0:T(8,128)(2,1)S(1)}, u32[]{:S(2)}) copy-start(bf16[3,128,1536]{2,1,0:T(8,128)(2,1)S(1)} %collective-permute-done.7.refs_1_.y) | copy-start | bytes 3538948
  48.2 15.5 %collective-permute-start.9 = (bf16[2,128,1536]{2,1,0:T(8,128)(2,1)}, bf16[2,128,1536]{2,1,0:T(8,128)(2,1)}, u32[]{:S(2)}, u32[]{:S(2)}) collective-permute-start(bf16[2,128,1536]{2,1,0:T(8,128)(2,1)} %bitcast.47), channel_id=1, source_target_pairs={{0,31},{1,28},{2,29},{3,30},{4,3},{5,0},{6,1},{7,2},{8,7},{9,4},{1... | collective-permute-start | bytes 2359304 | tf_op jit(solution)/shard_map/ppermute | solution.py:59
  63.7 17.0 %collective-permute-start.10 = (bf16[2,128,1536]{2,1,0:T(8,128)(2,1)}, bf16[2,128,1536]{2,1,0:T(8,128)(2,1)S(1)}, u32[]{:S(2)}, u32[]{:S(2)}) collective-permute-start(bf16[2,128,1536]{2,1,0:T(8,128)(2,1)} %collective-permute-done.9.dkv), channel_id=1, source_target_pairs={{0,32},{1,33},{2,34},{3,35},{4,36},{5,37},{6,38},{7,39},{8,40},{9,... | collective-permute-start | bytes 2359304 | tf_op jit(solution)/shard_map/ppermute | solution.py:59
  80.8 27.9 %collective-permute-start.20 = (bf16[384,1536]{1,0:T(8,128)(2,1)}, bf16[384,1536]{1,0:T(8,128)(2,1)S(1)}, u32[]{:S(2)}, u32[]{:S(2)}) collective-permute-start(bf16[384,1536]{1,0:T(8,128)(2,1)} %all-gather.2.cloned.1.call-done.refs_8_), channel_id=1, source_target_pairs={{0,16},{1,17},{2,18},{3,19},{4,20},{5,21},{6,22},{7,23},{8,24},{9,... | collective-permute-start | bytes 3538952 | tf_op jit(solution)/shard_map/ppermute | solution.py:59
  83.4 35.2 %collective-permute-start.2 = (bf16[2,128,1536]{2,1,0:T(8,128)(2,1)}, bf16[2,128,1536]{2,1,0:T(8,128)(2,1)S(1)}, u32[]{:S(2)}, u32[]{:S(2)}) collective-permute-start(bf16[2,128,1536]{2,1,0:T(8,128)(2,1)} %bitcast.21.skv), channel_id=1, source_target_pairs={{0,32},{1,33},{2,34},{3,35},{4,36},{5,37},{6,38},{7,39},{8,40},{9,... | collective-permute-start | bytes 2359304 | tf_op jit(solution)/shard_map/ppermute | solution.py:59
  88.2 30.4 %collective-permute-start = (bf16[3,128,1536]{2,1,0:T(8,128)(2,1)}, bf16[3,128,1536]{2,1,0:T(8,128)(2,1)S(1)}, u32[]{:S(2)}, u32[]{:S(2)}) collective-permute-start(bf16[3,128,1536]{2,1,0:T(8,128)(2,1)} %bitcast.17), channel_id=1, source_target_pairs={{0,4},{1,5},{2,6},{3,7},{4,8},{5,9},{6,10},{7,11},{8,12},{9,13},{1... | collective-permute-start | bytes 3538952 | tf_op jit(solution)/shard_map/ppermute | solution.py:59
  89.5 30.0 %collective-permute-start.1 = (bf16[3,128,1536]{2,1,0:T(8,128)(2,1)S(1)}, bf16[3,128,1536]{2,1,0:T(8,128)(2,1)S(1)}, u32[]{:S(2)}, u32[]{:S(2)}) collective-permute-start(bf16[3,128,1536]{2,1,0:T(8,128)(2,1)S(1)} %bitcast.42), channel_id=1, source_target_pairs={{0,1},{1,2},{2,3},{3,0},{4,5},{5,6},{6,7},{7,4},{8,9},{9,10},{10,1... | collective-permute-start | bytes 3538952 | tf_op jit(solution)/shard_map/ppermute | solution.py:59
  108.7 33.8 %copy-start.1 = (bf16[384,1536]{1,0:T(8,128)(2,1)}, bf16[384,1536]{1,0:T(8,128)(2,1)S(1)}, u32[]{:S(2)}) copy-start(bf16[384,1536]{1,0:T(8,128)(2,1)S(1)} %collective-permute-done.20.refs_9_) | copy-start | bytes 3538948
  108.7 33.7 %collective-permute-start.21 = (bf16[384,1536]{1,0:T(8,128)(2,1)S(1)}, bf16[384,1536]{1,0:T(8,128)(2,1)S(1)}, u32[]{:S(2)}, u32[]{:S(2)}) collective-permute-start(bf16[384,1536]{1,0:T(8,128)(2,1)S(1)} %collective-permute-done.20.refs_9_), channel_id=1, source_target_pairs={{0,16},{1,17},{2,18},{3,19},{4,20},{5,21},{6,22},{7,23},{8,24},{9,... | collective-permute-start | bytes 3538952 | tf_op jit(solution)/shard_map/ppermute | solution.py:59
  118.6 23.8 %copy-start = (bf16[384,1536]{1,0:T(8,128)(2,1)S(1)}, bf16[384,1536]{1,0:T(8,128)(2,1)}, u32[]{:S(2)}) copy-start(bf16[384,1536]{1,0:T(8,128)(2,1)} %all-gather.2.cloned.1.call-done.refs_8_) | copy-start | bytes 3538948
  118.6 28.6 %collective-permute-start.3 = (bf16[3,128,1536]{2,1,0:T(8,128)(2,1)}, bf16[3,128,1536]{2,1,0:T(8,128)(2,1)}, u32[]{:S(2)}, u32[]{:S(2)}) collective-permute-start(bf16[3,128,1536]{2,1,0:T(8,128)(2,1)} %bitcast.41), channel_id=1, source_target_pairs={{0,28},{1,29},{2,30},{3,31},{4,0},{5,1},{6,2},{7,3},{8,4},{9,5},{1... | collective-permute-start | bytes 3538952 | tf_op jit(solution)/shard_map/ppermute | solution.py:59
  123.9 43.4 %collective-permute-start.15 = (bf16[2,2,128,1536]{3,2,1,0:T(8,128)(2,1)}, bf16[2,2,128,1536]{3,2,1,0:T(8,128)(2,1)}, u32[]{:S(2)}, u32[]{:S(2)}) collective-permute-start(bf16[2,2,128,1536]{3,2,1,0:T(8,128)(2,1)} %halo_pack.3), channel_id=1, source_target_pairs={{32,0},{33,1},{34,2},{35,3},{36,4},{37,5},{38,6},{39,7},{40,8},{41... | collective-permute-start | bytes 4718600 | tf_op jit(solution)/shard_map/ppermute | solution.py:59
  142.9 98.6 %collective-permute-start.23 = (bf16[3,384,1536]{2,1,0:T(8,128)(2,1)S(1)}, bf16[3,384,1536]{2,1,0:T(8,128)(2,1)}, u32[]{:S(2)}, u32[]{:S(2)}) collective-permute-start(bf16[3,384,1536]{2,1,0:T(8,128)(2,1)S(1)} %pad_maximum_fusion), channel_id=1, source_target_pairs={{0,32},{1,33},{2,34},{3,35},{4,36},{5,37},{6,38},{7,39},{8,40},{9,... | collective-permute-start | bytes 10616840 | tf_op jit(solution)/shard_map/ppermute | solution.py:59
  147.2 45.8 %copy-start.14 = (bf16[1,2,8,8,1536]{4,3,2,1,0:T(8,128)(2,1)S(1)}, bf16[1,2,8,8,1536]{4,3,2,1,0:T(8,128)(2,1)}, u32[]{:S(2)}) copy-start(bf16[1,2,8,8,1536]{4,3,2,1,0:T(8,128)(2,1)} %get-tuple-element.41) | copy-start | bytes 1179652
  147.2 14.4 %collective-permute-start.4 = (bf16[2,128,1536]{2,1,0:T(8,128)(2,1)S(1)}, bf16[2,128,1536]{2,1,0:T(8,128)(2,1)S(1)}, u32[]{:S(2)}, u32[]{:S(2)}) collective-permute-start(bf16[2,128,1536]{2,1,0:T(8,128)(2,1)S(1)} %bitcast.46), channel_id=1, source_target_pairs={{0,5},{1,6},{2,7},{3,4},{4,9},{5,10},{6,11},{7,8},{8,13},{9,14},{1... | collective-permute-start | bytes 2359304 | tf_op jit(solution)/shard_map/ppermute | solution.py:59
  152.6 42.6 %collective-permute-start.22 = (bf16[384,1536]{1,0:T(8,128)(2,1)S(1)}, bf16[384,1536]{1,0:T(8,128)(2,1)}, u32[]{:S(2)}, u32[]{:S(2)}) collective-permute-start(bf16[384,1536]{1,0:T(8,128)(2,1)S(1)} %collective-permute-done.21.refs_10_), channel_id=1, source_target_pairs={{0,16},{1,17},{2,18},{3,19},{4,20},{5,21},{6,22},{7,23},{8,24},{9,... | collective-permute-start | bytes 3538952 | tf_op jit(solution)/shard_map/ppermute | solution.py:59
  154.9 58.4 %collective-permute-start.8 = (bf16[2,2,128,1536]{3,2,1,0:T(8,128)(2,1)}, bf16[2,2,128,1536]{3,2,1,0:T(8,128)(2,1)S(1)}, u32[]{:S(2)}, u32[]{:S(2)}) collective-permute-start(bf16[2,2,128,1536]{3,2,1,0:T(8,128)(2,1)} %halo_pack.2), channel_id=1, source_target_pairs={{0,32},{1,33},{2,34},{3,35},{4,36},{5,37},{6,38},{7,39},{8,40},{9,... | collective-permute-start | bytes 4718600 | tf_op jit(solution)/shard_map/ppermute | solution.py:59
  161.6 49.7 %copy-start.12 = (bf16[2,128,1536]{2,1,0:T(8,128)(2,1)}, bf16[2,128,1536]{2,1,0:T(8,128)(2,1)S(1)}, u32[]{:S(2)}) copy-start(bf16[2,128,1536]{2,1,0:T(8,128)(2,1)S(1)} %collective-permute-done.4.dkv) | copy-start | bytes 2359300
  161.6 35.1 %collective-permute-start.16 = (bf16[2,128,1536]{2,1,0:T(8,128)(2,1)S(1)}, bf16[2,128,1536]{2,1,0:T(8,128)(2,1)S(1)}, u32[]{:S(2)}, u32[]{:S(2)}) collective-permute-start(bf16[2,128,1536]{2,1,0:T(8,128)(2,1)S(1)} %collective-permute-done.4.dkv), channel_id=1, source_target_pairs={{32,0},{33,1},{34,2},{35,3},{36,4},{37,5},{38,6},{39,7},{40,8},{41... | collective-permute-start | bytes 2359304 | tf_op jit(solution)/shard_map/ppermute | solution.py:59
  167.3 25.6 %collective-permute-start.14 = (bf16[1,128,1536]{2,1,0:T(8,128)(2,1)}, bf16[1,128,1536]{2,1,0:T(8,128)(2,1)S(1)}, u32[]{:S(2)}, u32[]{:S(2)}) collective-permute-start(bf16[1,128,1536]{2,1,0:T(8,128)(2,1)} %bitcast.51), channel_id=1, source_target_pairs={{0,31},{1,28},{2,29},{3,30},{4,3},{5,0},{6,1},{7,2},{8,7},{9,4},{1... | collective-permute-start | bytes 1179656 | tf_op jit(solution)/shard_map/ppermute | solution.py:59
  193.0 18.4 %collective-permute-start.5 = (bf16[1,128,1536]{2,1,0:T(8,128)(2,1)S(1)}, bf16[1,128,1536]{2,1,0:T(8,128)(2,1)}, u32[]{:S(2)}, u32[]{:S(2)}) collective-permute-start(bf16[1,128,1536]{2,1,0:T(8,128)(2,1)S(1)} %bitcast.49), channel_id=1, source_target_pairs={{0,5},{1,6},{2,7},{3,4},{4,9},{5,10},{6,11},{7,8},{8,13},{9,14},{1... | collective-permute-start | bytes 1179656 | tf_op jit(solution)/shard_map/ppermute | solution.py:59
  195.2 46.3 %collective-permute-start.24 = (bf16[384,1536]{1,0:T(8,128)(2,1)}, bf16[384,1536]{1,0:T(8,128)(2,1)}, u32[]{:S(2)}, u32[]{:S(2)}) collective-permute-start(bf16[384,1536]{1,0:T(8,128)(2,1)} %collective-permute-done.22.refs_11_), channel_id=1, source_target_pairs={{0,32},{1,33},{2,34},{3,35},{4,36},{5,37},{6,38},{7,39},{8,40},{9,... | collective-permute-start | bytes 3538952 | tf_op jit(solution)/shard_map/ppermute | solution.py:59
  211.3 16.9 %collective-permute-start.17 = (bf16[128,1536]{1,0:T(8,128)(2,1)}, bf16[128,1536]{1,0:T(8,128)(2,1)}, u32[]{:S(2)}, u32[]{:S(2)}) collective-permute-start(bf16[128,1536]{1,0:T(8,128)(2,1)} %get-tuple-element.55), channel_id=1, source_target_pairs={{28,0},{29,1},{30,2},{31,3},{0,4},{1,5},{2,6},{3,7},{4,8},{5,9},{6... | collective-permute-start | bytes 1179656 | tf_op jit(solution)/shard_map/ppermute | solution.py:59
  211.4 18.2 %collective-permute-start.18 = (bf16[128,1536]{1,0:T(8,128)(2,1)}, bf16[128,1536]{1,0:T(8,128)(2,1)}, u32[]{:S(2)}, u32[]{:S(2)}) collective-permute-start(bf16[128,1536]{1,0:T(8,128)(2,1)} %get-tuple-element.56), channel_id=1, source_target_pairs={{3,0},{0,1},{1,2},{2,3},{7,4},{4,5},{5,6},{6,7},{11,8},{8,9},{9,10... | collective-permute-start | bytes 1179656 | tf_op jit(solution)/shard_map/ppermute | solution.py:59
  213.4 16.4 %collective-permute-start.19 = (bf16[128,1536]{1,0:T(8,128)(2,1)}, bf16[128,1536]{1,0:T(8,128)(2,1)}, u32[]{:S(2)}, u32[]{:S(2)}) collective-permute-start(bf16[128,1536]{1,0:T(8,128)(2,1)} %get-tuple-element.57), channel_id=1, source_target_pairs={{31,0},{28,1},{29,2},{30,3},{3,4},{0,5},{1,6},{2,7},{7,8},{4,9},{5... | collective-permute-start | bytes 1179656 | tf_op jit(solution)/shard_map/ppermute | solution.py:59
  228.2 9.3 %collective-permute-start.11 = (bf16[128,1536]{1,0:T(8,128)(2,1)}, bf16[128,1536]{1,0:T(8,128)(2,1)}, u32[]{:S(2)}, u32[]{:S(2)}) collective-permute-start(bf16[128,1536]{1,0:T(8,128)(2,1)} %get-tuple-element.48), channel_id=1, source_target_pairs={{4,0},{5,1},{6,2},{7,3},{8,4},{9,5},{10,6},{11,7},{12,8},{13,9},{1... | collective-permute-start | bytes 1179656 | tf_op jit(solution)/shard_map/ppermute | solution.py:59
  229.6 8.3 %collective-permute-start.12 = (bf16[128,1536]{1,0:T(8,128)(2,1)}, bf16[128,1536]{1,0:T(8,128)(2,1)}, u32[]{:S(2)}, u32[]{:S(2)}) collective-permute-start(bf16[128,1536]{1,0:T(8,128)(2,1)} %get-tuple-element.49), channel_id=1, source_target_pairs={{1,0},{2,1},{3,2},{0,3},{5,4},{6,5},{7,6},{4,7},{9,8},{10,9},{11,1... | collective-permute-start | bytes 1179656 | tf_op jit(solution)/shard_map/ppermute | solution.py:59
  229.7 11.8 %collective-permute-start.13 = (bf16[128,1536]{1,0:T(8,128)(2,1)}, bf16[128,1536]{1,0:T(8,128)(2,1)}, u32[]{:S(2)}, u32[]{:S(2)}) collective-permute-start(bf16[128,1536]{1,0:T(8,128)(2,1)} %get-tuple-element.50), channel_id=1, source_target_pairs={{5,0},{6,1},{7,2},{4,3},{9,4},{10,5},{11,6},{8,7},{13,8},{14,9},{1... | collective-permute-start | bytes 1179656 | tf_op jit(solution)/shard_map/ppermute | solution.py:59
  (10 other events, 33.3 us)
Sparse Core Ops, SparseCore 0:
  32.5 48.2 all-gather.1

commit v4 on v3

--- a/solution.py
+++ b/solution.py
@@ -45,6 +45,14 @@
     return [(index(f, r, c), index(f ^ 1, r, c)) for f, r, c in every()]
 
 
+def plane_pairs(dx, dy):
+    pairs = []
+    for f, r, c in every():
+        zlo, x = divmod(r, 4)
+        pairs.append((index(f, r, c), index(f, zlo * 4 + (x + dx) % 4, c + dy)))
+    return pairs
+
+
 def depth_pairs():
     pairs = []
     for f, r, c in every():
@@ -60,10 +68,6 @@
 
 
 MOVES = ((0, 0), (1, 0), (0, 1), (1, 1))
-
-
-def after(value, *first):
-    return lax.optimization_barrier((value, *first))[0]
 
 
 def sign_of(half, frame):
@@ -227,9 +231,11 @@
     )(meta, *pieces)
 
 
-def project_kernel(meta, places, *refs):
-    attended, (c0, c1, c2, c3, near, far), (tokens, out, lhs, held, sems) = refs[:8], refs[8:14], refs[14:]
-    chunks = (c0, c1, c2, c3, near.at[0], near.at[1], near.at[2], far)
+def project_kernel(first, shapes, meta, places, *refs):
+    count = len(shapes)
+    attended, sources, (tokens, *rest) = refs[:8], refs[8 : 8 + count], refs[8 + count :]
+    out, lhs, held, sems = rest[-4:]
+    chunks = [ref.at[n] if lead else ref for ref, lead in zip(sources, shapes) for n in range(lead or 1)]
     step = pl.program_id(0)
 
     def fetch(n):
@@ -245,12 +251,12 @@
                 j = s + b * (1 - 2 * s)
                 lhs[half * 4 + i * 2 + j] = attended[half * 4 + piece][...]
 
-    for n in range(8):
+    for n in range(len(chunks)):
 
         @pl.when(step == n)
         def _():
             fetch(n).wait()
-            if n < 7:
+            if n + 1 < len(chunks):
                 fetch(n + 1).start()
 
     total = lax.dot_general(
@@ -263,14 +269,20 @@
             out[at] = (block + tokens[at].astype(jnp.float32)).astype(jnp.bfloat16)
 
 
-def project(attended, meta, places, chunks, tokens):
+def project(attended, meta, places, chunks, tokens, partial=None):
+    shapes = tuple(chunk.shape[0] if chunk.ndim == 3 else 0 for chunk in chunks)
+    steps = sum(max(lead, 1) for lead in shapes)
+    extra = [] if partial is None else [partial]
+    any_spec = pl.BlockSpec(memory_space=pl.ANY)
+    block = pl.BlockSpec((4, 16, 16, TILE), lambda t, m, p: (0, 0, 0, p[t]))
     grid_spec = pltpu.PrefetchScalarGridSpec(
         num_scalar_prefetch=2,
-        grid=(D // TILE,),
+        grid=(steps,),
         in_specs=[pl.BlockSpec((128, HD), lambda t, m, p: (0, 0))] * 8
-        + [pl.BlockSpec(memory_space=pl.ANY)] * 6
-        + [pl.BlockSpec((4, 16, 16, TILE), lambda t, m, p: (0, 0, 0, p[t]))],
-        out_specs=pl.BlockSpec((4, 16, 16, TILE), lambda t, m, p: (0, 0, 0, p[t])),
+        + [any_spec] * len(chunks)
+        + [block]
+        + [any_spec] * len(extra),
+        out_specs=block,
         scratch_shapes=[
             pltpu.VMEM((8, 128, HD), jnp.bfloat16),
             pltpu.VMEM((2, TILE, HD), jnp.bfloat16),
@@ -278,63 +290,86 @@
         ],
     )
     return pl.pallas_call(
-        project_kernel,
+        functools.partial(project_kernel, partial is None, shapes),
         grid_spec=grid_spec,
         out_shape=jax.ShapeDtypeStruct((4, 16, 16, D), jnp.bfloat16),
+        input_output_aliases={} if partial is None else {11 + len(chunks): 0},
         compiler_params=pltpu.CompilerParams(vmem_limit_bytes=VMEM),
-        cost_estimate=pl.CostEstimate(flops=2 * 1024 * HD * D, bytes_accessed=25 * 2**20, transcendentals=0),
+        cost_estimate=pl.CostEstimate(flops=2 * 1024 * HD * TILE * steps, bytes_accessed=3 * 2**20 * (steps + 1), transcendentals=0),
         name="project",
-    )(meta, places, *attended, *chunks, tokens)
-
-
-def plane_groups():
-    return [[index(f, zlo * 4 + x, c) for x in range(4) for c in range(C)] for f in range(F) for zlo in range(2)]
+    )(meta, places, *attended, *chunks, tokens, *extra)
+
+
+def ring_order(own, first, second, third, place):
+    row = jnp.stack([third, second, first, own, third, second, first])
+    return lax.dynamic_slice_in_dim(row, 3 - place, 4, axis=0).reshape((-1,) + own.shape[1:])
 
 
 def weight_places(f, r):
-    core, z = f % 2, (f // 2) * 2 + r // 4
+    core, z = f & 1, (f >> 1) * 2 + (r >> 2)
     places = []
     for k in (core, 1 - core):
-        for n in range(4):
-            at = (z + n * (2 * k - 1) + 4) % 4
-            places.append(((at // 2) * 2 + k) * 2 + at % 2)
-    return jnp.stack(places).astype(jnp.int32)
+        at = [(z + n * (2 * k - 1) + 4) & 3 for n in range(4)]
+        places.append([((a >> 1) * 2 + k) * 2 + (a & 1) for a in at])
+    (a0, a1, a2, a3), (b0, b1, b2, b3) = places
+    return jnp.stack([a0, a1, a2, b0, b1, a3, b2, b3]).astype(jnp.int32)
+
+
+def together(*values):
+    return lax.optimization_barrier(values)
 
 
 def local(tokens_in, queries, key_rows, value_rows, out_weight, row_valid):
     f, r, c = (lax.axis_index(a) for a in AXES)
     meta = jnp.stack([f, r, c, jnp.sum(row_valid)]).astype(jnp.int32)
+    places = weight_places(f, r)
     split = lambda a: a.reshape(4, 2, 8, 2, 8, HD)
     arrays = (meta, split(key_rows), split(value_rows), split(queries))
-    chunk = lax.all_gather(out_weight.T, AXES, axis=0, tiled=True, axis_index_groups=plane_groups())
+    shard = out_weight.T
+    shards = [send(shard, plane_pairs(0, d)) for d in (1, 2, 3)]
 
     row, col, both = MOVES[1:]
     go = lambda value, half, move: send(value, window_pairs(half, *move))
+    up = lambda value: send(value, frame_pairs(1))
+    down = lambda value: send(value, frame_pairs(-1))
+
     skv0, skv1, x0, y0 = pack(((0, 0, "kv"), (1, 0, "kv"), (0, 1, "kvq"), (0, 2, "kvq")), *arrays)
-    up0, down0 = send(skv1, frame_pairs(1)), send(skv0, frame_pairs(-1))
-    x0, y0 = go(x0, 0, row), go(y0, 0, col)
+    x0, y0, skv1, skv0, meta, *shards = together(x0, y0, skv1, skv0, meta, *shards)
+    strip = ring_order(shard, *shards, c)
     x1, y1, dkv0, dkv1, dq0, dq1, sq0, sq1 = pack(
-        ((1, 1, "kvq"), (1, 2, "kvq"), (0, 3, "kv"), (1, 3, "kv"), (0, 3, "q"), (1, 3, "q"), (0, 0, "q"), (1, 0, "q")), *arrays
+        ((1, 1, "kvq"), (1, 2, "kvq"), (0, 3, "kv"), (1, 3, "kv"), (0, 3, "q"), (1, 3, "q"), (0, 0, "q"), (1, 0, "q")), meta, *arrays[1:]
     )
-    x1, y1 = go(after(x1, up0), 1, row), go(after(y1, down0), 1, col)
-    down1 = send(halo_pack(x0, y0), frame_pairs(-1))
-    dkv0, dkv1 = go(after(dkv0, x1), 0, both), go(after(dkv1, y1), 1, both)
-    up1 = send(halo_pack(x1, y1), frame_pairs(1))
-    dq0, dq1 = go(after(dq0, dkv0), 0, both), go(after(dq1, dkv1), 1, both)
-    down2, up2 = send(dkv0, frame_pairs(-1)), send(dkv1, frame_pairs(1))
-
-    ring = [after(chunk, up2)]
-    for _ in range(3):
-        ring.append(send(ring[-1], depth_pairs()))
-    near = send(jnp.stack(ring[:3]), core_pairs())
-    far = send(ring[3], core_pairs())
-
+    first = go(x0, 0, row), go(y0, 0, col), up(skv1), down(skv0)
+    x1, y1, strip, *first = together(x1, y1, strip, *first)
+    x0, y0, up0, down0 = first
+    second = go(x1, 1, row), go(y1, 1, col), *(send(strip, plane_pairs(d, 0)) for d in (1, 2, 3))
+    dkv0, dkv1, x0, y0, *second = together(dkv0, dkv1, x0, y0, *second)
+    x1, y1, *strips = second
+    chunk = ring_order(strip, *strips, r & 3)
+    third = go(dkv0, 0, both), go(dkv1, 1, both), down(halo_pack(x0, y0)), up(halo_pack(x1, y1))
+    dq0, dq1, chunk, *third = together(dq0, dq1, chunk, *third)
+    dkv0, dkv1, down1, up1 = third
+    fourth = go(dq0, 0, both), go(dq1, 1, both), down(dkv0), up(dkv1)
+    chunk, *fourth = together(chunk, *fourth)
+    dq0, dq1, down2, up2 = fourth
+
+    ring = [chunk, send(chunk, depth_pairs())]
     mixed1 = attend(1, meta, skv1, sq1, x1, y1, dkv1, dq1, down0, down1, down2)
+    ring[1], skv0, *mixed1 = together(ring[1], skv0, *mixed1)
+    back = lambda half, mixed: [mixed[0]] + [send(mixed[n], window_pairs(half, *MOVES[n], back=True)) for n in (1, 2, 3)]
+    near = send(jnp.stack(ring[:2]), core_pairs())
+    ring.append(send(ring[1], depth_pairs()))
+    attended1 = back(1, mixed1)
     mixed0 = attend(0, meta, skv0, sq0, x0, y0, dkv0, dq0, up0, up1, up2)
-    attended = []
-    for half, mixed in enumerate((mixed0, mixed1)):
-        attended += [mixed[0]] + [send(mixed[n], window_pairs(half, *MOVES[n], back=True)) for n in (1, 2, 3)]
-    return project(attended, meta, weight_places(f, r), (*ring, near, far), tokens_in)
+    near, ring[2], *rest = together(near, ring[2], *attended1, *mixed0)
+    attended1, mixed0 = rest[:4], rest[4:]
+    attended0 = back(0, mixed0)
+    ring.append(send(ring[2], depth_pairs()))
+    attended = attended0 + attended1
+    out = project(attended, meta, places[:5], (*ring[:3], near), tokens_in)
+    last = together(ring[3], *attended)[0]
+    far = send(jnp.stack([ring[2], last]), core_pairs())
+    return project(attended, meta, places[5:], (ring[3], far), tokens_in, out)
 
 
 def solution(mesh):

time: 270 us -> 252 us (0.933)
  between operations: 13.6 us -> 0.69 us
  Pallas kernels: 62 us -> 67.3 us
  starting transfers between devices: 49.3 us -> 45.3 us
  waiting for transfers between devices: 134 us -> 130 us
  local copies, waits for them, and re-layouts: 6.59 us -> 3.18 us
    all_gather x1 -> x0, waiting for transfers between devices: 13.8 us -> none  [local(): lax.all_gather(out_weight.T, AXES, axis=0, tiled=True, axis_index_groups=...]
    ppermute x25 -> x31, waiting for transfers between devices: 120 us -> 130 us  [send(): return lax.ppermute(value, AXES, pairs)]
    pallas_call x1 -> x2, Pallas kernels: 20.1 us -> 25 us  [project(): pl.pallas_call(functools.partial(project_kernel, partial is None, shapes)...]
    ppermute x25 -> x31, starting transfers between devices: 49.3 us -> 45.3 us  [send(): return lax.ppermute(value, AXES, pairs)]
    unnamed x32 -> x68, local copies, waits for them, and re-layouts: 5.9 us -> 2.37 us
  transfers between devices with their start and end apart: 26 -> 31, of which waited for: 14 -> 18; matrix products, arithmetic and copies ran while one was open for 0% -> 2% of each run, Pallas kernels for 14% -> 22%
where the time goes in v4:
time: 252 us
  waiting for transfers between devices  130 us (52%)
  Pallas kernels  67.3 us (27%)
  starting transfers between devices  45.3 us (18%)
  other arithmetic  5.28 us (2%)
  local copies, waits for them, and re-layouts  3.18 us (1%)
    ppermute x31, waiting for transfers between devices, send(): return lax.ppermute(value, AXES, pairs)  130 us
    ppermute x31, starting transfers between devices, send(): return lax.ppermute(value, AXES, pairs)  45.3 us
    pallas_call x2, Pallas kernels, attend(): pl.pallas_call(functools.partial(attend_kernel, half), grid=(H // STEP,),...  27.5 us
    pallas_call x2, Pallas kernels, project(): pl.pallas_call(functools.partial(project_kernel, partial is None, shapes)...  25 us
    pallas_call x2, Pallas kernels, pack(): pl.pallas_call(functools.partial(pack_kernel, parts), out_shape=[jax.Shap...  10.1 us
  transfers between devices with their start and end apart: 31, of which 18 were waited for; matrix products, arithmetic and copies ran while one was open for 2% of the time, Pallas kernels for 22%

profile of v4, /device:TPU:1, one launch (start us, length us, event | category | flops | bytes accessed | tf_op | source)
XLA Modules:
  0.0 251.7 jit_solution(9410689071178342663)
XLA Ops:
  2.1 2.6 %collective-permute-start.1 = (bf16[24,1536]{1,0:T(8,128)(2,1)}, bf16[24,1536]{1,0:T(8,128)(2,1)S(1)}, u32[]{:S(2)}, u32[]{:S(2)}) collective-permute-start(bf16[24,1536]{1,0:T(8,128)(2,1)} %bitcast.74), channel_id=1, source_target_pairs={{0,2},{1,3},{2,0},{3,1},{4,6},{5,7},{6,4},{7,5},{8,10},{9,11},{10,... | collective-permute-start | bytes 221192 | tf_op jit(solution)/shard_map/ppermute | solution.py:67
  8.3 4.3 %pack.2 = (bf16[2,2,8,8,1536]{4,3,2,1,0:T(8,128)(2,1)}, bf16[2,2,8,8,1536]{4,3,2,1,0:T(8,128)(2,1)}, bf16[3,2,8,8,1536]{4,3,2,1,0:T(8,128)(2,1)}, bf16[3,2,8,8,1536]{4,3,2,1,0:T(8,128)(2,1)}) custom-call(s32[4]{0:T(128)} %pad_add_fusion.meta, bf16[4,2,8,2,8,1536]{5,4,3,2,1,0:T(8,128)(2,1)} %bitcast.57, bf16[4,2,8,2,8,1536]{5,4,3,2,1,0:T(8,128)(2,1)} %bitcast.59, ...), custom_call_target="tpu_custom_call" | custom-call | bytes 10485760 | tf_op jit(solution)/shard_map/pack/pallas_call | solution.py:106
  12.7 3.9 %collective-permute-start.3 = (bf16[3,128,1536]{2,1,0:T(8,128)(2,1)}, bf16[3,128,1536]{2,1,0:T(8,128)(2,1)S(1)}, u32[]{:S(2)}, u32[]{:S(2)}) collective-permute-start(bf16[3,128,1536]{2,1,0:T(8,128)(2,1)} %bitcast.79), channel_id=1, source_target_pairs={{0,4},{1,5},{2,6},{3,7},{4,8},{5,9},{6,10},{7,11},{8,12},{9,13},{1... | collective-permute-start | bytes 3538952 | tf_op jit(solution)/shard_map/ppermute | solution.py:67
  16.6 5.2 %collective-permute-start.5 = (bf16[2,128,1536]{2,1,0:T(8,128)(2,1)}, bf16[2,128,1536]{2,1,0:T(8,128)(2,1)S(1)}, u32[]{:S(2)}, u32[]{:S(2)}) collective-permute-start(bf16[2,128,1536]{2,1,0:T(8,128)(2,1)} %bitcast.82), channel_id=1, source_target_pairs={{0,32},{1,33},{2,34},{3,35},{4,36},{5,37},{6,38},{7,39},{8,40},{9,... | collective-permute-start | bytes 2359304 | tf_op jit(solution)/shard_map/ppermute | solution.py:67
  23.8 5.8 %pack.3 = (bf16[3,2,8,8,1536]{4,3,2,1,0:T(8,128)(2,1)}, bf16[3,2,8,8,1536]{4,3,2,1,0:T(8,128)(2,1)}, bf16[2,2,8,8,1536]{4,3,2,1,0:T(8,128)(2,1)}, bf16[2,2,8,8,1...) custom-call(s32[4]{0:T(128)} %pad_add_fusion.meta, ...), custom_call_target="tpu_custom_call" | custom-call | bytes 14680064 | tf_op jit(solution)/shard_map/pack/pallas_call | solution.py:106
  29.7 10.7 %collective-permute-done.5.h0 = bf16[2,128,1536]{2,1,0:T(8,128)(2,1)S(1)} collective-permute-done((bf16[2,128,1536]{2,1,0:T(8,128)(2,1)}, bf16[2,128,1536]{2,1,0:T(8,128)(2,1)S(1)}, u32[]{:S(2)}, u32[]{:S(2)}) %collective-permute-start.5) | collective-permute-done | bytes 786464 | tf_op jit(solution)/shard_map/ppermute | solution.py:67
  40.4 16.3 %collective-permute-done.6.h0 = bf16[2,128,1536]{2,1,0:T(8,128)(2,1)S(1)} collective-permute-done((bf16[2,128,1536]{2,1,0:T(8,128)(2,1)}, bf16[2,128,1536]{2,1,0:T(8,128)(2,1)S(1)}, u32[]{:S(2)}, u32[]{:S(2)}) %collective-permute-start.6) | collective-permute-done | bytes 786464 | tf_op jit(solution)/shard_map/ppermute | solution.py:67
  59.7 13.6 %collective-permute-done.10 = bf16[96,1536]{1,0:T(8,128)(2,1)S(1)} collective-permute-done((bf16[96,1536]{1,0:T(8,128)(2,1)S(1)}, bf16[96,1536]{1,0:T(8,128)(2,1)S(1)}, u32[]{:S(2)}, u32[]{:S(2)}) %collective-permute-start.10) | collective-permute-done | bytes 294944 | tf_op jit(solution)/shard_map/ppermute | solution.py:67
  73.3 5.5 %collective-permute-done.9 = bf16[96,1536]{1,0:T(8,128)(2,1)S(1)} collective-permute-done((bf16[96,1536]{1,0:T(8,128)(2,1)S(1)}, bf16[96,1536]{1,0:T(8,128)(2,1)S(1)}, u32[]{:S(2)}, u32[]{:S(2)}) %collective-permute-start.9) | collective-permute-done | bytes 294944 | tf_op jit(solution)/shard_map/ppermute | solution.py:67
  78.8 2.3 halo_pack.3
  81.1 2.6 %collective-permute-start.15 = (bf16[2,2,128,1536]{3,2,1,0:T(8,128)(2,1)}, bf16[2,2,128,1536]{3,2,1,0:T(8,128)(2,1)}, u32[]{:S(2)}, u32[]{:S(2)}) collective-permute-start(bf16[2,2,128,1536]{3,2,1,0:T(8,128)(2,1)} %halo_pack.3), channel_id=1, source_target_pairs={{0,32},{1,33},{2,34},{3,35},{4,36},{5,37},{6,38},{7,39},{8,40},{9,... | collective-permute-start | bytes 4718600 | tf_op jit(solution)/shard_map/ppermute | solution.py:67
  83.8 2.3 halo_pack.2
  86.1 3.0 %collective-permute-start.14 = (bf16[2,2,128,1536]{3,2,1,0:T(8,128)(2,1)}, bf16[2,2,128,1536]{3,2,1,0:T(8,128)(2,1)S(1)}, u32[]{:S(2)}, u32[]{:S(2)}) collective-permute-start(bf16[2,2,128,1536]{3,2,1,0:T(8,128)(2,1)} %halo_pack.2), channel_id=1, source_target_pairs={{32,0},{33,1},{34,2},{35,3},{36,4},{37,5},{38,6},{39,7},{40,8},{41... | collective-permute-start | bytes 4718600 | tf_op jit(solution)/shard_map/ppermute | solution.py:67
  91.9 17.8 %collective-permute-done.12.dkv = bf16[2,128,1536]{2,1,0:T(8,128)(2,1)S(1)} collective-permute-done((bf16[2,128,1536]{2,1,0:T(8,128)(2,1)S(1)}, bf16[2,128,1536]{2,1,0:T(8,128)(2,1)S(1)}, u32[]{:S(2)}, u32[]{:S(2)}) %collective-permute-start.12) | collective-permute-done | bytes 786464 | tf_op jit(solution)/shard_map/ppermute | solution.py:67
  109.7 3.0 %collective-permute-done.13.dkv = bf16[2,128,1536]{2,1,0:T(8,128)(2,1)S(1)} collective-permute-done((bf16[2,128,1536]{2,1,0:T(8,128)(2,1)S(1)}, bf16[2,128,1536]{2,1,0:T(8,128)(2,1)S(1)}, u32[]{:S(2)}, u32[]{:S(2)}) %collective-permute-start.13) | collective-permute-done | bytes 786464 | tf_op jit(solution)/shard_map/ppermute | solution.py:67
  112.8 5.5 %collective-permute-done.15.hxy = bf16[2,2,128,1536]{3,2,1,0:T(8,128)(2,1)} collective-permute-done((bf16[2,2,128,1536]{3,2,1,0:T(8,128)(2,1)}, bf16[2,2,128,1536]{3,2,1,0:T(8,128)(2,1)}, u32[]{:S(2)}, u32[]{:S(2)}) %collective-permute-start.15) | collective-permute-done | bytes 1572896 | tf_op jit(solution)/shard_map/ppermute | solution.py:67
  118.3 8.3 %collective-permute-done.14.hxy = bf16[2,2,128,1536]{3,2,1,0:T(8,128)(2,1)S(1)} collective-permute-done((bf16[2,2,128,1536]{3,2,1,0:T(8,128)(2,1)}, bf16[2,2,128,1536]{3,2,1,0:T(8,128)(2,1)S(1)}, u32[]{:S(2)}, u32[]{:S(2)}) %collective-permute-start.14) | collective-permute-done | bytes 1572896 | tf_op jit(solution)/shard_map/ppermute | solution.py:67
  128.5 5.1 %collective-permute-start.19 = (bf16[2,128,1536]{2,1,0:T(8,128)(2,1)S(1)}, bf16[2,128,1536]{2,1,0:T(8,128)(2,1)S(1)}, u32[]{:S(2)}, u32[]{:S(2)}) collective-permute-start(bf16[2,128,1536]{2,1,0:T(8,128)(2,1)S(1)} %collective-permute-done.13.dkv), channel_id=1, source_target_pairs={{0,32},{1,33},{2,34},{3,35},{4,36},{5,37},{6,38},{7,39},{8,40},{9,... | collective-permute-start | bytes 2359304 | tf_op jit(solution)/shard_map/ppermute | solution.py:67
  136.1 7.5 %collective-permute-done.16.dq = bf16[1,128,1536]{2,1,0:T(8,128)(2,1)S(1)} collective-permute-done((bf16[1,128,1536]{2,1,0:T(8,128)(2,1)S(1)}, bf16[1,128,1536]{2,1,0:T(8,128)(2,1)S(1)}, u32[]{:S(2)}, u32[]{:S(2)}) %collective-permute-start.16) | collective-permute-done | bytes 393248 | tf_op jit(solution)/shard_map/ppermute | solution.py:67
  143.6 3.0 %collective-permute-done.17.dq = bf16[1,128,1536]{2,1,0:T(8,128)(2,1)S(1)} collective-permute-done((bf16[1,128,1536]{2,1,0:T(8,128)(2,1)S(1)}, bf16[1,128,1536]{2,1,0:T(8,128)(2,1)S(1)}, u32[]{:S(2)}, u32[]{:S(2)}) %collective-permute-start.17) | collective-permute-done | bytes 393248 | tf_op jit(solution)/shard_map/ppermute | solution.py:67
  146.6 3.1 %collective-permute-done.18.hd = bf16[2,128,1536]{2,1,0:T(8,128)(2,1)S(1)} collective-permute-done((bf16[2,128,1536]{2,1,0:T(8,128)(2,1)S(1)}, bf16[2,128,1536]{2,1,0:T(8,128)(2,1)S(1)}, u32[]{:S(2)}, u32[]{:S(2)}) %collective-permute-start.18) | collective-permute-done | bytes 786464 | tf_op jit(solution)/shard_map/ppermute | solution.py:67
  149.8 6.1 %collective-permute-done.19.hd = bf16[2,128,1536]{2,1,0:T(8,128)(2,1)S(1)} collective-permute-done((bf16[2,128,1536]{2,1,0:T(8,128)(2,1)S(1)}, bf16[2,128,1536]{2,1,0:T(8,128)(2,1)S(1)}, u32[]{:S(2)}, u32[]{:S(2)}) %collective-permute-start.19) | collective-permute-done | bytes 786464 | tf_op jit(solution)/shard_map/ppermute | solution.py:67
  155.9 13.9 %attend.2 = (bf16[128,1536]{1,0:T(8,128)(2,1)}, bf16[128,1536]{1,0:T(8,128)(2,1)}, bf16[128,1536]{1,0:T(8,128)(2,1)}, bf16[128,1536]{1,0:T(8,128)(2,1)}) custom-call(s32[4]{0:T(128)} %pad_add_fusion.meta, bf16[2,128,1536]{2,1,0:T(8,128)(2,1)} %bitcast.83, bf16[1,128,1536]{2,1,0:T(8,128)(2,1)} %bitcast.87, ...), custom_call_target="tpu_custom_call" | custom-call | flops 6442450944 | bytes 10485760 | tf_op jit(solution)/shard_map/attend/pallas_call | solution.py:216
  171.9 3.1 %collective-permute-start.22 = (bf16[384,1536]{1,0:T(8,128)(2,1)S(1)}, bf16[384,1536]{1,0:T(8,128)(2,1)S(1)}, u32[]{:S(2)}, u32[]{:S(2)}) collective-permute-start(bf16[384,1536]{1,0:T(8,128)(2,1)S(1)} %collective-permute-done.20.refs_9_), channel_id=1, source_target_pairs={{0,16},{1,17},{2,18},{3,19},{4,20},{5,21},{6,22},{7,23},{8,24},{9,... | collective-permute-start | bytes 3538952 | tf_op jit(solution)/shard_map/ppermute | solution.py:67
  175.0 13.6 %attend.3 = (bf16[128,1536]{1,0:T(8,128)(2,1)}, bf16[128,1536]{1,0:T(8,128)(2,1)}, bf16[128,1536]{1,0:T(8,128)(2,1)}, bf16[128,1536]{1,0:T(8,128)(2,1)}) custom-call(s32[4]{0:T(128)} %pad_add_fusion.meta, bf16[2,128,1536]{2,1,0:T(8,128)(2,1)} %bitcast.81, bf16[1,128,1536]{2,1,0:T(8,128)(2,1)} %bitcast.86, bf16[3,128,1536]{2,1,0:T(8,128)(2,1)} %copy-done.5, ...), custom_call_target="tpu_custom_call" | custom-call | flops 6442450944 | bytes 10485760 | tf_op jit(solution)/shard_map/attend/pallas_call | solution.py:216
  188.7 7.2 %collective-permute-done.22.refs_10_ = bf16[384,1536]{1,0:T(8,128)(2,1)S(1)} collective-permute-done((bf16[384,1536]{1,0:T(8,128)(2,1)S(1)}, bf16[384,1536]{1,0:T(8,128)(2,1)S(1)}, u32[]{:S(2)}, u32[]{:S(2)}) %collective-permute-start.22) | collective-permute-done | bytes 1179680 | tf_op jit(solution)/shard_map/ppermute | solution.py:67
  195.9 2.4 collective-permute-start.29
  198.3 10.6 %collective-permute-done.26.refs_1_ = bf16[128,1536]{1,0:T(8,128)(2,1)S(1)} collective-permute-done((bf16[128,1536]{1,0:T(8,128)(2,1)}, bf16[128,1536]{1,0:T(8,128)(2,1)S(1)}, u32[]{:S(2)}, u32[]{:S(2)}) %collective-permute-start.26) | collective-permute-done | bytes 393248 | tf_op jit(solution)/shard_map/ppermute | solution.py:67
  211.6 7.9 %collective-permute-done.29.refs_8_ = bf16[384,1536]{1,0:T(8,128)(2,1)S(1)} collective-permute-done((bf16[384,1536]{1,0:T(8,128)(2,1)S(1)}, bf16[384,1536]{1,0:T(8,128)(2,1)S(1)}, u32[]{:S(2)}, u32[]{:S(2)}) %collective-permute-start.29) | collective-permute-done | bytes 1179680 | tf_op jit(solution)/shard_map/ppermute | solution.py:67
  221.5 2.4 collective-permute-start.30
  225.1 14.4 %project.2.refs_11_ = bf16[4,16,16,3072]{3,2,1,0:T(8,128)(2,1)} custom-call(s32[4]{0:T(128)} %pad_add_fusion.meta, s32[5]{0:T(128)} %stack.128.places, bf16[128,1536]{1,0:T(8,128)(2,1)} %get-tuple-element.140.refs_0_, bf16[128,1536]{1,0:T(8,128)(2,1)} %copy-done.10, bf16[128,1536]{1,0:T(8,128)(2,1)} %copy-done.11, bf16[128,1536]{1,0:T(8,128)(2,1)} %copy-done.12, ...), custom_call_target="tpu_custom_call" | custom-call | flops 6039797760 | bytes 18874368 | tf_op jit(solution)/shard_map/project/pallas_call | solution.py:292
  240.9 10.6 %project.3 = bf16[4,16,16,3072]{3,2,1,0:T(8,128)(2,1)} custom-call(s32[4]{0:T(128)} %pad_add_fusion.meta, s32[3]{0:T(128)} %pad_add_fusion.1.places, bf16[128,1536]{1,0:T(8,128)(2,1)} %get-tuple-element.140.refs_0_, bf16[128,1536]{1,0:T(8,128)(2,1)} %copy-done.10, bf16[128,1536]{1,0:T(8,128)(2,1)} %copy-done.11, ...), custom_call_target="tpu_custom_call", output_to_operand_aliasing={{}: (13, {})} | custom-call | flops 3623878656 | bytes 12582912 | tf_op jit(solution)/shard_map/project/pallas_call | solution.py:292
  (116 shorter events, 27.3 us)
Async XLA Ops:
  0.0 12.6 %collective-permute-start = (bf16[24,1536]{1,0:T(8,128)(2,1)}, bf16[24,1536]{1,0:T(8,128)(2,1)S(1)}, u32[]{:S(2)}, u32[]{:S(2)}) collective-permute-start(bf16[24,1536]{1,0:T(8,128)(2,1)} %bitcast.73), channel_id=1, source_target_pairs={{0,1},{1,2},{2,3},{3,0},{4,5},{5,6},{6,7},{7,4},{8,9},{9,10},{10,1... | collective-permute-start | bytes 221192 | tf_op jit(solution)/shard_map/ppermute | solution.py:67
  2.1 10.5 %collective-permute-start.1 = (bf16[24,1536]{1,0:T(8,128)(2,1)}, bf16[24,1536]{1,0:T(8,128)(2,1)S(1)}, u32[]{:S(2)}, u32[]{:S(2)}) collective-permute-start(bf16[24,1536]{1,0:T(8,128)(2,1)} %bitcast.74), channel_id=1, source_target_pairs={{0,2},{1,3},{2,0},{3,1},{4,6},{5,7},{6,4},{7,5},{8,10},{9,11},{10,... | collective-permute-start | bytes 221192 | tf_op jit(solution)/shard_map/ppermute | solution.py:67
  4.7 7.9 %collective-permute-start.2 = (bf16[24,1536]{1,0:T(8,128)(2,1)}, bf16[24,1536]{1,0:T(8,128)(2,1)S(1)}, u32[]{:S(2)}, u32[]{:S(2)}) collective-permute-start(bf16[24,1536]{1,0:T(8,128)(2,1)} %bitcast.75), channel_id=1, source_target_pairs={{0,3},{1,0},{2,1},{3,2},{4,7},{5,4},{6,5},{7,6},{8,11},{9,8},{10,9... | collective-permute-start | bytes 221192 | tf_op jit(solution)/shard_map/ppermute | solution.py:67
  12.7 44.0 %collective-permute-start.3 = (bf16[3,128,1536]{2,1,0:T(8,128)(2,1)}, bf16[3,128,1536]{2,1,0:T(8,128)(2,1)S(1)}, u32[]{:S(2)}, u32[]{:S(2)}) collective-permute-start(bf16[3,128,1536]{2,1,0:T(8,128)(2,1)} %bitcast.79), channel_id=1, source_target_pairs={{0,4},{1,5},{2,6},{3,7},{4,8},{5,9},{6,10},{7,11},{8,12},{9,13},{1... | collective-permute-start | bytes 3538952 | tf_op jit(solution)/shard_map/ppermute | solution.py:67
  16.6 40.1 %collective-permute-start.4 = (bf16[3,128,1536]{2,1,0:T(8,128)(2,1)}, bf16[3,128,1536]{2,1,0:T(8,128)(2,1)S(1)}, u32[]{:S(2)}, u32[]{:S(2)}) collective-permute-start(bf16[3,128,1536]{2,1,0:T(8,128)(2,1)} %bitcast.78), channel_id=1, source_target_pairs={{0,1},{1,2},{2,3},{3,0},{4,5},{5,6},{6,7},{7,4},{8,9},{9,10},{10,1... | collective-permute-start | bytes 3538952 | tf_op jit(solution)/shard_map/ppermute | solution.py:67
  16.6 23.8 %collective-permute-start.5 = (bf16[2,128,1536]{2,1,0:T(8,128)(2,1)}, bf16[2,128,1536]{2,1,0:T(8,128)(2,1)S(1)}, u32[]{:S(2)}, u32[]{:S(2)}) collective-permute-start(bf16[2,128,1536]{2,1,0:T(8,128)(2,1)} %bitcast.82), channel_id=1, source_target_pairs={{0,32},{1,33},{2,34},{3,35},{4,36},{5,37},{6,38},{7,39},{8,40},{9,... | collective-permute-start | bytes 2359304 | tf_op jit(solution)/shard_map/ppermute | solution.py:67
  21.9 34.8 %collective-permute-start.6 = (bf16[2,128,1536]{2,1,0:T(8,128)(2,1)}, bf16[2,128,1536]{2,1,0:T(8,128)(2,1)S(1)}, u32[]{:S(2)}, u32[]{:S(2)}) collective-permute-start(bf16[2,128,1536]{2,1,0:T(8,128)(2,1)} %bitcast.80), channel_id=1, source_target_pairs={{32,0},{33,1},{34,2},{35,3},{36,4},{37,5},{38,6},{39,7},{40,8},{41... | collective-permute-start | bytes 2359304 | tf_op jit(solution)/shard_map/ppermute | solution.py:67
  56.7 22.1 %collective-permute-start.7 = (bf16[3,128,1536]{2,1,0:T(8,128)(2,1)}, bf16[3,128,1536]{2,1,0:T(8,128)(2,1)}, u32[]{:S(2)}, u32[]{:S(2)}) collective-permute-start(bf16[3,128,1536]{2,1,0:T(8,128)(2,1)} %bitcast.77), channel_id=1, source_target_pairs={{0,28},{1,29},{2,30},{3,31},{4,0},{5,1},{6,2},{7,3},{8,4},{9,5},{1... | collective-permute-start | bytes 3538952 | tf_op jit(solution)/shard_map/ppermute | solution.py:67
  56.8 22.0 %collective-permute-start.8 = (bf16[3,128,1536]{2,1,0:T(8,128)(2,1)}, bf16[3,128,1536]{2,1,0:T(8,128)(2,1)}, u32[]{:S(2)}, u32[]{:S(2)}) collective-permute-start(bf16[3,128,1536]{2,1,0:T(8,128)(2,1)} %bitcast.76), channel_id=1, source_target_pairs={{0,3},{1,0},{2,1},{3,2},{4,7},{5,4},{6,5},{7,6},{8,11},{9,8},{10,9... | collective-permute-start | bytes 3538952 | tf_op jit(solution)/shard_map/ppermute | solution.py:67
  57.3 16.0 %collective-permute-start.10 = (bf16[96,1536]{1,0:T(8,128)(2,1)S(1)}, bf16[96,1536]{1,0:T(8,128)(2,1)S(1)}, u32[]{:S(2)}, u32[]{:S(2)}) collective-permute-start(bf16[96,1536]{1,0:T(8,128)(2,1)S(1)} %bitcast.67), channel_id=1, source_target_pairs={{0,8},{1,9},{2,10},{3,11},{4,12},{5,13},{6,14},{7,15},{8,0},{9,1},... | collective-permute-start | bytes 884744 | tf_op jit(solution)/shard_map/ppermute | solution.py:67
  57.3 16.0 %collective-permute-start.11 = (bf16[96,1536]{1,0:T(8,128)(2,1)S(1)}, bf16[96,1536]{1,0:T(8,128)(2,1)S(1)}, u32[]{:S(2)}, u32[]{:S(2)}) collective-permute-start(bf16[96,1536]{1,0:T(8,128)(2,1)S(1)} %bitcast.68), channel_id=1, source_target_pairs={{0,12},{1,13},{2,14},{3,15},{4,0},{5,1},{6,2},{7,3},{8,4},{9,5},{1... | collective-permute-start | bytes 884744 | tf_op jit(solution)/shard_map/ppermute | solution.py:67
  59.1 19.7 %collective-permute-start.9 = (bf16[96,1536]{1,0:T(8,128)(2,1)S(1)}, bf16[96,1536]{1,0:T(8,128)(2,1)S(1)}, u32[]{:S(2)}, u32[]{:S(2)}) collective-permute-start(bf16[96,1536]{1,0:T(8,128)(2,1)S(1)} %bitcast.69), channel_id=1, source_target_pairs={{0,4},{1,5},{2,6},{3,7},{4,8},{5,9},{6,10},{7,11},{8,12},{9,13},{1... | collective-permute-start | bytes 884744 | tf_op jit(solution)/shard_map/ppermute | solution.py:67
  81.1 37.1 %collective-permute-start.15 = (bf16[2,2,128,1536]{3,2,1,0:T(8,128)(2,1)}, bf16[2,2,128,1536]{3,2,1,0:T(8,128)(2,1)}, u32[]{:S(2)}, u32[]{:S(2)}) collective-permute-start(bf16[2,2,128,1536]{3,2,1,0:T(8,128)(2,1)} %halo_pack.3), channel_id=1, source_target_pairs={{0,32},{1,33},{2,34},{3,35},{4,36},{5,37},{6,38},{7,39},{8,40},{9,... | collective-permute-start | bytes 4718600 | tf_op jit(solution)/shard_map/ppermute | solution.py:67
  86.1 40.4 %collective-permute-start.14 = (bf16[2,2,128,1536]{3,2,1,0:T(8,128)(2,1)}, bf16[2,2,128,1536]{3,2,1,0:T(8,128)(2,1)S(1)}, u32[]{:S(2)}, u32[]{:S(2)}) collective-permute-start(bf16[2,2,128,1536]{3,2,1,0:T(8,128)(2,1)} %halo_pack.2), channel_id=1, source_target_pairs={{32,0},{33,1},{34,2},{35,3},{36,4},{37,5},{38,6},{39,7},{40,8},{41... | collective-permute-start | bytes 4718600 | tf_op jit(solution)/shard_map/ppermute | solution.py:67
  89.3 20.5 %collective-permute-start.12 = (bf16[2,128,1536]{2,1,0:T(8,128)(2,1)S(1)}, bf16[2,128,1536]{2,1,0:T(8,128)(2,1)S(1)}, u32[]{:S(2)}, u32[]{:S(2)}) collective-permute-start(bf16[2,128,1536]{2,1,0:T(8,128)(2,1)S(1)} %bitcast.85), channel_id=1, source_target_pairs={{0,5},{1,6},{2,7},{3,4},{4,9},{5,10},{6,11},{7,8},{8,13},{9,14},{1... | collective-permute-start | bytes 2359304 | tf_op jit(solution)/shard_map/ppermute | solution.py:67
  90.0 22.8 %collective-permute-start.13 = (bf16[2,128,1536]{2,1,0:T(8,128)(2,1)S(1)}, bf16[2,128,1536]{2,1,0:T(8,128)(2,1)S(1)}, u32[]{:S(2)}, u32[]{:S(2)}) collective-permute-start(bf16[2,128,1536]{2,1,0:T(8,128)(2,1)S(1)} %bitcast.84), channel_id=1, source_target_pairs={{0,31},{1,28},{2,29},{3,30},{4,3},{5,0},{6,1},{7,2},{8,7},{9,4},{1... | collective-permute-start | bytes 2359304 | tf_op jit(solution)/shard_map/ppermute | solution.py:67
  91.9 79.0 %copy-start.1 = (bf16[4,96,1536]{2,1,0:T(8,128)(2,1)}, bf16[4,96,1536]{2,1,0:T(8,128)(2,1)S(1)}, u32[]{:S(2)}) copy-start(bf16[4,96,1536]{2,1,0:T(8,128)(2,1)S(1)} %constant_dynamic-slice_fusion) | copy-start | bytes 3538948
  126.5 23.2 %collective-permute-start.18 = (bf16[2,128,1536]{2,1,0:T(8,128)(2,1)S(1)}, bf16[2,128,1536]{2,1,0:T(8,128)(2,1)S(1)}, u32[]{:S(2)}, u32[]{:S(2)}) collective-permute-start(bf16[2,128,1536]{2,1,0:T(8,128)(2,1)S(1)} %collective-permute-done.12.dkv), channel_id=1, source_target_pairs={{32,0},{33,1},{34,2},{35,3},{36,4},{37,5},{38,6},{39,7},{40,8},{41... | collective-permute-start | bytes 2359304 | tf_op jit(solution)/shard_map/ppermute | solution.py:67
  128.5 27.4 %collective-permute-start.19 = (bf16[2,128,1536]{2,1,0:T(8,128)(2,1)S(1)}, bf16[2,128,1536]{2,1,0:T(8,128)(2,1)S(1)}, u32[]{:S(2)}, u32[]{:S(2)}) collective-permute-start(bf16[2,128,1536]{2,1,0:T(8,128)(2,1)S(1)} %collective-permute-done.13.dkv), channel_id=1, source_target_pairs={{0,32},{1,33},{2,34},{3,35},{4,36},{5,37},{6,38},{7,39},{8,40},{9,... | collective-permute-start | bytes 2359304 | tf_op jit(solution)/shard_map/ppermute | solution.py:67
  133.6 10.0 %collective-permute-start.16 = (bf16[1,128,1536]{2,1,0:T(8,128)(2,1)S(1)}, bf16[1,128,1536]{2,1,0:T(8,128)(2,1)S(1)}, u32[]{:S(2)}, u32[]{:S(2)}) collective-permute-start(bf16[1,128,1536]{2,1,0:T(8,128)(2,1)S(1)} %bitcast.89), channel_id=1, source_target_pairs={{0,5},{1,6},{2,7},{3,4},{4,9},{5,10},{6,11},{7,8},{8,13},{9,14},{1... | collective-permute-start | bytes 1179656 | tf_op jit(solution)/shard_map/ppermute | solution.py:67
  134.5 12.1 %collective-permute-start.17 = (bf16[1,128,1536]{2,1,0:T(8,128)(2,1)S(1)}, bf16[1,128,1536]{2,1,0:T(8,128)(2,1)S(1)}, u32[]{:S(2)}, u32[]{:S(2)}) collective-permute-start(bf16[1,128,1536]{2,1,0:T(8,128)(2,1)S(1)} %bitcast.88), channel_id=1, source_target_pairs={{0,31},{1,28},{2,29},{3,30},{4,3},{5,0},{6,1},{7,2},{8,7},{9,4},{1... | collective-permute-start | bytes 1179656 | tf_op jit(solution)/shard_map/ppermute | solution.py:67
  155.8 15.1 %collective-permute-start.20 = (bf16[384,1536]{1,0:T(8,128)(2,1)S(1)}, bf16[384,1536]{1,0:T(8,128)(2,1)S(1)}, u32[]{:S(2)}, u32[]{:S(2)}) collective-permute-start(bf16[384,1536]{1,0:T(8,128)(2,1)S(1)} %bitcast.64), channel_id=1, source_target_pairs={{0,16},{1,17},{2,18},{3,19},{4,20},{5,21},{6,22},{7,23},{8,24},{9,... | collective-permute-start | bytes 3538952 | tf_op jit(solution)/shard_map/ppermute | solution.py:67
  171.1 24.8 %collective-permute-start.21 = (bf16[2,384,1536]{2,1,0:T(8,128)(2,1)S(1)}, bf16[2,384,1536]{2,1,0:T(8,128)(2,1)S(1)}, u32[]{:S(2)}, u32[]{:S(2)}) collective-permute-start(bf16[2,384,1536]{2,1,0:T(8,128)(2,1)S(1)} %pad_maximum_fusion), channel_id=1, source_target_pairs={{0,32},{1,33},{2,34},{3,35},{4,36},{5,37},{6,38},{7,39},{8,40},{9,... | collective-permute-start | bytes 7077896 | tf_op jit(solution)/shard_map/ppermute | solution.py:67
  171.9 24.0 %collective-permute-start.22 = (bf16[384,1536]{1,0:T(8,128)(2,1)S(1)}, bf16[384,1536]{1,0:T(8,128)(2,1)S(1)}, u32[]{:S(2)}, u32[]{:S(2)}) collective-permute-start(bf16[384,1536]{1,0:T(8,128)(2,1)S(1)} %collective-permute-done.20.refs_9_), channel_id=1, source_target_pairs={{0,16},{1,17},{2,18},{3,19},{4,20},{5,21},{6,22},{7,23},{8,24},{9,... | collective-permute-start | bytes 3538952 | tf_op jit(solution)/shard_map/ppermute | solution.py:67
  175.0 13.7 %collective-permute-start.23 = (bf16[128,1536]{1,0:T(8,128)(2,1)}, bf16[128,1536]{1,0:T(8,128)(2,1)S(1)}, u32[]{:S(2)}, u32[]{:S(2)}) collective-permute-start(bf16[128,1536]{1,0:T(8,128)(2,1)} %get-tuple-element.127), channel_id=1, source_target_pairs={{28,0},{29,1},{30,2},{31,3},{0,4},{1,5},{2,6},{3,7},{4,8},{5,9},{6... | collective-permute-start | bytes 1179656 | tf_op jit(solution)/shard_map/ppermute | solution.py:67
  175.0 13.7 %collective-permute-start.24 = (bf16[128,1536]{1,0:T(8,128)(2,1)}, bf16[128,1536]{1,0:T(8,128)(2,1)S(1)}, u32[]{:S(2)}, u32[]{:S(2)}) collective-permute-start(bf16[128,1536]{1,0:T(8,128)(2,1)} %get-tuple-element.128), channel_id=1, source_target_pairs={{3,0},{0,1},{1,2},{2,3},{7,4},{4,5},{5,6},{6,7},{11,8},{8,9},{9,10... | collective-permute-start | bytes 1179656 | tf_op jit(solution)/shard_map/ppermute | solution.py:67
  175.0 13.7 %collective-permute-start.25 = (bf16[128,1536]{1,0:T(8,128)(2,1)}, bf16[128,1536]{1,0:T(8,128)(2,1)S(1)}, u32[]{:S(2)}, u32[]{:S(2)}) collective-permute-start(bf16[128,1536]{1,0:T(8,128)(2,1)} %get-tuple-element.129), channel_id=1, source_target_pairs={{31,0},{28,1},{29,2},{30,3},{3,4},{0,5},{1,6},{2,7},{7,8},{4,9},{5... | collective-permute-start | bytes 1179656 | tf_op jit(solution)/shard_map/ppermute | solution.py:67
  195.9 23.5 %collective-permute-start.29 = (bf16[384,1536]{1,0:T(8,128)(2,1)S(1)}, bf16[384,1536]{1,0:T(8,128)(2,1)S(1)}, u32[]{:S(2)}, u32[]{:S(2)}) collective-permute-start(bf16[384,1536]{1,0:T(8,128)(2,1)S(1)} %collective-permute-done.22.refs_10_), channel_id=1, source_target_pairs={{0,16},{1,17},{2,18},{3,19},{4,20},{5,21},{6,22},{7,23},{8,24},{9,... | collective-permute-start | bytes 3538952 | tf_op jit(solution)/shard_map/ppermute | solution.py:67
  198.3 10.6 %collective-permute-start.26 = (bf16[128,1536]{1,0:T(8,128)(2,1)}, bf16[128,1536]{1,0:T(8,128)(2,1)S(1)}, u32[]{:S(2)}, u32[]{:S(2)}) collective-permute-start(bf16[128,1536]{1,0:T(8,128)(2,1)} %get-tuple-element.141), channel_id=1, source_target_pairs={{4,0},{5,1},{6,2},{7,3},{8,4},{9,5},{10,6},{11,7},{12,8},{13,9},{1... | collective-permute-start | bytes 1179656 | tf_op jit(solution)/shard_map/ppermute | solution.py:67
  198.3 12.6 %collective-permute-start.27 = (bf16[128,1536]{1,0:T(8,128)(2,1)}, bf16[128,1536]{1,0:T(8,128)(2,1)S(1)}, u32[]{:S(2)}, u32[]{:S(2)}) collective-permute-start(bf16[128,1536]{1,0:T(8,128)(2,1)} %get-tuple-element.142), channel_id=1, source_target_pairs={{1,0},{2,1},{3,2},{0,3},{5,4},{6,5},{7,6},{4,7},{9,8},{10,9},{11,1... | collective-permute-start | bytes 1179656 | tf_op jit(solution)/shard_map/ppermute | solution.py:67
  198.3 13.3 %collective-permute-start.28 = (bf16[128,1536]{1,0:T(8,128)(2,1)}, bf16[128,1536]{1,0:T(8,128)(2,1)S(1)}, u32[]{:S(2)}, u32[]{:S(2)}) collective-permute-start(bf16[128,1536]{1,0:T(8,128)(2,1)} %get-tuple-element.143), channel_id=1, source_target_pairs={{5,0},{6,1},{7,2},{4,3},{9,4},{10,5},{11,6},{8,7},{13,8},{14,9},{1... | collective-permute-start | bytes 1179656 | tf_op jit(solution)/shard_map/ppermute | solution.py:67
  221.5 18.1 %collective-permute-start.30 = (bf16[2,384,1536]{2,1,0:T(8,128)(2,1)}, bf16[2,384,1536]{2,1,0:T(8,128)(2,1)S(1)}, u32[]{:S(2)}, u32[]{:S(2)}) collective-permute-start(bf16[2,384,1536]{2,1,0:T(8,128)(2,1)} %pad_maximum_fusion.1), channel_id=1, source_target_pairs={{0,32},{1,33},{2,34},{3,35},{4,36},{5,37},{6,38},{7,39},{8,40},{9,... | collective-permute-start | bytes 7077896 | tf_op jit(solution)/shard_map/ppermute | solution.py:67
  (27 other events, 540.8 us)

commit v5 on v4

--- a/solution.py
+++ b/solution.py
@@ -43,14 +43,6 @@
 
 def core_pairs():
     return [(index(f, r, c), index(f ^ 1, r, c)) for f, r, c in every()]
-
-
-def plane_pairs(dx, dy):
-    pairs = []
-    for f, r, c in every():
-        zlo, x = divmod(r, 4)
-        pairs.append((index(f, r, c), index(f, zlo * 4 + (x + dx) % 4, c + dy)))
-    return pairs
 
 
 def depth_pairs():
@@ -164,7 +156,7 @@
     alive[...] = jnp.where(live, 1.0, 0.0)
 
 
-def attend_kernel(half, meta, skv, sq, x, y, dkv, dq, h0, hxy, hd, o0, o1, o2, o3, kaug, vaug, qaug, alive):
+def attend_kernel(half, meta, skv, sq, x, y, d, h3, hd, o0, o1, o2, o3, kaug, vaug, qaug, alive):
     outs = (o0, o1, o2, o3)
 
     @pl.when(pl.program_id(0) == 0)
@@ -175,8 +167,8 @@
             qaug[n, :, HS:] = qaug[0, :, HS:]
         vaug[:, :, HS:] = jnp.ones((STEP, 1024, HS), jnp.bfloat16)
 
-    keys = (skv, x, y, dkv, h0, hxy.at[0], hxy.at[1], hd)
-    asks = (sq.at[0], x.at[2], y.at[2], dq.at[0])
+    keys = (skv, x, y, d, h3.at[0], h3.at[1], h3.at[2], hd)
+    asks = (sq.at[0], x.at[2], y.at[2], d.at[2])
     for h in range(STEP):
         lanes = pl.ds(h * HS, HS)
         for n, ref in enumerate(keys):
@@ -231,78 +223,81 @@
     )(meta, *pieces)
 
 
-def project_kernel(first, shapes, meta, places, *refs):
+def project_kernel(shapes, frame, places, *refs):
     count = len(shapes)
-    attended, sources, (tokens, *rest) = refs[:8], refs[8 : 8 + count], refs[8 + count :]
-    out, lhs, held, sems = rest[-4:]
+    attended, sources, tokens, rest = refs[:8], refs[8 : 8 + count], refs[8 + count], refs[9 + count :]
+    out, lhs, held, given, made, sems = rest[-6:]
     chunks = [ref.at[n] if lead else ref for ref, lead in zip(sources, shapes) for n in range(lead or 1)]
-    step = pl.program_id(0)
-
-    def fetch(n):
-        return pltpu.make_async_copy(chunks[n], held.at[n % 2], sems.at[n % 2])
-
-    @pl.when(step == 0)
-    def _():
-        fetch(0).start()
-        for half in range(2):
-            s = sign_of(half, meta[0])
-            for piece, (a, b) in enumerate(MOVES):
-                i = s + a * (1 - 2 * s)
-                j = s + b * (1 - 2 * s)
-                lhs[half * 4 + i * 2 + j] = attended[half * 4 + piece][...]
-
+    pairs = len(chunks) // 2
+
+    def columns(n):
+        return pl.ds(pl.multiple_of(places[n] * TILE, 128), TILE)
+
+    fetches = [
+        [pltpu.make_async_copy(chunks[n], held.at[n], sems.at[0, n]) for n in range(len(chunks))],
+        [pltpu.make_async_copy(tokens.at[:, :, :, columns(n)], given.at[n], sems.at[1, n]) for n in range(len(chunks))],
+    ]
+    stores = [pltpu.make_async_copy(made.at[n], out.at[:, :, :, columns(n)], sems.at[2, n]) for n in range(len(chunks))]
     for n in range(len(chunks)):
-
-        @pl.when(step == n)
-        def _():
-            fetch(n).wait()
-            if n + 1 < len(chunks):
-                fetch(n + 1).start()
-
-    total = lax.dot_general(
-        lhs[...].reshape(1024, HD), held[lax.rem(step, 2)], (((1,), (1,)), ((), ())), preferred_element_type=jnp.float32
-    ).reshape(2, 2, 2, 2, 8, 8, TILE)
+        fetches[0][n].start()
+        fetches[1][n].start()
     for half in range(2):
-        for i in range(2):
-            block = jnp.concatenate([total[half, i, 0], total[half, i, 1]], axis=2)
-            at = (slice(2 * half, 2 * half + 2), slice(8 * i, 8 * i + 8))
-            out[at] = (block + tokens[at].astype(jnp.float32)).astype(jnp.bfloat16)
-
-
-def project(attended, meta, places, chunks, tokens, partial=None):
+        s = sign_of(half, frame[0])
+        for piece, (a, b) in enumerate(MOVES):
+            i = s + a * (1 - 2 * s)
+            j = s + b * (1 - 2 * s)
+            lhs[half * 4 + i * 2 + j] = attended[half * 4 + piece][...]
+    for pair in range(pairs):
+        for n in (2 * pair, 2 * pair + 1):
+            fetches[0][n].wait()
+            fetches[1][n].wait()
+        total = lax.dot_general(
+            lhs[...].reshape(1024, HD),
+            held[2 * pair : 2 * pair + 2].reshape(2 * TILE, HD),
+            (((1,), (1,)), ((), ())),
+            preferred_element_type=jnp.float32,
+        ).reshape(2, 2, 2, 2, 8, 8, 2 * TILE)
+        for m in range(2):
+            n = 2 * pair + m
+            part = total[..., m * TILE : (m + 1) * TILE]
+            for half in range(2):
+                for i in range(2):
+                    block = jnp.concatenate([part[half, i, 0], part[half, i, 1]], axis=2)
+                    at = (n, slice(2 * half, 2 * half + 2), slice(8 * i, 8 * i + 8))
+                    made[at] = (block + given[at].astype(jnp.float32)).astype(jnp.bfloat16)
+            stores[n].start()
+    for store in stores:
+        store.wait()
+
+
+def project(attended, frame, places, chunks, tokens, partial=None):
     shapes = tuple(chunk.shape[0] if chunk.ndim == 3 else 0 for chunk in chunks)
-    steps = sum(max(lead, 1) for lead in shapes)
+    count = sum(max(lead, 1) for lead in shapes)
     extra = [] if partial is None else [partial]
     any_spec = pl.BlockSpec(memory_space=pl.ANY)
-    block = pl.BlockSpec((4, 16, 16, TILE), lambda t, m, p: (0, 0, 0, p[t]))
-    grid_spec = pltpu.PrefetchScalarGridSpec(
-        num_scalar_prefetch=2,
-        grid=(steps,),
-        in_specs=[pl.BlockSpec((128, HD), lambda t, m, p: (0, 0))] * 8
-        + [any_spec] * len(chunks)
-        + [block]
-        + [any_spec] * len(extra),
-        out_specs=block,
+    smem = pl.BlockSpec(memory_space=pltpu.SMEM)
+    vmem = pl.BlockSpec(memory_space=pltpu.VMEM)
+    return pl.pallas_call(
+        functools.partial(project_kernel, shapes),
+        in_specs=[smem] * 2 + [vmem] * 8 + [any_spec] * (len(chunks) + 1 + len(extra)),
+        out_specs=any_spec,
+        out_shape=jax.ShapeDtypeStruct((4, 16, 16, D), jnp.bfloat16),
         scratch_shapes=[
             pltpu.VMEM((8, 128, HD), jnp.bfloat16),
-            pltpu.VMEM((2, TILE, HD), jnp.bfloat16),
-            pltpu.SemaphoreType.DMA((2,)),
+            pltpu.VMEM((count, TILE, HD), jnp.bfloat16),
+            pltpu.VMEM((count, 4, 16, 16, TILE), jnp.bfloat16),
+            pltpu.VMEM((count, 4, 16, 16, TILE), jnp.bfloat16),
+            pltpu.SemaphoreType.DMA((3, count)),
         ],
-    )
-    return pl.pallas_call(
-        functools.partial(project_kernel, partial is None, shapes),
-        grid_spec=grid_spec,
-        out_shape=jax.ShapeDtypeStruct((4, 16, 16, D), jnp.bfloat16),
         input_output_aliases={} if partial is None else {11 + len(chunks): 0},
         compiler_params=pltpu.CompilerParams(vmem_limit_bytes=VMEM),
-        cost_estimate=pl.CostEstimate(flops=2 * 1024 * HD * TILE * steps, bytes_accessed=3 * 2**20 * (steps + 1), transcendentals=0),
+        cost_estimate=pl.CostEstimate(flops=2 * 1024 * HD * TILE * count, bytes_accessed=3 * 2**20 * (count + 1), transcendentals=0),
         name="project",
-    )(meta, places, *attended, *chunks, tokens, *extra)
-
-
-def ring_order(own, first, second, third, place):
-    row = jnp.stack([third, second, first, own, third, second, first])
-    return lax.dynamic_slice_in_dim(row, 3 - place, 4, axis=0).reshape((-1,) + own.shape[1:])
+    )(frame, places, *attended, *chunks, tokens, *extra)
+
+
+def plane_groups():
+    return [[index(f, zlo * 4 + x, c) for x in range(4) for c in range(C)] for f in range(F) for zlo in range(2)]
 
 
 def weight_places(f, r):
@@ -312,7 +307,7 @@
         at = [(z + n * (2 * k - 1) + 4) & 3 for n in range(4)]
         places.append([((a >> 1) * 2 + k) * 2 + (a & 1) for a in at])
     (a0, a1, a2, a3), (b0, b1, b2, b3) = places
-    return jnp.stack([a0, a1, a2, b0, b1, a3, b2, b3]).astype(jnp.int32)
+    return jnp.stack([a0, a1, b0, b1, a2, a3, b2, b3]).astype(jnp.int32)
 
 
 def together(*values):
@@ -321,55 +316,50 @@
 
 def local(tokens_in, queries, key_rows, value_rows, out_weight, row_valid):
     f, r, c = (lax.axis_index(a) for a in AXES)
+    frame = f.astype(jnp.int32).reshape(1)
     meta = jnp.stack([f, r, c, jnp.sum(row_valid)]).astype(jnp.int32)
     places = weight_places(f, r)
     split = lambda a: a.reshape(4, 2, 8, 2, 8, HD)
-    arrays = (meta, split(key_rows), split(value_rows), split(queries))
-    shard = out_weight.T
-    shards = [send(shard, plane_pairs(0, d)) for d in (1, 2, 3)]
+    arrays = (split(key_rows), split(value_rows), split(queries))
+    chunk = lax.all_gather(out_weight.T, AXES, axis=0, tiled=True, axis_index_groups=plane_groups())
 
     row, col, both = MOVES[1:]
     go = lambda value, half, move: send(value, window_pairs(half, *move))
     up = lambda value: send(value, frame_pairs(1))
     down = lambda value: send(value, frame_pairs(-1))
-
-    skv0, skv1, x0, y0 = pack(((0, 0, "kv"), (1, 0, "kv"), (0, 1, "kvq"), (0, 2, "kvq")), *arrays)
-    x0, y0, skv1, skv0, meta, *shards = together(x0, y0, skv1, skv0, meta, *shards)
-    strip = ring_order(shard, *shards, c)
-    x1, y1, dkv0, dkv1, dq0, dq1, sq0, sq1 = pack(
-        ((1, 1, "kvq"), (1, 2, "kvq"), (0, 3, "kv"), (1, 3, "kv"), (0, 3, "q"), (1, 3, "q"), (0, 0, "q"), (1, 0, "q")), meta, *arrays[1:]
+    swap = lambda value: send(value, core_pairs())
+    turn = lambda value: send(value, depth_pairs())
+    back = lambda half, mixed: [mixed[0]] + [send(mixed[n], window_pairs(half, *MOVES[n], back=True)) for n in (1, 2, 3)]
+
+    x0, y0, x1, y1 = pack(((0, 1, "kvq"), (0, 2, "kvq"), (1, 1, "kvq"), (1, 2, "kvq")), frame, *arrays)
+    x0, y0, x1, y1, frame = together(x0, y0, x1, y1, frame)
+    first = go(x0, 0, row), go(y0, 0, col), go(x1, 1, row), go(y1, 1, col)
+    skv0, skv1, d0, d1, sq0, sq1 = pack(
+        ((0, 0, "kv"), (1, 0, "kv"), (0, 3, "kvq"), (1, 3, "kvq"), (0, 0, "q"), (1, 0, "q")), frame, *arrays
     )
-    first = go(x0, 0, row), go(y0, 0, col), up(skv1), down(skv0)
-    x1, y1, strip, *first = together(x1, y1, strip, *first)
-    x0, y0, up0, down0 = first
-    second = go(x1, 1, row), go(y1, 1, col), *(send(strip, plane_pairs(d, 0)) for d in (1, 2, 3))
-    dkv0, dkv1, x0, y0, *second = together(dkv0, dkv1, x0, y0, *second)
-    x1, y1, *strips = second
-    chunk = ring_order(strip, *strips, r & 3)
-    third = go(dkv0, 0, both), go(dkv1, 1, both), down(halo_pack(x0, y0)), up(halo_pack(x1, y1))
-    dq0, dq1, chunk, *third = together(dq0, dq1, chunk, *third)
-    dkv0, dkv1, down1, up1 = third
-    fourth = go(dq0, 0, both), go(dq1, 1, both), down(dkv0), up(dkv1)
-    chunk, *fourth = together(chunk, *fourth)
-    dq0, dq1, down2, up2 = fourth
-
-    ring = [chunk, send(chunk, depth_pairs())]
-    mixed1 = attend(1, meta, skv1, sq1, x1, y1, dkv1, dq1, down0, down1, down2)
-    ring[1], skv0, *mixed1 = together(ring[1], skv0, *mixed1)
-    back = lambda half, mixed: [mixed[0]] + [send(mixed[n], window_pairs(half, *MOVES[n], back=True)) for n in (1, 2, 3)]
-    near = send(jnp.stack(ring[:2]), core_pairs())
-    ring.append(send(ring[1], depth_pairs()))
+    d0, d1, *first = together(d0, d1, *first)
+    x0, y0, x1, y1 = first
+    second = go(d0, 0, both), go(d1, 1, both), down(halo_pack(skv0, x0, y0)), up(halo_pack(skv1, x1, y1))
+    chunk, *second = together(chunk, *second)
+    d0, d1, down3, up3 = second
+    third = down(d0[:2]), up(d1[:2])
+    chunk, downd, upd = together(chunk, *third)
+
+    c1, other0 = turn(chunk), swap(chunk)
+    mixed1 = attend(1, meta, skv1, sq1, x1, y1, d1, down3, downd)
+    c1, other0, skv0, *mixed1 = together(c1, other0, skv0, *mixed1)
+    c2 = turn(c1)
     attended1 = back(1, mixed1)
-    mixed0 = attend(0, meta, skv0, sq0, x0, y0, dkv0, dq0, up0, up1, up2)
-    near, ring[2], *rest = together(near, ring[2], *attended1, *mixed0)
+    mixed0 = attend(0, meta, skv0, sq0, x0, y0, d0, up3, upd)
+    c2, *rest = together(c2, *attended1, *mixed0)
     attended1, mixed0 = rest[:4], rest[4:]
     attended0 = back(0, mixed0)
-    ring.append(send(ring[2], depth_pairs()))
+    c3, other1 = turn(c2), swap(c1)
     attended = attended0 + attended1
-    out = project(attended, meta, places[:5], (*ring[:3], near), tokens_in)
-    last = together(ring[3], *attended)[0]
-    far = send(jnp.stack([ring[2], last]), core_pairs())
-    return project(attended, meta, places[5:], (ring[3], far), tokens_in, out)
+    out = project(attended, frame, places[:4], (chunk, c1, other0, other1), tokens_in)
+    last = together(c3, *attended)[0]
+    pair = jnp.stack([c2, last])
+    return project(attended, frame, places[4:], (pair, swap(pair)), tokens_in, out)
 
 
 def solution(mesh):

time: 252 us -> 234 us (0.929)
  between operations: 0.69 us -> 13.7 us
  waiting for transfers between devices: 130 us -> 117 us
  starting transfers between devices: 45.3 us -> 33.2 us
  Pallas kernels: 67.3 us -> 64.7 us
    ppermute x31 -> x22, waiting for transfers between devices: 130 us -> 70.3 us  [send(): return lax.ppermute(value, AXES, pairs)]
    all_gather x0 -> x1, waiting for transfers between devices: none -> 46.6 us  [local(): lax.all_gather(out_weight.T, AXES, axis=0, tiled=True, axis_index_groups=...]
    ppermute x31 -> x22, starting transfers between devices: 45.3 us -> 33.1 us  [send(): return lax.ppermute(value, AXES, pairs)]
  transfers between devices with their start and end apart: 31 -> 23, of which waited for: 18 -> 13; matrix products, arithmetic and copies ran while one was open for 2% -> 1% of each run, Pallas kernels for 22% -> 20%
where the time goes in v5:
time: 234 us
  waiting for transfers between devices  117 us (50%)
  Pallas kernels  64.7 us (28%)
  starting transfers between devices  33.2 us (14%)
  between operations  13.7 us (6%)
  other arithmetic  3.35 us (1%)
    ppermute x22, waiting for transfers between devices, send(): return lax.ppermute(value, AXES, pairs)  70.3 us
    all_gather x1, waiting for transfers between devices, local(): lax.all_gather(out_weight.T, AXES, axis=0, tiled=True, axis_index_groups=...  46.6 us
    ppermute x22, starting transfers between devices, send(): return lax.ppermute(value, AXES, pairs)  33.1 us
    pallas_call x2, Pallas kernels, attend(): pl.pallas_call(functools.partial(attend_kernel, half), grid=(H // STEP,),...  27.2 us
    pallas_call x2, Pallas kernels, project(): pl.pallas_call(functools.partial(project_kernel, shapes), in_specs=[smem]...  23.6 us
    pallas_call x2, Pallas kernels, pack(): pl.pallas_call(functools.partial(pack_kernel, parts), out_shape=[jax.Shap...  8.65 us
    pallas_call x2, Pallas kernels, halo_pack(): pl.pallas_call(halo_kernel, out_shape=jax.ShapeDtypeStruct((count, 2, 128...  5.29 us
  transfers between devices with their start and end apart: 23, of which 13 were waited for; matrix products, arithmetic and copies ran while one was open for 1% of the time, Pallas kernels for 20%

profile of v5, /device:TPU:1, one launch (start us, length us, event | category | flops | bytes accessed | tf_op | source)
XLA Modules:
  0.0 234.2 jit_solution(1725340868833898651)
XLA Ops:
  6.5 4.3 %pack.2 = (bf16[3,2,8,8,1536]{4,3,2,1,0:T(8,128)(2,1)}, bf16[3,2,8,8,1536]{4,3,2,1,0:T(8,128)(2,1)}, bf16[3,2,8,8,1536]{4,3,2,1,0:T(8,128)(2,1)}, bf16[3,2,8,8,1536]{4,3,2,1,0:T(8,128)(2,1)}) custom-call(s32[1]{0:T(128)} %bitcast.meta.frame, bf16[4,2,8,2,8,1536]{5,4,3,2,1,0:T(8,128)(2,1)} %bitcast.28, bf16[4,2,8,2,8,1536]{5,4,3,2,1,0:T(8,128)(2,1)} %bitcast.30, ...), custom_call_target="tpu_custom_call" | custom-call | bytes 12582912 | tf_op jit(solution)/shard_map/pack/pallas_call | solution.py:98
  10.9 4.7 %collective-permute-start = (bf16[3,128,1536]{2,1,0:T(8,128)(2,1)}, bf16[3,128,1536]{2,1,0:T(8,128)(2,1)S(1)}, u32[]{:S(2)}, u32[]{:S(2)}) collective-permute-start(bf16[3,128,1536]{2,1,0:T(8,128)(2,1)} %bitcast.45), channel_id=1, source_target_pairs={{0,4},{1,5},{2,6},{3,7},{4,8},{5,9},{6,10},{7,11},{8,12},{9,13},{1... | collective-permute-start | bytes 3538952 | tf_op jit(solution)/shard_map/ppermute | solution.py:59
  15.6 2.7 %collective-permute-start.1 = (bf16[3,128,1536]{2,1,0:T(8,128)(2,1)}, bf16[3,128,1536]{2,1,0:T(8,128)(2,1)S(1)}, u32[]{:S(2)}, u32[]{:S(2)}) collective-permute-start(bf16[3,128,1536]{2,1,0:T(8,128)(2,1)} %bitcast.44), channel_id=1, source_target_pairs={{0,1},{1,2},{2,3},{3,0},{4,5},{5,6},{6,7},{7,4},{8,9},{9,10},{10,1... | collective-permute-start | bytes 3538952 | tf_op jit(solution)/shard_map/ppermute | solution.py:59
  18.3 4.3 %pack.3 = (bf16[2,2,8,8,1536]{4,3,2,1,0:T(8,128)(2,1)}, bf16[2,2,8,8,1536]{4,3,2,1,0:T(8,128)(2,1)}, bf16[3,2,8,8,1536]{4,3,2,1,0:T(8,128)(2,1)}, bf16[3,2,8,8,1...) custom-call(s32[1]{0:T(128)} %bitcast.meta.frame, ...), custom_call_target="tpu_custom_call" | custom-call | bytes 12582912 | tf_op jit(solution)/shard_map/pack/pallas_call | solution.py:98
  22.7 16.2 %collective-permute-done.refs_1_.x = bf16[3,128,1536]{2,1,0:T(8,128)(2,1)S(1)} collective-permute-done((bf16[3,128,1536]{2,1,0:T(8,128)(2,1)}, bf16[3,128,1536]{2,1,0:T(8,128)(2,1)S(1)}, u32[]{:S(2)}, u32[]{:S(2)}) %collective-permute-start) | collective-permute-done | bytes 1179680 | tf_op jit(solution)/shard_map/ppermute | solution.py:59
  38.8 3.8 %collective-permute-done.1.refs_2_.y = bf16[3,128,1536]{2,1,0:T(8,128)(2,1)S(1)} collective-permute-done((bf16[3,128,1536]{2,1,0:T(8,128)(2,1)}, bf16[3,128,1536]{2,1,0:T(8,128)(2,1)S(1)}, u32[]{:S(2)}, u32[]{:S(2)}) %collective-permute-start.1) | collective-permute-done | bytes 1179680 | tf_op jit(solution)/shard_map/ppermute | solution.py:59
  44.5 2.6 %halo_pack.3 = bf16[3,2,128,1536]{3,2,1,0:T(8,128)(2,1)} custom-call(bf16[2,128,1536]{2,1,0:T(8,128)(2,1)} %bitcast.38, bf16[3,128,1536]{2,1,0:T(8,128)(2,1)} %copy-done.12, bf16[3,128,1536]{2,1,0:T(8,128)(2,1)} %copy-done.13), custom_call_target="tpu_custom_call" | custom-call | bytes 4718592 | tf_op jit(solution)/shard_map/halo_pack/pallas_call | solution.py:119
  47.1 6.4 %collective-permute-start.7 = (bf16[3,2,128,1536]{3,2,1,0:T(8,128)(2,1)}, bf16[3,2,128,1536]{3,2,1,0:T(8,128)(2,1)}, u32[]{:S(2)}, u32[]{:S(2)}) collective-permute-start(bf16[3,2,128,1536]{3,2,1,0:T(8,128)(2,1)} %halo_pack.3), channel_id=1, source_target_pairs={{0,32},{1,33},{2,34},{3,35},{4,36},{5,37},{6,38},{7,39},{8,40},{9,... | collective-permute-start | bytes 7077896 | tf_op jit(solution)/shard_map/ppermute | solution.py:59
  53.6 2.7 %halo_pack.2 = bf16[3,2,128,1536]{3,2,1,0:T(8,128)(2,1)} custom-call(bf16[2,128,1536]{2,1,0:T(8,128)(2,1)} %bitcast.36, bf16[3,128,1536]{2,1,0:T(8,128)(2,1)} %copy-done.10, bf16[3,128,1536]{2,1,0:T(8,128)(2,1)} %copy-done.11), custom_call_target="tpu_custom_call" | custom-call | bytes 4718592 | tf_op jit(solution)/shard_map/halo_pack/pallas_call | solution.py:119
  56.3 1.9 collective-permute-start.6
  58.2 3.8 %collective-permute-start.4 = (bf16[3,128,1536]{2,1,0:T(8,128)(2,1)}, bf16[3,128,1536]{2,1,0:T(8,128)(2,1)S(1)}, u32[]{:S(2)}, u32[]{:S(2)}) collective-permute-start(bf16[3,128,1536]{2,1,0:T(8,128)(2,1)} %bitcast.13), channel_id=1, source_target_pairs={{0,5},{1,6},{2,7},{3,4},{4,9},{5,10},{6,11},{7,8},{8,13},{9,14},{1... | collective-permute-start | bytes 3538952 | tf_op jit(solution)/shard_map/ppermute | solution.py:59
  62.0 46.6 %all-gather.2.cloned.1.call-done.refs_8_ = bf16[384,1536]{1,0:T(8,128)(2,1)} async-done(((bf16[24,1536]{1,0:T(8,128)(2,1)}), bf16[384,1536]{1,0:T(8,128)(2,1)}) %all-gather.2.cloned.1.call-update) | async-done | bytes 1179664 | tf_op jit(solution)/shard_map/all_gather | solution.py:324
  108.7 4.8 %collective-permute-done.6.h3 = bf16[3,2,128,1536]{3,2,1,0:T(8,128)(2,1)} collective-permute-done((bf16[3,2,128,1536]{3,2,1,0:T(8,128)(2,1)}, bf16[3,2,128,1536]{3,2,1,0:T(8,128)(2,1)}, u32[]{:S(2)}, u32[]{:S(2)}) %collective-permute-start.6) | collective-permute-done | bytes 2359328 | tf_op jit(solution)/shard_map/ppermute | solution.py:59
  113.7 2.8 %collective-permute-start.9 = (bf16[2,128,1536]{2,1,0:T(8,128)(2,1)S(1)}, bf16[2,128,1536]{2,1,0:T(8,128)(2,1)S(1)}, u32[]{:S(2)}, u32[]{:S(2)}) collective-permute-start(bf16[2,128,1536]{2,1,0:T(8,128)(2,1)S(1)} %slice.11), channel_id=1, source_target_pairs={{0,32},{1,33},{2,34},{3,35},{4,36},{5,37},{6,38},{7,39},{8,40},{9,... | collective-permute-start | bytes 2359304 | tf_op jit(solution)/shard_map/ppermute | solution.py:59
  116.5 1.9 collective-permute-start.8
  118.4 7.0 %collective-permute-done.9.hd = bf16[2,128,1536]{2,1,0:T(8,128)(2,1)S(1)} collective-permute-done((bf16[2,128,1536]{2,1,0:T(8,128)(2,1)S(1)}, bf16[2,128,1536]{2,1,0:T(8,128)(2,1)S(1)}, u32[]{:S(2)}, u32[]{:S(2)}) %collective-permute-start.9) | collective-permute-done | bytes 786464 | tf_op jit(solution)/shard_map/ppermute | solution.py:59
  125.4 5.9 %collective-permute-done.8.hd = bf16[2,128,1536]{2,1,0:T(8,128)(2,1)S(1)} collective-permute-done((bf16[2,128,1536]{2,1,0:T(8,128)(2,1)S(1)}, bf16[2,128,1536]{2,1,0:T(8,128)(2,1)S(1)}, u32[]{:S(2)}, u32[]{:S(2)}) %collective-permute-start.8) | collective-permute-done | bytes 786464 | tf_op jit(solution)/shard_map/ppermute | solution.py:59
  132.2 1.3 pad_add_fusion.1.meta
  133.4 13.6 %attend.2 = (bf16[128,1536]{1,0:T(8,128)(2,1)}, bf16[128,1536]{1,0:T(8,128)(2,1)}, bf16[128,1536]{1,0:T(8,128)(2,1)}, bf16[128,1536]{1,0:T(8,128)(2,1)}) custom-call(s32[4]{0:T(128)} %pad_add_fusion.1.meta, bf16[2,128,1536]{2,1,0:T(8,128)(2,1)} %bitcast.39, bf16[1,128,1536]{2,1,0:T(8,128)(2,1)} %bitcast.47, bf16[3,128,1536]{2,1,0:T(8,128)(2,1)} %copy-done.12, ...), custom_call_target="tpu_custom_call" | custom-call | flops 6442450944 | bytes 10485760 | tf_op jit(solution)/shard_map/attend/pallas_call | solution.py:208
  147.8 2.4 %collective-permute-start.13 = (bf16[128,1536]{1,0:T(8,128)(2,1)}, bf16[128,1536]{1,0:T(8,128)(2,1)S(1)}, u32[]{:S(2)}, u32[]{:S(2)}) collective-permute-start(bf16[128,1536]{1,0:T(8,128)(2,1)} %get-tuple-element.91), channel_id=1, source_target_pairs={{28,0},{29,1},{30,2},{31,3},{0,4},{1,5},{2,6},{3,7},{4,8},{5,9},{6... | collective-permute-start | bytes 1179656 | tf_op jit(solution)/shard_map/ppermute | solution.py:59
  150.2 0.9 collective-permute-start.14
  151.2 1.0 collective-permute-start.15
  152.2 13.6 %attend.3 = (bf16[128,1536]{1,0:T(8,128)(2,1)}, bf16[128,1536]{1,0:T(8,128)(2,1)}, bf16[128,1536]{1,0:T(8,128)(2,1)}, bf16[128,1536]{1,0:T(8,128)(2,1)}) custom-call(s32[4]{0:T(128)} %pad_add_fusion.1.meta, bf16[2,128,1536]{2,1,0:T(8,128)(2,1)} %bitcast.37, bf16[1,128,1536]{2,1,0:T(8,128)(2,1)} %bitcast.46, bf16[3,128,1536]{2,1,0:T(8,128)(2,1)} %copy-done.10, ...), custom_call_target="tpu_custom_call" | custom-call | flops 6442450944 | bytes 10485760 | tf_op jit(solution)/shard_map/attend/pallas_call | solution.py:208
  165.9 4.9 %collective-permute-done.12 = bf16[384,1536]{1,0:T(8,128)(2,1)S(1)} collective-permute-done((bf16[384,1536]{1,0:T(8,128)(2,1)}, bf16[384,1536]{1,0:T(8,128)(2,1)S(1)}, u32[]{:S(2)}, u32[]{:S(2)}) %collective-permute-start.12) | collective-permute-done | bytes 1179680 | tf_op jit(solution)/shard_map/ppermute | solution.py:59
  172.1 8.4 %collective-permute-done.16.refs_1_ = bf16[128,1536]{1,0:T(8,128)(2,1)S(1)} collective-permute-done((bf16[128,1536]{1,0:T(8,128)(2,1)}, bf16[128,1536]{1,0:T(8,128)(2,1)S(1)}, u32[]{:S(2)}, u32[]{:S(2)}) %collective-permute-start.16) | collective-permute-done | bytes 393248 | tf_op jit(solution)/shard_map/ppermute | solution.py:59
  180.5 6.0 %collective-permute-done.18.refs_3_ = bf16[128,1536]{1,0:T(8,128)(2,1)S(1)} collective-permute-done((bf16[128,1536]{1,0:T(8,128)(2,1)}, bf16[128,1536]{1,0:T(8,128)(2,1)S(1)}, u32[]{:S(2)}, u32[]{:S(2)}) %collective-permute-start.18) | collective-permute-done | bytes 393248 | tf_op jit(solution)/shard_map/ppermute | solution.py:59
  186.4 7.8 %collective-permute-done.19 = bf16[384,1536]{1,0:T(8,128)(2,1)S(1)} collective-permute-done((bf16[384,1536]{1,0:T(8,128)(2,1)S(1)}, bf16[384,1536]{1,0:T(8,128)(2,1)S(1)}, u32[]{:S(2)}, u32[]{:S(2)}) %collective-permute-start.19) | collective-permute-done | bytes 1179680 | tf_op jit(solution)/shard_map/ppermute | solution.py:59
  194.6 2.2 collective-permute-start.20
  198.0 4.7 %collective-permute-done.21.refs_11_ = bf16[384,1536]{1,0:T(8,128)(2,1)S(1)} collective-permute-done((bf16[384,1536]{1,0:T(8,128)(2,1)}, bf16[384,1536]{1,0:T(8,128)(2,1)S(1)}, u32[]{:S(2)}, u32[]{:S(2)}) %collective-permute-start.21) | collective-permute-done | bytes 1179680 | tf_op jit(solution)/shard_map/ppermute | solution.py:59
  202.7 1.0 copy-done.9
  203.7 11.8 %project.2.refs_11_ = bf16[4,16,16,3072]{3,2,1,0:T(8,128)(2,1)} custom-call(s32[1]{0:T(128)} %bitcast.meta.frame, s32[4]{0:T(128)} %pad_add_fusion.2.places, bf16[128,1536]{1,0:T(8,128)(2,1)} %get-tuple-element.102.refs_0_, bf16[128,1536]{1,0:T(8,128)(2,1)} %copy-done.4, bf16[128,1536]{1,0:T(8,128)(2,1)} %copy-done.5, bf16[128,1536]{1,0:T(8,128)(2,1)} %copy-done.6, ...), custom_call_target="tpu_custom_call" | custom-call | flops 4831838208 | bytes 15728640 | tf_op jit(solution)/shard_map/project/pallas_call | solution.py:280
  215.5 11.8 %project.3 = bf16[4,16,16,3072]{3,2,1,0:T(8,128)(2,1)} custom-call(s32[1]{0:T(128)} %bitcast.meta.frame, s32[4]{0:T(128)} %pad_add_fusion.places, bf16[128,1536]{1,0:T(8,128)(2,1)} %get-tuple-element.102.refs_0_, bf16[128,1536]{1,0:T(8,128)(2,1)} %copy-done.4, bf16[128,1536]{1,0:T(8,128)(2,1)} %copy-done.5, ...), custom_call_target="tpu_custom_call", output_to_operand_aliasing={{}: (13, {})} | custom-call | flops 4831838208 | bytes 15728640 | tf_op jit(solution)/shard_map/project/pallas_call | solution.py:280
  (70 shorter events, 6.5 us)
Async XLA Ops:
  6.5 102.1 %all-gather.2.cloned.1.call-start = ((), (), s32[]{:S(2)}) async-start(), calls=%async_computation | async-start | bytes 1253376 | tf_op jit(solution)/shard_map/all_gather | solution.py:324
  10.9 28.0 %collective-permute-start = (bf16[3,128,1536]{2,1,0:T(8,128)(2,1)}, bf16[3,128,1536]{2,1,0:T(8,128)(2,1)S(1)}, u32[]{:S(2)}, u32[]{:S(2)}) collective-permute-start(bf16[3,128,1536]{2,1,0:T(8,128)(2,1)} %bitcast.45), channel_id=1, source_target_pairs={{0,4},{1,5},{2,6},{3,7},{4,8},{5,9},{6,10},{7,11},{8,12},{9,13},{1... | collective-permute-start | bytes 3538952 | tf_op jit(solution)/shard_map/ppermute | solution.py:59
  15.6 27.1 %collective-permute-start.1 = (bf16[3,128,1536]{2,1,0:T(8,128)(2,1)}, bf16[3,128,1536]{2,1,0:T(8,128)(2,1)S(1)}, u32[]{:S(2)}, u32[]{:S(2)}) collective-permute-start(bf16[3,128,1536]{2,1,0:T(8,128)(2,1)} %bitcast.44), channel_id=1, source_target_pairs={{0,1},{1,2},{2,3},{3,0},{4,5},{5,6},{6,7},{7,4},{8,9},{9,10},{10,1... | collective-permute-start | bytes 3538952 | tf_op jit(solution)/shard_map/ppermute | solution.py:59
  18.3 24.6 %collective-permute-start.2 = (bf16[3,128,1536]{2,1,0:T(8,128)(2,1)}, bf16[3,128,1536]{2,1,0:T(8,128)(2,1)S(1)}, u32[]{:S(2)}, u32[]{:S(2)}) collective-permute-start(bf16[3,128,1536]{2,1,0:T(8,128)(2,1)} %bitcast.43), channel_id=1, source_target_pairs={{0,28},{1,29},{2,30},{3,31},{4,0},{5,1},{6,2},{7,3},{8,4},{9,5},{1... | collective-permute-start | bytes 3538952 | tf_op jit(solution)/shard_map/ppermute | solution.py:59
  18.3 25.2 %collective-permute-start.3 = (bf16[3,128,1536]{2,1,0:T(8,128)(2,1)}, bf16[3,128,1536]{2,1,0:T(8,128)(2,1)S(1)}, u32[]{:S(2)}, u32[]{:S(2)}) collective-permute-start(bf16[3,128,1536]{2,1,0:T(8,128)(2,1)} %bitcast.42), channel_id=1, source_target_pairs={{0,3},{1,0},{2,1},{3,2},{4,7},{5,4},{6,5},{7,6},{8,11},{9,8},{10,9... | collective-permute-start | bytes 3538952 | tf_op jit(solution)/shard_map/ppermute | solution.py:59
  47.1 61.6 %collective-permute-start.7 = (bf16[3,2,128,1536]{3,2,1,0:T(8,128)(2,1)}, bf16[3,2,128,1536]{3,2,1,0:T(8,128)(2,1)}, u32[]{:S(2)}, u32[]{:S(2)}) collective-permute-start(bf16[3,2,128,1536]{3,2,1,0:T(8,128)(2,1)} %halo_pack.3), channel_id=1, source_target_pairs={{0,32},{1,33},{2,34},{3,35},{4,36},{5,37},{6,38},{7,39},{8,40},{9,... | collective-permute-start | bytes 7077896 | tf_op jit(solution)/shard_map/ppermute | solution.py:59
  56.3 57.3 %collective-permute-start.6 = (bf16[3,2,128,1536]{3,2,1,0:T(8,128)(2,1)}, bf16[3,2,128,1536]{3,2,1,0:T(8,128)(2,1)}, u32[]{:S(2)}, u32[]{:S(2)}) collective-permute-start(bf16[3,2,128,1536]{3,2,1,0:T(8,128)(2,1)} %halo_pack.2), channel_id=1, source_target_pairs={{32,0},{33,1},{34,2},{35,3},{36,4},{37,5},{38,6},{39,7},{40,8},{41... | collective-permute-start | bytes 7077896 | tf_op jit(solution)/shard_map/ppermute | solution.py:59
  58.2 50.4 %collective-permute-start.4 = (bf16[3,128,1536]{2,1,0:T(8,128)(2,1)}, bf16[3,128,1536]{2,1,0:T(8,128)(2,1)S(1)}, u32[]{:S(2)}, u32[]{:S(2)}) collective-permute-start(bf16[3,128,1536]{2,1,0:T(8,128)(2,1)} %bitcast.13), channel_id=1, source_target_pairs={{0,5},{1,6},{2,7},{3,4},{4,9},{5,10},{6,11},{7,8},{8,13},{9,14},{1... | collective-permute-start | bytes 3538952 | tf_op jit(solution)/shard_map/ppermute | solution.py:59
  62.0 46.7 %collective-permute-start.5 = (bf16[3,128,1536]{2,1,0:T(8,128)(2,1)S(1)}, bf16[3,128,1536]{2,1,0:T(8,128)(2,1)S(1)}, u32[]{:S(2)}, u32[]{:S(2)}) collective-permute-start(bf16[3,128,1536]{2,1,0:T(8,128)(2,1)S(1)} %bitcast.41), channel_id=1, source_target_pairs={{0,31},{1,28},{2,29},{3,30},{4,3},{5,0},{6,1},{7,2},{8,7},{9,4},{1... | collective-permute-start | bytes 3538952 | tf_op jit(solution)/shard_map/ppermute | solution.py:59
  113.6 17.7 %copy-start.7 = (bf16[384,1536]{1,0:T(8,128)(2,1)S(1)}, bf16[384,1536]{1,0:T(8,128)(2,1)}, u32[]{:S(2)}) copy-start(bf16[384,1536]{1,0:T(8,128)(2,1)} %all-gather.2.cloned.1.call-done.refs_8_) | copy-start | bytes 3538948
  113.6 17.8 %copy-start.19 = (s32[128]{0:T(128)S(1)}, s32[128]{0:T(128)}, u32[]{:S(2)}) copy-start(s32[128]{0:T(128)} %param.11) | copy-start | bytes 1540
  113.7 11.7 %collective-permute-start.9 = (bf16[2,128,1536]{2,1,0:T(8,128)(2,1)S(1)}, bf16[2,128,1536]{2,1,0:T(8,128)(2,1)S(1)}, u32[]{:S(2)}, u32[]{:S(2)}) collective-permute-start(bf16[2,128,1536]{2,1,0:T(8,128)(2,1)S(1)} %slice.11), channel_id=1, source_target_pairs={{0,32},{1,33},{2,34},{3,35},{4,36},{5,37},{6,38},{7,39},{8,40},{9,... | collective-permute-start | bytes 2359304 | tf_op jit(solution)/shard_map/ppermute | solution.py:59
  116.5 14.8 %collective-permute-start.8 = (bf16[2,128,1536]{2,1,0:T(8,128)(2,1)S(1)}, bf16[2,128,1536]{2,1,0:T(8,128)(2,1)S(1)}, u32[]{:S(2)}, u32[]{:S(2)}) collective-permute-start(bf16[2,128,1536]{2,1,0:T(8,128)(2,1)S(1)} %slice.10), channel_id=1, source_target_pairs={{32,0},{33,1},{34,2},{35,3},{36,4},{37,5},{38,6},{39,7},{40,8},{41... | collective-permute-start | bytes 2359304 | tf_op jit(solution)/shard_map/ppermute | solution.py:59
  131.3 15.7 %collective-permute-start.11 = (bf16[384,1536]{1,0:T(8,128)(2,1)S(1)}, bf16[384,1536]{1,0:T(8,128)(2,1)S(1)}, u32[]{:S(2)}, u32[]{:S(2)}) collective-permute-start(bf16[384,1536]{1,0:T(8,128)(2,1)S(1)} %copy-done.7), channel_id=1, source_target_pairs={{0,32},{1,33},{2,34},{3,35},{4,36},{5,37},{6,38},{7,39},{8,40},{9,... | collective-permute-start | bytes 3538952 | tf_op jit(solution)/shard_map/ppermute | solution.py:59
  131.4 15.7 %collective-permute-start.10 = (bf16[384,1536]{1,0:T(8,128)(2,1)S(1)}, bf16[384,1536]{1,0:T(8,128)(2,1)}, u32[]{:S(2)}, u32[]{:S(2)}) collective-permute-start(bf16[384,1536]{1,0:T(8,128)(2,1)S(1)} %copy-done.7), channel_id=1, source_target_pairs={{0,16},{1,17},{2,18},{3,19},{4,20},{5,21},{6,22},{7,23},{8,24},{9,... | collective-permute-start | bytes 3538952 | tf_op jit(solution)/shard_map/ppermute | solution.py:59
  147.0 18.8 %copy-start.8 = (bf16[384,1536]{1,0:T(8,128)(2,1)}, bf16[384,1536]{1,0:T(8,128)(2,1)S(1)}, u32[]{:S(2)}) copy-start(bf16[384,1536]{1,0:T(8,128)(2,1)S(1)} %collective-permute-done.11.refs_10_) | copy-start | bytes 3538948
  147.0 23.8 %collective-permute-start.12 = (bf16[384,1536]{1,0:T(8,128)(2,1)}, bf16[384,1536]{1,0:T(8,128)(2,1)S(1)}, u32[]{:S(2)}, u32[]{:S(2)}) collective-permute-start(bf16[384,1536]{1,0:T(8,128)(2,1)} %collective-permute-done.10.refs_9_), channel_id=1, source_target_pairs={{0,16},{1,17},{2,18},{3,19},{4,20},{5,21},{6,22},{7,23},{8,24},{9,... | collective-permute-start | bytes 3538952 | tf_op jit(solution)/shard_map/ppermute | solution.py:59
  147.8 18.0 %collective-permute-start.13 = (bf16[128,1536]{1,0:T(8,128)(2,1)}, bf16[128,1536]{1,0:T(8,128)(2,1)S(1)}, u32[]{:S(2)}, u32[]{:S(2)}) collective-permute-start(bf16[128,1536]{1,0:T(8,128)(2,1)} %get-tuple-element.91), channel_id=1, source_target_pairs={{28,0},{29,1},{30,2},{31,3},{0,4},{1,5},{2,6},{3,7},{4,8},{5,9},{6... | collective-permute-start | bytes 1179656 | tf_op jit(solution)/shard_map/ppermute | solution.py:59
  150.2 15.6 %collective-permute-start.14 = (bf16[128,1536]{1,0:T(8,128)(2,1)}, bf16[128,1536]{1,0:T(8,128)(2,1)S(1)}, u32[]{:S(2)}, u32[]{:S(2)}) collective-permute-start(bf16[128,1536]{1,0:T(8,128)(2,1)} %get-tuple-element.92), channel_id=1, source_target_pairs={{3,0},{0,1},{1,2},{2,3},{7,4},{4,5},{5,6},{6,7},{11,8},{8,9},{9,10... | collective-permute-start | bytes 1179656 | tf_op jit(solution)/shard_map/ppermute | solution.py:59
  151.2 14.7 %collective-permute-start.15 = (bf16[128,1536]{1,0:T(8,128)(2,1)}, bf16[128,1536]{1,0:T(8,128)(2,1)S(1)}, u32[]{:S(2)}, u32[]{:S(2)}) collective-permute-start(bf16[128,1536]{1,0:T(8,128)(2,1)} %get-tuple-element.93), channel_id=1, source_target_pairs={{31,0},{28,1},{29,2},{30,3},{3,4},{0,5},{1,6},{2,7},{7,8},{4,9},{5... | collective-permute-start | bytes 1179656 | tf_op jit(solution)/shard_map/ppermute | solution.py:59
  165.8 28.7 %copy-start.1 = (bf16[128,1536]{1,0:T(8,128)(2,1)}, bf16[128,1536]{1,0:T(8,128)(2,1)S(1)}, u32[]{:S(2)}) copy-start(bf16[128,1536]{1,0:T(8,128)(2,1)S(1)} %collective-permute-done.13.refs_5_) | copy-start | bytes 1179652
  165.8 28.7 %copy-start.2 = (bf16[128,1536]{1,0:T(8,128)(2,1)}, bf16[128,1536]{1,0:T(8,128)(2,1)S(1)}, u32[]{:S(2)}) copy-start(bf16[128,1536]{1,0:T(8,128)(2,1)S(1)} %collective-permute-done.14.refs_6_) | copy-start | bytes 1179652
  165.8 28.7 %copy-start.3 = (bf16[128,1536]{1,0:T(8,128)(2,1)}, bf16[128,1536]{1,0:T(8,128)(2,1)S(1)}, u32[]{:S(2)}) copy-start(bf16[128,1536]{1,0:T(8,128)(2,1)S(1)} %collective-permute-done.15.refs_7_) | copy-start | bytes 1179652
  170.8 23.5 %collective-permute-start.19 = (bf16[384,1536]{1,0:T(8,128)(2,1)S(1)}, bf16[384,1536]{1,0:T(8,128)(2,1)S(1)}, u32[]{:S(2)}, u32[]{:S(2)}) collective-permute-start(bf16[384,1536]{1,0:T(8,128)(2,1)S(1)} %collective-permute-done.12), channel_id=1, source_target_pairs={{0,16},{1,17},{2,18},{3,19},{4,20},{5,21},{6,22},{7,23},{8,24},{9,... | collective-permute-start | bytes 3538952 | tf_op jit(solution)/shard_map/ppermute | solution.py:59
  171.4 9.1 %collective-permute-start.16 = (bf16[128,1536]{1,0:T(8,128)(2,1)}, bf16[128,1536]{1,0:T(8,128)(2,1)S(1)}, u32[]{:S(2)}, u32[]{:S(2)}) collective-permute-start(bf16[128,1536]{1,0:T(8,128)(2,1)} %get-tuple-element.103), channel_id=1, source_target_pairs={{4,0},{5,1},{6,2},{7,3},{8,4},{9,5},{10,6},{11,7},{12,8},{13,9},{1... | collective-permute-start | bytes 1179656 | tf_op jit(solution)/shard_map/ppermute | solution.py:59
  171.4 9.1 %collective-permute-start.17 = (bf16[128,1536]{1,0:T(8,128)(2,1)}, bf16[128,1536]{1,0:T(8,128)(2,1)S(1)}, u32[]{:S(2)}, u32[]{:S(2)}) collective-permute-start(bf16[128,1536]{1,0:T(8,128)(2,1)} %get-tuple-element.104), channel_id=1, source_target_pairs={{1,0},{2,1},{3,2},{0,3},{5,4},{6,5},{7,6},{4,7},{9,8},{10,9},{11,1... | collective-permute-start | bytes 1179656 | tf_op jit(solution)/shard_map/ppermute | solution.py:59
  172.1 14.3 %collective-permute-start.18 = (bf16[128,1536]{1,0:T(8,128)(2,1)}, bf16[128,1536]{1,0:T(8,128)(2,1)S(1)}, u32[]{:S(2)}, u32[]{:S(2)}) collective-permute-start(bf16[128,1536]{1,0:T(8,128)(2,1)} %get-tuple-element.105), channel_id=1, source_target_pairs={{5,0},{6,1},{7,2},{4,3},{9,4},{10,5},{11,6},{8,7},{13,8},{14,9},{1... | collective-permute-start | bytes 1179656 | tf_op jit(solution)/shard_map/ppermute | solution.py:59
  180.5 13.8 %copy-start.4 = (bf16[128,1536]{1,0:T(8,128)(2,1)}, bf16[128,1536]{1,0:T(8,128)(2,1)S(1)}, u32[]{:S(2)}) copy-start(bf16[128,1536]{1,0:T(8,128)(2,1)S(1)} %collective-permute-done.16.refs_1_) | copy-start | bytes 1179652
  180.5 13.8 %copy-start.5 = (bf16[128,1536]{1,0:T(8,128)(2,1)}, bf16[128,1536]{1,0:T(8,128)(2,1)S(1)}, u32[]{:S(2)}) copy-start(bf16[128,1536]{1,0:T(8,128)(2,1)S(1)} %collective-permute-done.17.refs_2_) | copy-start | bytes 1179652
  194.5 20.9 %copy-start = (bf16[2,384,1536]{2,1,0:T(8,128)(2,1)}, bf16[2,384,1536]{2,1,0:T(8,128)(2,1)S(1)}, u32[]{:S(2)}) copy-start(bf16[2,384,1536]{2,1,0:T(8,128)(2,1)S(1)} %pad_maximum_fusion.refs_8_) | copy-start | bytes 7077892
  194.6 20.9 %collective-permute-start.20 = (bf16[2,384,1536]{2,1,0:T(8,128)(2,1)S(1)}, bf16[2,384,1536]{2,1,0:T(8,128)(2,1)}, u32[]{:S(2)}, u32[]{:S(2)}) collective-permute-start(bf16[2,384,1536]{2,1,0:T(8,128)(2,1)S(1)} %pad_maximum_fusion.refs_8_), channel_id=1, source_target_pairs={{0,32},{1,33},{2,34},{3,35},{4,36},{5,37},{6,38},{7,39},{8,40},{9,... | collective-permute-start | bytes 7077896 | tf_op jit(solution)/shard_map/ppermute | solution.py:59
  196.7 5.9 %collective-permute-start.21 = (bf16[384,1536]{1,0:T(8,128)(2,1)}, bf16[384,1536]{1,0:T(8,128)(2,1)S(1)}, u32[]{:S(2)}, u32[]{:S(2)}) collective-permute-start(bf16[384,1536]{1,0:T(8,128)(2,1)} %collective-permute-done.10.refs_9_), channel_id=1, source_target_pairs={{0,32},{1,33},{2,34},{3,35},{4,36},{5,37},{6,38},{7,39},{8,40},{9,... | collective-permute-start | bytes 3538952 | tf_op jit(solution)/shard_map/ppermute | solution.py:59
  (11 other events, 50.3 us)
Sparse Core Ops, SparseCore 0:
  58.4 50.2 all-gather.1

commit v6 on v3

--- a/solution.py
+++ b/solution.py
@@ -16,7 +16,7 @@
 AXES = ("frame", "row", "col")
 STEP = 2
 BIG = 1e30
-TILE = 384
+TILE = 768
 VMEM = 56 * 1024 * 1024
 
 
@@ -45,13 +45,11 @@
     return [(index(f, r, c), index(f ^ 1, r, c)) for f, r, c in every()]
 
 
-def depth_pairs():
+def turn_pairs():
     pairs = []
     for f, r, c in every():
-        zhi, core = divmod(f, 2)
         zlo, x = divmod(r, 4)
-        z = (zhi * 2 + zlo + (1 if core == 0 else -1)) % 4
-        pairs.append((index(f, r, c), index((z // 2) * 2 + core, (z % 2) * 4 + x, c)))
+        pairs.append((index(f, r, c), index(f, zlo * 4 + (x + 1 - 2 * (f % 2)) % 4, c)))
     return pairs
 
 
@@ -60,10 +58,6 @@
 
 
 MOVES = ((0, 0), (1, 0), (0, 1), (1, 1))
-
-
-def after(value, *first):
-    return lax.optimization_barrier((value, *first))[0]
 
 
 def sign_of(half, frame):
@@ -113,21 +107,27 @@
 
 
 def halo_kernel(*refs):
-    srcs, out, held, sems = refs[:-3], refs[-3], refs[-2], refs[-1]
-    relay([(src.at[pl.ds(0, 2)], held.at[n], out.at[n]) for n, src in enumerate(srcs)], sems)
+    srcs, outs, sems = refs[:6], refs[6:8], refs[8]
+    copies = []
+    for half in range(2):
+        for n in range(3):
+            src = srcs[3 * half + n].at[pl.ds(0, 2)]
+            copies.append(pltpu.make_async_copy(src, outs[half].at[n], sems.at[half, n]))
+    for copy in copies:
+        copy.start()
+    for copy in copies:
+        copy.wait()
 
 
 def halo_pack(*pieces):
-    any_spec = pl.BlockSpec(memory_space=pl.ANY)
-    count = len(pieces)
     return pl.pallas_call(
         halo_kernel,
-        out_shape=jax.ShapeDtypeStruct((count, 2, 128, HD), jnp.bfloat16),
-        in_specs=[any_spec] * count,
-        out_specs=any_spec,
-        scratch_shapes=[pltpu.VMEM((count, 2, 128, HD), jnp.bfloat16), pltpu.SemaphoreType.DMA((2, count))],
+        out_shape=[jax.ShapeDtypeStruct((3, 2, 128, HD), jnp.bfloat16)] * 2,
+        in_specs=[pl.BlockSpec(memory_space=pltpu.VMEM)] * 6,
+        out_specs=[pl.BlockSpec(memory_space=pl.ANY)] * 2,
+        scratch_shapes=[pltpu.SemaphoreType.DMA((2, 3))],
         compiler_params=pltpu.CompilerParams(vmem_limit_bytes=VMEM),
-        cost_estimate=pl.CostEstimate(flops=0, bytes_accessed=count * 3 * 2**19, transcendentals=0),
+        cost_estimate=pl.CostEstimate(flops=0, bytes_accessed=10 * 2**20, transcendentals=0),
         name="halo_pack",
     )(*pieces)
 
@@ -160,7 +160,7 @@
     alive[...] = jnp.where(live, 1.0, 0.0)
 
 
-def attend_kernel(half, meta, skv, sq, x, y, dkv, dq, h0, hxy, hd, o0, o1, o2, o3, kaug, vaug, qaug, alive):
+def attend_kernel(half, meta, skv, sq, x, y, d, h3, hd, o0, o1, o2, o3, kaug, vaug, qaug, alive):
     outs = (o0, o1, o2, o3)
 
     @pl.when(pl.program_id(0) == 0)
@@ -171,8 +171,8 @@
             qaug[n, :, HS:] = qaug[0, :, HS:]
         vaug[:, :, HS:] = jnp.ones((STEP, 1024, HS), jnp.bfloat16)
 
-    keys = (skv, x, y, dkv, h0, hxy.at[0], hxy.at[1], hd)
-    asks = (sq.at[0], x.at[2], y.at[2], dq.at[0])
+    keys = (skv, x, y, d, h3.at[0], h3.at[1], h3.at[2], hd)
+    asks = (sq.at[0], x.at[2], y.at[2], d.at[2])
     for h in range(STEP):
         lanes = pl.ds(h * HS, HS)
         for n, ref in enumerate(keys):
@@ -228,16 +228,29 @@
 
 
 def project_kernel(meta, places, *refs):
-    attended, (c0, c1, c2, c3, near, far), (tokens, out, lhs, held, sems) = refs[:8], refs[8:14], refs[14:]
-    chunks = (c0, c1, c2, c3, near.at[0], near.at[1], near.at[2], far)
+    attended, own, other, (tokens, out, lhs, held, sems) = refs[:8], refs[8:12], refs[12:16], refs[16:]
     step = pl.program_id(0)
+    core, x = lax.rem(meta[0], 2), lax.rem(meta[1], 4)
 
     def fetch(n):
-        return pltpu.make_async_copy(chunks[n], held.at[n % 2], sems.at[n % 2])
+        side, zhi = divmod(n, 2)
+        k = core if side == 0 else 1 - core
+        copies = []
+        for turn, src in enumerate(other if side else own):
+            at = lax.rem(x + turn * (2 * k - 1) + 4, 4)
+            for zlo in range(2):
+                to = pl.ds(pl.multiple_of(zlo * 384 + at * 96, 32), 96)
+                copies.append(
+                    pltpu.make_async_copy(
+                        src.at[pl.ds((2 * zhi + zlo) * 96, 96)], held.at[n % 2, to], sems.at[n % 2, 2 * turn + zlo]
+                    )
+                )
+        return copies
 
     @pl.when(step == 0)
     def _():
-        fetch(0).start()
+        for copy in fetch(0):
+            copy.start()
         for half in range(2):
             s = sign_of(half, meta[0])
             for piece, (a, b) in enumerate(MOVES):
@@ -245,13 +258,15 @@
                 j = s + b * (1 - 2 * s)
                 lhs[half * 4 + i * 2 + j] = attended[half * 4 + piece][...]
 
-    for n in range(8):
+    for n in range(4):
 
         @pl.when(step == n)
         def _():
-            fetch(n).wait()
-            if n < 7:
-                fetch(n + 1).start()
+            for copy in fetch(n):
+                copy.wait()
+            if n < 3:
+                for copy in fetch(n + 1):
+                    copy.start()
 
     total = lax.dot_general(
         lhs[...].reshape(1024, HD), held[lax.rem(step, 2)], (((1,), (1,)), ((), ())), preferred_element_type=jnp.float32
@@ -268,13 +283,13 @@
         num_scalar_prefetch=2,
         grid=(D // TILE,),
         in_specs=[pl.BlockSpec((128, HD), lambda t, m, p: (0, 0))] * 8
-        + [pl.BlockSpec(memory_space=pl.ANY)] * 6
+        + [pl.BlockSpec(memory_space=pl.ANY)] * 8
         + [pl.BlockSpec((4, 16, 16, TILE), lambda t, m, p: (0, 0, 0, p[t]))],
         out_specs=pl.BlockSpec((4, 16, 16, TILE), lambda t, m, p: (0, 0, 0, p[t])),
         scratch_shapes=[
             pltpu.VMEM((8, 128, HD), jnp.bfloat16),
             pltpu.VMEM((2, TILE, HD), jnp.bfloat16),
-            pltpu.SemaphoreType.DMA((2,)),
+            pltpu.SemaphoreType.DMA((2, 8)),
         ],
     )
     return pl.pallas_call(
@@ -287,54 +302,66 @@
     )(meta, places, *attended, *chunks, tokens)
 
 
-def plane_groups():
-    return [[index(f, zlo * 4 + x, c) for x in range(4) for c in range(C)] for f in range(F) for zlo in range(2)]
-
-
-def weight_places(f, r):
-    core, z = f % 2, (f // 2) * 2 + r // 4
-    places = []
-    for k in (core, 1 - core):
-        for n in range(4):
-            at = (z + n * (2 * k - 1) + 4) % 4
-            places.append(((at // 2) * 2 + k) * 2 + at % 2)
-    return jnp.stack(places).astype(jnp.int32)
+def strip_groups():
+    return [
+        [index(2 * zhi + core, zlo * 4 + x, c) for zhi in range(2) for zlo in range(2) for c in range(C)]
+        for core in range(2)
+        for x in range(4)
+    ]
+
+
+def together(*values):
+    return lax.optimization_barrier(values)
 
 
 def local(tokens_in, queries, key_rows, value_rows, out_weight, row_valid):
     f, r, c = (lax.axis_index(a) for a in AXES)
+    frame = f.astype(jnp.int32).reshape(1)
     meta = jnp.stack([f, r, c, jnp.sum(row_valid)]).astype(jnp.int32)
+    core = f & 1
+    places = jnp.stack([core, 2 + core, 1 - core, 3 - core]).astype(jnp.int32)
     split = lambda a: a.reshape(4, 2, 8, 2, 8, HD)
-    arrays = (meta, split(key_rows), split(value_rows), split(queries))
-    chunk = lax.all_gather(out_weight.T, AXES, axis=0, tiled=True, axis_index_groups=plane_groups())
+    arrays = (split(key_rows), split(value_rows), split(queries))
+    chunk = lax.all_gather(out_weight.T, AXES, axis=0, tiled=True, axis_index_groups=strip_groups())
 
     row, col, both = MOVES[1:]
     go = lambda value, half, move: send(value, window_pairs(half, *move))
-    skv0, skv1, x0, y0 = pack(((0, 0, "kv"), (1, 0, "kv"), (0, 1, "kvq"), (0, 2, "kvq")), *arrays)
-    up0, down0 = send(skv1, frame_pairs(1)), send(skv0, frame_pairs(-1))
+    up = lambda value: send(value, frame_pairs(1))
+    down = lambda value: send(value, frame_pairs(-1))
+    swap = lambda value: send(value, core_pairs())
+    turn = lambda value: send(value, turn_pairs())
+    back = lambda half, mixed: [mixed[0]] + [send(mixed[n], window_pairs(half, *MOVES[n], back=True)) for n in (1, 2, 3)]
+
+    x0, y0 = pack(((0, 1, "kvq"), (0, 2, "kvq")), frame, *arrays)
+    x0, y0, frame = together(x0, y0, frame)
     x0, y0 = go(x0, 0, row), go(y0, 0, col)
-    x1, y1, dkv0, dkv1, dq0, dq1, sq0, sq1 = pack(
-        ((1, 1, "kvq"), (1, 2, "kvq"), (0, 3, "kv"), (1, 3, "kv"), (0, 3, "q"), (1, 3, "q"), (0, 0, "q"), (1, 0, "q")), *arrays
+    x1, y1 = pack(((1, 1, "kvq"), (1, 2, "kvq")), frame, *arrays)
+    x1, y1, frame = together(x1, y1, frame)
+    x1, y1 = go(x1, 1, row), go(y1, 1, col)
+    skv0, skv1, d0, d1, sq0, sq1 = pack(
+        ((0, 0, "kv"), (1, 0, "kv"), (0, 3, "kvq"), (1, 3, "kvq"), (0, 0, "q"), (1, 0, "q")), frame, *arrays
     )
-    x1, y1 = go(after(x1, up0), 1, row), go(after(y1, down0), 1, col)
-    down1 = send(halo_pack(x0, y0), frame_pairs(-1))
-    dkv0, dkv1 = go(after(dkv0, x1), 0, both), go(after(dkv1, y1), 1, both)
-    up1 = send(halo_pack(x1, y1), frame_pairs(1))
-    dq0, dq1 = go(after(dq0, dkv0), 0, both), go(after(dq1, dkv1), 1, both)
-    down2, up2 = send(dkv0, frame_pairs(-1)), send(dkv1, frame_pairs(1))
-
-    ring = [after(chunk, up2)]
-    for _ in range(3):
-        ring.append(send(ring[-1], depth_pairs()))
-    near = send(jnp.stack(ring[:3]), core_pairs())
-    far = send(ring[3], core_pairs())
-
-    mixed1 = attend(1, meta, skv1, sq1, x1, y1, dkv1, dq1, down0, down1, down2)
-    mixed0 = attend(0, meta, skv0, sq0, x0, y0, dkv0, dq0, up0, up1, up2)
-    attended = []
-    for half, mixed in enumerate((mixed0, mixed1)):
-        attended += [mixed[0]] + [send(mixed[n], window_pairs(half, *MOVES[n], back=True)) for n in (1, 2, 3)]
-    return project(attended, meta, weight_places(f, r), (*ring, near, far), tokens_in)
+    d0, x0, y0, meta, places = together(d0, x0, y0, meta, places)
+    d1, x1, y1 = together(d1, x1, y1)
+    d0, d1 = go(d0, 0, both), go(d1, 1, both)
+    h0, h1 = halo_pack(skv0, x0, y0, skv1, x1, y1)
+    chunk, h0, h1 = together(chunk, h0, h1)
+    down3, up3 = down(h0), up(h1)
+    c0, d0, d1 = together(chunk, d0, d1)
+    c1 = turn(c0)
+    c1, down3, up3, hd0, hd1 = together(c1, down3, up3, d0[:2], d1[:2])
+    downd, upd, c2 = down(hd0), up(hd1), turn(c1)
+    c2, downd, upd = together(c2, downd, upd)
+
+    c3, s0, s1, s2 = turn(c2), swap(c0), swap(c1), swap(c2)
+    mixed1 = attend(1, meta, skv1, sq1, x1, y1, d1, down3, downd)
+    c3, s0, s1, s2, skv0, *mixed1 = together(c3, s0, s1, s2, skv0, *mixed1)
+    attended1, s3 = back(1, mixed1), swap(c3)
+    mixed0 = attend(0, meta, skv0, sq0, x0, y0, d0, up3, upd)
+    s3, *rest = together(s3, *attended1, *mixed0)
+    attended1, mixed0 = rest[:4], rest[4:]
+    attended0 = back(0, mixed0)
+    return project(attended0 + attended1, meta, places, (c0, c1, c2, c3, s0, s1, s2, s3), tokens_in)
 
 
 def solution(mesh):

time: 270 us -> 225 us (0.83)
  waiting for transfers between devices: 134 us -> 102 us
  starting transfers between devices: 49.3 us -> 41.1 us
  Pallas kernels: 62 us -> 58.8 us
    ppermute x25 -> x23, waiting for transfers between devices: 120 us -> 62 us  [send(): return lax.ppermute(value, AXES, pairs)]
    all_gather x1, waiting for transfers between devices: 13.8 us -> 39.6 us  [local(): lax.all_gather(out_weight.T, AXES, axis=0, tiled=True, axis_index_groups=...]
    ppermute x25 -> x23, starting transfers between devices: 49.3 us -> 41.1 us  [send(): return lax.ppermute(value, AXES, pairs)]
    unnamed x32 -> x36, local copies, waits for them, and re-layouts: 5.9 us -> 1.72 us
    pallas_call x1, Pallas kernels: 20.1 us -> 16.9 us  [project(): pl.pallas_call(project_kernel, grid_spec=grid_spec, out_shape=jax.ShapeDt...]
    pallas_call x2 -> x3, Pallas kernels: 9.92 us -> 9.51 us  [pack(): pl.pallas_call(functools.partial(pack_kernel, parts), out_shape=[jax.Shap...]
  transfers between devices with their start and end apart: 26 -> 24, of which waited for: 14 -> 14; matrix products, arithmetic and copies ran while one was open for 0% -> 2% of each run, Pallas kernels for 14% -> 19%
where the time goes in v6:
time: 225 us; the launch traced here: 222 us
  waiting for transfers between devices  102 us (45%)
  Pallas kernels  58.8 us (26%)
  starting transfers between devices  41.1 us (18%)
  between operations  13.7 us (6%)
  local copies, waits for them, and re-layouts  4.19 us (2%)
    ppermute x23, waiting for transfers between devices, send(): return lax.ppermute(value, AXES, pairs)  62 us
    ppermute x23, starting transfers between devices, send(): return lax.ppermute(value, AXES, pairs)  41.1 us
    all_gather x1, waiting for transfers between devices, local(): lax.all_gather(out_weight.T, AXES, axis=0, tiled=True, axis_index_groups=...  39.6 us
    pallas_call x2, Pallas kernels, attend(): pl.pallas_call(functools.partial(attend_kernel, half), grid=(H // STEP,),...  27.3 us
    pallas_call x1, Pallas kernels, project(): pl.pallas_call(project_kernel, grid_spec=grid_spec, out_shape=jax.ShapeDt...  16.9 us
    pallas_call x3, Pallas kernels, pack(): pl.pallas_call(functools.partial(pack_kernel, parts), out_shape=[jax.Shap...  9.51 us
    pallas_call x1, Pallas kernels, halo_pack(): pl.pallas_call(halo_kernel, out_shape=[jax.ShapeDtypeStruct((3, 2, 128, H...  5.07 us
  transfers between devices with their start and end apart: 24, of which 14 were waited for; matrix products, arithmetic and copies ran while one was open for 2% of the time, Pallas kernels for 19%

profile of v6, /device:TPU:1, one launch (start us, length us, event | category | flops | bytes accessed | tf_op | source)
XLA Modules:
  0.0 222.0 jit_solution(17937036151152573514)
XLA Ops:
  7.3 2.5 %pack.3 = (bf16[3,2,8,8,1536]{4,3,2,1,0:T(8,128)(2,1)}, bf16[3,2,8,8,1536]{4,3,2,1,0:T(8,128)(2,1)}) custom-call(s32[1]{0:T(128)} %bitcast.meta, bf16[4,2,8,2,8,1536]{5,4,3,2,1,0:T(8,128)(2,1)} %bitcast.22, bf16[4,2,8,2,8,1536]{5,4,3,2,1,0:T(8,128)(2,1)} %bitcast.25, bf16[4,2,8,2,8,1536]{5,4,3,2,1,0:T(8,128)(2,1)} %bitcast.28), custom_call_target="tpu_custom_call" | custom-call | bytes 6291456 | tf_op jit(solution)/shard_map/pack/pallas_call | solution.py:96
  9.8 2.7 %pack.4 = (bf16[3,2,8,8,1536]{4,3,2,1,0:T(8,128)(2,1)}, bf16[3,2,8,8,1536]{4,3,2,1,0:T(8,128)(2,1)}) custom-call(s32[1]{0:T(128)} %bitcast.meta, bf16[4,2,8,2,8,1536]{5,4,3,2,1,0:T(8,128)(2,1)} %bitcast.23, bf16[4,2,8,2,8,1536]{5,4,3,2,1,0:T(8,128)(2,1)} %bitcast.26, bf16[4,2,8,2,8,1536]{5,4,3,2,1,0:T(8,128)(2,1)} %bitcast.29), custom_call_target="tpu_custom_call" | custom-call | bytes 6291456 | tf_op jit(solution)/shard_map/pack/pallas_call | solution.py:96
  12.4 2.1 collective-permute-start.2
  14.5 1.3 collective-permute-start.3
  15.8 2.7 %collective-permute-start = (bf16[3,128,1536]{2,1,0:T(8,128)(2,1)}, bf16[3,128,1536]{2,1,0:T(8,128)(2,1)S(1)}, u32[]{:S(2)}, u32[]{:S(2)}) collective-permute-start(bf16[3,128,1536]{2,1,0:T(8,128)(2,1)} %bitcast.4), channel_id=1, source_target_pairs={{0,4},{1,5},{2,6},{3,7},{4,8},{5,9},{6,10},{7,11},{8,12},{9,13},{1... | collective-permute-start | bytes 3538952 | tf_op jit(solution)/shard_map/ppermute | solution.py:57
  18.5 1.5 collective-permute-start.1
  20.1 4.4 %pack.5 = (bf16[2,2,8,8,1536]{4,3,2,1,0:T(8,128)(2,1)}, bf16[2,2,8,8,1536]{4,3,2,1,0:T(8,128)(2,1)}, bf16[3,2,8,8,1536]{4,3,2,1,0:T(8,128)(2,1)}, bf16[3,2,8,8,1...) custom-call(s32[1]{0:T(128)} %bitcast.meta, ...), custom_call_target="tpu_custom_call" | custom-call | bytes 12582912 | tf_op jit(solution)/shard_map/pack/pallas_call | solution.py:96
  26.3 9.6 %collective-permute-done.2.refs_4_.x = bf16[3,128,1536]{2,1,0:T(8,128)(2,1)S(1)} collective-permute-done((bf16[3,128,1536]{2,1,0:T(8,128)(2,1)}, bf16[3,128,1536]{2,1,0:T(8,128)(2,1)S(1)}, u32[]{:S(2)}, u32[]{:S(2)}) %collective-permute-start.2) | collective-permute-done | bytes 1179680 | tf_op jit(solution)/shard_map/ppermute | solution.py:57
  35.9 1.7 collective-permute-done.3.refs_5_.y
  37.5 6.9 %collective-permute-done.refs_1_.x = bf16[3,128,1536]{2,1,0:T(8,128)(2,1)S(1)} collective-permute-done((bf16[3,128,1536]{2,1,0:T(8,128)(2,1)}, bf16[3,128,1536]{2,1,0:T(8,128)(2,1)S(1)}, u32[]{:S(2)}, u32[]{:S(2)}) %collective-permute-start) | collective-permute-done | bytes 1179680 | tf_op jit(solution)/shard_map/ppermute | solution.py:57
  44.4 3.0 %collective-permute-done.1.refs_2_.y = bf16[3,128,1536]{2,1,0:T(8,128)(2,1)S(1)} collective-permute-done((bf16[3,128,1536]{2,1,0:T(8,128)(2,1)}, bf16[3,128,1536]{2,1,0:T(8,128)(2,1)S(1)}, u32[]{:S(2)}, u32[]{:S(2)}) %collective-permute-start.1) | collective-permute-done | bytes 1179680 | tf_op jit(solution)/shard_map/ppermute | solution.py:57
  47.5 5.7 %collective-permute-start.4 = (bf16[3,128,1536]{2,1,0:T(8,128)(2,1)}, bf16[3,128,1536]{2,1,0:T(8,128)(2,1)}, u32[]{:S(2)}, u32[]{:S(2)}) collective-permute-start(bf16[3,128,1536]{2,1,0:T(8,128)(2,1)} %bitcast.36), channel_id=1, source_target_pairs={{0,5},{1,6},{2,7},{3,4},{4,9},{5,10},{6,11},{7,8},{8,13},{9,14},{1... | collective-permute-start | bytes 3538952 | tf_op jit(solution)/shard_map/ppermute | solution.py:57
  53.2 5.1 %halo_pack.1 = (bf16[3,2,128,1536]{3,2,1,0:T(8,128)(2,1)}, bf16[3,2,128,1536]{3,2,1,0:T(8,128)(2,1)}) custom-call(bf16[2,128,1536]{2,1,0:T(8,128)(2,1)} %bitcast.31, bf16[3,128,1536]{2,1,0:T(8,128)(2,1)} %copy-done, bf16[3,128,1536]{2,1,0:T(8,128)(2,1)} %copy-done.1, bf16[2,128,1536]{2,1,0:T(8,128)(2,1)} %bitcast.33, bf16[3,128,1536]{2,1,0:T(8,128)(2,1)} %copy-done.2, ...), custom_call_target="tpu_custom_call" | custom-call | bytes 10485760 | tf_op jit(solution)/shard_map/halo_pack/pallas_call | solution.py:123
  58.2 39.6 %all-gather.2.cloned.1.call-done.refs_8_ = bf16[384,1536]{1,0:T(8,128)(2,1)} async-done(((bf16[24,1536]{1,0:T(8,128)(2,1)}), bf16[384,1536]{1,0:T(8,128)(2,1)}) %all-gather.2.cloned.1.call-update) | async-done | bytes 1179664 | tf_op jit(solution)/shard_map/all_gather | solution.py:325
  97.9 3.4 %collective-permute-start.7 = (bf16[3,2,128,1536]{3,2,1,0:T(8,128)(2,1)}, bf16[3,2,128,1536]{3,2,1,0:T(8,128)(2,1)S(1)}, u32[]{:S(2)}, u32[]{:S(2)}) collective-permute-start(bf16[3,2,128,1536]{3,2,1,0:T(8,128)(2,1)} %get-tuple-element.97), channel_id=1, source_target_pairs={{32,0},{33,1},{34,2},{35,3},{36,4},{37,5},{38,6},{39,7},{40,8},{41... | collective-permute-start | bytes 7077896 | tf_op jit(solution)/shard_map/ppermute | solution.py:57
  101.3 3.8 %collective-permute-start.8 = (bf16[3,2,128,1536]{3,2,1,0:T(8,128)(2,1)}, bf16[3,2,128,1536]{3,2,1,0:T(8,128)(2,1)S(1)}, u32[]{:S(2)}, u32[]{:S(2)}) collective-permute-start(bf16[3,2,128,1536]{3,2,1,0:T(8,128)(2,1)} %get-tuple-element.98), channel_id=1, source_target_pairs={{0,32},{1,33},{2,34},{3,35},{4,36},{5,37},{6,38},{7,39},{8,40},{9,... | collective-permute-start | bytes 7077896 | tf_op jit(solution)/shard_map/ppermute | solution.py:57
  105.1 2.5 %collective-permute-start.6 = (bf16[384,1536]{1,0:T(8,128)(2,1)}, bf16[384,1536]{1,0:T(8,128)(2,1)S(1)}, u32[]{:S(2)}, u32[]{:S(2)}) collective-permute-start(bf16[384,1536]{1,0:T(8,128)(2,1)} %all-gather.2.cloned.1.call-done.refs_8_), channel_id=1, source_target_pairs={{0,4},{1,5},{2,6},{3,7},{4,8},{5,9},{6,10},{7,11},{8,12},{9,13},{1... | collective-permute-start | bytes 3538952 | tf_op jit(solution)/shard_map/ppermute | solution.py:57
  108.8 1.3 slice.7
  110.1 11.0 %collective-permute-done.6.refs_9_ = bf16[384,1536]{1,0:T(8,128)(2,1)S(1)} collective-permute-done((bf16[384,1536]{1,0:T(8,128)(2,1)}, bf16[384,1536]{1,0:T(8,128)(2,1)S(1)}, u32[]{:S(2)}, u32[]{:S(2)}) %collective-permute-start.6) | collective-permute-done | bytes 1179680 | tf_op jit(solution)/shard_map/ppermute | solution.py:57
  121.1 8.8 %collective-permute-done.7.h3 = bf16[3,2,128,1536]{3,2,1,0:T(8,128)(2,1)S(1)} collective-permute-done((bf16[3,2,128,1536]{3,2,1,0:T(8,128)(2,1)}, bf16[3,2,128,1536]{3,2,1,0:T(8,128)(2,1)S(1)}, u32[]{:S(2)}, u32[]{:S(2)}) %collective-permute-start.7) | collective-permute-done | bytes 2359328 | tf_op jit(solution)/shard_map/ppermute | solution.py:57
  129.9 1.3 collective-permute-done.8.h3
  131.2 2.4 %collective-permute-start.9 = (bf16[384,1536]{1,0:T(8,128)(2,1)S(1)}, bf16[384,1536]{1,0:T(8,128)(2,1)}, u32[]{:S(2)}, u32[]{:S(2)}) collective-permute-start(bf16[384,1536]{1,0:T(8,128)(2,1)S(1)} %collective-permute-done.6.refs_9_), channel_id=1, source_target_pairs={{0,4},{1,5},{2,6},{3,7},{4,8},{5,9},{6,10},{7,11},{8,12},{9,13},{1... | collective-permute-start | bytes 3538952 | tf_op jit(solution)/shard_map/ppermute | solution.py:57
  133.6 1.9 collective-permute-start.10
  135.5 5.1 %collective-permute-start.11 = (bf16[2,128,1536]{2,1,0:T(8,128)(2,1)S(1)}, bf16[2,128,1536]{2,1,0:T(8,128)(2,1)S(1)}, u32[]{:S(2)}, u32[]{:S(2)}) collective-permute-start(bf16[2,128,1536]{2,1,0:T(8,128)(2,1)S(1)} %slice.7), channel_id=1, source_target_pairs={{0,32},{1,33},{2,34},{3,35},{4,36},{5,37},{6,38},{7,39},{8,40},{9,... | collective-permute-start | bytes 2359304 | tf_op jit(solution)/shard_map/ppermute | solution.py:57
  141.3 7.1 %collective-permute-done.10.hd = bf16[2,128,1536]{2,1,0:T(8,128)(2,1)S(1)} collective-permute-done((bf16[2,128,1536]{2,1,0:T(8,128)(2,1)S(1)}, bf16[2,128,1536]{2,1,0:T(8,128)(2,1)S(1)}, u32[]{:S(2)}, u32[]{:S(2)}) %collective-permute-start.10) | collective-permute-done | bytes 786464 | tf_op jit(solution)/shard_map/ppermute | solution.py:57
  151.7 13.6 %attend.2 = (bf16[128,1536]{1,0:T(8,128)(2,1)}, bf16[128,1536]{1,0:T(8,128)(2,1)}, bf16[128,1536]{1,0:T(8,128)(2,1)}, bf16[128,1536]{1,0:T(8,128)(2,1)}) custom-call(s32[4]{0:T(128)} %get-tuple-element.80.meta, bf16[2,128,1536]{2,1,0:T(8,128)(2,1)} %bitcast.34, bf16[1,128,1536]{2,1,0:T(8,128)(2,1)} %bitcast.41, bf16[3,128,1536]{2,1,0:T(8,128)(2,1)} %copy-done.2, ...), custom_call_target="tpu_custom_call" | custom-call | flops 6442450944 | bytes 10485760 | tf_op jit(solution)/shard_map/attend/pallas_call | solution.py:212
  166.0 2.7 %collective-permute-start.17 = (bf16[128,1536]{1,0:T(8,128)(2,1)}, bf16[128,1536]{1,0:T(8,128)(2,1)S(1)}, u32[]{:S(2)}, u32[]{:S(2)}) collective-permute-start(bf16[128,1536]{1,0:T(8,128)(2,1)} %get-tuple-element.114), channel_id=1, source_target_pairs={{28,0},{29,1},{30,2},{31,3},{0,4},{1,5},{2,6},{3,7},{4,8},{5,9},{6... | collective-permute-start | bytes 1179656 | tf_op jit(solution)/shard_map/ppermute | solution.py:57
  170.0 13.6 %attend.3 = (bf16[128,1536]{1,0:T(8,128)(2,1)}, bf16[128,1536]{1,0:T(8,128)(2,1)}, bf16[128,1536]{1,0:T(8,128)(2,1)}, bf16[128,1536]{1,0:T(8,128)(2,1)}) custom-call(s32[4]{0:T(128)} %get-tuple-element.80.meta, bf16[2,128,1536]{2,1,0:T(8,128)(2,1)} %bitcast.32, bf16[1,128,1536]{2,1,0:T(8,128)(2,1)} %bitcast.40, bf16[3,128,1536]{2,1,0:T(8,128)(2,1)} %copy-done, ...), custom_call_target="tpu_custom_call" | custom-call | flops 6442450944 | bytes 10485760 | tf_op jit(solution)/shard_map/attend/pallas_call | solution.py:212
  183.7 1.5 collective-permute-start.20
  186.4 6.3 %collective-permute-done.20.refs_1_ = bf16[128,1536]{1,0:T(8,128)(2,1)S(1)} collective-permute-done((bf16[128,1536]{1,0:T(8,128)(2,1)}, bf16[128,1536]{1,0:T(8,128)(2,1)S(1)}, u32[]{:S(2)}, u32[]{:S(2)}) %collective-permute-start.20) | collective-permute-done | bytes 393248 | tf_op jit(solution)/shard_map/ppermute | solution.py:57
  193.2 4.2 %collective-permute-done.22.refs_3_ = bf16[128,1536]{1,0:T(8,128)(2,1)S(1)} collective-permute-done((bf16[128,1536]{1,0:T(8,128)(2,1)}, bf16[128,1536]{1,0:T(8,128)(2,1)S(1)}, u32[]{:S(2)}, u32[]{:S(2)}) %collective-permute-start.22) | collective-permute-done | bytes 393248 | tf_op jit(solution)/shard_map/ppermute | solution.py:57
  198.2 16.9 %project.1 = bf16[4,16,16,3072]{3,2,1,0:T(8,128)(2,1)} custom-call(s32[4]{0:T(128)} %get-tuple-element.80.meta, s32[4]{0:T(128)} %get-tuple-element.81.places, bf16[128,1536]{1,0:T(8,128)(2,1)} %get-tuple-element.125.refs_0_, bf16[128,1536]{1,0:T(8,128)(2,1)} %copy-done.14, bf16[128,1536]{1,0:T(8,128)(2,1)} %copy-done.15, bf16[128,1536]{1,0:T(8,128)(2,1)} %copy-done.16, ...), custom_call_target="tpu_custom_call" | custom-call | flops 9663676416 | bytes 26214400 | tf_op jit(solution)/shard_map/project/pallas_call | solution.py:295
  (64 shorter events, 12.0 us)
Async XLA Ops:
  6.5 91.3 %all-gather.2.cloned.1.call-start = ((), (), s32[]{:S(2)}) async-start(), calls=%async_computation | async-start | bytes 1253376 | tf_op jit(solution)/shard_map/all_gather | solution.py:325
  12.4 23.4 %collective-permute-start.2 = (bf16[3,128,1536]{2,1,0:T(8,128)(2,1)}, bf16[3,128,1536]{2,1,0:T(8,128)(2,1)S(1)}, u32[]{:S(2)}, u32[]{:S(2)}) collective-permute-start(bf16[3,128,1536]{2,1,0:T(8,128)(2,1)} %bitcast.39), channel_id=1, source_target_pairs={{0,28},{1,29},{2,30},{3,31},{4,0},{5,1},{6,2},{7,3},{8,4},{9,5},{1... | collective-permute-start | bytes 3538952 | tf_op jit(solution)/shard_map/ppermute | solution.py:57
  14.5 23.0 %collective-permute-start.3 = (bf16[3,128,1536]{2,1,0:T(8,128)(2,1)}, bf16[3,128,1536]{2,1,0:T(8,128)(2,1)}, u32[]{:S(2)}, u32[]{:S(2)}) collective-permute-start(bf16[3,128,1536]{2,1,0:T(8,128)(2,1)} %bitcast.38), channel_id=1, source_target_pairs={{0,3},{1,0},{2,1},{3,2},{4,7},{5,4},{6,5},{7,6},{8,11},{9,8},{10,9... | collective-permute-start | bytes 3538952 | tf_op jit(solution)/shard_map/ppermute | solution.py:57
  15.8 28.6 %collective-permute-start = (bf16[3,128,1536]{2,1,0:T(8,128)(2,1)}, bf16[3,128,1536]{2,1,0:T(8,128)(2,1)S(1)}, u32[]{:S(2)}, u32[]{:S(2)}) collective-permute-start(bf16[3,128,1536]{2,1,0:T(8,128)(2,1)} %bitcast.4), channel_id=1, source_target_pairs={{0,4},{1,5},{2,6},{3,7},{4,8},{5,9},{6,10},{7,11},{8,12},{9,13},{1... | collective-permute-start | bytes 3538952 | tf_op jit(solution)/shard_map/ppermute | solution.py:57
  18.5 28.9 %collective-permute-start.1 = (bf16[3,128,1536]{2,1,0:T(8,128)(2,1)}, bf16[3,128,1536]{2,1,0:T(8,128)(2,1)S(1)}, u32[]{:S(2)}, u32[]{:S(2)}) collective-permute-start(bf16[3,128,1536]{2,1,0:T(8,128)(2,1)} %bitcast.5), channel_id=1, source_target_pairs={{0,1},{1,2},{2,3},{3,0},{4,5},{5,6},{6,7},{7,4},{8,9},{9,10},{10,1... | collective-permute-start | bytes 3538952 | tf_op jit(solution)/shard_map/ppermute | solution.py:57
  35.9 17.3 %copy-start.2 = (bf16[3,128,1536]{2,1,0:T(8,128)(2,1)}, bf16[3,128,1536]{2,1,0:T(8,128)(2,1)S(1)}, u32[]{:S(2)}) copy-start(bf16[3,128,1536]{2,1,0:T(8,128)(2,1)S(1)} %collective-permute-done.2.refs_4_.x) | copy-start | bytes 3538948
  47.5 57.6 %collective-permute-start.5 = (bf16[3,128,1536]{2,1,0:T(8,128)(2,1)}, bf16[3,128,1536]{2,1,0:T(8,128)(2,1)}, u32[]{:S(2)}, u32[]{:S(2)}) collective-permute-start(bf16[3,128,1536]{2,1,0:T(8,128)(2,1)} %bitcast.37), channel_id=1, source_target_pairs={{0,31},{1,28},{2,29},{3,30},{4,3},{5,0},{6,1},{7,2},{8,7},{9,4},{1... | collective-permute-start | bytes 3538952 | tf_op jit(solution)/shard_map/ppermute | solution.py:57
  47.5 57.7 %collective-permute-start.4 = (bf16[3,128,1536]{2,1,0:T(8,128)(2,1)}, bf16[3,128,1536]{2,1,0:T(8,128)(2,1)}, u32[]{:S(2)}, u32[]{:S(2)}) collective-permute-start(bf16[3,128,1536]{2,1,0:T(8,128)(2,1)} %bitcast.36), channel_id=1, source_target_pairs={{0,5},{1,6},{2,7},{3,4},{4,9},{5,10},{6,11},{7,8},{8,13},{9,14},{1... | collective-permute-start | bytes 3538952 | tf_op jit(solution)/shard_map/ppermute | solution.py:57
  97.9 32.0 %collective-permute-start.7 = (bf16[3,2,128,1536]{3,2,1,0:T(8,128)(2,1)}, bf16[3,2,128,1536]{3,2,1,0:T(8,128)(2,1)S(1)}, u32[]{:S(2)}, u32[]{:S(2)}) collective-permute-start(bf16[3,2,128,1536]{3,2,1,0:T(8,128)(2,1)} %get-tuple-element.97), channel_id=1, source_target_pairs={{32,0},{33,1},{34,2},{35,3},{36,4},{37,5},{38,6},{39,7},{40,8},{41... | collective-permute-start | bytes 7077896 | tf_op jit(solution)/shard_map/ppermute | solution.py:57
  101.3 29.9 %collective-permute-start.8 = (bf16[3,2,128,1536]{3,2,1,0:T(8,128)(2,1)}, bf16[3,2,128,1536]{3,2,1,0:T(8,128)(2,1)S(1)}, u32[]{:S(2)}, u32[]{:S(2)}) collective-permute-start(bf16[3,2,128,1536]{3,2,1,0:T(8,128)(2,1)} %get-tuple-element.98), channel_id=1, source_target_pairs={{0,32},{1,33},{2,34},{3,35},{4,36},{5,37},{6,38},{7,39},{8,40},{9,... | collective-permute-start | bytes 7077896 | tf_op jit(solution)/shard_map/ppermute | solution.py:57
  105.1 15.9 %collective-permute-start.6 = (bf16[384,1536]{1,0:T(8,128)(2,1)}, bf16[384,1536]{1,0:T(8,128)(2,1)S(1)}, u32[]{:S(2)}, u32[]{:S(2)}) collective-permute-start(bf16[384,1536]{1,0:T(8,128)(2,1)} %all-gather.2.cloned.1.call-done.refs_8_), channel_id=1, source_target_pairs={{0,4},{1,5},{2,6},{3,7},{4,8},{5,9},{6,10},{7,11},{8,12},{9,13},{1... | collective-permute-start | bytes 3538952 | tf_op jit(solution)/shard_map/ppermute | solution.py:57
  108.8 31.9 %copy-start.5 = (bf16[384,1536]{1,0:T(8,128)(2,1)S(1)}, bf16[384,1536]{1,0:T(8,128)(2,1)}, u32[]{:S(2)}) copy-start(bf16[384,1536]{1,0:T(8,128)(2,1)} %all-gather.2.cloned.1.call-done.refs_8_) | copy-start | bytes 3538948
  121.1 44.3 %copy-start.6 = (bf16[384,1536]{1,0:T(8,128)(2,1)}, bf16[384,1536]{1,0:T(8,128)(2,1)S(1)}, u32[]{:S(2)}) copy-start(bf16[384,1536]{1,0:T(8,128)(2,1)S(1)} %collective-permute-done.6.refs_9_) | copy-start | bytes 3538948
  129.9 21.8 %copy-start.4 = (bf16[3,2,128,1536]{3,2,1,0:T(8,128)(2,1)}, bf16[3,2,128,1536]{3,2,1,0:T(8,128)(2,1)S(1)}, u32[]{:S(2)}) copy-start(bf16[3,2,128,1536]{3,2,1,0:T(8,128)(2,1)S(1)} %collective-permute-done.7.h3) | copy-start | bytes 7077892
  131.2 34.2 %copy-start.3 = (bf16[3,2,128,1536]{3,2,1,0:T(8,128)(2,1)}, bf16[3,2,128,1536]{3,2,1,0:T(8,128)(2,1)S(1)}, u32[]{:S(2)}) copy-start(bf16[3,2,128,1536]{3,2,1,0:T(8,128)(2,1)S(1)} %collective-permute-done.8.h3) | copy-start | bytes 7077892
  131.2 18.4 %collective-permute-start.9 = (bf16[384,1536]{1,0:T(8,128)(2,1)S(1)}, bf16[384,1536]{1,0:T(8,128)(2,1)}, u32[]{:S(2)}, u32[]{:S(2)}) collective-permute-start(bf16[384,1536]{1,0:T(8,128)(2,1)S(1)} %collective-permute-done.6.refs_9_), channel_id=1, source_target_pairs={{0,4},{1,5},{2,6},{3,7},{4,8},{5,9},{6,10},{7,11},{8,12},{9,13},{1... | collective-permute-start | bytes 3538952 | tf_op jit(solution)/shard_map/ppermute | solution.py:57
  133.6 14.8 %collective-permute-start.10 = (bf16[2,128,1536]{2,1,0:T(8,128)(2,1)S(1)}, bf16[2,128,1536]{2,1,0:T(8,128)(2,1)S(1)}, u32[]{:S(2)}, u32[]{:S(2)}) collective-permute-start(bf16[2,128,1536]{2,1,0:T(8,128)(2,1)S(1)} %slice.6), channel_id=1, source_target_pairs={{32,0},{33,1},{34,2},{35,3},{36,4},{37,5},{38,6},{39,7},{40,8},{41... | collective-permute-start | bytes 2359304 | tf_op jit(solution)/shard_map/ppermute | solution.py:57
  135.5 14.1 %collective-permute-start.11 = (bf16[2,128,1536]{2,1,0:T(8,128)(2,1)S(1)}, bf16[2,128,1536]{2,1,0:T(8,128)(2,1)S(1)}, u32[]{:S(2)}, u32[]{:S(2)}) collective-permute-start(bf16[2,128,1536]{2,1,0:T(8,128)(2,1)S(1)} %slice.7), channel_id=1, source_target_pairs={{0,32},{1,33},{2,34},{3,35},{4,36},{5,37},{6,38},{7,39},{8,40},{9,... | collective-permute-start | bytes 2359304 | tf_op jit(solution)/shard_map/ppermute | solution.py:57
  140.7 24.7 %collective-permute-start.13 = (bf16[384,1536]{1,0:T(8,128)(2,1)S(1)}, bf16[384,1536]{1,0:T(8,128)(2,1)}, u32[]{:S(2)}, u32[]{:S(2)}) collective-permute-start(bf16[384,1536]{1,0:T(8,128)(2,1)S(1)} %copy-done.5), channel_id=1, source_target_pairs={{0,32},{1,33},{2,34},{3,35},{4,36},{5,37},{6,38},{7,39},{8,40},{9,... | collective-permute-start | bytes 3538952 | tf_op jit(solution)/shard_map/ppermute | solution.py:57
  140.8 24.6 %collective-permute-start.14 = (bf16[384,1536]{1,0:T(8,128)(2,1)S(1)}, bf16[384,1536]{1,0:T(8,128)(2,1)}, u32[]{:S(2)}, u32[]{:S(2)}) collective-permute-start(bf16[384,1536]{1,0:T(8,128)(2,1)S(1)} %collective-permute-done.6.refs_9_), channel_id=1, source_target_pairs={{0,32},{1,33},{2,34},{3,35},{4,36},{5,37},{6,38},{7,39},{8,40},{9,... | collective-permute-start | bytes 3538952 | tf_op jit(solution)/shard_map/ppermute | solution.py:57
  150.5 15.3 %collective-permute-start.12 = (bf16[384,1536]{1,0:T(8,128)(2,1)}, bf16[384,1536]{1,0:T(8,128)(2,1)S(1)}, u32[]{:S(2)}, u32[]{:S(2)}) collective-permute-start(bf16[384,1536]{1,0:T(8,128)(2,1)} %collective-permute-done.9.refs_10_), channel_id=1, source_target_pairs={{0,4},{1,5},{2,6},{3,7},{4,8},{5,9},{6,10},{7,11},{8,12},{9,13},{1... | collective-permute-start | bytes 3538952 | tf_op jit(solution)/shard_map/ppermute | solution.py:57
  151.7 14.1 %collective-permute-start.15 = (bf16[384,1536]{1,0:T(8,128)(2,1)}, bf16[384,1536]{1,0:T(8,128)(2,1)}, u32[]{:S(2)}, u32[]{:S(2)}) collective-permute-start(bf16[384,1536]{1,0:T(8,128)(2,1)} %collective-permute-done.9.refs_10_), channel_id=1, source_target_pairs={{0,32},{1,33},{2,34},{3,35},{4,36},{5,37},{6,38},{7,39},{8,40},{9,... | collective-permute-start | bytes 3538952 | tf_op jit(solution)/shard_map/ppermute | solution.py:57
  165.8 17.8 %copy-start.7 = (bf16[384,1536]{1,0:T(8,128)(2,1)}, bf16[384,1536]{1,0:T(8,128)(2,1)S(1)}, u32[]{:S(2)}) copy-start(bf16[384,1536]{1,0:T(8,128)(2,1)S(1)} %collective-permute-done.12.refs_11_) | copy-start | bytes 3538948
  165.8 17.9 %collective-permute-start.16 = (bf16[384,1536]{1,0:T(8,128)(2,1)S(1)}, bf16[384,1536]{1,0:T(8,128)(2,1)S(1)}, u32[]{:S(2)}, u32[]{:S(2)}) collective-permute-start(bf16[384,1536]{1,0:T(8,128)(2,1)S(1)} %collective-permute-done.12.refs_11_), channel_id=1, source_target_pairs={{0,32},{1,33},{2,34},{3,35},{4,36},{5,37},{6,38},{7,39},{8,40},{9,... | collective-permute-start | bytes 3538952 | tf_op jit(solution)/shard_map/ppermute | solution.py:57
  166.0 17.6 %collective-permute-start.17 = (bf16[128,1536]{1,0:T(8,128)(2,1)}, bf16[128,1536]{1,0:T(8,128)(2,1)S(1)}, u32[]{:S(2)}, u32[]{:S(2)}) collective-permute-start(bf16[128,1536]{1,0:T(8,128)(2,1)} %get-tuple-element.114), channel_id=1, source_target_pairs={{28,0},{29,1},{30,2},{31,3},{0,4},{1,5},{2,6},{3,7},{4,8},{5,9},{6... | collective-permute-start | bytes 1179656 | tf_op jit(solution)/shard_map/ppermute | solution.py:57
  168.7 14.9 %collective-permute-start.18 = (bf16[128,1536]{1,0:T(8,128)(2,1)}, bf16[128,1536]{1,0:T(8,128)(2,1)S(1)}, u32[]{:S(2)}, u32[]{:S(2)}) collective-permute-start(bf16[128,1536]{1,0:T(8,128)(2,1)} %get-tuple-element.115), channel_id=1, source_target_pairs={{3,0},{0,1},{1,2},{2,3},{7,4},{4,5},{5,6},{6,7},{11,8},{8,9},{9,10... | collective-permute-start | bytes 1179656 | tf_op jit(solution)/shard_map/ppermute | solution.py:57
  169.8 13.9 %collective-permute-start.19 = (bf16[128,1536]{1,0:T(8,128)(2,1)}, bf16[128,1536]{1,0:T(8,128)(2,1)S(1)}, u32[]{:S(2)}, u32[]{:S(2)}) collective-permute-start(bf16[128,1536]{1,0:T(8,128)(2,1)} %get-tuple-element.116), channel_id=1, source_target_pairs={{31,0},{28,1},{29,2},{30,3},{3,4},{0,5},{1,6},{2,7},{7,8},{4,9},{5... | collective-permute-start | bytes 1179656 | tf_op jit(solution)/shard_map/ppermute | solution.py:57
  183.6 13.8 %copy-start.11 = (bf16[128,1536]{1,0:T(8,128)(2,1)}, bf16[128,1536]{1,0:T(8,128)(2,1)S(1)}, u32[]{:S(2)}) copy-start(bf16[128,1536]{1,0:T(8,128)(2,1)S(1)} %collective-permute-done.17.refs_5_) | copy-start | bytes 1179652
  183.6 13.7 %copy-start.12 = (bf16[128,1536]{1,0:T(8,128)(2,1)}, bf16[128,1536]{1,0:T(8,128)(2,1)S(1)}, u32[]{:S(2)}) copy-start(bf16[128,1536]{1,0:T(8,128)(2,1)S(1)} %collective-permute-done.18.refs_6_) | copy-start | bytes 1179652
  183.7 9.0 %collective-permute-start.20 = (bf16[128,1536]{1,0:T(8,128)(2,1)}, bf16[128,1536]{1,0:T(8,128)(2,1)S(1)}, u32[]{:S(2)}, u32[]{:S(2)}) collective-permute-start(bf16[128,1536]{1,0:T(8,128)(2,1)} %get-tuple-element.126), channel_id=1, source_target_pairs={{4,0},{5,1},{6,2},{7,3},{8,4},{9,5},{10,6},{11,7},{12,8},{13,9},{1... | collective-permute-start | bytes 1179656 | tf_op jit(solution)/shard_map/ppermute | solution.py:57
  185.2 8.0 %collective-permute-start.21 = (bf16[128,1536]{1,0:T(8,128)(2,1)}, bf16[128,1536]{1,0:T(8,128)(2,1)S(1)}, u32[]{:S(2)}, u32[]{:S(2)}) collective-permute-start(bf16[128,1536]{1,0:T(8,128)(2,1)} %get-tuple-element.127), channel_id=1, source_target_pairs={{1,0},{2,1},{3,2},{0,3},{5,4},{6,5},{7,6},{4,7},{9,8},{10,9},{11,1... | collective-permute-start | bytes 1179656 | tf_op jit(solution)/shard_map/ppermute | solution.py:57
  186.2 11.2 %collective-permute-start.22 = (bf16[128,1536]{1,0:T(8,128)(2,1)}, bf16[128,1536]{1,0:T(8,128)(2,1)S(1)}, u32[]{:S(2)}, u32[]{:S(2)}) collective-permute-start(bf16[128,1536]{1,0:T(8,128)(2,1)} %get-tuple-element.128), channel_id=1, source_target_pairs={{5,0},{6,1},{7,2},{4,3},{9,4},{10,5},{11,6},{8,7},{13,8},{14,9},{1... | collective-permute-start | bytes 1179656 | tf_op jit(solution)/shard_map/ppermute | solution.py:57
  (10 other events, 60.1 us)
Sparse Core Ops, SparseCore 0:
  9.5 88.3 all-gather.1

commit v7 on v6

--- a/solution.py
+++ b/solution.py
@@ -45,11 +45,13 @@
     return [(index(f, r, c), index(f ^ 1, r, c)) for f, r, c in every()]
 
 
-def turn_pairs():
+def shift_pairs(dx=0, dy=0, dz=0, opposed=False):
     pairs = []
     for f, r, c in every():
-        zlo, x = divmod(r, 4)
-        pairs.append((index(f, r, c), index(f, zlo * 4 + (x + 1 - 2 * (f % 2)) % 4, c)))
+        (zhi, core), (zlo, x) = divmod(f, 2), divmod(r, 4)
+        way = -1 if opposed and core else 1
+        z = (2 * zhi + zlo + way * dz) % 4
+        pairs.append((index(f, r, c), index((z // 2) * 2 + core, (z % 2) * 4 + (x + way * dx) % 4, c + way * dy)))
     return pairs
 
 
@@ -302,12 +304,9 @@
     )(meta, places, *attended, *chunks, tokens)
 
 
-def strip_groups():
-    return [
-        [index(2 * zhi + core, zlo * 4 + x, c) for zhi in range(2) for zlo in range(2) for c in range(C)]
-        for core in range(2)
-        for x in range(4)
-    ]
+def ring_order(own, first, second, third, place):
+    row = jnp.stack([third, second, first, own, third, second, first])
+    return lax.dynamic_slice_in_dim(row, 3 - place, 4, axis=0)
 
 
 def together(*values):
@@ -322,45 +321,49 @@
     places = jnp.stack([core, 2 + core, 1 - core, 3 - core]).astype(jnp.int32)
     split = lambda a: a.reshape(4, 2, 8, 2, 8, HD)
     arrays = (split(key_rows), split(value_rows), split(queries))
-    chunk = lax.all_gather(out_weight.T, AXES, axis=0, tiled=True, axis_index_groups=strip_groups())
+    shard = out_weight.T
 
     row, col, both = MOVES[1:]
     go = lambda value, half, move: send(value, window_pairs(half, *move))
     up = lambda value: send(value, frame_pairs(1))
     down = lambda value: send(value, frame_pairs(-1))
     swap = lambda value: send(value, core_pairs())
-    turn = lambda value: send(value, turn_pairs())
+    turn = lambda value: send(value, shift_pairs(dx=1, opposed=True))
     back = lambda half, mixed: [mixed[0]] + [send(mixed[n], window_pairs(half, *MOVES[n], back=True)) for n in (1, 2, 3)]
 
     x0, y0 = pack(((0, 1, "kvq"), (0, 2, "kvq")), frame, *arrays)
-    x0, y0, frame = together(x0, y0, frame)
+    x0, y0, frame, shard = together(x0, y0, frame, shard)
     x0, y0 = go(x0, 0, row), go(y0, 0, col)
+    shards = [send(shard, shift_pairs(dz=n)) for n in (1, 2, 3)]
     x1, y1 = pack(((1, 1, "kvq"), (1, 2, "kvq")), frame, *arrays)
-    x1, y1, frame = together(x1, y1, frame)
+    x1, y1, frame, *shards = together(x1, y1, frame, *shards)
     x1, y1 = go(x1, 1, row), go(y1, 1, col)
     skv0, skv1, d0, d1, sq0, sq1 = pack(
         ((0, 0, "kv"), (1, 0, "kv"), (0, 3, "kvq"), (1, 3, "kvq"), (0, 0, "q"), (1, 0, "q")), frame, *arrays
     )
-    d0, x0, y0, meta, places = together(d0, x0, y0, meta, places)
-    d1, x1, y1 = together(d1, x1, y1)
+    strip = ring_order(shard, *shards, (f >> 1) * 2 + (r >> 2))
+    d0, x0, y0, meta, places, strip = together(d0, x0, y0, meta, places, strip)
+    h0, h1 = halo_pack(skv0, x0, y0, skv1, x1, y1)
+    d1, h0, h1 = together(d1, h0, h1)
     d0, d1 = go(d0, 0, both), go(d1, 1, both)
-    h0, h1 = halo_pack(skv0, x0, y0, skv1, x1, y1)
-    chunk, h0, h1 = together(chunk, h0, h1)
     down3, up3 = down(h0), up(h1)
-    c0, d0, d1 = together(chunk, d0, d1)
-    c1 = turn(c0)
-    c1, down3, up3, hd0, hd1 = together(c1, down3, up3, d0[:2], d1[:2])
-    downd, upd, c2 = down(hd0), up(hd1), turn(c1)
-    c2, downd, upd = together(c2, downd, upd)
-
-    c3, s0, s1, s2 = turn(c2), swap(c0), swap(c1), swap(c2)
+    strips = [send(strip, shift_pairs(dy=n)) for n in (1, 2, 3)]
+    c0 = ring_order(strip, *strips, c).swapaxes(0, 1).reshape(384, HD)
+    c0, d0, d1, down3, up3 = together(c0, d0, d1, down3, up3)
+    downd, upd, c1 = down(d0[:2]), up(d1[:2]), turn(c0)
+    c1, downd, upd = together(c1, downd, upd)
+
+    c2, s0, s1 = turn(c1), swap(c0), swap(c1)
     mixed1 = attend(1, meta, skv1, sq1, x1, y1, d1, down3, downd)
-    c3, s0, s1, s2, skv0, *mixed1 = together(c3, s0, s1, s2, skv0, *mixed1)
-    attended1, s3 = back(1, mixed1), swap(c3)
+    c2, s0, s1, skv0, *mixed1 = together(c2, s0, s1, skv0, *mixed1)
+    attended1, c3 = back(1, mixed1), turn(c2)
+    s2 = swap(c2)
     mixed0 = attend(0, meta, skv0, sq0, x0, y0, d0, up3, upd)
-    s3, *rest = together(s3, *attended1, *mixed0)
+    s2, *rest = together(s2, *attended1, *mixed0)
     attended1, mixed0 = rest[:4], rest[4:]
     attended0 = back(0, mixed0)
+    c3, *attended0 = together(c3, *attended0)
+    s3 = swap(c3)
     return project(attended0 + attended1, meta, places, (c0, c1, c2, c3, s0, s1, s2, s3), tokens_in)
 
 

time: 225 us -> 209 us (0.929)
  waiting for transfers between devices: 102 us -> 88.5 us
  between operations: 13.7 us -> 0.63 us
  starting transfers between devices: 41.1 us -> 54.1 us
  local copies, waits for them, and re-layouts: 4.19 us -> 1.61 us
    all_gather x1 -> x0, waiting for transfers between devices: 39.6 us -> none  [local(): lax.all_gather(out_weight.T, AXES, axis=0, tiled=True, axis_index_groups=...]
    ppermute x23 -> x29, waiting for transfers between devices: 62 us -> 88.5 us  [send(): return lax.ppermute(value, AXES, pairs)]
    ppermute x23 -> x29, starting transfers between devices: 41.1 us -> 54.1 us  [send(): return lax.ppermute(value, AXES, pairs)]
    slice x2, local copies, waits for them, and re-layouts: 2.46 us -> 0.1 us  [local(): downd, upd, c1 = (down(d0[:2]), up(d1[:2]), turn(c0))]
  transfers between devices with their start and end apart: 24 -> 29, of which waited for: 14 -> 14; matrix products, arithmetic and copies ran while one was open for 2% -> 1% of each run, Pallas kernels for 19% -> 19%
where the time goes in v7:
time: 209 us; the launch traced here: 205 us
  waiting for transfers between devices  88.5 us (42%)
  Pallas kernels  58.6 us (28%)
  starting transfers between devices  54.1 us (26%)
    ppermute x29, waiting for transfers between devices, send(): return lax.ppermute(value, AXES, pairs)  88.5 us
    ppermute x29, starting transfers between devices, send(): return lax.ppermute(value, AXES, pairs)  54.1 us
    pallas_call x2, Pallas kernels, attend(): pl.pallas_call(functools.partial(attend_kernel, half), grid=(H // STEP,),...  27.2 us
    pallas_call x1, Pallas kernels, project(): pl.pallas_call(project_kernel, grid_spec=grid_spec, out_shape=jax.ShapeDt...  16.9 us
    pallas_call x3, Pallas kernels, pack(): pl.pallas_call(functools.partial(pack_kernel, parts), out_shape=[jax.Shap...  9.41 us
    pallas_call x1, Pallas kernels, halo_pack(): pl.pallas_call(halo_kernel, out_shape=[jax.ShapeDtypeStruct((3, 2, 128, H...  5.07 us
  transfers between devices with their start and end apart: 29, of which 14 were waited for; matrix products, arithmetic and copies ran while one was open for 1% of the time, Pallas kernels for 19%

profile of v7, /device:TPU:1, one launch (start us, length us, event | category | flops | bytes accessed | tf_op | source)
XLA Modules:
  0.0 205.4 jit_solution(6125016303759882467)
XLA Ops:
  0.0 2.5 %pack.3 = (bf16[3,2,8,8,1536]{4,3,2,1,0:T(8,128)(2,1)}, bf16[3,2,8,8,1536]{4,3,2,1,0:T(8,128)(2,1)}) custom-call(s32[1]{0:T(128)} %bitcast.meta, bf16[4,2,8,2,8,1536]{5,4,3,2,1,0:T(8,128)(2,1)} %bitcast.47, bf16[4,2,8,2,8,1536]{5,4,3,2,1,0:T(8,128)(2,1)} %bitcast.50, bf16[4,2,8,2,8,1536]{5,4,3,2,1,0:T(8,128)(2,1)} %bitcast.53), custom_call_target="tpu_custom_call" | custom-call | bytes 6291456 | tf_op jit(solution)/shard_map/pack/pallas_call | solution.py:98
  2.6 2.5 %collective-permute-start = (bf16[24,1536]{1,0:T(8,128)(2,1)S(1)}, bf16[24,1536]{1,0:T(8,128)(2,1)S(1)}, u32[]{:S(2)}, u32[]{:S(2)}) collective-permute-start(bf16[24,1536]{1,0:T(8,128)(2,1)S(1)} %bitcast.63), channel_id=1, source_target_pairs={{0,16},{1,17},{2,18},{3,19},{4,20},{5,21},{6,22},{7,23},{8,24},{9,... | collective-permute-start | bytes 221192 | tf_op jit(solution)/shard_map/ppermute | solution.py:59
  5.1 3.3 %collective-permute-start.1 = (bf16[24,1536]{1,0:T(8,128)(2,1)S(1)}, bf16[24,1536]{1,0:T(8,128)(2,1)S(1)}, u32[]{:S(2)}, u32[]{:S(2)}) collective-permute-start(bf16[24,1536]{1,0:T(8,128)(2,1)S(1)} %bitcast.64), channel_id=1, source_target_pairs={{0,64},{1,65},{2,66},{3,67},{4,68},{5,69},{6,70},{7,71},{8,72},{9,... | collective-permute-start | bytes 221192 | tf_op jit(solution)/shard_map/ppermute | solution.py:59
  9.1 2.9 %collective-permute-start.3 = (bf16[3,128,1536]{2,1,0:T(8,128)(2,1)}, bf16[3,128,1536]{2,1,0:T(8,128)(2,1)S(1)}, u32[]{:S(2)}, u32[]{:S(2)}) collective-permute-start(bf16[3,128,1536]{2,1,0:T(8,128)(2,1)} %bitcast.70), channel_id=1, source_target_pairs={{0,4},{1,5},{2,6},{3,7},{4,8},{5,9},{6,10},{7,11},{8,12},{9,13},{1... | collective-permute-start | bytes 3538952 | tf_op jit(solution)/shard_map/ppermute | solution.py:59
  12.1 2.7 %collective-permute-start.4 = (bf16[3,128,1536]{2,1,0:T(8,128)(2,1)}, bf16[3,128,1536]{2,1,0:T(8,128)(2,1)S(1)}, u32[]{:S(2)}, u32[]{:S(2)}) collective-permute-start(bf16[3,128,1536]{2,1,0:T(8,128)(2,1)} %bitcast.69), channel_id=1, source_target_pairs={{0,1},{1,2},{2,3},{3,0},{4,5},{5,6},{6,7},{7,4},{8,9},{9,10},{10,1... | collective-permute-start | bytes 3538952 | tf_op jit(solution)/shard_map/ppermute | solution.py:59
  14.8 2.5 %pack.4 = (bf16[3,2,8,8,1536]{4,3,2,1,0:T(8,128)(2,1)}, bf16[3,2,8,8,1536]{4,3,2,1,0:T(8,128)(2,1)}) custom-call(s32[1]{0:T(128)} %bitcast.meta, bf16[4,2,8,2,8,1536]{5,4,3,2,1,0:T(8,128)(2,1)} %bitcast.48, bf16[4,2,8,2,8,1536]{5,4,3,2,1,0:T(8,128)(2,1)} %bitcast.51, bf16[4,2,8,2,8,1536]{5,4,3,2,1,0:T(8,128)(2,1)} %bitcast.54), custom_call_target="tpu_custom_call" | custom-call | bytes 6291456 | tf_op jit(solution)/shard_map/pack/pallas_call | solution.py:98
  19.6 4.3 %pack.5 = (bf16[2,2,8,8,1536]{4,3,2,1,0:T(8,128)(2,1)}, bf16[2,2,8,8,1536]{4,3,2,1,0:T(8,128)(2,1)}, bf16[3,2,8,8,1536]{4,3,2,1,0:T(8,128)(2,1)}, bf16[3,2,8,8,1...) custom-call(s32[1]{0:T(128)} %bitcast.meta, ...), custom_call_target="tpu_custom_call" | custom-call | bytes 12582912 | tf_op jit(solution)/shard_map/pack/pallas_call | solution.py:98
  24.0 3.2 %collective-permute-done.3.refs_1_.x = bf16[3,128,1536]{2,1,0:T(8,128)(2,1)S(1)} collective-permute-done((bf16[3,128,1536]{2,1,0:T(8,128)(2,1)}, bf16[3,128,1536]{2,1,0:T(8,128)(2,1)S(1)}, u32[]{:S(2)}, u32[]{:S(2)}) %collective-permute-start.3) | collective-permute-done | bytes 1179680 | tf_op jit(solution)/shard_map/ppermute | solution.py:59
  27.2 8.1 %collective-permute-done.4.refs_2_.y = bf16[3,128,1536]{2,1,0:T(8,128)(2,1)S(1)} collective-permute-done((bf16[3,128,1536]{2,1,0:T(8,128)(2,1)}, bf16[3,128,1536]{2,1,0:T(8,128)(2,1)S(1)}, u32[]{:S(2)}, u32[]{:S(2)}) %collective-permute-start.4) | collective-permute-done | bytes 1179680 | tf_op jit(solution)/shard_map/ppermute | solution.py:59
  35.3 3.4 %collective-permute-start.5 = (bf16[4,24,1536]{2,1,0:T(8,128)(2,1)S(1)}, bf16[4,24,1536]{2,1,0:T(8,128)(2,1)S(1)}, u32[]{:S(2)}, u32[]{:S(2)}) collective-permute-start(bf16[4,24,1536]{2,1,0:T(8,128)(2,1)S(1)} %constant_dynamic-slice_fusion), channel_id=1, source_target_pairs={{0,3},{1,0},{2,1},{3,2},{4,7},{5,4},{6,5},{7,6},{8,11},{9,8},{10,9... | collective-permute-start | bytes 884744 | tf_op jit(solution)/shard_map/ppermute | solution.py:59
  39.3 2.5 %collective-permute-done.10.refs_5_.y = bf16[3,128,1536]{2,1,0:T(8,128)(2,1)} collective-permute-done((bf16[3,128,1536]{2,1,0:T(8,128)(2,1)}, bf16[3,128,1536]{2,1,0:T(8,128)(2,1)}, u32[]{:S(2)}, u32[]{:S(2)}) %collective-permute-start.10) | collective-permute-done | bytes 1179680 | tf_op jit(solution)/shard_map/ppermute | solution.py:59
  41.8 3.9 %collective-permute-start.8 = (bf16[3,128,1536]{2,1,0:T(8,128)(2,1)}, bf16[3,128,1536]{2,1,0:T(8,128)(2,1)S(1)}, u32[]{:S(2)}, u32[]{:S(2)}) collective-permute-start(bf16[3,128,1536]{2,1,0:T(8,128)(2,1)} %bitcast.72), channel_id=1, source_target_pairs={{0,5},{1,6},{2,7},{3,4},{4,9},{5,10},{6,11},{7,8},{8,13},{9,14},{1... | collective-permute-start | bytes 3538952 | tf_op jit(solution)/shard_map/ppermute | solution.py:59
  45.7 5.1 %halo_pack.1 = (bf16[3,2,128,1536]{3,2,1,0:T(8,128)(2,1)}, bf16[3,2,128,1536]{3,2,1,0:T(8,128)(2,1)}) custom-call(bf16[2,128,1536]{2,1,0:T(8,128)(2,1)} %bitcast.59, bf16[3,128,1536]{2,1,0:T(8,128)(2,1)} %copy-done.1, bf16[3,128,1536]{2,1,0:T(8,128)(2,1)} %copy-done.2, bf16[2,128,1536]{2,1,0:T(8,128)(2,1)} %bitcast.61, ...), custom_call_target="tpu_custom_call" | custom-call | bytes 10485760 | tf_op jit(solution)/shard_map/halo_pack/pallas_call | solution.py:125
  50.8 2.8 %collective-permute-start.12 = (bf16[3,2,128,1536]{3,2,1,0:T(8,128)(2,1)}, bf16[3,2,128,1536]{3,2,1,0:T(8,128)(2,1)S(1)}, u32[]{:S(2)}, u32[]{:S(2)}) collective-permute-start(bf16[3,2,128,1536]{3,2,1,0:T(8,128)(2,1)} %get-tuple-element.101), channel_id=1, source_target_pairs={{32,0},{33,1},{34,2},{35,3},{36,4},{37,5},{38,6},{39,7},{40,8},{41... | collective-permute-start | bytes 7077896 | tf_op jit(solution)/shard_map/ppermute | solution.py:59
  53.6 6.4 %collective-permute-done.5 = bf16[4,24,1536]{2,1,0:T(8,128)(2,1)S(1)} collective-permute-done((bf16[4,24,1536]{2,1,0:T(8,128)(2,1)S(1)}, bf16[4,24,1536]{2,1,0:T(8,128)(2,1)S(1)}, u32[]{:S(2)}, u32[]{:S(2)}) %collective-permute-start.5) | collective-permute-done | bytes 294944 | tf_op jit(solution)/shard_map/ppermute | solution.py:59
  60.0 8.7 %collective-permute-start.13 = (bf16[3,2,128,1536]{3,2,1,0:T(8,128)(2,1)}, bf16[3,2,128,1536]{3,2,1,0:T(8,128)(2,1)S(1)}, u32[]{:S(2)}, u32[]{:S(2)}) collective-permute-start(bf16[3,2,128,1536]{3,2,1,0:T(8,128)(2,1)} %get-tuple-element.102), channel_id=1, source_target_pairs={{0,32},{1,33},{2,34},{3,35},{4,36},{5,37},{6,38},{7,39},{8,40},{9,... | collective-permute-start | bytes 7077896 | tf_op jit(solution)/shard_map/ppermute | solution.py:59
  69.2 19.1 %collective-permute-done.11.d = bf16[3,128,1536]{2,1,0:T(8,128)(2,1)S(1)} collective-permute-done((bf16[3,128,1536]{2,1,0:T(8,128)(2,1)}, bf16[3,128,1536]{2,1,0:T(8,128)(2,1)S(1)}, u32[]{:S(2)}, u32[]{:S(2)}) %collective-permute-start.11) | collective-permute-done | bytes 1179680 | tf_op jit(solution)/shard_map/ppermute | solution.py:59
  88.4 12.9 %collective-permute-done.12.h3 = bf16[3,2,128,1536]{3,2,1,0:T(8,128)(2,1)S(1)} collective-permute-done((bf16[3,2,128,1536]{3,2,1,0:T(8,128)(2,1)}, bf16[3,2,128,1536]{3,2,1,0:T(8,128)(2,1)S(1)}, u32[]{:S(2)}, u32[]{:S(2)}) %collective-permute-start.12) | collective-permute-done | bytes 2359328 | tf_op jit(solution)/shard_map/ppermute | solution.py:59
  101.3 6.1 %collective-permute-done.13.h3 = bf16[3,2,128,1536]{3,2,1,0:T(8,128)(2,1)S(1)} collective-permute-done((bf16[3,2,128,1536]{3,2,1,0:T(8,128)(2,1)}, bf16[3,2,128,1536]{3,2,1,0:T(8,128)(2,1)S(1)}, u32[]{:S(2)}, u32[]{:S(2)}) %collective-permute-start.13) | collective-permute-done | bytes 2359328 | tf_op jit(solution)/shard_map/ppermute | solution.py:59
  109.7 5.6 %collective-permute-start.16 = (bf16[2,128,1536]{2,1,0:T(8,128)(2,1)S(1)}, bf16[2,128,1536]{2,1,0:T(8,128)(2,1)S(1)}, u32[]{:S(2)}, u32[]{:S(2)}) collective-permute-start(bf16[2,128,1536]{2,1,0:T(8,128)(2,1)S(1)} %slice.7), channel_id=1, source_target_pairs={{0,32},{1,33},{2,34},{3,35},{4,36},{5,37},{6,38},{7,39},{8,40},{9,... | collective-permute-start | bytes 2359304 | tf_op jit(solution)/shard_map/ppermute | solution.py:59
  115.4 7.6 %collective-permute-done.15.hd = bf16[2,128,1536]{2,1,0:T(8,128)(2,1)S(1)} collective-permute-done((bf16[2,128,1536]{2,1,0:T(8,128)(2,1)S(1)}, bf16[2,128,1536]{2,1,0:T(8,128)(2,1)S(1)}, u32[]{:S(2)}, u32[]{:S(2)}) %collective-permute-start.15) | collective-permute-done | bytes 786464 | tf_op jit(solution)/shard_map/ppermute | solution.py:59
  124.2 3.0 %collective-permute-start.17 = (bf16[384,1536]{1,0:T(8,128)(2,1)}, bf16[384,1536]{1,0:T(8,128)(2,1)}, u32[]{:S(2)}, u32[]{:S(2)}) collective-permute-start(bf16[384,1536]{1,0:T(8,128)(2,1)} %collective-permute-done.14.refs_9_), channel_id=1, source_target_pairs={{0,4},{1,5},{2,6},{3,7},{4,8},{5,9},{6,10},{7,11},{8,12},{9,13},{1... | collective-permute-start | bytes 3538952 | tf_op jit(solution)/shard_map/ppermute | solution.py:59
  127.2 13.6 %attend.2 = (bf16[128,1536]{1,0:T(8,128)(2,1)}, bf16[128,1536]{1,0:T(8,128)(2,1)}, bf16[128,1536]{1,0:T(8,128)(2,1)}, bf16[128,1536]{1,0:T(8,128)(2,1)}) custom-call(s32[4]{0:T(128)} %get-tuple-element.87.meta, bf16[2,128,1536]{2,1,0:T(8,128)(2,1)} %bitcast.62, bf16[1,128,1536]{2,1,0:T(8,128)(2,1)} %bitcast.74, ...), custom_call_target="tpu_custom_call" | custom-call | flops 6442450944 | bytes 10485760 | tf_op jit(solution)/shard_map/attend/pallas_call | solution.py:214
  141.4 2.4 %collective-permute-start.20 = (bf16[384,1536]{1,0:T(8,128)(2,1)}, bf16[384,1536]{1,0:T(8,128)(2,1)S(1)}, u32[]{:S(2)}, u32[]{:S(2)}) collective-permute-start(bf16[384,1536]{1,0:T(8,128)(2,1)} %collective-permute-done.17.refs_10_), channel_id=1, source_target_pairs={{0,4},{1,5},{2,6},{3,7},{4,8},{5,9},{6,10},{7,11},{8,12},{9,13},{1... | collective-permute-start | bytes 3538952 | tf_op jit(solution)/shard_map/ppermute | solution.py:59
  143.8 3.4 %collective-permute-start.23 = (bf16[128,1536]{1,0:T(8,128)(2,1)}, bf16[128,1536]{1,0:T(8,128)(2,1)S(1)}, u32[]{:S(2)}, u32[]{:S(2)}) collective-permute-start(bf16[128,1536]{1,0:T(8,128)(2,1)} %get-tuple-element.117), channel_id=1, source_target_pairs={{3,0},{0,1},{1,2},{2,3},{7,4},{4,5},{5,6},{6,7},{11,8},{8,9},{9,10... | collective-permute-start | bytes 1179656 | tf_op jit(solution)/shard_map/ppermute | solution.py:59
  147.3 13.6 %attend.3 = (bf16[128,1536]{1,0:T(8,128)(2,1)}, bf16[128,1536]{1,0:T(8,128)(2,1)}, bf16[128,1536]{1,0:T(8,128)(2,1)}, bf16[128,1536]{1,0:T(8,128)(2,1)}) custom-call(s32[4]{0:T(128)} %get-tuple-element.87.meta, bf16[2,128,1536]{2,1,0:T(8,128)(2,1)} %bitcast.60, bf16[1,128,1536]{2,1,0:T(8,128)(2,1)} %bitcast.73, bf16[3,128,1536]{2,1,0:T(8,128)(2,1)} %copy-done.1, ...), custom_call_target="tpu_custom_call" | custom-call | flops 6442450944 | bytes 10485760 | tf_op jit(solution)/shard_map/attend/pallas_call | solution.py:214
  163.1 4.2 %collective-permute-done.24.refs_7_ = bf16[128,1536]{1,0:T(8,128)(2,1)S(1)} collective-permute-done((bf16[128,1536]{1,0:T(8,128)(2,1)}, bf16[128,1536]{1,0:T(8,128)(2,1)S(1)}, u32[]{:S(2)}, u32[]{:S(2)}) %collective-permute-start.24) | collective-permute-done | bytes 393248 | tf_op jit(solution)/shard_map/ppermute | solution.py:59
  167.4 3.2 %collective-permute-start.27 = (bf16[128,1536]{1,0:T(8,128)(2,1)}, bf16[128,1536]{1,0:T(8,128)(2,1)S(1)}, u32[]{:S(2)}, u32[]{:S(2)}) collective-permute-start(bf16[128,1536]{1,0:T(8,128)(2,1)} %get-tuple-element.130), channel_id=1, source_target_pairs={{5,0},{6,1},{7,2},{4,3},{9,4},{10,5},{11,6},{8,7},{13,8},{14,9},{1... | collective-permute-start | bytes 1179656 | tf_op jit(solution)/shard_map/ppermute | solution.py:59
  170.7 5.6 %collective-permute-done.25.refs_1_ = bf16[128,1536]{1,0:T(8,128)(2,1)S(1)} collective-permute-done((bf16[128,1536]{1,0:T(8,128)(2,1)}, bf16[128,1536]{1,0:T(8,128)(2,1)S(1)}, u32[]{:S(2)}, u32[]{:S(2)}) %collective-permute-start.25) | collective-permute-done | bytes 393248 | tf_op jit(solution)/shard_map/ppermute | solution.py:59
  176.3 6.7 %collective-permute-done.27.refs_3_ = bf16[128,1536]{1,0:T(8,128)(2,1)S(1)} collective-permute-done((bf16[128,1536]{1,0:T(8,128)(2,1)}, bf16[128,1536]{1,0:T(8,128)(2,1)S(1)}, u32[]{:S(2)}, u32[]{:S(2)}) %collective-permute-start.27) | collective-permute-done | bytes 393248 | tf_op jit(solution)/shard_map/ppermute | solution.py:59
  184.8 2.5 %collective-permute-done.28.refs_15_ = bf16[384,1536]{1,0:T(8,128)(2,1)S(1)} collective-permute-done((bf16[384,1536]{1,0:T(8,128)(2,1)S(1)}, bf16[384,1536]{1,0:T(8,128)(2,1)S(1)}, u32[]{:S(2)}, u32[]{:S(2)}) %collective-permute-start.28) | collective-permute-done | bytes 1179680 | tf_op jit(solution)/shard_map/ppermute | solution.py:59
  188.3 16.9 %project.1 = bf16[4,16,16,3072]{3,2,1,0:T(8,128)(2,1)} custom-call(s32[4]{0:T(128)} %get-tuple-element.87.meta, s32[4]{0:T(128)} %get-tuple-element.88.places, bf16[128,1536]{1,0:T(8,128)(2,1)} %get-tuple-element.131.refs_0_, bf16[128,1536]{1,0:T(8,128)(2,1)} %copy-done.17, bf16[128,1536]{1,0:T(8,128)(2,1)} %copy-done.18, bf16[128,1536]{1,0:T(8,128)(2,1)} %copy-done.19, ...), custom_call_target="tpu_custom_call" | custom-call | flops 9663676416 | bytes 26214400 | tf_op jit(solution)/shard_map/project/pallas_call | solution.py:297
  (96 shorter events, 13.3 us)
Async XLA Ops:
  2.6 16.8 %collective-permute-start = (bf16[24,1536]{1,0:T(8,128)(2,1)S(1)}, bf16[24,1536]{1,0:T(8,128)(2,1)S(1)}, u32[]{:S(2)}, u32[]{:S(2)}) collective-permute-start(bf16[24,1536]{1,0:T(8,128)(2,1)S(1)} %bitcast.63), channel_id=1, source_target_pairs={{0,16},{1,17},{2,18},{3,19},{4,20},{5,21},{6,22},{7,23},{8,24},{9,... | collective-permute-start | bytes 221192 | tf_op jit(solution)/shard_map/ppermute | solution.py:59
  5.1 14.3 %collective-permute-start.1 = (bf16[24,1536]{1,0:T(8,128)(2,1)S(1)}, bf16[24,1536]{1,0:T(8,128)(2,1)S(1)}, u32[]{:S(2)}, u32[]{:S(2)}) collective-permute-start(bf16[24,1536]{1,0:T(8,128)(2,1)S(1)} %bitcast.64), channel_id=1, source_target_pairs={{0,64},{1,65},{2,66},{3,67},{4,68},{5,69},{6,70},{7,71},{8,72},{9,... | collective-permute-start | bytes 221192 | tf_op jit(solution)/shard_map/ppermute | solution.py:59
  8.4 11.0 %collective-permute-start.2 = (bf16[24,1536]{1,0:T(8,128)(2,1)S(1)}, bf16[24,1536]{1,0:T(8,128)(2,1)S(1)}, u32[]{:S(2)}, u32[]{:S(2)}) collective-permute-start(bf16[24,1536]{1,0:T(8,128)(2,1)S(1)} %bitcast.65), channel_id=1, source_target_pairs={{0,80},{1,81},{2,82},{3,83},{4,84},{5,85},{6,86},{7,87},{8,88},{9,... | collective-permute-start | bytes 221192 | tf_op jit(solution)/shard_map/ppermute | solution.py:59
  9.1 18.1 %collective-permute-start.3 = (bf16[3,128,1536]{2,1,0:T(8,128)(2,1)}, bf16[3,128,1536]{2,1,0:T(8,128)(2,1)S(1)}, u32[]{:S(2)}, u32[]{:S(2)}) collective-permute-start(bf16[3,128,1536]{2,1,0:T(8,128)(2,1)} %bitcast.70), channel_id=1, source_target_pairs={{0,4},{1,5},{2,6},{3,7},{4,8},{5,9},{6,10},{7,11},{8,12},{9,13},{1... | collective-permute-start | bytes 3538952 | tf_op jit(solution)/shard_map/ppermute | solution.py:59
  12.1 23.3 %collective-permute-start.4 = (bf16[3,128,1536]{2,1,0:T(8,128)(2,1)}, bf16[3,128,1536]{2,1,0:T(8,128)(2,1)S(1)}, u32[]{:S(2)}, u32[]{:S(2)}) collective-permute-start(bf16[3,128,1536]{2,1,0:T(8,128)(2,1)} %bitcast.69), channel_id=1, source_target_pairs={{0,1},{1,2},{2,3},{3,0},{4,5},{5,6},{6,7},{7,4},{8,9},{9,10},{10,1... | collective-permute-start | bytes 3538952 | tf_op jit(solution)/shard_map/ppermute | solution.py:59
  19.5 22.4 %collective-permute-start.10 = (bf16[3,128,1536]{2,1,0:T(8,128)(2,1)}, bf16[3,128,1536]{2,1,0:T(8,128)(2,1)}, u32[]{:S(2)}, u32[]{:S(2)}) collective-permute-start(bf16[3,128,1536]{2,1,0:T(8,128)(2,1)} %bitcast.68), channel_id=1, source_target_pairs={{0,3},{1,0},{2,1},{3,2},{4,7},{5,4},{6,5},{7,6},{8,11},{9,8},{10,9... | collective-permute-start | bytes 3538952 | tf_op jit(solution)/shard_map/ppermute | solution.py:59
  19.5 26.2 %collective-permute-start.9 = (bf16[3,128,1536]{2,1,0:T(8,128)(2,1)}, bf16[3,128,1536]{2,1,0:T(8,128)(2,1)}, u32[]{:S(2)}, u32[]{:S(2)}) collective-permute-start(bf16[3,128,1536]{2,1,0:T(8,128)(2,1)} %bitcast.67), channel_id=1, source_target_pairs={{0,28},{1,29},{2,30},{3,31},{4,0},{5,1},{6,2},{7,3},{8,4},{9,5},{1... | collective-permute-start | bytes 3538952 | tf_op jit(solution)/shard_map/ppermute | solution.py:59
  35.3 24.7 %collective-permute-start.5 = (bf16[4,24,1536]{2,1,0:T(8,128)(2,1)S(1)}, bf16[4,24,1536]{2,1,0:T(8,128)(2,1)S(1)}, u32[]{:S(2)}, u32[]{:S(2)}) collective-permute-start(bf16[4,24,1536]{2,1,0:T(8,128)(2,1)S(1)} %constant_dynamic-slice_fusion), channel_id=1, source_target_pairs={{0,3},{1,0},{2,1},{3,2},{4,7},{5,4},{6,5},{7,6},{8,11},{9,8},{10,9... | collective-permute-start | bytes 884744 | tf_op jit(solution)/shard_map/ppermute | solution.py:59
  38.8 30.0 %collective-permute-start.6 = (bf16[4,24,1536]{2,1,0:T(8,128)(2,1)S(1)}, bf16[4,24,1536]{2,1,0:T(8,128)(2,1)S(1)}, u32[]{:S(2)}, u32[]{:S(2)}) collective-permute-start(bf16[4,24,1536]{2,1,0:T(8,128)(2,1)S(1)} %constant_dynamic-slice_fusion), channel_id=1, source_target_pairs={{0,2},{1,3},{2,0},{3,1},{4,6},{5,7},{6,4},{7,5},{8,10},{9,11},{10,... | collective-permute-start | bytes 884744 | tf_op jit(solution)/shard_map/ppermute | solution.py:59
  38.8 30.1 %collective-permute-start.7 = (bf16[4,24,1536]{2,1,0:T(8,128)(2,1)S(1)}, bf16[4,24,1536]{2,1,0:T(8,128)(2,1)S(1)}, u32[]{:S(2)}, u32[]{:S(2)}) collective-permute-start(bf16[4,24,1536]{2,1,0:T(8,128)(2,1)S(1)} %constant_dynamic-slice_fusion), channel_id=1, source_target_pairs={{0,1},{1,2},{2,3},{3,0},{4,5},{5,6},{6,7},{7,4},{8,9},{9,10},{10,1... | collective-permute-start | bytes 884744 | tf_op jit(solution)/shard_map/ppermute | solution.py:59
  41.8 27.4 %collective-permute-start.8 = (bf16[3,128,1536]{2,1,0:T(8,128)(2,1)}, bf16[3,128,1536]{2,1,0:T(8,128)(2,1)S(1)}, u32[]{:S(2)}, u32[]{:S(2)}) collective-permute-start(bf16[3,128,1536]{2,1,0:T(8,128)(2,1)} %bitcast.72), channel_id=1, source_target_pairs={{0,5},{1,6},{2,7},{3,4},{4,9},{5,10},{6,11},{7,8},{8,13},{9,14},{1... | collective-permute-start | bytes 3538952 | tf_op jit(solution)/shard_map/ppermute | solution.py:59
  50.8 50.5 %collective-permute-start.12 = (bf16[3,2,128,1536]{3,2,1,0:T(8,128)(2,1)}, bf16[3,2,128,1536]{3,2,1,0:T(8,128)(2,1)S(1)}, u32[]{:S(2)}, u32[]{:S(2)}) collective-permute-start(bf16[3,2,128,1536]{3,2,1,0:T(8,128)(2,1)} %get-tuple-element.101), channel_id=1, source_target_pairs={{32,0},{33,1},{34,2},{35,3},{36,4},{37,5},{38,6},{39,7},{40,8},{41... | collective-permute-start | bytes 7077896 | tf_op jit(solution)/shard_map/ppermute | solution.py:59
  60.0 47.4 %collective-permute-start.13 = (bf16[3,2,128,1536]{3,2,1,0:T(8,128)(2,1)}, bf16[3,2,128,1536]{3,2,1,0:T(8,128)(2,1)S(1)}, u32[]{:S(2)}, u32[]{:S(2)}) collective-permute-start(bf16[3,2,128,1536]{3,2,1,0:T(8,128)(2,1)} %get-tuple-element.102), channel_id=1, source_target_pairs={{0,32},{1,33},{2,34},{3,35},{4,36},{5,37},{6,38},{7,39},{8,40},{9,... | collective-permute-start | bytes 7077896 | tf_op jit(solution)/shard_map/ppermute | solution.py:59
  68.7 19.7 %collective-permute-start.11 = (bf16[3,128,1536]{2,1,0:T(8,128)(2,1)}, bf16[3,128,1536]{2,1,0:T(8,128)(2,1)S(1)}, u32[]{:S(2)}, u32[]{:S(2)}) collective-permute-start(bf16[3,128,1536]{2,1,0:T(8,128)(2,1)} %bitcast.71), channel_id=1, source_target_pairs={{0,31},{1,28},{2,29},{3,30},{4,3},{5,0},{6,1},{7,2},{8,7},{9,4},{1... | collective-permute-start | bytes 3538952 | tf_op jit(solution)/shard_map/ppermute | solution.py:59
  69.2 71.5 %copy-start = (bf16[4,4,24,1536]{3,2,1,0:T(8,128)(2,1)}, bf16[4,4,24,1536]{3,2,1,0:T(8,128)(2,1)S(1)}, u32[]{:S(2)}) copy-start(bf16[4,4,24,1536]{3,2,1,0:T(8,128)(2,1)S(1)} %copy.7) | copy-start | bytes 3538948
  69.2 71.5 %copy-start.3 = (bf16[3,128,1536]{2,1,0:T(8,128)(2,1)}, bf16[3,128,1536]{2,1,0:T(8,128)(2,1)S(1)}, u32[]{:S(2)}) copy-start(bf16[3,128,1536]{2,1,0:T(8,128)(2,1)S(1)} %collective-permute-done.8.d) | copy-start | bytes 3538948
  88.4 38.8 %copy-start.4 = (bf16[3,128,1536]{2,1,0:T(8,128)(2,1)}, bf16[3,128,1536]{2,1,0:T(8,128)(2,1)S(1)}, u32[]{:S(2)}) copy-start(bf16[3,128,1536]{2,1,0:T(8,128)(2,1)S(1)} %collective-permute-done.11.d) | copy-start | bytes 3538948
  107.4 16.8 %collective-permute-start.14 = (bf16[384,1536]{1,0:T(8,128)(2,1)S(1)}, bf16[384,1536]{1,0:T(8,128)(2,1)}, u32[]{:S(2)}, u32[]{:S(2)}) collective-permute-start(bf16[384,1536]{1,0:T(8,128)(2,1)S(1)} %bitcast.56), channel_id=1, source_target_pairs={{0,4},{1,5},{2,6},{3,7},{4,8},{5,9},{6,10},{7,11},{8,12},{9,13},{1... | collective-permute-start | bytes 3538952 | tf_op jit(solution)/shard_map/ppermute | solution.py:59
  107.7 15.3 %collective-permute-start.15 = (bf16[2,128,1536]{2,1,0:T(8,128)(2,1)S(1)}, bf16[2,128,1536]{2,1,0:T(8,128)(2,1)S(1)}, u32[]{:S(2)}, u32[]{:S(2)}) collective-permute-start(bf16[2,128,1536]{2,1,0:T(8,128)(2,1)S(1)} %slice.6), channel_id=1, source_target_pairs={{32,0},{33,1},{34,2},{35,3},{36,4},{37,5},{38,6},{39,7},{40,8},{41... | collective-permute-start | bytes 2359304 | tf_op jit(solution)/shard_map/ppermute | solution.py:59
  109.7 14.5 %collective-permute-start.16 = (bf16[2,128,1536]{2,1,0:T(8,128)(2,1)S(1)}, bf16[2,128,1536]{2,1,0:T(8,128)(2,1)S(1)}, u32[]{:S(2)}, u32[]{:S(2)}) collective-permute-start(bf16[2,128,1536]{2,1,0:T(8,128)(2,1)S(1)} %slice.7), channel_id=1, source_target_pairs={{0,32},{1,33},{2,34},{3,35},{4,36},{5,37},{6,38},{7,39},{8,40},{9,... | collective-permute-start | bytes 2359304 | tf_op jit(solution)/shard_map/ppermute | solution.py:59
  115.3 25.5 %collective-permute-start.18 = (bf16[384,1536]{1,0:T(8,128)(2,1)S(1)}, bf16[384,1536]{1,0:T(8,128)(2,1)}, u32[]{:S(2)}, u32[]{:S(2)}) collective-permute-start(bf16[384,1536]{1,0:T(8,128)(2,1)S(1)} %bitcast.57), channel_id=1, source_target_pairs={{0,32},{1,33},{2,34},{3,35},{4,36},{5,37},{6,38},{7,39},{8,40},{9,... | collective-permute-start | bytes 3538952 | tf_op jit(solution)/shard_map/ppermute | solution.py:59
  124.2 16.6 %collective-permute-start.17 = (bf16[384,1536]{1,0:T(8,128)(2,1)}, bf16[384,1536]{1,0:T(8,128)(2,1)}, u32[]{:S(2)}, u32[]{:S(2)}) collective-permute-start(bf16[384,1536]{1,0:T(8,128)(2,1)} %collective-permute-done.14.refs_9_), channel_id=1, source_target_pairs={{0,4},{1,5},{2,6},{3,7},{4,8},{5,9},{6,10},{7,11},{8,12},{9,13},{1... | collective-permute-start | bytes 3538952 | tf_op jit(solution)/shard_map/ppermute | solution.py:59
  127.1 13.6 %collective-permute-start.19 = (bf16[384,1536]{1,0:T(8,128)(2,1)}, bf16[384,1536]{1,0:T(8,128)(2,1)S(1)}, u32[]{:S(2)}, u32[]{:S(2)}) collective-permute-start(bf16[384,1536]{1,0:T(8,128)(2,1)} %collective-permute-done.14.refs_9_), channel_id=1, source_target_pairs={{0,32},{1,33},{2,34},{3,35},{4,36},{5,37},{6,38},{7,39},{8,40},{9,... | collective-permute-start | bytes 3538952 | tf_op jit(solution)/shard_map/ppermute | solution.py:59
  140.8 26.5 %collective-permute-start.21 = (bf16[384,1536]{1,0:T(8,128)(2,1)}, bf16[384,1536]{1,0:T(8,128)(2,1)S(1)}, u32[]{:S(2)}, u32[]{:S(2)}) collective-permute-start(bf16[384,1536]{1,0:T(8,128)(2,1)} %collective-permute-done.17.refs_10_), channel_id=1, source_target_pairs={{0,32},{1,33},{2,34},{3,35},{4,36},{5,37},{6,38},{7,39},{8,40},{9,... | collective-permute-start | bytes 3538952 | tf_op jit(solution)/shard_map/ppermute | solution.py:59
  141.4 29.3 %collective-permute-start.20 = (bf16[384,1536]{1,0:T(8,128)(2,1)}, bf16[384,1536]{1,0:T(8,128)(2,1)S(1)}, u32[]{:S(2)}, u32[]{:S(2)}) collective-permute-start(bf16[384,1536]{1,0:T(8,128)(2,1)} %collective-permute-done.17.refs_10_), channel_id=1, source_target_pairs={{0,4},{1,5},{2,6},{3,7},{4,8},{5,9},{6,10},{7,11},{8,12},{9,13},{1... | collective-permute-start | bytes 3538952 | tf_op jit(solution)/shard_map/ppermute | solution.py:59
  143.8 19.3 %collective-permute-start.22 = (bf16[128,1536]{1,0:T(8,128)(2,1)}, bf16[128,1536]{1,0:T(8,128)(2,1)S(1)}, u32[]{:S(2)}, u32[]{:S(2)}) collective-permute-start(bf16[128,1536]{1,0:T(8,128)(2,1)} %get-tuple-element.116), channel_id=1, source_target_pairs={{28,0},{29,1},{30,2},{31,3},{0,4},{1,5},{2,6},{3,7},{4,8},{5,9},{6... | collective-permute-start | bytes 1179656 | tf_op jit(solution)/shard_map/ppermute | solution.py:59
  143.8 19.3 %collective-permute-start.23 = (bf16[128,1536]{1,0:T(8,128)(2,1)}, bf16[128,1536]{1,0:T(8,128)(2,1)S(1)}, u32[]{:S(2)}, u32[]{:S(2)}) collective-permute-start(bf16[128,1536]{1,0:T(8,128)(2,1)} %get-tuple-element.117), channel_id=1, source_target_pairs={{3,0},{0,1},{1,2},{2,3},{7,4},{4,5},{5,6},{6,7},{11,8},{8,9},{9,10... | collective-permute-start | bytes 1179656 | tf_op jit(solution)/shard_map/ppermute | solution.py:59
  147.2 20.1 %collective-permute-start.24 = (bf16[128,1536]{1,0:T(8,128)(2,1)}, bf16[128,1536]{1,0:T(8,128)(2,1)S(1)}, u32[]{:S(2)}, u32[]{:S(2)}) collective-permute-start(bf16[128,1536]{1,0:T(8,128)(2,1)} %get-tuple-element.118), channel_id=1, source_target_pairs={{31,0},{28,1},{29,2},{30,3},{3,4},{0,5},{1,6},{2,7},{7,8},{4,9},{5... | collective-permute-start | bytes 1179656 | tf_op jit(solution)/shard_map/ppermute | solution.py:59
  167.3 8.9 %collective-permute-start.25 = (bf16[128,1536]{1,0:T(8,128)(2,1)}, bf16[128,1536]{1,0:T(8,128)(2,1)S(1)}, u32[]{:S(2)}, u32[]{:S(2)}) collective-permute-start(bf16[128,1536]{1,0:T(8,128)(2,1)} %get-tuple-element.128), channel_id=1, source_target_pairs={{4,0},{5,1},{6,2},{7,3},{8,4},{9,5},{10,6},{11,7},{12,8},{13,9},{1... | collective-permute-start | bytes 1179656 | tf_op jit(solution)/shard_map/ppermute | solution.py:59
  167.3 8.9 %collective-permute-start.26 = (bf16[128,1536]{1,0:T(8,128)(2,1)}, bf16[128,1536]{1,0:T(8,128)(2,1)S(1)}, u32[]{:S(2)}, u32[]{:S(2)}) collective-permute-start(bf16[128,1536]{1,0:T(8,128)(2,1)} %get-tuple-element.129), channel_id=1, source_target_pairs={{1,0},{2,1},{3,2},{0,3},{5,4},{6,5},{7,6},{4,7},{9,8},{10,9},{11,1... | collective-permute-start | bytes 1179656 | tf_op jit(solution)/shard_map/ppermute | solution.py:59
  167.4 15.6 %collective-permute-start.27 = (bf16[128,1536]{1,0:T(8,128)(2,1)}, bf16[128,1536]{1,0:T(8,128)(2,1)S(1)}, u32[]{:S(2)}, u32[]{:S(2)}) collective-permute-start(bf16[128,1536]{1,0:T(8,128)(2,1)} %get-tuple-element.130), channel_id=1, source_target_pairs={{5,0},{6,1},{7,2},{4,3},{9,4},{10,5},{11,6},{8,7},{13,8},{14,9},{1... | collective-permute-start | bytes 1179656 | tf_op jit(solution)/shard_map/ppermute | solution.py:59
  183.0 4.2 %collective-permute-start.28 = (bf16[384,1536]{1,0:T(8,128)(2,1)S(1)}, bf16[384,1536]{1,0:T(8,128)(2,1)S(1)}, u32[]{:S(2)}, u32[]{:S(2)}) collective-permute-start(bf16[384,1536]{1,0:T(8,128)(2,1)S(1)} %collective-permute-done.20.refs_11_), channel_id=1, source_target_pairs={{0,32},{1,33},{2,34},{3,35},{4,36},{5,37},{6,38},{7,39},{8,40},{9,... | collective-permute-start | bytes 3538952 | tf_op jit(solution)/shard_map/ppermute | solution.py:59
  (18 other events, 235.9 us)

commit v8 on v6

--- a/solution.py
+++ b/solution.py
@@ -45,11 +45,11 @@
     return [(index(f, r, c), index(f ^ 1, r, c)) for f, r, c in every()]
 
 
-def turn_pairs():
+def turn_pairs(step):
     pairs = []
     for f, r, c in every():
         zlo, x = divmod(r, 4)
-        pairs.append((index(f, r, c), index(f, zlo * 4 + (x + 1 - 2 * (f % 2)) % 4, c)))
+        pairs.append((index(f, r, c), index(f, zlo * 4 + (x + step * (1 - 2 * (f % 2))) % 4, c)))
     return pairs
 
 
@@ -104,32 +104,6 @@
         name="pack",
     )(meta, k, v, q)
     return [o.reshape(-1, 128, HD) for o in outs]
-
-
-def halo_kernel(*refs):
-    srcs, outs, sems = refs[:6], refs[6:8], refs[8]
-    copies = []
-    for half in range(2):
-        for n in range(3):
-            src = srcs[3 * half + n].at[pl.ds(0, 2)]
-            copies.append(pltpu.make_async_copy(src, outs[half].at[n], sems.at[half, n]))
-    for copy in copies:
-        copy.start()
-    for copy in copies:
-        copy.wait()
-
-
-def halo_pack(*pieces):
-    return pl.pallas_call(
-        halo_kernel,
-        out_shape=[jax.ShapeDtypeStruct((3, 2, 128, HD), jnp.bfloat16)] * 2,
-        in_specs=[pl.BlockSpec(memory_space=pltpu.VMEM)] * 6,
-        out_specs=[pl.BlockSpec(memory_space=pl.ANY)] * 2,
-        scratch_shapes=[pltpu.SemaphoreType.DMA((2, 3))],
-        compiler_params=pltpu.CompilerParams(vmem_limit_bytes=VMEM),
-        cost_estimate=pl.CostEstimate(flops=0, bytes_accessed=10 * 2**20, transcendentals=0),
-        name="halo_pack",
-    )(*pieces)
 
 
 def features(half, meta, kaug, qaug, alive):
@@ -329,7 +303,7 @@
     up = lambda value: send(value, frame_pairs(1))
     down = lambda value: send(value, frame_pairs(-1))
     swap = lambda value: send(value, core_pairs())
-    turn = lambda value: send(value, turn_pairs())
+    turn = lambda value, step=1: send(value, turn_pairs(step))
     back = lambda half, mixed: [mixed[0]] + [send(mixed[n], window_pairs(half, *MOVES[n], back=True)) for n in (1, 2, 3)]
 
     x0, y0 = pack(((0, 1, "kvq"), (0, 2, "kvq")), frame, *arrays)
@@ -344,23 +318,19 @@
     d0, x0, y0, meta, places = together(d0, x0, y0, meta, places)
     d1, x1, y1 = together(d1, x1, y1)
     d0, d1 = go(d0, 0, both), go(d1, 1, both)
-    h0, h1 = halo_pack(skv0, x0, y0, skv1, x1, y1)
-    chunk, h0, h1 = together(chunk, h0, h1)
-    down3, up3 = down(h0), up(h1)
-    c0, d0, d1 = together(chunk, d0, d1)
-    c1 = turn(c0)
-    c1, down3, up3, hd0, hd1 = together(c1, down3, up3, d0[:2], d1[:2])
-    downd, upd, c2 = down(hd0), up(hd1), turn(c1)
-    c2, downd, upd = together(c2, downd, upd)
-
-    c3, s0, s1, s2 = turn(c2), swap(c0), swap(c1), swap(c2)
+    down3, up3 = down(jnp.stack([skv0, x0[:2], y0[:2]])), up(jnp.stack([skv1, x1[:2], y1[:2]]))
+    c0, d0, d1, down3, up3 = together(chunk, d0, d1, down3, up3)
+    downd, upd, c1 = down(d0[:2]), up(d1[:2]), turn(c0)
+    c0, c1, downd, upd = together(c0, c1, downd, upd)
+
+    c2, c3, s0, s1 = turn(c1), turn(c0, -1), swap(c0), swap(c1)
     mixed1 = attend(1, meta, skv1, sq1, x1, y1, d1, down3, downd)
-    c3, s0, s1, s2, skv0, *mixed1 = together(c3, s0, s1, s2, skv0, *mixed1)
-    attended1, s3 = back(1, mixed1), swap(c3)
+    s0, s1, skv0, *mixed1 = together(s0, s1, skv0, *mixed1)
+    attended1 = back(1, mixed1)
     mixed0 = attend(0, meta, skv0, sq0, x0, y0, d0, up3, upd)
-    s3, *rest = together(s3, *attended1, *mixed0)
+    c2, c3, *rest = together(c2, c3, *attended1, *mixed0)
     attended1, mixed0 = rest[:4], rest[4:]
-    attended0 = back(0, mixed0)
+    attended0, s2, s3 = back(0, mixed0), swap(c2), swap(c3)
     return project(attended0 + attended1, meta, places, (c0, c1, c2, c3, s0, s1, s2, s3), tokens_in)
 
 

time: 225 us -> 236 us (1.049); the launches traced: 222 us -> 236 us
  waiting for transfers between devices: 102 us -> 120 us
  Pallas kernels: 58.8 us -> 53.5 us
  starting transfers between devices: 41.1 us -> 38.4 us
    all_gather x1, waiting for transfers between devices: 39.6 us -> 71.5 us  [local(): lax.all_gather(out_weight.T, AXES, axis=0, tiled=True, axis_index_groups=...]
    ppermute x23, waiting for transfers between devices: 62 us -> 48.9 us  [send(): return lax.ppermute(value, AXES, pairs)]
    pallas_call x1 -> x0, Pallas kernels: 5.07 us -> none  [halo_pack(): pl.pallas_call(halo_kernel, out_shape=[jax.ShapeDtypeStruct((3, 2, 128, H...]
    ppermute x23, starting transfers between devices: 41.1 us -> 38.4 us  [send(): return lax.ppermute(value, AXES, pairs)]
  transfers between devices with their start and end apart: 24 -> 24, of which waited for: 14 -> 10; matrix products, arithmetic and copies ran while one was open for 2% -> 2% of each run, Pallas kernels for 19% -> 13%
where the time goes in v8:
time: 236 us
  waiting for transfers between devices  120 us (51%)
  Pallas kernels  53.5 us (23%)
  starting transfers between devices  38.4 us (16%)
  between operations  13.8 us (6%)
  local copies, waits for them, and re-layouts  5.85 us (2%)
  other arithmetic  3.78 us (2%)
    all_gather x1, waiting for transfers between devices, local(): lax.all_gather(out_weight.T, AXES, axis=0, tiled=True, axis_index_groups=...  71.5 us
    ppermute x23, waiting for transfers between devices, send(): return lax.ppermute(value, AXES, pairs)  48.9 us
    ppermute x23, starting transfers between devices, send(): return lax.ppermute(value, AXES, pairs)  38.4 us
    pallas_call x2, Pallas kernels, attend(): pl.pallas_call(functools.partial(attend_kernel, half), grid=(H // STEP,),...  27.2 us
    pallas_call x1, Pallas kernels, project(): pl.pallas_call(project_kernel, grid_spec=grid_spec, out_shape=jax.ShapeDt...  16.9 us
    pallas_call x3, Pallas kernels, pack(): pl.pallas_call(functools.partial(pack_kernel, parts), out_shape=[jax.Shap...  9.39 us
  transfers between devices with their start and end apart: 24, of which 10 were waited for; matrix products, arithmetic and copies ran while one was open for 2% of the time, Pallas kernels for 13%

profile of v8, /device:TPU:1, one launch (start us, length us, event | category | flops | bytes accessed | tf_op | source)
XLA Modules:
  0.0 235.7 jit_solution(5322002890926704965)
XLA Ops:
  6.5 2.5 %pack.3 = (bf16[3,2,8,8,1536]{4,3,2,1,0:T(8,128)(2,1)}, bf16[3,2,8,8,1536]{4,3,2,1,0:T(8,128)(2,1)}) custom-call(s32[1]{0:T(128)} %bitcast.meta, bf16[4,2,8,2,8,1536]{5,4,3,2,1,0:T(8,128)(2,1)} %bitcast.32, bf16[4,2,8,2,8,1536]{5,4,3,2,1,0:T(8,128)(2,1)} %bitcast.35, bf16[4,2,8,2,8,1536]{5,4,3,2,1,0:T(8,128)(2,1)} %bitcast.38), custom_call_target="tpu_custom_call" | custom-call | bytes 6291456 | tf_op jit(solution)/shard_map/pack/pallas_call | solution.py:96
  9.0 2.6 %pack.4 = (bf16[3,2,8,8,1536]{4,3,2,1,0:T(8,128)(2,1)}, bf16[3,2,8,8,1536]{4,3,2,1,0:T(8,128)(2,1)}) custom-call(s32[1]{0:T(128)} %bitcast.meta, bf16[4,2,8,2,8,1536]{5,4,3,2,1,0:T(8,128)(2,1)} %bitcast.33, bf16[4,2,8,2,8,1536]{5,4,3,2,1,0:T(8,128)(2,1)} %bitcast.36, bf16[4,2,8,2,8,1536]{5,4,3,2,1,0:T(8,128)(2,1)} %bitcast.39), custom_call_target="tpu_custom_call" | custom-call | bytes 6291456 | tf_op jit(solution)/shard_map/pack/pallas_call | solution.py:96
  11.6 2.1 collective-permute-start.3
  13.7 1.3 collective-permute-start.4
  15.0 2.7 %collective-permute-start = (bf16[3,128,1536]{2,1,0:T(8,128)(2,1)}, bf16[3,128,1536]{2,1,0:T(8,128)(2,1)S(1)}, u32[]{:S(2)}, u32[]{:S(2)}) collective-permute-start(bf16[3,128,1536]{2,1,0:T(8,128)(2,1)} %bitcast.4), channel_id=1, source_target_pairs={{0,4},{1,5},{2,6},{3,7},{4,8},{5,9},{6,10},{7,11},{8,12},{9,13},{1... | collective-permute-start | bytes 3538952 | tf_op jit(solution)/shard_map/ppermute | solution.py:57
  17.7 1.5 collective-permute-start.1
  19.2 4.3 %pack.5 = (bf16[2,2,8,8,1536]{4,3,2,1,0:T(8,128)(2,1)}, bf16[2,2,8,8,1536]{4,3,2,1,0:T(8,128)(2,1)}, bf16[3,2,8,8,1536]{4,3,2,1,0:T(8,128)(2,1)}, bf16[3,2,8,8,1...) custom-call(s32[1]{0:T(128)} %bitcast.meta, ...), custom_call_target="tpu_custom_call" | custom-call | bytes 12582912 | tf_op jit(solution)/shard_map/pack/pallas_call | solution.py:96
  24.2 1.2 pad_add_fusion
  25.5 9.6 %collective-permute-done.3.x = bf16[3,128,1536]{2,1,0:T(8,128)(2,1)S(1)} collective-permute-done((bf16[3,128,1536]{2,1,0:T(8,128)(2,1)}, bf16[3,128,1536]{2,1,0:T(8,128)(2,1)S(1)}, u32[]{:S(2)}, u32[]{:S(2)}) %collective-permute-start.3) | collective-permute-done | bytes 1179680 | tf_op jit(solution)/shard_map/ppermute | solution.py:57
  36.1 7.4 %collective-permute-done.x = bf16[3,128,1536]{2,1,0:T(8,128)(2,1)S(1)} collective-permute-done((bf16[3,128,1536]{2,1,0:T(8,128)(2,1)}, bf16[3,128,1536]{2,1,0:T(8,128)(2,1)S(1)}, u32[]{:S(2)}, u32[]{:S(2)}) %collective-permute-start) | collective-permute-done | bytes 1179680 | tf_op jit(solution)/shard_map/ppermute | solution.py:57
  43.6 2.4 %collective-permute-done.1.y = bf16[3,128,1536]{2,1,0:T(8,128)(2,1)S(1)} collective-permute-done((bf16[3,128,1536]{2,1,0:T(8,128)(2,1)}, bf16[3,128,1536]{2,1,0:T(8,128)(2,1)S(1)}, u32[]{:S(2)}, u32[]{:S(2)}) %collective-permute-start.1) | collective-permute-done | bytes 1179680 | tf_op jit(solution)/shard_map/ppermute | solution.py:57
  47.0 1.3 slice_bitcast_fusion
  48.6 5.9 %collective-permute-start.7 = (bf16[3,2,128,1536]{3,2,1,0:T(8,128)(2,1)S(1)}, bf16[3,2,128,1536]{3,2,1,0:T(8,128)(2,1)}, u32[]{:S(2)}, u32[]{:S(2)}) collective-permute-start(bf16[3,2,128,1536]{3,2,1,0:T(8,128)(2,1)S(1)} %pad_maximum_fusion.1), channel_id=1, source_target_pairs={{0,32},{1,33},{2,34},{3,35},{4,36},{5,37},{6,38},{7,39},{8,40},{9,... | collective-permute-start | bytes 7077896 | tf_op jit(solution)/shard_map/ppermute | solution.py:57
  54.6 1.7 pad_maximum_fusion
  56.3 1.9 collective-permute-start.6
  58.2 3.2 %collective-permute-start.2 = (bf16[3,128,1536]{2,1,0:T(8,128)(2,1)}, bf16[3,128,1536]{2,1,0:T(8,128)(2,1)S(1)}, u32[]{:S(2)}, u32[]{:S(2)}) collective-permute-start(bf16[3,128,1536]{2,1,0:T(8,128)(2,1)} %bitcast.47), channel_id=1, source_target_pairs={{0,5},{1,6},{2,7},{3,4},{4,9},{5,10},{6,11},{7,8},{8,13},{9,14},{1... | collective-permute-start | bytes 3538952 | tf_op jit(solution)/shard_map/ppermute | solution.py:57
  61.4 71.5 %all-gather.2.cloned.1.call-done.refs_8_ = bf16[384,1536]{1,0:T(8,128)(2,1)} async-done(((bf16[24,1536]{1,0:T(8,128)(2,1)}), bf16[384,1536]{1,0:T(8,128)(2,1)}) %all-gather.2.cloned.1.call-update) | async-done | bytes 1179664 | tf_op jit(solution)/shard_map/all_gather | solution.py:299
  133.0 2.5 %collective-permute-start.8 = (bf16[384,1536]{1,0:T(8,128)(2,1)}, bf16[384,1536]{1,0:T(8,128)(2,1)S(1)}, u32[]{:S(2)}, u32[]{:S(2)}) collective-permute-start(bf16[384,1536]{1,0:T(8,128)(2,1)} %all-gather.2.cloned.1.call-done.refs_8_), channel_id=1, source_target_pairs={{0,4},{1,5},{2,6},{3,7},{4,8},{5,9},{6,10},{7,11},{8,12},{9,13},{1... | collective-permute-start | bytes 3538952 | tf_op jit(solution)/shard_map/ppermute | solution.py:57
  135.5 1.3 slice.23
  136.8 4.4 %collective-permute-start.10 = (bf16[2,128,1536]{2,1,0:T(8,128)(2,1)S(1)}, bf16[2,128,1536]{2,1,0:T(8,128)(2,1)S(1)}, u32[]{:S(2)}, u32[]{:S(2)}) collective-permute-start(bf16[2,128,1536]{2,1,0:T(8,128)(2,1)S(1)} %slice.23), channel_id=1, source_target_pairs={{0,32},{1,33},{2,34},{3,35},{4,36},{5,37},{6,38},{7,39},{8,40},{9,... | collective-permute-start | bytes 2359304 | tf_op jit(solution)/shard_map/ppermute | solution.py:57
  141.2 1.9 collective-permute-start.9
  143.1 7.0 %collective-permute-done.10.hd = bf16[2,128,1536]{2,1,0:T(8,128)(2,1)S(1)} collective-permute-done((bf16[2,128,1536]{2,1,0:T(8,128)(2,1)S(1)}, bf16[2,128,1536]{2,1,0:T(8,128)(2,1)S(1)}, u32[]{:S(2)}, u32[]{:S(2)}) %collective-permute-start.10) | collective-permute-done | bytes 786464 | tf_op jit(solution)/shard_map/ppermute | solution.py:57
  150.1 5.9 %collective-permute-done.9.hd = bf16[2,128,1536]{2,1,0:T(8,128)(2,1)S(1)} collective-permute-done((bf16[2,128,1536]{2,1,0:T(8,128)(2,1)S(1)}, bf16[2,128,1536]{2,1,0:T(8,128)(2,1)S(1)}, u32[]{:S(2)}, u32[]{:S(2)}) %collective-permute-start.9) | collective-permute-done | bytes 786464 | tf_op jit(solution)/shard_map/ppermute | solution.py:57
  156.6 1.5 collective-permute-start.11
  158.1 13.6 %attend.2 = (bf16[128,1536]{1,0:T(8,128)(2,1)}, bf16[128,1536]{1,0:T(8,128)(2,1)}, bf16[128,1536]{1,0:T(8,128)(2,1)}, bf16[128,1536]{1,0:T(8,128)(2,1)}) custom-call(s32[4]{0:T(128)} %get-tuple-element.72.meta, bf16[2,128,1536]{2,1,0:T(8,128)(2,1)} %bitcast.43, bf16[1,128,1536]{2,1,0:T(8,128)(2,1)} %bitcast.51, bf16[3,128,1536]{2,1,0:T(8,128)(2,1)} %copy-done.5, ...), custom_call_target="tpu_custom_call" | custom-call | flops 6442450944 | bytes 10485760 | tf_op jit(solution)/shard_map/attend/pallas_call | solution.py:186
  171.8 3.2 %collective-permute-start.15 = (bf16[128,1536]{1,0:T(8,128)(2,1)}, bf16[128,1536]{1,0:T(8,128)(2,1)S(1)}, u32[]{:S(2)}, u32[]{:S(2)}) collective-permute-start(bf16[128,1536]{1,0:T(8,128)(2,1)} %get-tuple-element.98), channel_id=1, source_target_pairs={{28,0},{29,1},{30,2},{31,3},{0,4},{1,5},{2,6},{3,7},{4,8},{5,9},{6... | collective-permute-start | bytes 1179656 | tf_op jit(solution)/shard_map/ppermute | solution.py:57
  176.2 13.6 %attend.3 = (bf16[128,1536]{1,0:T(8,128)(2,1)}, bf16[128,1536]{1,0:T(8,128)(2,1)}, bf16[128,1536]{1,0:T(8,128)(2,1)}, bf16[128,1536]{1,0:T(8,128)(2,1)}) custom-call(s32[4]{0:T(128)} %get-tuple-element.72.meta, bf16[2,128,1536]{2,1,0:T(8,128)(2,1)} %bitcast.41, bf16[1,128,1536]{2,1,0:T(8,128)(2,1)} %bitcast.50, bf16[3,128,1536]{2,1,0:T(8,128)(2,1)} %copy-done.2, ...), custom_call_target="tpu_custom_call" | custom-call | flops 6442450944 | bytes 10485760 | tf_op jit(solution)/shard_map/attend/pallas_call | solution.py:186
  189.9 2.9 %collective-permute-done.17.refs_7_ = bf16[128,1536]{1,0:T(8,128)(2,1)S(1)} collective-permute-done((bf16[128,1536]{1,0:T(8,128)(2,1)}, bf16[128,1536]{1,0:T(8,128)(2,1)S(1)}, u32[]{:S(2)}, u32[]{:S(2)}) %collective-permute-start.17) | collective-permute-done | bytes 393248 | tf_op jit(solution)/shard_map/ppermute | solution.py:57
  192.8 3.1 %collective-permute-start.21 = (bf16[384,1536]{1,0:T(8,128)(2,1)S(1)}, bf16[384,1536]{1,0:T(8,128)(2,1)S(1)}, u32[]{:S(2)}, u32[]{:S(2)}) collective-permute-start(bf16[384,1536]{1,0:T(8,128)(2,1)S(1)} %collective-permute-done.11.refs_10_), channel_id=1, source_target_pairs={{0,32},{1,33},{2,34},{3,35},{4,36},{5,37},{6,38},{7,39},{8,40},{9,... | collective-permute-start | bytes 3538952 | tf_op jit(solution)/shard_map/ppermute | solution.py:57
  197.1 7.7 %collective-permute-done.18.refs_1_ = bf16[128,1536]{1,0:T(8,128)(2,1)S(1)} collective-permute-done((bf16[128,1536]{1,0:T(8,128)(2,1)}, bf16[128,1536]{1,0:T(8,128)(2,1)S(1)}, u32[]{:S(2)}, u32[]{:S(2)}) %collective-permute-start.18) | collective-permute-done | bytes 393248 | tf_op jit(solution)/shard_map/ppermute | solution.py:57
  204.9 4.9 %collective-permute-done.20.refs_3_ = bf16[128,1536]{1,0:T(8,128)(2,1)S(1)} collective-permute-done((bf16[128,1536]{1,0:T(8,128)(2,1)}, bf16[128,1536]{1,0:T(8,128)(2,1)S(1)}, u32[]{:S(2)}, u32[]{:S(2)}) %collective-permute-start.20) | collective-permute-done | bytes 393248 | tf_op jit(solution)/shard_map/ppermute | solution.py:57
  211.9 16.9 %project.1 = bf16[4,16,16,3072]{3,2,1,0:T(8,128)(2,1)} custom-call(s32[4]{0:T(128)} %get-tuple-element.72.meta, s32[4]{0:T(128)} %get-tuple-element.73.places, bf16[128,1536]{1,0:T(8,128)(2,1)} %get-tuple-element.109.refs_0_, bf16[128,1536]{1,0:T(8,128)(2,1)} %copy-done.19, bf16[128,1536]{1,0:T(8,128)(2,1)} %copy-done.20, bf16[128,1536]{1,0:T(8,128)(2,1)} %copy-done.21, ...), custom_call_target="tpu_custom_call" | custom-call | flops 9663676416 | bytes 26214400 | tf_op jit(solution)/shard_map/project/pallas_call | solution.py:269
  (78 shorter events, 8.4 us)
Async XLA Ops:
  6.5 126.4 %all-gather.2.cloned.1.call-start = ((), (), s32[]{:S(2)}) async-start(), calls=%async_computation | async-start | bytes 1253376 | tf_op jit(solution)/shard_map/all_gather | solution.py:299
  11.6 23.4 %collective-permute-start.3 = (bf16[3,128,1536]{2,1,0:T(8,128)(2,1)}, bf16[3,128,1536]{2,1,0:T(8,128)(2,1)S(1)}, u32[]{:S(2)}, u32[]{:S(2)}) collective-permute-start(bf16[3,128,1536]{2,1,0:T(8,128)(2,1)} %bitcast.49), channel_id=1, source_target_pairs={{0,28},{1,29},{2,30},{3,31},{4,0},{5,1},{6,2},{7,3},{8,4},{9,5},{1... | collective-permute-start | bytes 3538952 | tf_op jit(solution)/shard_map/ppermute | solution.py:57
  13.7 22.4 %collective-permute-start.4 = (bf16[3,128,1536]{2,1,0:T(8,128)(2,1)}, bf16[3,128,1536]{2,1,0:T(8,128)(2,1)}, u32[]{:S(2)}, u32[]{:S(2)}) collective-permute-start(bf16[3,128,1536]{2,1,0:T(8,128)(2,1)} %bitcast.48), channel_id=1, source_target_pairs={{0,3},{1,0},{2,1},{3,2},{4,7},{5,4},{6,5},{7,6},{8,11},{9,8},{10,9... | collective-permute-start | bytes 3538952 | tf_op jit(solution)/shard_map/ppermute | solution.py:57
  15.0 28.6 %collective-permute-start = (bf16[3,128,1536]{2,1,0:T(8,128)(2,1)}, bf16[3,128,1536]{2,1,0:T(8,128)(2,1)S(1)}, u32[]{:S(2)}, u32[]{:S(2)}) collective-permute-start(bf16[3,128,1536]{2,1,0:T(8,128)(2,1)} %bitcast.4), channel_id=1, source_target_pairs={{0,4},{1,5},{2,6},{3,7},{4,8},{5,9},{6,10},{7,11},{8,12},{9,13},{1... | collective-permute-start | bytes 3538952 | tf_op jit(solution)/shard_map/ppermute | solution.py:57
  17.7 28.3 %collective-permute-start.1 = (bf16[3,128,1536]{2,1,0:T(8,128)(2,1)}, bf16[3,128,1536]{2,1,0:T(8,128)(2,1)S(1)}, u32[]{:S(2)}, u32[]{:S(2)}) collective-permute-start(bf16[3,128,1536]{2,1,0:T(8,128)(2,1)} %bitcast.5), channel_id=1, source_target_pairs={{0,1},{1,2},{2,3},{3,0},{4,5},{5,6},{6,7},{7,4},{8,9},{9,10},{10,1... | collective-permute-start | bytes 3538952 | tf_op jit(solution)/shard_map/ppermute | solution.py:57
  48.6 84.3 %collective-permute-start.7 = (bf16[3,2,128,1536]{3,2,1,0:T(8,128)(2,1)S(1)}, bf16[3,2,128,1536]{3,2,1,0:T(8,128)(2,1)}, u32[]{:S(2)}, u32[]{:S(2)}) collective-permute-start(bf16[3,2,128,1536]{3,2,1,0:T(8,128)(2,1)S(1)} %pad_maximum_fusion.1), channel_id=1, source_target_pairs={{0,32},{1,33},{2,34},{3,35},{4,36},{5,37},{6,38},{7,39},{8,40},{9,... | collective-permute-start | bytes 7077896 | tf_op jit(solution)/shard_map/ppermute | solution.py:57
  56.3 76.7 %collective-permute-start.6 = (bf16[3,2,128,1536]{3,2,1,0:T(8,128)(2,1)}, bf16[3,2,128,1536]{3,2,1,0:T(8,128)(2,1)}, u32[]{:S(2)}, u32[]{:S(2)}) collective-permute-start(bf16[3,2,128,1536]{3,2,1,0:T(8,128)(2,1)} %pad_maximum_fusion), channel_id=1, source_target_pairs={{32,0},{33,1},{34,2},{35,3},{36,4},{37,5},{38,6},{39,7},{40,8},{41... | collective-permute-start | bytes 7077896 | tf_op jit(solution)/shard_map/ppermute | solution.py:57
  58.2 74.7 %collective-permute-start.2 = (bf16[3,128,1536]{2,1,0:T(8,128)(2,1)}, bf16[3,128,1536]{2,1,0:T(8,128)(2,1)S(1)}, u32[]{:S(2)}, u32[]{:S(2)}) collective-permute-start(bf16[3,128,1536]{2,1,0:T(8,128)(2,1)} %bitcast.47), channel_id=1, source_target_pairs={{0,5},{1,6},{2,7},{3,4},{4,9},{5,10},{6,11},{7,8},{8,13},{9,14},{1... | collective-permute-start | bytes 3538952 | tf_op jit(solution)/shard_map/ppermute | solution.py:57
  61.4 71.5 %collective-permute-start.5 = (bf16[3,128,1536]{2,1,0:T(8,128)(2,1)}, bf16[3,128,1536]{2,1,0:T(8,128)(2,1)}, u32[]{:S(2)}, u32[]{:S(2)}) collective-permute-start(bf16[3,128,1536]{2,1,0:T(8,128)(2,1)} %bitcast.46), channel_id=1, source_target_pairs={{0,31},{1,28},{2,29},{3,30},{4,3},{5,0},{6,1},{7,2},{8,7},{9,4},{1... | collective-permute-start | bytes 3538952 | tf_op jit(solution)/shard_map/ppermute | solution.py:57
  133.0 23.1 %collective-permute-start.8 = (bf16[384,1536]{1,0:T(8,128)(2,1)}, bf16[384,1536]{1,0:T(8,128)(2,1)S(1)}, u32[]{:S(2)}, u32[]{:S(2)}) collective-permute-start(bf16[384,1536]{1,0:T(8,128)(2,1)} %all-gather.2.cloned.1.call-done.refs_8_), channel_id=1, source_target_pairs={{0,4},{1,5},{2,6},{3,7},{4,8},{5,9},{6,10},{7,11},{8,12},{9,13},{1... | collective-permute-start | bytes 3538952 | tf_op jit(solution)/shard_map/ppermute | solution.py:57
  135.5 20.6 %copy-start.6 = (bf16[384,1536]{1,0:T(8,128)(2,1)S(1)}, bf16[384,1536]{1,0:T(8,128)(2,1)}, u32[]{:S(2)}) copy-start(bf16[384,1536]{1,0:T(8,128)(2,1)} %all-gather.2.cloned.1.call-done.refs_8_) | copy-start | bytes 3538948
  136.8 13.3 %collective-permute-start.10 = (bf16[2,128,1536]{2,1,0:T(8,128)(2,1)S(1)}, bf16[2,128,1536]{2,1,0:T(8,128)(2,1)S(1)}, u32[]{:S(2)}, u32[]{:S(2)}) collective-permute-start(bf16[2,128,1536]{2,1,0:T(8,128)(2,1)S(1)} %slice.23), channel_id=1, source_target_pairs={{0,32},{1,33},{2,34},{3,35},{4,36},{5,37},{6,38},{7,39},{8,40},{9,... | collective-permute-start | bytes 2359304 | tf_op jit(solution)/shard_map/ppermute | solution.py:57
  141.2 14.8 %collective-permute-start.9 = (bf16[2,128,1536]{2,1,0:T(8,128)(2,1)S(1)}, bf16[2,128,1536]{2,1,0:T(8,128)(2,1)S(1)}, u32[]{:S(2)}, u32[]{:S(2)}) collective-permute-start(bf16[2,128,1536]{2,1,0:T(8,128)(2,1)S(1)} %slice.22), channel_id=1, source_target_pairs={{32,0},{33,1},{34,2},{35,3},{36,4},{37,5},{38,6},{39,7},{40,8},{41... | collective-permute-start | bytes 2359304 | tf_op jit(solution)/shard_map/ppermute | solution.py:57
  156.0 15.7 %collective-permute-start.14 = (bf16[384,1536]{1,0:T(8,128)(2,1)S(1)}, bf16[384,1536]{1,0:T(8,128)(2,1)S(1)}, u32[]{:S(2)}, u32[]{:S(2)}) collective-permute-start(bf16[384,1536]{1,0:T(8,128)(2,1)S(1)} %collective-permute-done.8.refs_9_), channel_id=1, source_target_pairs={{0,32},{1,33},{2,34},{3,35},{4,36},{5,37},{6,38},{7,39},{8,40},{9,... | collective-permute-start | bytes 3538952 | tf_op jit(solution)/shard_map/ppermute | solution.py:57
  156.1 15.6 %collective-permute-start.13 = (bf16[384,1536]{1,0:T(8,128)(2,1)S(1)}, bf16[384,1536]{1,0:T(8,128)(2,1)S(1)}, u32[]{:S(2)}, u32[]{:S(2)}) collective-permute-start(bf16[384,1536]{1,0:T(8,128)(2,1)S(1)} %copy-done.6), channel_id=1, source_target_pairs={{0,32},{1,33},{2,34},{3,35},{4,36},{5,37},{6,38},{7,39},{8,40},{9,... | collective-permute-start | bytes 3538952 | tf_op jit(solution)/shard_map/ppermute | solution.py:57
  156.6 33.2 %collective-permute-start.11 = (bf16[384,1536]{1,0:T(8,128)(2,1)S(1)}, bf16[384,1536]{1,0:T(8,128)(2,1)S(1)}, u32[]{:S(2)}, u32[]{:S(2)}) collective-permute-start(bf16[384,1536]{1,0:T(8,128)(2,1)S(1)} %collective-permute-done.8.refs_9_), channel_id=1, source_target_pairs={{0,4},{1,5},{2,6},{3,7},{4,8},{5,9},{6,10},{7,11},{8,12},{9,13},{1... | collective-permute-start | bytes 3538952 | tf_op jit(solution)/shard_map/ppermute | solution.py:57
  158.1 31.7 %collective-permute-start.12 = (bf16[384,1536]{1,0:T(8,128)(2,1)S(1)}, bf16[384,1536]{1,0:T(8,128)(2,1)S(1)}, u32[]{:S(2)}, u32[]{:S(2)}) collective-permute-start(bf16[384,1536]{1,0:T(8,128)(2,1)S(1)} %copy-done.6), channel_id=1, source_target_pairs={{0,12},{1,13},{2,14},{3,15},{4,0},{5,1},{6,2},{7,3},{8,4},{9,5},{1... | collective-permute-start | bytes 3538952 | tf_op jit(solution)/shard_map/ppermute | solution.py:57
  171.7 18.1 %copy-start.8 = (bf16[384,1536]{1,0:T(8,128)(2,1)}, bf16[384,1536]{1,0:T(8,128)(2,1)S(1)}, u32[]{:S(2)}) copy-start(bf16[384,1536]{1,0:T(8,128)(2,1)S(1)} %collective-permute-done.14.refs_13_) | copy-start | bytes 3538948
  171.8 18.1 %copy-start.9 = (bf16[384,1536]{1,0:T(8,128)(2,1)}, bf16[384,1536]{1,0:T(8,128)(2,1)S(1)}, u32[]{:S(2)}) copy-start(bf16[384,1536]{1,0:T(8,128)(2,1)S(1)} %collective-permute-done.13.refs_12_) | copy-start | bytes 3538948
  171.8 18.1 %collective-permute-start.15 = (bf16[128,1536]{1,0:T(8,128)(2,1)}, bf16[128,1536]{1,0:T(8,128)(2,1)S(1)}, u32[]{:S(2)}, u32[]{:S(2)}) collective-permute-start(bf16[128,1536]{1,0:T(8,128)(2,1)} %get-tuple-element.98), channel_id=1, source_target_pairs={{28,0},{29,1},{30,2},{31,3},{0,4},{1,5},{2,6},{3,7},{4,8},{5,9},{6... | collective-permute-start | bytes 1179656 | tf_op jit(solution)/shard_map/ppermute | solution.py:57
  174.9 15.0 %collective-permute-start.16 = (bf16[128,1536]{1,0:T(8,128)(2,1)}, bf16[128,1536]{1,0:T(8,128)(2,1)S(1)}, u32[]{:S(2)}, u32[]{:S(2)}) collective-permute-start(bf16[128,1536]{1,0:T(8,128)(2,1)} %get-tuple-element.99), channel_id=1, source_target_pairs={{3,0},{0,1},{1,2},{2,3},{7,4},{4,5},{5,6},{6,7},{11,8},{8,9},{9,10... | collective-permute-start | bytes 1179656 | tf_op jit(solution)/shard_map/ppermute | solution.py:57
  175.5 17.3 %collective-permute-start.17 = (bf16[128,1536]{1,0:T(8,128)(2,1)}, bf16[128,1536]{1,0:T(8,128)(2,1)S(1)}, u32[]{:S(2)}, u32[]{:S(2)}) collective-permute-start(bf16[128,1536]{1,0:T(8,128)(2,1)} %get-tuple-element.100), channel_id=1, source_target_pairs={{31,0},{28,1},{29,2},{30,3},{3,4},{0,5},{1,6},{2,7},{7,8},{4,9},{5... | collective-permute-start | bytes 1179656 | tf_op jit(solution)/shard_map/ppermute | solution.py:57
  189.8 19.9 %copy-start.10 = (bf16[384,1536]{1,0:T(8,128)(2,1)}, bf16[384,1536]{1,0:T(8,128)(2,1)S(1)}, u32[]{:S(2)}) copy-start(bf16[384,1536]{1,0:T(8,128)(2,1)S(1)} %collective-permute-done.11.refs_10_) | copy-start | bytes 3538948
  189.9 19.9 %copy-start.11 = (bf16[384,1536]{1,0:T(8,128)(2,1)}, bf16[384,1536]{1,0:T(8,128)(2,1)S(1)}, u32[]{:S(2)}) copy-start(bf16[384,1536]{1,0:T(8,128)(2,1)S(1)} %collective-permute-done.12.refs_11_) | copy-start | bytes 3538948
  189.9 19.9 %copy-start.16 = (bf16[128,1536]{1,0:T(8,128)(2,1)}, bf16[128,1536]{1,0:T(8,128)(2,1)S(1)}, u32[]{:S(2)}) copy-start(bf16[128,1536]{1,0:T(8,128)(2,1)S(1)} %collective-permute-done.15.refs_5_) | copy-start | bytes 1179652
  189.9 19.9 %copy-start.17 = (bf16[128,1536]{1,0:T(8,128)(2,1)}, bf16[128,1536]{1,0:T(8,128)(2,1)S(1)}, u32[]{:S(2)}) copy-start(bf16[128,1536]{1,0:T(8,128)(2,1)S(1)} %collective-permute-done.16.refs_6_) | copy-start | bytes 1179652
  192.8 17.0 %copy-start.18 = (bf16[128,1536]{1,0:T(8,128)(2,1)}, bf16[128,1536]{1,0:T(8,128)(2,1)S(1)}, u32[]{:S(2)}) copy-start(bf16[128,1536]{1,0:T(8,128)(2,1)S(1)} %collective-permute-done.17.refs_7_) | copy-start | bytes 1179652
  192.8 16.9 %collective-permute-start.21 = (bf16[384,1536]{1,0:T(8,128)(2,1)S(1)}, bf16[384,1536]{1,0:T(8,128)(2,1)S(1)}, u32[]{:S(2)}, u32[]{:S(2)}) collective-permute-start(bf16[384,1536]{1,0:T(8,128)(2,1)S(1)} %collective-permute-done.11.refs_10_), channel_id=1, source_target_pairs={{0,32},{1,33},{2,34},{3,35},{4,36},{5,37},{6,38},{7,39},{8,40},{9,... | collective-permute-start | bytes 3538952 | tf_op jit(solution)/shard_map/ppermute | solution.py:57
  195.9 13.8 %collective-permute-start.22 = (bf16[384,1536]{1,0:T(8,128)(2,1)S(1)}, bf16[384,1536]{1,0:T(8,128)(2,1)S(1)}, u32[]{:S(2)}, u32[]{:S(2)}) collective-permute-start(bf16[384,1536]{1,0:T(8,128)(2,1)S(1)} %collective-permute-done.12.refs_11_), channel_id=1, source_target_pairs={{0,32},{1,33},{2,34},{3,35},{4,36},{5,37},{6,38},{7,39},{8,40},{9,... | collective-permute-start | bytes 3538952 | tf_op jit(solution)/shard_map/ppermute | solution.py:57
  195.9 8.9 %collective-permute-start.18 = (bf16[128,1536]{1,0:T(8,128)(2,1)}, bf16[128,1536]{1,0:T(8,128)(2,1)S(1)}, u32[]{:S(2)}, u32[]{:S(2)}) collective-permute-start(bf16[128,1536]{1,0:T(8,128)(2,1)} %get-tuple-element.110), channel_id=1, source_target_pairs={{4,0},{5,1},{6,2},{7,3},{8,4},{9,5},{10,6},{11,7},{12,8},{13,9},{1... | collective-permute-start | bytes 1179656 | tf_op jit(solution)/shard_map/ppermute | solution.py:57
  196.0 8.9 %collective-permute-start.19 = (bf16[128,1536]{1,0:T(8,128)(2,1)}, bf16[128,1536]{1,0:T(8,128)(2,1)S(1)}, u32[]{:S(2)}, u32[]{:S(2)}) collective-permute-start(bf16[128,1536]{1,0:T(8,128)(2,1)} %get-tuple-element.111), channel_id=1, source_target_pairs={{1,0},{2,1},{3,2},{0,3},{5,4},{6,5},{7,6},{4,7},{9,8},{10,9},{11,1... | collective-permute-start | bytes 1179656 | tf_op jit(solution)/shard_map/ppermute | solution.py:57
  196.8 12.9 %collective-permute-start.20 = (bf16[128,1536]{1,0:T(8,128)(2,1)}, bf16[128,1536]{1,0:T(8,128)(2,1)S(1)}, u32[]{:S(2)}, u32[]{:S(2)}) collective-permute-start(bf16[128,1536]{1,0:T(8,128)(2,1)} %get-tuple-element.112), channel_id=1, source_target_pairs={{5,0},{6,1},{7,2},{4,3},{9,4},{10,5},{11,6},{8,7},{13,8},{14,9},{1... | collective-permute-start | bytes 1179656 | tf_op jit(solution)/shard_map/ppermute | solution.py:57
  (15 other events, 69.2 us)
Sparse Core Ops, SparseCore 0:
  58.3 74.5 all-gather.1

commit v9 on v8

--- a/solution.py
+++ b/solution.py
@@ -45,11 +45,13 @@
     return [(index(f, r, c), index(f ^ 1, r, c)) for f, r, c in every()]
 
 
-def turn_pairs(step):
+def shift_pairs(dx=0, dy=0, dz=0, opposed=False):
     pairs = []
     for f, r, c in every():
-        zlo, x = divmod(r, 4)
-        pairs.append((index(f, r, c), index(f, zlo * 4 + (x + step * (1 - 2 * (f % 2))) % 4, c)))
+        (zhi, core), (zlo, x) = divmod(f, 2), divmod(r, 4)
+        way = -1 if opposed and core else 1
+        z = (2 * zhi + zlo + way * dz) % 4
+        pairs.append((index(f, r, c), index((z // 2) * 2 + core, (z % 2) * 4 + (x + way * dx) % 4, c + way * dy)))
     return pairs
 
 
@@ -276,12 +278,9 @@
     )(meta, places, *attended, *chunks, tokens)
 
 
-def strip_groups():
-    return [
-        [index(2 * zhi + core, zlo * 4 + x, c) for zhi in range(2) for zlo in range(2) for c in range(C)]
-        for core in range(2)
-        for x in range(4)
-    ]
+def ring_order(own, first, second, third, place):
+    row = jnp.stack([third, second, first, own, third, second, first])
+    return lax.dynamic_slice_in_dim(row, 3 - place, 4, axis=0)
 
 
 def together(*values):
@@ -296,32 +295,35 @@
     places = jnp.stack([core, 2 + core, 1 - core, 3 - core]).astype(jnp.int32)
     split = lambda a: a.reshape(4, 2, 8, 2, 8, HD)
     arrays = (split(key_rows), split(value_rows), split(queries))
-    chunk = lax.all_gather(out_weight.T, AXES, axis=0, tiled=True, axis_index_groups=strip_groups())
+    shard = out_weight.T
 
     row, col, both = MOVES[1:]
     go = lambda value, half, move: send(value, window_pairs(half, *move))
     up = lambda value: send(value, frame_pairs(1))
     down = lambda value: send(value, frame_pairs(-1))
     swap = lambda value: send(value, core_pairs())
-    turn = lambda value, step=1: send(value, turn_pairs(step))
+    turn = lambda value, step=1: send(value, shift_pairs(dx=step, opposed=True))
     back = lambda half, mixed: [mixed[0]] + [send(mixed[n], window_pairs(half, *MOVES[n], back=True)) for n in (1, 2, 3)]
 
     x0, y0 = pack(((0, 1, "kvq"), (0, 2, "kvq")), frame, *arrays)
-    x0, y0, frame = together(x0, y0, frame)
+    x0, y0, frame, shard = together(x0, y0, frame, shard)
     x0, y0 = go(x0, 0, row), go(y0, 0, col)
+    shards = [send(shard, shift_pairs(dz=n)) for n in (1, 2, 3)]
     x1, y1 = pack(((1, 1, "kvq"), (1, 2, "kvq")), frame, *arrays)
-    x1, y1, frame = together(x1, y1, frame)
+    x1, y1, frame, *shards = together(x1, y1, frame, *shards)
     x1, y1 = go(x1, 1, row), go(y1, 1, col)
     skv0, skv1, d0, d1, sq0, sq1 = pack(
         ((0, 0, "kv"), (1, 0, "kv"), (0, 3, "kvq"), (1, 3, "kvq"), (0, 0, "q"), (1, 0, "q")), frame, *arrays
     )
-    d0, x0, y0, meta, places = together(d0, x0, y0, meta, places)
-    d1, x1, y1 = together(d1, x1, y1)
-    d0, d1 = go(d0, 0, both), go(d1, 1, both)
-    down3, up3 = down(jnp.stack([skv0, x0[:2], y0[:2]])), up(jnp.stack([skv1, x1[:2], y1[:2]]))
-    c0, d0, d1, down3, up3 = together(chunk, d0, d1, down3, up3)
+    strip = ring_order(shard, *shards, (f >> 1) * 2 + (r >> 2))
+    strips = [send(strip, shift_pairs(dy=n)) for n in (1, 2, 3)]
+    h0, h1 = jnp.stack([skv0, x0[:2], y0[:2]]), jnp.stack([skv1, x1[:2], y1[:2]])
+    d0, d1, h0, h1, x0, y0, x1, y1, meta, places, *strips = together(d0, d1, h0, h1, x0, y0, x1, y1, meta, places, *strips)
+    d0, d1, down3, up3 = go(d0, 0, both), go(d1, 1, both), down(h0), up(h1)
+    c0 = ring_order(strip, *strips, c).swapaxes(0, 1).reshape(384, HD)
+    c0, d0, d1 = together(c0, d0, d1)
     downd, upd, c1 = down(d0[:2]), up(d1[:2]), turn(c0)
-    c0, c1, downd, upd = together(c0, c1, downd, upd)
+    c0, c1, downd, upd, down3, up3 = together(c0, c1, downd, upd, down3, up3)
 
     c2, c3, s0, s1 = turn(c1), turn(c0, -1), swap(c0), swap(c1)
     mixed1 = attend(1, meta, skv1, sq1, x1, y1, d1, down3, downd)

time: 236 us -> 196 us (0.83)
  waiting for transfers between devices: 120 us -> 92.6 us
  between operations: 13.8 us -> 0.68 us
  starting transfers between devices: 38.4 us -> 40.9 us
    all_gather x1 -> x0, waiting for transfers between devices: 71.5 us -> none  [local(): lax.all_gather(out_weight.T, AXES, axis=0, tiled=True, axis_index_groups=...]
    ppermute x23 -> x29, waiting for transfers between devices: 48.9 us -> 92.6 us  [send(): return lax.ppermute(value, AXES, pairs)]
    ppermute x23 -> x29, starting transfers between devices: 38.4 us -> 40.9 us  [send(): return lax.ppermute(value, AXES, pairs)]
    unnamed x46 -> x64, local copies, waits for them, and re-layouts: 3.11 us -> 4.8 us
  transfers between devices with their start and end apart: 24 -> 29, of which waited for: 10 -> 11; matrix products, arithmetic and copies ran while one was open for 2% -> 2% of each run, Pallas kernels for 13% -> 17%
where the time goes in v9:
time: 196 us
  waiting for transfers between devices  92.6 us (47%)
  Pallas kernels  53.6 us (27%)
  starting transfers between devices  40.9 us (21%)
  local copies, waits for them, and re-layouts  5.36 us (3%)
  other arithmetic  2.46 us (1%)
    ppermute x29, waiting for transfers between devices, send(): return lax.ppermute(value, AXES, pairs)  92.6 us
    ppermute x29, starting transfers between devices, send(): return lax.ppermute(value, AXES, pairs)  40.9 us
    pallas_call x2, Pallas kernels, attend(): pl.pallas_call(functools.partial(attend_kernel, half), grid=(H // STEP,),...  27.2 us
    pallas_call x1, Pallas kernels, project(): pl.pallas_call(project_kernel, grid_spec=grid_spec, out_shape=jax.ShapeDt...  16.9 us
    pallas_call x3, Pallas kernels, pack(): pl.pallas_call(functools.partial(pack_kernel, parts), out_shape=[jax.Shap...  9.49 us
    unnamed x64, local copies, waits for them, and re-layouts  4.8 us
  transfers between devices with their start and end apart: 29, of which 11 were waited for; matrix products, arithmetic and copies ran while one was open for 2% of the time, Pallas kernels for 17%

profile of v9, /device:TPU:1, one launch (start us, length us, event | category | flops | bytes accessed | tf_op | source)
XLA Modules:
  0.0 195.6 jit_solution(16571084822858090616)
XLA Ops:
  0.0 2.6 %pack.3 = (bf16[3,2,8,8,1536]{4,3,2,1,0:T(8,128)(2,1)}, bf16[3,2,8,8,1536]{4,3,2,1,0:T(8,128)(2,1)}) custom-call(s32[1]{0:T(128)} %bitcast.meta, bf16[4,2,8,2,8,1536]{5,4,3,2,1,0:T(8,128)(2,1)} %bitcast.57, bf16[4,2,8,2,8,1536]{5,4,3,2,1,0:T(8,128)(2,1)} %bitcast.60, bf16[4,2,8,2,8,1536]{5,4,3,2,1,0:T(8,128)(2,1)} %bitcast.63), custom_call_target="tpu_custom_call" | custom-call | bytes 6291456 | tf_op jit(solution)/shard_map/pack/pallas_call | solution.py:98
  2.6 4.7 %collective-permute-start.2 = (bf16[24,1536]{1,0:T(8,128)(2,1)S(1)}, bf16[24,1536]{1,0:T(8,128)(2,1)S(1)}, u32[]{:S(2)}, u32[]{:S(2)}) collective-permute-start(bf16[24,1536]{1,0:T(8,128)(2,1)S(1)} %bitcast.74), channel_id=1, source_target_pairs={{0,80},{1,81},{2,82},{3,83},{4,84},{5,85},{6,86},{7,87},{8,88},{9,... | collective-permute-start | bytes 221192 | tf_op jit(solution)/shard_map/ppermute | solution.py:59
  8.0 4.1 %collective-permute-start.3 = (bf16[3,128,1536]{2,1,0:T(8,128)(2,1)}, bf16[3,128,1536]{2,1,0:T(8,128)(2,1)S(1)}, u32[]{:S(2)}, u32[]{:S(2)}) collective-permute-start(bf16[3,128,1536]{2,1,0:T(8,128)(2,1)} %bitcast.79), channel_id=1, source_target_pairs={{0,4},{1,5},{2,6},{3,7},{4,8},{5,9},{6,10},{7,11},{8,12},{9,13},{1... | collective-permute-start | bytes 3538952 | tf_op jit(solution)/shard_map/ppermute | solution.py:59
  12.1 2.7 %collective-permute-start.4 = (bf16[3,128,1536]{2,1,0:T(8,128)(2,1)}, bf16[3,128,1536]{2,1,0:T(8,128)(2,1)S(1)}, u32[]{:S(2)}, u32[]{:S(2)}) collective-permute-start(bf16[3,128,1536]{2,1,0:T(8,128)(2,1)} %bitcast.78), channel_id=1, source_target_pairs={{0,1},{1,2},{2,3},{3,0},{4,5},{5,6},{6,7},{7,4},{8,9},{9,10},{10,1... | collective-permute-start | bytes 3538952 | tf_op jit(solution)/shard_map/ppermute | solution.py:59
  15.5 2.6 %pack.4 = (bf16[3,2,8,8,1536]{4,3,2,1,0:T(8,128)(2,1)}, bf16[3,2,8,8,1536]{4,3,2,1,0:T(8,128)(2,1)}) custom-call(s32[1]{0:T(128)} %bitcast.meta, bf16[4,2,8,2,8,1536]{5,4,3,2,1,0:T(8,128)(2,1)} %bitcast.58, bf16[4,2,8,2,8,1536]{5,4,3,2,1,0:T(8,128)(2,1)} %bitcast.61, bf16[4,2,8,2,8,1536]{5,4,3,2,1,0:T(8,128)(2,1)} %bitcast.64), custom_call_target="tpu_custom_call" | custom-call | bytes 6291456 | tf_op jit(solution)/shard_map/pack/pallas_call | solution.py:98
  18.1 1.3 pad_add_fusion
  20.1 0.9 collective-permute-start.7
  21.1 4.3 %pack.5 = (bf16[2,2,8,8,1536]{4,3,2,1,0:T(8,128)(2,1)}, bf16[2,2,8,8,1536]{4,3,2,1,0:T(8,128)(2,1)}, bf16[3,2,8,8,1536]{4,3,2,1,0:T(8,128)(2,1)}, bf16[3,2,8,8,1...) custom-call(s32[1]{0:T(128)} %bitcast.meta, ...), custom_call_target="tpu_custom_call" | custom-call | bytes 12582912 | tf_op jit(solution)/shard_map/pack/pallas_call | solution.py:98
  25.6 9.0 %collective-permute-done.4.y = bf16[3,128,1536]{2,1,0:T(8,128)(2,1)S(1)} collective-permute-done((bf16[3,128,1536]{2,1,0:T(8,128)(2,1)}, bf16[3,128,1536]{2,1,0:T(8,128)(2,1)S(1)}, u32[]{:S(2)}, u32[]{:S(2)}) %collective-permute-start.4) | collective-permute-done | bytes 1179680 | tf_op jit(solution)/shard_map/ppermute | solution.py:59
  35.7 7.6 %collective-permute-done.5.x = bf16[3,128,1536]{2,1,0:T(8,128)(2,1)S(1)} collective-permute-done((bf16[3,128,1536]{2,1,0:T(8,128)(2,1)}, bf16[3,128,1536]{2,1,0:T(8,128)(2,1)S(1)}, u32[]{:S(2)}, u32[]{:S(2)}) %collective-permute-start.5) | collective-permute-done | bytes 1179680 | tf_op jit(solution)/shard_map/ppermute | solution.py:59
  43.3 9.8 %collective-permute-done.6.y = bf16[3,128,1536]{2,1,0:T(8,128)(2,1)S(1)} collective-permute-done((bf16[3,128,1536]{2,1,0:T(8,128)(2,1)}, bf16[3,128,1536]{2,1,0:T(8,128)(2,1)S(1)}, u32[]{:S(2)}, u32[]{:S(2)}) %collective-permute-start.6) | collective-permute-done | bytes 1179680 | tf_op jit(solution)/shard_map/ppermute | solution.py:59
  54.9 4.0 %collective-permute-start.10 = (bf16[3,128,1536]{2,1,0:T(8,128)(2,1)S(1)}, bf16[3,128,1536]{2,1,0:T(8,128)(2,1)S(1)}, u32[]{:S(2)}, u32[]{:S(2)}) collective-permute-start(bf16[3,128,1536]{2,1,0:T(8,128)(2,1)S(1)} %bitcast.82), channel_id=1, source_target_pairs={{0,5},{1,6},{2,7},{3,4},{4,9},{5,10},{6,11},{7,8},{8,13},{9,14},{1... | collective-permute-start | bytes 3538952 | tf_op jit(solution)/shard_map/ppermute | solution.py:59
  59.0 5.0 %collective-permute-start.15 = (bf16[3,2,128,1536]{3,2,1,0:T(8,128)(2,1)S(1)}, bf16[3,2,128,1536]{3,2,1,0:T(8,128)(2,1)S(1)}, u32[]{:S(2)}, u32[]{:S(2)}) collective-permute-start(bf16[3,2,128,1536]{3,2,1,0:T(8,128)(2,1)S(1)} %pad_maximum_fusion), channel_id=1, source_target_pairs={{32,0},{33,1},{34,2},{35,3},{36,4},{37,5},{38,6},{39,7},{40,8},{41... | collective-permute-start | bytes 7077896 | tf_op jit(solution)/shard_map/ppermute | solution.py:59
  64.0 3.0 %collective-permute-start.16 = (bf16[3,2,128,1536]{3,2,1,0:T(8,128)(2,1)S(1)}, bf16[3,2,128,1536]{3,2,1,0:T(8,128)(2,1)S(1)}, u32[]{:S(2)}, u32[]{:S(2)}) collective-permute-start(bf16[3,2,128,1536]{3,2,1,0:T(8,128)(2,1)S(1)} %pad_maximum_fusion.1), channel_id=1, source_target_pairs={{0,32},{1,33},{2,34},{3,35},{4,36},{5,37},{6,38},{7,39},{8,40},{9,... | collective-permute-start | bytes 7077896 | tf_op jit(solution)/shard_map/ppermute | solution.py:59
  67.3 14.0 %collective-permute-done.10.d = bf16[3,128,1536]{2,1,0:T(8,128)(2,1)S(1)} collective-permute-done((bf16[3,128,1536]{2,1,0:T(8,128)(2,1)S(1)}, bf16[3,128,1536]{2,1,0:T(8,128)(2,1)S(1)}, u32[]{:S(2)}, u32[]{:S(2)}) %collective-permute-start.10) | collective-permute-done | bytes 1179680 | tf_op jit(solution)/shard_map/ppermute | solution.py:59
  81.3 6.8 %collective-permute-done.11.d = bf16[3,128,1536]{2,1,0:T(8,128)(2,1)S(1)} collective-permute-done((bf16[3,128,1536]{2,1,0:T(8,128)(2,1)S(1)}, bf16[3,128,1536]{2,1,0:T(8,128)(2,1)S(1)}, u32[]{:S(2)}, u32[]{:S(2)}) %collective-permute-start.11) | collective-permute-done | bytes 1179680 | tf_op jit(solution)/shard_map/ppermute | solution.py:59
  88.5 1.9 collective-permute-start.14
  90.4 2.5 %collective-permute-start.13 = (bf16[2,128,1536]{2,1,0:T(8,128)(2,1)S(1)}, bf16[2,128,1536]{2,1,0:T(8,128)(2,1)S(1)}, u32[]{:S(2)}, u32[]{:S(2)}) collective-permute-start(bf16[2,128,1536]{2,1,0:T(8,128)(2,1)S(1)} %slice.22), channel_id=1, source_target_pairs={{32,0},{33,1},{34,2},{35,3},{36,4},{37,5},{38,6},{39,7},{40,8},{41... | collective-permute-start | bytes 2359304 | tf_op jit(solution)/shard_map/ppermute | solution.py:59
  92.9 26.6 %collective-permute-done.14.hd = bf16[2,128,1536]{2,1,0:T(8,128)(2,1)S(1)} collective-permute-done((bf16[2,128,1536]{2,1,0:T(8,128)(2,1)S(1)}, bf16[2,128,1536]{2,1,0:T(8,128)(2,1)S(1)}, u32[]{:S(2)}, u32[]{:S(2)}) %collective-permute-start.14) | collective-permute-done | bytes 786464 | tf_op jit(solution)/shard_map/ppermute | solution.py:59
  119.5 2.6 %collective-permute-done.13.hd = bf16[2,128,1536]{2,1,0:T(8,128)(2,1)S(1)} collective-permute-done((bf16[2,128,1536]{2,1,0:T(8,128)(2,1)S(1)}, bf16[2,128,1536]{2,1,0:T(8,128)(2,1)S(1)}, u32[]{:S(2)}, u32[]{:S(2)}) %collective-permute-start.13) | collective-permute-done | bytes 786464 | tf_op jit(solution)/shard_map/ppermute | solution.py:59
  122.7 1.0 copy-done.11
  124.1 1.1 collective-permute-start.18
  125.2 13.6 %attend.2 = (bf16[128,1536]{1,0:T(8,128)(2,1)}, bf16[128,1536]{1,0:T(8,128)(2,1)}, bf16[128,1536]{1,0:T(8,128)(2,1)}, bf16[128,1536]{1,0:T(8,128)(2,1)}) custom-call(s32[4]{0:T(128)} %get-tuple-element.90.meta, bf16[2,128,1536]{2,1,0:T(8,128)(2,1)} %bitcast.72, bf16[1,128,1536]{2,1,0:T(8,128)(2,1)} %bitcast.84, bf16[3,128,1536]{2,1,0:T(8,128)(2,1)} %copy-done.5, ...), custom_call_target="tpu_custom_call" | custom-call | flops 6442450944 | bytes 10485760 | tf_op jit(solution)/shard_map/attend/pallas_call | solution.py:188
  138.9 1.8 collective-permute-start.21
  140.7 2.8 %collective-permute-start.22 = (bf16[128,1536]{1,0:T(8,128)(2,1)}, bf16[128,1536]{1,0:T(8,128)(2,1)S(1)}, u32[]{:S(2)}, u32[]{:S(2)}) collective-permute-start(bf16[128,1536]{1,0:T(8,128)(2,1)} %get-tuple-element.115), channel_id=1, source_target_pairs={{3,0},{0,1},{1,2},{2,3},{7,4},{4,5},{5,6},{6,7},{11,8},{8,9},{9,10... | collective-permute-start | bytes 1179656 | tf_op jit(solution)/shard_map/ppermute | solution.py:59
  143.5 13.6 %attend.3 = (bf16[128,1536]{1,0:T(8,128)(2,1)}, bf16[128,1536]{1,0:T(8,128)(2,1)}, bf16[128,1536]{1,0:T(8,128)(2,1)}, bf16[128,1536]{1,0:T(8,128)(2,1)}) custom-call(s32[4]{0:T(128)} %get-tuple-element.90.meta, bf16[2,128,1536]{2,1,0:T(8,128)(2,1)} %bitcast.70, bf16[1,128,1536]{2,1,0:T(8,128)(2,1)} %bitcast.83, bf16[3,128,1536]{2,1,0:T(8,128)(2,1)} %copy-done.3, ...), custom_call_target="tpu_custom_call" | custom-call | flops 6442450944 | bytes 10485760 | tf_op jit(solution)/shard_map/attend/pallas_call | solution.py:188
  157.2 2.8 %collective-permute-done.23.refs_7_ = bf16[128,1536]{1,0:T(8,128)(2,1)S(1)} collective-permute-done((bf16[128,1536]{1,0:T(8,128)(2,1)}, bf16[128,1536]{1,0:T(8,128)(2,1)S(1)}, u32[]{:S(2)}, u32[]{:S(2)}) %collective-permute-start.23) | collective-permute-done | bytes 393248 | tf_op jit(solution)/shard_map/ppermute | solution.py:59
  160.0 3.2 %collective-permute-start.27 = (bf16[384,1536]{1,0:T(8,128)(2,1)}, bf16[384,1536]{1,0:T(8,128)(2,1)S(1)}, u32[]{:S(2)}, u32[]{:S(2)}) collective-permute-start(bf16[384,1536]{1,0:T(8,128)(2,1)} %collective-permute-done.17.refs_10_), channel_id=1, source_target_pairs={{0,32},{1,33},{2,34},{3,35},{4,36},{5,37},{6,38},{7,39},{8,40},{9,... | collective-permute-start | bytes 3538952 | tf_op jit(solution)/shard_map/ppermute | solution.py:59
  163.2 8.9 %collective-permute-done.24.refs_1_ = bf16[128,1536]{1,0:T(8,128)(2,1)S(1)} collective-permute-done((bf16[128,1536]{1,0:T(8,128)(2,1)}, bf16[128,1536]{1,0:T(8,128)(2,1)S(1)}, u32[]{:S(2)}, u32[]{:S(2)}) %collective-permute-start.24) | collective-permute-done | bytes 393248 | tf_op jit(solution)/shard_map/ppermute | solution.py:59
  172.1 4.2 %collective-permute-done.26.refs_3_ = bf16[128,1536]{1,0:T(8,128)(2,1)S(1)} collective-permute-done((bf16[128,1536]{1,0:T(8,128)(2,1)}, bf16[128,1536]{1,0:T(8,128)(2,1)S(1)}, u32[]{:S(2)}, u32[]{:S(2)}) %collective-permute-start.26) | collective-permute-done | bytes 393248 | tf_op jit(solution)/shard_map/ppermute | solution.py:59
  177.5 1.0 copy-done.16
  178.5 16.9 %project.1 = bf16[4,16,16,3072]{3,2,1,0:T(8,128)(2,1)} custom-call(s32[4]{0:T(128)} %get-tuple-element.90.meta, s32[4]{0:T(128)} %get-tuple-element.91.places, bf16[128,1536]{1,0:T(8,128)(2,1)} %get-tuple-element.127.refs_0_, bf16[128,1536]{1,0:T(8,128)(2,1)} %copy-done.22, bf16[128,1536]{1,0:T(8,128)(2,1)} %copy-done.23, bf16[128,1536]{1,0:T(8,128)(2,1)} %copy-done.24, ...), custom_call_target="tpu_custom_call" | custom-call | flops 9663676416 | bytes 26214400 | tf_op jit(solution)/shard_map/project/pallas_call | solution.py:271
  (111 shorter events, 7.9 us)
Async XLA Ops:
  2.6 16.8 %collective-permute-start.2 = (bf16[24,1536]{1,0:T(8,128)(2,1)S(1)}, bf16[24,1536]{1,0:T(8,128)(2,1)S(1)}, u32[]{:S(2)}, u32[]{:S(2)}) collective-permute-start(bf16[24,1536]{1,0:T(8,128)(2,1)S(1)} %bitcast.74), channel_id=1, source_target_pairs={{0,80},{1,81},{2,82},{3,83},{4,84},{5,85},{6,86},{7,87},{8,88},{9,... | collective-permute-start | bytes 221192 | tf_op jit(solution)/shard_map/ppermute | solution.py:59
  7.3 12.1 %collective-permute-start.1 = (bf16[24,1536]{1,0:T(8,128)(2,1)S(1)}, bf16[24,1536]{1,0:T(8,128)(2,1)S(1)}, u32[]{:S(2)}, u32[]{:S(2)}) collective-permute-start(bf16[24,1536]{1,0:T(8,128)(2,1)S(1)} %bitcast.75), channel_id=1, source_target_pairs={{0,64},{1,65},{2,66},{3,67},{4,68},{5,69},{6,70},{7,71},{8,72},{9,... | collective-permute-start | bytes 221192 | tf_op jit(solution)/shard_map/ppermute | solution.py:59
  7.3 12.1 %collective-permute-start = (bf16[24,1536]{1,0:T(8,128)(2,1)S(1)}, bf16[24,1536]{1,0:T(8,128)(2,1)S(1)}, u32[]{:S(2)}, u32[]{:S(2)}) collective-permute-start(bf16[24,1536]{1,0:T(8,128)(2,1)S(1)} %bitcast.76), channel_id=1, source_target_pairs={{0,16},{1,17},{2,18},{3,19},{4,20},{5,21},{6,22},{7,23},{8,24},{9,... | collective-permute-start | bytes 221192 | tf_op jit(solution)/shard_map/ppermute | solution.py:59
  8.0 17.6 %collective-permute-start.3 = (bf16[3,128,1536]{2,1,0:T(8,128)(2,1)}, bf16[3,128,1536]{2,1,0:T(8,128)(2,1)S(1)}, u32[]{:S(2)}, u32[]{:S(2)}) collective-permute-start(bf16[3,128,1536]{2,1,0:T(8,128)(2,1)} %bitcast.79), channel_id=1, source_target_pairs={{0,4},{1,5},{2,6},{3,7},{4,8},{5,9},{6,10},{7,11},{8,12},{9,13},{1... | collective-permute-start | bytes 3538952 | tf_op jit(solution)/shard_map/ppermute | solution.py:59
  12.1 22.5 %collective-permute-start.4 = (bf16[3,128,1536]{2,1,0:T(8,128)(2,1)}, bf16[3,128,1536]{2,1,0:T(8,128)(2,1)S(1)}, u32[]{:S(2)}, u32[]{:S(2)}) collective-permute-start(bf16[3,128,1536]{2,1,0:T(8,128)(2,1)} %bitcast.78), channel_id=1, source_target_pairs={{0,1},{1,2},{2,3},{3,0},{4,5},{5,6},{6,7},{7,4},{8,9},{9,10},{10,1... | collective-permute-start | bytes 3538952 | tf_op jit(solution)/shard_map/ppermute | solution.py:59
  19.5 34.7 %collective-permute-start.9 = (bf16[4,24,1536]{2,1,0:T(8,128)(2,1)S(1)}, bf16[4,24,1536]{2,1,0:T(8,128)(2,1)S(1)}, u32[]{:S(2)}, u32[]{:S(2)}) collective-permute-start(bf16[4,24,1536]{2,1,0:T(8,128)(2,1)S(1)} %constant_dynamic-slice_fusion), channel_id=1, source_target_pairs={{0,3},{1,0},{2,1},{3,2},{4,7},{5,4},{6,5},{7,6},{8,11},{9,8},{10,9... | collective-permute-start | bytes 884744 | tf_op jit(solution)/shard_map/ppermute | solution.py:59
  20.1 34.1 %collective-permute-start.8 = (bf16[4,24,1536]{2,1,0:T(8,128)(2,1)S(1)}, bf16[4,24,1536]{2,1,0:T(8,128)(2,1)S(1)}, u32[]{:S(2)}, u32[]{:S(2)}) collective-permute-start(bf16[4,24,1536]{2,1,0:T(8,128)(2,1)S(1)} %constant_dynamic-slice_fusion), channel_id=1, source_target_pairs={{0,2},{1,3},{2,0},{3,1},{4,6},{5,7},{6,4},{7,5},{8,10},{9,11},{10,... | collective-permute-start | bytes 884744 | tf_op jit(solution)/shard_map/ppermute | solution.py:59
  20.1 34.1 %collective-permute-start.7 = (bf16[4,24,1536]{2,1,0:T(8,128)(2,1)S(1)}, bf16[4,24,1536]{2,1,0:T(8,128)(2,1)S(1)}, u32[]{:S(2)}, u32[]{:S(2)}) collective-permute-start(bf16[4,24,1536]{2,1,0:T(8,128)(2,1)S(1)} %constant_dynamic-slice_fusion), channel_id=1, source_target_pairs={{0,1},{1,2},{2,3},{3,0},{4,5},{5,6},{6,7},{7,4},{8,9},{9,10},{10,1... | collective-permute-start | bytes 884744 | tf_op jit(solution)/shard_map/ppermute | solution.py:59
  25.6 17.7 %collective-permute-start.5 = (bf16[3,128,1536]{2,1,0:T(8,128)(2,1)}, bf16[3,128,1536]{2,1,0:T(8,128)(2,1)S(1)}, u32[]{:S(2)}, u32[]{:S(2)}) collective-permute-start(bf16[3,128,1536]{2,1,0:T(8,128)(2,1)} %bitcast.7), channel_id=1, source_target_pairs={{0,28},{1,29},{2,30},{3,31},{4,0},{5,1},{6,2},{7,3},{8,4},{9,5},{1... | collective-permute-start | bytes 3538952 | tf_op jit(solution)/shard_map/ppermute | solution.py:59
  34.6 18.6 %collective-permute-start.6 = (bf16[3,128,1536]{2,1,0:T(8,128)(2,1)}, bf16[3,128,1536]{2,1,0:T(8,128)(2,1)S(1)}, u32[]{:S(2)}, u32[]{:S(2)}) collective-permute-start(bf16[3,128,1536]{2,1,0:T(8,128)(2,1)} %bitcast.81), channel_id=1, source_target_pairs={{0,3},{1,0},{2,1},{3,2},{4,7},{5,4},{6,5},{7,6},{8,11},{9,8},{10,9... | collective-permute-start | bytes 3538952 | tf_op jit(solution)/shard_map/ppermute | solution.py:59
  54.9 26.4 %collective-permute-start.10 = (bf16[3,128,1536]{2,1,0:T(8,128)(2,1)S(1)}, bf16[3,128,1536]{2,1,0:T(8,128)(2,1)S(1)}, u32[]{:S(2)}, u32[]{:S(2)}) collective-permute-start(bf16[3,128,1536]{2,1,0:T(8,128)(2,1)S(1)} %bitcast.82), channel_id=1, source_target_pairs={{0,5},{1,6},{2,7},{3,4},{4,9},{5,10},{6,11},{7,8},{8,13},{9,14},{1... | collective-permute-start | bytes 3538952 | tf_op jit(solution)/shard_map/ppermute | solution.py:59
  58.9 29.3 %collective-permute-start.11 = (bf16[3,128,1536]{2,1,0:T(8,128)(2,1)S(1)}, bf16[3,128,1536]{2,1,0:T(8,128)(2,1)S(1)}, u32[]{:S(2)}, u32[]{:S(2)}) collective-permute-start(bf16[3,128,1536]{2,1,0:T(8,128)(2,1)S(1)} %bitcast.80), channel_id=1, source_target_pairs={{0,31},{1,28},{2,29},{3,30},{4,3},{5,0},{6,1},{7,2},{8,7},{9,4},{1... | collective-permute-start | bytes 3538952 | tf_op jit(solution)/shard_map/ppermute | solution.py:59
  59.0 63.1 %collective-permute-start.15 = (bf16[3,2,128,1536]{3,2,1,0:T(8,128)(2,1)S(1)}, bf16[3,2,128,1536]{3,2,1,0:T(8,128)(2,1)S(1)}, u32[]{:S(2)}, u32[]{:S(2)}) collective-permute-start(bf16[3,2,128,1536]{3,2,1,0:T(8,128)(2,1)S(1)} %pad_maximum_fusion), channel_id=1, source_target_pairs={{32,0},{33,1},{34,2},{35,3},{36,4},{37,5},{38,6},{39,7},{40,8},{41... | collective-permute-start | bytes 7077896 | tf_op jit(solution)/shard_map/ppermute | solution.py:59
  64.0 58.1 %collective-permute-start.16 = (bf16[3,2,128,1536]{3,2,1,0:T(8,128)(2,1)S(1)}, bf16[3,2,128,1536]{3,2,1,0:T(8,128)(2,1)S(1)}, u32[]{:S(2)}, u32[]{:S(2)}) collective-permute-start(bf16[3,2,128,1536]{3,2,1,0:T(8,128)(2,1)S(1)} %pad_maximum_fusion.1), channel_id=1, source_target_pairs={{0,32},{1,33},{2,34},{3,35},{4,36},{5,37},{6,38},{7,39},{8,40},{9,... | collective-permute-start | bytes 7077896 | tf_op jit(solution)/shard_map/ppermute | solution.py:59
  67.3 71.5 %copy-start = (bf16[4,4,24,1536]{3,2,1,0:T(8,128)(2,1)}, bf16[4,4,24,1536]{3,2,1,0:T(8,128)(2,1)S(1)}, u32[]{:S(2)}) copy-start(bf16[4,4,24,1536]{3,2,1,0:T(8,128)(2,1)S(1)} %copy.7) | copy-start | bytes 3538948
  81.3 57.5 %copy-start.6 = (bf16[3,128,1536]{2,1,0:T(8,128)(2,1)}, bf16[3,128,1536]{2,1,0:T(8,128)(2,1)S(1)}, u32[]{:S(2)}) copy-start(bf16[3,128,1536]{2,1,0:T(8,128)(2,1)S(1)} %collective-permute-done.10.d) | copy-start | bytes 3538948
  88.2 37.0 %copy-start.8 = (bf16[3,128,1536]{2,1,0:T(8,128)(2,1)}, bf16[3,128,1536]{2,1,0:T(8,128)(2,1)S(1)}, u32[]{:S(2)}) copy-start(bf16[3,128,1536]{2,1,0:T(8,128)(2,1)S(1)} %collective-permute-done.11.d) | copy-start | bytes 3538948
  88.2 33.9 %collective-permute-start.12 = (bf16[384,1536]{1,0:T(8,128)(2,1)S(1)}, bf16[384,1536]{1,0:T(8,128)(2,1)S(1)}, u32[]{:S(2)}, u32[]{:S(2)}) collective-permute-start(bf16[384,1536]{1,0:T(8,128)(2,1)S(1)} %bitcast.66), channel_id=1, source_target_pairs={{0,4},{1,5},{2,6},{3,7},{4,8},{5,9},{6,10},{7,11},{8,12},{9,13},{1... | collective-permute-start | bytes 3538952 | tf_op jit(solution)/shard_map/ppermute | solution.py:59
  88.5 31.0 %collective-permute-start.14 = (bf16[2,128,1536]{2,1,0:T(8,128)(2,1)S(1)}, bf16[2,128,1536]{2,1,0:T(8,128)(2,1)S(1)}, u32[]{:S(2)}, u32[]{:S(2)}) collective-permute-start(bf16[2,128,1536]{2,1,0:T(8,128)(2,1)S(1)} %slice.23), channel_id=1, source_target_pairs={{0,32},{1,33},{2,34},{3,35},{4,36},{5,37},{6,38},{7,39},{8,40},{9,... | collective-permute-start | bytes 2359304 | tf_op jit(solution)/shard_map/ppermute | solution.py:59
  90.4 31.7 %collective-permute-start.13 = (bf16[2,128,1536]{2,1,0:T(8,128)(2,1)S(1)}, bf16[2,128,1536]{2,1,0:T(8,128)(2,1)S(1)}, u32[]{:S(2)}, u32[]{:S(2)}) collective-permute-start(bf16[2,128,1536]{2,1,0:T(8,128)(2,1)S(1)} %slice.22), channel_id=1, source_target_pairs={{32,0},{33,1},{34,2},{35,3},{36,4},{37,5},{38,6},{39,7},{40,8},{41... | collective-permute-start | bytes 2359304 | tf_op jit(solution)/shard_map/ppermute | solution.py:59
  122.1 16.7 %collective-permute-start.20 = (bf16[384,1536]{1,0:T(8,128)(2,1)S(1)}, bf16[384,1536]{1,0:T(8,128)(2,1)}, u32[]{:S(2)}, u32[]{:S(2)}) collective-permute-start(bf16[384,1536]{1,0:T(8,128)(2,1)S(1)} %collective-permute-done.12.refs_9_), channel_id=1, source_target_pairs={{0,32},{1,33},{2,34},{3,35},{4,36},{5,37},{6,38},{7,39},{8,40},{9,... | collective-permute-start | bytes 3538952 | tf_op jit(solution)/shard_map/ppermute | solution.py:59
  122.2 16.6 %collective-permute-start.19 = (bf16[384,1536]{1,0:T(8,128)(2,1)S(1)}, bf16[384,1536]{1,0:T(8,128)(2,1)}, u32[]{:S(2)}, u32[]{:S(2)}) collective-permute-start(bf16[384,1536]{1,0:T(8,128)(2,1)S(1)} %bitcast.67), channel_id=1, source_target_pairs={{0,32},{1,33},{2,34},{3,35},{4,36},{5,37},{6,38},{7,39},{8,40},{9,... | collective-permute-start | bytes 3538952 | tf_op jit(solution)/shard_map/ppermute | solution.py:59
  123.7 33.4 %collective-permute-start.17 = (bf16[384,1536]{1,0:T(8,128)(2,1)S(1)}, bf16[384,1536]{1,0:T(8,128)(2,1)}, u32[]{:S(2)}, u32[]{:S(2)}) collective-permute-start(bf16[384,1536]{1,0:T(8,128)(2,1)S(1)} %collective-permute-done.12.refs_9_), channel_id=1, source_target_pairs={{0,4},{1,5},{2,6},{3,7},{4,8},{5,9},{6,10},{7,11},{8,12},{9,13},{1... | collective-permute-start | bytes 3538952 | tf_op jit(solution)/shard_map/ppermute | solution.py:59
  124.1 33.0 %collective-permute-start.18 = (bf16[384,1536]{1,0:T(8,128)(2,1)S(1)}, bf16[384,1536]{1,0:T(8,128)(2,1)}, u32[]{:S(2)}, u32[]{:S(2)}) collective-permute-start(bf16[384,1536]{1,0:T(8,128)(2,1)S(1)} %bitcast.68), channel_id=1, source_target_pairs={{0,12},{1,13},{2,14},{3,15},{4,0},{5,1},{6,2},{7,3},{8,4},{9,5},{1... | collective-permute-start | bytes 3538952 | tf_op jit(solution)/shard_map/ppermute | solution.py:59
  138.9 18.3 %collective-permute-start.21 = (bf16[128,1536]{1,0:T(8,128)(2,1)}, bf16[128,1536]{1,0:T(8,128)(2,1)S(1)}, u32[]{:S(2)}, u32[]{:S(2)}) collective-permute-start(bf16[128,1536]{1,0:T(8,128)(2,1)} %get-tuple-element.114), channel_id=1, source_target_pairs={{28,0},{29,1},{30,2},{31,3},{0,4},{1,5},{2,6},{3,7},{4,8},{5,9},{6... | collective-permute-start | bytes 1179656 | tf_op jit(solution)/shard_map/ppermute | solution.py:59
  140.7 16.4 %collective-permute-start.22 = (bf16[128,1536]{1,0:T(8,128)(2,1)}, bf16[128,1536]{1,0:T(8,128)(2,1)S(1)}, u32[]{:S(2)}, u32[]{:S(2)}) collective-permute-start(bf16[128,1536]{1,0:T(8,128)(2,1)} %get-tuple-element.115), channel_id=1, source_target_pairs={{3,0},{0,1},{1,2},{2,3},{7,4},{4,5},{5,6},{6,7},{11,8},{8,9},{9,10... | collective-permute-start | bytes 1179656 | tf_op jit(solution)/shard_map/ppermute | solution.py:59
  143.5 16.5 %collective-permute-start.23 = (bf16[128,1536]{1,0:T(8,128)(2,1)}, bf16[128,1536]{1,0:T(8,128)(2,1)S(1)}, u32[]{:S(2)}, u32[]{:S(2)}) collective-permute-start(bf16[128,1536]{1,0:T(8,128)(2,1)} %get-tuple-element.116), channel_id=1, source_target_pairs={{31,0},{28,1},{29,2},{30,3},{3,4},{0,5},{1,6},{2,7},{7,8},{4,9},{5... | collective-permute-start | bytes 1179656 | tf_op jit(solution)/shard_map/ppermute | solution.py:59
  160.0 16.3 %collective-permute-start.27 = (bf16[384,1536]{1,0:T(8,128)(2,1)}, bf16[384,1536]{1,0:T(8,128)(2,1)S(1)}, u32[]{:S(2)}, u32[]{:S(2)}) collective-permute-start(bf16[384,1536]{1,0:T(8,128)(2,1)} %collective-permute-done.17.refs_10_), channel_id=1, source_target_pairs={{0,32},{1,33},{2,34},{3,35},{4,36},{5,37},{6,38},{7,39},{8,40},{9,... | collective-permute-start | bytes 3538952 | tf_op jit(solution)/shard_map/ppermute | solution.py:59
  163.1 13.2 %collective-permute-start.28 = (bf16[384,1536]{1,0:T(8,128)(2,1)}, bf16[384,1536]{1,0:T(8,128)(2,1)S(1)}, u32[]{:S(2)}, u32[]{:S(2)}) collective-permute-start(bf16[384,1536]{1,0:T(8,128)(2,1)} %collective-permute-done.18.refs_11_), channel_id=1, source_target_pairs={{0,32},{1,33},{2,34},{3,35},{4,36},{5,37},{6,38},{7,39},{8,40},{9,... | collective-permute-start | bytes 3538952 | tf_op jit(solution)/shard_map/ppermute | solution.py:59
  163.1 8.9 %collective-permute-start.24 = (bf16[128,1536]{1,0:T(8,128)(2,1)}, bf16[128,1536]{1,0:T(8,128)(2,1)S(1)}, u32[]{:S(2)}, u32[]{:S(2)}) collective-permute-start(bf16[128,1536]{1,0:T(8,128)(2,1)} %get-tuple-element.128), channel_id=1, source_target_pairs={{4,0},{5,1},{6,2},{7,3},{8,4},{9,5},{10,6},{11,7},{12,8},{13,9},{1... | collective-permute-start | bytes 1179656 | tf_op jit(solution)/shard_map/ppermute | solution.py:59
  163.1 8.9 %collective-permute-start.25 = (bf16[128,1536]{1,0:T(8,128)(2,1)}, bf16[128,1536]{1,0:T(8,128)(2,1)S(1)}, u32[]{:S(2)}, u32[]{:S(2)}) collective-permute-start(bf16[128,1536]{1,0:T(8,128)(2,1)} %get-tuple-element.129), channel_id=1, source_target_pairs={{1,0},{2,1},{3,2},{0,3},{5,4},{6,5},{7,6},{4,7},{9,8},{10,9},{11,1... | collective-permute-start | bytes 1179656 | tf_op jit(solution)/shard_map/ppermute | solution.py:59
  163.1 13.2 %collective-permute-start.26 = (bf16[128,1536]{1,0:T(8,128)(2,1)}, bf16[128,1536]{1,0:T(8,128)(2,1)S(1)}, u32[]{:S(2)}, u32[]{:S(2)}) collective-permute-start(bf16[128,1536]{1,0:T(8,128)(2,1)} %get-tuple-element.130), channel_id=1, source_target_pairs={{5,0},{6,1},{7,2},{4,3},{9,4},{10,5},{11,6},{8,7},{13,8},{14,9},{1... | collective-permute-start | bytes 1179656 | tf_op jit(solution)/shard_map/ppermute | solution.py:59
  (23 other events, 197.2 us)

commit v10 on v9

--- a/solution.py
+++ b/solution.py
@@ -203,8 +203,9 @@
     )(meta, *pieces)
 
 
-def project_kernel(meta, places, *refs):
-    attended, own, other, (tokens, out, lhs, held, sems) = refs[:8], refs[8:12], refs[12:16], refs[16:]
+def project_kernel(half, meta, places, *refs):
+    attended, own, other, tokens = refs[:4], refs[4:8], refs[8:12], refs[12]
+    out, lhs, held, sems = refs[-4:]
     step = pl.program_id(0)
     core, x = lax.rem(meta[0], 2), lax.rem(meta[1], 4)
 
@@ -227,12 +228,11 @@
     def _():
         for copy in fetch(0):
             copy.start()
-        for half in range(2):
-            s = sign_of(half, meta[0])
-            for piece, (a, b) in enumerate(MOVES):
-                i = s + a * (1 - 2 * s)
-                j = s + b * (1 - 2 * s)
-                lhs[half * 4 + i * 2 + j] = attended[half * 4 + piece][...]
+        s = sign_of(half, meta[0])
+        for piece, (a, b) in enumerate(MOVES):
+            i = s + a * (1 - 2 * s)
+            j = s + b * (1 - 2 * s)
+            lhs[i * 2 + j] = attended[piece][...]
 
     for n in range(4):
 
@@ -245,37 +245,40 @@
                     copy.start()
 
     total = lax.dot_general(
-        lhs[...].reshape(1024, HD), held[lax.rem(step, 2)], (((1,), (1,)), ((), ())), preferred_element_type=jnp.float32
-    ).reshape(2, 2, 2, 2, 8, 8, TILE)
-    for half in range(2):
-        for i in range(2):
-            block = jnp.concatenate([total[half, i, 0], total[half, i, 1]], axis=2)
-            at = (slice(2 * half, 2 * half + 2), slice(8 * i, 8 * i + 8))
-            out[at] = (block + tokens[at].astype(jnp.float32)).astype(jnp.bfloat16)
-
-
-def project(attended, meta, places, chunks, tokens):
+        lhs[...].reshape(512, HD), held[lax.rem(step, 2)], (((1,), (1,)), ((), ())), preferred_element_type=jnp.float32
+    ).reshape(2, 2, 2, 8, 8, TILE)
+    for i in range(2):
+        block = jnp.concatenate([total[i, 0], total[i, 1]], axis=2)
+        at = (slice(0, 2), slice(8 * i, 8 * i + 8))
+        out[at] = (block + tokens[at].astype(jnp.float32)).astype(jnp.bfloat16)
+
+
+def project(half, attended, meta, places, chunks, tokens, partial=None):
+    extra = [] if partial is None else [partial]
+    block = pl.BlockSpec((2, 16, 16, TILE), lambda t, m, p: (half, 0, 0, p[t]))
     grid_spec = pltpu.PrefetchScalarGridSpec(
         num_scalar_prefetch=2,
         grid=(D // TILE,),
-        in_specs=[pl.BlockSpec((128, HD), lambda t, m, p: (0, 0))] * 8
+        in_specs=[pl.BlockSpec((128, HD), lambda t, m, p: (0, 0))] * 4
         + [pl.BlockSpec(memory_space=pl.ANY)] * 8
-        + [pl.BlockSpec((4, 16, 16, TILE), lambda t, m, p: (0, 0, 0, p[t]))],
-        out_specs=pl.BlockSpec((4, 16, 16, TILE), lambda t, m, p: (0, 0, 0, p[t])),
+        + [block]
+        + [pl.BlockSpec(memory_space=pl.ANY)] * len(extra),
+        out_specs=block,
         scratch_shapes=[
-            pltpu.VMEM((8, 128, HD), jnp.bfloat16),
+            pltpu.VMEM((4, 128, HD), jnp.bfloat16),
             pltpu.VMEM((2, TILE, HD), jnp.bfloat16),
             pltpu.SemaphoreType.DMA((2, 8)),
         ],
     )
     return pl.pallas_call(
-        project_kernel,
+        functools.partial(project_kernel, half),
         grid_spec=grid_spec,
         out_shape=jax.ShapeDtypeStruct((4, 16, 16, D), jnp.bfloat16),
+        input_output_aliases={} if partial is None else {15: 0},
         compiler_params=pltpu.CompilerParams(vmem_limit_bytes=VMEM),
-        cost_estimate=pl.CostEstimate(flops=2 * 1024 * HD * D, bytes_accessed=25 * 2**20, transcendentals=0),
+        cost_estimate=pl.CostEstimate(flops=1024 * HD * D, bytes_accessed=17 * 2**20, transcendentals=0),
         name="project",
-    )(meta, places, *attended, *chunks, tokens)
+    )(meta, places, *attended, *chunks, tokens, *extra)
 
 
 def ring_order(own, first, second, third, place):
@@ -316,11 +319,11 @@
         ((0, 0, "kv"), (1, 0, "kv"), (0, 3, "kvq"), (1, 3, "kvq"), (0, 0, "q"), (1, 0, "q")), frame, *arrays
     )
     strip = ring_order(shard, *shards, (f >> 1) * 2 + (r >> 2))
-    strips = [send(strip, shift_pairs(dy=n)) for n in (1, 2, 3)]
     h0, h1 = jnp.stack([skv0, x0[:2], y0[:2]]), jnp.stack([skv1, x1[:2], y1[:2]])
-    d0, d1, h0, h1, x0, y0, x1, y1, meta, places, *strips = together(d0, d1, h0, h1, x0, y0, x1, y1, meta, places, *strips)
+    d0, d1, h0, h1, x0, y0, x1, y1, meta, places, strip = together(d0, d1, h0, h1, x0, y0, x1, y1, meta, places, strip)
     d0, d1, down3, up3 = go(d0, 0, both), go(d1, 1, both), down(h0), up(h1)
-    c0 = ring_order(strip, *strips, c).swapaxes(0, 1).reshape(384, HD)
+    strips = lax.all_gather(strip.reshape(96, HD), "col", axis=0, tiled=True)
+    c0 = strips.reshape(4, 4, 24, HD).swapaxes(0, 1).reshape(384, HD)
     c0, d0, d1 = together(c0, d0, d1)
     downd, upd, c1 = down(d0[:2]), up(d1[:2]), turn(c0)
     c0, c1, downd, upd, down3, up3 = together(c0, c1, downd, upd, down3, up3)
@@ -333,7 +336,9 @@
     c2, c3, *rest = together(c2, c3, *attended1, *mixed0)
     attended1, mixed0 = rest[:4], rest[4:]
     attended0, s2, s3 = back(0, mixed0), swap(c2), swap(c3)
-    return project(attended0 + attended1, meta, places, (c0, c1, c2, c3, s0, s1, s2, s3), tokens_in)
+    chunks = (c0, c1, c2, c3, s0, s1, s2, s3)
+    out = project(1, attended1, meta, places, chunks, tokens_in)
+    return project(0, attended0, meta, places, chunks, tokens_in, out)
 
 
 def solution(mesh):

time: 196 us -> 195 us (level)
  waiting for transfers between devices: 92.6 us -> 64.4 us
  between operations: 0.68 us -> 13.9 us
  Pallas kernels: 53.6 us -> 59.6 us
  local copies, waits for them, and re-layouts: 5.36 us -> 8.66 us
  starting transfers between devices: 40.9 us -> 43.7 us
    ppermute x29 -> x26, waiting for transfers between devices: 92.6 us -> 34.8 us  [send(): return lax.ppermute(value, AXES, pairs)]
    all_gather x0 -> x1, waiting for transfers between devices: none -> 29.6 us  [local(): strips = lax.all_gather(strip.reshape(96, HD), 'col', axis=0, tiled=True)]
    pallas_call x1 -> x2, Pallas kernels: 16.9 us -> 23 us  [project(): pl.pallas_call(functools.partial(project_kernel, half), grid_spec=grid_sp...]
    ppermute x29 -> x26, starting transfers between devices: 40.9 us -> 43.7 us  [send(): return lax.ppermute(value, AXES, pairs)]
    unnamed x64 -> x56, local copies, waits for them, and re-layouts: 4.8 us -> 5.1 us
  transfers between devices with their start and end apart: 29 -> 27, of which waited for: 11 -> 11; matrix products, arithmetic and copies ran while one was open for 2% -> 3% of each run, Pallas kernels for 17% -> 23%
where the time goes in v10:
time: 195 us; the launch traced here: 194 us
  waiting for transfers between devices  64.4 us (33%)
  Pallas kernels  59.6 us (31%)
  starting transfers between devices  43.7 us (22%)
  between operations  13.9 us (7%)
  local copies, waits for them, and re-layouts  8.66 us (4%)
  other arithmetic  3.88 us (2%)
    ppermute x26, starting transfers between devices, send(): return lax.ppermute(value, AXES, pairs)  43.7 us
    ppermute x26, waiting for transfers between devices, send(): return lax.ppermute(value, AXES, pairs)  34.8 us
    all_gather x1, waiting for transfers between devices, local(): strips = lax.all_gather(strip.reshape(96, HD), 'col', axis=0, tiled=True)  29.6 us
    pallas_call x2, Pallas kernels, attend(): pl.pallas_call(functools.partial(attend_kernel, half), grid=(H // STEP,),...  27.2 us
    pallas_call x2, Pallas kernels, project(): pl.pallas_call(functools.partial(project_kernel, half), grid_spec=grid_sp...  23 us
    pallas_call x3, Pallas kernels, pack(): pl.pallas_call(functools.partial(pack_kernel, parts), out_shape=[jax.Shap...  9.37 us
    unnamed x56, local copies, waits for them, and re-layouts  5.1 us
  transfers between devices with their start and end apart: 27, of which 11 were waited for; matrix products, arithmetic and copies ran while one was open for 3% of the time, Pallas kernels for 23%

profile of v10, /device:TPU:1, one launch (start us, length us, event | category | flops | bytes accessed | tf_op | source)
XLA Modules:
  0.0 194.1 jit_solution(15561553198624994980)
XLA Ops:
  6.5 2.5 %pack.3 = (bf16[3,2,8,8,1536]{4,3,2,1,0:T(8,128)(2,1)}, bf16[3,2,8,8,1536]{4,3,2,1,0:T(8,128)(2,1)}) custom-call(s32[1]{0:T(128)} %bitcast.meta, bf16[4,2,8,2,8,1536]{5,4,3,2,1,0:T(8,128)(2,1)} %bitcast.48, bf16[4,2,8,2,8,1536]{5,4,3,2,1,0:T(8,128)(2,1)} %bitcast.51, bf16[4,2,8,2,8,1536]{5,4,3,2,1,0:T(8,128)(2,1)} %bitcast.54), custom_call_target="tpu_custom_call" | custom-call | bytes 6291456 | tf_op jit(solution)/shard_map/pack/pallas_call | solution.py:98
  9.1 4.7 %collective-permute-start.2 = (bf16[24,1536]{1,0:T(8,128)(2,1)S(1)}, bf16[24,1536]{1,0:T(8,128)(2,1)S(1)}, u32[]{:S(2)}, u32[]{:S(2)}) collective-permute-start(bf16[24,1536]{1,0:T(8,128)(2,1)S(1)} %bitcast.68), channel_id=1, source_target_pairs={{0,80},{1,81},{2,82},{3,83},{4,84},{5,85},{6,86},{7,87},{8,88},{9,... | collective-permute-start | bytes 221192 | tf_op jit(solution)/shard_map/ppermute | solution.py:59
  14.4 4.1 %collective-permute-start.3 = (bf16[3,128,1536]{2,1,0:T(8,128)(2,1)}, bf16[3,128,1536]{2,1,0:T(8,128)(2,1)S(1)}, u32[]{:S(2)}, u32[]{:S(2)}) collective-permute-start(bf16[3,128,1536]{2,1,0:T(8,128)(2,1)} %bitcast.73), channel_id=1, source_target_pairs={{0,4},{1,5},{2,6},{3,7},{4,8},{5,9},{6,10},{7,11},{8,12},{9,13},{1... | collective-permute-start | bytes 3538952 | tf_op jit(solution)/shard_map/ppermute | solution.py:59
  18.6 2.7 %collective-permute-start.4 = (bf16[3,128,1536]{2,1,0:T(8,128)(2,1)}, bf16[3,128,1536]{2,1,0:T(8,128)(2,1)S(1)}, u32[]{:S(2)}, u32[]{:S(2)}) collective-permute-start(bf16[3,128,1536]{2,1,0:T(8,128)(2,1)} %bitcast.72), channel_id=1, source_target_pairs={{0,1},{1,2},{2,3},{3,0},{4,5},{5,6},{6,7},{7,4},{8,9},{9,10},{10,1... | collective-permute-start | bytes 3538952 | tf_op jit(solution)/shard_map/ppermute | solution.py:59
  22.0 2.5 %pack.4 = (bf16[3,2,8,8,1536]{4,3,2,1,0:T(8,128)(2,1)}, bf16[3,2,8,8,1536]{4,3,2,1,0:T(8,128)(2,1)}) custom-call(s32[1]{0:T(128)} %bitcast.meta, bf16[4,2,8,2,8,1536]{5,4,3,2,1,0:T(8,128)(2,1)} %bitcast.49, bf16[4,2,8,2,8,1536]{5,4,3,2,1,0:T(8,128)(2,1)} %bitcast.52, bf16[4,2,8,2,8,1536]{5,4,3,2,1,0:T(8,128)(2,1)} %bitcast.55), custom_call_target="tpu_custom_call" | custom-call | bytes 6291456 | tf_op jit(solution)/shard_map/pack/pallas_call | solution.py:98
  24.5 1.3 pad_add_fusion
  26.0 4.3 %pack.5 = (bf16[2,2,8,8,1536]{4,3,2,1,0:T(8,128)(2,1)}, bf16[2,2,8,8,1536]{4,3,2,1,0:T(8,128)(2,1)}, bf16[3,2,8,8,1536]{4,3,2,1,0:T(8,128)(2,1)}, bf16[3,2,8,8,1...) custom-call(s32[1]{0:T(128)} %bitcast.meta, ...), custom_call_target="tpu_custom_call" | custom-call | bytes 12582912 | tf_op jit(solution)/shard_map/pack/pallas_call | solution.py:98
  31.2 5.3 %collective-permute-done.3.x = bf16[3,128,1536]{2,1,0:T(8,128)(2,1)S(1)} collective-permute-done((bf16[3,128,1536]{2,1,0:T(8,128)(2,1)}, bf16[3,128,1536]{2,1,0:T(8,128)(2,1)S(1)}, u32[]{:S(2)}, u32[]{:S(2)}) %collective-permute-start.3) | collective-permute-done | bytes 1179680 | tf_op jit(solution)/shard_map/ppermute | solution.py:59
  36.5 3.7 %collective-permute-done.4.y = bf16[3,128,1536]{2,1,0:T(8,128)(2,1)S(1)} collective-permute-done((bf16[3,128,1536]{2,1,0:T(8,128)(2,1)}, bf16[3,128,1536]{2,1,0:T(8,128)(2,1)S(1)}, u32[]{:S(2)}, u32[]{:S(2)}) %collective-permute-start.4) | collective-permute-done | bytes 1179680 | tf_op jit(solution)/shard_map/ppermute | solution.py:59
  41.5 5.2 %collective-permute-done.5.x = bf16[3,128,1536]{2,1,0:T(8,128)(2,1)S(1)} collective-permute-done((bf16[3,128,1536]{2,1,0:T(8,128)(2,1)}, bf16[3,128,1536]{2,1,0:T(8,128)(2,1)S(1)}, u32[]{:S(2)}, u32[]{:S(2)}) %collective-permute-start.5) | collective-permute-done | bytes 1179680 | tf_op jit(solution)/shard_map/ppermute | solution.py:59
  48.5 1.7 pad_maximum_fusion.1
  50.2 4.6 %collective-permute-start.7 = (bf16[3,128,1536]{2,1,0:T(8,128)(2,1)}, bf16[3,128,1536]{2,1,0:T(8,128)(2,1)S(1)}, u32[]{:S(2)}, u32[]{:S(2)}) collective-permute-start(bf16[3,128,1536]{2,1,0:T(8,128)(2,1)} %bitcast.77), channel_id=1, source_target_pairs={{0,5},{1,6},{2,7},{3,4},{4,9},{5,10},{6,11},{7,8},{8,13},{9,14},{1... | collective-permute-start | bytes 3538952 | tf_op jit(solution)/shard_map/ppermute | solution.py:59
  54.7 3.1 %collective-permute-start.12 = (bf16[3,2,128,1536]{3,2,1,0:T(8,128)(2,1)S(1)}, bf16[3,2,128,1536]{3,2,1,0:T(8,128)(2,1)}, u32[]{:S(2)}, u32[]{:S(2)}) collective-permute-start(bf16[3,2,128,1536]{3,2,1,0:T(8,128)(2,1)S(1)} %pad_maximum_fusion), channel_id=1, source_target_pairs={{32,0},{33,1},{34,2},{35,3},{36,4},{37,5},{38,6},{39,7},{40,8},{41... | collective-permute-start | bytes 7077896 | tf_op jit(solution)/shard_map/ppermute | solution.py:59
  57.9 3.9 %collective-permute-start.13 = (bf16[3,2,128,1536]{3,2,1,0:T(8,128)(2,1)}, bf16[3,2,128,1536]{3,2,1,0:T(8,128)(2,1)}, u32[]{:S(2)}, u32[]{:S(2)}) collective-permute-start(bf16[3,2,128,1536]{3,2,1,0:T(8,128)(2,1)} %pad_maximum_fusion.1), channel_id=1, source_target_pairs={{0,32},{1,33},{2,34},{3,35},{4,36},{5,37},{6,38},{7,39},{8,40},{9,... | collective-permute-start | bytes 7077896 | tf_op jit(solution)/shard_map/ppermute | solution.py:59
  61.8 29.6 %all-gather.2.cloned.1.call-done = bf16[384,1536]{1,0:T(8,128)(2,1)} async-done(((bf16[96,1536]{1,0:T(8,128)(2,1)}), bf16[384,1536]{1,0:T(8,128)(2,1)}) %all-gather.2.cloned.1.call-update) | async-done | bytes 1179664 | tf_op jit(solution)/shard_map/all_gather | solution.py:325
  91.4 1.4 copy.8
  92.9 3.2 %collective-permute-start.9 = (bf16[384,1536]{1,0:T(8,128)(2,1)S(1)}, bf16[384,1536]{1,0:T(8,128)(2,1)S(1)}, u32[]{:S(2)}, u32[]{:S(2)}) collective-permute-start(bf16[384,1536]{1,0:T(8,128)(2,1)S(1)} %bitcast.57), channel_id=1, source_target_pairs={{0,4},{1,5},{2,6},{3,7},{4,8},{5,9},{6,10},{7,11},{8,12},{9,13},{1... | collective-permute-start | bytes 3538952 | tf_op jit(solution)/shard_map/ppermute | solution.py:59
  97.3 2.8 %collective-permute-start.11 = (bf16[2,128,1536]{2,1,0:T(8,128)(2,1)S(1)}, bf16[2,128,1536]{2,1,0:T(8,128)(2,1)S(1)}, u32[]{:S(2)}, u32[]{:S(2)}) collective-permute-start(bf16[2,128,1536]{2,1,0:T(8,128)(2,1)S(1)} %slice.23), channel_id=1, source_target_pairs={{0,32},{1,33},{2,34},{3,35},{4,36},{5,37},{6,38},{7,39},{8,40},{9,... | collective-permute-start | bytes 2359304 | tf_op jit(solution)/shard_map/ppermute | solution.py:59
  100.1 1.9 collective-permute-start.10
  102.1 5.9 %collective-permute-done.12.h3 = bf16[3,2,128,1536]{3,2,1,0:T(8,128)(2,1)} collective-permute-done((bf16[3,2,128,1536]{3,2,1,0:T(8,128)(2,1)S(1)}, bf16[3,2,128,1536]{3,2,1,0:T(8,128)(2,1)}, u32[]{:S(2)}, u32[]{:S(2)}) %collective-permute-start.12) | collective-permute-done | bytes 2359328 | tf_op jit(solution)/shard_map/ppermute | solution.py:59
  108.0 5.7 %collective-permute-done.11.hd = bf16[2,128,1536]{2,1,0:T(8,128)(2,1)S(1)} collective-permute-done((bf16[2,128,1536]{2,1,0:T(8,128)(2,1)S(1)}, bf16[2,128,1536]{2,1,0:T(8,128)(2,1)S(1)}, u32[]{:S(2)}, u32[]{:S(2)}) %collective-permute-start.11) | collective-permute-done | bytes 786464 | tf_op jit(solution)/shard_map/ppermute | solution.py:59
  113.7 2.6 %collective-permute-done.10.hd = bf16[2,128,1536]{2,1,0:T(8,128)(2,1)S(1)} collective-permute-done((bf16[2,128,1536]{2,1,0:T(8,128)(2,1)S(1)}, bf16[2,128,1536]{2,1,0:T(8,128)(2,1)S(1)}, u32[]{:S(2)}, u32[]{:S(2)}) %collective-permute-start.10) | collective-permute-done | bytes 786464 | tf_op jit(solution)/shard_map/ppermute | solution.py:59
  118.4 13.6 %attend.2 = (bf16[128,1536]{1,0:T(8,128)(2,1)}, bf16[128,1536]{1,0:T(8,128)(2,1)}, bf16[128,1536]{1,0:T(8,128)(2,1)}, bf16[128,1536]{1,0:T(8,128)(2,1)}) custom-call(s32[4]{0:T(128)} %get-tuple-element.88.meta, bf16[2,128,1536]{2,1,0:T(8,128)(2,1)} %bitcast.66, bf16[1,128,1536]{2,1,0:T(8,128)(2,1)} %bitcast.79, bf16[3,128,1536]{2,1,0:T(8,128)(2,1)} %copy-done.12, ...), custom_call_target="tpu_custom_call" | custom-call | flops 6442450944 | bytes 10485760 | tf_op jit(solution)/shard_map/attend/pallas_call | solution.py:188
  132.0 2.2 %collective-permute-start.18 = (bf16[128,1536]{1,0:T(8,128)(2,1)}, bf16[128,1536]{1,0:T(8,128)(2,1)S(1)}, u32[]{:S(2)}, u32[]{:S(2)}) collective-permute-start(bf16[128,1536]{1,0:T(8,128)(2,1)} %get-tuple-element.110), channel_id=1, source_target_pairs={{28,0},{29,1},{30,2},{31,3},{0,4},{1,5},{2,6},{3,7},{4,8},{5,9},{6... | collective-permute-start | bytes 1179656 | tf_op jit(solution)/shard_map/ppermute | solution.py:59
  134.2 2.8 %collective-permute-start.19 = (bf16[128,1536]{1,0:T(8,128)(2,1)}, bf16[128,1536]{1,0:T(8,128)(2,1)S(1)}, u32[]{:S(2)}, u32[]{:S(2)}) collective-permute-start(bf16[128,1536]{1,0:T(8,128)(2,1)} %get-tuple-element.111), channel_id=1, source_target_pairs={{3,0},{0,1},{1,2},{2,3},{7,4},{4,5},{5,6},{6,7},{11,8},{8,9},{9,10... | collective-permute-start | bytes 1179656 | tf_op jit(solution)/shard_map/ppermute | solution.py:59
  137.1 13.6 %attend.3 = (bf16[128,1536]{1,0:T(8,128)(2,1)}, bf16[128,1536]{1,0:T(8,128)(2,1)}, bf16[128,1536]{1,0:T(8,128)(2,1)}, bf16[128,1536]{1,0:T(8,128)(2,1)}) custom-call(s32[4]{0:T(128)} %get-tuple-element.88.meta, bf16[2,128,1536]{2,1,0:T(8,128)(2,1)} %bitcast.64, bf16[1,128,1536]{2,1,0:T(8,128)(2,1)} %bitcast.78, bf16[3,128,1536]{2,1,0:T(8,128)(2,1)} %copy-done.10, ...), custom_call_target="tpu_custom_call" | custom-call | flops 6442450944 | bytes 10485760 | tf_op jit(solution)/shard_map/attend/pallas_call | solution.py:188
  150.8 2.1 %collective-permute-done.20.refs_3_ = bf16[128,1536]{1,0:T(8,128)(2,1)S(1)} collective-permute-done((bf16[128,1536]{1,0:T(8,128)(2,1)}, bf16[128,1536]{1,0:T(8,128)(2,1)S(1)}, u32[]{:S(2)}, u32[]{:S(2)}) %collective-permute-start.20) | collective-permute-done | bytes 393248 | tf_op jit(solution)/shard_map/ppermute | solution.py:59
  152.9 4.4 %collective-permute-start.24 = (bf16[384,1536]{1,0:T(8,128)(2,1)S(1)}, bf16[384,1536]{1,0:T(8,128)(2,1)S(1)}, u32[]{:S(2)}, u32[]{:S(2)}) collective-permute-start(bf16[384,1536]{1,0:T(8,128)(2,1)S(1)} %collective-permute-done.14.refs_6_), channel_id=1, source_target_pairs={{0,32},{1,33},{2,34},{3,35},{4,36},{5,37},{6,38},{7,39},{8,40},{9,... | collective-permute-start | bytes 3538952 | tf_op jit(solution)/shard_map/ppermute | solution.py:59
  157.5 2.3 %collective-permute-done.24.refs_10_ = bf16[384,1536]{1,0:T(8,128)(2,1)S(1)} collective-permute-done((bf16[384,1536]{1,0:T(8,128)(2,1)S(1)}, bf16[384,1536]{1,0:T(8,128)(2,1)S(1)}, u32[]{:S(2)}, u32[]{:S(2)}) %collective-permute-start.24) | collective-permute-done | bytes 1179680 | tf_op jit(solution)/shard_map/ppermute | solution.py:59
  159.8 1.7 collective-permute-done.25.refs_11_
  162.5 11.5 %project.2.refs_13_ = bf16[4,16,16,3072]{3,2,1,0:T(8,128)(2,1)} custom-call(s32[4]{0:T(128)} %get-tuple-element.88.meta, s32[4]{0:T(128)} %get-tuple-element.89.places, bf16[128,1536]{1,0:T(8,128)(2,1)} %get-tuple-element.131.refs_0_, bf16[128,1536]{1,0:T(8,128)(2,1)} %copy-done.18, bf16[128,1536]{1,0:T(8,128)(2,1)} %copy-done.19, ...), custom_call_target="tpu_custom_call" | custom-call | flops 4831838208 | bytes 17825792 | tf_op jit(solution)/shard_map/project/pallas_call | solution.py:273
  175.7 11.5 %project.3 = bf16[4,16,16,3072]{3,2,1,0:T(8,128)(2,1)} custom-call(s32[4]{0:T(128)} %get-tuple-element.88.meta, s32[4]{0:T(128)} %get-tuple-element.89.places, bf16[128,1536]{1,0:T(8,128)(2,1)} %get-tuple-element.123.refs_0_, bf16[128,1536]{1,0:T(8,128)(2,1)} %copy-done.15, bf16[128,1536]{1,0:T(8,128)(2,1)} %copy-done.16, ...), custom_call_target="tpu_custom_call", output_to_operand_aliasing={{}: (15, {})} | custom-call | flops 4831838208 | bytes 17825792 | tf_op jit(solution)/shard_map/project/pallas_call | solution.py:273
  (99 shorter events, 11.7 us)
Async XLA Ops:
  6.5 84.9 %all-gather.2.cloned.1.call-start = ((), (), s32[]{:S(2)}) async-start(), calls=%async_computation | async-start | bytes 1474560 | tf_op jit(solution)/shard_map/all_gather | solution.py:325
  6.5 14.8 %copy-start.24 = (s32[128]{0:T(128)S(1)}, s32[128]{0:T(128)}, u32[]{:S(2)}) copy-start(s32[128]{0:T(128)} %param.11) | copy-start | bytes 1540
  9.1 16.7 %collective-permute-start.2 = (bf16[24,1536]{1,0:T(8,128)(2,1)S(1)}, bf16[24,1536]{1,0:T(8,128)(2,1)S(1)}, u32[]{:S(2)}, u32[]{:S(2)}) collective-permute-start(bf16[24,1536]{1,0:T(8,128)(2,1)S(1)} %bitcast.68), channel_id=1, source_target_pairs={{0,80},{1,81},{2,82},{3,83},{4,84},{5,85},{6,86},{7,87},{8,88},{9,... | collective-permute-start | bytes 221192 | tf_op jit(solution)/shard_map/ppermute | solution.py:59
  13.7 12.1 %collective-permute-start.1 = (bf16[24,1536]{1,0:T(8,128)(2,1)S(1)}, bf16[24,1536]{1,0:T(8,128)(2,1)S(1)}, u32[]{:S(2)}, u32[]{:S(2)}) collective-permute-start(bf16[24,1536]{1,0:T(8,128)(2,1)S(1)} %bitcast.69), channel_id=1, source_target_pairs={{0,64},{1,65},{2,66},{3,67},{4,68},{5,69},{6,70},{7,71},{8,72},{9,... | collective-permute-start | bytes 221192 | tf_op jit(solution)/shard_map/ppermute | solution.py:59
  13.7 12.1 %collective-permute-start = (bf16[24,1536]{1,0:T(8,128)(2,1)S(1)}, bf16[24,1536]{1,0:T(8,128)(2,1)S(1)}, u32[]{:S(2)}, u32[]{:S(2)}) collective-permute-start(bf16[24,1536]{1,0:T(8,128)(2,1)S(1)} %bitcast.70), channel_id=1, source_target_pairs={{0,16},{1,17},{2,18},{3,19},{4,20},{5,21},{6,22},{7,23},{8,24},{9,... | collective-permute-start | bytes 221192 | tf_op jit(solution)/shard_map/ppermute | solution.py:59
  14.4 22.0 %collective-permute-start.3 = (bf16[3,128,1536]{2,1,0:T(8,128)(2,1)}, bf16[3,128,1536]{2,1,0:T(8,128)(2,1)S(1)}, u32[]{:S(2)}, u32[]{:S(2)}) collective-permute-start(bf16[3,128,1536]{2,1,0:T(8,128)(2,1)} %bitcast.73), channel_id=1, source_target_pairs={{0,4},{1,5},{2,6},{3,7},{4,8},{5,9},{6,10},{7,11},{8,12},{9,13},{1... | collective-permute-start | bytes 3538952 | tf_op jit(solution)/shard_map/ppermute | solution.py:59
  18.6 21.7 %collective-permute-start.4 = (bf16[3,128,1536]{2,1,0:T(8,128)(2,1)}, bf16[3,128,1536]{2,1,0:T(8,128)(2,1)S(1)}, u32[]{:S(2)}, u32[]{:S(2)}) collective-permute-start(bf16[3,128,1536]{2,1,0:T(8,128)(2,1)} %bitcast.72), channel_id=1, source_target_pairs={{0,1},{1,2},{2,3},{3,0},{4,5},{5,6},{6,7},{7,4},{8,9},{9,10},{10,1... | collective-permute-start | bytes 3538952 | tf_op jit(solution)/shard_map/ppermute | solution.py:59
  25.9 20.8 %collective-permute-start.5 = (bf16[3,128,1536]{2,1,0:T(8,128)(2,1)}, bf16[3,128,1536]{2,1,0:T(8,128)(2,1)S(1)}, u32[]{:S(2)}, u32[]{:S(2)}) collective-permute-start(bf16[3,128,1536]{2,1,0:T(8,128)(2,1)} %bitcast.76), channel_id=1, source_target_pairs={{0,28},{1,29},{2,30},{3,31},{4,0},{5,1},{6,2},{7,3},{8,4},{9,5},{1... | collective-permute-start | bytes 3538952 | tf_op jit(solution)/shard_map/ppermute | solution.py:59
  26.0 21.1 %collective-permute-start.6 = (bf16[3,128,1536]{2,1,0:T(8,128)(2,1)}, bf16[3,128,1536]{2,1,0:T(8,128)(2,1)S(1)}, u32[]{:S(2)}, u32[]{:S(2)}) collective-permute-start(bf16[3,128,1536]{2,1,0:T(8,128)(2,1)} %bitcast.74), channel_id=1, source_target_pairs={{0,3},{1,0},{2,1},{3,2},{4,7},{5,4},{6,5},{7,6},{8,11},{9,8},{10,9... | collective-permute-start | bytes 3538952 | tf_op jit(solution)/shard_map/ppermute | solution.py:59
  50.2 42.7 %collective-permute-start.7 = (bf16[3,128,1536]{2,1,0:T(8,128)(2,1)}, bf16[3,128,1536]{2,1,0:T(8,128)(2,1)S(1)}, u32[]{:S(2)}, u32[]{:S(2)}) collective-permute-start(bf16[3,128,1536]{2,1,0:T(8,128)(2,1)} %bitcast.77), channel_id=1, source_target_pairs={{0,5},{1,6},{2,7},{3,4},{4,9},{5,10},{6,11},{7,8},{8,13},{9,14},{1... | collective-permute-start | bytes 3538952 | tf_op jit(solution)/shard_map/ppermute | solution.py:59
  54.7 38.1 %collective-permute-start.8 = (bf16[3,128,1536]{2,1,0:T(8,128)(2,1)}, bf16[3,128,1536]{2,1,0:T(8,128)(2,1)}, u32[]{:S(2)}, u32[]{:S(2)}) collective-permute-start(bf16[3,128,1536]{2,1,0:T(8,128)(2,1)} %bitcast.75), channel_id=1, source_target_pairs={{0,31},{1,28},{2,29},{3,30},{4,3},{5,0},{6,1},{7,2},{8,7},{9,4},{1... | collective-permute-start | bytes 3538952 | tf_op jit(solution)/shard_map/ppermute | solution.py:59
  54.7 53.3 %collective-permute-start.12 = (bf16[3,2,128,1536]{3,2,1,0:T(8,128)(2,1)S(1)}, bf16[3,2,128,1536]{3,2,1,0:T(8,128)(2,1)}, u32[]{:S(2)}, u32[]{:S(2)}) collective-permute-start(bf16[3,2,128,1536]{3,2,1,0:T(8,128)(2,1)S(1)} %pad_maximum_fusion), channel_id=1, source_target_pairs={{32,0},{33,1},{34,2},{35,3},{36,4},{37,5},{38,6},{39,7},{40,8},{41... | collective-permute-start | bytes 7077896 | tf_op jit(solution)/shard_map/ppermute | solution.py:59
  57.9 50.1 %collective-permute-start.13 = (bf16[3,2,128,1536]{3,2,1,0:T(8,128)(2,1)}, bf16[3,2,128,1536]{3,2,1,0:T(8,128)(2,1)}, u32[]{:S(2)}, u32[]{:S(2)}) collective-permute-start(bf16[3,2,128,1536]{3,2,1,0:T(8,128)(2,1)} %pad_maximum_fusion.1), channel_id=1, source_target_pairs={{0,32},{1,33},{2,34},{3,35},{4,36},{5,37},{6,38},{7,39},{8,40},{9,... | collective-permute-start | bytes 7077896 | tf_op jit(solution)/shard_map/ppermute | solution.py:59
  92.8 25.1 %copy-start = (bf16[4,4,24,1536]{3,2,1,0:T(8,128)(2,1)}, bf16[4,4,24,1536]{3,2,1,0:T(8,128)(2,1)S(1)}, u32[]{:S(2)}) copy-start(bf16[4,4,24,1536]{3,2,1,0:T(8,128)(2,1)S(1)} %copy.8) | copy-start | bytes 3538948
  92.9 23.5 %collective-permute-start.9 = (bf16[384,1536]{1,0:T(8,128)(2,1)S(1)}, bf16[384,1536]{1,0:T(8,128)(2,1)S(1)}, u32[]{:S(2)}, u32[]{:S(2)}) collective-permute-start(bf16[384,1536]{1,0:T(8,128)(2,1)S(1)} %bitcast.57), channel_id=1, source_target_pairs={{0,4},{1,5},{2,6},{3,7},{4,8},{5,9},{6,10},{7,11},{8,12},{9,13},{1... | collective-permute-start | bytes 3538952 | tf_op jit(solution)/shard_map/ppermute | solution.py:59
  97.3 16.4 %collective-permute-start.11 = (bf16[2,128,1536]{2,1,0:T(8,128)(2,1)S(1)}, bf16[2,128,1536]{2,1,0:T(8,128)(2,1)S(1)}, u32[]{:S(2)}, u32[]{:S(2)}) collective-permute-start(bf16[2,128,1536]{2,1,0:T(8,128)(2,1)S(1)} %slice.23), channel_id=1, source_target_pairs={{0,32},{1,33},{2,34},{3,35},{4,36},{5,37},{6,38},{7,39},{8,40},{9,... | collective-permute-start | bytes 2359304 | tf_op jit(solution)/shard_map/ppermute | solution.py:59
  100.1 16.2 %collective-permute-start.10 = (bf16[2,128,1536]{2,1,0:T(8,128)(2,1)S(1)}, bf16[2,128,1536]{2,1,0:T(8,128)(2,1)S(1)}, u32[]{:S(2)}, u32[]{:S(2)}) collective-permute-start(bf16[2,128,1536]{2,1,0:T(8,128)(2,1)S(1)} %slice.22), channel_id=1, source_target_pairs={{32,0},{33,1},{34,2},{35,3},{36,4},{37,5},{38,6},{39,7},{40,8},{41... | collective-permute-start | bytes 2359304 | tf_op jit(solution)/shard_map/ppermute | solution.py:59
  116.3 15.7 %copy-start.1 = (bf16[384,1536]{1,0:T(8,128)(2,1)}, bf16[384,1536]{1,0:T(8,128)(2,1)S(1)}, u32[]{:S(2)}) copy-start(bf16[384,1536]{1,0:T(8,128)(2,1)S(1)} %collective-permute-done.9.refs_5_) | copy-start | bytes 3538948
  116.3 15.7 %collective-permute-start.17 = (bf16[384,1536]{1,0:T(8,128)(2,1)S(1)}, bf16[384,1536]{1,0:T(8,128)(2,1)S(1)}, u32[]{:S(2)}, u32[]{:S(2)}) collective-permute-start(bf16[384,1536]{1,0:T(8,128)(2,1)S(1)} %collective-permute-done.9.refs_5_), channel_id=1, source_target_pairs={{0,32},{1,33},{2,34},{3,35},{4,36},{5,37},{6,38},{7,39},{8,40},{9,... | collective-permute-start | bytes 3538952 | tf_op jit(solution)/shard_map/ppermute | solution.py:59
  116.4 15.6 %collective-permute-start.16 = (bf16[384,1536]{1,0:T(8,128)(2,1)S(1)}, bf16[384,1536]{1,0:T(8,128)(2,1)S(1)}, u32[]{:S(2)}, u32[]{:S(2)}) collective-permute-start(bf16[384,1536]{1,0:T(8,128)(2,1)S(1)} %bitcast.58), channel_id=1, source_target_pairs={{0,32},{1,33},{2,34},{3,35},{4,36},{5,37},{6,38},{7,39},{8,40},{9,... | collective-permute-start | bytes 3538952 | tf_op jit(solution)/shard_map/ppermute | solution.py:59
  116.9 33.8 %collective-permute-start.14 = (bf16[384,1536]{1,0:T(8,128)(2,1)S(1)}, bf16[384,1536]{1,0:T(8,128)(2,1)S(1)}, u32[]{:S(2)}, u32[]{:S(2)}) collective-permute-start(bf16[384,1536]{1,0:T(8,128)(2,1)S(1)} %collective-permute-done.9.refs_5_), channel_id=1, source_target_pairs={{0,4},{1,5},{2,6},{3,7},{4,8},{5,9},{6,10},{7,11},{8,12},{9,13},{1... | collective-permute-start | bytes 3538952 | tf_op jit(solution)/shard_map/ppermute | solution.py:59
  117.9 32.9 %collective-permute-start.15 = (bf16[384,1536]{1,0:T(8,128)(2,1)S(1)}, bf16[384,1536]{1,0:T(8,128)(2,1)S(1)}, u32[]{:S(2)}, u32[]{:S(2)}) collective-permute-start(bf16[384,1536]{1,0:T(8,128)(2,1)S(1)} %bitcast.59), channel_id=1, source_target_pairs={{0,12},{1,13},{2,14},{3,15},{4,0},{5,1},{6,2},{7,3},{8,4},{9,5},{1... | collective-permute-start | bytes 3538952 | tf_op jit(solution)/shard_map/ppermute | solution.py:59
  132.0 18.7 %copy-start.2 = (bf16[384,1536]{1,0:T(8,128)(2,1)}, bf16[384,1536]{1,0:T(8,128)(2,1)S(1)}, u32[]{:S(2)}) copy-start(bf16[384,1536]{1,0:T(8,128)(2,1)S(1)} %collective-permute-done.17.refs_9_) | copy-start | bytes 3538948
  132.0 18.7 %copy-start.3 = (bf16[384,1536]{1,0:T(8,128)(2,1)}, bf16[384,1536]{1,0:T(8,128)(2,1)S(1)}, u32[]{:S(2)}) copy-start(bf16[384,1536]{1,0:T(8,128)(2,1)S(1)} %collective-permute-done.16.refs_8_) | copy-start | bytes 3538948
  132.0 18.8 %collective-permute-start.18 = (bf16[128,1536]{1,0:T(8,128)(2,1)}, bf16[128,1536]{1,0:T(8,128)(2,1)S(1)}, u32[]{:S(2)}, u32[]{:S(2)}) collective-permute-start(bf16[128,1536]{1,0:T(8,128)(2,1)} %get-tuple-element.110), channel_id=1, source_target_pairs={{28,0},{29,1},{30,2},{31,3},{0,4},{1,5},{2,6},{3,7},{4,8},{5,9},{6... | collective-permute-start | bytes 1179656 | tf_op jit(solution)/shard_map/ppermute | solution.py:59
  134.2 16.6 %collective-permute-start.19 = (bf16[128,1536]{1,0:T(8,128)(2,1)}, bf16[128,1536]{1,0:T(8,128)(2,1)S(1)}, u32[]{:S(2)}, u32[]{:S(2)}) collective-permute-start(bf16[128,1536]{1,0:T(8,128)(2,1)} %get-tuple-element.111), channel_id=1, source_target_pairs={{3,0},{0,1},{1,2},{2,3},{7,4},{4,5},{5,6},{6,7},{11,8},{8,9},{9,10... | collective-permute-start | bytes 1179656 | tf_op jit(solution)/shard_map/ppermute | solution.py:59
  137.1 15.8 %collective-permute-start.20 = (bf16[128,1536]{1,0:T(8,128)(2,1)}, bf16[128,1536]{1,0:T(8,128)(2,1)S(1)}, u32[]{:S(2)}, u32[]{:S(2)}) collective-permute-start(bf16[128,1536]{1,0:T(8,128)(2,1)} %get-tuple-element.112), channel_id=1, source_target_pairs={{31,0},{28,1},{29,2},{30,3},{3,4},{0,5},{1,6},{2,7},{7,8},{4,9},{5... | collective-permute-start | bytes 1179656 | tf_op jit(solution)/shard_map/ppermute | solution.py:59
  152.9 6.9 %collective-permute-start.24 = (bf16[384,1536]{1,0:T(8,128)(2,1)S(1)}, bf16[384,1536]{1,0:T(8,128)(2,1)S(1)}, u32[]{:S(2)}, u32[]{:S(2)}) collective-permute-start(bf16[384,1536]{1,0:T(8,128)(2,1)S(1)} %collective-permute-done.14.refs_6_), channel_id=1, source_target_pairs={{0,32},{1,33},{2,34},{3,35},{4,36},{5,37},{6,38},{7,39},{8,40},{9,... | collective-permute-start | bytes 3538952 | tf_op jit(solution)/shard_map/ppermute | solution.py:59
  157.3 4.2 %collective-permute-start.25 = (bf16[384,1536]{1,0:T(8,128)(2,1)S(1)}, bf16[384,1536]{1,0:T(8,128)(2,1)S(1)}, u32[]{:S(2)}, u32[]{:S(2)}) collective-permute-start(bf16[384,1536]{1,0:T(8,128)(2,1)S(1)} %collective-permute-done.15.refs_7_), channel_id=1, source_target_pairs={{0,32},{1,33},{2,34},{3,35},{4,36},{5,37},{6,38},{7,39},{8,40},{9,... | collective-permute-start | bytes 3538952 | tf_op jit(solution)/shard_map/ppermute | solution.py:59
  157.3 16.7 %collective-permute-start.21 = (bf16[128,1536]{1,0:T(8,128)(2,1)}, bf16[128,1536]{1,0:T(8,128)(2,1)S(1)}, u32[]{:S(2)}, u32[]{:S(2)}) collective-permute-start(bf16[128,1536]{1,0:T(8,128)(2,1)} %get-tuple-element.124), channel_id=1, source_target_pairs={{4,0},{5,1},{6,2},{7,3},{8,4},{9,5},{10,6},{11,7},{12,8},{13,9},{1... | collective-permute-start | bytes 1179656 | tf_op jit(solution)/shard_map/ppermute | solution.py:59
  157.3 16.7 %collective-permute-start.22 = (bf16[128,1536]{1,0:T(8,128)(2,1)}, bf16[128,1536]{1,0:T(8,128)(2,1)S(1)}, u32[]{:S(2)}, u32[]{:S(2)}) collective-permute-start(bf16[128,1536]{1,0:T(8,128)(2,1)} %get-tuple-element.125), channel_id=1, source_target_pairs={{1,0},{2,1},{3,2},{0,3},{5,4},{6,5},{7,6},{4,7},{9,8},{10,9},{11,1... | collective-permute-start | bytes 1179656 | tf_op jit(solution)/shard_map/ppermute | solution.py:59
  157.3 16.7 %collective-permute-start.23 = (bf16[128,1536]{1,0:T(8,128)(2,1)}, bf16[128,1536]{1,0:T(8,128)(2,1)S(1)}, u32[]{:S(2)}, u32[]{:S(2)}) collective-permute-start(bf16[128,1536]{1,0:T(8,128)(2,1)} %get-tuple-element.126), channel_id=1, source_target_pairs={{5,0},{6,1},{7,2},{4,3},{9,4},{10,5},{11,6},{8,7},{13,8},{14,9},{1... | collective-permute-start | bytes 1179656 | tf_op jit(solution)/shard_map/ppermute | solution.py:59
  (20 other events, 84.3 us)
Sparse Core Ops, SparseCore 0:
  50.3 41.1 all-gather.1

commit v11 on v10

--- a/solution.py
+++ b/solution.py
@@ -136,7 +136,7 @@
     alive[...] = jnp.where(live, 1.0, 0.0)
 
 
-def attend_kernel(half, meta, skv, sq, x, y, d, h3, hd, o0, o1, o2, o3, kaug, vaug, qaug, alive):
+def attend_kernel(half, meta, skv, sq, x, y, d, hs, h2, hd, o0, o1, o2, o3, kaug, vaug, qaug, alive):
     outs = (o0, o1, o2, o3)
 
     @pl.when(pl.program_id(0) == 0)
@@ -147,7 +147,7 @@
             qaug[n, :, HS:] = qaug[0, :, HS:]
         vaug[:, :, HS:] = jnp.ones((STEP, 1024, HS), jnp.bfloat16)
 
-    keys = (skv, x, y, d, h3.at[0], h3.at[1], h3.at[2], hd)
+    keys = (skv, x, y, d, hs, h2.at[0], h2.at[1], hd)
     asks = (sq.at[0], x.at[2], y.at[2], d.at[2])
     for h in range(STEP):
         lanes = pl.ds(h * HS, HS)
@@ -228,11 +228,12 @@
     def _():
         for copy in fetch(0):
             copy.start()
-        s = sign_of(half, meta[0])
-        for piece, (a, b) in enumerate(MOVES):
-            i = s + a * (1 - 2 * s)
-            j = s + b * (1 - 2 * s)
-            lhs[i * 2 + j] = attended[piece][...]
+        ahead = sign_of(half, meta[0]) == 0
+        pieces = [piece[...].astype(jnp.float32).reshape(2, 8, 8, HD) for piece in attended]
+        for i in range(2):
+            left = jnp.where(ahead, pieces[i], pieces[3 - i])
+            right = jnp.where(ahead, pieces[2 + i], pieces[1 - i])
+            lhs[:, 8 * i : 8 * i + 8] = jnp.concatenate([left, right], axis=2).astype(jnp.bfloat16)
 
     for n in range(4):
 
@@ -246,11 +247,8 @@
 
     total = lax.dot_general(
         lhs[...].reshape(512, HD), held[lax.rem(step, 2)], (((1,), (1,)), ((), ())), preferred_element_type=jnp.float32
-    ).reshape(2, 2, 2, 8, 8, TILE)
-    for i in range(2):
-        block = jnp.concatenate([total[i, 0], total[i, 1]], axis=2)
-        at = (slice(0, 2), slice(8 * i, 8 * i + 8))
-        out[at] = (block + tokens[at].astype(jnp.float32)).astype(jnp.bfloat16)
+    ).reshape(2, 16, 16, TILE)
+    out[...] = (total + tokens[...].astype(jnp.float32)).astype(jnp.bfloat16)
 
 
 def project(half, attended, meta, places, chunks, tokens, partial=None):
@@ -265,7 +263,7 @@
         + [pl.BlockSpec(memory_space=pl.ANY)] * len(extra),
         out_specs=block,
         scratch_shapes=[
-            pltpu.VMEM((4, 128, HD), jnp.bfloat16),
+            pltpu.VMEM((2, 16, 16, HD), jnp.bfloat16),
             pltpu.VMEM((2, TILE, HD), jnp.bfloat16),
             pltpu.SemaphoreType.DMA((2, 8)),
         ],
@@ -312,27 +310,30 @@
     x0, y0, frame, shard = together(x0, y0, frame, shard)
     x0, y0 = go(x0, 0, row), go(y0, 0, col)
     shards = [send(shard, shift_pairs(dz=n)) for n in (1, 2, 3)]
-    x1, y1 = pack(((1, 1, "kvq"), (1, 2, "kvq")), frame, *arrays)
-    x1, y1, frame, *shards = together(x1, y1, frame, *shards)
+    skv0, skv1, x1, y1 = pack(((0, 0, "kv"), (1, 0, "kv"), (1, 1, "kvq"), (1, 2, "kvq")), frame, *arrays)
+    skv0, skv1, x1, y1, frame = together(skv0, skv1, x1, y1, frame)
+    downs, ups = down(skv0), up(skv1)
+    x1, x0 = together(x1, x0)
+    y1, y0 = together(y1, y0)
     x1, y1 = go(x1, 1, row), go(y1, 1, col)
-    skv0, skv1, d0, d1, sq0, sq1 = pack(
-        ((0, 0, "kv"), (1, 0, "kv"), (0, 3, "kvq"), (1, 3, "kvq"), (0, 0, "q"), (1, 0, "q")), frame, *arrays
+    d0, d1, sq0, sq1 = pack(((0, 3, "kvq"), (1, 3, "kvq"), (0, 0, "q"), (1, 0, "q")), frame, *arrays)
+    strip = ring_order(shard, *shards, (f >> 1) * 2 + (r >> 2))
+    h0, h1 = jnp.stack([x0[:2], y0[:2]]), jnp.stack([x1[:2], y1[:2]])
+    d0, d1, h0, h1, x0, y0, x1, y1, downs, ups, meta, places, strip = together(
+        d0, d1, h0, h1, x0, y0, x1, y1, downs, ups, meta, places, strip
     )
-    strip = ring_order(shard, *shards, (f >> 1) * 2 + (r >> 2))
-    h0, h1 = jnp.stack([skv0, x0[:2], y0[:2]]), jnp.stack([skv1, x1[:2], y1[:2]])
-    d0, d1, h0, h1, x0, y0, x1, y1, meta, places, strip = together(d0, d1, h0, h1, x0, y0, x1, y1, meta, places, strip)
-    d0, d1, down3, up3 = go(d0, 0, both), go(d1, 1, both), down(h0), up(h1)
+    d0, d1, down2, up2 = go(d0, 0, both), go(d1, 1, both), down(h0), up(h1)
     strips = lax.all_gather(strip.reshape(96, HD), "col", axis=0, tiled=True)
     c0 = strips.reshape(4, 4, 24, HD).swapaxes(0, 1).reshape(384, HD)
     c0, d0, d1 = together(c0, d0, d1)
     downd, upd, c1 = down(d0[:2]), up(d1[:2]), turn(c0)
-    c0, c1, downd, upd, down3, up3 = together(c0, c1, downd, upd, down3, up3)
+    c0, c1, downd, upd, down2, up2 = together(c0, c1, downd, upd, down2, up2)
 
     c2, c3, s0, s1 = turn(c1), turn(c0, -1), swap(c0), swap(c1)
-    mixed1 = attend(1, meta, skv1, sq1, x1, y1, d1, down3, downd)
+    mixed1 = attend(1, meta, skv1, sq1, x1, y1, d1, downs, down2, downd)
     s0, s1, skv0, *mixed1 = together(s0, s1, skv0, *mixed1)
     attended1 = back(1, mixed1)
-    mixed0 = attend(0, meta, skv0, sq0, x0, y0, d0, up3, upd)
+    mixed0 = attend(0, meta, skv0, sq0, x0, y0, d0, ups, up2, upd)
     c2, c3, *rest = together(c2, c3, *attended1, *mixed0)
     attended1, mixed0 = rest[:4], rest[4:]
     attended0, s2, s3 = back(0, mixed0), swap(c2), swap(c3)

time: 195 us -> 200 us (1.026)
  starting transfers between devices: 43.7 us -> 49.9 us
    ppermute x26 -> x28, starting transfers between devices: 43.7 us -> 49.9 us  [send(): return lax.ppermute(value, AXES, pairs)]
    all_gather x1, waiting for transfers between devices: 29.6 us -> 26.1 us  [local(): strips = lax.all_gather(strip.reshape(96, HD), 'col', axis=0, tiled=True)]
    ppermute x26 -> x28, waiting for transfers between devices: 34.8 us -> 36.5 us  [send(): return lax.ppermute(value, AXES, pairs)]
    unnamed x56 -> x54, local copies, waits for them, and re-layouts: 5.1 us -> 5.69 us
  transfers between devices with their start and end apart: 27 -> 29, of which waited for: 11 -> 10; matrix products, arithmetic and copies ran while one was open for 3% -> 4% of each run, Pallas kernels for 23% -> 23%
where the time goes in v11:
time: 200 us; the launch traced here: 198 us
  waiting for transfers between devices  62.6 us (31%)
  Pallas kernels  59.2 us (30%)
  starting transfers between devices  49.9 us (25%)
  between operations  13.9 us (7%)
  local copies, waits for them, and re-layouts  10.5 us (5%)
  other arithmetic  2.29 us (1%)
    ppermute x28, starting transfers between devices, send(): return lax.ppermute(value, AXES, pairs)  49.9 us
    ppermute x28, waiting for transfers between devices, send(): return lax.ppermute(value, AXES, pairs)  36.5 us
    pallas_call x2, Pallas kernels, attend(): pl.pallas_call(functools.partial(attend_kernel, half), grid=(H // STEP,),...  27.3 us
    all_gather x1, waiting for transfers between devices, local(): strips = lax.all_gather(strip.reshape(96, HD), 'col', axis=0, tiled=True)  26.1 us
    pallas_call x2, Pallas kernels, project(): pl.pallas_call(functools.partial(project_kernel, half), grid_spec=grid_sp...  23.1 us
    pallas_call x3, Pallas kernels, pack(): pl.pallas_call(functools.partial(pack_kernel, parts), out_shape=[jax.Shap...  8.85 us
    unnamed x54, local copies, waits for them, and re-layouts  5.69 us
  transfers between devices with their start and end apart: 29, of which 10 were waited for; matrix products, arithmetic and copies ran while one was open for 4% of the time, Pallas kernels for 23%

profile of v11, /device:TPU:1, one launch (start us, length us, event | category | flops | bytes accessed | tf_op | source)
XLA Modules:
  0.0 198.4 jit_solution(10145675805258632477)
XLA Ops:
  6.5 2.6 %pack.3 = (bf16[3,2,8,8,1536]{4,3,2,1,0:T(8,128)(2,1)}, bf16[3,2,8,8,1536]{4,3,2,1,0:T(8,128)(2,1)}) custom-call(s32[1]{0:T(128)} %bitcast.meta, bf16[4,2,8,2,8,1536]{5,4,3,2,1,0:T(8,128)(2,1)} %bitcast.46, bf16[4,2,8,2,8,1536]{5,4,3,2,1,0:T(8,128)(2,1)} %bitcast.49, bf16[4,2,8,2,8,1536]{5,4,3,2,1,0:T(8,128)(2,1)} %bitcast.52), custom_call_target="tpu_custom_call" | custom-call | bytes 6291456 | tf_op jit(solution)/shard_map/pack/pallas_call | solution.py:98
  9.2 2.5 %collective-permute-start.8 = (bf16[24,1536]{1,0:T(8,128)(2,1)S(1)}, bf16[24,1536]{1,0:T(8,128)(2,1)S(1)}, u32[]{:S(2)}, u32[]{:S(2)}) collective-permute-start(bf16[24,1536]{1,0:T(8,128)(2,1)S(1)} %bitcast.62), channel_id=1, source_target_pairs={{0,16},{1,17},{2,18},{3,19},{4,20},{5,21},{6,22},{7,23},{8,24},{9,... | collective-permute-start | bytes 221192 | tf_op jit(solution)/shard_map/ppermute | solution.py:59
  11.7 3.3 %collective-permute-start.7 = (bf16[24,1536]{1,0:T(8,128)(2,1)S(1)}, bf16[24,1536]{1,0:T(8,128)(2,1)S(1)}, u32[]{:S(2)}, u32[]{:S(2)}) collective-permute-start(bf16[24,1536]{1,0:T(8,128)(2,1)S(1)} %bitcast.63), channel_id=1, source_target_pairs={{0,64},{1,65},{2,66},{3,67},{4,68},{5,69},{6,70},{7,71},{8,72},{9,... | collective-permute-start | bytes 221192 | tf_op jit(solution)/shard_map/ppermute | solution.py:59
  15.7 2.9 %collective-permute-start = (bf16[3,128,1536]{2,1,0:T(8,128)(2,1)}, bf16[3,128,1536]{2,1,0:T(8,128)(2,1)S(1)}, u32[]{:S(2)}, u32[]{:S(2)}) collective-permute-start(bf16[3,128,1536]{2,1,0:T(8,128)(2,1)} %bitcast.69), channel_id=1, source_target_pairs={{0,4},{1,5},{2,6},{3,7},{4,8},{5,9},{6,10},{7,11},{8,12},{9,13},{1... | collective-permute-start | bytes 3538952 | tf_op jit(solution)/shard_map/ppermute | solution.py:59
  18.7 2.7 %collective-permute-start.1 = (bf16[3,128,1536]{2,1,0:T(8,128)(2,1)}, bf16[3,128,1536]{2,1,0:T(8,128)(2,1)S(1)}, u32[]{:S(2)}, u32[]{:S(2)}) collective-permute-start(bf16[3,128,1536]{2,1,0:T(8,128)(2,1)} %bitcast.68), channel_id=1, source_target_pairs={{0,1},{1,2},{2,3},{3,0},{4,5},{5,6},{6,7},{7,4},{8,9},{9,10},{10,1... | collective-permute-start | bytes 3538952 | tf_op jit(solution)/shard_map/ppermute | solution.py:59
  22.1 3.4 %pack.4 = (bf16[2,2,8,8,1536]{4,3,2,1,0:T(8,128)(2,1)}, bf16[2,2,8,8,1536]{4,3,2,1,0:T(8,128)(2,1)}, bf16[3,2,8,8,1536]{4,3,2,1,0:T(8,128)(2,1)}, bf16[3,2,8,8,1536]{4,3,2,1,0:T(8,128)(2,1)}) custom-call(s32[1]{0:T(128)} %bitcast.meta, bf16[4,2,8,2,8,1536]{5,4,3,2,1,0:T(8,128)(2,1)} %bitcast.47, bf16[4,2,8,2,8,1536]{5,4,3,2,1,0:T(8,128)(2,1)} %bitcast.50, ...), custom_call_target="tpu_custom_call" | custom-call | bytes 10485760 | tf_op jit(solution)/shard_map/pack/pallas_call | solution.py:98
  25.5 2.8 %pack.5 = (bf16[3,2,8,8,1536]{4,3,2,1,0:T(8,128)(2,1)}, bf16[3,2,8,8,1536]{4,3,2,1,0:T(8,128)(2,1)}, bf16[1,2,8,8,1536]{4,3,2,1,0:T(8,128)(2,1)}, bf16[1,2,8,8,1536]{4,3,2,1,0:T(8,128)(2,1)}) custom-call(s32[1]{0:T(128)} %bitcast.meta, bf16[4,2,8,2,8,1536]{5,4,3,2,1,0:T(8,128)(2,1)} %bitcast.48, bf16[4,2,8,2,8,1536]{5,4,3,2,1,0:T(8,128)(2,1)} %bitcast.51, ...), custom_call_target="tpu_custom_call" | custom-call | bytes 8388608 | tf_op jit(solution)/shard_map/pack/pallas_call | solution.py:98
  28.3 1.3 pad_add_fusion
  29.7 1.9 collective-permute-start.4
  31.6 5.1 %collective-permute-start.5 = (bf16[2,128,1536]{2,1,0:T(8,128)(2,1)}, bf16[2,128,1536]{2,1,0:T(8,128)(2,1)}, u32[]{:S(2)}, u32[]{:S(2)}) collective-permute-start(bf16[2,128,1536]{2,1,0:T(8,128)(2,1)} %bitcast.8.skv), channel_id=1, source_target_pairs={{0,32},{1,33},{2,34},{3,35},{4,36},{5,37},{6,38},{7,39},{8,40},{9,... | collective-permute-start | bytes 2359304 | tf_op jit(solution)/shard_map/ppermute | solution.py:59
  39.3 14.9 %collective-permute-done.3.y = bf16[3,128,1536]{2,1,0:T(8,128)(2,1)S(1)} collective-permute-done((bf16[3,128,1536]{2,1,0:T(8,128)(2,1)}, bf16[3,128,1536]{2,1,0:T(8,128)(2,1)S(1)}, u32[]{:S(2)}, u32[]{:S(2)}) %collective-permute-start.3) | collective-permute-done | bytes 1179680 | tf_op jit(solution)/shard_map/ppermute | solution.py:59
  56.1 1.2 collective-permute-done.4.hs
  59.8 1.3 collective-permute-start.10
  61.1 4.1 %collective-permute-start.14 = (bf16[2,2,128,1536]{3,2,1,0:T(8,128)(2,1)S(1)}, bf16[2,2,128,1536]{3,2,1,0:T(8,128)(2,1)}, u32[]{:S(2)}, u32[]{:S(2)}) collective-permute-start(bf16[2,2,128,1536]{3,2,1,0:T(8,128)(2,1)S(1)} %pad_maximum_fusion), channel_id=1, source_target_pairs={{32,0},{33,1},{34,2},{35,3},{36,4},{37,5},{38,6},{39,7},{40,8},{41... | collective-permute-start | bytes 4718600 | tf_op jit(solution)/shard_map/ppermute | solution.py:59
  65.2 7.6 %collective-permute-start.15 = (bf16[2,2,128,1536]{3,2,1,0:T(8,128)(2,1)S(1)}, bf16[2,2,128,1536]{3,2,1,0:T(8,128)(2,1)}, u32[]{:S(2)}, u32[]{:S(2)}) collective-permute-start(bf16[2,2,128,1536]{3,2,1,0:T(8,128)(2,1)S(1)} %pad_maximum_fusion.1), channel_id=1, source_target_pairs={{0,32},{1,33},{2,34},{3,35},{4,36},{5,37},{6,38},{7,39},{8,40},{9,... | collective-permute-start | bytes 4718600 | tf_op jit(solution)/shard_map/ppermute | solution.py:59
  72.8 26.1 %all-gather.2.cloned.1.call-done = bf16[384,1536]{1,0:T(8,128)(2,1)} async-done(((bf16[96,1536]{1,0:T(8,128)(2,1)}), bf16[384,1536]{1,0:T(8,128)(2,1)}) %all-gather.2.cloned.1.call-update) | async-done | bytes 1179664 | tf_op jit(solution)/shard_map/all_gather | solution.py:326
  98.9 1.4 copy.8
  100.7 1.3 slice.22
  103.1 3.4 %collective-permute-start.13 = (bf16[2,128,1536]{2,1,0:T(8,128)(2,1)S(1)}, bf16[2,128,1536]{2,1,0:T(8,128)(2,1)S(1)}, u32[]{:S(2)}, u32[]{:S(2)}) collective-permute-start(bf16[2,128,1536]{2,1,0:T(8,128)(2,1)S(1)} %slice.23), channel_id=1, source_target_pairs={{0,32},{1,33},{2,34},{3,35},{4,36},{5,37},{6,38},{7,39},{8,40},{9,... | collective-permute-start | bytes 2359304 | tf_op jit(solution)/shard_map/ppermute | solution.py:59
  106.5 1.9 collective-permute-start.12
  108.4 7.0 %collective-permute-done.13.hd = bf16[2,128,1536]{2,1,0:T(8,128)(2,1)S(1)} collective-permute-done((bf16[2,128,1536]{2,1,0:T(8,128)(2,1)S(1)}, bf16[2,128,1536]{2,1,0:T(8,128)(2,1)S(1)}, u32[]{:S(2)}, u32[]{:S(2)}) %collective-permute-start.13) | collective-permute-done | bytes 786464 | tf_op jit(solution)/shard_map/ppermute | solution.py:59
  115.4 5.9 %collective-permute-done.12.hd = bf16[2,128,1536]{2,1,0:T(8,128)(2,1)S(1)} collective-permute-done((bf16[2,128,1536]{2,1,0:T(8,128)(2,1)S(1)}, bf16[2,128,1536]{2,1,0:T(8,128)(2,1)S(1)}, u32[]{:S(2)}, u32[]{:S(2)}) %collective-permute-start.12) | collective-permute-done | bytes 786464 | tf_op jit(solution)/shard_map/ppermute | solution.py:59
  121.9 2.6 %collective-permute-start.16 = (bf16[384,1536]{1,0:T(8,128)(2,1)S(1)}, bf16[384,1536]{1,0:T(8,128)(2,1)S(1)}, u32[]{:S(2)}, u32[]{:S(2)}) collective-permute-start(bf16[384,1536]{1,0:T(8,128)(2,1)S(1)} %collective-permute-done.11.refs_5_), channel_id=1, source_target_pairs={{0,4},{1,5},{2,6},{3,7},{4,8},{5,9},{6,10},{7,11},{8,12},{9,13},{1... | collective-permute-start | bytes 3538952 | tf_op jit(solution)/shard_map/ppermute | solution.py:59
  124.6 13.7 %attend.2 = (bf16[128,1536]{1,0:T(8,128)(2,1)}, bf16[128,1536]{1,0:T(8,128)(2,1)}, bf16[128,1536]{1,0:T(8,128)(2,1)}, bf16[128,1536]{1,0:T(8,128)(2,1)}) custom-call(s32[4]{0:T(128)} %get-tuple-element.96.meta, bf16[2,128,1536]{2,1,0:T(8,128)(2,1)} %bitcast.8.skv, bf16[1,128,1536]{2,1,0:T(8,128)(2,1)} %bitcast.73, bf16[3,128,1536]{2,1,0:T(8,128)(2,1)} %copy-done.11, ...), custom_call_target="tpu_custom_call" | custom-call | flops 6442450944 | bytes 10485760 | tf_op jit(solution)/shard_map/attend/pallas_call | solution.py:188
  138.3 2.5 %collective-permute-start.20 = (bf16[128,1536]{1,0:T(8,128)(2,1)}, bf16[128,1536]{1,0:T(8,128)(2,1)S(1)}, u32[]{:S(2)}, u32[]{:S(2)}) collective-permute-start(bf16[128,1536]{1,0:T(8,128)(2,1)} %get-tuple-element.119), channel_id=1, source_target_pairs={{28,0},{29,1},{30,2},{31,3},{0,4},{1,5},{2,6},{3,7},{4,8},{5,9},{6... | collective-permute-start | bytes 1179656 | tf_op jit(solution)/shard_map/ppermute | solution.py:59
  142.8 13.6 %attend.3 = (bf16[128,1536]{1,0:T(8,128)(2,1)}, bf16[128,1536]{1,0:T(8,128)(2,1)}, bf16[128,1536]{1,0:T(8,128)(2,1)}, bf16[128,1536]{1,0:T(8,128)(2,1)}) custom-call(s32[4]{0:T(128)} %get-tuple-element.96.meta, bf16[2,128,1536]{2,1,0:T(8,128)(2,1)} %bitcast.7.skv, bf16[1,128,1536]{2,1,0:T(8,128)(2,1)} %bitcast.72, bf16[3,128,1536]{2,1,0:T(8,128)(2,1)} %copy-done.8, ...), custom_call_target="tpu_custom_call" | custom-call | flops 6442450944 | bytes 10485760 | tf_op jit(solution)/shard_map/attend/pallas_call | solution.py:188
  156.5 2.3 %collective-permute-done.22.refs_3_ = bf16[128,1536]{1,0:T(8,128)(2,1)S(1)} collective-permute-done((bf16[128,1536]{1,0:T(8,128)(2,1)}, bf16[128,1536]{1,0:T(8,128)(2,1)S(1)}, u32[]{:S(2)}, u32[]{:S(2)}) %collective-permute-start.22) | collective-permute-done | bytes 393248 | tf_op jit(solution)/shard_map/ppermute | solution.py:59
  158.9 2.7 %collective-permute-start.26 = (bf16[384,1536]{1,0:T(8,128)(2,1)S(1)}, bf16[384,1536]{1,0:T(8,128)(2,1)S(1)}, u32[]{:S(2)}, u32[]{:S(2)}) collective-permute-start(bf16[384,1536]{1,0:T(8,128)(2,1)S(1)} %collective-permute-done.16.refs_6_), channel_id=1, source_target_pairs={{0,32},{1,33},{2,34},{3,35},{4,36},{5,37},{6,38},{7,39},{8,40},{9,... | collective-permute-start | bytes 3538952 | tf_op jit(solution)/shard_map/ppermute | solution.py:59
  161.9 2.2 %collective-permute-done.26.refs_10_ = bf16[384,1536]{1,0:T(8,128)(2,1)S(1)} collective-permute-done((bf16[384,1536]{1,0:T(8,128)(2,1)S(1)}, bf16[384,1536]{1,0:T(8,128)(2,1)S(1)}, u32[]{:S(2)}, u32[]{:S(2)}) %collective-permute-start.26) | collective-permute-done | bytes 1179680 | tf_op jit(solution)/shard_map/ppermute | solution.py:59
  164.1 1.7 collective-permute-done.27.refs_11_
  166.8 11.5 %project.2.refs_13_ = bf16[4,16,16,3072]{3,2,1,0:T(8,128)(2,1)} custom-call(s32[4]{0:T(128)} %get-tuple-element.96.meta, s32[4]{0:T(128)} %get-tuple-element.97.places, bf16[128,1536]{1,0:T(8,128)(2,1)} %get-tuple-element.141.refs_0_, bf16[128,1536]{1,0:T(8,128)(2,1)} %copy-done.15, bf16[128,1536]{1,0:T(8,128)(2,1)} %copy-done.16, ...), custom_call_target="tpu_custom_call" | custom-call | flops 4831838208 | bytes 17825792 | tf_op jit(solution)/shard_map/project/pallas_call | solution.py:271
  180.0 11.5 %project.3 = bf16[4,16,16,3072]{3,2,1,0:T(8,128)(2,1)} custom-call(s32[4]{0:T(128)} %get-tuple-element.96.meta, s32[4]{0:T(128)} %get-tuple-element.97.places, bf16[128,1536]{1,0:T(8,128)(2,1)} %get-tuple-element.133.refs_0_, bf16[128,1536]{1,0:T(8,128)(2,1)} %copy-done.12, bf16[128,1536]{1,0:T(8,128)(2,1)} %copy-done.13, ...), custom_call_target="tpu_custom_call", output_to_operand_aliasing={{}: (15, {})} | custom-call | flops 4831838208 | bytes 17825792 | tf_op jit(solution)/shard_map/project/pallas_call | solution.py:271
  (101 shorter events, 15.3 us)
Async XLA Ops:
  6.5 92.4 %all-gather.2.cloned.1.call-start = ((), (), s32[]{:S(2)}) async-start(), calls=%async_computation | async-start | bytes 1474560 | tf_op jit(solution)/shard_map/all_gather | solution.py:326
  9.2 27.6 %collective-permute-start.8 = (bf16[24,1536]{1,0:T(8,128)(2,1)S(1)}, bf16[24,1536]{1,0:T(8,128)(2,1)S(1)}, u32[]{:S(2)}, u32[]{:S(2)}) collective-permute-start(bf16[24,1536]{1,0:T(8,128)(2,1)S(1)} %bitcast.62), channel_id=1, source_target_pairs={{0,16},{1,17},{2,18},{3,19},{4,20},{5,21},{6,22},{7,23},{8,24},{9,... | collective-permute-start | bytes 221192 | tf_op jit(solution)/shard_map/ppermute | solution.py:59
  11.7 19.9 %collective-permute-start.7 = (bf16[24,1536]{1,0:T(8,128)(2,1)S(1)}, bf16[24,1536]{1,0:T(8,128)(2,1)S(1)}, u32[]{:S(2)}, u32[]{:S(2)}) collective-permute-start(bf16[24,1536]{1,0:T(8,128)(2,1)S(1)} %bitcast.63), channel_id=1, source_target_pairs={{0,64},{1,65},{2,66},{3,67},{4,68},{5,69},{6,70},{7,71},{8,72},{9,... | collective-permute-start | bytes 221192 | tf_op jit(solution)/shard_map/ppermute | solution.py:59
  15.0 14.7 %collective-permute-start.6 = (bf16[24,1536]{1,0:T(8,128)(2,1)S(1)}, bf16[24,1536]{1,0:T(8,128)(2,1)S(1)}, u32[]{:S(2)}, u32[]{:S(2)}) collective-permute-start(bf16[24,1536]{1,0:T(8,128)(2,1)S(1)} %bitcast.64), channel_id=1, source_target_pairs={{0,80},{1,81},{2,82},{3,83},{4,84},{5,85},{6,86},{7,87},{8,88},{9,... | collective-permute-start | bytes 221192 | tf_op jit(solution)/shard_map/ppermute | solution.py:59
  15.7 21.9 %collective-permute-start = (bf16[3,128,1536]{2,1,0:T(8,128)(2,1)}, bf16[3,128,1536]{2,1,0:T(8,128)(2,1)S(1)}, u32[]{:S(2)}, u32[]{:S(2)}) collective-permute-start(bf16[3,128,1536]{2,1,0:T(8,128)(2,1)} %bitcast.69), channel_id=1, source_target_pairs={{0,4},{1,5},{2,6},{3,7},{4,8},{5,9},{6,10},{7,11},{8,12},{9,13},{1... | collective-permute-start | bytes 3538952 | tf_op jit(solution)/shard_map/ppermute | solution.py:59
  18.7 19.0 %collective-permute-start.1 = (bf16[3,128,1536]{2,1,0:T(8,128)(2,1)}, bf16[3,128,1536]{2,1,0:T(8,128)(2,1)S(1)}, u32[]{:S(2)}, u32[]{:S(2)}) collective-permute-start(bf16[3,128,1536]{2,1,0:T(8,128)(2,1)} %bitcast.68), channel_id=1, source_target_pairs={{0,1},{1,2},{2,3},{3,0},{4,5},{5,6},{6,7},{7,4},{8,9},{9,10},{10,1... | collective-permute-start | bytes 3538952 | tf_op jit(solution)/shard_map/ppermute | solution.py:59
  29.7 27.7 %collective-permute-start.4 = (bf16[2,128,1536]{2,1,0:T(8,128)(2,1)}, bf16[2,128,1536]{2,1,0:T(8,128)(2,1)S(1)}, u32[]{:S(2)}, u32[]{:S(2)}) collective-permute-start(bf16[2,128,1536]{2,1,0:T(8,128)(2,1)} %bitcast.7.skv), channel_id=1, source_target_pairs={{32,0},{33,1},{34,2},{35,3},{36,4},{37,5},{38,6},{39,7},{40,8},{41... | collective-permute-start | bytes 2359304 | tf_op jit(solution)/shard_map/ppermute | solution.py:59
  31.6 27.0 %collective-permute-start.5 = (bf16[2,128,1536]{2,1,0:T(8,128)(2,1)}, bf16[2,128,1536]{2,1,0:T(8,128)(2,1)}, u32[]{:S(2)}, u32[]{:S(2)}) collective-permute-start(bf16[2,128,1536]{2,1,0:T(8,128)(2,1)} %bitcast.8.skv), channel_id=1, source_target_pairs={{0,32},{1,33},{2,34},{3,35},{4,36},{5,37},{6,38},{7,39},{8,40},{9,... | collective-permute-start | bytes 2359304 | tf_op jit(solution)/shard_map/ppermute | solution.py:59
  37.6 16.5 %collective-permute-start.3 = (bf16[3,128,1536]{2,1,0:T(8,128)(2,1)}, bf16[3,128,1536]{2,1,0:T(8,128)(2,1)S(1)}, u32[]{:S(2)}, u32[]{:S(2)}) collective-permute-start(bf16[3,128,1536]{2,1,0:T(8,128)(2,1)} %bitcast.71), channel_id=1, source_target_pairs={{0,3},{1,0},{2,1},{3,2},{4,7},{5,4},{6,5},{7,6},{8,11},{9,8},{10,9... | collective-permute-start | bytes 3538952 | tf_op jit(solution)/shard_map/ppermute | solution.py:59
  37.7 17.3 %collective-permute-start.2 = (bf16[3,128,1536]{2,1,0:T(8,128)(2,1)S(1)}, bf16[3,128,1536]{2,1,0:T(8,128)(2,1)S(1)}, u32[]{:S(2)}, u32[]{:S(2)}) collective-permute-start(bf16[3,128,1536]{2,1,0:T(8,128)(2,1)S(1)} %bitcast.70), channel_id=1, source_target_pairs={{0,28},{1,29},{2,30},{3,31},{4,0},{5,1},{6,2},{7,3},{8,4},{9,5},{1... | collective-permute-start | bytes 3538952 | tf_op jit(solution)/shard_map/ppermute | solution.py:59
  58.7 41.7 %collective-permute-start.9 = (bf16[3,128,1536]{2,1,0:T(8,128)(2,1)}, bf16[3,128,1536]{2,1,0:T(8,128)(2,1)}, u32[]{:S(2)}, u32[]{:S(2)}) collective-permute-start(bf16[3,128,1536]{2,1,0:T(8,128)(2,1)} %bitcast.67), channel_id=1, source_target_pairs={{0,5},{1,6},{2,7},{3,4},{4,9},{5,10},{6,11},{7,8},{8,13},{9,14},{1... | collective-permute-start | bytes 3538952 | tf_op jit(solution)/shard_map/ppermute | solution.py:59
  59.8 40.6 %collective-permute-start.10 = (bf16[3,128,1536]{2,1,0:T(8,128)(2,1)}, bf16[3,128,1536]{2,1,0:T(8,128)(2,1)}, u32[]{:S(2)}, u32[]{:S(2)}) collective-permute-start(bf16[3,128,1536]{2,1,0:T(8,128)(2,1)} %bitcast.66), channel_id=1, source_target_pairs={{0,31},{1,28},{2,29},{3,30},{4,3},{5,0},{6,1},{7,2},{8,7},{9,4},{1... | collective-permute-start | bytes 3538952 | tf_op jit(solution)/shard_map/ppermute | solution.py:59
  61.1 47.3 %collective-permute-start.14 = (bf16[2,2,128,1536]{3,2,1,0:T(8,128)(2,1)S(1)}, bf16[2,2,128,1536]{3,2,1,0:T(8,128)(2,1)}, u32[]{:S(2)}, u32[]{:S(2)}) collective-permute-start(bf16[2,2,128,1536]{3,2,1,0:T(8,128)(2,1)S(1)} %pad_maximum_fusion), channel_id=1, source_target_pairs={{32,0},{33,1},{34,2},{35,3},{36,4},{37,5},{38,6},{39,7},{40,8},{41... | collective-permute-start | bytes 4718600 | tf_op jit(solution)/shard_map/ppermute | solution.py:59
  65.2 43.2 %collective-permute-start.15 = (bf16[2,2,128,1536]{3,2,1,0:T(8,128)(2,1)S(1)}, bf16[2,2,128,1536]{3,2,1,0:T(8,128)(2,1)}, u32[]{:S(2)}, u32[]{:S(2)}) collective-permute-start(bf16[2,2,128,1536]{3,2,1,0:T(8,128)(2,1)S(1)} %pad_maximum_fusion.1), channel_id=1, source_target_pairs={{0,32},{1,33},{2,34},{3,35},{4,36},{5,37},{6,38},{7,39},{8,40},{9,... | collective-permute-start | bytes 4718600 | tf_op jit(solution)/shard_map/ppermute | solution.py:59
  100.3 24.2 %copy-start = (bf16[4,4,24,1536]{3,2,1,0:T(8,128)(2,1)}, bf16[4,4,24,1536]{3,2,1,0:T(8,128)(2,1)S(1)}, u32[]{:S(2)}) copy-start(bf16[4,4,24,1536]{3,2,1,0:T(8,128)(2,1)S(1)} %copy.8) | copy-start | bytes 3538948
  100.4 21.0 %collective-permute-start.11 = (bf16[384,1536]{1,0:T(8,128)(2,1)S(1)}, bf16[384,1536]{1,0:T(8,128)(2,1)S(1)}, u32[]{:S(2)}, u32[]{:S(2)}) collective-permute-start(bf16[384,1536]{1,0:T(8,128)(2,1)S(1)} %bitcast.55), channel_id=1, source_target_pairs={{0,4},{1,5},{2,6},{3,7},{4,8},{5,9},{6,10},{7,11},{8,12},{9,13},{1... | collective-permute-start | bytes 3538952 | tf_op jit(solution)/shard_map/ppermute | solution.py:59
  103.1 12.3 %collective-permute-start.13 = (bf16[2,128,1536]{2,1,0:T(8,128)(2,1)S(1)}, bf16[2,128,1536]{2,1,0:T(8,128)(2,1)S(1)}, u32[]{:S(2)}, u32[]{:S(2)}) collective-permute-start(bf16[2,128,1536]{2,1,0:T(8,128)(2,1)S(1)} %slice.23), channel_id=1, source_target_pairs={{0,32},{1,33},{2,34},{3,35},{4,36},{5,37},{6,38},{7,39},{8,40},{9,... | collective-permute-start | bytes 2359304 | tf_op jit(solution)/shard_map/ppermute | solution.py:59
  106.5 14.8 %collective-permute-start.12 = (bf16[2,128,1536]{2,1,0:T(8,128)(2,1)S(1)}, bf16[2,128,1536]{2,1,0:T(8,128)(2,1)S(1)}, u32[]{:S(2)}, u32[]{:S(2)}) collective-permute-start(bf16[2,128,1536]{2,1,0:T(8,128)(2,1)S(1)} %slice.22), channel_id=1, source_target_pairs={{32,0},{33,1},{34,2},{35,3},{36,4},{37,5},{38,6},{39,7},{40,8},{41... | collective-permute-start | bytes 2359304 | tf_op jit(solution)/shard_map/ppermute | solution.py:59
  121.3 16.9 %collective-permute-start.19 = (bf16[384,1536]{1,0:T(8,128)(2,1)S(1)}, bf16[384,1536]{1,0:T(8,128)(2,1)S(1)}, u32[]{:S(2)}, u32[]{:S(2)}) collective-permute-start(bf16[384,1536]{1,0:T(8,128)(2,1)S(1)} %collective-permute-done.11.refs_5_), channel_id=1, source_target_pairs={{0,32},{1,33},{2,34},{3,35},{4,36},{5,37},{6,38},{7,39},{8,40},{9,... | collective-permute-start | bytes 3538952 | tf_op jit(solution)/shard_map/ppermute | solution.py:59
  121.4 16.8 %collective-permute-start.18 = (bf16[384,1536]{1,0:T(8,128)(2,1)S(1)}, bf16[384,1536]{1,0:T(8,128)(2,1)S(1)}, u32[]{:S(2)}, u32[]{:S(2)}) collective-permute-start(bf16[384,1536]{1,0:T(8,128)(2,1)S(1)} %bitcast.56), channel_id=1, source_target_pairs={{0,32},{1,33},{2,34},{3,35},{4,36},{5,37},{6,38},{7,39},{8,40},{9,... | collective-permute-start | bytes 3538952 | tf_op jit(solution)/shard_map/ppermute | solution.py:59
  121.9 34.6 %collective-permute-start.16 = (bf16[384,1536]{1,0:T(8,128)(2,1)S(1)}, bf16[384,1536]{1,0:T(8,128)(2,1)S(1)}, u32[]{:S(2)}, u32[]{:S(2)}) collective-permute-start(bf16[384,1536]{1,0:T(8,128)(2,1)S(1)} %collective-permute-done.11.refs_5_), channel_id=1, source_target_pairs={{0,4},{1,5},{2,6},{3,7},{4,8},{5,9},{6,10},{7,11},{8,12},{9,13},{1... | collective-permute-start | bytes 3538952 | tf_op jit(solution)/shard_map/ppermute | solution.py:59
  124.5 31.9 %collective-permute-start.17 = (bf16[384,1536]{1,0:T(8,128)(2,1)S(1)}, bf16[384,1536]{1,0:T(8,128)(2,1)S(1)}, u32[]{:S(2)}, u32[]{:S(2)}) collective-permute-start(bf16[384,1536]{1,0:T(8,128)(2,1)S(1)} %bitcast.57), channel_id=1, source_target_pairs={{0,12},{1,13},{2,14},{3,15},{4,0},{5,1},{6,2},{7,3},{8,4},{9,5},{1... | collective-permute-start | bytes 3538952 | tf_op jit(solution)/shard_map/ppermute | solution.py:59
  138.2 18.2 %copy-start.2 = (bf16[384,1536]{1,0:T(8,128)(2,1)}, bf16[384,1536]{1,0:T(8,128)(2,1)S(1)}, u32[]{:S(2)}) copy-start(bf16[384,1536]{1,0:T(8,128)(2,1)S(1)} %collective-permute-done.19.refs_9_) | copy-start | bytes 3538948
  138.3 18.2 %copy-start.3 = (bf16[384,1536]{1,0:T(8,128)(2,1)}, bf16[384,1536]{1,0:T(8,128)(2,1)S(1)}, u32[]{:S(2)}) copy-start(bf16[384,1536]{1,0:T(8,128)(2,1)S(1)} %collective-permute-done.18.refs_8_) | copy-start | bytes 3538948
  138.3 18.2 %collective-permute-start.20 = (bf16[128,1536]{1,0:T(8,128)(2,1)}, bf16[128,1536]{1,0:T(8,128)(2,1)S(1)}, u32[]{:S(2)}, u32[]{:S(2)}) collective-permute-start(bf16[128,1536]{1,0:T(8,128)(2,1)} %get-tuple-element.119), channel_id=1, source_target_pairs={{28,0},{29,1},{30,2},{31,3},{0,4},{1,5},{2,6},{3,7},{4,8},{5,9},{6... | collective-permute-start | bytes 1179656 | tf_op jit(solution)/shard_map/ppermute | solution.py:59
  140.8 15.8 %collective-permute-start.21 = (bf16[128,1536]{1,0:T(8,128)(2,1)}, bf16[128,1536]{1,0:T(8,128)(2,1)S(1)}, u32[]{:S(2)}, u32[]{:S(2)}) collective-permute-start(bf16[128,1536]{1,0:T(8,128)(2,1)} %get-tuple-element.120), channel_id=1, source_target_pairs={{3,0},{0,1},{1,2},{2,3},{7,4},{4,5},{5,6},{6,7},{11,8},{8,9},{9,10... | collective-permute-start | bytes 1179656 | tf_op jit(solution)/shard_map/ppermute | solution.py:59
  141.8 17.1 %collective-permute-start.22 = (bf16[128,1536]{1,0:T(8,128)(2,1)}, bf16[128,1536]{1,0:T(8,128)(2,1)S(1)}, u32[]{:S(2)}, u32[]{:S(2)}) collective-permute-start(bf16[128,1536]{1,0:T(8,128)(2,1)} %get-tuple-element.121), channel_id=1, source_target_pairs={{31,0},{28,1},{29,2},{30,3},{3,4},{0,5},{1,6},{2,7},{7,8},{4,9},{5... | collective-permute-start | bytes 1179656 | tf_op jit(solution)/shard_map/ppermute | solution.py:59
  158.9 5.2 %collective-permute-start.26 = (bf16[384,1536]{1,0:T(8,128)(2,1)S(1)}, bf16[384,1536]{1,0:T(8,128)(2,1)S(1)}, u32[]{:S(2)}, u32[]{:S(2)}) collective-permute-start(bf16[384,1536]{1,0:T(8,128)(2,1)S(1)} %collective-permute-done.16.refs_6_), channel_id=1, source_target_pairs={{0,32},{1,33},{2,34},{3,35},{4,36},{5,37},{6,38},{7,39},{8,40},{9,... | collective-permute-start | bytes 3538952 | tf_op jit(solution)/shard_map/ppermute | solution.py:59
  161.6 4.2 %collective-permute-start.27 = (bf16[384,1536]{1,0:T(8,128)(2,1)S(1)}, bf16[384,1536]{1,0:T(8,128)(2,1)S(1)}, u32[]{:S(2)}, u32[]{:S(2)}) collective-permute-start(bf16[384,1536]{1,0:T(8,128)(2,1)S(1)} %collective-permute-done.17.refs_7_), channel_id=1, source_target_pairs={{0,32},{1,33},{2,34},{3,35},{4,36},{5,37},{6,38},{7,39},{8,40},{9,... | collective-permute-start | bytes 3538952 | tf_op jit(solution)/shard_map/ppermute | solution.py:59
  161.6 16.8 %collective-permute-start.23 = (bf16[128,1536]{1,0:T(8,128)(2,1)}, bf16[128,1536]{1,0:T(8,128)(2,1)S(1)}, u32[]{:S(2)}, u32[]{:S(2)}) collective-permute-start(bf16[128,1536]{1,0:T(8,128)(2,1)} %get-tuple-element.134), channel_id=1, source_target_pairs={{4,0},{5,1},{6,2},{7,3},{8,4},{9,5},{10,6},{11,7},{12,8},{13,9},{1... | collective-permute-start | bytes 1179656 | tf_op jit(solution)/shard_map/ppermute | solution.py:59
  161.6 16.8 %collective-permute-start.24 = (bf16[128,1536]{1,0:T(8,128)(2,1)}, bf16[128,1536]{1,0:T(8,128)(2,1)S(1)}, u32[]{:S(2)}, u32[]{:S(2)}) collective-permute-start(bf16[128,1536]{1,0:T(8,128)(2,1)} %get-tuple-element.135), channel_id=1, source_target_pairs={{1,0},{2,1},{3,2},{0,3},{5,4},{6,5},{7,6},{4,7},{9,8},{10,9},{11,1... | collective-permute-start | bytes 1179656 | tf_op jit(solution)/shard_map/ppermute | solution.py:59
  161.9 16.5 %collective-permute-start.25 = (bf16[128,1536]{1,0:T(8,128)(2,1)}, bf16[128,1536]{1,0:T(8,128)(2,1)S(1)}, u32[]{:S(2)}, u32[]{:S(2)}) collective-permute-start(bf16[128,1536]{1,0:T(8,128)(2,1)} %get-tuple-element.136), channel_id=1, source_target_pairs={{5,0},{6,1},{7,2},{4,3},{9,4},{10,5},{11,6},{8,7},{13,8},{14,9},{1... | collective-permute-start | bytes 1179656 | tf_op jit(solution)/shard_map/ppermute | solution.py:59
  (21 other events, 108.0 us)
Sparse Core Ops, SparseCore 0:
  58.8 40.1 all-gather.1

commit v12 on v9

--- a/solution.py
+++ b/solution.py
@@ -136,7 +136,7 @@
     alive[...] = jnp.where(live, 1.0, 0.0)
 
 
-def attend_kernel(half, meta, skv, sq, x, y, d, h3, hd, o0, o1, o2, o3, kaug, vaug, qaug, alive):
+def attend_kernel(half, meta, skv, sq, x, y, d, hs, h2, hd, o0, o1, o2, o3, kaug, vaug, qaug, alive):
     outs = (o0, o1, o2, o3)
 
     @pl.when(pl.program_id(0) == 0)
@@ -147,7 +147,7 @@
             qaug[n, :, HS:] = qaug[0, :, HS:]
         vaug[:, :, HS:] = jnp.ones((STEP, 1024, HS), jnp.bfloat16)
 
-    keys = (skv, x, y, d, h3.at[0], h3.at[1], h3.at[2], hd)
+    keys = (skv, x, y, d, hs, h2.at[0], h2.at[1], hd)
     asks = (sq.at[0], x.at[2], y.at[2], d.at[2])
     for h in range(STEP):
         lanes = pl.ds(h * HS, HS)
@@ -204,7 +204,8 @@
 
 
 def project_kernel(meta, places, *refs):
-    attended, own, other, (tokens, out, lhs, held, sems) = refs[:8], refs[8:12], refs[12:16], refs[16:]
+    attended, own, (s0, s13, s2), (tokens, out, lhs, held, sems) = refs[:8], refs[8:12], refs[12:15], refs[15:]
+    other = (s0, s13.at[0], s2, s13.at[1])
     step = pl.program_id(0)
     core, x = lax.rem(meta[0], 2), lax.rem(meta[1], 4)
 
@@ -259,7 +260,7 @@
         num_scalar_prefetch=2,
         grid=(D // TILE,),
         in_specs=[pl.BlockSpec((128, HD), lambda t, m, p: (0, 0))] * 8
-        + [pl.BlockSpec(memory_space=pl.ANY)] * 8
+        + [pl.BlockSpec(memory_space=pl.ANY)] * 7
         + [pl.BlockSpec((4, 16, 16, TILE), lambda t, m, p: (0, 0, 0, p[t]))],
         out_specs=pl.BlockSpec((4, 16, 16, TILE), lambda t, m, p: (0, 0, 0, p[t])),
         scratch_shapes=[
@@ -309,31 +310,35 @@
     x0, y0, frame, shard = together(x0, y0, frame, shard)
     x0, y0 = go(x0, 0, row), go(y0, 0, col)
     shards = [send(shard, shift_pairs(dz=n)) for n in (1, 2, 3)]
-    x1, y1 = pack(((1, 1, "kvq"), (1, 2, "kvq")), frame, *arrays)
-    x1, y1, frame, *shards = together(x1, y1, frame, *shards)
+    frame, *shards = together(frame, *shards)
+    skv0, skv1, x1, y1 = pack(((0, 0, "kv"), (1, 0, "kv"), (1, 1, "kvq"), (1, 2, "kvq")), frame, *arrays)
+    skv0, skv1, x1, y1, frame = together(skv0, skv1, x1, y1, frame)
+    downs, ups = down(skv0), up(skv1)
     x1, y1 = go(x1, 1, row), go(y1, 1, col)
-    skv0, skv1, d0, d1, sq0, sq1 = pack(
-        ((0, 0, "kv"), (1, 0, "kv"), (0, 3, "kvq"), (1, 3, "kvq"), (0, 0, "q"), (1, 0, "q")), frame, *arrays
+    d0, d1, sq0, sq1 = pack(((0, 3, "kvq"), (1, 3, "kvq"), (0, 0, "q"), (1, 0, "q")), frame, *arrays)
+    strip = ring_order(shard, *shards, (f >> 1) * 2 + (r >> 2))
+    h0, h1 = jnp.stack([x0[:2], y0[:2]]), jnp.stack([x1[:2], y1[:2]])
+    d0, d1, h0, h1, x0, y0, x1, y1, downs, ups, meta, places, strip = together(
+        d0, d1, h0, h1, x0, y0, x1, y1, downs, ups, meta, places, strip
     )
-    strip = ring_order(shard, *shards, (f >> 1) * 2 + (r >> 2))
-    strips = [send(strip, shift_pairs(dy=n)) for n in (1, 2, 3)]
-    h0, h1 = jnp.stack([skv0, x0[:2], y0[:2]]), jnp.stack([skv1, x1[:2], y1[:2]])
-    d0, d1, h0, h1, x0, y0, x1, y1, meta, places, *strips = together(d0, d1, h0, h1, x0, y0, x1, y1, meta, places, *strips)
-    d0, d1, down3, up3 = go(d0, 0, both), go(d1, 1, both), down(h0), up(h1)
-    c0 = ring_order(strip, *strips, c).swapaxes(0, 1).reshape(384, HD)
-    c0, d0, d1 = together(c0, d0, d1)
-    downd, upd, c1 = down(d0[:2]), up(d1[:2]), turn(c0)
-    c0, c1, downd, upd, down3, up3 = together(c0, c1, downd, upd, down3, up3)
-
-    c2, c3, s0, s1 = turn(c1), turn(c0, -1), swap(c0), swap(c1)
-    mixed1 = attend(1, meta, skv1, sq1, x1, y1, d1, down3, downd)
-    s0, s1, skv0, *mixed1 = together(s0, s1, skv0, *mixed1)
-    attended1 = back(1, mixed1)
-    mixed0 = attend(0, meta, skv0, sq0, x0, y0, d0, up3, upd)
-    c2, c3, *rest = together(c2, c3, *attended1, *mixed0)
+    d0, d1, down2, up2 = go(d0, 0, both), go(d1, 1, both), down(h0), up(h1)
+    strips = lax.all_gather(strip.reshape(96, HD), "col", axis=0, tiled=True)
+    c0 = strips.reshape(4, 4, 24, HD).swapaxes(0, 1).reshape(384, HD)
+    downd, upd = down(d0[:2]), up(d1[:2])
+    c0, down2 = together(c0, down2)
+    c1 = turn(c0)
+    c0, downd, upd, down2, up2 = together(c0, downd, upd, down2, up2)
+
+    c3, s0 = turn(c0, -1), swap(c0)
+    mixed1 = attend(1, meta, skv1, sq1, x1, y1, d1, downs, down2, downd)
+    c1, s0, skv0, *mixed1 = together(c1, s0, skv0, *mixed1)
+    attended1, c2 = back(1, mixed1), turn(c1)
+    mixed0 = attend(0, meta, skv0, sq0, x0, y0, d0, ups, up2, upd)
+    c1, c3, *rest = together(c1, c3, *attended1, *mixed0)
     attended1, mixed0 = rest[:4], rest[4:]
-    attended0, s2, s3 = back(0, mixed0), swap(c2), swap(c3)
-    return project(attended0 + attended1, meta, places, (c0, c1, c2, c3, s0, s1, s2, s3), tokens_in)
+    attended0, s13 = back(0, mixed0), swap(jnp.stack([c1, c3]))
+    c2, s13, *attended0 = together(c2, s13, *attended0)
+    return project(attended0 + attended1, meta, places, (c0, c1, c2, c3, s0, s13, swap(c2)), tokens_in)
 
 
 def solution(mesh):

time: 196 us -> 218 us (1.11)
  starting transfers between devices: 40.9 us -> 83 us
  waiting for transfers between devices: 92.6 us -> 53 us
  between operations: 0.68 us -> 13.9 us
  local copies, waits for them, and re-layouts: 5.36 us -> 11.8 us
    ppermute x29 -> x27, starting transfers between devices: 40.9 us -> 83 us  [send(): return lax.ppermute(value, AXES, pairs)]
    ppermute x29 -> x27, waiting for transfers between devices: 92.6 us -> 53 us  [send(): return lax.ppermute(value, AXES, pairs)]
    slice x2, local copies, waits for them, and re-layouts: 0.1 us -> 4.14 us  [local(): downd, upd = (down(d0[:2]), up(d1[:2]))]
    unnamed x64 -> x58, local copies, waits for them, and re-layouts: 4.8 us -> 5.3 us
  transfers between devices with their start and end apart: 29 -> 28, of which waited for: 11 -> 8; matrix products, arithmetic and copies ran while one was open for 2% -> 4% of each run, Pallas kernels for 17% -> 15%
where the time goes in v12:
time: 218 us; the launch traced here: 217 us
  starting transfers between devices  83 us (38%)
  Pallas kernels  53.2 us (24%)
  waiting for transfers between devices  53 us (24%)
  between operations  13.9 us (6%)
  local copies, waits for them, and re-layouts  11.8 us (5%)
  other arithmetic  2.44 us (1%)
    ppermute x27, starting transfers between devices, send(): return lax.ppermute(value, AXES, pairs)  83 us
    ppermute x27, waiting for transfers between devices, send(): return lax.ppermute(value, AXES, pairs)  53 us
    pallas_call x2, Pallas kernels, attend(): pl.pallas_call(functools.partial(attend_kernel, half), grid=(H // STEP,),...  27.3 us
    pallas_call x1, Pallas kernels, project(): pl.pallas_call(project_kernel, grid_spec=grid_spec, out_shape=jax.ShapeDt...  16.9 us
    pallas_call x3, Pallas kernels, pack(): pl.pallas_call(functools.partial(pack_kernel, parts), out_shape=[jax.Shap...  8.96 us
    unnamed x58, local copies, waits for them, and re-layouts  5.3 us
  transfers between devices with their start and end apart: 28, of which 8 were waited for; matrix products, arithmetic and copies ran while one was open for 4% of the time, Pallas kernels for 15%

profile of v12, /device:TPU:1, one launch (start us, length us, event | category | flops | bytes accessed | tf_op | source)
XLA Modules:
  0.0 217.4 jit_solution(6967111353580195091)
XLA Ops:
  6.5 2.6 %pack.3 = (bf16[3,2,8,8,1536]{4,3,2,1,0:T(8,128)(2,1)}, bf16[3,2,8,8,1536]{4,3,2,1,0:T(8,128)(2,1)}) custom-call(s32[1]{0:T(128)} %bitcast.meta, bf16[4,2,8,2,8,1536]{5,4,3,2,1,0:T(8,128)(2,1)} %bitcast.48, bf16[4,2,8,2,8,1536]{5,4,3,2,1,0:T(8,128)(2,1)} %bitcast.51, bf16[4,2,8,2,8,1536]{5,4,3,2,1,0:T(8,128)(2,1)} %bitcast.54), custom_call_target="tpu_custom_call" | custom-call | bytes 6291456 | tf_op jit(solution)/shard_map/pack/pallas_call | solution.py:98
  9.2 2.5 %collective-permute-start = (bf16[24,1536]{1,0:T(8,128)(2,1)S(1)}, bf16[24,1536]{1,0:T(8,128)(2,1)S(1)}, u32[]{:S(2)}, u32[]{:S(2)}) collective-permute-start(bf16[24,1536]{1,0:T(8,128)(2,1)S(1)} %bitcast.65), channel_id=1, source_target_pairs={{0,16},{1,17},{2,18},{3,19},{4,20},{5,21},{6,22},{7,23},{8,24},{9,... | collective-permute-start | bytes 221192 | tf_op jit(solution)/shard_map/ppermute | solution.py:59
  11.7 3.3 %collective-permute-start.1 = (bf16[24,1536]{1,0:T(8,128)(2,1)S(1)}, bf16[24,1536]{1,0:T(8,128)(2,1)S(1)}, u32[]{:S(2)}, u32[]{:S(2)}) collective-permute-start(bf16[24,1536]{1,0:T(8,128)(2,1)S(1)} %bitcast.66), channel_id=1, source_target_pairs={{0,64},{1,65},{2,66},{3,67},{4,68},{5,69},{6,70},{7,71},{8,72},{9,... | collective-permute-start | bytes 221192 | tf_op jit(solution)/shard_map/ppermute | solution.py:59
  15.7 2.7 %collective-permute-start.4 = (bf16[3,128,1536]{2,1,0:T(8,128)(2,1)}, bf16[3,128,1536]{2,1,0:T(8,128)(2,1)S(1)}, u32[]{:S(2)}, u32[]{:S(2)}) collective-permute-start(bf16[3,128,1536]{2,1,0:T(8,128)(2,1)} %bitcast.70), channel_id=1, source_target_pairs={{0,1},{1,2},{2,3},{3,0},{4,5},{5,6},{6,7},{7,4},{8,9},{9,10},{10,1... | collective-permute-start | bytes 3538952 | tf_op jit(solution)/shard_map/ppermute | solution.py:59
  18.5 2.9 %collective-permute-start.3 = (bf16[3,128,1536]{2,1,0:T(8,128)(2,1)}, bf16[3,128,1536]{2,1,0:T(8,128)(2,1)S(1)}, u32[]{:S(2)}, u32[]{:S(2)}) collective-permute-start(bf16[3,128,1536]{2,1,0:T(8,128)(2,1)} %bitcast.69), channel_id=1, source_target_pairs={{0,4},{1,5},{2,6},{3,7},{4,8},{5,9},{6,10},{7,11},{8,12},{9,13},{1... | collective-permute-start | bytes 3538952 | tf_op jit(solution)/shard_map/ppermute | solution.py:59
  22.0 1.3 pad_add_fusion
  23.4 3.5 %pack.4 = (bf16[2,2,8,8,1536]{4,3,2,1,0:T(8,128)(2,1)}, bf16[2,2,8,8,1536]{4,3,2,1,0:T(8,128)(2,1)}, bf16[3,2,8,8,1536]{4,3,2,1,0:T(8,128)(2,1)}, bf16[3,2,8,8,1536]{4,3,2,1,0:T(8,128)(2,1)}) custom-call(s32[1]{0:T(128)} %bitcast.meta, bf16[4,2,8,2,8,1536]{5,4,3,2,1,0:T(8,128)(2,1)} %bitcast.49, bf16[4,2,8,2,8,1536]{5,4,3,2,1,0:T(8,128)(2,1)} %bitcast.52, ...), custom_call_target="tpu_custom_call" | custom-call | bytes 10485760 | tf_op jit(solution)/shard_map/pack/pallas_call | solution.py:98
  27.1 2.9 %pack.5 = (bf16[3,2,8,8,1536]{4,3,2,1,0:T(8,128)(2,1)}, bf16[3,2,8,8,1536]{4,3,2,1,0:T(8,128)(2,1)}, bf16[1,2,8,8,1536]{4,3,2,1,0:T(8,128)(2,1)}, bf16[1,2,8,8,1536]{4,3,2,1,0:T(8,128)(2,1)}) custom-call(s32[1]{0:T(128)} %bitcast.meta, bf16[4,2,8,2,8,1536]{5,4,3,2,1,0:T(8,128)(2,1)} %bitcast.50, bf16[4,2,8,2,8,1536]{5,4,3,2,1,0:T(8,128)(2,1)} %bitcast.53, ...), custom_call_target="tpu_custom_call" | custom-call | bytes 8388608 | tf_op jit(solution)/shard_map/pack/pallas_call | solution.py:98
  30.0 4.9 %collective-permute-start.7 = (bf16[2,128,1536]{2,1,0:T(8,128)(2,1)S(1)}, bf16[2,128,1536]{2,1,0:T(8,128)(2,1)S(1)}, u32[]{:S(2)}, u32[]{:S(2)}) collective-permute-start(bf16[2,128,1536]{2,1,0:T(8,128)(2,1)S(1)} %bitcast.74), channel_id=1, source_target_pairs={{32,0},{33,1},{34,2},{35,3},{36,4},{37,5},{38,6},{39,7},{40,8},{41... | collective-permute-start | bytes 2359304 | tf_op jit(solution)/shard_map/ppermute | solution.py:59
  35.7 4.4 %collective-permute-start.8 = (bf16[2,128,1536]{2,1,0:T(8,128)(2,1)S(1)}, bf16[2,128,1536]{2,1,0:T(8,128)(2,1)S(1)}, u32[]{:S(2)}, u32[]{:S(2)}) collective-permute-start(bf16[2,128,1536]{2,1,0:T(8,128)(2,1)S(1)} %bitcast.76), channel_id=1, source_target_pairs={{0,32},{1,33},{2,34},{3,35},{4,36},{5,37},{6,38},{7,39},{8,40},{9,... | collective-permute-start | bytes 2359304 | tf_op jit(solution)/shard_map/ppermute | solution.py:59
  41.5 5.3 %collective-permute-done.6.y = bf16[3,128,1536]{2,1,0:T(8,128)(2,1)S(1)} collective-permute-done((bf16[3,128,1536]{2,1,0:T(8,128)(2,1)}, bf16[3,128,1536]{2,1,0:T(8,128)(2,1)S(1)}, u32[]{:S(2)}, u32[]{:S(2)}) %collective-permute-start.6) | collective-permute-done | bytes 1179680 | tf_op jit(solution)/shard_map/ppermute | solution.py:59
  46.9 2.5 %collective-permute-done.5.x = bf16[3,128,1536]{2,1,0:T(8,128)(2,1)S(1)} collective-permute-done((bf16[3,128,1536]{2,1,0:T(8,128)(2,1)}, bf16[3,128,1536]{2,1,0:T(8,128)(2,1)S(1)}, u32[]{:S(2)}, u32[]{:S(2)}) %collective-permute-start.5) | collective-permute-done | bytes 1179680 | tf_op jit(solution)/shard_map/ppermute | solution.py:59
  50.4 6.8 %collective-permute-done.7.hs = bf16[2,128,1536]{2,1,0:T(8,128)(2,1)S(1)} collective-permute-done((bf16[2,128,1536]{2,1,0:T(8,128)(2,1)S(1)}, bf16[2,128,1536]{2,1,0:T(8,128)(2,1)S(1)}, u32[]{:S(2)}, u32[]{:S(2)}) %collective-permute-start.7) | collective-permute-done | bytes 786464 | tf_op jit(solution)/shard_map/ppermute | solution.py:59
  58.4 2.5 %collective-permute-start.11 = (bf16[3,128,1536]{2,1,0:T(8,128)(2,1)}, bf16[3,128,1536]{2,1,0:T(8,128)(2,1)}, u32[]{:S(2)}, u32[]{:S(2)}) collective-permute-start(bf16[3,128,1536]{2,1,0:T(8,128)(2,1)} %bitcast.11), channel_id=1, source_target_pairs={{0,5},{1,6},{2,7},{3,4},{4,9},{5,10},{6,11},{7,8},{8,13},{9,14},{1... | collective-permute-start | bytes 3538952 | tf_op jit(solution)/shard_map/ppermute | solution.py:59
  60.8 1.9 collective-permute-start.9
  62.8 34.0 %collective-permute-start.15 = (bf16[2,2,128,1536]{3,2,1,0:T(8,128)(2,1)S(1)}, bf16[2,2,128,1536]{3,2,1,0:T(8,128)(2,1)}, u32[]{:S(2)}, u32[]{:S(2)}) collective-permute-start(bf16[2,2,128,1536]{3,2,1,0:T(8,128)(2,1)S(1)} %pad_maximum_fusion.2), channel_id=1, source_target_pairs={{0,32},{1,33},{2,34},{3,35},{4,36},{5,37},{6,38},{7,39},{8,40},{9,... | collective-permute-start | bytes 4718600 | tf_op jit(solution)/shard_map/ppermute | solution.py:59
  96.8 2.1 slice.28
  98.9 1.9 collective-permute-start.12
  100.8 2.1 slice.29
  102.9 12.7 %collective-permute-start.14 = (bf16[2,128,1536]{2,1,0:T(8,128)(2,1)}, bf16[2,128,1536]{2,1,0:T(8,128)(2,1)}, u32[]{:S(2)}, u32[]{:S(2)}) collective-permute-start(bf16[2,128,1536]{2,1,0:T(8,128)(2,1)} %slice.29), channel_id=1, source_target_pairs={{0,32},{1,33},{2,34},{3,35},{4,36},{5,37},{6,38},{7,39},{8,40},{9,... | collective-permute-start | bytes 2359304 | tf_op jit(solution)/shard_map/ppermute | solution.py:59
  115.6 1.4 copy.7
  117.0 6.6 %collective-permute-done.9.h2 = bf16[2,2,128,1536]{3,2,1,0:T(8,128)(2,1)} collective-permute-done((bf16[2,2,128,1536]{3,2,1,0:T(8,128)(2,1)S(1)}, bf16[2,2,128,1536]{3,2,1,0:T(8,128)(2,1)}, u32[]{:S(2)}, u32[]{:S(2)}) %collective-permute-start.9) | collective-permute-done | bytes 1572896 | tf_op jit(solution)/shard_map/ppermute | solution.py:59
  123.6 8.4 %collective-permute-done.12.hd = bf16[2,128,1536]{2,1,0:T(8,128)(2,1)} collective-permute-done((bf16[2,128,1536]{2,1,0:T(8,128)(2,1)}, bf16[2,128,1536]{2,1,0:T(8,128)(2,1)}, u32[]{:S(2)}, u32[]{:S(2)}) %collective-permute-start.12) | collective-permute-done | bytes 786464 | tf_op jit(solution)/shard_map/ppermute | solution.py:59
  132.0 13.7 %attend.2 = (bf16[128,1536]{1,0:T(8,128)(2,1)}, bf16[128,1536]{1,0:T(8,128)(2,1)}, bf16[128,1536]{1,0:T(8,128)(2,1)}, bf16[128,1536]{1,0:T(8,128)(2,1)}) custom-call(s32[4]{0:T(128)} %get-tuple-element.100.meta, bf16[2,128,1536]{2,1,0:T(8,128)(2,1)} %bitcast.75, bf16[1,128,1536]{2,1,0:T(8,128)(2,1)} %bitcast.78, bf16[3,128,1536]{2,1,0:T(8,128)(2,1)} %copy-done.6, ...), custom_call_target="tpu_custom_call" | custom-call | flops 6442450944 | bytes 10485760 | tf_op jit(solution)/shard_map/attend/pallas_call | solution.py:188
  145.8 2.0 collective-permute-start.19
  148.5 13.6 %attend.3 = (bf16[128,1536]{1,0:T(8,128)(2,1)}, bf16[128,1536]{1,0:T(8,128)(2,1)}, bf16[128,1536]{1,0:T(8,128)(2,1)}, bf16[128,1536]{1,0:T(8,128)(2,1)}) custom-call(s32[4]{0:T(128)} %get-tuple-element.100.meta, bf16[2,128,1536]{2,1,0:T(8,128)(2,1)} %bitcast.73, bf16[1,128,1536]{2,1,0:T(8,128)(2,1)} %bitcast.77, bf16[3,128,1536]{2,1,0:T(8,128)(2,1)} %copy-done.4, ...), custom_call_target="tpu_custom_call" | custom-call | flops 6442450944 | bytes 10485760 | tf_op jit(solution)/shard_map/attend/pallas_call | solution.py:188
  165.2 2.0 collective-permute-start.24
  167.2 1.1 collective-permute-start.25
  168.3 8.8 %collective-permute-done.23.refs_1_ = bf16[128,1536]{1,0:T(8,128)(2,1)S(1)} collective-permute-done((bf16[128,1536]{1,0:T(8,128)(2,1)S(1)}, bf16[128,1536]{1,0:T(8,128)(2,1)S(1)}, u32[]{:S(2)}, u32[]{:S(2)}) %collective-permute-start.23) | collective-permute-done | bytes 393248 | tf_op jit(solution)/shard_map/ppermute | solution.py:59
  177.1 12.1 %collective-permute-done.25.refs_3_ = bf16[128,1536]{1,0:T(8,128)(2,1)S(1)} collective-permute-done((bf16[128,1536]{1,0:T(8,128)(2,1)S(1)}, bf16[128,1536]{1,0:T(8,128)(2,1)S(1)}, u32[]{:S(2)}, u32[]{:S(2)}) %collective-permute-start.25) | collective-permute-done | bytes 393248 | tf_op jit(solution)/shard_map/ppermute | solution.py:59
  190.0 2.5 %collective-permute-done.26.refs_14_ = bf16[384,1536]{1,0:T(8,128)(2,1)S(1)} collective-permute-done((bf16[384,1536]{1,0:T(8,128)(2,1)S(1)}, bf16[384,1536]{1,0:T(8,128)(2,1)S(1)}, u32[]{:S(2)}, u32[]{:S(2)}) %collective-permute-start.26) | collective-permute-done | bytes 1179680 | tf_op jit(solution)/shard_map/ppermute | solution.py:59
  193.6 16.9 %project.1 = bf16[4,16,16,3072]{3,2,1,0:T(8,128)(2,1)} custom-call(s32[4]{0:T(128)} %get-tuple-element.100.meta, s32[4]{0:T(128)} %get-tuple-element.101.places, bf16[128,1536]{1,0:T(8,128)(2,1)} %get-tuple-element.142.refs_0_, bf16[128,1536]{1,0:T(8,128)(2,1)} %copy-done.22, bf16[128,1536]{1,0:T(8,128)(2,1)} %copy-done.23, bf16[128,1536]{1,0:T(8,128)(2,1)} %copy-done.24, ...), custom_call_target="tpu_custom_call" | custom-call | flops 9663676416 | bytes 26214400 | tf_op jit(solution)/shard_map/project/pallas_call | solution.py:272
  (103 shorter events, 11.6 us)
Async XLA Ops:
  6.5 109.0 %all-gather.2.cloned.1.call-start = ((), (), s32[]{:S(2)}) async-start(), calls=%async_computation | async-start | bytes 1474560 | tf_op jit(solution)/shard_map/all_gather | solution.py:325
  9.2 14.2 %collective-permute-start = (bf16[24,1536]{1,0:T(8,128)(2,1)S(1)}, bf16[24,1536]{1,0:T(8,128)(2,1)S(1)}, u32[]{:S(2)}, u32[]{:S(2)}) collective-permute-start(bf16[24,1536]{1,0:T(8,128)(2,1)S(1)} %bitcast.65), channel_id=1, source_target_pairs={{0,16},{1,17},{2,18},{3,19},{4,20},{5,21},{6,22},{7,23},{8,24},{9,... | collective-permute-start | bytes 221192 | tf_op jit(solution)/shard_map/ppermute | solution.py:59
  11.7 11.6 %collective-permute-start.1 = (bf16[24,1536]{1,0:T(8,128)(2,1)S(1)}, bf16[24,1536]{1,0:T(8,128)(2,1)S(1)}, u32[]{:S(2)}, u32[]{:S(2)}) collective-permute-start(bf16[24,1536]{1,0:T(8,128)(2,1)S(1)} %bitcast.66), channel_id=1, source_target_pairs={{0,64},{1,65},{2,66},{3,67},{4,68},{5,69},{6,70},{7,71},{8,72},{9,... | collective-permute-start | bytes 221192 | tf_op jit(solution)/shard_map/ppermute | solution.py:59
  15.0 8.3 %collective-permute-start.2 = (bf16[24,1536]{1,0:T(8,128)(2,1)S(1)}, bf16[24,1536]{1,0:T(8,128)(2,1)S(1)}, u32[]{:S(2)}, u32[]{:S(2)}) collective-permute-start(bf16[24,1536]{1,0:T(8,128)(2,1)S(1)} %bitcast.67), channel_id=1, source_target_pairs={{0,80},{1,81},{2,82},{3,83},{4,84},{5,85},{6,86},{7,87},{8,88},{9,... | collective-permute-start | bytes 221192 | tf_op jit(solution)/shard_map/ppermute | solution.py:59
  15.7 20.0 %collective-permute-start.4 = (bf16[3,128,1536]{2,1,0:T(8,128)(2,1)}, bf16[3,128,1536]{2,1,0:T(8,128)(2,1)S(1)}, u32[]{:S(2)}, u32[]{:S(2)}) collective-permute-start(bf16[3,128,1536]{2,1,0:T(8,128)(2,1)} %bitcast.70), channel_id=1, source_target_pairs={{0,1},{1,2},{2,3},{3,0},{4,5},{5,6},{6,7},{7,4},{8,9},{9,10},{10,1... | collective-permute-start | bytes 3538952 | tf_op jit(solution)/shard_map/ppermute | solution.py:59
  18.5 21.8 %collective-permute-start.3 = (bf16[3,128,1536]{2,1,0:T(8,128)(2,1)}, bf16[3,128,1536]{2,1,0:T(8,128)(2,1)S(1)}, u32[]{:S(2)}, u32[]{:S(2)}) collective-permute-start(bf16[3,128,1536]{2,1,0:T(8,128)(2,1)} %bitcast.69), channel_id=1, source_target_pairs={{0,4},{1,5},{2,6},{3,7},{4,8},{5,9},{6,10},{7,11},{8,12},{9,13},{1... | collective-permute-start | bytes 3538952 | tf_op jit(solution)/shard_map/ppermute | solution.py:59
  26.9 19.9 %collective-permute-start.6 = (bf16[3,128,1536]{2,1,0:T(8,128)(2,1)}, bf16[3,128,1536]{2,1,0:T(8,128)(2,1)S(1)}, u32[]{:S(2)}, u32[]{:S(2)}) collective-permute-start(bf16[3,128,1536]{2,1,0:T(8,128)(2,1)} %bitcast.72), channel_id=1, source_target_pairs={{0,3},{1,0},{2,1},{3,2},{4,7},{5,4},{6,5},{7,6},{8,11},{9,8},{10,9... | collective-permute-start | bytes 3538952 | tf_op jit(solution)/shard_map/ppermute | solution.py:59
  27.0 22.4 %collective-permute-start.5 = (bf16[3,128,1536]{2,1,0:T(8,128)(2,1)}, bf16[3,128,1536]{2,1,0:T(8,128)(2,1)S(1)}, u32[]{:S(2)}, u32[]{:S(2)}) collective-permute-start(bf16[3,128,1536]{2,1,0:T(8,128)(2,1)} %bitcast.71), channel_id=1, source_target_pairs={{0,28},{1,29},{2,30},{3,31},{4,0},{5,1},{6,2},{7,3},{8,4},{9,5},{1... | collective-permute-start | bytes 3538952 | tf_op jit(solution)/shard_map/ppermute | solution.py:59
  30.0 27.2 %collective-permute-start.7 = (bf16[2,128,1536]{2,1,0:T(8,128)(2,1)S(1)}, bf16[2,128,1536]{2,1,0:T(8,128)(2,1)S(1)}, u32[]{:S(2)}, u32[]{:S(2)}) collective-permute-start(bf16[2,128,1536]{2,1,0:T(8,128)(2,1)S(1)} %bitcast.74), channel_id=1, source_target_pairs={{32,0},{33,1},{34,2},{35,3},{36,4},{37,5},{38,6},{39,7},{40,8},{41... | collective-permute-start | bytes 2359304 | tf_op jit(solution)/shard_map/ppermute | solution.py:59
  35.7 21.4 %collective-permute-start.8 = (bf16[2,128,1536]{2,1,0:T(8,128)(2,1)S(1)}, bf16[2,128,1536]{2,1,0:T(8,128)(2,1)S(1)}, u32[]{:S(2)}, u32[]{:S(2)}) collective-permute-start(bf16[2,128,1536]{2,1,0:T(8,128)(2,1)S(1)} %bitcast.76), channel_id=1, source_target_pairs={{0,32},{1,33},{2,34},{3,35},{4,36},{5,37},{6,38},{7,39},{8,40},{9,... | collective-permute-start | bytes 2359304 | tf_op jit(solution)/shard_map/ppermute | solution.py:59
  58.4 38.5 %collective-permute-start.11 = (bf16[3,128,1536]{2,1,0:T(8,128)(2,1)}, bf16[3,128,1536]{2,1,0:T(8,128)(2,1)}, u32[]{:S(2)}, u32[]{:S(2)}) collective-permute-start(bf16[3,128,1536]{2,1,0:T(8,128)(2,1)} %bitcast.11), channel_id=1, source_target_pairs={{0,5},{1,6},{2,7},{3,4},{4,9},{5,10},{6,11},{7,8},{8,13},{9,14},{1... | collective-permute-start | bytes 3538952 | tf_op jit(solution)/shard_map/ppermute | solution.py:59
  60.8 40.0 %collective-permute-start.13 = (bf16[3,128,1536]{2,1,0:T(8,128)(2,1)}, bf16[3,128,1536]{2,1,0:T(8,128)(2,1)}, u32[]{:S(2)}, u32[]{:S(2)}) collective-permute-start(bf16[3,128,1536]{2,1,0:T(8,128)(2,1)} %bitcast.12), channel_id=1, source_target_pairs={{0,31},{1,28},{2,29},{3,30},{4,3},{5,0},{6,1},{7,2},{8,7},{9,4},{1... | collective-permute-start | bytes 3538952 | tf_op jit(solution)/shard_map/ppermute | solution.py:59
  60.8 62.7 %collective-permute-start.9 = (bf16[2,2,128,1536]{3,2,1,0:T(8,128)(2,1)S(1)}, bf16[2,2,128,1536]{3,2,1,0:T(8,128)(2,1)}, u32[]{:S(2)}, u32[]{:S(2)}) collective-permute-start(bf16[2,2,128,1536]{3,2,1,0:T(8,128)(2,1)S(1)} %pad_maximum_fusion.1), channel_id=1, source_target_pairs={{32,0},{33,1},{34,2},{35,3},{36,4},{37,5},{38,6},{39,7},{40,8},{41... | collective-permute-start | bytes 4718600 | tf_op jit(solution)/shard_map/ppermute | solution.py:59
  62.8 60.8 %collective-permute-start.15 = (bf16[2,2,128,1536]{3,2,1,0:T(8,128)(2,1)S(1)}, bf16[2,2,128,1536]{3,2,1,0:T(8,128)(2,1)}, u32[]{:S(2)}, u32[]{:S(2)}) collective-permute-start(bf16[2,2,128,1536]{3,2,1,0:T(8,128)(2,1)S(1)} %pad_maximum_fusion.2), channel_id=1, source_target_pairs={{0,32},{1,33},{2,34},{3,35},{4,36},{5,37},{6,38},{7,39},{8,40},{9,... | collective-permute-start | bytes 4718600 | tf_op jit(solution)/shard_map/ppermute | solution.py:59
  98.9 33.1 %collective-permute-start.12 = (bf16[2,128,1536]{2,1,0:T(8,128)(2,1)}, bf16[2,128,1536]{2,1,0:T(8,128)(2,1)}, u32[]{:S(2)}, u32[]{:S(2)}) collective-permute-start(bf16[2,128,1536]{2,1,0:T(8,128)(2,1)} %slice.28), channel_id=1, source_target_pairs={{32,0},{33,1},{34,2},{35,3},{36,4},{37,5},{38,6},{39,7},{40,8},{41... | collective-permute-start | bytes 2359304 | tf_op jit(solution)/shard_map/ppermute | solution.py:59
  102.9 29.1 %collective-permute-start.14 = (bf16[2,128,1536]{2,1,0:T(8,128)(2,1)}, bf16[2,128,1536]{2,1,0:T(8,128)(2,1)}, u32[]{:S(2)}, u32[]{:S(2)}) collective-permute-start(bf16[2,128,1536]{2,1,0:T(8,128)(2,1)} %slice.29), channel_id=1, source_target_pairs={{0,32},{1,33},{2,34},{3,35},{4,36},{5,37},{6,38},{7,39},{8,40},{9,... | collective-permute-start | bytes 2359304 | tf_op jit(solution)/shard_map/ppermute | solution.py:59
  117.0 28.8 %copy-start = (bf16[4,4,24,1536]{3,2,1,0:T(8,128)(2,1)}, bf16[4,4,24,1536]{3,2,1,0:T(8,128)(2,1)S(1)}, u32[]{:S(2)}) copy-start(bf16[4,4,24,1536]{3,2,1,0:T(8,128)(2,1)S(1)} %copy.7) | copy-start | bytes 3538948
  123.6 22.2 %collective-permute-start.10 = (bf16[384,1536]{1,0:T(8,128)(2,1)S(1)}, bf16[384,1536]{1,0:T(8,128)(2,1)S(1)}, u32[]{:S(2)}, u32[]{:S(2)}) collective-permute-start(bf16[384,1536]{1,0:T(8,128)(2,1)S(1)} %bitcast.57), channel_id=1, source_target_pairs={{0,4},{1,5},{2,6},{3,7},{4,8},{5,9},{6,10},{7,11},{8,12},{9,13},{1... | collective-permute-start | bytes 3538952 | tf_op jit(solution)/shard_map/ppermute | solution.py:59
  132.0 13.7 %collective-permute-start.16 = (bf16[384,1536]{1,0:T(8,128)(2,1)S(1)}, bf16[384,1536]{1,0:T(8,128)(2,1)S(1)}, u32[]{:S(2)}, u32[]{:S(2)}) collective-permute-start(bf16[384,1536]{1,0:T(8,128)(2,1)S(1)} %bitcast.58), channel_id=1, source_target_pairs={{0,32},{1,33},{2,34},{3,35},{4,36},{5,37},{6,38},{7,39},{8,40},{9,... | collective-permute-start | bytes 3538952 | tf_op jit(solution)/shard_map/ppermute | solution.py:59
  132.0 30.2 %collective-permute-start.18 = (bf16[384,1536]{1,0:T(8,128)(2,1)S(1)}, bf16[384,1536]{1,0:T(8,128)(2,1)S(1)}, u32[]{:S(2)}, u32[]{:S(2)}) collective-permute-start(bf16[384,1536]{1,0:T(8,128)(2,1)S(1)} %bitcast.59), channel_id=1, source_target_pairs={{0,12},{1,13},{2,14},{3,15},{4,0},{5,1},{6,2},{7,3},{8,4},{9,5},{1... | collective-permute-start | bytes 3538952 | tf_op jit(solution)/shard_map/ppermute | solution.py:59
  145.7 18.0 %copy-start.1 = (bf16[384,1536]{1,0:T(8,128)(2,1)}, bf16[384,1536]{1,0:T(8,128)(2,1)S(1)}, u32[]{:S(2)}) copy-start(bf16[384,1536]{1,0:T(8,128)(2,1)S(1)} %collective-permute-done.10.refs_9_) | copy-start | bytes 3538948
  145.8 16.4 %copy-start.9 = (bf16[384,1536]{1,0:T(8,128)(2,1)}, bf16[384,1536]{1,0:T(8,128)(2,1)S(1)}, u32[]{:S(2)}) copy-start(bf16[384,1536]{1,0:T(8,128)(2,1)S(1)} %collective-permute-done.16.refs_12_) | copy-start | bytes 3538948
  145.8 16.4 %collective-permute-start.19 = (bf16[128,1536]{1,0:T(8,128)(2,1)}, bf16[128,1536]{1,0:T(8,128)(2,1)S(1)}, u32[]{:S(2)}, u32[]{:S(2)}) collective-permute-start(bf16[128,1536]{1,0:T(8,128)(2,1)} %get-tuple-element.122), channel_id=1, source_target_pairs={{28,0},{29,1},{30,2},{31,3},{0,4},{1,5},{2,6},{3,7},{4,8},{5,9},{6... | collective-permute-start | bytes 1179656 | tf_op jit(solution)/shard_map/ppermute | solution.py:59
  147.7 14.5 %collective-permute-start.20 = (bf16[128,1536]{1,0:T(8,128)(2,1)}, bf16[128,1536]{1,0:T(8,128)(2,1)S(1)}, u32[]{:S(2)}, u32[]{:S(2)}) collective-permute-start(bf16[128,1536]{1,0:T(8,128)(2,1)} %get-tuple-element.123), channel_id=1, source_target_pairs={{3,0},{0,1},{1,2},{2,3},{7,4},{4,5},{5,6},{6,7},{11,8},{8,9},{9,10... | collective-permute-start | bytes 1179656 | tf_op jit(solution)/shard_map/ppermute | solution.py:59
  147.7 14.5 %collective-permute-start.21 = (bf16[128,1536]{1,0:T(8,128)(2,1)}, bf16[128,1536]{1,0:T(8,128)(2,1)S(1)}, u32[]{:S(2)}, u32[]{:S(2)}) collective-permute-start(bf16[128,1536]{1,0:T(8,128)(2,1)} %get-tuple-element.124), channel_id=1, source_target_pairs={{31,0},{28,1},{29,2},{30,3},{3,4},{0,5},{1,6},{2,7},{7,8},{4,9},{5... | collective-permute-start | bytes 1179656 | tf_op jit(solution)/shard_map/ppermute | solution.py:59
  163.6 25.6 %collective-permute-start.22 = (bf16[2,384,1536]{2,1,0:T(8,128)(2,1)S(1)}, bf16[2,384,1536]{2,1,0:T(8,128)(2,1)S(1)}, u32[]{:S(2)}, u32[]{:S(2)}) collective-permute-start(bf16[2,384,1536]{2,1,0:T(8,128)(2,1)S(1)} %pad_maximum_fusion), channel_id=1, source_target_pairs={{0,32},{1,33},{2,34},{3,35},{4,36},{5,37},{6,38},{7,39},{8,40},{9,... | collective-permute-start | bytes 7077896 | tf_op jit(solution)/shard_map/ppermute | solution.py:59
  163.7 25.5 %collective-permute-start.17 = (bf16[384,1536]{1,0:T(8,128)(2,1)S(1)}, bf16[384,1536]{1,0:T(8,128)(2,1)S(1)}, u32[]{:S(2)}, u32[]{:S(2)}) collective-permute-start(bf16[384,1536]{1,0:T(8,128)(2,1)S(1)} %collective-permute-done.10.refs_9_), channel_id=1, source_target_pairs={{0,4},{1,5},{2,6},{3,7},{4,8},{5,9},{6,10},{7,11},{8,12},{9,13},{1... | collective-permute-start | bytes 3538952 | tf_op jit(solution)/shard_map/ppermute | solution.py:59
  164.7 12.4 %collective-permute-start.23 = (bf16[128,1536]{1,0:T(8,128)(2,1)S(1)}, bf16[128,1536]{1,0:T(8,128)(2,1)S(1)}, u32[]{:S(2)}, u32[]{:S(2)}) collective-permute-start(bf16[128,1536]{1,0:T(8,128)(2,1)S(1)} %copy-done.21), channel_id=1, source_target_pairs={{4,0},{5,1},{6,2},{7,3},{8,4},{9,5},{10,6},{11,7},{12,8},{13,9},{1... | collective-permute-start | bytes 1179656 | tf_op jit(solution)/shard_map/ppermute | solution.py:59
  165.2 11.9 %collective-permute-start.24 = (bf16[128,1536]{1,0:T(8,128)(2,1)S(1)}, bf16[128,1536]{1,0:T(8,128)(2,1)S(1)}, u32[]{:S(2)}, u32[]{:S(2)}) collective-permute-start(bf16[128,1536]{1,0:T(8,128)(2,1)S(1)} %copy-done.20), channel_id=1, source_target_pairs={{1,0},{2,1},{3,2},{0,3},{5,4},{6,5},{7,6},{4,7},{9,8},{10,9},{11,1... | collective-permute-start | bytes 1179656 | tf_op jit(solution)/shard_map/ppermute | solution.py:59
  167.2 22.0 %collective-permute-start.25 = (bf16[128,1536]{1,0:T(8,128)(2,1)S(1)}, bf16[128,1536]{1,0:T(8,128)(2,1)S(1)}, u32[]{:S(2)}, u32[]{:S(2)}) collective-permute-start(bf16[128,1536]{1,0:T(8,128)(2,1)S(1)} %copy-done.19), channel_id=1, source_target_pairs={{5,0},{6,1},{7,2},{4,3},{9,4},{10,5},{11,6},{8,7},{13,8},{14,9},{1... | collective-permute-start | bytes 1179656 | tf_op jit(solution)/shard_map/ppermute | solution.py:59
  177.1 15.4 %copy-start.22 = (bf16[128,1536]{1,0:T(8,128)(2,1)}, bf16[128,1536]{1,0:T(8,128)(2,1)S(1)}, u32[]{:S(2)}) copy-start(bf16[128,1536]{1,0:T(8,128)(2,1)S(1)} %collective-permute-done.23.refs_1_) | copy-start | bytes 1179652
  189.2 3.3 %collective-permute-start.26 = (bf16[384,1536]{1,0:T(8,128)(2,1)S(1)}, bf16[384,1536]{1,0:T(8,128)(2,1)S(1)}, u32[]{:S(2)}, u32[]{:S(2)}) collective-permute-start(bf16[384,1536]{1,0:T(8,128)(2,1)S(1)} %collective-permute-done.17.refs_10_), channel_id=1, source_target_pairs={{0,32},{1,33},{2,34},{3,35},{4,36},{5,37},{6,38},{7,39},{8,40},{9,... | collective-permute-start | bytes 3538952 | tf_op jit(solution)/shard_map/ppermute | solution.py:59
  (22 other events, 82.3 us)
Sparse Core Ops, SparseCore 0:
  61.0 48.6 all-gather.1

commit v13 on v10

--- a/solution.py
+++ b/solution.py
@@ -14,7 +14,7 @@
 HD = 1536
 F, R, C = 4, 8, 4
 AXES = ("frame", "row", "col")
-STEP = 2
+STEP = 4
 BIG = 1e30
 TILE = 768
 VMEM = 56 * 1024 * 1024
@@ -281,9 +281,13 @@
     )(meta, places, *attended, *chunks, tokens, *extra)
 
 
-def ring_order(own, first, second, third, place):
-    row = jnp.stack([third, second, first, own, third, second, first])
-    return lax.dynamic_slice_in_dim(row, 3 - place, 4, axis=0)
+def depth_groups():
+    return [
+        [index(2 * zhi + core, zlo * 4 + x, c) for zhi in range(2) for zlo in range(2)]
+        for core in range(2)
+        for x in range(4)
+        for c in range(C)
+    ]
 
 
 def together(*values):
@@ -309,20 +313,20 @@
     back = lambda half, mixed: [mixed[0]] + [send(mixed[n], window_pairs(half, *MOVES[n], back=True)) for n in (1, 2, 3)]
 
     x0, y0 = pack(((0, 1, "kvq"), (0, 2, "kvq")), frame, *arrays)
-    x0, y0, frame, shard = together(x0, y0, frame, shard)
+    x0, y0, frame = together(x0, y0, frame)
     x0, y0 = go(x0, 0, row), go(y0, 0, col)
-    shards = [send(shard, shift_pairs(dz=n)) for n in (1, 2, 3)]
     x1, y1 = pack(((1, 1, "kvq"), (1, 2, "kvq")), frame, *arrays)
-    x1, y1, frame, *shards = together(x1, y1, frame, *shards)
+    x1, y1, frame = together(x1, y1, frame)
     x1, y1 = go(x1, 1, row), go(y1, 1, col)
     skv0, skv1, d0, d1, sq0, sq1 = pack(
         ((0, 0, "kv"), (1, 0, "kv"), (0, 3, "kvq"), (1, 3, "kvq"), (0, 0, "q"), (1, 0, "q")), frame, *arrays
     )
-    strip = ring_order(shard, *shards, (f >> 1) * 2 + (r >> 2))
+    d0, shard = together(d0, shard)
+    strip = lax.all_gather(shard, AXES, axis=0, tiled=True, axis_index_groups=depth_groups())
     h0, h1 = jnp.stack([skv0, x0[:2], y0[:2]]), jnp.stack([skv1, x1[:2], y1[:2]])
     d0, d1, h0, h1, x0, y0, x1, y1, meta, places, strip = together(d0, d1, h0, h1, x0, y0, x1, y1, meta, places, strip)
     d0, d1, down3, up3 = go(d0, 0, both), go(d1, 1, both), down(h0), up(h1)
-    strips = lax.all_gather(strip.reshape(96, HD), "col", axis=0, tiled=True)
+    strips = lax.all_gather(strip, "col", axis=0, tiled=True)
     c0 = strips.reshape(4, 4, 24, HD).swapaxes(0, 1).reshape(384, HD)
     c0, d0, d1 = together(c0, d0, d1)
     downd, upd, c1 = down(d0[:2]), up(d1[:2]), turn(c0)

time: 195 us -> 206 us (1.056)
  blocking collectives: 0 us -> 26.4 us
  waiting for transfers between devices: 64.4 us -> 54.2 us
  starting transfers between devices: 43.7 us -> 38.4 us
    all_gather x0 -> x1, blocking collectives: none -> 26.4 us  [local(): lax.all_gather(shard, AXES, axis=0, tiled=True, axis_index_groups=depth_g...]
    ppermute x26 -> x23, waiting for transfers between devices: 34.8 us -> 23.3 us  [send(): return lax.ppermute(value, AXES, pairs)]
    ppermute x26 -> x23, starting transfers between devices: 43.7 us -> 38.4 us  [send(): return lax.ppermute(value, AXES, pairs)]
    unnamed x56 -> x46, local copies, waits for them, and re-layouts: 5.1 us -> 5.42 us
  transfers between devices with their start and end apart: 27 -> 24, of which waited for: 11 -> 8; matrix products, arithmetic and copies ran while one was open for 3% -> 3% of each run, Pallas kernels for 23% -> 20%
where the time goes in v13:
time: 206 us; the launch traced here: 205 us
  Pallas kernels  58.4 us (28%)
  waiting for transfers between devices  54.2 us (26%)
  starting transfers between devices  38.4 us (19%)
  blocking collectives  26.4 us (13%)
  between operations  13.8 us (7%)
  local copies, waits for them, and re-layouts  9.93 us (5%)
  other arithmetic  3.82 us (2%)
    ppermute x23, starting transfers between devices, send(): return lax.ppermute(value, AXES, pairs)  38.4 us
    all_gather x1, waiting for transfers between devices, local(): strips = lax.all_gather(strip, 'col', axis=0, tiled=True)  30.9 us
    all_gather x1, blocking collectives, local(): lax.all_gather(shard, AXES, axis=0, tiled=True, axis_index_groups=depth_g...  26.4 us
    pallas_call x2, Pallas kernels, attend(): pl.pallas_call(functools.partial(attend_kernel, half), grid=(H // STEP,),...  26.1 us
    ppermute x23, waiting for transfers between devices, send(): return lax.ppermute(value, AXES, pairs)  23.3 us
    pallas_call x2, Pallas kernels, project(): pl.pallas_call(functools.partial(project_kernel, half), grid_spec=grid_sp...  23 us
    pallas_call x3, Pallas kernels, pack(): pl.pallas_call(functools.partial(pack_kernel, parts), out_shape=[jax.Shap...  9.32 us
    unnamed x46, local copies, waits for them, and re-layouts  5.42 us
  transfers between devices with their start and end apart: 24, of which 8 were waited for; matrix products, arithmetic and copies ran while one was open for 3% of the time, Pallas kernels for 20%

profile of v13, /device:TPU:1, one launch (start us, length us, event | category | flops | bytes accessed | tf_op | source)
XLA Modules:
  0.0 205.0 jit_solution(6047516122347201453)
XLA Ops:
  6.5 2.5 %pack.3 = (bf16[3,2,8,8,1536]{4,3,2,1,0:T(8,128)(2,1)}, bf16[3,2,8,8,1536]{4,3,2,1,0:T(8,128)(2,1)}) custom-call(s32[1]{0:T(128)} %bitcast.meta, bf16[4,2,8,2,8,1536]{5,4,3,2,1,0:T(8,128)(2,1)} %bitcast.36, bf16[4,2,8,2,8,1536]{5,4,3,2,1,0:T(8,128)(2,1)} %bitcast.39, bf16[4,2,8,2,8,1536]{5,4,3,2,1,0:T(8,128)(2,1)} %bitcast.42), custom_call_target="tpu_custom_call" | custom-call | bytes 6291456 | tf_op jit(solution)/shard_map/pack/pallas_call | solution.py:98
  9.0 2.5 %pack.4 = (bf16[3,2,8,8,1536]{4,3,2,1,0:T(8,128)(2,1)}, bf16[3,2,8,8,1536]{4,3,2,1,0:T(8,128)(2,1)}) custom-call(s32[1]{0:T(128)} %bitcast.meta, bf16[4,2,8,2,8,1536]{5,4,3,2,1,0:T(8,128)(2,1)} %bitcast.37, bf16[4,2,8,2,8,1536]{5,4,3,2,1,0:T(8,128)(2,1)} %bitcast.40, bf16[4,2,8,2,8,1536]{5,4,3,2,1,0:T(8,128)(2,1)} %bitcast.43), custom_call_target="tpu_custom_call" | custom-call | bytes 6291456 | tf_op jit(solution)/shard_map/pack/pallas_call | solution.py:98
  11.5 2.1 %collective-permute-start.2 = (bf16[3,128,1536]{2,1,0:T(8,128)(2,1)}, bf16[3,128,1536]{2,1,0:T(8,128)(2,1)S(1)}, u32[]{:S(2)}, u32[]{:S(2)}) collective-permute-start(bf16[3,128,1536]{2,1,0:T(8,128)(2,1)} %bitcast.59), channel_id=1, source_target_pairs={{0,28},{1,29},{2,30},{3,31},{4,0},{5,1},{6,2},{7,3},{8,4},{9,5},{1... | collective-permute-start | bytes 3538952 | tf_op jit(solution)/shard_map/ppermute | solution.py:59
  13.7 1.3 collective-permute-start.3
  15.0 2.7 %collective-permute-start = (bf16[3,128,1536]{2,1,0:T(8,128)(2,1)}, bf16[3,128,1536]{2,1,0:T(8,128)(2,1)S(1)}, u32[]{:S(2)}, u32[]{:S(2)}) collective-permute-start(bf16[3,128,1536]{2,1,0:T(8,128)(2,1)} %bitcast.4), channel_id=1, source_target_pairs={{0,4},{1,5},{2,6},{3,7},{4,8},{5,9},{6,10},{7,11},{8,12},{9,13},{1... | collective-permute-start | bytes 3538952 | tf_op jit(solution)/shard_map/ppermute | solution.py:59
  17.7 1.5 collective-permute-start.1
  19.2 4.3 %pack.5 = (bf16[2,2,8,8,1536]{4,3,2,1,0:T(8,128)(2,1)}, bf16[2,2,8,8,1536]{4,3,2,1,0:T(8,128)(2,1)}, bf16[3,2,8,8,1536]{4,3,2,1,0:T(8,128)(2,1)}, bf16[3,2,8,8,1...) custom-call(s32[1]{0:T(128)} %bitcast.meta, ...), custom_call_target="tpu_custom_call" | custom-call | bytes 12582912 | tf_op jit(solution)/shard_map/pack/pallas_call | solution.py:98
  24.2 26.4 %all_gather.6 = bf16[96,1536]{1,0:T(8,128)(2,1)} all-gather(bf16[24,1536]{1,0:T(8,128)(2,1)} %bitcast.55), channel_id=1, replica_groups={{0,16,64,80},{1,17,65,81},{2,18,66,82},{3,19,67,83},{4,20,68,84},{5,21,..., dimensions={0}, use_global_device_ids=true | all-gather | bytes 368640 | tf_op jit(solution)/shard_map/all_gather | solution.py:325
  50.6 1.2 pad_add_fusion
  54.9 1.3 slice_bitcast_fusion.2
  56.3 1.7 pad_maximum_fusion
  58.0 5.8 %collective-permute-start.4 = (bf16[3,128,1536]{2,1,0:T(8,128)(2,1)}, bf16[3,128,1536]{2,1,0:T(8,128)(2,1)S(1)}, u32[]{:S(2)}, u32[]{:S(2)}) collective-permute-start(bf16[3,128,1536]{2,1,0:T(8,128)(2,1)} %bitcast.57), channel_id=1, source_target_pairs={{0,5},{1,6},{2,7},{3,4},{4,9},{5,10},{6,11},{7,8},{8,13},{9,14},{1... | collective-permute-start | bytes 3538952 | tf_op jit(solution)/shard_map/ppermute | solution.py:59
  63.8 4.6 %collective-permute-start.9 = (bf16[3,2,128,1536]{3,2,1,0:T(8,128)(2,1)}, bf16[3,2,128,1536]{3,2,1,0:T(8,128)(2,1)}, u32[]{:S(2)}, u32[]{:S(2)}) collective-permute-start(bf16[3,2,128,1536]{3,2,1,0:T(8,128)(2,1)} %pad_maximum_fusion), channel_id=1, source_target_pairs={{32,0},{33,1},{34,2},{35,3},{36,4},{37,5},{38,6},{39,7},{40,8},{41... | collective-permute-start | bytes 7077896 | tf_op jit(solution)/shard_map/ppermute | solution.py:59
  68.4 4.2 %collective-permute-start.10 = (bf16[3,2,128,1536]{3,2,1,0:T(8,128)(2,1)S(1)}, bf16[3,2,128,1536]{3,2,1,0:T(8,128)(2,1)}, u32[]{:S(2)}, u32[]{:S(2)}) collective-permute-start(bf16[3,2,128,1536]{3,2,1,0:T(8,128)(2,1)S(1)} %pad_maximum_fusion.1), channel_id=1, source_target_pairs={{0,32},{1,33},{2,34},{3,35},{4,36},{5,37},{6,38},{7,39},{8,40},{9,... | collective-permute-start | bytes 7077896 | tf_op jit(solution)/shard_map/ppermute | solution.py:59
  72.6 30.9 %all-gather.2.cloned.1.call-done = bf16[384,1536]{1,0:T(8,128)(2,1)} async-done(((bf16[96,1536]{1,0:T(8,128)(2,1)}), bf16[384,1536]{1,0:T(8,128)(2,1)}) %all-gather.2.cloned.1.call-update) | async-done | bytes 1179664 | tf_op jit(solution)/shard_map/all_gather | solution.py:329
  103.4 1.4 copy.8
  105.1 1.7 slice.23
  106.8 4.9 %collective-permute-start.8 = (bf16[2,128,1536]{2,1,0:T(8,128)(2,1)S(1)}, bf16[2,128,1536]{2,1,0:T(8,128)(2,1)S(1)}, u32[]{:S(2)}, u32[]{:S(2)}) collective-permute-start(bf16[2,128,1536]{2,1,0:T(8,128)(2,1)S(1)} %slice.23), channel_id=1, source_target_pairs={{0,32},{1,33},{2,34},{3,35},{4,36},{5,37},{6,38},{7,39},{8,40},{9,... | collective-permute-start | bytes 2359304 | tf_op jit(solution)/shard_map/ppermute | solution.py:59
  111.8 1.9 collective-permute-start.7
  113.7 6.4 %collective-permute-done.9.h3 = bf16[3,2,128,1536]{3,2,1,0:T(8,128)(2,1)} collective-permute-done((bf16[3,2,128,1536]{3,2,1,0:T(8,128)(2,1)}, bf16[3,2,128,1536]{3,2,1,0:T(8,128)(2,1)}, u32[]{:S(2)}, u32[]{:S(2)}) %collective-permute-start.9) | collective-permute-done | bytes 2359328 | tf_op jit(solution)/shard_map/ppermute | solution.py:59
  120.1 5.5 %collective-permute-done.8.hd = bf16[2,128,1536]{2,1,0:T(8,128)(2,1)S(1)} collective-permute-done((bf16[2,128,1536]{2,1,0:T(8,128)(2,1)S(1)}, bf16[2,128,1536]{2,1,0:T(8,128)(2,1)S(1)}, u32[]{:S(2)}, u32[]{:S(2)}) %collective-permute-start.8) | collective-permute-done | bytes 786464 | tf_op jit(solution)/shard_map/ppermute | solution.py:59
  125.6 2.8 %collective-permute-done.7.hd = bf16[2,128,1536]{2,1,0:T(8,128)(2,1)S(1)} collective-permute-done((bf16[2,128,1536]{2,1,0:T(8,128)(2,1)S(1)}, bf16[2,128,1536]{2,1,0:T(8,128)(2,1)S(1)}, u32[]{:S(2)}, u32[]{:S(2)}) %collective-permute-start.7) | collective-permute-done | bytes 786464 | tf_op jit(solution)/shard_map/ppermute | solution.py:59
  130.5 13.0 %attend.2 = (bf16[128,1536]{1,0:T(8,128)(2,1)}, bf16[128,1536]{1,0:T(8,128)(2,1)}, bf16[128,1536]{1,0:T(8,128)(2,1)}, bf16[128,1536]{1,0:T(8,128)(2,1)}) custom-call(s32[4]{0:T(128)} %get-tuple-element.84.meta, bf16[2,128,1536]{2,1,0:T(8,128)(2,1)} %bitcast.53, bf16[1,128,1536]{2,1,0:T(8,128)(2,1)} %bitcast.61, bf16[3,128,1536]{2,1,0:T(8,128)(2,1)} %copy-done.11, ...), custom_call_target="tpu_custom_call" | custom-call | flops 6442450944 | bytes 10485760 | tf_op jit(solution)/shard_map/attend/pallas_call | solution.py:188
  143.6 1.3 collective-permute-start.15
  144.9 2.2 %collective-permute-start.16 = (bf16[128,1536]{1,0:T(8,128)(2,1)}, bf16[128,1536]{1,0:T(8,128)(2,1)S(1)}, u32[]{:S(2)}, u32[]{:S(2)}) collective-permute-start(bf16[128,1536]{1,0:T(8,128)(2,1)} %get-tuple-element.107), channel_id=1, source_target_pairs={{3,0},{0,1},{1,2},{2,3},{7,4},{4,5},{5,6},{6,7},{11,8},{8,9},{9,10... | collective-permute-start | bytes 1179656 | tf_op jit(solution)/shard_map/ppermute | solution.py:59
  147.1 13.0 %attend.3 = (bf16[128,1536]{1,0:T(8,128)(2,1)}, bf16[128,1536]{1,0:T(8,128)(2,1)}, bf16[128,1536]{1,0:T(8,128)(2,1)}, bf16[128,1536]{1,0:T(8,128)(2,1)}) custom-call(s32[4]{0:T(128)} %get-tuple-element.84.meta, bf16[2,128,1536]{2,1,0:T(8,128)(2,1)} %bitcast.51, bf16[1,128,1536]{2,1,0:T(8,128)(2,1)} %bitcast.60, bf16[3,128,1536]{2,1,0:T(8,128)(2,1)} %copy-done.10, ...), custom_call_target="tpu_custom_call" | custom-call | flops 6442450944 | bytes 10485760 | tf_op jit(solution)/shard_map/attend/pallas_call | solution.py:188
  161.2 3.5 %collective-permute-done.17.refs_3_ = bf16[128,1536]{1,0:T(8,128)(2,1)S(1)} collective-permute-done((bf16[128,1536]{1,0:T(8,128)(2,1)}, bf16[128,1536]{1,0:T(8,128)(2,1)S(1)}, u32[]{:S(2)}, u32[]{:S(2)}) %collective-permute-start.17) | collective-permute-done | bytes 393248 | tf_op jit(solution)/shard_map/ppermute | solution.py:59
  164.7 3.5 %collective-permute-start.21 = (bf16[384,1536]{1,0:T(8,128)(2,1)S(1)}, bf16[384,1536]{1,0:T(8,128)(2,1)S(1)}, u32[]{:S(2)}, u32[]{:S(2)}) collective-permute-start(bf16[384,1536]{1,0:T(8,128)(2,1)S(1)} %collective-permute-done.11.refs_6_), channel_id=1, source_target_pairs={{0,32},{1,33},{2,34},{3,35},{4,36},{5,37},{6,38},{7,39},{8,40},{9,... | collective-permute-start | bytes 3538952 | tf_op jit(solution)/shard_map/ppermute | solution.py:59
  168.3 2.4 %collective-permute-done.21.refs_10_ = bf16[384,1536]{1,0:T(8,128)(2,1)S(1)} collective-permute-done((bf16[384,1536]{1,0:T(8,128)(2,1)S(1)}, bf16[384,1536]{1,0:T(8,128)(2,1)S(1)}, u32[]{:S(2)}, u32[]{:S(2)}) %collective-permute-start.21) | collective-permute-done | bytes 1179680 | tf_op jit(solution)/shard_map/ppermute | solution.py:59
  170.7 1.7 collective-permute-done.22.refs_11_
  173.4 11.5 %project.2.refs_13_ = bf16[4,16,16,3072]{3,2,1,0:T(8,128)(2,1)} custom-call(s32[4]{0:T(128)} %get-tuple-element.84.meta, s32[4]{0:T(128)} %get-tuple-element.85.places, bf16[128,1536]{1,0:T(8,128)(2,1)} %get-tuple-element.127.refs_0_, bf16[128,1536]{1,0:T(8,128)(2,1)} %copy-done.17, bf16[128,1536]{1,0:T(8,128)(2,1)} %copy-done.18, ...), custom_call_target="tpu_custom_call" | custom-call | flops 4831838208 | bytes 17825792 | tf_op jit(solution)/shard_map/project/pallas_call | solution.py:273
  186.6 11.5 %project.3 = bf16[4,16,16,3072]{3,2,1,0:T(8,128)(2,1)} custom-call(s32[4]{0:T(128)} %get-tuple-element.84.meta, s32[4]{0:T(128)} %get-tuple-element.85.places, bf16[128,1536]{1,0:T(8,128)(2,1)} %get-tuple-element.119.refs_0_, bf16[128,1536]{1,0:T(8,128)(2,1)} %copy-done.14, bf16[128,1536]{1,0:T(8,128)(2,1)} %copy-done.15, ...), custom_call_target="tpu_custom_call", output_to_operand_aliasing={{}: (15, {})} | custom-call | flops 4831838208 | bytes 17825792 | tf_op jit(solution)/shard_map/project/pallas_call | solution.py:273
  (82 shorter events, 10.1 us)
Async XLA Ops:
  6.5 96.9 %all-gather.2.cloned.1.call-start = ((), (), s32[]{:S(2)}) async-start(), calls=%async_computation | async-start | bytes 1474560 | tf_op jit(solution)/shard_map/all_gather | solution.py:329
  11.5 40.3 %collective-permute-start.2 = (bf16[3,128,1536]{2,1,0:T(8,128)(2,1)}, bf16[3,128,1536]{2,1,0:T(8,128)(2,1)S(1)}, u32[]{:S(2)}, u32[]{:S(2)}) collective-permute-start(bf16[3,128,1536]{2,1,0:T(8,128)(2,1)} %bitcast.59), channel_id=1, source_target_pairs={{0,28},{1,29},{2,30},{3,31},{4,0},{5,1},{6,2},{7,3},{8,4},{9,5},{1... | collective-permute-start | bytes 3538952 | tf_op jit(solution)/shard_map/ppermute | solution.py:59
  13.7 38.2 %collective-permute-start.3 = (bf16[3,128,1536]{2,1,0:T(8,128)(2,1)}, bf16[3,128,1536]{2,1,0:T(8,128)(2,1)S(1)}, u32[]{:S(2)}, u32[]{:S(2)}) collective-permute-start(bf16[3,128,1536]{2,1,0:T(8,128)(2,1)} %bitcast.58), channel_id=1, source_target_pairs={{0,3},{1,0},{2,1},{3,2},{4,7},{5,4},{6,5},{7,6},{8,11},{9,8},{10,9... | collective-permute-start | bytes 3538952 | tf_op jit(solution)/shard_map/ppermute | solution.py:59
  15.0 38.9 %collective-permute-start = (bf16[3,128,1536]{2,1,0:T(8,128)(2,1)}, bf16[3,128,1536]{2,1,0:T(8,128)(2,1)S(1)}, u32[]{:S(2)}, u32[]{:S(2)}) collective-permute-start(bf16[3,128,1536]{2,1,0:T(8,128)(2,1)} %bitcast.4), channel_id=1, source_target_pairs={{0,4},{1,5},{2,6},{3,7},{4,8},{5,9},{6,10},{7,11},{8,12},{9,13},{1... | collective-permute-start | bytes 3538952 | tf_op jit(solution)/shard_map/ppermute | solution.py:59
  17.7 37.3 %collective-permute-start.1 = (bf16[3,128,1536]{2,1,0:T(8,128)(2,1)}, bf16[3,128,1536]{2,1,0:T(8,128)(2,1)}, u32[]{:S(2)}, u32[]{:S(2)}) collective-permute-start(bf16[3,128,1536]{2,1,0:T(8,128)(2,1)} %bitcast.5), channel_id=1, source_target_pairs={{0,1},{1,2},{2,3},{3,0},{4,5},{5,6},{6,7},{7,4},{8,9},{9,10},{10,1... | collective-permute-start | bytes 3538952 | tf_op jit(solution)/shard_map/ppermute | solution.py:59
  58.0 46.8 %collective-permute-start.4 = (bf16[3,128,1536]{2,1,0:T(8,128)(2,1)}, bf16[3,128,1536]{2,1,0:T(8,128)(2,1)S(1)}, u32[]{:S(2)}, u32[]{:S(2)}) collective-permute-start(bf16[3,128,1536]{2,1,0:T(8,128)(2,1)} %bitcast.57), channel_id=1, source_target_pairs={{0,5},{1,6},{2,7},{3,4},{4,9},{5,10},{6,11},{7,8},{8,13},{9,14},{1... | collective-permute-start | bytes 3538952 | tf_op jit(solution)/shard_map/ppermute | solution.py:59
  63.8 41.1 %collective-permute-start.5 = (bf16[3,128,1536]{2,1,0:T(8,128)(2,1)}, bf16[3,128,1536]{2,1,0:T(8,128)(2,1)}, u32[]{:S(2)}, u32[]{:S(2)}) collective-permute-start(bf16[3,128,1536]{2,1,0:T(8,128)(2,1)} %bitcast.56), channel_id=1, source_target_pairs={{0,31},{1,28},{2,29},{3,30},{4,3},{5,0},{6,1},{7,2},{8,7},{9,4},{1... | collective-permute-start | bytes 3538952 | tf_op jit(solution)/shard_map/ppermute | solution.py:59
  63.8 56.3 %collective-permute-start.9 = (bf16[3,2,128,1536]{3,2,1,0:T(8,128)(2,1)}, bf16[3,2,128,1536]{3,2,1,0:T(8,128)(2,1)}, u32[]{:S(2)}, u32[]{:S(2)}) collective-permute-start(bf16[3,2,128,1536]{3,2,1,0:T(8,128)(2,1)} %pad_maximum_fusion), channel_id=1, source_target_pairs={{32,0},{33,1},{34,2},{35,3},{36,4},{37,5},{38,6},{39,7},{40,8},{41... | collective-permute-start | bytes 7077896 | tf_op jit(solution)/shard_map/ppermute | solution.py:59
  68.4 51.7 %collective-permute-start.10 = (bf16[3,2,128,1536]{3,2,1,0:T(8,128)(2,1)S(1)}, bf16[3,2,128,1536]{3,2,1,0:T(8,128)(2,1)}, u32[]{:S(2)}, u32[]{:S(2)}) collective-permute-start(bf16[3,2,128,1536]{3,2,1,0:T(8,128)(2,1)S(1)} %pad_maximum_fusion.1), channel_id=1, source_target_pairs={{0,32},{1,33},{2,34},{3,35},{4,36},{5,37},{6,38},{7,39},{8,40},{9,... | collective-permute-start | bytes 7077896 | tf_op jit(solution)/shard_map/ppermute | solution.py:59
  104.8 24.7 %copy-start = (bf16[4,4,24,1536]{3,2,0,1:T(8,128)(2,1)}, bf16[4,4,24,1536]{3,2,0,1:T(8,128)(2,1)S(1)}, u32[]{:S(2)}) copy-start(bf16[4,4,24,1536]{3,2,0,1:T(8,128)(2,1)S(1)} %copy.8) | copy-start | bytes 3538948
  104.8 23.6 %collective-permute-start.6 = (bf16[384,1536]{1,0:T(8,128)(2,1)S(1)}, bf16[384,1536]{1,0:T(8,128)(2,1)S(1)}, u32[]{:S(2)}, u32[]{:S(2)}) collective-permute-start(bf16[384,1536]{1,0:T(8,128)(2,1)S(1)} %bitcast.45), channel_id=1, source_target_pairs={{0,4},{1,5},{2,6},{3,7},{4,8},{5,9},{6,10},{7,11},{8,12},{9,13},{1... | collective-permute-start | bytes 3538952 | tf_op jit(solution)/shard_map/ppermute | solution.py:59
  106.8 18.8 %collective-permute-start.8 = (bf16[2,128,1536]{2,1,0:T(8,128)(2,1)S(1)}, bf16[2,128,1536]{2,1,0:T(8,128)(2,1)S(1)}, u32[]{:S(2)}, u32[]{:S(2)}) collective-permute-start(bf16[2,128,1536]{2,1,0:T(8,128)(2,1)S(1)} %slice.23), channel_id=1, source_target_pairs={{0,32},{1,33},{2,34},{3,35},{4,36},{5,37},{6,38},{7,39},{8,40},{9,... | collective-permute-start | bytes 2359304 | tf_op jit(solution)/shard_map/ppermute | solution.py:59
  111.8 16.6 %collective-permute-start.7 = (bf16[2,128,1536]{2,1,0:T(8,128)(2,1)S(1)}, bf16[2,128,1536]{2,1,0:T(8,128)(2,1)S(1)}, u32[]{:S(2)}, u32[]{:S(2)}) collective-permute-start(bf16[2,128,1536]{2,1,0:T(8,128)(2,1)S(1)} %slice.22), channel_id=1, source_target_pairs={{32,0},{33,1},{34,2},{35,3},{36,4},{37,5},{38,6},{39,7},{40,8},{41... | collective-permute-start | bytes 2359304 | tf_op jit(solution)/shard_map/ppermute | solution.py:59
  128.4 15.1 %copy-start.1 = (bf16[384,1536]{1,0:T(8,128)(2,1)}, bf16[384,1536]{1,0:T(8,128)(2,1)S(1)}, u32[]{:S(2)}) copy-start(bf16[384,1536]{1,0:T(8,128)(2,1)S(1)} %collective-permute-done.6.refs_5_) | copy-start | bytes 3538948
  128.4 15.1 %collective-permute-start.14 = (bf16[384,1536]{1,0:T(8,128)(2,1)S(1)}, bf16[384,1536]{1,0:T(8,128)(2,1)S(1)}, u32[]{:S(2)}, u32[]{:S(2)}) collective-permute-start(bf16[384,1536]{1,0:T(8,128)(2,1)S(1)} %collective-permute-done.6.refs_5_), channel_id=1, source_target_pairs={{0,32},{1,33},{2,34},{3,35},{4,36},{5,37},{6,38},{7,39},{8,40},{9,... | collective-permute-start | bytes 3538952 | tf_op jit(solution)/shard_map/ppermute | solution.py:59
  128.5 15.0 %collective-permute-start.13 = (bf16[384,1536]{1,0:T(8,128)(2,1)S(1)}, bf16[384,1536]{1,0:T(8,128)(2,1)S(1)}, u32[]{:S(2)}, u32[]{:S(2)}) collective-permute-start(bf16[384,1536]{1,0:T(8,128)(2,1)S(1)} %bitcast.46), channel_id=1, source_target_pairs={{0,32},{1,33},{2,34},{3,35},{4,36},{5,37},{6,38},{7,39},{8,40},{9,... | collective-permute-start | bytes 3538952 | tf_op jit(solution)/shard_map/ppermute | solution.py:59
  129.0 31.2 %collective-permute-start.11 = (bf16[384,1536]{1,0:T(8,128)(2,1)S(1)}, bf16[384,1536]{1,0:T(8,128)(2,1)S(1)}, u32[]{:S(2)}, u32[]{:S(2)}) collective-permute-start(bf16[384,1536]{1,0:T(8,128)(2,1)S(1)} %collective-permute-done.6.refs_5_), channel_id=1, source_target_pairs={{0,4},{1,5},{2,6},{3,7},{4,8},{5,9},{6,10},{7,11},{8,12},{9,13},{1... | collective-permute-start | bytes 3538952 | tf_op jit(solution)/shard_map/ppermute | solution.py:59
  129.5 30.6 %collective-permute-start.12 = (bf16[384,1536]{1,0:T(8,128)(2,1)S(1)}, bf16[384,1536]{1,0:T(8,128)(2,1)S(1)}, u32[]{:S(2)}, u32[]{:S(2)}) collective-permute-start(bf16[384,1536]{1,0:T(8,128)(2,1)S(1)} %bitcast.47), channel_id=1, source_target_pairs={{0,12},{1,13},{2,14},{3,15},{4,0},{5,1},{6,2},{7,3},{8,4},{9,5},{1... | collective-permute-start | bytes 3538952 | tf_op jit(solution)/shard_map/ppermute | solution.py:59
  143.5 16.6 %copy-start.2 = (bf16[384,1536]{1,0:T(8,128)(2,1)}, bf16[384,1536]{1,0:T(8,128)(2,1)S(1)}, u32[]{:S(2)}) copy-start(bf16[384,1536]{1,0:T(8,128)(2,1)S(1)} %collective-permute-done.14.refs_9_) | copy-start | bytes 3538948
  143.6 16.6 %copy-start.3 = (bf16[384,1536]{1,0:T(8,128)(2,1)}, bf16[384,1536]{1,0:T(8,128)(2,1)S(1)}, u32[]{:S(2)}) copy-start(bf16[384,1536]{1,0:T(8,128)(2,1)S(1)} %collective-permute-done.13.refs_8_) | copy-start | bytes 3538948
  143.6 17.6 %collective-permute-start.15 = (bf16[128,1536]{1,0:T(8,128)(2,1)}, bf16[128,1536]{1,0:T(8,128)(2,1)S(1)}, u32[]{:S(2)}, u32[]{:S(2)}) collective-permute-start(bf16[128,1536]{1,0:T(8,128)(2,1)} %get-tuple-element.106), channel_id=1, source_target_pairs={{28,0},{29,1},{30,2},{31,3},{0,4},{1,5},{2,6},{3,7},{4,8},{5,9},{6... | collective-permute-start | bytes 1179656 | tf_op jit(solution)/shard_map/ppermute | solution.py:59
  144.9 16.3 %collective-permute-start.16 = (bf16[128,1536]{1,0:T(8,128)(2,1)}, bf16[128,1536]{1,0:T(8,128)(2,1)S(1)}, u32[]{:S(2)}, u32[]{:S(2)}) collective-permute-start(bf16[128,1536]{1,0:T(8,128)(2,1)} %get-tuple-element.107), channel_id=1, source_target_pairs={{3,0},{0,1},{1,2},{2,3},{7,4},{4,5},{5,6},{6,7},{11,8},{8,9},{9,10... | collective-permute-start | bytes 1179656 | tf_op jit(solution)/shard_map/ppermute | solution.py:59
  147.1 17.7 %collective-permute-start.17 = (bf16[128,1536]{1,0:T(8,128)(2,1)}, bf16[128,1536]{1,0:T(8,128)(2,1)S(1)}, u32[]{:S(2)}, u32[]{:S(2)}) collective-permute-start(bf16[128,1536]{1,0:T(8,128)(2,1)} %get-tuple-element.108), channel_id=1, source_target_pairs={{31,0},{28,1},{29,2},{30,3},{3,4},{0,5},{1,6},{2,7},{7,8},{4,9},{5... | collective-permute-start | bytes 1179656 | tf_op jit(solution)/shard_map/ppermute | solution.py:59
  160.2 12.2 %copy-start.4 = (bf16[384,1536]{1,0:T(8,128)(2,1)}, bf16[384,1536]{1,0:T(8,128)(2,1)S(1)}, u32[]{:S(2)}) copy-start(bf16[384,1536]{1,0:T(8,128)(2,1)S(1)} %collective-permute-done.11.refs_6_) | copy-start | bytes 3538948
  160.2 12.2 %copy-start.5 = (bf16[384,1536]{1,0:T(8,128)(2,1)}, bf16[384,1536]{1,0:T(8,128)(2,1)S(1)}, u32[]{:S(2)}) copy-start(bf16[384,1536]{1,0:T(8,128)(2,1)S(1)} %collective-permute-done.12.refs_7_) | copy-start | bytes 3538948
  161.2 11.2 %copy-start.17 = (bf16[128,1536]{1,0:T(8,128)(2,1)}, bf16[128,1536]{1,0:T(8,128)(2,1)S(1)}, u32[]{:S(2)}) copy-start(bf16[128,1536]{1,0:T(8,128)(2,1)S(1)} %collective-permute-done.15.refs_1_) | copy-start | bytes 1179652
  161.2 11.2 %copy-start.18 = (bf16[128,1536]{1,0:T(8,128)(2,1)}, bf16[128,1536]{1,0:T(8,128)(2,1)S(1)}, u32[]{:S(2)}) copy-start(bf16[128,1536]{1,0:T(8,128)(2,1)S(1)} %collective-permute-done.16.refs_2_) | copy-start | bytes 1179652
  164.7 6.0 %collective-permute-start.21 = (bf16[384,1536]{1,0:T(8,128)(2,1)S(1)}, bf16[384,1536]{1,0:T(8,128)(2,1)S(1)}, u32[]{:S(2)}, u32[]{:S(2)}) collective-permute-start(bf16[384,1536]{1,0:T(8,128)(2,1)S(1)} %collective-permute-done.11.refs_6_), channel_id=1, source_target_pairs={{0,32},{1,33},{2,34},{3,35},{4,36},{5,37},{6,38},{7,39},{8,40},{9,... | collective-permute-start | bytes 3538952 | tf_op jit(solution)/shard_map/ppermute | solution.py:59
  168.2 4.2 %collective-permute-start.22 = (bf16[384,1536]{1,0:T(8,128)(2,1)S(1)}, bf16[384,1536]{1,0:T(8,128)(2,1)S(1)}, u32[]{:S(2)}, u32[]{:S(2)}) collective-permute-start(bf16[384,1536]{1,0:T(8,128)(2,1)S(1)} %collective-permute-done.12.refs_7_), channel_id=1, source_target_pairs={{0,32},{1,33},{2,34},{3,35},{4,36},{5,37},{6,38},{7,39},{8,40},{9,... | collective-permute-start | bytes 3538952 | tf_op jit(solution)/shard_map/ppermute | solution.py:59
  168.2 16.7 %collective-permute-start.18 = (bf16[128,1536]{1,0:T(8,128)(2,1)}, bf16[128,1536]{1,0:T(8,128)(2,1)S(1)}, u32[]{:S(2)}, u32[]{:S(2)}) collective-permute-start(bf16[128,1536]{1,0:T(8,128)(2,1)} %get-tuple-element.120), channel_id=1, source_target_pairs={{4,0},{5,1},{6,2},{7,3},{8,4},{9,5},{10,6},{11,7},{12,8},{13,9},{1... | collective-permute-start | bytes 1179656 | tf_op jit(solution)/shard_map/ppermute | solution.py:59
  168.2 16.8 %collective-permute-start.19 = (bf16[128,1536]{1,0:T(8,128)(2,1)}, bf16[128,1536]{1,0:T(8,128)(2,1)S(1)}, u32[]{:S(2)}, u32[]{:S(2)}) collective-permute-start(bf16[128,1536]{1,0:T(8,128)(2,1)} %get-tuple-element.121), channel_id=1, source_target_pairs={{1,0},{2,1},{3,2},{0,3},{5,4},{6,5},{7,6},{4,7},{9,8},{10,9},{11,1... | collective-permute-start | bytes 1179656 | tf_op jit(solution)/shard_map/ppermute | solution.py:59
  168.3 16.7 %collective-permute-start.20 = (bf16[128,1536]{1,0:T(8,128)(2,1)}, bf16[128,1536]{1,0:T(8,128)(2,1)S(1)}, u32[]{:S(2)}, u32[]{:S(2)}) collective-permute-start(bf16[128,1536]{1,0:T(8,128)(2,1)} %get-tuple-element.122), channel_id=1, source_target_pairs={{5,0},{6,1},{7,2},{4,3},{9,4},{10,5},{11,6},{8,7},{13,8},{14,9},{1... | collective-permute-start | bytes 1179656 | tf_op jit(solution)/shard_map/ppermute | solution.py:59
  (15 other events, 31.2 us)
Sparse Core Ops, SparseCore 0:
  58.1 45.2 all-gather.1

commit v14 on v10

--- a/solution.py
+++ b/solution.py
@@ -14,7 +14,7 @@
 HD = 1536
 F, R, C = 4, 8, 4
 AXES = ("frame", "row", "col")
-STEP = 2
+STEP = 4
 BIG = 1e30
 TILE = 768
 VMEM = 56 * 1024 * 1024
@@ -324,8 +324,8 @@
     d0, d1, down3, up3 = go(d0, 0, both), go(d1, 1, both), down(h0), up(h1)
     strips = lax.all_gather(strip.reshape(96, HD), "col", axis=0, tiled=True)
     c0 = strips.reshape(4, 4, 24, HD).swapaxes(0, 1).reshape(384, HD)
-    c0, d0, d1 = together(c0, d0, d1)
-    downd, upd, c1 = down(d0[:2]), up(d1[:2]), turn(c0)
+    downd, upd = down(d0[:2]), up(d1[:2])
+    c1 = turn(c0)
     c0, c1, downd, upd, down3, up3 = together(c0, c1, downd, upd, down3, up3)
 
     c2, c3, s0, s1 = turn(c1), turn(c0, -1), swap(c0), swap(c1)

time: 195 us -> 197 us (1.010)
    all_gather x1, waiting for transfers between devices: 29.6 us -> 35.2 us  [local(): strips = lax.all_gather(strip.reshape(96, HD), 'col', axis=0, tiled=True)]
    ppermute x26, waiting for transfers between devices: 34.8 us -> 31.1 us  [send(): return lax.ppermute(value, AXES, pairs)]
  transfers between devices with their start and end apart: 27 -> 27, of which waited for: 11 -> 10; matrix products, arithmetic and copies ran while one was open for 3% -> 3% of each run, Pallas kernels for 23% -> 23%
where the time goes in v14:
time: 197 us
  waiting for transfers between devices  66.3 us (34%)
  Pallas kernels  58.5 us (30%)
  starting transfers between devices  45.3 us (23%)
  between operations  13.9 us (7%)
  local copies, waits for them, and re-layouts  8.9 us (5%)
  other arithmetic  3.97 us (2%)
    ppermute x26, starting transfers between devices, send(): return lax.ppermute(value, AXES, pairs)  45.3 us
    all_gather x1, waiting for transfers between devices, local(): strips = lax.all_gather(strip.reshape(96, HD), 'col', axis=0, tiled=True)  35.2 us
    ppermute x26, waiting for transfers between devices, send(): return lax.ppermute(value, AXES, pairs)  31.1 us
    pallas_call x2, Pallas kernels, attend(): pl.pallas_call(functools.partial(attend_kernel, half), grid=(H // STEP,),...  26.1 us
    pallas_call x2, Pallas kernels, project(): pl.pallas_call(functools.partial(project_kernel, half), grid_spec=grid_sp...  23 us
    pallas_call x3, Pallas kernels, pack(): pl.pallas_call(functools.partial(pack_kernel, parts), out_shape=[jax.Shap...  9.37 us
    unnamed x56, local copies, waits for them, and re-layouts  5.34 us
  transfers between devices with their start and end apart: 27, of which 10 were waited for; matrix products, arithmetic and copies ran while one was open for 3% of the time, Pallas kernels for 23%

profile of v14, /device:TPU:1, one launch (start us, length us, event | category | flops | bytes accessed | tf_op | source)
XLA Modules:
  0.0 196.7 jit_solution(10979438883559587304)
XLA Ops:
  6.5 2.5 %pack.3 = (bf16[3,2,8,8,1536]{4,3,2,1,0:T(8,128)(2,1)}, bf16[3,2,8,8,1536]{4,3,2,1,0:T(8,128)(2,1)}) custom-call(s32[1]{0:T(128)} %bitcast.meta, bf16[4,2,8,2,8,1536]{5,4,3,2,1,0:T(8,128)(2,1)} %bitcast.48, bf16[4,2,8,2,8,1536]{5,4,3,2,1,0:T(8,128)(2,1)} %bitcast.51, bf16[4,2,8,2,8,1536]{5,4,3,2,1,0:T(8,128)(2,1)} %bitcast.54), custom_call_target="tpu_custom_call" | custom-call | bytes 6291456 | tf_op jit(solution)/shard_map/pack/pallas_call | solution.py:98
  9.1 4.7 %collective-permute-start.2 = (bf16[24,1536]{1,0:T(8,128)(2,1)S(1)}, bf16[24,1536]{1,0:T(8,128)(2,1)S(1)}, u32[]{:S(2)}, u32[]{:S(2)}) collective-permute-start(bf16[24,1536]{1,0:T(8,128)(2,1)S(1)} %bitcast.68), channel_id=1, source_target_pairs={{0,80},{1,81},{2,82},{3,83},{4,84},{5,85},{6,86},{7,87},{8,88},{9,... | collective-permute-start | bytes 221192 | tf_op jit(solution)/shard_map/ppermute | solution.py:59
  14.4 4.1 %collective-permute-start.3 = (bf16[3,128,1536]{2,1,0:T(8,128)(2,1)}, bf16[3,128,1536]{2,1,0:T(8,128)(2,1)S(1)}, u32[]{:S(2)}, u32[]{:S(2)}) collective-permute-start(bf16[3,128,1536]{2,1,0:T(8,128)(2,1)} %bitcast.73), channel_id=1, source_target_pairs={{0,4},{1,5},{2,6},{3,7},{4,8},{5,9},{6,10},{7,11},{8,12},{9,13},{1... | collective-permute-start | bytes 3538952 | tf_op jit(solution)/shard_map/ppermute | solution.py:59
  18.6 2.7 %collective-permute-start.4 = (bf16[3,128,1536]{2,1,0:T(8,128)(2,1)}, bf16[3,128,1536]{2,1,0:T(8,128)(2,1)S(1)}, u32[]{:S(2)}, u32[]{:S(2)}) collective-permute-start(bf16[3,128,1536]{2,1,0:T(8,128)(2,1)} %bitcast.72), channel_id=1, source_target_pairs={{0,1},{1,2},{2,3},{3,0},{4,5},{5,6},{6,7},{7,4},{8,9},{9,10},{10,1... | collective-permute-start | bytes 3538952 | tf_op jit(solution)/shard_map/ppermute | solution.py:59
  22.0 2.5 %pack.4 = (bf16[3,2,8,8,1536]{4,3,2,1,0:T(8,128)(2,1)}, bf16[3,2,8,8,1536]{4,3,2,1,0:T(8,128)(2,1)}) custom-call(s32[1]{0:T(128)} %bitcast.meta, bf16[4,2,8,2,8,1536]{5,4,3,2,1,0:T(8,128)(2,1)} %bitcast.49, bf16[4,2,8,2,8,1536]{5,4,3,2,1,0:T(8,128)(2,1)} %bitcast.52, bf16[4,2,8,2,8,1536]{5,4,3,2,1,0:T(8,128)(2,1)} %bitcast.55), custom_call_target="tpu_custom_call" | custom-call | bytes 6291456 | tf_op jit(solution)/shard_map/pack/pallas_call | solution.py:98
  24.5 1.4 pad_add_fusion
  26.1 4.3 %pack.5 = (bf16[2,2,8,8,1536]{4,3,2,1,0:T(8,128)(2,1)}, bf16[2,2,8,8,1536]{4,3,2,1,0:T(8,128)(2,1)}, bf16[3,2,8,8,1536]{4,3,2,1,0:T(8,128)(2,1)}, bf16[3,2,8,8,1...) custom-call(s32[1]{0:T(128)} %bitcast.meta, ...), custom_call_target="tpu_custom_call" | custom-call | bytes 12582912 | tf_op jit(solution)/shard_map/pack/pallas_call | solution.py:98
  31.3 5.1 %collective-permute-done.3.x = bf16[3,128,1536]{2,1,0:T(8,128)(2,1)S(1)} collective-permute-done((bf16[3,128,1536]{2,1,0:T(8,128)(2,1)}, bf16[3,128,1536]{2,1,0:T(8,128)(2,1)S(1)}, u32[]{:S(2)}, u32[]{:S(2)}) %collective-permute-start.3) | collective-permute-done | bytes 1179680 | tf_op jit(solution)/shard_map/ppermute | solution.py:59
  36.4 3.7 %collective-permute-done.4.y = bf16[3,128,1536]{2,1,0:T(8,128)(2,1)S(1)} collective-permute-done((bf16[3,128,1536]{2,1,0:T(8,128)(2,1)}, bf16[3,128,1536]{2,1,0:T(8,128)(2,1)S(1)}, u32[]{:S(2)}, u32[]{:S(2)}) %collective-permute-start.4) | collective-permute-done | bytes 1179680 | tf_op jit(solution)/shard_map/ppermute | solution.py:59
  41.4 5.3 %collective-permute-done.5.x = bf16[3,128,1536]{2,1,0:T(8,128)(2,1)S(1)} collective-permute-done((bf16[3,128,1536]{2,1,0:T(8,128)(2,1)}, bf16[3,128,1536]{2,1,0:T(8,128)(2,1)S(1)}, u32[]{:S(2)}, u32[]{:S(2)}) %collective-permute-start.5) | collective-permute-done | bytes 1179680 | tf_op jit(solution)/shard_map/ppermute | solution.py:59
  48.5 1.7 pad_maximum_fusion.1
  50.2 1.9 collective-permute-start.12
  52.1 5.1 %collective-permute-start.13 = (bf16[3,2,128,1536]{3,2,1,0:T(8,128)(2,1)}, bf16[3,2,128,1536]{3,2,1,0:T(8,128)(2,1)}, u32[]{:S(2)}, u32[]{:S(2)}) collective-permute-start(bf16[3,2,128,1536]{3,2,1,0:T(8,128)(2,1)} %pad_maximum_fusion.1), channel_id=1, source_target_pairs={{0,32},{1,33},{2,34},{3,35},{4,36},{5,37},{6,38},{7,39},{8,40},{9,... | collective-permute-start | bytes 7077896 | tf_op jit(solution)/shard_map/ppermute | solution.py:59
  57.3 4.6 %collective-permute-start.8 = (bf16[3,128,1536]{2,1,0:T(8,128)(2,1)}, bf16[3,128,1536]{2,1,0:T(8,128)(2,1)S(1)}, u32[]{:S(2)}, u32[]{:S(2)}) collective-permute-start(bf16[3,128,1536]{2,1,0:T(8,128)(2,1)} %bitcast.76), channel_id=1, source_target_pairs={{0,5},{1,6},{2,7},{3,4},{4,9},{5,10},{6,11},{7,8},{8,13},{9,14},{1... | collective-permute-start | bytes 3538952 | tf_op jit(solution)/shard_map/ppermute | solution.py:59
  61.8 35.2 %all-gather.2.cloned.1.call-done = bf16[384,1536]{1,0:T(8,128)(2,1)} async-done(((bf16[96,1536]{1,0:T(8,128)(2,1)}), bf16[384,1536]{1,0:T(8,128)(2,1)}) %all-gather.2.cloned.1.call-update) | async-done | bytes 1179664 | tf_op jit(solution)/shard_map/all_gather | solution.py:325
  97.0 1.4 copy.8
  98.4 2.0 %collective-permute-start.7 = (bf16[384,1536]{1,0:T(8,128)(2,1)S(1)}, bf16[384,1536]{1,0:T(8,128)(2,1)S(1)}, u32[]{:S(2)}, u32[]{:S(2)}) collective-permute-start(bf16[384,1536]{1,0:T(8,128)(2,1)S(1)} %bitcast.57), channel_id=1, source_target_pairs={{0,4},{1,5},{2,6},{3,7},{4,8},{5,9},{6,10},{7,11},{8,12},{9,13},{1... | collective-permute-start | bytes 3538952 | tf_op jit(solution)/shard_map/ppermute | solution.py:59
  100.4 2.1 %collective-permute-start.9 = (bf16[2,128,1536]{2,1,0:T(8,128)(2,1)S(1)}, bf16[2,128,1536]{2,1,0:T(8,128)(2,1)S(1)}, u32[]{:S(2)}, u32[]{:S(2)}) collective-permute-start(bf16[2,128,1536]{2,1,0:T(8,128)(2,1)S(1)} %slice.28), channel_id=1, source_target_pairs={{32,0},{33,1},{34,2},{35,3},{36,4},{37,5},{38,6},{39,7},{40,8},{41... | collective-permute-start | bytes 2359304 | tf_op jit(solution)/shard_map/ppermute | solution.py:59
  103.8 5.0 %collective-permute-start.11 = (bf16[2,128,1536]{2,1,0:T(8,128)(2,1)S(1)}, bf16[2,128,1536]{2,1,0:T(8,128)(2,1)S(1)}, u32[]{:S(2)}, u32[]{:S(2)}) collective-permute-start(bf16[2,128,1536]{2,1,0:T(8,128)(2,1)S(1)} %slice.29), channel_id=1, source_target_pairs={{0,32},{1,33},{2,34},{3,35},{4,36},{5,37},{6,38},{7,39},{8,40},{9,... | collective-permute-start | bytes 2359304 | tf_op jit(solution)/shard_map/ppermute | solution.py:59
  108.7 6.8 %collective-permute-done.9.hd = bf16[2,128,1536]{2,1,0:T(8,128)(2,1)S(1)} collective-permute-done((bf16[2,128,1536]{2,1,0:T(8,128)(2,1)S(1)}, bf16[2,128,1536]{2,1,0:T(8,128)(2,1)S(1)}, u32[]{:S(2)}, u32[]{:S(2)}) %collective-permute-start.9) | collective-permute-done | bytes 786464 | tf_op jit(solution)/shard_map/ppermute | solution.py:59
  115.6 2.1 %collective-permute-done.11.hd = bf16[2,128,1536]{2,1,0:T(8,128)(2,1)S(1)} collective-permute-done((bf16[2,128,1536]{2,1,0:T(8,128)(2,1)S(1)}, bf16[2,128,1536]{2,1,0:T(8,128)(2,1)S(1)}, u32[]{:S(2)}, u32[]{:S(2)}) %collective-permute-start.11) | collective-permute-done | bytes 786464 | tf_op jit(solution)/shard_map/ppermute | solution.py:59
  118.5 2.6 %collective-permute-start.14 = (bf16[384,1536]{1,0:T(8,128)(2,1)S(1)}, bf16[384,1536]{1,0:T(8,128)(2,1)S(1)}, u32[]{:S(2)}, u32[]{:S(2)}) collective-permute-start(bf16[384,1536]{1,0:T(8,128)(2,1)S(1)} %collective-permute-done.7.refs_5_), channel_id=1, source_target_pairs={{0,4},{1,5},{2,6},{3,7},{4,8},{5,9},{6,10},{7,11},{8,12},{9,13},{1... | collective-permute-start | bytes 3538952 | tf_op jit(solution)/shard_map/ppermute | solution.py:59
  121.2 13.0 %attend.2 = (bf16[128,1536]{1,0:T(8,128)(2,1)}, bf16[128,1536]{1,0:T(8,128)(2,1)}, bf16[128,1536]{1,0:T(8,128)(2,1)}, bf16[128,1536]{1,0:T(8,128)(2,1)}) custom-call(s32[4]{0:T(128)} %get-tuple-element.85.meta, bf16[2,128,1536]{2,1,0:T(8,128)(2,1)} %bitcast.66, bf16[1,128,1536]{2,1,0:T(8,128)(2,1)} %bitcast.79, bf16[3,128,1536]{2,1,0:T(8,128)(2,1)} %copy-done.12, ...), custom_call_target="tpu_custom_call" | custom-call | flops 6442450944 | bytes 10485760 | tf_op jit(solution)/shard_map/attend/pallas_call | solution.py:188
  134.2 2.0 %collective-permute-start.18 = (bf16[128,1536]{1,0:T(8,128)(2,1)}, bf16[128,1536]{1,0:T(8,128)(2,1)S(1)}, u32[]{:S(2)}, u32[]{:S(2)}) collective-permute-start(bf16[128,1536]{1,0:T(8,128)(2,1)} %get-tuple-element.104), channel_id=1, source_target_pairs={{28,0},{29,1},{30,2},{31,3},{0,4},{1,5},{2,6},{3,7},{4,8},{5,9},{6... | collective-permute-start | bytes 1179656 | tf_op jit(solution)/shard_map/ppermute | solution.py:59
  136.3 2.3 %collective-permute-start.19 = (bf16[128,1536]{1,0:T(8,128)(2,1)}, bf16[128,1536]{1,0:T(8,128)(2,1)S(1)}, u32[]{:S(2)}, u32[]{:S(2)}) collective-permute-start(bf16[128,1536]{1,0:T(8,128)(2,1)} %get-tuple-element.105), channel_id=1, source_target_pairs={{3,0},{0,1},{1,2},{2,3},{7,4},{4,5},{5,6},{6,7},{11,8},{8,9},{9,10... | collective-permute-start | bytes 1179656 | tf_op jit(solution)/shard_map/ppermute | solution.py:59
  138.8 13.1 %attend.3 = (bf16[128,1536]{1,0:T(8,128)(2,1)}, bf16[128,1536]{1,0:T(8,128)(2,1)}, bf16[128,1536]{1,0:T(8,128)(2,1)}, bf16[128,1536]{1,0:T(8,128)(2,1)}) custom-call(s32[4]{0:T(128)} %get-tuple-element.85.meta, bf16[2,128,1536]{2,1,0:T(8,128)(2,1)} %bitcast.64, bf16[1,128,1536]{2,1,0:T(8,128)(2,1)} %bitcast.78, bf16[3,128,1536]{2,1,0:T(8,128)(2,1)} %copy-done.10, ...), custom_call_target="tpu_custom_call" | custom-call | flops 6442450944 | bytes 10485760 | tf_op jit(solution)/shard_map/attend/pallas_call | solution.py:188
  152.0 3.7 %collective-permute-done.20.refs_3_ = bf16[128,1536]{1,0:T(8,128)(2,1)S(1)} collective-permute-done((bf16[128,1536]{1,0:T(8,128)(2,1)}, bf16[128,1536]{1,0:T(8,128)(2,1)S(1)}, u32[]{:S(2)}, u32[]{:S(2)}) %collective-permute-start.20) | collective-permute-done | bytes 393248 | tf_op jit(solution)/shard_map/ppermute | solution.py:59
  155.7 4.3 %collective-permute-start.24 = (bf16[384,1536]{1,0:T(8,128)(2,1)S(1)}, bf16[384,1536]{1,0:T(8,128)(2,1)S(1)}, u32[]{:S(2)}, u32[]{:S(2)}) collective-permute-start(bf16[384,1536]{1,0:T(8,128)(2,1)S(1)} %collective-permute-done.14.refs_6_), channel_id=1, source_target_pairs={{0,32},{1,33},{2,34},{3,35},{4,36},{5,37},{6,38},{7,39},{8,40},{9,... | collective-permute-start | bytes 3538952 | tf_op jit(solution)/shard_map/ppermute | solution.py:59
  160.1 2.4 %collective-permute-done.24.refs_10_ = bf16[384,1536]{1,0:T(8,128)(2,1)S(1)} collective-permute-done((bf16[384,1536]{1,0:T(8,128)(2,1)S(1)}, bf16[384,1536]{1,0:T(8,128)(2,1)S(1)}, u32[]{:S(2)}, u32[]{:S(2)}) %collective-permute-start.24) | collective-permute-done | bytes 1179680 | tf_op jit(solution)/shard_map/ppermute | solution.py:59
  162.4 1.7 collective-permute-done.25.refs_11_
  165.2 11.5 %project.2.refs_13_ = bf16[4,16,16,3072]{3,2,1,0:T(8,128)(2,1)} custom-call(s32[4]{0:T(128)} %get-tuple-element.85.meta, s32[4]{0:T(128)} %get-tuple-element.86.places, bf16[128,1536]{1,0:T(8,128)(2,1)} %get-tuple-element.125.refs_0_, bf16[128,1536]{1,0:T(8,128)(2,1)} %copy-done.18, bf16[128,1536]{1,0:T(8,128)(2,1)} %copy-done.19, ...), custom_call_target="tpu_custom_call" | custom-call | flops 4831838208 | bytes 17825792 | tf_op jit(solution)/shard_map/project/pallas_call | solution.py:273
  178.4 11.5 %project.3 = bf16[4,16,16,3072]{3,2,1,0:T(8,128)(2,1)} custom-call(s32[4]{0:T(128)} %get-tuple-element.85.meta, s32[4]{0:T(128)} %get-tuple-element.86.places, bf16[128,1536]{1,0:T(8,128)(2,1)} %get-tuple-element.117.refs_0_, bf16[128,1536]{1,0:T(8,128)(2,1)} %copy-done.15, bf16[128,1536]{1,0:T(8,128)(2,1)} %copy-done.16, ...), custom_call_target="tpu_custom_call", output_to_operand_aliasing={{}: (15, {})} | custom-call | flops 4831838208 | bytes 17825792 | tf_op jit(solution)/shard_map/project/pallas_call | solution.py:273
  (99 shorter events, 10.6 us)
Async XLA Ops:
  6.5 90.5 %all-gather.2.cloned.1.call-start = ((), (), s32[]{:S(2)}) async-start(), calls=%async_computation | async-start | bytes 1474560 | tf_op jit(solution)/shard_map/all_gather | solution.py:325
  6.5 14.8 %copy-start.24 = (s32[128]{0:T(128)S(1)}, s32[128]{0:T(128)}, u32[]{:S(2)}) copy-start(s32[128]{0:T(128)} %param.11) | copy-start | bytes 1540
  9.1 16.8 %collective-permute-start.2 = (bf16[24,1536]{1,0:T(8,128)(2,1)S(1)}, bf16[24,1536]{1,0:T(8,128)(2,1)S(1)}, u32[]{:S(2)}, u32[]{:S(2)}) collective-permute-start(bf16[24,1536]{1,0:T(8,128)(2,1)S(1)} %bitcast.68), channel_id=1, source_target_pairs={{0,80},{1,81},{2,82},{3,83},{4,84},{5,85},{6,86},{7,87},{8,88},{9,... | collective-permute-start | bytes 221192 | tf_op jit(solution)/shard_map/ppermute | solution.py:59
  13.7 12.2 %collective-permute-start.1 = (bf16[24,1536]{1,0:T(8,128)(2,1)S(1)}, bf16[24,1536]{1,0:T(8,128)(2,1)S(1)}, u32[]{:S(2)}, u32[]{:S(2)}) collective-permute-start(bf16[24,1536]{1,0:T(8,128)(2,1)S(1)} %bitcast.69), channel_id=1, source_target_pairs={{0,64},{1,65},{2,66},{3,67},{4,68},{5,69},{6,70},{7,71},{8,72},{9,... | collective-permute-start | bytes 221192 | tf_op jit(solution)/shard_map/ppermute | solution.py:59
  13.7 12.2 %collective-permute-start = (bf16[24,1536]{1,0:T(8,128)(2,1)S(1)}, bf16[24,1536]{1,0:T(8,128)(2,1)S(1)}, u32[]{:S(2)}, u32[]{:S(2)}) collective-permute-start(bf16[24,1536]{1,0:T(8,128)(2,1)S(1)} %bitcast.70), channel_id=1, source_target_pairs={{0,16},{1,17},{2,18},{3,19},{4,20},{5,21},{6,22},{7,23},{8,24},{9,... | collective-permute-start | bytes 221192 | tf_op jit(solution)/shard_map/ppermute | solution.py:59
  14.4 21.9 %collective-permute-start.3 = (bf16[3,128,1536]{2,1,0:T(8,128)(2,1)}, bf16[3,128,1536]{2,1,0:T(8,128)(2,1)S(1)}, u32[]{:S(2)}, u32[]{:S(2)}) collective-permute-start(bf16[3,128,1536]{2,1,0:T(8,128)(2,1)} %bitcast.73), channel_id=1, source_target_pairs={{0,4},{1,5},{2,6},{3,7},{4,8},{5,9},{6,10},{7,11},{8,12},{9,13},{1... | collective-permute-start | bytes 3538952 | tf_op jit(solution)/shard_map/ppermute | solution.py:59
  18.6 21.6 %collective-permute-start.4 = (bf16[3,128,1536]{2,1,0:T(8,128)(2,1)}, bf16[3,128,1536]{2,1,0:T(8,128)(2,1)S(1)}, u32[]{:S(2)}, u32[]{:S(2)}) collective-permute-start(bf16[3,128,1536]{2,1,0:T(8,128)(2,1)} %bitcast.72), channel_id=1, source_target_pairs={{0,1},{1,2},{2,3},{3,0},{4,5},{5,6},{6,7},{7,4},{8,9},{9,10},{10,1... | collective-permute-start | bytes 3538952 | tf_op jit(solution)/shard_map/ppermute | solution.py:59
  26.0 20.7 %collective-permute-start.5 = (bf16[3,128,1536]{2,1,0:T(8,128)(2,1)}, bf16[3,128,1536]{2,1,0:T(8,128)(2,1)S(1)}, u32[]{:S(2)}, u32[]{:S(2)}) collective-permute-start(bf16[3,128,1536]{2,1,0:T(8,128)(2,1)} %bitcast.77), channel_id=1, source_target_pairs={{0,28},{1,29},{2,30},{3,31},{4,0},{5,1},{6,2},{7,3},{8,4},{9,5},{1... | collective-permute-start | bytes 3538952 | tf_op jit(solution)/shard_map/ppermute | solution.py:59
  26.1 21.0 %collective-permute-start.6 = (bf16[3,128,1536]{2,1,0:T(8,128)(2,1)}, bf16[3,128,1536]{2,1,0:T(8,128)(2,1)S(1)}, u32[]{:S(2)}, u32[]{:S(2)}) collective-permute-start(bf16[3,128,1536]{2,1,0:T(8,128)(2,1)} %bitcast.75), channel_id=1, source_target_pairs={{0,3},{1,0},{2,1},{3,2},{4,7},{5,4},{6,5},{7,6},{8,11},{9,8},{10,9... | collective-permute-start | bytes 3538952 | tf_op jit(solution)/shard_map/ppermute | solution.py:59
  50.2 67.5 %collective-permute-start.12 = (bf16[3,2,128,1536]{3,2,1,0:T(8,128)(2,1)S(1)}, bf16[3,2,128,1536]{3,2,1,0:T(8,128)(2,1)}, u32[]{:S(2)}, u32[]{:S(2)}) collective-permute-start(bf16[3,2,128,1536]{3,2,1,0:T(8,128)(2,1)S(1)} %pad_maximum_fusion), channel_id=1, source_target_pairs={{32,0},{33,1},{34,2},{35,3},{36,4},{37,5},{38,6},{39,7},{40,8},{41... | collective-permute-start | bytes 7077896 | tf_op jit(solution)/shard_map/ppermute | solution.py:59
  52.1 65.6 %collective-permute-start.13 = (bf16[3,2,128,1536]{3,2,1,0:T(8,128)(2,1)}, bf16[3,2,128,1536]{3,2,1,0:T(8,128)(2,1)}, u32[]{:S(2)}, u32[]{:S(2)}) collective-permute-start(bf16[3,2,128,1536]{3,2,1,0:T(8,128)(2,1)} %pad_maximum_fusion.1), channel_id=1, source_target_pairs={{0,32},{1,33},{2,34},{3,35},{4,36},{5,37},{6,38},{7,39},{8,40},{9,... | collective-permute-start | bytes 7077896 | tf_op jit(solution)/shard_map/ppermute | solution.py:59
  57.3 43.1 %collective-permute-start.8 = (bf16[3,128,1536]{2,1,0:T(8,128)(2,1)}, bf16[3,128,1536]{2,1,0:T(8,128)(2,1)S(1)}, u32[]{:S(2)}, u32[]{:S(2)}) collective-permute-start(bf16[3,128,1536]{2,1,0:T(8,128)(2,1)} %bitcast.76), channel_id=1, source_target_pairs={{0,5},{1,6},{2,7},{3,4},{4,9},{5,10},{6,11},{7,8},{8,13},{9,14},{1... | collective-permute-start | bytes 3538952 | tf_op jit(solution)/shard_map/ppermute | solution.py:59
  61.8 40.7 %collective-permute-start.10 = (bf16[3,128,1536]{2,1,0:T(8,128)(2,1)}, bf16[3,128,1536]{2,1,0:T(8,128)(2,1)}, u32[]{:S(2)}, u32[]{:S(2)}) collective-permute-start(bf16[3,128,1536]{2,1,0:T(8,128)(2,1)} %bitcast.74), channel_id=1, source_target_pairs={{0,31},{1,28},{2,29},{3,30},{4,3},{5,0},{6,1},{7,2},{8,7},{9,4},{1... | collective-permute-start | bytes 3538952 | tf_op jit(solution)/shard_map/ppermute | solution.py:59
  98.4 22.8 %copy-start = (bf16[4,4,24,1536]{3,2,1,0:T(8,128)(2,1)}, bf16[4,4,24,1536]{3,2,1,0:T(8,128)(2,1)S(1)}, u32[]{:S(2)}) copy-start(bf16[4,4,24,1536]{3,2,1,0:T(8,128)(2,1)S(1)} %copy.8) | copy-start | bytes 3538948
  98.4 19.3 %collective-permute-start.7 = (bf16[384,1536]{1,0:T(8,128)(2,1)S(1)}, bf16[384,1536]{1,0:T(8,128)(2,1)S(1)}, u32[]{:S(2)}, u32[]{:S(2)}) collective-permute-start(bf16[384,1536]{1,0:T(8,128)(2,1)S(1)} %bitcast.57), channel_id=1, source_target_pairs={{0,4},{1,5},{2,6},{3,7},{4,8},{5,9},{6,10},{7,11},{8,12},{9,13},{1... | collective-permute-start | bytes 3538952 | tf_op jit(solution)/shard_map/ppermute | solution.py:59
  100.4 15.1 %collective-permute-start.9 = (bf16[2,128,1536]{2,1,0:T(8,128)(2,1)S(1)}, bf16[2,128,1536]{2,1,0:T(8,128)(2,1)S(1)}, u32[]{:S(2)}, u32[]{:S(2)}) collective-permute-start(bf16[2,128,1536]{2,1,0:T(8,128)(2,1)S(1)} %slice.28), channel_id=1, source_target_pairs={{32,0},{33,1},{34,2},{35,3},{36,4},{37,5},{38,6},{39,7},{40,8},{41... | collective-permute-start | bytes 2359304 | tf_op jit(solution)/shard_map/ppermute | solution.py:59
  103.8 13.9 %collective-permute-start.11 = (bf16[2,128,1536]{2,1,0:T(8,128)(2,1)S(1)}, bf16[2,128,1536]{2,1,0:T(8,128)(2,1)S(1)}, u32[]{:S(2)}, u32[]{:S(2)}) collective-permute-start(bf16[2,128,1536]{2,1,0:T(8,128)(2,1)S(1)} %slice.29), channel_id=1, source_target_pairs={{0,32},{1,33},{2,34},{3,35},{4,36},{5,37},{6,38},{7,39},{8,40},{9,... | collective-permute-start | bytes 2359304 | tf_op jit(solution)/shard_map/ppermute | solution.py:59
  117.7 16.5 %copy-start.1 = (bf16[384,1536]{1,0:T(8,128)(2,1)}, bf16[384,1536]{1,0:T(8,128)(2,1)S(1)}, u32[]{:S(2)}) copy-start(bf16[384,1536]{1,0:T(8,128)(2,1)S(1)} %collective-permute-done.7.refs_5_) | copy-start | bytes 3538948
  117.7 16.5 %collective-permute-start.17 = (bf16[384,1536]{1,0:T(8,128)(2,1)S(1)}, bf16[384,1536]{1,0:T(8,128)(2,1)S(1)}, u32[]{:S(2)}, u32[]{:S(2)}) collective-permute-start(bf16[384,1536]{1,0:T(8,128)(2,1)S(1)} %collective-permute-done.7.refs_5_), channel_id=1, source_target_pairs={{0,32},{1,33},{2,34},{3,35},{4,36},{5,37},{6,38},{7,39},{8,40},{9,... | collective-permute-start | bytes 3538952 | tf_op jit(solution)/shard_map/ppermute | solution.py:59
  118.0 16.3 %collective-permute-start.16 = (bf16[384,1536]{1,0:T(8,128)(2,1)S(1)}, bf16[384,1536]{1,0:T(8,128)(2,1)S(1)}, u32[]{:S(2)}, u32[]{:S(2)}) collective-permute-start(bf16[384,1536]{1,0:T(8,128)(2,1)S(1)} %bitcast.58), channel_id=1, source_target_pairs={{0,32},{1,33},{2,34},{3,35},{4,36},{5,37},{6,38},{7,39},{8,40},{9,... | collective-permute-start | bytes 3538952 | tf_op jit(solution)/shard_map/ppermute | solution.py:59
  118.5 33.4 %collective-permute-start.14 = (bf16[384,1536]{1,0:T(8,128)(2,1)S(1)}, bf16[384,1536]{1,0:T(8,128)(2,1)S(1)}, u32[]{:S(2)}, u32[]{:S(2)}) collective-permute-start(bf16[384,1536]{1,0:T(8,128)(2,1)S(1)} %collective-permute-done.7.refs_5_), channel_id=1, source_target_pairs={{0,4},{1,5},{2,6},{3,7},{4,8},{5,9},{6,10},{7,11},{8,12},{9,13},{1... | collective-permute-start | bytes 3538952 | tf_op jit(solution)/shard_map/ppermute | solution.py:59
  121.2 30.8 %collective-permute-start.15 = (bf16[384,1536]{1,0:T(8,128)(2,1)S(1)}, bf16[384,1536]{1,0:T(8,128)(2,1)S(1)}, u32[]{:S(2)}, u32[]{:S(2)}) collective-permute-start(bf16[384,1536]{1,0:T(8,128)(2,1)S(1)} %bitcast.59), channel_id=1, source_target_pairs={{0,12},{1,13},{2,14},{3,15},{4,0},{5,1},{6,2},{7,3},{8,4},{9,5},{1... | collective-permute-start | bytes 3538952 | tf_op jit(solution)/shard_map/ppermute | solution.py:59
  134.2 17.7 %copy-start.2 = (bf16[384,1536]{1,0:T(8,128)(2,1)}, bf16[384,1536]{1,0:T(8,128)(2,1)S(1)}, u32[]{:S(2)}) copy-start(bf16[384,1536]{1,0:T(8,128)(2,1)S(1)} %collective-permute-done.17.refs_9_) | copy-start | bytes 3538948
  134.2 17.7 %copy-start.3 = (bf16[384,1536]{1,0:T(8,128)(2,1)}, bf16[384,1536]{1,0:T(8,128)(2,1)S(1)}, u32[]{:S(2)}) copy-start(bf16[384,1536]{1,0:T(8,128)(2,1)S(1)} %collective-permute-done.16.refs_8_) | copy-start | bytes 3538948
  134.2 17.7 %collective-permute-start.18 = (bf16[128,1536]{1,0:T(8,128)(2,1)}, bf16[128,1536]{1,0:T(8,128)(2,1)S(1)}, u32[]{:S(2)}, u32[]{:S(2)}) collective-permute-start(bf16[128,1536]{1,0:T(8,128)(2,1)} %get-tuple-element.104), channel_id=1, source_target_pairs={{28,0},{29,1},{30,2},{31,3},{0,4},{1,5},{2,6},{3,7},{4,8},{5,9},{6... | collective-permute-start | bytes 1179656 | tf_op jit(solution)/shard_map/ppermute | solution.py:59
  136.3 15.7 %collective-permute-start.19 = (bf16[128,1536]{1,0:T(8,128)(2,1)}, bf16[128,1536]{1,0:T(8,128)(2,1)S(1)}, u32[]{:S(2)}, u32[]{:S(2)}) collective-permute-start(bf16[128,1536]{1,0:T(8,128)(2,1)} %get-tuple-element.105), channel_id=1, source_target_pairs={{3,0},{0,1},{1,2},{2,3},{7,4},{4,5},{5,6},{6,7},{11,8},{8,9},{9,10... | collective-permute-start | bytes 1179656 | tf_op jit(solution)/shard_map/ppermute | solution.py:59
  138.6 17.1 %collective-permute-start.20 = (bf16[128,1536]{1,0:T(8,128)(2,1)}, bf16[128,1536]{1,0:T(8,128)(2,1)S(1)}, u32[]{:S(2)}, u32[]{:S(2)}) collective-permute-start(bf16[128,1536]{1,0:T(8,128)(2,1)} %get-tuple-element.106), channel_id=1, source_target_pairs={{31,0},{28,1},{29,2},{30,3},{3,4},{0,5},{1,6},{2,7},{7,8},{4,9},{5... | collective-permute-start | bytes 1179656 | tf_op jit(solution)/shard_map/ppermute | solution.py:59
  155.7 6.8 %collective-permute-start.24 = (bf16[384,1536]{1,0:T(8,128)(2,1)S(1)}, bf16[384,1536]{1,0:T(8,128)(2,1)S(1)}, u32[]{:S(2)}, u32[]{:S(2)}) collective-permute-start(bf16[384,1536]{1,0:T(8,128)(2,1)S(1)} %collective-permute-done.14.refs_6_), channel_id=1, source_target_pairs={{0,32},{1,33},{2,34},{3,35},{4,36},{5,37},{6,38},{7,39},{8,40},{9,... | collective-permute-start | bytes 3538952 | tf_op jit(solution)/shard_map/ppermute | solution.py:59
  160.0 4.2 %collective-permute-start.25 = (bf16[384,1536]{1,0:T(8,128)(2,1)S(1)}, bf16[384,1536]{1,0:T(8,128)(2,1)S(1)}, u32[]{:S(2)}, u32[]{:S(2)}) collective-permute-start(bf16[384,1536]{1,0:T(8,128)(2,1)S(1)} %collective-permute-done.15.refs_7_), channel_id=1, source_target_pairs={{0,32},{1,33},{2,34},{3,35},{4,36},{5,37},{6,38},{7,39},{8,40},{9,... | collective-permute-start | bytes 3538952 | tf_op jit(solution)/shard_map/ppermute | solution.py:59
  160.0 16.7 %collective-permute-start.21 = (bf16[128,1536]{1,0:T(8,128)(2,1)}, bf16[128,1536]{1,0:T(8,128)(2,1)S(1)}, u32[]{:S(2)}, u32[]{:S(2)}) collective-permute-start(bf16[128,1536]{1,0:T(8,128)(2,1)} %get-tuple-element.118), channel_id=1, source_target_pairs={{4,0},{5,1},{6,2},{7,3},{8,4},{9,5},{10,6},{11,7},{12,8},{13,9},{1... | collective-permute-start | bytes 1179656 | tf_op jit(solution)/shard_map/ppermute | solution.py:59
  160.0 16.7 %collective-permute-start.22 = (bf16[128,1536]{1,0:T(8,128)(2,1)}, bf16[128,1536]{1,0:T(8,128)(2,1)S(1)}, u32[]{:S(2)}, u32[]{:S(2)}) collective-permute-start(bf16[128,1536]{1,0:T(8,128)(2,1)} %get-tuple-element.119), channel_id=1, source_target_pairs={{1,0},{2,1},{3,2},{0,3},{5,4},{6,5},{7,6},{4,7},{9,8},{10,9},{11,1... | collective-permute-start | bytes 1179656 | tf_op jit(solution)/shard_map/ppermute | solution.py:59
  160.0 16.8 %collective-permute-start.23 = (bf16[128,1536]{1,0:T(8,128)(2,1)}, bf16[128,1536]{1,0:T(8,128)(2,1)S(1)}, u32[]{:S(2)}, u32[]{:S(2)}) collective-permute-start(bf16[128,1536]{1,0:T(8,128)(2,1)} %get-tuple-element.120), channel_id=1, source_target_pairs={{5,0},{6,1},{7,2},{4,3},{9,4},{10,5},{11,6},{8,7},{13,8},{14,9},{1... | collective-permute-start | bytes 1179656 | tf_op jit(solution)/shard_map/ppermute | solution.py:59
  (20 other events, 90.2 us)
Sparse Core Ops, SparseCore 0:
  50.3 46.6 all-gather.1

commit v15 on v10

--- a/solution.py
+++ b/solution.py
@@ -14,7 +14,7 @@
 HD = 1536
 F, R, C = 4, 8, 4
 AXES = ("frame", "row", "col")
-STEP = 2
+STEP = 4
 BIG = 1e30
 TILE = 768
 VMEM = 56 * 1024 * 1024
@@ -203,17 +203,18 @@
     )(meta, *pieces)
 
 
-def project_kernel(half, meta, places, *refs):
-    attended, own, other, tokens = refs[:4], refs[4:8], refs[8:12], refs[12]
+def project_kernel(half, sides, meta, places, *refs):
+    attended, chunks, tokens = refs[:4], refs[4 : 4 + 4 * len(sides)], refs[4 + 4 * len(sides)]
     out, lhs, held, sems = refs[-4:]
+    steps = 2 * len(sides)
     step = pl.program_id(0)
     core, x = lax.rem(meta[0], 2), lax.rem(meta[1], 4)
 
     def fetch(n):
-        side, zhi = divmod(n, 2)
-        k = core if side == 0 else 1 - core
+        which, zhi = divmod(n, 2)
+        k = core if sides[which] == 0 else 1 - core
         copies = []
-        for turn, src in enumerate(other if side else own):
+        for turn, src in enumerate(chunks[4 * which : 4 * which + 4]):
             at = lax.rem(x + turn * (2 * k - 1) + 4, 4)
             for zlo in range(2):
                 to = pl.ds(pl.multiple_of(zlo * 384 + at * 96, 32), 96)
@@ -234,13 +235,13 @@
             j = s + b * (1 - 2 * s)
             lhs[i * 2 + j] = attended[piece][...]
 
-    for n in range(4):
+    for n in range(steps):
 
         @pl.when(step == n)
         def _():
             for copy in fetch(n):
                 copy.wait()
-            if n < 3:
+            if n + 1 < steps:
                 for copy in fetch(n + 1):
                     copy.start()
 
@@ -253,14 +254,15 @@
         out[at] = (block + tokens[at].astype(jnp.float32)).astype(jnp.bfloat16)
 
 
-def project(half, attended, meta, places, chunks, tokens, partial=None):
+def project(half, sides, attended, meta, places, chunks, tokens, partial=None):
     extra = [] if partial is None else [partial]
-    block = pl.BlockSpec((2, 16, 16, TILE), lambda t, m, p: (half, 0, 0, p[t]))
+    first = 2 * sides[0]
+    block = pl.BlockSpec((2, 16, 16, TILE), lambda t, m, p: (half, 0, 0, p[t + first]))
     grid_spec = pltpu.PrefetchScalarGridSpec(
         num_scalar_prefetch=2,
-        grid=(D // TILE,),
+        grid=(2 * len(sides),),
         in_specs=[pl.BlockSpec((128, HD), lambda t, m, p: (0, 0))] * 4
-        + [pl.BlockSpec(memory_space=pl.ANY)] * 8
+        + [pl.BlockSpec(memory_space=pl.ANY)] * len(chunks)
         + [block]
         + [pl.BlockSpec(memory_space=pl.ANY)] * len(extra),
         out_specs=block,
@@ -271,12 +273,12 @@
         ],
     )
     return pl.pallas_call(
-        functools.partial(project_kernel, half),
+        functools.partial(project_kernel, half, sides),
         grid_spec=grid_spec,
         out_shape=jax.ShapeDtypeStruct((4, 16, 16, D), jnp.bfloat16),
-        input_output_aliases={} if partial is None else {15: 0},
+        input_output_aliases={} if partial is None else {7 + len(chunks): 0},
         compiler_params=pltpu.CompilerParams(vmem_limit_bytes=VMEM),
-        cost_estimate=pl.CostEstimate(flops=1024 * HD * D, bytes_accessed=17 * 2**20, transcendentals=0),
+        cost_estimate=pl.CostEstimate(flops=512 * len(sides) * HD * D, bytes_accessed=9 * len(sides) * 2**20, transcendentals=0),
         name="project",
     )(meta, places, *attended, *chunks, tokens, *extra)
 
@@ -336,9 +338,10 @@
     c2, c3, *rest = together(c2, c3, *attended1, *mixed0)
     attended1, mixed0 = rest[:4], rest[4:]
     attended0, s2, s3 = back(0, mixed0), swap(c2), swap(c3)
-    chunks = (c0, c1, c2, c3, s0, s1, s2, s3)
-    out = project(1, attended1, meta, places, chunks, tokens_in)
-    return project(0, attended0, meta, places, chunks, tokens_in, out)
+    own, other = (c0, c1, c2, c3), (s0, s1, s2, s3)
+    out = project(1, (0,), attended1, meta, places, own, tokens_in)
+    out = project(1, (1,), attended1, meta, places, other, tokens_in, out)
+    return project(0, (0, 1), attended0, meta, places, own + other, tokens_in, out)
 
 
 def solution(mesh):

time: 195 us -> 199 us (1.021); the launches traced: 194 us -> 196 us
  Pallas kernels: 59.6 us -> 62.9 us
  waiting for transfers between devices: 64.4 us -> 61.4 us
    pallas_call x2 -> x3, Pallas kernels: 23 us -> 27.4 us  [project(): pl.pallas_call(functools.partial(project_kernel, half, sides), grid_spec=...]
    ppermute x26, waiting for transfers between devices: 34.8 us -> 31.8 us  [send(): return lax.ppermute(value, AXES, pairs)]
  transfers between devices with their start and end apart: 27 -> 27, of which waited for: 11 -> 9; matrix products, arithmetic and copies ran while one was open for 3% -> 3% of each run, Pallas kernels for 23% -> 25%
where the time goes in v15:
time: 199 us; the launch traced here: 196 us
  Pallas kernels  62.9 us (32%)
  waiting for transfers between devices  61.4 us (31%)
  starting transfers between devices  43.8 us (22%)
  between operations  13.9 us (7%)
  local copies, waits for them, and re-layouts  9.75 us (5%)
  other arithmetic  3.88 us (2%)
    ppermute x26, starting transfers between devices, send(): return lax.ppermute(value, AXES, pairs)  43.8 us
    ppermute x26, waiting for transfers between devices, send(): return lax.ppermute(value, AXES, pairs)  31.8 us
    all_gather x1, waiting for transfers between devices, local(): strips = lax.all_gather(strip.reshape(96, HD), 'col', axis=0, tiled=True)  29.6 us
    pallas_call x3, Pallas kernels, project(): pl.pallas_call(functools.partial(project_kernel, half, sides), grid_spec=...  27.4 us
    pallas_call x2, Pallas kernels, attend(): pl.pallas_call(functools.partial(attend_kernel, half), grid=(H // STEP,),...  26.1 us
    pallas_call x3, Pallas kernels, pack(): pl.pallas_call(functools.partial(pack_kernel, parts), out_shape=[jax.Shap...  9.37 us
    unnamed x56, local copies, waits for them, and re-layouts  6.19 us
  transfers between devices with their start and end apart: 27, of which 9 were waited for; matrix products, arithmetic and copies ran while one was open for 3% of the time, Pallas kernels for 25%

profile of v15, /device:TPU:1, one launch (start us, length us, event | category | flops | bytes accessed | tf_op | source)
XLA Modules:
  0.0 195.7 jit_solution(17861229874817535486)
XLA Ops:
  6.5 2.5 %pack.3 = (bf16[3,2,8,8,1536]{4,3,2,1,0:T(8,128)(2,1)}, bf16[3,2,8,8,1536]{4,3,2,1,0:T(8,128)(2,1)}) custom-call(s32[1]{0:T(128)} %bitcast.meta, bf16[4,2,8,2,8,1536]{5,4,3,2,1,0:T(8,128)(2,1)} %bitcast.48, bf16[4,2,8,2,8,1536]{5,4,3,2,1,0:T(8,128)(2,1)} %bitcast.51, bf16[4,2,8,2,8,1536]{5,4,3,2,1,0:T(8,128)(2,1)} %bitcast.54), custom_call_target="tpu_custom_call" | custom-call | bytes 6291456 | tf_op jit(solution)/shard_map/pack/pallas_call | solution.py:98
  9.1 4.7 %collective-permute-start.2 = (bf16[24,1536]{1,0:T(8,128)(2,1)S(1)}, bf16[24,1536]{1,0:T(8,128)(2,1)S(1)}, u32[]{:S(2)}, u32[]{:S(2)}) collective-permute-start(bf16[24,1536]{1,0:T(8,128)(2,1)S(1)} %bitcast.68), channel_id=1, source_target_pairs={{0,80},{1,81},{2,82},{3,83},{4,84},{5,85},{6,86},{7,87},{8,88},{9,... | collective-permute-start | bytes 221192 | tf_op jit(solution)/shard_map/ppermute | solution.py:59
  14.4 4.1 %collective-permute-start.3 = (bf16[3,128,1536]{2,1,0:T(8,128)(2,1)}, bf16[3,128,1536]{2,1,0:T(8,128)(2,1)S(1)}, u32[]{:S(2)}, u32[]{:S(2)}) collective-permute-start(bf16[3,128,1536]{2,1,0:T(8,128)(2,1)} %bitcast.73), channel_id=1, source_target_pairs={{0,4},{1,5},{2,6},{3,7},{4,8},{5,9},{6,10},{7,11},{8,12},{9,13},{1... | collective-permute-start | bytes 3538952 | tf_op jit(solution)/shard_map/ppermute | solution.py:59
  18.6 2.7 %collective-permute-start.4 = (bf16[3,128,1536]{2,1,0:T(8,128)(2,1)}, bf16[3,128,1536]{2,1,0:T(8,128)(2,1)S(1)}, u32[]{:S(2)}, u32[]{:S(2)}) collective-permute-start(bf16[3,128,1536]{2,1,0:T(8,128)(2,1)} %bitcast.72), channel_id=1, source_target_pairs={{0,1},{1,2},{2,3},{3,0},{4,5},{5,6},{6,7},{7,4},{8,9},{9,10},{10,1... | collective-permute-start | bytes 3538952 | tf_op jit(solution)/shard_map/ppermute | solution.py:59
  22.0 2.5 %pack.4 = (bf16[3,2,8,8,1536]{4,3,2,1,0:T(8,128)(2,1)}, bf16[3,2,8,8,1536]{4,3,2,1,0:T(8,128)(2,1)}) custom-call(s32[1]{0:T(128)} %bitcast.meta, bf16[4,2,8,2,8,1536]{5,4,3,2,1,0:T(8,128)(2,1)} %bitcast.49, bf16[4,2,8,2,8,1536]{5,4,3,2,1,0:T(8,128)(2,1)} %bitcast.52, bf16[4,2,8,2,8,1536]{5,4,3,2,1,0:T(8,128)(2,1)} %bitcast.55), custom_call_target="tpu_custom_call" | custom-call | bytes 6291456 | tf_op jit(solution)/shard_map/pack/pallas_call | solution.py:98
  24.5 1.3 pad_add_fusion
  26.0 4.3 %pack.5 = (bf16[2,2,8,8,1536]{4,3,2,1,0:T(8,128)(2,1)}, bf16[2,2,8,8,1536]{4,3,2,1,0:T(8,128)(2,1)}, bf16[3,2,8,8,1536]{4,3,2,1,0:T(8,128)(2,1)}, bf16[3,2,8,8,1...) custom-call(s32[1]{0:T(128)} %bitcast.meta, ...), custom_call_target="tpu_custom_call" | custom-call | bytes 12582912 | tf_op jit(solution)/shard_map/pack/pallas_call | solution.py:98
  31.2 5.3 %collective-permute-done.3.x = bf16[3,128,1536]{2,1,0:T(8,128)(2,1)S(1)} collective-permute-done((bf16[3,128,1536]{2,1,0:T(8,128)(2,1)}, bf16[3,128,1536]{2,1,0:T(8,128)(2,1)S(1)}, u32[]{:S(2)}, u32[]{:S(2)}) %collective-permute-start.3) | collective-permute-done | bytes 1179680 | tf_op jit(solution)/shard_map/ppermute | solution.py:59
  36.5 3.7 %collective-permute-done.4.y = bf16[3,128,1536]{2,1,0:T(8,128)(2,1)S(1)} collective-permute-done((bf16[3,128,1536]{2,1,0:T(8,128)(2,1)}, bf16[3,128,1536]{2,1,0:T(8,128)(2,1)S(1)}, u32[]{:S(2)}, u32[]{:S(2)}) %collective-permute-start.4) | collective-permute-done | bytes 1179680 | tf_op jit(solution)/shard_map/ppermute | solution.py:59
  41.5 5.2 %collective-permute-done.5.x = bf16[3,128,1536]{2,1,0:T(8,128)(2,1)S(1)} collective-permute-done((bf16[3,128,1536]{2,1,0:T(8,128)(2,1)}, bf16[3,128,1536]{2,1,0:T(8,128)(2,1)S(1)}, u32[]{:S(2)}, u32[]{:S(2)}) %collective-permute-start.5) | collective-permute-done | bytes 1179680 | tf_op jit(solution)/shard_map/ppermute | solution.py:59
  48.5 1.7 pad_maximum_fusion.1
  50.2 4.6 %collective-permute-start.7 = (bf16[3,128,1536]{2,1,0:T(8,128)(2,1)}, bf16[3,128,1536]{2,1,0:T(8,128)(2,1)S(1)}, u32[]{:S(2)}, u32[]{:S(2)}) collective-permute-start(bf16[3,128,1536]{2,1,0:T(8,128)(2,1)} %bitcast.77), channel_id=1, source_target_pairs={{0,5},{1,6},{2,7},{3,4},{4,9},{5,10},{6,11},{7,8},{8,13},{9,14},{1... | collective-permute-start | bytes 3538952 | tf_op jit(solution)/shard_map/ppermute | solution.py:59
  54.7 3.1 %collective-permute-start.12 = (bf16[3,2,128,1536]{3,2,1,0:T(8,128)(2,1)S(1)}, bf16[3,2,128,1536]{3,2,1,0:T(8,128)(2,1)}, u32[]{:S(2)}, u32[]{:S(2)}) collective-permute-start(bf16[3,2,128,1536]{3,2,1,0:T(8,128)(2,1)S(1)} %pad_maximum_fusion), channel_id=1, source_target_pairs={{32,0},{33,1},{34,2},{35,3},{36,4},{37,5},{38,6},{39,7},{40,8},{41... | collective-permute-start | bytes 7077896 | tf_op jit(solution)/shard_map/ppermute | solution.py:59
  57.9 3.9 %collective-permute-start.13 = (bf16[3,2,128,1536]{3,2,1,0:T(8,128)(2,1)}, bf16[3,2,128,1536]{3,2,1,0:T(8,128)(2,1)}, u32[]{:S(2)}, u32[]{:S(2)}) collective-permute-start(bf16[3,2,128,1536]{3,2,1,0:T(8,128)(2,1)} %pad_maximum_fusion.1), channel_id=1, source_target_pairs={{0,32},{1,33},{2,34},{3,35},{4,36},{5,37},{6,38},{7,39},{8,40},{9,... | collective-permute-start | bytes 7077896 | tf_op jit(solution)/shard_map/ppermute | solution.py:59
  61.8 29.6 %all-gather.2.cloned.1.call-done = bf16[384,1536]{1,0:T(8,128)(2,1)} async-done(((bf16[96,1536]{1,0:T(8,128)(2,1)}), bf16[384,1536]{1,0:T(8,128)(2,1)}) %all-gather.2.cloned.1.call-update) | async-done | bytes 1179664 | tf_op jit(solution)/shard_map/all_gather | solution.py:327
  91.4 1.4 copy.9
  92.9 3.2 %collective-permute-start.9 = (bf16[384,1536]{1,0:T(8,128)(2,1)S(1)}, bf16[384,1536]{1,0:T(8,128)(2,1)S(1)}, u32[]{:S(2)}, u32[]{:S(2)}) collective-permute-start(bf16[384,1536]{1,0:T(8,128)(2,1)S(1)} %bitcast.57), channel_id=1, source_target_pairs={{0,4},{1,5},{2,6},{3,7},{4,8},{5,9},{6,10},{7,11},{8,12},{9,13},{1... | collective-permute-start | bytes 3538952 | tf_op jit(solution)/shard_map/ppermute | solution.py:59
  96.1 1.2 slice.23
  97.3 2.8 %collective-permute-start.11 = (bf16[2,128,1536]{2,1,0:T(8,128)(2,1)S(1)}, bf16[2,128,1536]{2,1,0:T(8,128)(2,1)S(1)}, u32[]{:S(2)}, u32[]{:S(2)}) collective-permute-start(bf16[2,128,1536]{2,1,0:T(8,128)(2,1)S(1)} %slice.23), channel_id=1, source_target_pairs={{0,32},{1,33},{2,34},{3,35},{4,36},{5,37},{6,38},{7,39},{8,40},{9,... | collective-permute-start | bytes 2359304 | tf_op jit(solution)/shard_map/ppermute | solution.py:59
  100.1 1.9 collective-permute-start.10
  102.1 5.9 %collective-permute-done.12.h3 = bf16[3,2,128,1536]{3,2,1,0:T(8,128)(2,1)} collective-permute-done((bf16[3,2,128,1536]{3,2,1,0:T(8,128)(2,1)S(1)}, bf16[3,2,128,1536]{3,2,1,0:T(8,128)(2,1)}, u32[]{:S(2)}, u32[]{:S(2)}) %collective-permute-start.12) | collective-permute-done | bytes 2359328 | tf_op jit(solution)/shard_map/ppermute | solution.py:59
  108.0 5.7 %collective-permute-done.11.hd = bf16[2,128,1536]{2,1,0:T(8,128)(2,1)S(1)} collective-permute-done((bf16[2,128,1536]{2,1,0:T(8,128)(2,1)S(1)}, bf16[2,128,1536]{2,1,0:T(8,128)(2,1)S(1)}, u32[]{:S(2)}, u32[]{:S(2)}) %collective-permute-start.11) | collective-permute-done | bytes 786464 | tf_op jit(solution)/shard_map/ppermute | solution.py:59
  113.7 2.6 %collective-permute-done.10.hd = bf16[2,128,1536]{2,1,0:T(8,128)(2,1)S(1)} collective-permute-done((bf16[2,128,1536]{2,1,0:T(8,128)(2,1)S(1)}, bf16[2,128,1536]{2,1,0:T(8,128)(2,1)S(1)}, u32[]{:S(2)}, u32[]{:S(2)}) %collective-permute-start.10) | collective-permute-done | bytes 786464 | tf_op jit(solution)/shard_map/ppermute | solution.py:59
  118.4 13.1 %attend.2 = (bf16[128,1536]{1,0:T(8,128)(2,1)}, bf16[128,1536]{1,0:T(8,128)(2,1)}, bf16[128,1536]{1,0:T(8,128)(2,1)}, bf16[128,1536]{1,0:T(8,128)(2,1)}) custom-call(s32[4]{0:T(128)} %get-tuple-element.88.meta, bf16[2,128,1536]{2,1,0:T(8,128)(2,1)} %bitcast.66, bf16[1,128,1536]{2,1,0:T(8,128)(2,1)} %bitcast.79, bf16[3,128,1536]{2,1,0:T(8,128)(2,1)} %copy-done.15, ...), custom_call_target="tpu_custom_call" | custom-call | flops 6442450944 | bytes 10485760 | tf_op jit(solution)/shard_map/attend/pallas_call | solution.py:188
  131.5 2.4 %collective-permute-start.18 = (bf16[128,1536]{1,0:T(8,128)(2,1)}, bf16[128,1536]{1,0:T(8,128)(2,1)S(1)}, u32[]{:S(2)}, u32[]{:S(2)}) collective-permute-start(bf16[128,1536]{1,0:T(8,128)(2,1)} %get-tuple-element.110), channel_id=1, source_target_pairs={{28,0},{29,1},{30,2},{31,3},{0,4},{1,5},{2,6},{3,7},{4,8},{5,9},{6... | collective-permute-start | bytes 1179656 | tf_op jit(solution)/shard_map/ppermute | solution.py:59
  133.9 2.8 %collective-permute-start.19 = (bf16[128,1536]{1,0:T(8,128)(2,1)}, bf16[128,1536]{1,0:T(8,128)(2,1)S(1)}, u32[]{:S(2)}, u32[]{:S(2)}) collective-permute-start(bf16[128,1536]{1,0:T(8,128)(2,1)} %get-tuple-element.111), channel_id=1, source_target_pairs={{3,0},{0,1},{1,2},{2,3},{7,4},{4,5},{5,6},{6,7},{11,8},{8,9},{9,10... | collective-permute-start | bytes 1179656 | tf_op jit(solution)/shard_map/ppermute | solution.py:59
  136.8 13.0 %attend.3 = (bf16[128,1536]{1,0:T(8,128)(2,1)}, bf16[128,1536]{1,0:T(8,128)(2,1)}, bf16[128,1536]{1,0:T(8,128)(2,1)}, bf16[128,1536]{1,0:T(8,128)(2,1)}) custom-call(s32[4]{0:T(128)} %get-tuple-element.88.meta, bf16[2,128,1536]{2,1,0:T(8,128)(2,1)} %bitcast.64, bf16[1,128,1536]{2,1,0:T(8,128)(2,1)} %bitcast.78, bf16[3,128,1536]{2,1,0:T(8,128)(2,1)} %copy-done.13, ...), custom_call_target="tpu_custom_call" | custom-call | flops 6442450944 | bytes 10485760 | tf_op jit(solution)/shard_map/attend/pallas_call | solution.py:188
  149.9 3.0 %collective-permute-done.20.refs_3_ = bf16[128,1536]{1,0:T(8,128)(2,1)S(1)} collective-permute-done((bf16[128,1536]{1,0:T(8,128)(2,1)}, bf16[128,1536]{1,0:T(8,128)(2,1)S(1)}, u32[]{:S(2)}, u32[]{:S(2)}) %collective-permute-start.20) | collective-permute-done | bytes 393248 | tf_op jit(solution)/shard_map/ppermute | solution.py:59
  152.9 4.4 %collective-permute-start.24 = (bf16[384,1536]{1,0:T(8,128)(2,1)S(1)}, bf16[384,1536]{1,0:T(8,128)(2,1)S(1)}, u32[]{:S(2)}, u32[]{:S(2)}) collective-permute-start(bf16[384,1536]{1,0:T(8,128)(2,1)S(1)} %collective-permute-done.14.refs_6_), channel_id=1, source_target_pairs={{0,32},{1,33},{2,34},{3,35},{4,36},{5,37},{6,38},{7,39},{8,40},{9,... | collective-permute-start | bytes 3538952 | tf_op jit(solution)/shard_map/ppermute | solution.py:59
  157.5 8.0 %project.3.refs_9_ = bf16[4,16,16,3072]{3,2,1,0:T(8,128)(2,1)} custom-call(s32[4]{0:T(128)} %get-tuple-element.88.meta, s32[4]{0:T(128)} %get-tuple-element.89.places, bf16[128,1536]{1,0:T(8,128)(2,1)} %get-tuple-element.131.refs_0_, bf16[128,1536]{1,0:T(8,128)(2,1)} %copy-done.8, bf16[128,1536]{1,0:T(8,128)(2,1)} %copy-done.9, ...), custom_call_target="tpu_custom_call" | custom-call | flops 2415919104 | bytes 9437184 | tf_op jit(solution)/shard_map/project/pallas_call | solution.py:275
  167.6 8.0 %project.4.refs_13_ = bf16[4,16,16,3072]{3,2,1,0:T(8,128)(2,1)} custom-call(s32[4]{0:T(128)} %get-tuple-element.88.meta, s32[4]{0:T(128)} %get-tuple-element.89.places, bf16[128,1536]{1,0:T(8,128)(2,1)} %get-tuple-element.131.refs_0_, bf16[128,1536]{1,0:T(8,128)(2,1)} %copy-done.8, bf16[128,1536]{1,0:T(8,128)(2,1)} %copy-done.9, ...), custom_call_target="tpu_custom_call", output_to_operand_aliasing={{}: (11, {})} | custom-call | flops 2415919104 | bytes 9437184 | tf_op jit(solution)/shard_map/project/pallas_call | solution.py:275
  177.3 11.5 %project.5 = bf16[4,16,16,3072]{3,2,1,0:T(8,128)(2,1)} custom-call(s32[4]{0:T(128)} %get-tuple-element.88.meta, s32[4]{0:T(128)} %get-tuple-element.89.places, bf16[128,1536]{1,0:T(8,128)(2,1)} %get-tuple-element.123.refs_0_, bf16[128,1536]{1,0:T(8,128)(2,1)} %copy-done.18, bf16[128,1536]{1,0:T(8,128)(2,1)} %copy-done.19, ...), custom_call_target="tpu_custom_call", output_to_operand_aliasing={{}: (15, {})} | custom-call | flops 4831838208 | bytes 18874368 | tf_op jit(solution)/shard_map/project/pallas_call | solution.py:275
  (100 shorter events, 11.5 us)
Async XLA Ops:
  6.5 84.9 %all-gather.2.cloned.1.call-start = ((), (), s32[]{:S(2)}) async-start(), calls=%async_computation | async-start | bytes 1474560 | tf_op jit(solution)/shard_map/all_gather | solution.py:327
  6.5 14.8 %copy-start.24 = (s32[128]{0:T(128)S(1)}, s32[128]{0:T(128)}, u32[]{:S(2)}) copy-start(s32[128]{0:T(128)} %param.11) | copy-start | bytes 1540
  9.1 16.7 %collective-permute-start.2 = (bf16[24,1536]{1,0:T(8,128)(2,1)S(1)}, bf16[24,1536]{1,0:T(8,128)(2,1)S(1)}, u32[]{:S(2)}, u32[]{:S(2)}) collective-permute-start(bf16[24,1536]{1,0:T(8,128)(2,1)S(1)} %bitcast.68), channel_id=1, source_target_pairs={{0,80},{1,81},{2,82},{3,83},{4,84},{5,85},{6,86},{7,87},{8,88},{9,... | collective-permute-start | bytes 221192 | tf_op jit(solution)/shard_map/ppermute | solution.py:59
  13.7 12.1 %collective-permute-start.1 = (bf16[24,1536]{1,0:T(8,128)(2,1)S(1)}, bf16[24,1536]{1,0:T(8,128)(2,1)S(1)}, u32[]{:S(2)}, u32[]{:S(2)}) collective-permute-start(bf16[24,1536]{1,0:T(8,128)(2,1)S(1)} %bitcast.69), channel_id=1, source_target_pairs={{0,64},{1,65},{2,66},{3,67},{4,68},{5,69},{6,70},{7,71},{8,72},{9,... | collective-permute-start | bytes 221192 | tf_op jit(solution)/shard_map/ppermute | solution.py:59
  13.7 12.1 %collective-permute-start = (bf16[24,1536]{1,0:T(8,128)(2,1)S(1)}, bf16[24,1536]{1,0:T(8,128)(2,1)S(1)}, u32[]{:S(2)}, u32[]{:S(2)}) collective-permute-start(bf16[24,1536]{1,0:T(8,128)(2,1)S(1)} %bitcast.70), channel_id=1, source_target_pairs={{0,16},{1,17},{2,18},{3,19},{4,20},{5,21},{6,22},{7,23},{8,24},{9,... | collective-permute-start | bytes 221192 | tf_op jit(solution)/shard_map/ppermute | solution.py:59
  14.4 22.0 %collective-permute-start.3 = (bf16[3,128,1536]{2,1,0:T(8,128)(2,1)}, bf16[3,128,1536]{2,1,0:T(8,128)(2,1)S(1)}, u32[]{:S(2)}, u32[]{:S(2)}) collective-permute-start(bf16[3,128,1536]{2,1,0:T(8,128)(2,1)} %bitcast.73), channel_id=1, source_target_pairs={{0,4},{1,5},{2,6},{3,7},{4,8},{5,9},{6,10},{7,11},{8,12},{9,13},{1... | collective-permute-start | bytes 3538952 | tf_op jit(solution)/shard_map/ppermute | solution.py:59
  18.6 21.7 %collective-permute-start.4 = (bf16[3,128,1536]{2,1,0:T(8,128)(2,1)}, bf16[3,128,1536]{2,1,0:T(8,128)(2,1)S(1)}, u32[]{:S(2)}, u32[]{:S(2)}) collective-permute-start(bf16[3,128,1536]{2,1,0:T(8,128)(2,1)} %bitcast.72), channel_id=1, source_target_pairs={{0,1},{1,2},{2,3},{3,0},{4,5},{5,6},{6,7},{7,4},{8,9},{9,10},{10,1... | collective-permute-start | bytes 3538952 | tf_op jit(solution)/shard_map/ppermute | solution.py:59
  25.9 20.8 %collective-permute-start.5 = (bf16[3,128,1536]{2,1,0:T(8,128)(2,1)}, bf16[3,128,1536]{2,1,0:T(8,128)(2,1)S(1)}, u32[]{:S(2)}, u32[]{:S(2)}) collective-permute-start(bf16[3,128,1536]{2,1,0:T(8,128)(2,1)} %bitcast.76), channel_id=1, source_target_pairs={{0,28},{1,29},{2,30},{3,31},{4,0},{5,1},{6,2},{7,3},{8,4},{9,5},{1... | collective-permute-start | bytes 3538952 | tf_op jit(solution)/shard_map/ppermute | solution.py:59
  26.0 21.1 %collective-permute-start.6 = (bf16[3,128,1536]{2,1,0:T(8,128)(2,1)}, bf16[3,128,1536]{2,1,0:T(8,128)(2,1)S(1)}, u32[]{:S(2)}, u32[]{:S(2)}) collective-permute-start(bf16[3,128,1536]{2,1,0:T(8,128)(2,1)} %bitcast.74), channel_id=1, source_target_pairs={{0,3},{1,0},{2,1},{3,2},{4,7},{5,4},{6,5},{7,6},{8,11},{9,8},{10,9... | collective-permute-start | bytes 3538952 | tf_op jit(solution)/shard_map/ppermute | solution.py:59
  50.2 42.7 %collective-permute-start.7 = (bf16[3,128,1536]{2,1,0:T(8,128)(2,1)}, bf16[3,128,1536]{2,1,0:T(8,128)(2,1)S(1)}, u32[]{:S(2)}, u32[]{:S(2)}) collective-permute-start(bf16[3,128,1536]{2,1,0:T(8,128)(2,1)} %bitcast.77), channel_id=1, source_target_pairs={{0,5},{1,6},{2,7},{3,4},{4,9},{5,10},{6,11},{7,8},{8,13},{9,14},{1... | collective-permute-start | bytes 3538952 | tf_op jit(solution)/shard_map/ppermute | solution.py:59
  54.7 38.1 %collective-permute-start.8 = (bf16[3,128,1536]{2,1,0:T(8,128)(2,1)}, bf16[3,128,1536]{2,1,0:T(8,128)(2,1)}, u32[]{:S(2)}, u32[]{:S(2)}) collective-permute-start(bf16[3,128,1536]{2,1,0:T(8,128)(2,1)} %bitcast.75), channel_id=1, source_target_pairs={{0,31},{1,28},{2,29},{3,30},{4,3},{5,0},{6,1},{7,2},{8,7},{9,4},{1... | collective-permute-start | bytes 3538952 | tf_op jit(solution)/shard_map/ppermute | solution.py:59
  54.7 53.3 %collective-permute-start.12 = (bf16[3,2,128,1536]{3,2,1,0:T(8,128)(2,1)S(1)}, bf16[3,2,128,1536]{3,2,1,0:T(8,128)(2,1)}, u32[]{:S(2)}, u32[]{:S(2)}) collective-permute-start(bf16[3,2,128,1536]{3,2,1,0:T(8,128)(2,1)S(1)} %pad_maximum_fusion), channel_id=1, source_target_pairs={{32,0},{33,1},{34,2},{35,3},{36,4},{37,5},{38,6},{39,7},{40,8},{41... | collective-permute-start | bytes 7077896 | tf_op jit(solution)/shard_map/ppermute | solution.py:59
  57.9 50.1 %collective-permute-start.13 = (bf16[3,2,128,1536]{3,2,1,0:T(8,128)(2,1)}, bf16[3,2,128,1536]{3,2,1,0:T(8,128)(2,1)}, u32[]{:S(2)}, u32[]{:S(2)}) collective-permute-start(bf16[3,2,128,1536]{3,2,1,0:T(8,128)(2,1)} %pad_maximum_fusion.1), channel_id=1, source_target_pairs={{0,32},{1,33},{2,34},{3,35},{4,36},{5,37},{6,38},{7,39},{8,40},{9,... | collective-permute-start | bytes 7077896 | tf_op jit(solution)/shard_map/ppermute | solution.py:59
  92.8 25.1 %copy-start = (bf16[4,4,24,1536]{3,2,1,0:T(8,128)(2,1)}, bf16[4,4,24,1536]{3,2,1,0:T(8,128)(2,1)S(1)}, u32[]{:S(2)}) copy-start(bf16[4,4,24,1536]{3,2,1,0:T(8,128)(2,1)S(1)} %copy.9) | copy-start | bytes 3538948
  92.9 23.5 %collective-permute-start.9 = (bf16[384,1536]{1,0:T(8,128)(2,1)S(1)}, bf16[384,1536]{1,0:T(8,128)(2,1)S(1)}, u32[]{:S(2)}, u32[]{:S(2)}) collective-permute-start(bf16[384,1536]{1,0:T(8,128)(2,1)S(1)} %bitcast.57), channel_id=1, source_target_pairs={{0,4},{1,5},{2,6},{3,7},{4,8},{5,9},{6,10},{7,11},{8,12},{9,13},{1... | collective-permute-start | bytes 3538952 | tf_op jit(solution)/shard_map/ppermute | solution.py:59
  97.3 16.4 %collective-permute-start.11 = (bf16[2,128,1536]{2,1,0:T(8,128)(2,1)S(1)}, bf16[2,128,1536]{2,1,0:T(8,128)(2,1)S(1)}, u32[]{:S(2)}, u32[]{:S(2)}) collective-permute-start(bf16[2,128,1536]{2,1,0:T(8,128)(2,1)S(1)} %slice.23), channel_id=1, source_target_pairs={{0,32},{1,33},{2,34},{3,35},{4,36},{5,37},{6,38},{7,39},{8,40},{9,... | collective-permute-start | bytes 2359304 | tf_op jit(solution)/shard_map/ppermute | solution.py:59
  100.1 16.2 %collective-permute-start.10 = (bf16[2,128,1536]{2,1,0:T(8,128)(2,1)S(1)}, bf16[2,128,1536]{2,1,0:T(8,128)(2,1)S(1)}, u32[]{:S(2)}, u32[]{:S(2)}) collective-permute-start(bf16[2,128,1536]{2,1,0:T(8,128)(2,1)S(1)} %slice.22), channel_id=1, source_target_pairs={{32,0},{33,1},{34,2},{35,3},{36,4},{37,5},{38,6},{39,7},{40,8},{41... | collective-permute-start | bytes 2359304 | tf_op jit(solution)/shard_map/ppermute | solution.py:59
  116.3 15.1 %copy-start.1 = (bf16[384,1536]{1,0:T(8,128)(2,1)}, bf16[384,1536]{1,0:T(8,128)(2,1)S(1)}, u32[]{:S(2)}) copy-start(bf16[384,1536]{1,0:T(8,128)(2,1)S(1)} %collective-permute-done.9.refs_5_) | copy-start | bytes 3538948
  116.3 15.1 %collective-permute-start.17 = (bf16[384,1536]{1,0:T(8,128)(2,1)S(1)}, bf16[384,1536]{1,0:T(8,128)(2,1)S(1)}, u32[]{:S(2)}, u32[]{:S(2)}) collective-permute-start(bf16[384,1536]{1,0:T(8,128)(2,1)S(1)} %collective-permute-done.9.refs_5_), channel_id=1, source_target_pairs={{0,32},{1,33},{2,34},{3,35},{4,36},{5,37},{6,38},{7,39},{8,40},{9,... | collective-permute-start | bytes 3538952 | tf_op jit(solution)/shard_map/ppermute | solution.py:59
  116.4 15.1 %collective-permute-start.16 = (bf16[384,1536]{1,0:T(8,128)(2,1)S(1)}, bf16[384,1536]{1,0:T(8,128)(2,1)S(1)}, u32[]{:S(2)}, u32[]{:S(2)}) collective-permute-start(bf16[384,1536]{1,0:T(8,128)(2,1)S(1)} %bitcast.58), channel_id=1, source_target_pairs={{0,32},{1,33},{2,34},{3,35},{4,36},{5,37},{6,38},{7,39},{8,40},{9,... | collective-permute-start | bytes 3538952 | tf_op jit(solution)/shard_map/ppermute | solution.py:59
  116.9 32.9 %collective-permute-start.14 = (bf16[384,1536]{1,0:T(8,128)(2,1)S(1)}, bf16[384,1536]{1,0:T(8,128)(2,1)S(1)}, u32[]{:S(2)}, u32[]{:S(2)}) collective-permute-start(bf16[384,1536]{1,0:T(8,128)(2,1)S(1)} %collective-permute-done.9.refs_5_), channel_id=1, source_target_pairs={{0,4},{1,5},{2,6},{3,7},{4,8},{5,9},{6,10},{7,11},{8,12},{9,13},{1... | collective-permute-start | bytes 3538952 | tf_op jit(solution)/shard_map/ppermute | solution.py:59
  117.9 31.9 %collective-permute-start.15 = (bf16[384,1536]{1,0:T(8,128)(2,1)S(1)}, bf16[384,1536]{1,0:T(8,128)(2,1)S(1)}, u32[]{:S(2)}, u32[]{:S(2)}) collective-permute-start(bf16[384,1536]{1,0:T(8,128)(2,1)S(1)} %bitcast.59), channel_id=1, source_target_pairs={{0,12},{1,13},{2,14},{3,15},{4,0},{5,1},{6,2},{7,3},{8,4},{9,5},{1... | collective-permute-start | bytes 3538952 | tf_op jit(solution)/shard_map/ppermute | solution.py:59
  131.5 18.3 %copy-start.2 = (bf16[384,1536]{1,0:T(8,128)(2,1)}, bf16[384,1536]{1,0:T(8,128)(2,1)S(1)}, u32[]{:S(2)}) copy-start(bf16[384,1536]{1,0:T(8,128)(2,1)S(1)} %collective-permute-done.17.refs_5_.refs_9_) | copy-start | bytes 3538948
  131.5 18.3 %copy-start.3 = (bf16[384,1536]{1,0:T(8,128)(2,1)}, bf16[384,1536]{1,0:T(8,128)(2,1)S(1)}, u32[]{:S(2)}) copy-start(bf16[384,1536]{1,0:T(8,128)(2,1)S(1)} %collective-permute-done.16.refs_4_.refs_8_) | copy-start | bytes 3538948
  131.5 18.3 %collective-permute-start.18 = (bf16[128,1536]{1,0:T(8,128)(2,1)}, bf16[128,1536]{1,0:T(8,128)(2,1)S(1)}, u32[]{:S(2)}, u32[]{:S(2)}) collective-permute-start(bf16[128,1536]{1,0:T(8,128)(2,1)} %get-tuple-element.110), channel_id=1, source_target_pairs={{28,0},{29,1},{30,2},{31,3},{0,4},{1,5},{2,6},{3,7},{4,8},{5,9},{6... | collective-permute-start | bytes 1179656 | tf_op jit(solution)/shard_map/ppermute | solution.py:59
  133.9 16.0 %collective-permute-start.19 = (bf16[128,1536]{1,0:T(8,128)(2,1)}, bf16[128,1536]{1,0:T(8,128)(2,1)S(1)}, u32[]{:S(2)}, u32[]{:S(2)}) collective-permute-start(bf16[128,1536]{1,0:T(8,128)(2,1)} %get-tuple-element.111), channel_id=1, source_target_pairs={{3,0},{0,1},{1,2},{2,3},{7,4},{4,5},{5,6},{6,7},{11,8},{8,9},{9,10... | collective-permute-start | bytes 1179656 | tf_op jit(solution)/shard_map/ppermute | solution.py:59
  136.7 16.2 %collective-permute-start.20 = (bf16[128,1536]{1,0:T(8,128)(2,1)}, bf16[128,1536]{1,0:T(8,128)(2,1)S(1)}, u32[]{:S(2)}, u32[]{:S(2)}) collective-permute-start(bf16[128,1536]{1,0:T(8,128)(2,1)} %get-tuple-element.112), channel_id=1, source_target_pairs={{31,0},{28,1},{29,2},{30,3},{3,4},{0,5},{1,6},{2,7},{7,8},{4,9},{5... | collective-permute-start | bytes 1179656 | tf_op jit(solution)/shard_map/ppermute | solution.py:59
  152.9 12.6 %collective-permute-start.24 = (bf16[384,1536]{1,0:T(8,128)(2,1)S(1)}, bf16[384,1536]{1,0:T(8,128)(2,1)S(1)}, u32[]{:S(2)}, u32[]{:S(2)}) collective-permute-start(bf16[384,1536]{1,0:T(8,128)(2,1)S(1)} %collective-permute-done.14.refs_6_), channel_id=1, source_target_pairs={{0,32},{1,33},{2,34},{3,35},{4,36},{5,37},{6,38},{7,39},{8,40},{9,... | collective-permute-start | bytes 3538952 | tf_op jit(solution)/shard_map/ppermute | solution.py:59
  157.3 8.2 %collective-permute-start.25 = (bf16[384,1536]{1,0:T(8,128)(2,1)S(1)}, bf16[384,1536]{1,0:T(8,128)(2,1)S(1)}, u32[]{:S(2)}, u32[]{:S(2)}) collective-permute-start(bf16[384,1536]{1,0:T(8,128)(2,1)S(1)} %collective-permute-done.15.refs_7_), channel_id=1, source_target_pairs={{0,32},{1,33},{2,34},{3,35},{4,36},{5,37},{6,38},{7,39},{8,40},{9,... | collective-permute-start | bytes 3538952 | tf_op jit(solution)/shard_map/ppermute | solution.py:59
  157.3 18.3 %collective-permute-start.21 = (bf16[128,1536]{1,0:T(8,128)(2,1)}, bf16[128,1536]{1,0:T(8,128)(2,1)S(1)}, u32[]{:S(2)}, u32[]{:S(2)}) collective-permute-start(bf16[128,1536]{1,0:T(8,128)(2,1)} %get-tuple-element.124), channel_id=1, source_target_pairs={{4,0},{5,1},{6,2},{7,3},{8,4},{9,5},{10,6},{11,7},{12,8},{13,9},{1... | collective-permute-start | bytes 1179656 | tf_op jit(solution)/shard_map/ppermute | solution.py:59
  157.3 18.3 %collective-permute-start.22 = (bf16[128,1536]{1,0:T(8,128)(2,1)}, bf16[128,1536]{1,0:T(8,128)(2,1)S(1)}, u32[]{:S(2)}, u32[]{:S(2)}) collective-permute-start(bf16[128,1536]{1,0:T(8,128)(2,1)} %get-tuple-element.125), channel_id=1, source_target_pairs={{1,0},{2,1},{3,2},{0,3},{5,4},{6,5},{7,6},{4,7},{9,8},{10,9},{11,1... | collective-permute-start | bytes 1179656 | tf_op jit(solution)/shard_map/ppermute | solution.py:59
  157.3 18.3 %collective-permute-start.23 = (bf16[128,1536]{1,0:T(8,128)(2,1)}, bf16[128,1536]{1,0:T(8,128)(2,1)S(1)}, u32[]{:S(2)}, u32[]{:S(2)}) collective-permute-start(bf16[128,1536]{1,0:T(8,128)(2,1)} %get-tuple-element.126), channel_id=1, source_target_pairs={{5,0},{6,1},{7,2},{4,3},{9,4},{10,5},{11,6},{8,7},{13,8},{14,9},{1... | collective-permute-start | bytes 1179656 | tf_op jit(solution)/shard_map/ppermute | solution.py:59
  (20 other events, 67.6 us)
Sparse Core Ops, SparseCore 0:
  50.3 41.1 all-gather.1

commit v16 on v10

--- a/solution.py
+++ b/solution.py
@@ -14,7 +14,7 @@
 HD = 1536
 F, R, C = 4, 8, 4
 AXES = ("frame", "row", "col")
-STEP = 2
+STEP = 4
 BIG = 1e30
 TILE = 768
 VMEM = 56 * 1024 * 1024
@@ -219,15 +219,16 @@
                 to = pl.ds(pl.multiple_of(zlo * 384 + at * 96, 32), 96)
                 copies.append(
                     pltpu.make_async_copy(
-                        src.at[pl.ds((2 * zhi + zlo) * 96, 96)], held.at[n % 2, to], sems.at[n % 2, 2 * turn + zlo]
+                        src.at[pl.ds((2 * zhi + zlo) * 96, 96)], held.at[n, to], sems.at[n, 2 * turn + zlo]
                     )
                 )
         return copies
 
     @pl.when(step == 0)
     def _():
-        for copy in fetch(0):
-            copy.start()
+        for n in range(4):
+            for copy in fetch(n):
+                copy.start()
         s = sign_of(half, meta[0])
         for piece, (a, b) in enumerate(MOVES):
             i = s + a * (1 - 2 * s)
@@ -240,12 +241,9 @@
         def _():
             for copy in fetch(n):
                 copy.wait()
-            if n < 3:
-                for copy in fetch(n + 1):
-                    copy.start()
 
     total = lax.dot_general(
-        lhs[...].reshape(512, HD), held[lax.rem(step, 2)], (((1,), (1,)), ((), ())), preferred_element_type=jnp.float32
+        lhs[...].reshape(512, HD), held[step], (((1,), (1,)), ((), ())), preferred_element_type=jnp.float32
     ).reshape(2, 2, 2, 8, 8, TILE)
     for i in range(2):
         block = jnp.concatenate([total[i, 0], total[i, 1]], axis=2)
@@ -266,8 +264,8 @@
         out_specs=block,
         scratch_shapes=[
             pltpu.VMEM((4, 128, HD), jnp.bfloat16),
-            pltpu.VMEM((2, TILE, HD), jnp.bfloat16),
-            pltpu.SemaphoreType.DMA((2, 8)),
+            pltpu.VMEM((4, TILE, HD), jnp.bfloat16),
+            pltpu.SemaphoreType.DMA((4, 8)),
         ],
     )
     return pl.pallas_call(

time: 195 us -> 194 us (level)
  Pallas kernels: 59.6 us -> 57.6 us
where the time goes in v16:
time: 194 us; the launch traced here: 193 us
  waiting for transfers between devices  65.4 us (34%)
  Pallas kernels  57.6 us (30%)
  starting transfers between devices  43.8 us (23%)
  between operations  13.9 us (7%)
  local copies, waits for them, and re-layouts  8.66 us (4%)
  other arithmetic  3.88 us (2%)
    ppermute x26, starting transfers between devices, send(): return lax.ppermute(value, AXES, pairs)  43.8 us
    ppermute x26, waiting for transfers between devices, send(): return lax.ppermute(value, AXES, pairs)  35.7 us
    all_gather x1, waiting for transfers between devices, local(): strips = lax.all_gather(strip.reshape(96, HD), 'col', axis=0, tiled=True)  29.6 us
    pallas_call x2, Pallas kernels, attend(): pl.pallas_call(functools.partial(attend_kernel, half), grid=(H // STEP,),...  26.1 us
    pallas_call x2, Pallas kernels, project(): pl.pallas_call(functools.partial(project_kernel, half), grid_spec=grid_sp...  22.1 us
    pallas_call x3, Pallas kernels, pack(): pl.pallas_call(functools.partial(pack_kernel, parts), out_shape=[jax.Shap...  9.37 us
    unnamed x56, local copies, waits for them, and re-layouts  5.1 us
  transfers between devices with their start and end apart: 27, of which 11 were waited for; matrix products, arithmetic and copies ran while one was open for 3% of the time, Pallas kernels for 23%

profile of v16, /device:TPU:1, one launch (start us, length us, event | category | flops | bytes accessed | tf_op | source)
XLA Modules:
  0.0 193.1 jit_solution(17645300156537791630)
XLA Ops:
  6.5 2.5 %pack.3 = (bf16[3,2,8,8,1536]{4,3,2,1,0:T(8,128)(2,1)}, bf16[3,2,8,8,1536]{4,3,2,1,0:T(8,128)(2,1)}) custom-call(s32[1]{0:T(128)} %bitcast.meta, bf16[4,2,8,2,8,1536]{5,4,3,2,1,0:T(8,128)(2,1)} %bitcast.48, bf16[4,2,8,2,8,1536]{5,4,3,2,1,0:T(8,128)(2,1)} %bitcast.51, bf16[4,2,8,2,8,1536]{5,4,3,2,1,0:T(8,128)(2,1)} %bitcast.54), custom_call_target="tpu_custom_call" | custom-call | bytes 6291456 | tf_op jit(solution)/shard_map/pack/pallas_call | solution.py:98
  9.1 4.7 %collective-permute-start.2 = (bf16[24,1536]{1,0:T(8,128)(2,1)S(1)}, bf16[24,1536]{1,0:T(8,128)(2,1)S(1)}, u32[]{:S(2)}, u32[]{:S(2)}) collective-permute-start(bf16[24,1536]{1,0:T(8,128)(2,1)S(1)} %bitcast.68), channel_id=1, source_target_pairs={{0,80},{1,81},{2,82},{3,83},{4,84},{5,85},{6,86},{7,87},{8,88},{9,... | collective-permute-start | bytes 221192 | tf_op jit(solution)/shard_map/ppermute | solution.py:59
  14.4 4.1 %collective-permute-start.3 = (bf16[3,128,1536]{2,1,0:T(8,128)(2,1)}, bf16[3,128,1536]{2,1,0:T(8,128)(2,1)S(1)}, u32[]{:S(2)}, u32[]{:S(2)}) collective-permute-start(bf16[3,128,1536]{2,1,0:T(8,128)(2,1)} %bitcast.73), channel_id=1, source_target_pairs={{0,4},{1,5},{2,6},{3,7},{4,8},{5,9},{6,10},{7,11},{8,12},{9,13},{1... | collective-permute-start | bytes 3538952 | tf_op jit(solution)/shard_map/ppermute | solution.py:59
  18.6 2.7 %collective-permute-start.4 = (bf16[3,128,1536]{2,1,0:T(8,128)(2,1)}, bf16[3,128,1536]{2,1,0:T(8,128)(2,1)S(1)}, u32[]{:S(2)}, u32[]{:S(2)}) collective-permute-start(bf16[3,128,1536]{2,1,0:T(8,128)(2,1)} %bitcast.72), channel_id=1, source_target_pairs={{0,1},{1,2},{2,3},{3,0},{4,5},{5,6},{6,7},{7,4},{8,9},{9,10},{10,1... | collective-permute-start | bytes 3538952 | tf_op jit(solution)/shard_map/ppermute | solution.py:59
  22.0 2.5 %pack.4 = (bf16[3,2,8,8,1536]{4,3,2,1,0:T(8,128)(2,1)}, bf16[3,2,8,8,1536]{4,3,2,1,0:T(8,128)(2,1)}) custom-call(s32[1]{0:T(128)} %bitcast.meta, bf16[4,2,8,2,8,1536]{5,4,3,2,1,0:T(8,128)(2,1)} %bitcast.49, bf16[4,2,8,2,8,1536]{5,4,3,2,1,0:T(8,128)(2,1)} %bitcast.52, bf16[4,2,8,2,8,1536]{5,4,3,2,1,0:T(8,128)(2,1)} %bitcast.55), custom_call_target="tpu_custom_call" | custom-call | bytes 6291456 | tf_op jit(solution)/shard_map/pack/pallas_call | solution.py:98
  24.5 1.3 pad_add_fusion
  26.0 4.3 %pack.5 = (bf16[2,2,8,8,1536]{4,3,2,1,0:T(8,128)(2,1)}, bf16[2,2,8,8,1536]{4,3,2,1,0:T(8,128)(2,1)}, bf16[3,2,8,8,1536]{4,3,2,1,0:T(8,128)(2,1)}, bf16[3,2,8,8,1...) custom-call(s32[1]{0:T(128)} %bitcast.meta, ...), custom_call_target="tpu_custom_call" | custom-call | bytes 12582912 | tf_op jit(solution)/shard_map/pack/pallas_call | solution.py:98
  31.2 5.3 %collective-permute-done.3.x = bf16[3,128,1536]{2,1,0:T(8,128)(2,1)S(1)} collective-permute-done((bf16[3,128,1536]{2,1,0:T(8,128)(2,1)}, bf16[3,128,1536]{2,1,0:T(8,128)(2,1)S(1)}, u32[]{:S(2)}, u32[]{:S(2)}) %collective-permute-start.3) | collective-permute-done | bytes 1179680 | tf_op jit(solution)/shard_map/ppermute | solution.py:59
  36.5 3.7 %collective-permute-done.4.y = bf16[3,128,1536]{2,1,0:T(8,128)(2,1)S(1)} collective-permute-done((bf16[3,128,1536]{2,1,0:T(8,128)(2,1)}, bf16[3,128,1536]{2,1,0:T(8,128)(2,1)S(1)}, u32[]{:S(2)}, u32[]{:S(2)}) %collective-permute-start.4) | collective-permute-done | bytes 1179680 | tf_op jit(solution)/shard_map/ppermute | solution.py:59
  41.5 5.2 %collective-permute-done.5.x = bf16[3,128,1536]{2,1,0:T(8,128)(2,1)S(1)} collective-permute-done((bf16[3,128,1536]{2,1,0:T(8,128)(2,1)}, bf16[3,128,1536]{2,1,0:T(8,128)(2,1)S(1)}, u32[]{:S(2)}, u32[]{:S(2)}) %collective-permute-start.5) | collective-permute-done | bytes 1179680 | tf_op jit(solution)/shard_map/ppermute | solution.py:59
  48.5 1.7 pad_maximum_fusion.1
  50.2 4.6 %collective-permute-start.7 = (bf16[3,128,1536]{2,1,0:T(8,128)(2,1)}, bf16[3,128,1536]{2,1,0:T(8,128)(2,1)S(1)}, u32[]{:S(2)}, u32[]{:S(2)}) collective-permute-start(bf16[3,128,1536]{2,1,0:T(8,128)(2,1)} %bitcast.77), channel_id=1, source_target_pairs={{0,5},{1,6},{2,7},{3,4},{4,9},{5,10},{6,11},{7,8},{8,13},{9,14},{1... | collective-permute-start | bytes 3538952 | tf_op jit(solution)/shard_map/ppermute | solution.py:59
  54.7 3.1 %collective-permute-start.12 = (bf16[3,2,128,1536]{3,2,1,0:T(8,128)(2,1)S(1)}, bf16[3,2,128,1536]{3,2,1,0:T(8,128)(2,1)}, u32[]{:S(2)}, u32[]{:S(2)}) collective-permute-start(bf16[3,2,128,1536]{3,2,1,0:T(8,128)(2,1)S(1)} %pad_maximum_fusion), channel_id=1, source_target_pairs={{32,0},{33,1},{34,2},{35,3},{36,4},{37,5},{38,6},{39,7},{40,8},{41... | collective-permute-start | bytes 7077896 | tf_op jit(solution)/shard_map/ppermute | solution.py:59
  57.9 3.9 %collective-permute-start.13 = (bf16[3,2,128,1536]{3,2,1,0:T(8,128)(2,1)}, bf16[3,2,128,1536]{3,2,1,0:T(8,128)(2,1)}, u32[]{:S(2)}, u32[]{:S(2)}) collective-permute-start(bf16[3,2,128,1536]{3,2,1,0:T(8,128)(2,1)} %pad_maximum_fusion.1), channel_id=1, source_target_pairs={{0,32},{1,33},{2,34},{3,35},{4,36},{5,37},{6,38},{7,39},{8,40},{9,... | collective-permute-start | bytes 7077896 | tf_op jit(solution)/shard_map/ppermute | solution.py:59
  61.8 29.6 %all-gather.2.cloned.1.call-done = bf16[384,1536]{1,0:T(8,128)(2,1)} async-done(((bf16[96,1536]{1,0:T(8,128)(2,1)}), bf16[384,1536]{1,0:T(8,128)(2,1)}) %all-gather.2.cloned.1.call-update) | async-done | bytes 1179664 | tf_op jit(solution)/shard_map/all_gather | solution.py:323
  91.4 1.4 copy.8
  92.9 3.2 %collective-permute-start.9 = (bf16[384,1536]{1,0:T(8,128)(2,1)S(1)}, bf16[384,1536]{1,0:T(8,128)(2,1)S(1)}, u32[]{:S(2)}, u32[]{:S(2)}) collective-permute-start(bf16[384,1536]{1,0:T(8,128)(2,1)S(1)} %bitcast.57), channel_id=1, source_target_pairs={{0,4},{1,5},{2,6},{3,7},{4,8},{5,9},{6,10},{7,11},{8,12},{9,13},{1... | collective-permute-start | bytes 3538952 | tf_op jit(solution)/shard_map/ppermute | solution.py:59
  97.3 2.8 %collective-permute-start.11 = (bf16[2,128,1536]{2,1,0:T(8,128)(2,1)S(1)}, bf16[2,128,1536]{2,1,0:T(8,128)(2,1)S(1)}, u32[]{:S(2)}, u32[]{:S(2)}) collective-permute-start(bf16[2,128,1536]{2,1,0:T(8,128)(2,1)S(1)} %slice.23), channel_id=1, source_target_pairs={{0,32},{1,33},{2,34},{3,35},{4,36},{5,37},{6,38},{7,39},{8,40},{9,... | collective-permute-start | bytes 2359304 | tf_op jit(solution)/shard_map/ppermute | solution.py:59
  100.1 1.9 collective-permute-start.10
  102.1 5.9 %collective-permute-done.12.h3 = bf16[3,2,128,1536]{3,2,1,0:T(8,128)(2,1)} collective-permute-done((bf16[3,2,128,1536]{3,2,1,0:T(8,128)(2,1)S(1)}, bf16[3,2,128,1536]{3,2,1,0:T(8,128)(2,1)}, u32[]{:S(2)}, u32[]{:S(2)}) %collective-permute-start.12) | collective-permute-done | bytes 2359328 | tf_op jit(solution)/shard_map/ppermute | solution.py:59
  108.0 5.7 %collective-permute-done.11.hd = bf16[2,128,1536]{2,1,0:T(8,128)(2,1)S(1)} collective-permute-done((bf16[2,128,1536]{2,1,0:T(8,128)(2,1)S(1)}, bf16[2,128,1536]{2,1,0:T(8,128)(2,1)S(1)}, u32[]{:S(2)}, u32[]{:S(2)}) %collective-permute-start.11) | collective-permute-done | bytes 786464 | tf_op jit(solution)/shard_map/ppermute | solution.py:59
  113.7 2.6 %collective-permute-done.10.hd = bf16[2,128,1536]{2,1,0:T(8,128)(2,1)S(1)} collective-permute-done((bf16[2,128,1536]{2,1,0:T(8,128)(2,1)S(1)}, bf16[2,128,1536]{2,1,0:T(8,128)(2,1)S(1)}, u32[]{:S(2)}, u32[]{:S(2)}) %collective-permute-start.10) | collective-permute-done | bytes 786464 | tf_op jit(solution)/shard_map/ppermute | solution.py:59
  118.4 13.1 %attend.2 = (bf16[128,1536]{1,0:T(8,128)(2,1)}, bf16[128,1536]{1,0:T(8,128)(2,1)}, bf16[128,1536]{1,0:T(8,128)(2,1)}, bf16[128,1536]{1,0:T(8,128)(2,1)}) custom-call(s32[4]{0:T(128)} %get-tuple-element.88.meta, bf16[2,128,1536]{2,1,0:T(8,128)(2,1)} %bitcast.66, bf16[1,128,1536]{2,1,0:T(8,128)(2,1)} %bitcast.79, bf16[3,128,1536]{2,1,0:T(8,128)(2,1)} %copy-done.12, ...), custom_call_target="tpu_custom_call" | custom-call | flops 6442450944 | bytes 10485760 | tf_op jit(solution)/shard_map/attend/pallas_call | solution.py:188
  131.5 2.4 %collective-permute-start.18 = (bf16[128,1536]{1,0:T(8,128)(2,1)}, bf16[128,1536]{1,0:T(8,128)(2,1)S(1)}, u32[]{:S(2)}, u32[]{:S(2)}) collective-permute-start(bf16[128,1536]{1,0:T(8,128)(2,1)} %get-tuple-element.110), channel_id=1, source_target_pairs={{28,0},{29,1},{30,2},{31,3},{0,4},{1,5},{2,6},{3,7},{4,8},{5,9},{6... | collective-permute-start | bytes 1179656 | tf_op jit(solution)/shard_map/ppermute | solution.py:59
  133.9 2.8 %collective-permute-start.19 = (bf16[128,1536]{1,0:T(8,128)(2,1)}, bf16[128,1536]{1,0:T(8,128)(2,1)S(1)}, u32[]{:S(2)}, u32[]{:S(2)}) collective-permute-start(bf16[128,1536]{1,0:T(8,128)(2,1)} %get-tuple-element.111), channel_id=1, source_target_pairs={{3,0},{0,1},{1,2},{2,3},{7,4},{4,5},{5,6},{6,7},{11,8},{8,9},{9,10... | collective-permute-start | bytes 1179656 | tf_op jit(solution)/shard_map/ppermute | solution.py:59
  136.8 13.0 %attend.3 = (bf16[128,1536]{1,0:T(8,128)(2,1)}, bf16[128,1536]{1,0:T(8,128)(2,1)}, bf16[128,1536]{1,0:T(8,128)(2,1)}, bf16[128,1536]{1,0:T(8,128)(2,1)}) custom-call(s32[4]{0:T(128)} %get-tuple-element.88.meta, bf16[2,128,1536]{2,1,0:T(8,128)(2,1)} %bitcast.64, bf16[1,128,1536]{2,1,0:T(8,128)(2,1)} %bitcast.78, bf16[3,128,1536]{2,1,0:T(8,128)(2,1)} %copy-done.10, ...), custom_call_target="tpu_custom_call" | custom-call | flops 6442450944 | bytes 10485760 | tf_op jit(solution)/shard_map/attend/pallas_call | solution.py:188
  149.9 3.0 %collective-permute-done.20.refs_3_ = bf16[128,1536]{1,0:T(8,128)(2,1)S(1)} collective-permute-done((bf16[128,1536]{1,0:T(8,128)(2,1)}, bf16[128,1536]{1,0:T(8,128)(2,1)S(1)}, u32[]{:S(2)}, u32[]{:S(2)}) %collective-permute-start.20) | collective-permute-done | bytes 393248 | tf_op jit(solution)/shard_map/ppermute | solution.py:59
  152.9 4.4 %collective-permute-start.24 = (bf16[384,1536]{1,0:T(8,128)(2,1)S(1)}, bf16[384,1536]{1,0:T(8,128)(2,1)S(1)}, u32[]{:S(2)}, u32[]{:S(2)}) collective-permute-start(bf16[384,1536]{1,0:T(8,128)(2,1)S(1)} %collective-permute-done.14.refs_6_), channel_id=1, source_target_pairs={{0,32},{1,33},{2,34},{3,35},{4,36},{5,37},{6,38},{7,39},{8,40},{9,... | collective-permute-start | bytes 3538952 | tf_op jit(solution)/shard_map/ppermute | solution.py:59
  157.5 2.3 %collective-permute-done.24.refs_10_ = bf16[384,1536]{1,0:T(8,128)(2,1)S(1)} collective-permute-done((bf16[384,1536]{1,0:T(8,128)(2,1)S(1)}, bf16[384,1536]{1,0:T(8,128)(2,1)S(1)}, u32[]{:S(2)}, u32[]{:S(2)}) %collective-permute-start.24) | collective-permute-done | bytes 1179680 | tf_op jit(solution)/shard_map/ppermute | solution.py:59
  159.8 1.7 collective-permute-done.25.refs_11_
  162.5 11.0 %project.2.refs_13_ = bf16[4,16,16,3072]{3,2,1,0:T(8,128)(2,1)} custom-call(s32[4]{0:T(128)} %get-tuple-element.88.meta, s32[4]{0:T(128)} %get-tuple-element.89.places, bf16[128,1536]{1,0:T(8,128)(2,1)} %get-tuple-element.131.refs_0_, bf16[128,1536]{1,0:T(8,128)(2,1)} %copy-done.18, bf16[128,1536]{1,0:T(8,128)(2,1)} %copy-done.19, ...), custom_call_target="tpu_custom_call" | custom-call | flops 4831838208 | bytes 17825792 | tf_op jit(solution)/shard_map/project/pallas_call | solution.py:271
  175.2 11.0 %project.3 = bf16[4,16,16,3072]{3,2,1,0:T(8,128)(2,1)} custom-call(s32[4]{0:T(128)} %get-tuple-element.88.meta, s32[4]{0:T(128)} %get-tuple-element.89.places, bf16[128,1536]{1,0:T(8,128)(2,1)} %get-tuple-element.123.refs_0_, bf16[128,1536]{1,0:T(8,128)(2,1)} %copy-done.15, bf16[128,1536]{1,0:T(8,128)(2,1)} %copy-done.16, ...), custom_call_target="tpu_custom_call", output_to_operand_aliasing={{}: (15, {})} | custom-call | flops 4831838208 | bytes 17825792 | tf_op jit(solution)/shard_map/project/pallas_call | solution.py:271
  (99 shorter events, 11.6 us)
Async XLA Ops:
  6.5 84.9 %all-gather.2.cloned.1.call-start = ((), (), s32[]{:S(2)}) async-start(), calls=%async_computation | async-start | bytes 1474560 | tf_op jit(solution)/shard_map/all_gather | solution.py:323
  6.5 14.8 %copy-start.24 = (s32[128]{0:T(128)S(1)}, s32[128]{0:T(128)}, u32[]{:S(2)}) copy-start(s32[128]{0:T(128)} %param.11) | copy-start | bytes 1540
  9.1 16.7 %collective-permute-start.2 = (bf16[24,1536]{1,0:T(8,128)(2,1)S(1)}, bf16[24,1536]{1,0:T(8,128)(2,1)S(1)}, u32[]{:S(2)}, u32[]{:S(2)}) collective-permute-start(bf16[24,1536]{1,0:T(8,128)(2,1)S(1)} %bitcast.68), channel_id=1, source_target_pairs={{0,80},{1,81},{2,82},{3,83},{4,84},{5,85},{6,86},{7,87},{8,88},{9,... | collective-permute-start | bytes 221192 | tf_op jit(solution)/shard_map/ppermute | solution.py:59
  13.7 12.1 %collective-permute-start.1 = (bf16[24,1536]{1,0:T(8,128)(2,1)S(1)}, bf16[24,1536]{1,0:T(8,128)(2,1)S(1)}, u32[]{:S(2)}, u32[]{:S(2)}) collective-permute-start(bf16[24,1536]{1,0:T(8,128)(2,1)S(1)} %bitcast.69), channel_id=1, source_target_pairs={{0,64},{1,65},{2,66},{3,67},{4,68},{5,69},{6,70},{7,71},{8,72},{9,... | collective-permute-start | bytes 221192 | tf_op jit(solution)/shard_map/ppermute | solution.py:59
  13.7 12.1 %collective-permute-start = (bf16[24,1536]{1,0:T(8,128)(2,1)S(1)}, bf16[24,1536]{1,0:T(8,128)(2,1)S(1)}, u32[]{:S(2)}, u32[]{:S(2)}) collective-permute-start(bf16[24,1536]{1,0:T(8,128)(2,1)S(1)} %bitcast.70), channel_id=1, source_target_pairs={{0,16},{1,17},{2,18},{3,19},{4,20},{5,21},{6,22},{7,23},{8,24},{9,... | collective-permute-start | bytes 221192 | tf_op jit(solution)/shard_map/ppermute | solution.py:59
  14.4 22.0 %collective-permute-start.3 = (bf16[3,128,1536]{2,1,0:T(8,128)(2,1)}, bf16[3,128,1536]{2,1,0:T(8,128)(2,1)S(1)}, u32[]{:S(2)}, u32[]{:S(2)}) collective-permute-start(bf16[3,128,1536]{2,1,0:T(8,128)(2,1)} %bitcast.73), channel_id=1, source_target_pairs={{0,4},{1,5},{2,6},{3,7},{4,8},{5,9},{6,10},{7,11},{8,12},{9,13},{1... | collective-permute-start | bytes 3538952 | tf_op jit(solution)/shard_map/ppermute | solution.py:59
  18.6 21.7 %collective-permute-start.4 = (bf16[3,128,1536]{2,1,0:T(8,128)(2,1)}, bf16[3,128,1536]{2,1,0:T(8,128)(2,1)S(1)}, u32[]{:S(2)}, u32[]{:S(2)}) collective-permute-start(bf16[3,128,1536]{2,1,0:T(8,128)(2,1)} %bitcast.72), channel_id=1, source_target_pairs={{0,1},{1,2},{2,3},{3,0},{4,5},{5,6},{6,7},{7,4},{8,9},{9,10},{10,1... | collective-permute-start | bytes 3538952 | tf_op jit(solution)/shard_map/ppermute | solution.py:59
  25.9 20.8 %collective-permute-start.5 = (bf16[3,128,1536]{2,1,0:T(8,128)(2,1)}, bf16[3,128,1536]{2,1,0:T(8,128)(2,1)S(1)}, u32[]{:S(2)}, u32[]{:S(2)}) collective-permute-start(bf16[3,128,1536]{2,1,0:T(8,128)(2,1)} %bitcast.76), channel_id=1, source_target_pairs={{0,28},{1,29},{2,30},{3,31},{4,0},{5,1},{6,2},{7,3},{8,4},{9,5},{1... | collective-permute-start | bytes 3538952 | tf_op jit(solution)/shard_map/ppermute | solution.py:59
  26.0 21.1 %collective-permute-start.6 = (bf16[3,128,1536]{2,1,0:T(8,128)(2,1)}, bf16[3,128,1536]{2,1,0:T(8,128)(2,1)S(1)}, u32[]{:S(2)}, u32[]{:S(2)}) collective-permute-start(bf16[3,128,1536]{2,1,0:T(8,128)(2,1)} %bitcast.74), channel_id=1, source_target_pairs={{0,3},{1,0},{2,1},{3,2},{4,7},{5,4},{6,5},{7,6},{8,11},{9,8},{10,9... | collective-permute-start | bytes 3538952 | tf_op jit(solution)/shard_map/ppermute | solution.py:59
  50.2 42.7 %collective-permute-start.7 = (bf16[3,128,1536]{2,1,0:T(8,128)(2,1)}, bf16[3,128,1536]{2,1,0:T(8,128)(2,1)S(1)}, u32[]{:S(2)}, u32[]{:S(2)}) collective-permute-start(bf16[3,128,1536]{2,1,0:T(8,128)(2,1)} %bitcast.77), channel_id=1, source_target_pairs={{0,5},{1,6},{2,7},{3,4},{4,9},{5,10},{6,11},{7,8},{8,13},{9,14},{1... | collective-permute-start | bytes 3538952 | tf_op jit(solution)/shard_map/ppermute | solution.py:59
  54.7 38.1 %collective-permute-start.8 = (bf16[3,128,1536]{2,1,0:T(8,128)(2,1)}, bf16[3,128,1536]{2,1,0:T(8,128)(2,1)}, u32[]{:S(2)}, u32[]{:S(2)}) collective-permute-start(bf16[3,128,1536]{2,1,0:T(8,128)(2,1)} %bitcast.75), channel_id=1, source_target_pairs={{0,31},{1,28},{2,29},{3,30},{4,3},{5,0},{6,1},{7,2},{8,7},{9,4},{1... | collective-permute-start | bytes 3538952 | tf_op jit(solution)/shard_map/ppermute | solution.py:59
  54.7 53.3 %collective-permute-start.12 = (bf16[3,2,128,1536]{3,2,1,0:T(8,128)(2,1)S(1)}, bf16[3,2,128,1536]{3,2,1,0:T(8,128)(2,1)}, u32[]{:S(2)}, u32[]{:S(2)}) collective-permute-start(bf16[3,2,128,1536]{3,2,1,0:T(8,128)(2,1)S(1)} %pad_maximum_fusion), channel_id=1, source_target_pairs={{32,0},{33,1},{34,2},{35,3},{36,4},{37,5},{38,6},{39,7},{40,8},{41... | collective-permute-start | bytes 7077896 | tf_op jit(solution)/shard_map/ppermute | solution.py:59
  57.9 50.1 %collective-permute-start.13 = (bf16[3,2,128,1536]{3,2,1,0:T(8,128)(2,1)}, bf16[3,2,128,1536]{3,2,1,0:T(8,128)(2,1)}, u32[]{:S(2)}, u32[]{:S(2)}) collective-permute-start(bf16[3,2,128,1536]{3,2,1,0:T(8,128)(2,1)} %pad_maximum_fusion.1), channel_id=1, source_target_pairs={{0,32},{1,33},{2,34},{3,35},{4,36},{5,37},{6,38},{7,39},{8,40},{9,... | collective-permute-start | bytes 7077896 | tf_op jit(solution)/shard_map/ppermute | solution.py:59
  92.8 25.1 %copy-start = (bf16[4,4,24,1536]{3,2,1,0:T(8,128)(2,1)}, bf16[4,4,24,1536]{3,2,1,0:T(8,128)(2,1)S(1)}, u32[]{:S(2)}) copy-start(bf16[4,4,24,1536]{3,2,1,0:T(8,128)(2,1)S(1)} %copy.8) | copy-start | bytes 3538948
  92.9 23.5 %collective-permute-start.9 = (bf16[384,1536]{1,0:T(8,128)(2,1)S(1)}, bf16[384,1536]{1,0:T(8,128)(2,1)S(1)}, u32[]{:S(2)}, u32[]{:S(2)}) collective-permute-start(bf16[384,1536]{1,0:T(8,128)(2,1)S(1)} %bitcast.57), channel_id=1, source_target_pairs={{0,4},{1,5},{2,6},{3,7},{4,8},{5,9},{6,10},{7,11},{8,12},{9,13},{1... | collective-permute-start | bytes 3538952 | tf_op jit(solution)/shard_map/ppermute | solution.py:59
  97.3 16.4 %collective-permute-start.11 = (bf16[2,128,1536]{2,1,0:T(8,128)(2,1)S(1)}, bf16[2,128,1536]{2,1,0:T(8,128)(2,1)S(1)}, u32[]{:S(2)}, u32[]{:S(2)}) collective-permute-start(bf16[2,128,1536]{2,1,0:T(8,128)(2,1)S(1)} %slice.23), channel_id=1, source_target_pairs={{0,32},{1,33},{2,34},{3,35},{4,36},{5,37},{6,38},{7,39},{8,40},{9,... | collective-permute-start | bytes 2359304 | tf_op jit(solution)/shard_map/ppermute | solution.py:59
  100.1 16.2 %collective-permute-start.10 = (bf16[2,128,1536]{2,1,0:T(8,128)(2,1)S(1)}, bf16[2,128,1536]{2,1,0:T(8,128)(2,1)S(1)}, u32[]{:S(2)}, u32[]{:S(2)}) collective-permute-start(bf16[2,128,1536]{2,1,0:T(8,128)(2,1)S(1)} %slice.22), channel_id=1, source_target_pairs={{32,0},{33,1},{34,2},{35,3},{36,4},{37,5},{38,6},{39,7},{40,8},{41... | collective-permute-start | bytes 2359304 | tf_op jit(solution)/shard_map/ppermute | solution.py:59
  116.3 15.1 %copy-start.1 = (bf16[384,1536]{1,0:T(8,128)(2,1)}, bf16[384,1536]{1,0:T(8,128)(2,1)S(1)}, u32[]{:S(2)}) copy-start(bf16[384,1536]{1,0:T(8,128)(2,1)S(1)} %collective-permute-done.9.refs_5_) | copy-start | bytes 3538948
  116.3 15.1 %collective-permute-start.17 = (bf16[384,1536]{1,0:T(8,128)(2,1)S(1)}, bf16[384,1536]{1,0:T(8,128)(2,1)S(1)}, u32[]{:S(2)}, u32[]{:S(2)}) collective-permute-start(bf16[384,1536]{1,0:T(8,128)(2,1)S(1)} %collective-permute-done.9.refs_5_), channel_id=1, source_target_pairs={{0,32},{1,33},{2,34},{3,35},{4,36},{5,37},{6,38},{7,39},{8,40},{9,... | collective-permute-start | bytes 3538952 | tf_op jit(solution)/shard_map/ppermute | solution.py:59
  116.4 15.1 %collective-permute-start.16 = (bf16[384,1536]{1,0:T(8,128)(2,1)S(1)}, bf16[384,1536]{1,0:T(8,128)(2,1)S(1)}, u32[]{:S(2)}, u32[]{:S(2)}) collective-permute-start(bf16[384,1536]{1,0:T(8,128)(2,1)S(1)} %bitcast.58), channel_id=1, source_target_pairs={{0,32},{1,33},{2,34},{3,35},{4,36},{5,37},{6,38},{7,39},{8,40},{9,... | collective-permute-start | bytes 3538952 | tf_op jit(solution)/shard_map/ppermute | solution.py:59
  116.9 32.9 %collective-permute-start.14 = (bf16[384,1536]{1,0:T(8,128)(2,1)S(1)}, bf16[384,1536]{1,0:T(8,128)(2,1)S(1)}, u32[]{:S(2)}, u32[]{:S(2)}) collective-permute-start(bf16[384,1536]{1,0:T(8,128)(2,1)S(1)} %collective-permute-done.9.refs_5_), channel_id=1, source_target_pairs={{0,4},{1,5},{2,6},{3,7},{4,8},{5,9},{6,10},{7,11},{8,12},{9,13},{1... | collective-permute-start | bytes 3538952 | tf_op jit(solution)/shard_map/ppermute | solution.py:59
  117.9 31.9 %collective-permute-start.15 = (bf16[384,1536]{1,0:T(8,128)(2,1)S(1)}, bf16[384,1536]{1,0:T(8,128)(2,1)S(1)}, u32[]{:S(2)}, u32[]{:S(2)}) collective-permute-start(bf16[384,1536]{1,0:T(8,128)(2,1)S(1)} %bitcast.59), channel_id=1, source_target_pairs={{0,12},{1,13},{2,14},{3,15},{4,0},{5,1},{6,2},{7,3},{8,4},{9,5},{1... | collective-permute-start | bytes 3538952 | tf_op jit(solution)/shard_map/ppermute | solution.py:59
  131.5 18.3 %copy-start.2 = (bf16[384,1536]{1,0:T(8,128)(2,1)}, bf16[384,1536]{1,0:T(8,128)(2,1)S(1)}, u32[]{:S(2)}) copy-start(bf16[384,1536]{1,0:T(8,128)(2,1)S(1)} %collective-permute-done.17.refs_9_) | copy-start | bytes 3538948
  131.5 18.3 %copy-start.3 = (bf16[384,1536]{1,0:T(8,128)(2,1)}, bf16[384,1536]{1,0:T(8,128)(2,1)S(1)}, u32[]{:S(2)}) copy-start(bf16[384,1536]{1,0:T(8,128)(2,1)S(1)} %collective-permute-done.16.refs_8_) | copy-start | bytes 3538948
  131.5 18.3 %collective-permute-start.18 = (bf16[128,1536]{1,0:T(8,128)(2,1)}, bf16[128,1536]{1,0:T(8,128)(2,1)S(1)}, u32[]{:S(2)}, u32[]{:S(2)}) collective-permute-start(bf16[128,1536]{1,0:T(8,128)(2,1)} %get-tuple-element.110), channel_id=1, source_target_pairs={{28,0},{29,1},{30,2},{31,3},{0,4},{1,5},{2,6},{3,7},{4,8},{5,9},{6... | collective-permute-start | bytes 1179656 | tf_op jit(solution)/shard_map/ppermute | solution.py:59
  133.9 16.0 %collective-permute-start.19 = (bf16[128,1536]{1,0:T(8,128)(2,1)}, bf16[128,1536]{1,0:T(8,128)(2,1)S(1)}, u32[]{:S(2)}, u32[]{:S(2)}) collective-permute-start(bf16[128,1536]{1,0:T(8,128)(2,1)} %get-tuple-element.111), channel_id=1, source_target_pairs={{3,0},{0,1},{1,2},{2,3},{7,4},{4,5},{5,6},{6,7},{11,8},{8,9},{9,10... | collective-permute-start | bytes 1179656 | tf_op jit(solution)/shard_map/ppermute | solution.py:59
  136.7 16.2 %collective-permute-start.20 = (bf16[128,1536]{1,0:T(8,128)(2,1)}, bf16[128,1536]{1,0:T(8,128)(2,1)S(1)}, u32[]{:S(2)}, u32[]{:S(2)}) collective-permute-start(bf16[128,1536]{1,0:T(8,128)(2,1)} %get-tuple-element.112), channel_id=1, source_target_pairs={{31,0},{28,1},{29,2},{30,3},{3,4},{0,5},{1,6},{2,7},{7,8},{4,9},{5... | collective-permute-start | bytes 1179656 | tf_op jit(solution)/shard_map/ppermute | solution.py:59
  152.9 6.9 %collective-permute-start.24 = (bf16[384,1536]{1,0:T(8,128)(2,1)S(1)}, bf16[384,1536]{1,0:T(8,128)(2,1)S(1)}, u32[]{:S(2)}, u32[]{:S(2)}) collective-permute-start(bf16[384,1536]{1,0:T(8,128)(2,1)S(1)} %collective-permute-done.14.refs_6_), channel_id=1, source_target_pairs={{0,32},{1,33},{2,34},{3,35},{4,36},{5,37},{6,38},{7,39},{8,40},{9,... | collective-permute-start | bytes 3538952 | tf_op jit(solution)/shard_map/ppermute | solution.py:59
  157.3 4.2 %collective-permute-start.25 = (bf16[384,1536]{1,0:T(8,128)(2,1)S(1)}, bf16[384,1536]{1,0:T(8,128)(2,1)S(1)}, u32[]{:S(2)}, u32[]{:S(2)}) collective-permute-start(bf16[384,1536]{1,0:T(8,128)(2,1)S(1)} %collective-permute-done.15.refs_7_), channel_id=1, source_target_pairs={{0,32},{1,33},{2,34},{3,35},{4,36},{5,37},{6,38},{7,39},{8,40},{9,... | collective-permute-start | bytes 3538952 | tf_op jit(solution)/shard_map/ppermute | solution.py:59
  157.3 16.2 %collective-permute-start.21 = (bf16[128,1536]{1,0:T(8,128)(2,1)}, bf16[128,1536]{1,0:T(8,128)(2,1)S(1)}, u32[]{:S(2)}, u32[]{:S(2)}) collective-permute-start(bf16[128,1536]{1,0:T(8,128)(2,1)} %get-tuple-element.124), channel_id=1, source_target_pairs={{4,0},{5,1},{6,2},{7,3},{8,4},{9,5},{10,6},{11,7},{12,8},{13,9},{1... | collective-permute-start | bytes 1179656 | tf_op jit(solution)/shard_map/ppermute | solution.py:59
  157.3 16.2 %collective-permute-start.22 = (bf16[128,1536]{1,0:T(8,128)(2,1)}, bf16[128,1536]{1,0:T(8,128)(2,1)S(1)}, u32[]{:S(2)}, u32[]{:S(2)}) collective-permute-start(bf16[128,1536]{1,0:T(8,128)(2,1)} %get-tuple-element.125), channel_id=1, source_target_pairs={{1,0},{2,1},{3,2},{0,3},{5,4},{6,5},{7,6},{4,7},{9,8},{10,9},{11,1... | collective-permute-start | bytes 1179656 | tf_op jit(solution)/shard_map/ppermute | solution.py:59
  157.3 16.3 %collective-permute-start.23 = (bf16[128,1536]{1,0:T(8,128)(2,1)}, bf16[128,1536]{1,0:T(8,128)(2,1)S(1)}, u32[]{:S(2)}, u32[]{:S(2)}) collective-permute-start(bf16[128,1536]{1,0:T(8,128)(2,1)} %get-tuple-element.126), channel_id=1, source_target_pairs={{5,0},{6,1},{7,2},{4,3},{9,4},{10,5},{11,6},{8,7},{13,8},{14,9},{1... | collective-permute-start | bytes 1179656 | tf_op jit(solution)/shard_map/ppermute | solution.py:59
  (20 other events, 88.0 us)
Sparse Core Ops, SparseCore 0:
  50.3 41.1 all-gather.1

commit v17 on v9

--- a/solution.py
+++ b/solution.py
@@ -14,7 +14,7 @@
 HD = 1536
 F, R, C = 4, 8, 4
 AXES = ("frame", "row", "col")
-STEP = 2
+STEP = 4
 BIG = 1e30
 TILE = 768
 VMEM = 56 * 1024 * 1024
@@ -316,24 +316,25 @@
         ((0, 0, "kv"), (1, 0, "kv"), (0, 3, "kvq"), (1, 3, "kvq"), (0, 0, "q"), (1, 0, "q")), frame, *arrays
     )
     strip = ring_order(shard, *shards, (f >> 1) * 2 + (r >> 2))
-    strips = [send(strip, shift_pairs(dy=n)) for n in (1, 2, 3)]
     h0, h1 = jnp.stack([skv0, x0[:2], y0[:2]]), jnp.stack([skv1, x1[:2], y1[:2]])
-    d0, d1, h0, h1, x0, y0, x1, y1, meta, places, *strips = together(d0, d1, h0, h1, x0, y0, x1, y1, meta, places, *strips)
+    d0, d1, h0, h1, x0, y0, x1, y1, meta, places, strip = together(d0, d1, h0, h1, x0, y0, x1, y1, meta, places, strip)
     d0, d1, down3, up3 = go(d0, 0, both), go(d1, 1, both), down(h0), up(h1)
-    c0 = ring_order(strip, *strips, c).swapaxes(0, 1).reshape(384, HD)
-    c0, d0, d1 = together(c0, d0, d1)
-    downd, upd, c1 = down(d0[:2]), up(d1[:2]), turn(c0)
-    c0, c1, downd, upd, down3, up3 = together(c0, c1, downd, upd, down3, up3)
-
-    c2, c3, s0, s1 = turn(c1), turn(c0, -1), swap(c0), swap(c1)
+    strips = lax.all_gather(strip.reshape(96, HD), "col", axis=0, tiled=True)
+    c0 = strips.reshape(4, 4, 24, HD).swapaxes(0, 1).reshape(384, HD)
+    downd, upd = down(d0[:2]), up(d1[:2])
+    c0, down3, up3, downd, upd = together(c0, down3, up3, downd, upd)
+
+    c1, s0 = turn(c0), swap(c0)
     mixed1 = attend(1, meta, skv1, sq1, x1, y1, d1, down3, downd)
-    s0, s1, skv0, *mixed1 = together(s0, s1, skv0, *mixed1)
-    attended1 = back(1, mixed1)
+    c0, c1, s0, skv0, *mixed1 = together(c0, c1, s0, skv0, *mixed1)
+    c2, c3, attended1 = turn(c1), turn(c0, -1), back(1, mixed1)
     mixed0 = attend(0, meta, skv0, sq0, x0, y0, d0, up3, upd)
-    c2, c3, *rest = together(c2, c3, *attended1, *mixed0)
+    rest = list(together(*attended1, *mixed0))
     attended1, mixed0 = rest[:4], rest[4:]
-    attended0, s2, s3 = back(0, mixed0), swap(c2), swap(c3)
-    return project(attended0 + attended1, meta, places, (c0, c1, c2, c3, s0, s1, s2, s3), tokens_in)
+    attended0 = back(0, mixed0)
+    c1, c2, c3, *attended0 = together(c1, c2, c3, *attended0)
+    chunks = (c0, c1, c2, c3, s0, swap(c1), swap(c2), swap(c3))
+    return project(attended0 + attended1, meta, places, chunks, tokens_in)
 
 
 def solution(mesh):

time: 196 us -> 219 us (1.12)
  between operations: 0.68 us -> 13.8 us
  local copies, waits for them, and re-layouts: 5.36 us -> 8.67 us
  waiting for transfers between devices: 92.6 us -> 95.4 us
  starting transfers between devices: 40.9 us -> 43.7 us
    slice x2, local copies, waits for them, and re-layouts: 0.1 us -> 3.29 us  [local(): downd, upd = (down(d0[:2]), up(d1[:2]))]
    ppermute x29 -> x26, starting transfers between devices: 40.9 us -> 43.7 us  [send(): return lax.ppermute(value, AXES, pairs)]
    ppermute x29 -> x26, waiting for transfers between devices: 92.6 us -> 94.4 us  [send(): return lax.ppermute(value, AXES, pairs)]
    unnamed x64 -> x54, local copies, waits for them, and re-layouts: 4.8 us -> 3.05 us
  transfers between devices with their start and end apart: 29 -> 27, of which waited for: 11 -> 16; matrix products, arithmetic and copies ran while one was open for 2% -> 4% of each run, Pallas kernels for 17% -> 15%
where the time goes in v17:
time: 219 us; the launch traced here: 218 us
  waiting for transfers between devices  95.4 us (44%)
  Pallas kernels  52.6 us (24%)
  starting transfers between devices  43.7 us (20%)
  between operations  13.8 us (6%)
  local copies, waits for them, and re-layouts  8.67 us (4%)
  other arithmetic  3.93 us (2%)
    ppermute x26, waiting for transfers between devices, send(): return lax.ppermute(value, AXES, pairs)  94.4 us
    ppermute x26, starting transfers between devices, send(): return lax.ppermute(value, AXES, pairs)  43.7 us
    pallas_call x2, Pallas kernels, attend(): pl.pallas_call(functools.partial(attend_kernel, half), grid=(H // STEP,),...  26 us
    pallas_call x1, Pallas kernels, project(): pl.pallas_call(project_kernel, grid_spec=grid_spec, out_shape=jax.ShapeDt...  16.9 us
    pallas_call x3, Pallas kernels, pack(): pl.pallas_call(functools.partial(pack_kernel, parts), out_shape=[jax.Shap...  9.62 us
  transfers between devices with their start and end apart: 27, of which 16 were waited for; matrix products, arithmetic and copies ran while one was open for 4% of the time, Pallas kernels for 15%

profile of v17, /device:TPU:1, one launch (start us, length us, event | category | flops | bytes accessed | tf_op | source)
XLA Modules:
  0.0 218.0 jit_solution(16975058768345405770)
XLA Ops:
  6.5 2.5 %pack.3 = (bf16[3,2,8,8,1536]{4,3,2,1,0:T(8,128)(2,1)}, bf16[3,2,8,8,1536]{4,3,2,1,0:T(8,128)(2,1)}) custom-call(s32[1]{0:T(128)} %bitcast.meta, bf16[4,2,8,2,8,1536]{5,4,3,2,1,0:T(8,128)(2,1)} %bitcast.48, bf16[4,2,8,2,8,1536]{5,4,3,2,1,0:T(8,128)(2,1)} %bitcast.51, bf16[4,2,8,2,8,1536]{5,4,3,2,1,0:T(8,128)(2,1)} %bitcast.54), custom_call_target="tpu_custom_call" | custom-call | bytes 6291456 | tf_op jit(solution)/shard_map/pack/pallas_call | solution.py:98
  9.1 2.5 %collective-permute-start = (bf16[24,1536]{1,0:T(8,128)(2,1)S(1)}, bf16[24,1536]{1,0:T(8,128)(2,1)S(1)}, u32[]{:S(2)}, u32[]{:S(2)}) collective-permute-start(bf16[24,1536]{1,0:T(8,128)(2,1)S(1)} %bitcast.67), channel_id=1, source_target_pairs={{0,16},{1,17},{2,18},{3,19},{4,20},{5,21},{6,22},{7,23},{8,24},{9,... | collective-permute-start | bytes 221192 | tf_op jit(solution)/shard_map/ppermute | solution.py:59
  11.6 3.3 %collective-permute-start.1 = (bf16[24,1536]{1,0:T(8,128)(2,1)S(1)}, bf16[24,1536]{1,0:T(8,128)(2,1)S(1)}, u32[]{:S(2)}, u32[]{:S(2)}) collective-permute-start(bf16[24,1536]{1,0:T(8,128)(2,1)S(1)} %bitcast.68), channel_id=1, source_target_pairs={{0,64},{1,65},{2,66},{3,67},{4,68},{5,69},{6,70},{7,71},{8,72},{9,... | collective-permute-start | bytes 221192 | tf_op jit(solution)/shard_map/ppermute | solution.py:59
  15.6 2.7 %collective-permute-start.4 = (bf16[3,128,1536]{2,1,0:T(8,128)(2,1)}, bf16[3,128,1536]{2,1,0:T(8,128)(2,1)S(1)}, u32[]{:S(2)}, u32[]{:S(2)}) collective-permute-start(bf16[3,128,1536]{2,1,0:T(8,128)(2,1)} %bitcast.72), channel_id=1, source_target_pairs={{0,1},{1,2},{2,3},{3,0},{4,5},{5,6},{6,7},{7,4},{8,9},{9,10},{10,1... | collective-permute-start | bytes 3538952 | tf_op jit(solution)/shard_map/ppermute | solution.py:59
  18.4 2.9 %collective-permute-start.3 = (bf16[3,128,1536]{2,1,0:T(8,128)(2,1)}, bf16[3,128,1536]{2,1,0:T(8,128)(2,1)S(1)}, u32[]{:S(2)}, u32[]{:S(2)}) collective-permute-start(bf16[3,128,1536]{2,1,0:T(8,128)(2,1)} %bitcast.71), channel_id=1, source_target_pairs={{0,4},{1,5},{2,6},{3,7},{4,8},{5,9},{6,10},{7,11},{8,12},{9,13},{1... | collective-permute-start | bytes 3538952 | tf_op jit(solution)/shard_map/ppermute | solution.py:59
  21.3 2.6 %pack.4 = (bf16[3,2,8,8,1536]{4,3,2,1,0:T(8,128)(2,1)}, bf16[3,2,8,8,1536]{4,3,2,1,0:T(8,128)(2,1)}) custom-call(s32[1]{0:T(128)} %bitcast.meta, bf16[4,2,8,2,8,1536]{5,4,3,2,1,0:T(8,128)(2,1)} %bitcast.49, bf16[4,2,8,2,8,1536]{5,4,3,2,1,0:T(8,128)(2,1)} %bitcast.52, bf16[4,2,8,2,8,1536]{5,4,3,2,1,0:T(8,128)(2,1)} %bitcast.55), custom_call_target="tpu_custom_call" | custom-call | bytes 6291456 | tf_op jit(solution)/shard_map/pack/pallas_call | solution.py:98
  26.0 4.5 %pack.5 = (bf16[2,2,8,8,1536]{4,3,2,1,0:T(8,128)(2,1)}, bf16[2,2,8,8,1536]{4,3,2,1,0:T(8,128)(2,1)}, bf16[3,2,8,8,1536]{4,3,2,1,0:T(8,128)(2,1)}, bf16[3,2,8,8,1...) custom-call(s32[1]{0:T(128)} %bitcast.meta, ...), custom_call_target="tpu_custom_call" | custom-call | bytes 12582912 | tf_op jit(solution)/shard_map/pack/pallas_call | solution.py:98
  31.9 2.9 %collective-permute-done.3.x = bf16[3,128,1536]{2,1,0:T(8,128)(2,1)S(1)} collective-permute-done((bf16[3,128,1536]{2,1,0:T(8,128)(2,1)}, bf16[3,128,1536]{2,1,0:T(8,128)(2,1)S(1)}, u32[]{:S(2)}, u32[]{:S(2)}) %collective-permute-start.3) | collective-permute-done | bytes 1179680 | tf_op jit(solution)/shard_map/ppermute | solution.py:59
  36.1 10.8 %collective-permute-done.6.y = bf16[3,128,1536]{2,1,0:T(8,128)(2,1)S(1)} collective-permute-done((bf16[3,128,1536]{2,1,0:T(8,128)(2,1)S(1)}, bf16[3,128,1536]{2,1,0:T(8,128)(2,1)S(1)}, u32[]{:S(2)}, u32[]{:S(2)}) %collective-permute-start.6) | collective-permute-done | bytes 1179680 | tf_op jit(solution)/shard_map/ppermute | solution.py:59
  46.9 2.3 %collective-permute-done.5.x = bf16[3,128,1536]{2,1,0:T(8,128)(2,1)S(1)} collective-permute-done((bf16[3,128,1536]{2,1,0:T(8,128)(2,1)S(1)}, bf16[3,128,1536]{2,1,0:T(8,128)(2,1)S(1)}, u32[]{:S(2)}, u32[]{:S(2)}) %collective-permute-start.5) | collective-permute-done | bytes 1179680 | tf_op jit(solution)/shard_map/ppermute | solution.py:59
  49.3 1.7 pad_maximum_fusion.1
  51.0 1.9 collective-permute-start.7
  52.9 5.1 %collective-permute-start.8 = (bf16[3,2,128,1536]{3,2,1,0:T(8,128)(2,1)}, bf16[3,2,128,1536]{3,2,1,0:T(8,128)(2,1)}, u32[]{:S(2)}, u32[]{:S(2)}) collective-permute-start(bf16[3,2,128,1536]{3,2,1,0:T(8,128)(2,1)} %pad_maximum_fusion.1), channel_id=1, source_target_pairs={{0,32},{1,33},{2,34},{3,35},{4,36},{5,37},{6,38},{7,39},{8,40},{9,... | collective-permute-start | bytes 7077896 | tf_op jit(solution)/shard_map/ppermute | solution.py:59
  58.1 3.7 %collective-permute-start.9 = (bf16[3,128,1536]{2,1,0:T(8,128)(2,1)}, bf16[3,128,1536]{2,1,0:T(8,128)(2,1)}, u32[]{:S(2)}, u32[]{:S(2)}) collective-permute-start(bf16[3,128,1536]{2,1,0:T(8,128)(2,1)} %bitcast.9), channel_id=1, source_target_pairs={{0,5},{1,6},{2,7},{3,4},{4,9},{5,10},{6,11},{7,8},{8,13},{9,14},{1... | collective-permute-start | bytes 3538952 | tf_op jit(solution)/shard_map/ppermute | solution.py:59
  61.8 25.3 %collective-permute-done.9.d = bf16[3,128,1536]{2,1,0:T(8,128)(2,1)} collective-permute-done((bf16[3,128,1536]{2,1,0:T(8,128)(2,1)}, bf16[3,128,1536]{2,1,0:T(8,128)(2,1)}, u32[]{:S(2)}, u32[]{:S(2)}) %collective-permute-start.9) | collective-permute-done | bytes 1179680 | tf_op jit(solution)/shard_map/ppermute | solution.py:59
  88.3 1.9 collective-permute-start.10
  90.2 2.1 slice.29
  92.4 5.4 %collective-permute-start.12 = (bf16[2,128,1536]{2,1,0:T(8,128)(2,1)}, bf16[2,128,1536]{2,1,0:T(8,128)(2,1)}, u32[]{:S(2)}, u32[]{:S(2)}) collective-permute-start(bf16[2,128,1536]{2,1,0:T(8,128)(2,1)} %slice.29), channel_id=1, source_target_pairs={{0,32},{1,33},{2,34},{3,35},{4,36},{5,37},{6,38},{7,39},{8,40},{9,... | collective-permute-start | bytes 2359304 | tf_op jit(solution)/shard_map/ppermute | solution.py:59
  100.1 16.4 %collective-permute-done.10.hd = bf16[2,128,1536]{2,1,0:T(8,128)(2,1)} collective-permute-done((bf16[2,128,1536]{2,1,0:T(8,128)(2,1)S(1)}, bf16[2,128,1536]{2,1,0:T(8,128)(2,1)}, u32[]{:S(2)}, u32[]{:S(2)}) %collective-permute-start.10) | collective-permute-done | bytes 786464 | tf_op jit(solution)/shard_map/ppermute | solution.py:59
  117.9 1.9 collective-permute-start.13
  119.8 13.0 %attend.2 = (bf16[128,1536]{1,0:T(8,128)(2,1)}, bf16[128,1536]{1,0:T(8,128)(2,1)}, bf16[128,1536]{1,0:T(8,128)(2,1)}, bf16[128,1536]{1,0:T(8,128)(2,1)}) custom-call(s32[4]{0:T(128)} %get-tuple-element.90.meta, bf16[2,128,1536]{2,1,0:T(8,128)(2,1)} %bitcast.65, bf16[1,128,1536]{2,1,0:T(8,128)(2,1)} %bitcast.76, bf16[3,128,1536]{2,1,0:T(8,128)(2,1)} %copy-done.6, ...), custom_call_target="tpu_custom_call" | custom-call | flops 6442450944 | bytes 10485760 | tf_op jit(solution)/shard_map/attend/pallas_call | solution.py:188
  133.0 3.2 %collective-permute-start.15 = (bf16[384,1536]{1,0:T(8,128)(2,1)S(1)}, bf16[384,1536]{1,0:T(8,128)(2,1)S(1)}, u32[]{:S(2)}, u32[]{:S(2)}) collective-permute-start(bf16[384,1536]{1,0:T(8,128)(2,1)S(1)} %collective-permute-done.13.refs_9_), channel_id=1, source_target_pairs={{0,4},{1,5},{2,6},{3,7},{4,8},{5,9},{6,10},{7,11},{8,12},{9,13},{1... | collective-permute-start | bytes 3538952 | tf_op jit(solution)/shard_map/ppermute | solution.py:59
  136.2 3.1 %collective-permute-start.17 = (bf16[128,1536]{1,0:T(8,128)(2,1)}, bf16[128,1536]{1,0:T(8,128)(2,1)S(1)}, u32[]{:S(2)}, u32[]{:S(2)}) collective-permute-start(bf16[128,1536]{1,0:T(8,128)(2,1)} %get-tuple-element.110), channel_id=1, source_target_pairs={{28,0},{29,1},{30,2},{31,3},{0,4},{1,5},{2,6},{3,7},{4,8},{5,9},{6... | collective-permute-start | bytes 1179656 | tf_op jit(solution)/shard_map/ppermute | solution.py:59
  140.8 13.0 %attend.3 = (bf16[128,1536]{1,0:T(8,128)(2,1)}, bf16[128,1536]{1,0:T(8,128)(2,1)}, bf16[128,1536]{1,0:T(8,128)(2,1)}, bf16[128,1536]{1,0:T(8,128)(2,1)}) custom-call(s32[4]{0:T(128)} %get-tuple-element.90.meta, bf16[2,128,1536]{2,1,0:T(8,128)(2,1)} %bitcast.63, bf16[1,128,1536]{2,1,0:T(8,128)(2,1)} %bitcast.75, bf16[3,128,1536]{2,1,0:T(8,128)(2,1)} %copy-done.4, ...), custom_call_target="tpu_custom_call" | custom-call | flops 6442450944 | bytes 10485760 | tf_op jit(solution)/shard_map/attend/pallas_call | solution.py:188
  153.8 12.4 %collective-permute-done.17.refs_5_ = bf16[128,1536]{1,0:T(8,128)(2,1)S(1)} collective-permute-done((bf16[128,1536]{1,0:T(8,128)(2,1)}, bf16[128,1536]{1,0:T(8,128)(2,1)S(1)}, u32[]{:S(2)}, u32[]{:S(2)}) %collective-permute-start.17) | collective-permute-done | bytes 393248 | tf_op jit(solution)/shard_map/ppermute | solution.py:59
  166.3 4.2 %collective-permute-done.19.refs_7_ = bf16[128,1536]{1,0:T(8,128)(2,1)S(1)} collective-permute-done((bf16[128,1536]{1,0:T(8,128)(2,1)}, bf16[128,1536]{1,0:T(8,128)(2,1)S(1)}, u32[]{:S(2)}, u32[]{:S(2)}) %collective-permute-start.19) | collective-permute-done | bytes 393248 | tf_op jit(solution)/shard_map/ppermute | solution.py:59
  171.4 2.0 collective-permute-start.22
  173.5 6.3 %collective-permute-done.20.refs_1_ = bf16[128,1536]{1,0:T(8,128)(2,1)S(1)} collective-permute-done((bf16[128,1536]{1,0:T(8,128)(2,1)}, bf16[128,1536]{1,0:T(8,128)(2,1)S(1)}, u32[]{:S(2)}, u32[]{:S(2)}) %collective-permute-start.20) | collective-permute-done | bytes 393248 | tf_op jit(solution)/shard_map/ppermute | solution.py:59
  179.8 6.3 %collective-permute-done.22.refs_3_ = bf16[128,1536]{1,0:T(8,128)(2,1)S(1)} collective-permute-done((bf16[128,1536]{1,0:T(8,128)(2,1)}, bf16[128,1536]{1,0:T(8,128)(2,1)S(1)}, u32[]{:S(2)}, u32[]{:S(2)}) %collective-permute-start.22) | collective-permute-done | bytes 393248 | tf_op jit(solution)/shard_map/ppermute | solution.py:59
  187.4 2.3 %collective-permute-done.23.refs_13_ = bf16[384,1536]{1,0:T(8,128)(2,1)S(1)} collective-permute-done((bf16[384,1536]{1,0:T(8,128)(2,1)S(1)}, bf16[384,1536]{1,0:T(8,128)(2,1)S(1)}, u32[]{:S(2)}, u32[]{:S(2)}) %collective-permute-start.23) | collective-permute-done | bytes 1179680 | tf_op jit(solution)/shard_map/ppermute | solution.py:59
  189.7 1.7 collective-permute-done.24.refs_14_
  194.2 16.9 %project.1 = bf16[4,16,16,3072]{3,2,1,0:T(8,128)(2,1)} custom-call(s32[4]{0:T(128)} %get-tuple-element.90.meta, s32[4]{0:T(128)} %get-tuple-element.91.places, bf16[128,1536]{1,0:T(8,128)(2,1)} %get-tuple-element.127.refs_0_, bf16[128,1536]{1,0:T(8,128)(2,1)} %copy-done.20, bf16[128,1536]{1,0:T(8,128)(2,1)} %copy-done.21, bf16[128,1536]{1,0:T(8,128)(2,1)} %copy-done.22, ...), custom_call_target="tpu_custom_call" | custom-call | flops 9663676416 | bytes 26214400 | tf_op jit(solution)/shard_map/project/pallas_call | solution.py:271
  (96 shorter events, 17.1 us)
Async XLA Ops:
  6.5 92.2 %all-gather.2.cloned.1.call-start = ((), (), s32[]{:S(2)}) async-start(), calls=%async_computation | async-start | bytes 1474560 | tf_op jit(solution)/shard_map/all_gather | solution.py:322
  9.1 16.8 %collective-permute-start = (bf16[24,1536]{1,0:T(8,128)(2,1)S(1)}, bf16[24,1536]{1,0:T(8,128)(2,1)S(1)}, u32[]{:S(2)}, u32[]{:S(2)}) collective-permute-start(bf16[24,1536]{1,0:T(8,128)(2,1)S(1)} %bitcast.67), channel_id=1, source_target_pairs={{0,16},{1,17},{2,18},{3,19},{4,20},{5,21},{6,22},{7,23},{8,24},{9,... | collective-permute-start | bytes 221192 | tf_op jit(solution)/shard_map/ppermute | solution.py:59
  11.6 14.3 %collective-permute-start.1 = (bf16[24,1536]{1,0:T(8,128)(2,1)S(1)}, bf16[24,1536]{1,0:T(8,128)(2,1)S(1)}, u32[]{:S(2)}, u32[]{:S(2)}) collective-permute-start(bf16[24,1536]{1,0:T(8,128)(2,1)S(1)} %bitcast.68), channel_id=1, source_target_pairs={{0,64},{1,65},{2,66},{3,67},{4,68},{5,69},{6,70},{7,71},{8,72},{9,... | collective-permute-start | bytes 221192 | tf_op jit(solution)/shard_map/ppermute | solution.py:59
  14.9 11.0 %collective-permute-start.2 = (bf16[24,1536]{1,0:T(8,128)(2,1)S(1)}, bf16[24,1536]{1,0:T(8,128)(2,1)S(1)}, u32[]{:S(2)}, u32[]{:S(2)}) collective-permute-start(bf16[24,1536]{1,0:T(8,128)(2,1)S(1)} %bitcast.69), channel_id=1, source_target_pairs={{0,80},{1,81},{2,82},{3,83},{4,84},{5,85},{6,86},{7,87},{8,88},{9,... | collective-permute-start | bytes 221192 | tf_op jit(solution)/shard_map/ppermute | solution.py:59
  15.6 16.2 %collective-permute-start.4 = (bf16[3,128,1536]{2,1,0:T(8,128)(2,1)}, bf16[3,128,1536]{2,1,0:T(8,128)(2,1)S(1)}, u32[]{:S(2)}, u32[]{:S(2)}) collective-permute-start(bf16[3,128,1536]{2,1,0:T(8,128)(2,1)} %bitcast.72), channel_id=1, source_target_pairs={{0,1},{1,2},{2,3},{3,0},{4,5},{5,6},{6,7},{7,4},{8,9},{9,10},{10,1... | collective-permute-start | bytes 3538952 | tf_op jit(solution)/shard_map/ppermute | solution.py:59
  18.4 16.4 %collective-permute-start.3 = (bf16[3,128,1536]{2,1,0:T(8,128)(2,1)}, bf16[3,128,1536]{2,1,0:T(8,128)(2,1)S(1)}, u32[]{:S(2)}, u32[]{:S(2)}) collective-permute-start(bf16[3,128,1536]{2,1,0:T(8,128)(2,1)} %bitcast.71), channel_id=1, source_target_pairs={{0,4},{1,5},{2,6},{3,7},{4,8},{5,9},{6,10},{7,11},{8,12},{9,13},{1... | collective-permute-start | bytes 3538952 | tf_op jit(solution)/shard_map/ppermute | solution.py:59
  30.5 16.3 %collective-permute-start.6 = (bf16[3,128,1536]{2,1,0:T(8,128)(2,1)S(1)}, bf16[3,128,1536]{2,1,0:T(8,128)(2,1)S(1)}, u32[]{:S(2)}, u32[]{:S(2)}) collective-permute-start(bf16[3,128,1536]{2,1,0:T(8,128)(2,1)S(1)} %bitcast.74), channel_id=1, source_target_pairs={{0,3},{1,0},{2,1},{3,2},{4,7},{5,4},{6,5},{7,6},{8,11},{9,8},{10,9... | collective-permute-start | bytes 3538952 | tf_op jit(solution)/shard_map/ppermute | solution.py:59
  30.7 18.5 %collective-permute-start.5 = (bf16[3,128,1536]{2,1,0:T(8,128)(2,1)S(1)}, bf16[3,128,1536]{2,1,0:T(8,128)(2,1)S(1)}, u32[]{:S(2)}, u32[]{:S(2)}) collective-permute-start(bf16[3,128,1536]{2,1,0:T(8,128)(2,1)S(1)} %bitcast.73), channel_id=1, source_target_pairs={{0,28},{1,29},{2,30},{3,31},{4,0},{5,1},{6,2},{7,3},{8,4},{9,5},{1... | collective-permute-start | bytes 3538952 | tf_op jit(solution)/shard_map/ppermute | solution.py:59
  51.0 66.9 %collective-permute-start.7 = (bf16[3,2,128,1536]{3,2,1,0:T(8,128)(2,1)S(1)}, bf16[3,2,128,1536]{3,2,1,0:T(8,128)(2,1)}, u32[]{:S(2)}, u32[]{:S(2)}) collective-permute-start(bf16[3,2,128,1536]{3,2,1,0:T(8,128)(2,1)S(1)} %pad_maximum_fusion), channel_id=1, source_target_pairs={{32,0},{33,1},{34,2},{35,3},{36,4},{37,5},{38,6},{39,7},{40,8},{41... | collective-permute-start | bytes 7077896 | tf_op jit(solution)/shard_map/ppermute | solution.py:59
  52.9 64.9 %collective-permute-start.8 = (bf16[3,2,128,1536]{3,2,1,0:T(8,128)(2,1)}, bf16[3,2,128,1536]{3,2,1,0:T(8,128)(2,1)}, u32[]{:S(2)}, u32[]{:S(2)}) collective-permute-start(bf16[3,2,128,1536]{3,2,1,0:T(8,128)(2,1)} %pad_maximum_fusion.1), channel_id=1, source_target_pairs={{0,32},{1,33},{2,34},{3,35},{4,36},{5,37},{6,38},{7,39},{8,40},{9,... | collective-permute-start | bytes 7077896 | tf_op jit(solution)/shard_map/ppermute | solution.py:59
  58.1 29.0 %collective-permute-start.9 = (bf16[3,128,1536]{2,1,0:T(8,128)(2,1)}, bf16[3,128,1536]{2,1,0:T(8,128)(2,1)}, u32[]{:S(2)}, u32[]{:S(2)}) collective-permute-start(bf16[3,128,1536]{2,1,0:T(8,128)(2,1)} %bitcast.9), channel_id=1, source_target_pairs={{0,5},{1,6},{2,7},{3,4},{4,9},{5,10},{6,11},{7,8},{8,13},{9,14},{1... | collective-permute-start | bytes 3538952 | tf_op jit(solution)/shard_map/ppermute | solution.py:59
  61.8 28.5 %collective-permute-start.11 = (bf16[3,128,1536]{2,1,0:T(8,128)(2,1)}, bf16[3,128,1536]{2,1,0:T(8,128)(2,1)}, u32[]{:S(2)}, u32[]{:S(2)}) collective-permute-start(bf16[3,128,1536]{2,1,0:T(8,128)(2,1)} %bitcast.10), channel_id=1, source_target_pairs={{0,31},{1,28},{2,29},{3,30},{4,3},{5,0},{6,1},{7,2},{8,7},{9,4},{1... | collective-permute-start | bytes 3538952 | tf_op jit(solution)/shard_map/ppermute | solution.py:59
  88.3 28.2 %collective-permute-start.10 = (bf16[2,128,1536]{2,1,0:T(8,128)(2,1)S(1)}, bf16[2,128,1536]{2,1,0:T(8,128)(2,1)}, u32[]{:S(2)}, u32[]{:S(2)}) collective-permute-start(bf16[2,128,1536]{2,1,0:T(8,128)(2,1)S(1)} %slice.28), channel_id=1, source_target_pairs={{32,0},{33,1},{34,2},{35,3},{36,4},{37,5},{38,6},{39,7},{40,8},{41... | collective-permute-start | bytes 2359304 | tf_op jit(solution)/shard_map/ppermute | solution.py:59
  92.4 25.5 %collective-permute-start.12 = (bf16[2,128,1536]{2,1,0:T(8,128)(2,1)}, bf16[2,128,1536]{2,1,0:T(8,128)(2,1)}, u32[]{:S(2)}, u32[]{:S(2)}) collective-permute-start(bf16[2,128,1536]{2,1,0:T(8,128)(2,1)} %slice.29), channel_id=1, source_target_pairs={{0,32},{1,33},{2,34},{3,35},{4,36},{5,37},{6,38},{7,39},{8,40},{9,... | collective-permute-start | bytes 2359304 | tf_op jit(solution)/shard_map/ppermute | solution.py:59
  100.1 36.1 %copy-start = (bf16[4,4,24,1536]{3,2,1,0:T(8,128)(2,1)}, bf16[4,4,24,1536]{3,2,1,0:T(8,128)(2,1)S(1)}, u32[]{:S(2)}) copy-start(bf16[4,4,24,1536]{3,2,1,0:T(8,128)(2,1)S(1)} %copy.7) | copy-start | bytes 3538948
  117.9 15.1 %collective-permute-start.13 = (bf16[384,1536]{1,0:T(8,128)(2,1)S(1)}, bf16[384,1536]{1,0:T(8,128)(2,1)S(1)}, u32[]{:S(2)}, u32[]{:S(2)}) collective-permute-start(bf16[384,1536]{1,0:T(8,128)(2,1)S(1)} %bitcast.57), channel_id=1, source_target_pairs={{0,4},{1,5},{2,6},{3,7},{4,8},{5,9},{6,10},{7,11},{8,12},{9,13},{1... | collective-permute-start | bytes 3538952 | tf_op jit(solution)/shard_map/ppermute | solution.py:59
  119.8 13.2 %collective-permute-start.14 = (bf16[384,1536]{1,0:T(8,128)(2,1)S(1)}, bf16[384,1536]{1,0:T(8,128)(2,1)S(1)}, u32[]{:S(2)}, u32[]{:S(2)}) collective-permute-start(bf16[384,1536]{1,0:T(8,128)(2,1)S(1)} %bitcast.58), channel_id=1, source_target_pairs={{0,32},{1,33},{2,34},{3,35},{4,36},{5,37},{6,38},{7,39},{8,40},{9,... | collective-permute-start | bytes 3538952 | tf_op jit(solution)/shard_map/ppermute | solution.py:59
  133.0 53.1 %copy-start.8 = (bf16[384,1536]{1,0:T(8,128)(2,1)}, bf16[384,1536]{1,0:T(8,128)(2,1)S(1)}, u32[]{:S(2)}) copy-start(bf16[384,1536]{1,0:T(8,128)(2,1)S(1)} %collective-permute-done.13.refs_9_) | copy-start | bytes 3538948
  133.0 53.1 %collective-permute-start.15 = (bf16[384,1536]{1,0:T(8,128)(2,1)S(1)}, bf16[384,1536]{1,0:T(8,128)(2,1)S(1)}, u32[]{:S(2)}, u32[]{:S(2)}) collective-permute-start(bf16[384,1536]{1,0:T(8,128)(2,1)S(1)} %collective-permute-done.13.refs_9_), channel_id=1, source_target_pairs={{0,4},{1,5},{2,6},{3,7},{4,8},{5,9},{6,10},{7,11},{8,12},{9,13},{1... | collective-permute-start | bytes 3538952 | tf_op jit(solution)/shard_map/ppermute | solution.py:59
  136.2 49.9 %collective-permute-start.16 = (bf16[384,1536]{1,0:T(8,128)(2,1)S(1)}, bf16[384,1536]{1,0:T(8,128)(2,1)S(1)}, u32[]{:S(2)}, u32[]{:S(2)}) collective-permute-start(bf16[384,1536]{1,0:T(8,128)(2,1)S(1)} %bitcast.59), channel_id=1, source_target_pairs={{0,12},{1,13},{2,14},{3,15},{4,0},{5,1},{6,2},{7,3},{8,4},{9,5},{1... | collective-permute-start | bytes 3538952 | tf_op jit(solution)/shard_map/ppermute | solution.py:59
  136.2 30.1 %collective-permute-start.17 = (bf16[128,1536]{1,0:T(8,128)(2,1)}, bf16[128,1536]{1,0:T(8,128)(2,1)S(1)}, u32[]{:S(2)}, u32[]{:S(2)}) collective-permute-start(bf16[128,1536]{1,0:T(8,128)(2,1)} %get-tuple-element.110), channel_id=1, source_target_pairs={{28,0},{29,1},{30,2},{31,3},{0,4},{1,5},{2,6},{3,7},{4,8},{5,9},{6... | collective-permute-start | bytes 1179656 | tf_op jit(solution)/shard_map/ppermute | solution.py:59
  139.3 27.0 %collective-permute-start.18 = (bf16[128,1536]{1,0:T(8,128)(2,1)}, bf16[128,1536]{1,0:T(8,128)(2,1)S(1)}, u32[]{:S(2)}, u32[]{:S(2)}) collective-permute-start(bf16[128,1536]{1,0:T(8,128)(2,1)} %get-tuple-element.111), channel_id=1, source_target_pairs={{3,0},{0,1},{1,2},{2,3},{7,4},{4,5},{5,6},{6,7},{11,8},{8,9},{9,10... | collective-permute-start | bytes 1179656 | tf_op jit(solution)/shard_map/ppermute | solution.py:59
  140.8 29.7 %collective-permute-start.19 = (bf16[128,1536]{1,0:T(8,128)(2,1)}, bf16[128,1536]{1,0:T(8,128)(2,1)S(1)}, u32[]{:S(2)}, u32[]{:S(2)}) collective-permute-start(bf16[128,1536]{1,0:T(8,128)(2,1)} %get-tuple-element.112), channel_id=1, source_target_pairs={{31,0},{28,1},{29,2},{30,3},{3,4},{0,5},{1,6},{2,7},{7,8},{4,9},{5... | collective-permute-start | bytes 1179656 | tf_op jit(solution)/shard_map/ppermute | solution.py:59
  166.3 26.8 %copy-start.17 = (bf16[128,1536]{1,0:T(8,128)(2,1)}, bf16[128,1536]{1,0:T(8,128)(2,1)S(1)}, u32[]{:S(2)}) copy-start(bf16[128,1536]{1,0:T(8,128)(2,1)S(1)} %collective-permute-done.17.refs_5_) | copy-start | bytes 1179652
  166.3 26.8 %copy-start.18 = (bf16[128,1536]{1,0:T(8,128)(2,1)}, bf16[128,1536]{1,0:T(8,128)(2,1)S(1)}, u32[]{:S(2)}) copy-start(bf16[128,1536]{1,0:T(8,128)(2,1)S(1)} %collective-permute-done.18.refs_6_) | copy-start | bytes 1179652
  170.5 22.6 %copy-start.19 = (bf16[128,1536]{1,0:T(8,128)(2,1)}, bf16[128,1536]{1,0:T(8,128)(2,1)S(1)}, u32[]{:S(2)}) copy-start(bf16[128,1536]{1,0:T(8,128)(2,1)S(1)} %collective-permute-done.19.refs_7_) | copy-start | bytes 1179652
  170.5 9.3 %collective-permute-start.20 = (bf16[128,1536]{1,0:T(8,128)(2,1)}, bf16[128,1536]{1,0:T(8,128)(2,1)S(1)}, u32[]{:S(2)}, u32[]{:S(2)}) collective-permute-start(bf16[128,1536]{1,0:T(8,128)(2,1)} %get-tuple-element.124), channel_id=1, source_target_pairs={{4,0},{5,1},{6,2},{7,3},{8,4},{9,5},{10,6},{11,7},{12,8},{13,9},{1... | collective-permute-start | bytes 1179656 | tf_op jit(solution)/shard_map/ppermute | solution.py:59
  170.5 9.3 %collective-permute-start.21 = (bf16[128,1536]{1,0:T(8,128)(2,1)}, bf16[128,1536]{1,0:T(8,128)(2,1)S(1)}, u32[]{:S(2)}, u32[]{:S(2)}) collective-permute-start(bf16[128,1536]{1,0:T(8,128)(2,1)} %get-tuple-element.125), channel_id=1, source_target_pairs={{1,0},{2,1},{3,2},{0,3},{5,4},{6,5},{7,6},{4,7},{9,8},{10,9},{11,1... | collective-permute-start | bytes 1179656 | tf_op jit(solution)/shard_map/ppermute | solution.py:59
  171.4 14.6 %collective-permute-start.22 = (bf16[128,1536]{1,0:T(8,128)(2,1)}, bf16[128,1536]{1,0:T(8,128)(2,1)S(1)}, u32[]{:S(2)}, u32[]{:S(2)}) collective-permute-start(bf16[128,1536]{1,0:T(8,128)(2,1)} %get-tuple-element.126), channel_id=1, source_target_pairs={{5,0},{6,1},{7,2},{4,3},{9,4},{10,5},{11,6},{8,7},{13,8},{14,9},{1... | collective-permute-start | bytes 1179656 | tf_op jit(solution)/shard_map/ppermute | solution.py:59
  186.9 2.8 %collective-permute-start.23 = (bf16[384,1536]{1,0:T(8,128)(2,1)S(1)}, bf16[384,1536]{1,0:T(8,128)(2,1)S(1)}, u32[]{:S(2)}, u32[]{:S(2)}) collective-permute-start(bf16[384,1536]{1,0:T(8,128)(2,1)S(1)} %collective-permute-done.13.refs_9_), channel_id=1, source_target_pairs={{0,32},{1,33},{2,34},{3,35},{4,36},{5,37},{6,38},{7,39},{8,40},{9,... | collective-permute-start | bytes 3538952 | tf_op jit(solution)/shard_map/ppermute | solution.py:59
  186.9 4.5 %collective-permute-start.24 = (bf16[384,1536]{1,0:T(8,128)(2,1)S(1)}, bf16[384,1536]{1,0:T(8,128)(2,1)S(1)}, u32[]{:S(2)}, u32[]{:S(2)}) collective-permute-start(bf16[384,1536]{1,0:T(8,128)(2,1)S(1)} %collective-permute-done.15.refs_10_), channel_id=1, source_target_pairs={{0,32},{1,33},{2,34},{3,35},{4,36},{5,37},{6,38},{7,39},{8,40},{9,... | collective-permute-start | bytes 3538952 | tf_op jit(solution)/shard_map/ppermute | solution.py:59
  187.4 5.7 %collective-permute-start.25 = (bf16[384,1536]{1,0:T(8,128)(2,1)S(1)}, bf16[384,1536]{1,0:T(8,128)(2,1)S(1)}, u32[]{:S(2)}, u32[]{:S(2)}) collective-permute-start(bf16[384,1536]{1,0:T(8,128)(2,1)S(1)} %collective-permute-done.16.refs_11_), channel_id=1, source_target_pairs={{0,32},{1,33},{2,34},{3,35},{4,36},{5,37},{6,38},{7,39},{8,40},{9,... | collective-permute-start | bytes 3538952 | tf_op jit(solution)/shard_map/ppermute | solution.py:59
  (19 other events, 82.8 us)
Sparse Core Ops, SparseCore 0:
  61.9 36.7 all-gather.1

commit v18 on v16

--- a/solution.py
+++ b/solution.py
@@ -279,9 +279,12 @@
     )(meta, places, *attended, *chunks, tokens, *extra)
 
 
-def ring_order(own, first, second, third, place):
-    row = jnp.stack([third, second, first, own, third, second, first])
-    return lax.dynamic_slice_in_dim(row, 3 - place, 4, axis=0)
+def flip_pairs(frame_bit, row_bit):
+    return [(index(f, r, c), index(f ^ frame_bit, r ^ row_bit, c)) for f, r, c in every()]
+
+
+def side_by_side(own, other, bit):
+    return jnp.where(bit == 0, jnp.stack([own, other]), jnp.stack([other, own]))
 
 
 def together(*values):
@@ -309,14 +312,15 @@
     x0, y0 = pack(((0, 1, "kvq"), (0, 2, "kvq")), frame, *arrays)
     x0, y0, frame, shard = together(x0, y0, frame, shard)
     x0, y0 = go(x0, 0, row), go(y0, 0, col)
-    shards = [send(shard, shift_pairs(dz=n)) for n in (1, 2, 3)]
+    pair = side_by_side(shard, send(shard, flip_pairs(0, 4)), (r >> 2) & 1)
+    rest_of_strip = send(pair, flip_pairs(2, 0))
     x1, y1 = pack(((1, 1, "kvq"), (1, 2, "kvq")), frame, *arrays)
-    x1, y1, frame, *shards = together(x1, y1, frame, *shards)
+    x1, y1, frame, pair = together(x1, y1, frame, pair)
     x1, y1 = go(x1, 1, row), go(y1, 1, col)
     skv0, skv1, d0, d1, sq0, sq1 = pack(
         ((0, 0, "kv"), (1, 0, "kv"), (0, 3, "kvq"), (1, 3, "kvq"), (0, 0, "q"), (1, 0, "q")), frame, *arrays
     )
-    strip = ring_order(shard, *shards, (f >> 1) * 2 + (r >> 2))
+    strip = side_by_side(pair, rest_of_strip, (f >> 1) & 1)
     h0, h1 = jnp.stack([skv0, x0[:2], y0[:2]]), jnp.stack([skv1, x1[:2], y1[:2]])
     d0, d1, h0, h1, x0, y0, x1, y1, meta, places, strip = together(d0, d1, h0, h1, x0, y0, x1, y1, meta, places, strip)
     d0, d1, down3, up3 = go(d0, 0, both), go(d1, 1, both), down(h0), up(h1)

time: 194 us -> 201 us (1.036)
  waiting for transfers between devices: 65.4 us -> 79.3 us
  starting transfers between devices: 43.8 us -> 35.7 us
    ppermute x26 -> x25, waiting for transfers between devices: 35.7 us -> 46 us  [send(): return lax.ppermute(value, AXES, pairs)]
    ppermute x26 -> x25, starting transfers between devices: 43.8 us -> 35.7 us  [send(): return lax.ppermute(value, AXES, pairs)]
    all_gather x1, waiting for transfers between devices: 29.6 us -> 33.4 us  [local(): strips = lax.all_gather(strip.reshape(96, HD), 'col', axis=0, tiled=True)]
    unnamed x56 -> x48, local copies, waits for them, and re-layouts: 5.1 us -> 4.54 us
  transfers between devices with their start and end apart: 27 -> 26, of which waited for: 11 -> 10; matrix products, arithmetic and copies ran while one was open for 3% -> 4% of each run, Pallas kernels for 23% -> 22%
where the time goes in v18:
time: 201 us
  waiting for transfers between devices  79.3 us (39%)
  Pallas kernels  57.5 us (29%)
  starting transfers between devices  35.7 us (18%)
  between operations  13.8 us (7%)
  local copies, waits for them, and re-layouts  9.47 us (5%)
  other arithmetic  4.72 us (2%)
    ppermute x25, waiting for transfers between devices, send(): return lax.ppermute(value, AXES, pairs)  46 us
    ppermute x25, starting transfers between devices, send(): return lax.ppermute(value, AXES, pairs)  35.7 us
    all_gather x1, waiting for transfers between devices, local(): strips = lax.all_gather(strip.reshape(96, HD), 'col', axis=0, tiled=True)  33.4 us
    pallas_call x2, Pallas kernels, attend(): pl.pallas_call(functools.partial(attend_kernel, half), grid=(H // STEP,),...  26.1 us
    pallas_call x2, Pallas kernels, project(): pl.pallas_call(functools.partial(project_kernel, half), grid_spec=grid_sp...  22.1 us
    pallas_call x3, Pallas kernels, pack(): pl.pallas_call(functools.partial(pack_kernel, parts), out_shape=[jax.Shap...  9.39 us
    unnamed x48, local copies, waits for them, and re-layouts  4.54 us
  transfers between devices with their start and end apart: 26, of which 10 were waited for; matrix products, arithmetic and copies ran while one was open for 4% of the time, Pallas kernels for 22%

profile of v18, /device:TPU:1, one launch (start us, length us, event | category | flops | bytes accessed | tf_op | source)
XLA Modules:
  0.0 200.6 jit_solution(1685438797064532705)
XLA Ops:
  6.5 2.5 %pack.3 = (bf16[3,2,8,8,1536]{4,3,2,1,0:T(8,128)(2,1)}, bf16[3,2,8,8,1536]{4,3,2,1,0:T(8,128)(2,1)}) custom-call(s32[1]{0:T(128)} %bitcast.meta, bf16[4,2,8,2,8,1536]{5,4,3,2,1,0:T(8,128)(2,1)} %bitcast.41, bf16[4,2,8,2,8,1536]{5,4,3,2,1,0:T(8,128)(2,1)} %bitcast.44, bf16[4,2,8,2,8,1536]{5,4,3,2,1,0:T(8,128)(2,1)} %bitcast.47), custom_call_target="tpu_custom_call" | custom-call | bytes 6291456 | tf_op jit(solution)/shard_map/pack/pallas_call | solution.py:98
  9.1 4.7 %collective-permute-start.1 = (bf16[3,128,1536]{2,1,0:T(8,128)(2,1)}, bf16[3,128,1536]{2,1,0:T(8,128)(2,1)S(1)}, u32[]{:S(2)}, u32[]{:S(2)}) collective-permute-start(bf16[3,128,1536]{2,1,0:T(8,128)(2,1)} %bitcast.67), channel_id=1, source_target_pairs={{0,4},{1,5},{2,6},{3,7},{4,8},{5,9},{6,10},{7,11},{8,12},{9,13},{1... | collective-permute-start | bytes 3538952 | tf_op jit(solution)/shard_map/ppermute | solution.py:59
  13.8 2.7 %collective-permute-start.2 = (bf16[3,128,1536]{2,1,0:T(8,128)(2,1)}, bf16[3,128,1536]{2,1,0:T(8,128)(2,1)}, u32[]{:S(2)}, u32[]{:S(2)}) collective-permute-start(bf16[3,128,1536]{2,1,0:T(8,128)(2,1)} %bitcast.66), channel_id=1, source_target_pairs={{0,1},{1,2},{2,3},{3,0},{4,5},{5,6},{6,7},{7,4},{8,9},{9,10},{10,1... | collective-permute-start | bytes 3538952 | tf_op jit(solution)/shard_map/ppermute | solution.py:59
  16.5 13.1 %collective-permute-done = bf16[24,1536]{1,0:T(8,128)(2,1)S(1)} collective-permute-done((bf16[24,1536]{1,0:T(8,128)(2,1)S(1)}, bf16[24,1536]{1,0:T(8,128)(2,1)S(1)}, u32[]{:S(2)}, u32[]{:S(2)}) %collective-permute-start) | collective-permute-done | bytes 73760 | tf_op jit(solution)/shard_map/ppermute | solution.py:59
  29.7 3.7 %collective-permute-start.5 = (bf16[2,24,1536]{2,1,0:T(8,128)(2,1)S(1)}, bf16[2,24,1536]{2,1,0:T(8,128)(2,1)S(1)}, u32[]{:S(2)}, u32[]{:S(2)}) collective-permute-start(bf16[2,24,1536]{2,1,0:T(8,128)(2,1)S(1)} %maximum_select_fusion.1), channel_id=1, source_target_pairs={{0,64},{1,65},{2,66},{3,67},{4,68},{5,69},{6,70},{7,71},{8,72},{9,... | collective-permute-start | bytes 442376 | tf_op jit(solution)/shard_map/ppermute | solution.py:59
  34.1 2.5 %pack.4 = (bf16[3,2,8,8,1536]{4,3,2,1,0:T(8,128)(2,1)}, bf16[3,2,8,8,1536]{4,3,2,1,0:T(8,128)(2,1)}) custom-call(s32[1]{0:T(128)} %bitcast.meta, bf16[4,2,8,2,8,1536]{5,4,3,2,1,0:T(8,128)(2,1)} %bitcast.42, bf16[4,2,8,2,8,1536]{5,4,3,2,1,0:T(8,128)(2,1)} %bitcast.45, bf16[4,2,8,2,8,1536]{5,4,3,2,1,0:T(8,128)(2,1)} %bitcast.48), custom_call_target="tpu_custom_call" | custom-call | bytes 6291456 | tf_op jit(solution)/shard_map/pack/pallas_call | solution.py:98
  36.6 1.3 pad_add_fusion
  37.9 1.3 collective-permute-start.4
  39.2 4.3 %pack.5 = (bf16[2,2,8,8,1536]{4,3,2,1,0:T(8,128)(2,1)}, bf16[2,2,8,8,1536]{4,3,2,1,0:T(8,128)(2,1)}, bf16[3,2,8,8,1536]{4,3,2,1,0:T(8,128)(2,1)}, bf16[3,2,8,8,1...) custom-call(s32[1]{0:T(128)} %bitcast.meta, ...), custom_call_target="tpu_custom_call" | custom-call | bytes 12582912 | tf_op jit(solution)/shard_map/pack/pallas_call | solution.py:98
  44.4 1.6 slice_bitcast_fusion.2
  46.4 8.9 %collective-permute-done.3.x = bf16[3,128,1536]{2,1,0:T(8,128)(2,1)S(1)} collective-permute-done((bf16[3,128,1536]{2,1,0:T(8,128)(2,1)}, bf16[3,128,1536]{2,1,0:T(8,128)(2,1)S(1)}, u32[]{:S(2)}, u32[]{:S(2)}) %collective-permute-start.3) | collective-permute-done | bytes 1179680 | tf_op jit(solution)/shard_map/ppermute | solution.py:59
  57.1 1.7 pad_maximum_fusion.1
  58.8 2.6 %collective-permute-start.6 = (bf16[3,128,1536]{2,1,0:T(8,128)(2,1)}, bf16[3,128,1536]{2,1,0:T(8,128)(2,1)S(1)}, u32[]{:S(2)}, u32[]{:S(2)}) collective-permute-start(bf16[3,128,1536]{2,1,0:T(8,128)(2,1)} %bitcast.69), channel_id=1, source_target_pairs={{0,5},{1,6},{2,7},{3,4},{4,9},{5,10},{6,11},{7,8},{8,13},{9,14},{1... | collective-permute-start | bytes 3538952 | tf_op jit(solution)/shard_map/ppermute | solution.py:59
  61.4 4.9 %collective-permute-start.11 = (bf16[3,2,128,1536]{3,2,1,0:T(8,128)(2,1)S(1)}, bf16[3,2,128,1536]{3,2,1,0:T(8,128)(2,1)}, u32[]{:S(2)}, u32[]{:S(2)}) collective-permute-start(bf16[3,2,128,1536]{3,2,1,0:T(8,128)(2,1)S(1)} %pad_maximum_fusion), channel_id=1, source_target_pairs={{32,0},{33,1},{34,2},{35,3},{36,4},{37,5},{38,6},{39,7},{40,8},{41... | collective-permute-start | bytes 7077896 | tf_op jit(solution)/shard_map/ppermute | solution.py:59
  66.3 2.4 %collective-permute-start.12 = (bf16[3,2,128,1536]{3,2,1,0:T(8,128)(2,1)}, bf16[3,2,128,1536]{3,2,1,0:T(8,128)(2,1)}, u32[]{:S(2)}, u32[]{:S(2)}) collective-permute-start(bf16[3,2,128,1536]{3,2,1,0:T(8,128)(2,1)} %pad_maximum_fusion.1), channel_id=1, source_target_pairs={{0,32},{1,33},{2,34},{3,35},{4,36},{5,37},{6,38},{7,39},{8,40},{9,... | collective-permute-start | bytes 7077896 | tf_op jit(solution)/shard_map/ppermute | solution.py:59
  68.7 33.4 %all-gather.2.cloned.1.call-done = bf16[384,1536]{1,0:T(8,128)(2,1)} async-done(((bf16[96,1536]{1,0:T(8,128)(2,1)}), bf16[384,1536]{1,0:T(8,128)(2,1)}) %all-gather.2.cloned.1.call-update) | async-done | bytes 1179664 | tf_op jit(solution)/shard_map/all_gather | solution.py:327
  102.1 1.4 copy.8
  103.6 1.8 slice.23
  105.4 3.5 %collective-permute-start.10 = (bf16[2,128,1536]{2,1,0:T(8,128)(2,1)S(1)}, bf16[2,128,1536]{2,1,0:T(8,128)(2,1)S(1)}, u32[]{:S(2)}, u32[]{:S(2)}) collective-permute-start(bf16[2,128,1536]{2,1,0:T(8,128)(2,1)S(1)} %slice.23), channel_id=1, source_target_pairs={{0,32},{1,33},{2,34},{3,35},{4,36},{5,37},{6,38},{7,39},{8,40},{9,... | collective-permute-start | bytes 2359304 | tf_op jit(solution)/shard_map/ppermute | solution.py:59
  108.9 1.9 collective-permute-start.9
  110.8 6.4 %collective-permute-done.11.h3 = bf16[3,2,128,1536]{3,2,1,0:T(8,128)(2,1)} collective-permute-done((bf16[3,2,128,1536]{3,2,1,0:T(8,128)(2,1)S(1)}, bf16[3,2,128,1536]{3,2,1,0:T(8,128)(2,1)}, u32[]{:S(2)}, u32[]{:S(2)}) %collective-permute-start.11) | collective-permute-done | bytes 2359328 | tf_op jit(solution)/shard_map/ppermute | solution.py:59
  117.2 8.1 %collective-permute-done.10.hd = bf16[2,128,1536]{2,1,0:T(8,128)(2,1)S(1)} collective-permute-done((bf16[2,128,1536]{2,1,0:T(8,128)(2,1)S(1)}, bf16[2,128,1536]{2,1,0:T(8,128)(2,1)S(1)}, u32[]{:S(2)}, u32[]{:S(2)}) %collective-permute-start.10) | collective-permute-done | bytes 786464 | tf_op jit(solution)/shard_map/ppermute | solution.py:59
  127.7 13.0 %attend.2 = (bf16[128,1536]{1,0:T(8,128)(2,1)}, bf16[128,1536]{1,0:T(8,128)(2,1)}, bf16[128,1536]{1,0:T(8,128)(2,1)}, bf16[128,1536]{1,0:T(8,128)(2,1)}) custom-call(s32[4]{0:T(128)} %get-tuple-element.84.meta, bf16[2,128,1536]{2,1,0:T(8,128)(2,1)} %bitcast.59, bf16[1,128,1536]{2,1,0:T(8,128)(2,1)} %bitcast.73, bf16[3,128,1536]{2,1,0:T(8,128)(2,1)} %copy-done.11, ...), custom_call_target="tpu_custom_call" | custom-call | flops 6442450944 | bytes 10485760 | tf_op jit(solution)/shard_map/attend/pallas_call | solution.py:188
  141.0 2.3 %collective-permute-start.18 = (bf16[128,1536]{1,0:T(8,128)(2,1)}, bf16[128,1536]{1,0:T(8,128)(2,1)S(1)}, u32[]{:S(2)}, u32[]{:S(2)}) collective-permute-start(bf16[128,1536]{1,0:T(8,128)(2,1)} %get-tuple-element.107), channel_id=1, source_target_pairs={{3,0},{0,1},{1,2},{2,3},{7,4},{4,5},{5,6},{6,7},{11,8},{8,9},{9,10... | collective-permute-start | bytes 1179656 | tf_op jit(solution)/shard_map/ppermute | solution.py:59
  143.4 13.1 %attend.3 = (bf16[128,1536]{1,0:T(8,128)(2,1)}, bf16[128,1536]{1,0:T(8,128)(2,1)}, bf16[128,1536]{1,0:T(8,128)(2,1)}, bf16[128,1536]{1,0:T(8,128)(2,1)}) custom-call(s32[4]{0:T(128)} %get-tuple-element.84.meta, bf16[2,128,1536]{2,1,0:T(8,128)(2,1)} %bitcast.57, bf16[1,128,1536]{2,1,0:T(8,128)(2,1)} %bitcast.72, bf16[3,128,1536]{2,1,0:T(8,128)(2,1)} %copy-done.10, ...), custom_call_target="tpu_custom_call" | custom-call | flops 6442450944 | bytes 10485760 | tf_op jit(solution)/shard_map/attend/pallas_call | solution.py:188
  156.5 1.9 collective-permute-done.17.refs_1_
  158.4 3.3 %collective-permute-done.19.refs_3_ = bf16[128,1536]{1,0:T(8,128)(2,1)S(1)} collective-permute-done((bf16[128,1536]{1,0:T(8,128)(2,1)}, bf16[128,1536]{1,0:T(8,128)(2,1)S(1)}, u32[]{:S(2)}, u32[]{:S(2)}) %collective-permute-start.19) | collective-permute-done | bytes 393248 | tf_op jit(solution)/shard_map/ppermute | solution.py:59
  161.7 3.1 %collective-permute-start.23 = (bf16[384,1536]{1,0:T(8,128)(2,1)S(1)}, bf16[384,1536]{1,0:T(8,128)(2,1)S(1)}, u32[]{:S(2)}, u32[]{:S(2)}) collective-permute-start(bf16[384,1536]{1,0:T(8,128)(2,1)S(1)} %collective-permute-done.13.refs_6_), channel_id=1, source_target_pairs={{0,32},{1,33},{2,34},{3,35},{4,36},{5,37},{6,38},{7,39},{8,40},{9,... | collective-permute-start | bytes 3538952 | tf_op jit(solution)/shard_map/ppermute | solution.py:59
  164.9 2.4 %collective-permute-done.23.refs_10_ = bf16[384,1536]{1,0:T(8,128)(2,1)S(1)} collective-permute-done((bf16[384,1536]{1,0:T(8,128)(2,1)S(1)}, bf16[384,1536]{1,0:T(8,128)(2,1)S(1)}, u32[]{:S(2)}, u32[]{:S(2)}) %collective-permute-start.23) | collective-permute-done | bytes 1179680 | tf_op jit(solution)/shard_map/ppermute | solution.py:59
  167.2 1.7 collective-permute-done.24.refs_11_
  170.0 11.0 %project.2.refs_13_ = bf16[4,16,16,3072]{3,2,1,0:T(8,128)(2,1)} custom-call(s32[4]{0:T(128)} %get-tuple-element.84.meta, s32[4]{0:T(128)} %get-tuple-element.85.places, bf16[128,1536]{1,0:T(8,128)(2,1)} %get-tuple-element.127.refs_0_, bf16[128,1536]{1,0:T(8,128)(2,1)} %copy-done.17, bf16[128,1536]{1,0:T(8,128)(2,1)} %copy-done.18, ...), custom_call_target="tpu_custom_call" | custom-call | flops 4831838208 | bytes 17825792 | tf_op jit(solution)/shard_map/project/pallas_call | solution.py:271
  182.7 11.1 %project.3 = bf16[4,16,16,3072]{3,2,1,0:T(8,128)(2,1)} custom-call(s32[4]{0:T(128)} %get-tuple-element.84.meta, s32[4]{0:T(128)} %get-tuple-element.85.places, bf16[128,1536]{1,0:T(8,128)(2,1)} %get-tuple-element.119.refs_0_, bf16[128,1536]{1,0:T(8,128)(2,1)} %copy-done.14, bf16[128,1536]{1,0:T(8,128)(2,1)} %copy-done.15, ...), custom_call_target="tpu_custom_call", output_to_operand_aliasing={{}: (15, {})} | custom-call | flops 4831838208 | bytes 17825792 | tf_op jit(solution)/shard_map/project/pallas_call | solution.py:271
  (89 shorter events, 9.4 us)
Async XLA Ops:
  6.5 95.5 %all-gather.2.cloned.1.call-start = ((), (), s32[]{:S(2)}) async-start(), calls=%async_computation | async-start | bytes 1474560 | tf_op jit(solution)/shard_map/all_gather | solution.py:327
  6.5 26.8 %copy-start.23 = (s32[128]{0:T(128)S(1)}, s32[128]{0:T(128)}, u32[]{:S(2)}) copy-start(s32[128]{0:T(128)} %param.11) | copy-start | bytes 1540
  9.1 35.3 %collective-permute-start.1 = (bf16[3,128,1536]{2,1,0:T(8,128)(2,1)}, bf16[3,128,1536]{2,1,0:T(8,128)(2,1)S(1)}, u32[]{:S(2)}, u32[]{:S(2)}) collective-permute-start(bf16[3,128,1536]{2,1,0:T(8,128)(2,1)} %bitcast.67), channel_id=1, source_target_pairs={{0,4},{1,5},{2,6},{3,7},{4,8},{5,9},{6,10},{7,11},{8,12},{9,13},{1... | collective-permute-start | bytes 3538952 | tf_op jit(solution)/shard_map/ppermute | solution.py:59
  13.8 15.8 %collective-permute-start = (bf16[24,1536]{1,0:T(8,128)(2,1)S(1)}, bf16[24,1536]{1,0:T(8,128)(2,1)S(1)}, u32[]{:S(2)}, u32[]{:S(2)}) collective-permute-start(bf16[24,1536]{1,0:T(8,128)(2,1)S(1)} %bitcast.63), channel_id=1, source_target_pairs={{0,16},{1,17},{2,18},{3,19},{4,20},{5,21},{6,22},{7,23},{8,24},{9,... | collective-permute-start | bytes 221192 | tf_op jit(solution)/shard_map/ppermute | solution.py:59
  13.8 30.6 %collective-permute-start.2 = (bf16[3,128,1536]{2,1,0:T(8,128)(2,1)}, bf16[3,128,1536]{2,1,0:T(8,128)(2,1)}, u32[]{:S(2)}, u32[]{:S(2)}) collective-permute-start(bf16[3,128,1536]{2,1,0:T(8,128)(2,1)} %bitcast.66), channel_id=1, source_target_pairs={{0,1},{1,2},{2,3},{3,0},{4,5},{5,6},{6,7},{7,4},{8,9},{9,10},{10,1... | collective-permute-start | bytes 3538952 | tf_op jit(solution)/shard_map/ppermute | solution.py:59
  29.7 13.9 %collective-permute-start.5 = (bf16[2,24,1536]{2,1,0:T(8,128)(2,1)S(1)}, bf16[2,24,1536]{2,1,0:T(8,128)(2,1)S(1)}, u32[]{:S(2)}, u32[]{:S(2)}) collective-permute-start(bf16[2,24,1536]{2,1,0:T(8,128)(2,1)S(1)} %maximum_select_fusion.1), channel_id=1, source_target_pairs={{0,64},{1,65},{2,66},{3,67},{4,68},{5,69},{6,70},{7,71},{8,72},{9,... | collective-permute-start | bytes 442376 | tf_op jit(solution)/shard_map/ppermute | solution.py:59
  37.9 17.4 %collective-permute-start.3 = (bf16[3,128,1536]{2,1,0:T(8,128)(2,1)}, bf16[3,128,1536]{2,1,0:T(8,128)(2,1)S(1)}, u32[]{:S(2)}, u32[]{:S(2)}) collective-permute-start(bf16[3,128,1536]{2,1,0:T(8,128)(2,1)} %bitcast.71), channel_id=1, source_target_pairs={{0,28},{1,29},{2,30},{3,31},{4,0},{5,1},{6,2},{7,3},{8,4},{9,5},{1... | collective-permute-start | bytes 3538952 | tf_op jit(solution)/shard_map/ppermute | solution.py:59
  37.9 17.4 %collective-permute-start.4 = (bf16[3,128,1536]{2,1,0:T(8,128)(2,1)}, bf16[3,128,1536]{2,1,0:T(8,128)(2,1)S(1)}, u32[]{:S(2)}, u32[]{:S(2)}) collective-permute-start(bf16[3,128,1536]{2,1,0:T(8,128)(2,1)} %bitcast.70), channel_id=1, source_target_pairs={{0,3},{1,0},{2,1},{3,2},{4,7},{5,4},{6,5},{7,6},{8,11},{9,8},{10,9... | collective-permute-start | bytes 3538952 | tf_op jit(solution)/shard_map/ppermute | solution.py:59
  58.8 44.7 %collective-permute-start.6 = (bf16[3,128,1536]{2,1,0:T(8,128)(2,1)}, bf16[3,128,1536]{2,1,0:T(8,128)(2,1)S(1)}, u32[]{:S(2)}, u32[]{:S(2)}) collective-permute-start(bf16[3,128,1536]{2,1,0:T(8,128)(2,1)} %bitcast.69), channel_id=1, source_target_pairs={{0,5},{1,6},{2,7},{3,4},{4,9},{5,10},{6,11},{7,8},{8,13},{9,14},{1... | collective-permute-start | bytes 3538952 | tf_op jit(solution)/shard_map/ppermute | solution.py:59
  61.4 42.1 %collective-permute-start.7 = (bf16[3,128,1536]{2,1,0:T(8,128)(2,1)}, bf16[3,128,1536]{2,1,0:T(8,128)(2,1)}, u32[]{:S(2)}, u32[]{:S(2)}) collective-permute-start(bf16[3,128,1536]{2,1,0:T(8,128)(2,1)} %bitcast.68), channel_id=1, source_target_pairs={{0,31},{1,28},{2,29},{3,30},{4,3},{5,0},{6,1},{7,2},{8,7},{9,4},{1... | collective-permute-start | bytes 3538952 | tf_op jit(solution)/shard_map/ppermute | solution.py:59
  61.4 55.8 %collective-permute-start.11 = (bf16[3,2,128,1536]{3,2,1,0:T(8,128)(2,1)S(1)}, bf16[3,2,128,1536]{3,2,1,0:T(8,128)(2,1)}, u32[]{:S(2)}, u32[]{:S(2)}) collective-permute-start(bf16[3,2,128,1536]{3,2,1,0:T(8,128)(2,1)S(1)} %pad_maximum_fusion), channel_id=1, source_target_pairs={{32,0},{33,1},{34,2},{35,3},{36,4},{37,5},{38,6},{39,7},{40,8},{41... | collective-permute-start | bytes 7077896 | tf_op jit(solution)/shard_map/ppermute | solution.py:59
  66.3 50.9 %collective-permute-start.12 = (bf16[3,2,128,1536]{3,2,1,0:T(8,128)(2,1)}, bf16[3,2,128,1536]{3,2,1,0:T(8,128)(2,1)}, u32[]{:S(2)}, u32[]{:S(2)}) collective-permute-start(bf16[3,2,128,1536]{3,2,1,0:T(8,128)(2,1)} %pad_maximum_fusion.1), channel_id=1, source_target_pairs={{0,32},{1,33},{2,34},{3,35},{4,36},{5,37},{6,38},{7,39},{8,40},{9,... | collective-permute-start | bytes 7077896 | tf_op jit(solution)/shard_map/ppermute | solution.py:59
  103.4 23.2 %copy-start = (bf16[4,4,24,1536]{3,2,1,0:T(8,128)(2,1)}, bf16[4,4,24,1536]{3,2,1,0:T(8,128)(2,1)S(1)}, u32[]{:S(2)}) copy-start(bf16[4,4,24,1536]{3,2,1,0:T(8,128)(2,1)S(1)} %copy.8) | copy-start | bytes 3538948
  103.5 22.0 %collective-permute-start.8 = (bf16[384,1536]{1,0:T(8,128)(2,1)S(1)}, bf16[384,1536]{1,0:T(8,128)(2,1)S(1)}, u32[]{:S(2)}, u32[]{:S(2)}) collective-permute-start(bf16[384,1536]{1,0:T(8,128)(2,1)S(1)} %bitcast.50), channel_id=1, source_target_pairs={{0,4},{1,5},{2,6},{3,7},{4,8},{5,9},{6,10},{7,11},{8,12},{9,13},{1... | collective-permute-start | bytes 3538952 | tf_op jit(solution)/shard_map/ppermute | solution.py:59
  105.4 19.9 %collective-permute-start.10 = (bf16[2,128,1536]{2,1,0:T(8,128)(2,1)S(1)}, bf16[2,128,1536]{2,1,0:T(8,128)(2,1)S(1)}, u32[]{:S(2)}, u32[]{:S(2)}) collective-permute-start(bf16[2,128,1536]{2,1,0:T(8,128)(2,1)S(1)} %slice.23), channel_id=1, source_target_pairs={{0,32},{1,33},{2,34},{3,35},{4,36},{5,37},{6,38},{7,39},{8,40},{9,... | collective-permute-start | bytes 2359304 | tf_op jit(solution)/shard_map/ppermute | solution.py:59
  108.9 16.6 %collective-permute-start.9 = (bf16[2,128,1536]{2,1,0:T(8,128)(2,1)S(1)}, bf16[2,128,1536]{2,1,0:T(8,128)(2,1)S(1)}, u32[]{:S(2)}, u32[]{:S(2)}) collective-permute-start(bf16[2,128,1536]{2,1,0:T(8,128)(2,1)S(1)} %slice.22), channel_id=1, source_target_pairs={{32,0},{33,1},{34,2},{35,3},{36,4},{37,5},{38,6},{39,7},{40,8},{41... | collective-permute-start | bytes 2359304 | tf_op jit(solution)/shard_map/ppermute | solution.py:59
  125.5 15.2 %copy-start.1 = (bf16[384,1536]{1,0:T(8,128)(2,1)}, bf16[384,1536]{1,0:T(8,128)(2,1)S(1)}, u32[]{:S(2)}) copy-start(bf16[384,1536]{1,0:T(8,128)(2,1)S(1)} %collective-permute-done.8.refs_5_) | copy-start | bytes 3538948
  125.5 15.2 %collective-permute-start.16 = (bf16[384,1536]{1,0:T(8,128)(2,1)S(1)}, bf16[384,1536]{1,0:T(8,128)(2,1)S(1)}, u32[]{:S(2)}, u32[]{:S(2)}) collective-permute-start(bf16[384,1536]{1,0:T(8,128)(2,1)S(1)} %collective-permute-done.8.refs_5_), channel_id=1, source_target_pairs={{0,32},{1,33},{2,34},{3,35},{4,36},{5,37},{6,38},{7,39},{8,40},{9,... | collective-permute-start | bytes 3538952 | tf_op jit(solution)/shard_map/ppermute | solution.py:59
  125.6 15.1 %collective-permute-start.15 = (bf16[384,1536]{1,0:T(8,128)(2,1)S(1)}, bf16[384,1536]{1,0:T(8,128)(2,1)S(1)}, u32[]{:S(2)}, u32[]{:S(2)}) collective-permute-start(bf16[384,1536]{1,0:T(8,128)(2,1)S(1)} %bitcast.51), channel_id=1, source_target_pairs={{0,32},{1,33},{2,34},{3,35},{4,36},{5,37},{6,38},{7,39},{8,40},{9,... | collective-permute-start | bytes 3538952 | tf_op jit(solution)/shard_map/ppermute | solution.py:59
  126.2 30.3 %collective-permute-start.13 = (bf16[384,1536]{1,0:T(8,128)(2,1)S(1)}, bf16[384,1536]{1,0:T(8,128)(2,1)S(1)}, u32[]{:S(2)}, u32[]{:S(2)}) collective-permute-start(bf16[384,1536]{1,0:T(8,128)(2,1)S(1)} %collective-permute-done.8.refs_5_), channel_id=1, source_target_pairs={{0,4},{1,5},{2,6},{3,7},{4,8},{5,9},{6,10},{7,11},{8,12},{9,13},{1... | collective-permute-start | bytes 3538952 | tf_op jit(solution)/shard_map/ppermute | solution.py:59
  126.6 29.9 %collective-permute-start.14 = (bf16[384,1536]{1,0:T(8,128)(2,1)S(1)}, bf16[384,1536]{1,0:T(8,128)(2,1)S(1)}, u32[]{:S(2)}, u32[]{:S(2)}) collective-permute-start(bf16[384,1536]{1,0:T(8,128)(2,1)S(1)} %bitcast.52), channel_id=1, source_target_pairs={{0,12},{1,13},{2,14},{3,15},{4,0},{5,1},{6,2},{7,3},{8,4},{9,5},{1... | collective-permute-start | bytes 3538952 | tf_op jit(solution)/shard_map/ppermute | solution.py:59
  140.7 15.8 %copy-start.2 = (bf16[384,1536]{1,0:T(8,128)(2,1)}, bf16[384,1536]{1,0:T(8,128)(2,1)S(1)}, u32[]{:S(2)}) copy-start(bf16[384,1536]{1,0:T(8,128)(2,1)S(1)} %collective-permute-done.16.refs_9_) | copy-start | bytes 3538948
  140.7 15.8 %copy-start.3 = (bf16[384,1536]{1,0:T(8,128)(2,1)}, bf16[384,1536]{1,0:T(8,128)(2,1)S(1)}, u32[]{:S(2)}) copy-start(bf16[384,1536]{1,0:T(8,128)(2,1)S(1)} %collective-permute-done.15.refs_8_) | copy-start | bytes 3538948
  140.7 17.7 %collective-permute-start.17 = (bf16[128,1536]{1,0:T(8,128)(2,1)}, bf16[128,1536]{1,0:T(8,128)(2,1)S(1)}, u32[]{:S(2)}, u32[]{:S(2)}) collective-permute-start(bf16[128,1536]{1,0:T(8,128)(2,1)} %get-tuple-element.106), channel_id=1, source_target_pairs={{28,0},{29,1},{30,2},{31,3},{0,4},{1,5},{2,6},{3,7},{4,8},{5,9},{6... | collective-permute-start | bytes 1179656 | tf_op jit(solution)/shard_map/ppermute | solution.py:59
  141.0 17.4 %collective-permute-start.18 = (bf16[128,1536]{1,0:T(8,128)(2,1)}, bf16[128,1536]{1,0:T(8,128)(2,1)S(1)}, u32[]{:S(2)}, u32[]{:S(2)}) collective-permute-start(bf16[128,1536]{1,0:T(8,128)(2,1)} %get-tuple-element.107), channel_id=1, source_target_pairs={{3,0},{0,1},{1,2},{2,3},{7,4},{4,5},{5,6},{6,7},{11,8},{8,9},{9,10... | collective-permute-start | bytes 1179656 | tf_op jit(solution)/shard_map/ppermute | solution.py:59
  143.4 18.3 %collective-permute-start.19 = (bf16[128,1536]{1,0:T(8,128)(2,1)}, bf16[128,1536]{1,0:T(8,128)(2,1)S(1)}, u32[]{:S(2)}, u32[]{:S(2)}) collective-permute-start(bf16[128,1536]{1,0:T(8,128)(2,1)} %get-tuple-element.108), channel_id=1, source_target_pairs={{31,0},{28,1},{29,2},{30,3},{3,4},{0,5},{1,6},{2,7},{7,8},{4,9},{5... | collective-permute-start | bytes 1179656 | tf_op jit(solution)/shard_map/ppermute | solution.py:59
  156.5 12.4 %copy-start.4 = (bf16[384,1536]{1,0:T(8,128)(2,1)}, bf16[384,1536]{1,0:T(8,128)(2,1)S(1)}, u32[]{:S(2)}) copy-start(bf16[384,1536]{1,0:T(8,128)(2,1)S(1)} %collective-permute-done.13.refs_6_) | copy-start | bytes 3538948
  161.7 5.5 %collective-permute-start.23 = (bf16[384,1536]{1,0:T(8,128)(2,1)S(1)}, bf16[384,1536]{1,0:T(8,128)(2,1)S(1)}, u32[]{:S(2)}, u32[]{:S(2)}) collective-permute-start(bf16[384,1536]{1,0:T(8,128)(2,1)S(1)} %collective-permute-done.13.refs_6_), channel_id=1, source_target_pairs={{0,32},{1,33},{2,34},{3,35},{4,36},{5,37},{6,38},{7,39},{8,40},{9,... | collective-permute-start | bytes 3538952 | tf_op jit(solution)/shard_map/ppermute | solution.py:59
  164.8 4.2 %collective-permute-start.24 = (bf16[384,1536]{1,0:T(8,128)(2,1)S(1)}, bf16[384,1536]{1,0:T(8,128)(2,1)S(1)}, u32[]{:S(2)}, u32[]{:S(2)}) collective-permute-start(bf16[384,1536]{1,0:T(8,128)(2,1)S(1)} %collective-permute-done.14.refs_7_), channel_id=1, source_target_pairs={{0,32},{1,33},{2,34},{3,35},{4,36},{5,37},{6,38},{7,39},{8,40},{9,... | collective-permute-start | bytes 3538952 | tf_op jit(solution)/shard_map/ppermute | solution.py:59
  164.8 16.2 %collective-permute-start.20 = (bf16[128,1536]{1,0:T(8,128)(2,1)}, bf16[128,1536]{1,0:T(8,128)(2,1)S(1)}, u32[]{:S(2)}, u32[]{:S(2)}) collective-permute-start(bf16[128,1536]{1,0:T(8,128)(2,1)} %get-tuple-element.120), channel_id=1, source_target_pairs={{4,0},{5,1},{6,2},{7,3},{8,4},{9,5},{10,6},{11,7},{12,8},{13,9},{1... | collective-permute-start | bytes 1179656 | tf_op jit(solution)/shard_map/ppermute | solution.py:59
  164.8 16.3 %collective-permute-start.21 = (bf16[128,1536]{1,0:T(8,128)(2,1)}, bf16[128,1536]{1,0:T(8,128)(2,1)S(1)}, u32[]{:S(2)}, u32[]{:S(2)}) collective-permute-start(bf16[128,1536]{1,0:T(8,128)(2,1)} %get-tuple-element.121), channel_id=1, source_target_pairs={{1,0},{2,1},{3,2},{0,3},{5,4},{6,5},{7,6},{4,7},{9,8},{10,9},{11,1... | collective-permute-start | bytes 1179656 | tf_op jit(solution)/shard_map/ppermute | solution.py:59
  164.8 16.3 %collective-permute-start.22 = (bf16[128,1536]{1,0:T(8,128)(2,1)}, bf16[128,1536]{1,0:T(8,128)(2,1)S(1)}, u32[]{:S(2)}, u32[]{:S(2)}) collective-permute-start(bf16[128,1536]{1,0:T(8,128)(2,1)} %get-tuple-element.122), channel_id=1, source_target_pairs={{5,0},{6,1},{7,2},{4,3},{9,4},{10,5},{11,6},{8,7},{13,8},{14,9},{1... | collective-permute-start | bytes 1179656 | tf_op jit(solution)/shard_map/ppermute | solution.py:59
  (18 other events, 67.6 us)
Sparse Core Ops, SparseCore 0:
  58.9 43.1 all-gather.1
